TPU v7x, 32 devices: a whole 2x2x4 slice. The times are simulated.
32 devices in a mesh: hours: 16 (over z, x, core), region: 2 (over y).
Axes of the slice: x: 2, y: 2, z: 4, core: 2. Of those that a mesh axis runs over, the one named last changes fastest.
Arguments:
- availability: float32 [1024, 16, 256], P('hours', None, 'region'), may hold values from 0.1 to 1
- demand: float32 [1024, 256], P('hours', 'region'), may hold values from 2 to 72, as said below
- gen_cost: float32 [16, 256], P(None, 'region'), may hold values from 0.05 to 1
- cap_cost: float32 [2, 2048], P('region', 'hours'), may hold values from 51.2 to 512
- owner_map: int32 [2, 2048], P('region'), may hold values from 0 to 2047, each once within a row
- line_ends: int32 [2, 512], P(None, 'region'), may hold values from 0 to 127
- line_limit: float32 [512], P('region'), may hold values from 0.5 to 4
- cross_ends: int32 [2, 2, 64], P(None, 'region'), may hold values from 0 to 127
- cross_limit: float32 [2, 64], P('region'), may hold values from 0.5 to 4
- pair_counts: int32 [2, 2], P('region'), may hold values from 0 to 32, as said below
- store_node: int32 [512], P('region'), may hold values from 0 to 127
- store_energy: float32 [512], P('region'), may hold values from 0.02 to 0.4
- store_power: float32 [512], P('region'), may hold values from 0.2 to 2
- price_start: float32 [1024, 256], P('hours', 'region'), may hold values from -3 to 0.5
Outputs:
- dispatch: float32 [1024, 16, 256], P('hours', None, 'region')
- capacity: float32 [2, 2048], P('region', 'hours')
- prices: float32 [1024, 256], P('hours', 'region')
- charge_state: float32 [1024, 512], P('hours', 'region')
Inputs may be any that keep to these rules, and one draw needn't show every extreme that they name: `demand`: loads are positive. `owner_map`: each row lists every capacity column of its region once. `pair_counts`: cross lines in use among the 32 slots of each ordered pair of regions; a region has none to itself; some pair uses all 32.
All inputs are finite; a program needn't handle non-finite values.
Results may differ from a plain program's by a relative error of at most 0.00018.
Values sent between devices are 32-bit elements; how exact they have to be, the bound alone decides.
No kernel may reach another device: no remote copies, remote signals or barrier semaphores. Data moves between devices by JAX's collectives and lax.ppermute only.
A program may use at most 64 MiB of HBM per device.

v0:
```python
import jax
import jax.numpy as jnp
from jax import lax
from jax.sharding import PartitionSpec as P

ITERS = 4


epsilon = 1e-06
highest = lax.Precision.HIGHEST


def shifted(value, axis, steps):
    count = lax.axis_size(axis)
    pairs = [(source, (source + steps) % count) for source in range(count)]
    return lax.ppermute(value, axis, pairs)


def one_hot(indices, labels):
    return (indices[:, None] == labels[None, :]).astype(jnp.float32)


def to_owners(partial_value, owned_cols):
    summed = lax.psum(partial_value, "hours")
    return lax.dynamic_slice_in_dim(summed, lax.axis_index("hours") * owned_cols, owned_cols)


def spread_columns(capacity_bar):
    return lax.all_gather(capacity_bar, "hours", axis=0, tiled=True)


def body(
    availability,
    demand,
    gen_cost,
    cap_cost,
    owner_map,
    line_ends,
    line_limit,
    cross_ends,
    cross_limit,
    pair_counts,
    store_node,
    store_energy,
    store_power,
    price_start,
):
    hour_rows, tech_count, node_count = availability.shape
    region_count = lax.axis_size("region")
    slot_count = cross_limit.shape[1]
    slot_width = slot_count // region_count
    owned_cols = cap_cost.shape[1]
    owner_cols = owner_map[0]
    inverse = jnp.argsort(owner_cols)
    node_ids = jnp.arange(node_count, dtype=jnp.int32)
    line_inc = one_hot(line_ends[1], node_ids) - one_hot(line_ends[0], node_ids)
    store_map = one_hot(store_node, node_ids)
    leave_map = one_hot(cross_ends[0, 0], node_ids)
    slot_ids = jnp.arange(slot_count, dtype=jnp.int32)
    pair_of = slot_ids // slot_width
    region_ids = jnp.arange(region_count, dtype=jnp.int32)
    in_use = jnp.sum(
        jnp.where(pair_of[:, None] == region_ids[None, :], pair_counts[0][None, :], 0), axis=1
    )
    cross_bound = jnp.where(slot_ids % slot_width < in_use, cross_limit[0], 0.0)
    reach_map = one_hot(
        pair_of * node_count + cross_ends[1, 0],
        jnp.arange(region_count * node_count, dtype=jnp.int32),
    )
    column_costs = cap_cost[0]
    col_weight = to_owners(jnp.sum(availability, axis=0).reshape(-1)[owner_cols], owned_cols)
    dispatch = jnp.zeros_like(availability)
    capacity = jnp.zeros((owned_cols,), jnp.float32)
    inner_flow = jnp.zeros((hour_rows, line_limit.shape[0]), jnp.float32)
    cross_flow = jnp.zeros((hour_rows, slot_count), jnp.float32)
    mirror_flow = jnp.zeros((hour_rows, slot_count), jnp.float32)
    discharge = jnp.zeros((hour_rows, store_node.shape[0]), jnp.float32)
    charge = jnp.zeros((hour_rows, store_node.shape[0]), jnp.float32)
    prices = price_start
    cap_duals = jnp.zeros_like(availability)
    store_duals = jnp.zeros((hour_rows, store_node.shape[0]), jnp.float32)
    weight = jnp.float32(1.0)
    for iteration in range(ITERS):
        final_sweep = iteration == ITERS - 1
        primal_step = 0.5 / weight
        far_side = jnp.dot(
            lax.all_gather(prices, "region", axis=1, tiled=True), reach_map.T, precision=highest
        )
        if iteration == 0:
            next_duals = jnp.zeros_like(store_duals)
            cap_pull = jnp.zeros((owned_cols,), jnp.float32)
        else:
            next_row = shifted(store_duals[:1], "hours", -1)
            next_duals = jnp.concatenate([store_duals[1:], next_row], axis=0)
            cap_pull = to_owners(
                jnp.sum(availability * cap_duals, axis=0).reshape(-1)[owner_cols], owned_cols
            )
        dispatch_new = jnp.maximum(
            dispatch - primal_step * (gen_cost[None] + prices[:, None, :] + cap_duals), 0.0
        )
        capacity_new = jnp.maximum(
            capacity - (column_costs - cap_pull) / (weight * col_weight), 0.0
        )
        inner_new = jnp.clip(
            inner_flow - primal_step * jnp.dot(prices, line_inc.T, precision=highest),
            -line_limit,
            line_limit,
        )
        cross_new = jnp.clip(
            cross_flow - primal_step * (far_side - jnp.dot(prices, leave_map.T, precision=highest)),
            -cross_bound,
            cross_bound,
        )
        mirror_new = mirror_flow
        discharge_new = jnp.clip(
            discharge
            - primal_step * (jnp.dot(prices, store_map.T, precision=highest) + store_duals),
            -store_power,
            store_power,
        )
        charge_new = jnp.clip(charge - primal_step * (store_duals - next_duals), 0.0, store_energy)
        if not final_sweep:
            cap_change = capacity_new - capacity
            primal_sq = (
                jnp.sum((dispatch_new - dispatch) ** 2)
                + jnp.sum(cap_change**2)
                + jnp.sum((inner_new - inner_flow) ** 2)
                + jnp.sum((cross_new - cross_flow) ** 2)
                + jnp.sum((discharge_new - discharge) ** 2)
                + jnp.sum((charge_new - charge) ** 2)
            )
            primal_sum = lax.psum(primal_sq, ("hours", "region"))
        dispatch_bar = 2.0 * dispatch_new - dispatch
        capacity_bar = 2.0 * capacity_new - capacity
        inner_bar = 2.0 * inner_new - inner_flow
        cross_bar = 2.0 * cross_new - cross_flow
        discharge_bar = 2.0 * discharge_new - discharge
        charge_bar = 2.0 * charge_new - charge
        capacity_all = spread_columns(capacity_bar)
        cap_dense = capacity_all[inverse].reshape(tech_count, node_count)
        per_dest = jnp.dot(cross_bar, reach_map, precision=highest)
        balance = (
            jnp.sum(dispatch_bar, axis=1)
            + jnp.dot(inner_bar, line_inc, precision=highest)
            + (
                lax.psum_scatter(per_dest, "region", scatter_dimension=1, tiled=True)
                - jnp.dot(cross_bar, leave_map, precision=highest)
            )
            + jnp.dot(discharge_bar, store_map, precision=highest)
            - demand
        )
        prev_row = shifted(charge_bar[-1:], "hours", 1)
        storage_rows = (
            charge_bar - jnp.concatenate([prev_row, charge_bar[:-1]], axis=0) + discharge_bar
        )
        cap_rows = dispatch_bar - availability * cap_dense[None]
        prices_new = prices + weight / (tech_count + 8.0) * balance
        cap_new = jnp.maximum(cap_duals + weight / 2.0 * cap_rows, 0.0)
        store_new = store_duals + weight / 3.0 * storage_rows
        if not final_sweep:
            dual_sq = (
                jnp.sum((prices_new - prices) ** 2)
                + jnp.sum((cap_new - cap_duals) ** 2)
                + jnp.sum((store_new - store_duals) ** 2)
            )
            dual_sum = lax.psum(dual_sq, ("hours", "region"))
            weight = jnp.sqrt(weight * jnp.sqrt((dual_sum + epsilon) / (primal_sum + epsilon)))
        dispatch, capacity, inner_flow, cross_flow = (
            dispatch_new,
            capacity_new,
            inner_new,
            cross_new,
        )
        mirror_flow = mirror_new
        discharge, charge = (discharge_new, charge_new)
        prices, cap_duals, store_duals = (prices_new, cap_new, store_new)
    return (dispatch, capacity[None], prices, charge)


def solution(mesh):
    placed = (
        P("hours", None, "region"),
        P("hours", "region"),
        P(None, "region"),
        P("region", "hours"),
        P("region", None),
        P(None, "region"),
        P("region"),
        P(None, "region", None),
        P("region", None),
        P("region", None),
        P("region"),
        P("region"),
        P("region"),
        P("hours", "region"),
    )
    return jax.shard_map(
        body,
        mesh=mesh,
        in_specs=placed,
        out_specs=(
            P("hours", None, "region"),
            P("region", "hours"),
            P("hours", "region"),
            P("hours", "region"),
        ),
        check_vma=False,
    )
```

profile of v0, /device:TPU:0, one launch (start us, length us, event | category | flops | bytes accessed | tf_op | source)
XLA Modules:
  0.0 507.8 jit_solution(10946836554110924094)
XLA Ops:
  7.2 0.7 broadcast_minimum_fusion
  8.4 0.7 slice_bitcast_fusion
  9.1 0.7 bitcast_add_fusion
  9.7 5.3 %all_gather.21 = f32[64,256]{1,0:T(8,128)S(1)} all-gather(f32[64,128]{1,0:T(8,128)} %param.27), channel_id=1, replica_groups=mesh['hours'=16,'region'=2] {'region'}, dimensions={1}, use_global_device_ids=true | all-gather | bytes 98304 | tf_op jit(solution)/shard_map/all_gather | solution.py:87
  15.1 0.7 fusion.155
  15.8 0.7 negate_bitcast_fusion
  16.7 1.6 multiply_reduce_fusion.24
  18.3 0.9 fusion.110
  19.3 0.7 copy-done.10
  20.0 0.7 broadcast_reduce_fusion
  20.8 11.8 %gather_fusion = f32[2048]{0:T(1024)S(1)} fusion(f32[2048]{0:T(1024)S(1)} %bitcast.91, s32[2048]{0:T(1024)S(1)} %broadcast_clamp_fusion), kind=kCustom, calls=%fused_computation | custom fusion | bytes 24576 | tf_op jit(solution)/shard_map/gather | solution.py:71
  32.6 33.6 %psum.70 = f32[2048]{0:T(1024)S(1)} all-reduce(f32[2048]{0:T(1024)S(1)} %gather_fusion), channel_id=1, replica_groups=mesh['hours'=16,'region'=2] {'hours'}, use_global_device_ids=true, to_apply=%region_5.6 | all-reduce | flops 2048 | bytes 16384 | tf_op jit(solution)/shard_map/psum | solution.py:24
  66.8 0.7 multiply_reduce_fusion.28
  67.5 17.0 %all-gather = f32[16,1,128]{2,1,0:T(1,128)S(1)} all-gather(f32[1,1,128]{2,1,0:T(1,128)S(1)} %multiply_bitcast_fusion), channel_id=1, replica_groups=mesh['hours'=16,'region'=2] {'hours'}, dimensions={0}, use_global_device_ids=true | all-gather | bytes 8704 | tf_op jit(solution)/shard_map/all_gather | solution.py:29
  84.5 5.0 sort.17
  89.5 11.8 %gather_fusion.1 = f32[2048]{0:T(1024)S(1)} fusion(f32[2048]{0:T(1024)S(1)} %bitcast.86, s32[2048]{0:T(1024)S(1)} %fusion.154), kind=kCustom, calls=%fused_computation.1 | custom fusion | bytes 24576 | tf_op jit(solution)/shard_map/gather | solution.py:140
  101.3 1.0 multiply_reduce_fusion.6
  102.4 11.8 %gather_fusion.2 = f32[2048]{0:T(1024)S(1)} fusion(f32[2048]{0:T(1024)S(1)} %bitcast.89, s32[2048]{0:T(1024)S(1)} %broadcast_clamp_fusion), kind=kCustom, calls=%fused_computation.2 | custom fusion | bytes 24576 | tf_op jit(solution)/shard_map/gather | solution.py:96
  114.1 1.0 multiply_reduce_fusion.18
  115.5 31.9 %psum.73 = f32[2048]{0:T(1024)S(1)} all-reduce(f32[2048]{0:T(1024)S(1)} %gather_fusion.2), channel_id=1, replica_groups=mesh['hours'=16,'region'=2] {'hours'}, use_global_device_ids=true, to_apply=%region_21.22 | all-reduce | flops 2048 | bytes 16384 | tf_op jit(solution)/shard_map/psum | solution.py:24
  150.6 0.9 multiply_reduce_fusion.17
  152.9 1.0 fusion.62
  153.9 0.9 multiply_reduce_fusion.25
  156.8 37.1 %all-reduce.2 = (f32[]{:T(128)}, f32[]{:T(128)}) all-reduce(f32[]{:T(128)S(6)} %add.309, f32[]{:T(128)S(6)} %add.315), channel_id=1, replica_groups=mesh['hours'=16,'region'=2] {'hours','region'}, use_global_device_ids=true, to_apply=%region_9.10 | all-reduce | flops 2 | bytes 16 | tf_op jit(solution)/shard_map/psum | solution.py:166
  195.3 0.7 multiply_reduce_fusion.27
  196.0 21.0 %all-gather.1 = f32[16,1,128]{2,1,0:T(1,128)S(1)} all-gather(f32[1,1,128]{2,1,0:T(1,128)S(1)} %subtract_bitcast_fusion.1), channel_id=1, replica_groups=mesh['hours'=16,'region'=2] {'hours'}, dimensions={0}, use_global_device_ids=true | all-gather | bytes 8704 | tf_op jit(solution)/shard_map/all_gather | solution.py:29
  216.9 11.8 %gather_fusion.3 = f32[2048]{0:T(1024)S(1)} fusion(f32[2048]{0:T(1024)S(1)} %bitcast.92, s32[2048]{0:T(1024)S(1)} %fusion.154), kind=kCustom, calls=%fused_computation.3 | custom fusion | bytes 24576 | tf_op jit(solution)/shard_map/gather | solution.py:140
  228.7 1.0 multiply_reduce_fusion.15
  229.8 1.2 multiply_reduce_fusion.3
  231.0 4.6 all_gather.23
  235.5 11.8 %gather_fusion.4 = f32[2048]{0:T(1024)S(1)} fusion(f32[2048]{0:T(1024)S(1)} %bitcast.87, s32[2048]{0:T(1024)S(1)} %broadcast_clamp_fusion), kind=kCustom, calls=%fused_computation.4 | custom fusion | bytes 24576 | tf_op jit(solution)/shard_map/gather | solution.py:96
  247.3 0.7 copy-done.6
  248.0 0.7 multiply_reduce_fusion.13
  249.0 0.9 multiply_reduce_fusion.22
  249.8 0.9 fusion.108
  251.1 34.5 %psum.76 = f32[2048]{0:T(1024)S(1)} all-reduce(f32[2048]{0:T(1024)S(1)} %gather_fusion.4), channel_id=1, replica_groups=mesh['hours'=16,'region'=2] {'hours'}, use_global_device_ids=true, to_apply=%region_36.37 | all-reduce | flops 2048 | bytes 16384 | tf_op jit(solution)/shard_map/psum | solution.py:24
  288.2 0.9 multiply_reduce_fusion.14
  290.4 2.7 reduce-scatter.7.cloned.1.call-done
  293.1 1.0 fusion.54
  294.1 0.9 multiply_reduce_fusion.23
  297.0 3.2 collective-permute-start.3
  300.2 36.8 %all-reduce.1 = (f32[]{:T(128)}, f32[]{:T(128)}) all-reduce(f32[]{:T(128)S(6)} %add.329, f32[]{:T(128)S(6)} %add.335), channel_id=1, replica_groups=mesh['hours'=16,'region'=2] {'hours','region'}, use_global_device_ids=true, to_apply=%region_24.25 | all-reduce | flops 2 | bytes 16 | tf_op jit(solution)/shard_map/psum | solution.py:166
  338.5 0.7 multiply_reduce_fusion.26
  339.2 1.0 multiply_reduce_fusion.11
  340.2 5.0 all_gather.25
  345.9 20.6 %all-gather.2 = f32[16,1,128]{2,1,0:T(1,128)S(1)} all-gather(f32[1,1,128]{2,1,0:T(1,128)S(1)} %subtract_bitcast_fusion), channel_id=1, replica_groups=mesh['hours'=16,'region'=2] {'hours'}, dimensions={0}, use_global_device_ids=true | all-gather | bytes 8704 | tf_op jit(solution)/shard_map/all_gather | solution.py:29
  366.5 11.8 %gather_fusion.5 = f32[2048]{0:T(1024)S(1)} fusion(f32[2048]{0:T(1024)S(1)} %bitcast.90, s32[2048]{0:T(1024)S(1)} %fusion.154), kind=kCustom, calls=%fused_computation.5 | custom fusion | bytes 24576 | tf_op jit(solution)/shard_map/gather | solution.py:140
  378.8 1.4 multiply_reduce_fusion
  380.2 11.8 %gather_fusion.6 = f32[2048]{0:T(1024)S(1)} fusion(f32[2048]{0:T(1024)S(1)} %bitcast.88, s32[2048]{0:T(1024)S(1)} %broadcast_clamp_fusion), kind=kCustom, calls=%fused_computation.6 | custom fusion | bytes 24576 | tf_op jit(solution)/shard_map/gather | solution.py:96
  392.2 0.9 multiply_reduce_fusion.20
  393.1 0.9 fusion.106
  394.3 34.1 %psum.79 = f32[2048]{0:T(1024)S(1)} all-reduce(f32[2048]{0:T(1024)S(1)} %gather_fusion.6), channel_id=1, replica_groups=mesh['hours'=16,'region'=2] {'hours'}, use_global_device_ids=true, to_apply=%region_48.49 | all-reduce | flops 2048 | bytes 16384 | tf_op jit(solution)/shard_map/psum | solution.py:24
  431.0 0.9 multiply_reduce_fusion.12
  433.3 2.0 reduce-scatter.9.cloned.1.call-done
  435.2 1.0 fusion.46
  436.2 0.9 multiply_reduce_fusion.21
  439.1 3.2 collective-permute-start.5
  442.3 36.8 %all-reduce = (f32[]{:T(128)}, f32[]{:T(128)}) all-reduce(f32[]{:T(128)S(6)} %add.349, f32[]{:T(128)S(6)} %add.355), channel_id=1, replica_groups=mesh['hours'=16,'region'=2] {'hours','region'}, use_global_device_ids=true, to_apply=%region_39.40 | all-reduce | flops 2 | bytes 16 | tf_op jit(solution)/shard_map/psum | solution.py:166
  481.3 5.0 all_gather.27
  486.3 1.6 subtract_reduce_fusion
  488.3 0.9 fusion.104
  490.8 8.7 %reduce-scatter.11.cloned.1.call-done = f32[64,128]{1,0:T(8,128)} async-done(((f32[64,256]{1,0:T(8,128)}), f32[64,128]{1,0:T(8,128)}) %reduce-scatter.11.cloned.1.call-update) | async-done | bytes 32784 | tf_op jit(solution)/shard_map/reduce_scatter | solution.py:146
  499.4 1.0 fusion.36
  500.4 0.9 fusion.35
  (76 shorter events, 7.9 us)
Async XLA Ops:
  7.2 13.5 %copy-start = (f32[64,16,128]{2,1,0:T(8,128)S(1)}, f32[64,16,128]{2,1,0:T(8,128)}, u32[]{:S(2)}) copy-start(f32[64,16,128]{2,1,0:T(8,128)} %param.14) | copy-start | bytes 1572868
  7.2 145.7 %reduce-scatter.5.cloned.1.call-start = ((), (), s32[]{:S(2)}) async-start(), calls=%async_computation.4 | async-start | bytes 98304 | tf_op jit(solution)/shard_map/reduce_scatter | solution.py:146
  8.0 142.0 %collective-permute-start = (f32[1,256]{1,0:T(1,128)S(1)}, f32[1,256]{1,0:T(1,128)S(1)}, u32[]{:S(2)}, u32[]{:S(2)}) collective-permute-start(f32[1,256]{1,0:T(1,128)S(1)} %bitcast.122), channel_id=1, source_target_pairs={{0,2},{2,4},{4,6},{6,8},{8,10},{10,12},{12,14},{14,16},{16,18},{18... | collective-permute-start | bytes 3080 | tf_op jit(solution)/shard_map/ppermute | solution.py:16
  19.2 273.9 %reduce-scatter.7.cloned.1.call-start = ((), (), s32[]{:S(2)}) async-start(), calls=%async_computation.5 | async-start | bytes 98304 | tf_op jit(solution)/shard_map/reduce_scatter | solution.py:146
  19.3 0.7 copy-start.9
  19.3 0.7 copy-start.10
  19.3 1.4 copy-start.5
  66.1 0.7 copy-start.8
  89.5 11.8 %copy-start.1 = (f32[64,128]{1,0:T(8,128)S(1)}, f32[64,128]{1,0:T(8,128)}, u32[]{:S(2)}) copy-start(f32[64,128]{1,0:T(8,128)} %param.27) | copy-start | bytes 98308
  89.5 11.8 %copy-start.3 = (f32[16,128]{1,0:T(8,128)S(1)}, f32[16,128]{1,0:T(8,128)}, u32[]{:S(2)}) copy-start(f32[16,128]{1,0:T(8,128)} %param.16) | copy-start | bytes 24580
  115.5 31.9 %copy-start.7 = (f32[256]{0:T(256)S(1)}, f32[256]{0:T(256)}, u32[]{:S(2)}) copy-start(f32[256]{0:T(256)} %param.26) | copy-start | bytes 3076
  149.9 0.7 copy-start.4
  152.8 1.0 copy-start.2
  156.7 90.6 %collective-permute-start.1 = (f32[1,256]{1,0:T(1,128)S(1)}, f32[1,256]{1,0:T(1,128)S(1)}, u32[]{:S(2)}, u32[]{:S(2)}) collective-permute-start(f32[1,256]{1,0:T(1,128)S(1)} %slice.79), channel_id=1, source_target_pairs={{0,30},{2,0},{4,2},{6,4},{8,6},{10,8},{12,10},{14,12},{16,14},{18,... | collective-permute-start | bytes 3080 | tf_op jit(solution)/shard_map/ppermute | solution.py:16
  247.3 0.7 copy-start.6
  248.7 39.5 %collective-permute-start.2 = (f32[1,256]{1,0:T(1,128)S(1)}, f32[1,256]{1,0:T(1,128)S(1)}, u32[]{:S(2)}, u32[]{:S(2)}) collective-permute-start(f32[1,256]{1,0:T(1,128)S(1)} %slice.80), channel_id=1, source_target_pairs={{0,2},{2,4},{4,6},{6,8},{8,10},{10,12},{12,14},{14,16},{16,18},{18... | collective-permute-start | bytes 3080 | tf_op jit(solution)/shard_map/ppermute | solution.py:16
  285.6 149.6 %reduce-scatter.9.cloned.1.call-start = ((), (), s32[]{:S(2)}) async-start(), calls=%async_computation.6 | async-start | bytes 98304 | tf_op jit(solution)/shard_map/reduce_scatter | solution.py:146
  297.0 48.3 %collective-permute-start.3 = (f32[1,256]{1,0:T(1,128)S(1)}, f32[1,256]{1,0:T(1,128)S(1)}, u32[]{:S(2)}, u32[]{:S(2)}) collective-permute-start(f32[1,256]{1,0:T(1,128)S(1)} %slice.83), channel_id=1, source_target_pairs={{0,30},{2,0},{4,2},{6,4},{8,6},{10,8},{12,10},{14,12},{16,14},{18,... | collective-permute-start | bytes 3080 | tf_op jit(solution)/shard_map/ppermute | solution.py:16
  378.3 52.8 %collective-permute-start.4 = (f32[1,256]{1,0:T(1,128)S(1)}, f32[1,256]{1,0:T(1,128)S(1)}, u32[]{:S(2)}, u32[]{:S(2)}) collective-permute-start(f32[1,256]{1,0:T(1,128)S(1)} %slice.84), channel_id=1, source_target_pairs={{0,2},{2,4},{4,6},{6,8},{8,10},{10,12},{12,14},{14,16},{16,18},{18... | collective-permute-start | bytes 3080 | tf_op jit(solution)/shard_map/ppermute | solution.py:16
  428.4 71.0 %reduce-scatter.11.cloned.1.call-start = ((), (), s32[]{:S(2)}) async-start(), calls=%async_computation.7 | async-start | bytes 98304 | tf_op jit(solution)/shard_map/reduce_scatter | solution.py:146
  439.1 50.5 %collective-permute-start.5 = (f32[1,256]{1,0:T(1,128)S(1)}, f32[1,256]{1,0:T(1,128)S(1)}, u32[]{:S(2)}, u32[]{:S(2)}) collective-permute-start(f32[1,256]{1,0:T(1,128)S(1)} %slice.87), channel_id=1, source_target_pairs={{0,30},{2,0},{4,2},{6,4},{8,6},{10,8},{12,10},{14,12},{16,14},{18,... | collective-permute-start | bytes 3080 | tf_op jit(solution)/shard_map/ppermute | solution.py:16
Sparse Core Ops, SparseCore 0:
  19.3 11.5 reduce-scatter.4
  285.7 7.3 reduce-scatter.6
  428.6 6.6 reduce-scatter.8
  489.3 10.0 reduce-scatter.10
where the time goes:
time: 509 us; the launch traced here: 508 us
  blocking collectives  323 us (63%)
  local copies, waits for them, and re-layouts  85.8 us (17%)
  between operations  35.9 us (7%)
  matrix products  23.3 us (5%)
  other arithmetic  18.4 us (4%)
  waiting for transfers between devices  13.5 us (3%)
  starting transfers between devices  7.73 us (2%)
    psum x4, blocking collectives, to_owners(): summed = lax.psum(partial_value, 'hours')  134 us
    psum x3, blocking collectives, body(): dual_sum = lax.psum(dual_sq, ('hours', 'region'))  111 us
    all_gather x3, blocking collectives, spread_columns(): return lax.all_gather(capacity_bar, 'hours', axis=0, tiled=True)  58.5 us
    gather x3, local copies, waits for them, and re-layouts, body(): cap_dense = capacity_all[inverse].reshape(tech_count, node_count)  35.3 us
    gather x3, local copies, waits for them, and re-layouts, body(): jnp.sum(availability * cap_duals, axis=0).reshape(-1)[owner_cols]  35.3 us
    all_gather x4, blocking collectives, body(): lax.all_gather(prices, 'region', axis=1, tiled=True)  19.9 us
    reduce_scatter x4, waiting for transfers between devices, body(): lax.psum_scatter(per_dest, 'region', scatter_dimension=1, tiled=True)  13.4 us
    gather x1, local copies, waits for them, and re-layouts, body(): jnp.sum(availability, axis=0).reshape(-1)[owner_cols]  11.8 us
  transfers between devices with their start and end apart: 10, of which 3 were waited for; matrix products, arithmetic and copies ran while one was open for 20% of the time, Pallas kernels for 0%

commit v1 on v0

v1 whole, which is shorter than its diff:
```python
import functools

import jax
import jax.numpy as jnp
from jax import lax
from jax.experimental import pallas as pl
from jax.experimental.pallas import tpu as pltpu
from jax.sharding import PartitionSpec as P

ITERS = 4
EPSILON = 1e-06
LANES = 128
VMEM_BYTES = 24 * 1024 * 1024


def round_up(value, multiple):
    return (value + multiple - 1) // multiple * multiple


def split3(value):
    high = value.astype(jnp.bfloat16)
    rest = value - high.astype(jnp.float32)
    middle = rest.astype(jnp.bfloat16)
    low = (rest - middle.astype(jnp.float32)).astype(jnp.bfloat16)
    return jnp.concatenate([high, middle, low], axis=0)


def dot3(value, matrix, transposed):
    rows = value.shape[0]
    contract = ((1,), (1 if transposed else 0,))
    product = lax.dot_general(
        split3(value), matrix, (contract, ((), ())), preferred_element_type=jnp.float32
    )
    return product[:rows] + product[rows : 2 * rows] + product[2 * rows :]


def row_sum(value):
    return jnp.sum(value, axis=0, keepdims=True)


def fold_lanes(row):
    total = row[:, :LANES]
    for start in range(LANES, row.shape[1], LANES):
        total = total + row[:, start : start + LANES]
    return total


def owned_one_hots(owner_ref, tech_count, node_count):
    owned = owner_ref[pl.ds(lax.axis_index("hours"), 1), :]
    shape_t = (tech_count, owned.shape[1])
    shape_n = (node_count, owned.shape[1])
    tech = lax.broadcasted_iota(jnp.int32, shape_t, 0) == owned // node_count
    node = lax.broadcasted_iota(jnp.int32, shape_n, 0) == owned % node_count
    return tech, node.astype(jnp.float32).astype(jnp.bfloat16)


def setup_kernel(
    sizes,
    avail_ref,
    price_ref,
    cost_ref,
    owner_ref,
    ends_ref,
    limit_ref,
    pairs_ref,
    avail_t_ref,
    sums_ref,
    region_ref,
):
    hours, regions, rows, techs, nodes, slots = sizes
    width = slots // regions
    own = lax.axis_index("region")
    total = jnp.zeros((techs, nodes), jnp.float32)
    for hour in range(rows):
        total = total + avail_ref[hour * techs : (hour + 1) * techs, :]
    for tech in range(techs):
        avail_t_ref[tech] = avail_ref[pl.ds(tech, rows, stride=techs), :]
    tech_hot, node_hot = owned_one_hots(owner_ref, techs, nodes)
    costs = jnp.where(tech_hot, cost_ref[...], 0.0)
    sums_ref[:techs, :] = total
    sums_ref[techs : 2 * techs, :] = dot3(costs, node_hot, True)
    slot = lax.broadcasted_iota(jnp.int32, (1, slots), 1)
    pair = slot // width
    in_use = jnp.zeros((1, slots), jnp.int32)
    for target in range(regions):
        in_use = jnp.where(pair == target, pairs_ref[0, target], in_use)
    bound = jnp.where(slot % width < in_use, limit_ref[...], 0.0)
    start = ends_ref[0:1, :] + own * nodes
    end = ends_ref[1:2, :] + pair * nodes
    info = jnp.concatenate(
        [start.astype(jnp.float32), end.astype(jnp.float32), bound, jnp.zeros((13, slots), jnp.float32)],
        axis=0,
    )
    place = lax.broadcasted_iota(jnp.int32, (slots, regions * slots), 1) == (
        own * slots + lax.broadcasted_iota(jnp.int32, (slots, regions * slots), 0)
    )
    info = dot3(info, place.astype(jnp.float32).astype(jnp.bfloat16), False)
    region_ref[:rows, :] = price_ref[...]
    for chunk in range(regions * slots // LANES):
        region_ref[rows + 8 * chunk : rows + 8 * chunk + 8, :] = info[
            :8, chunk * LANES : (chunk + 1) * LANES
        ]


def sweep_kernel(sizes, iteration, names_in, names_out, *refs):
    hours, regions, rows, techs, nodes, slots = sizes
    first = iteration == 0
    last = iteration == ITERS - 1
    given = dict(zip(names_in, refs[: len(names_in)]))
    gives = dict(zip(names_out, refs[len(names_in) :]))
    own = lax.axis_index("region")
    hour_index = lax.axis_index("hours")
    received, gathered = given["received"], given["gathered"]

    sums = received[0]
    for sender in range(1, hours):
        sums = sums + received[sender]
    if first:
        weight = jnp.ones((1, 1), jnp.float32)
        col_weight, cost = sums[:techs], sums[techs : 2 * techs]
        gives["col_weight"][...] = col_weight
        gives["cost"][...] = cost
        chunks = []
        for chunk in range(regions * slots // LANES):
            part = gathered[0, rows + 8 * chunk : rows + 8 * chunk + 8, :]
            for region in range(1, regions):
                part = part + gathered[region, rows + 8 * chunk : rows + 8 * chunk + 8, :]
            chunks.append(part)
        info = jnp.concatenate(chunks, axis=1) if len(chunks) > 1 else chunks[0]
        base = own * nodes
        line_ends, stores = given["line_ends"][...], given["store_node"][...]
        start = jnp.concatenate(
            [line_ends[0:1] + base, jnp.full_like(stores, -1), info[0:1].astype(jnp.int32)], axis=1
        )
        end = jnp.concatenate(
            [line_ends[1:2] + base, stores + base, info[1:2].astype(jnp.int32)], axis=1
        )
        limits = jnp.concatenate(
            [given["line_limit"][...], given["store_power"][...], info[2:3]], axis=1
        )
        node = lax.broadcasted_iota(jnp.int32, (regions * nodes, start.shape[1]), 0)
        maps = (node == end).astype(jnp.float32) - (node == start).astype(jnp.float32)
        gives["maps"][...] = maps.astype(jnp.bfloat16)
        gives["limits"][...] = limits
        maps_ref = gives["maps"]
    else:
        maps_ref = given["maps"]
        limits = given["limits"][...]
        col_weight, cost = given["col_weight"][...], given["cost"][...]
        squares = jnp.sum(sums[techs : techs + 2], axis=1, keepdims=True)
        weight = given["weight"][...][:, :1]
        weight = jnp.sqrt(
            weight * jnp.sqrt((squares[1:2] + EPSILON) / (squares[0:1] + EPSILON))
        )
    primal_step = 0.5 / weight
    lines = sizes_lines(maps_ref, regions, slots, given["store_energy"].shape[1])
    units = given["store_energy"].shape[1]
    energy = given["store_energy"][...]

    prices_all = jnp.concatenate([gathered[region, :rows, :] for region in range(regions)], axis=1)
    prices = gathered[own, :rows, :]
    difference = dot3(prices_all, maps_ref[...], False)

    if first:
        capacity_new = jnp.maximum(-cost / (weight * col_weight), 0.0)
        capacity_bar = 2.0 * capacity_new
        capacity_change = capacity_new
    else:
        capacity = given["capacity"][...]
        capacity_new = jnp.maximum(
            capacity - (cost - sums[:techs]) / (weight * col_weight), 0.0
        )
        capacity_bar = 2.0 * capacity_new - capacity
        capacity_change = capacity_new - capacity

    row_id = lax.broadcasted_iota(jnp.int32, (rows, units), 0)
    if not first:
        before = lax.rem(hour_index + hours - 1, hours)
        after = lax.rem(hour_index + 1, hours)
        halo = techs + 2
        span = units // LANES
        next_row = jnp.concatenate(
            [received[after, halo + i : halo + i + 1, :] for i in range(span)], axis=1
        )
        prev_row = jnp.concatenate(
            [received[before, halo + span + i : halo + span + i + 1, :] for i in range(span)],
            axis=1,
        )
        store_duals = given["store_duals"][...]
        next_duals = jnp.where(row_id == rows - 1, next_row, pltpu.roll(store_duals, rows - 1, 0))
        if iteration == 1:
            charge = jnp.zeros((rows, units), jnp.float32)
            charge_before = jnp.zeros((1, units), jnp.float32)
        else:
            charge = given["charge"][...]
            charge_before = given["charge_before"][...]
        charge_new = jnp.clip(charge - primal_step * (store_duals - next_duals), 0.0, energy)
        gives["charge"][...] = charge_new

    flows_new, flows_bar = [], []
    primal_row = jnp.zeros((1, LANES), jnp.float32)
    total_flows = limits.shape[1]
    for low, high in ((0, lines), (lines, lines + units), (lines + units, total_flows)):
        slope = difference[:, low:high]
        if low == lines and not first:
            slope = slope + store_duals
        bound = limits[:, low:high]
        old = None if first else given["flows"][:, low:high]
        moved = -primal_step * slope if first else old - primal_step * slope
        new = jnp.clip(moved, -bound, bound)
        flows_new.append(new)
        flows_bar.append(2.0 * new if first else 2.0 * new - old)
        if not last:
            gives["flows"][:, low:high] = new
            change = row_sum((new if first else new - old) ** 2)
            if low == lines + units:
                slot = lax.broadcasted_iota(jnp.int32, change.shape, 1)
                change = jnp.where(slot // slots == own, change, 0.0)
            primal_row = primal_row + fold_lanes(change)
    maps_own = maps_ref[pl.ds(pl.multiple_of(own * nodes, nodes), nodes), :]
    balance = dot3(jnp.concatenate(flows_bar, axis=1), maps_own, True) - given["demand"][...]

    gen_cost = given["gen_cost"][...]
    half_weight = weight / 2.0
    primal_acc = jnp.zeros((rows, nodes), jnp.float32)
    dual_acc = jnp.zeros((rows, nodes), jnp.float32)
    for tech in range(techs):
        slope = gen_cost[tech : tech + 1] + prices
        if first:
            dispatch_new = jnp.maximum(-primal_step * slope, 0.0)
            dispatch_bar = 2.0 * dispatch_new
        else:
            duals = given["cap_duals"][tech]
            dispatch = given["dispatch"][tech]
            dispatch_new = jnp.maximum(dispatch - primal_step * (slope + duals), 0.0)
            dispatch_bar = 2.0 * dispatch_new - dispatch
        balance = balance + dispatch_bar
        if last:
            gives["dispatch"][pl.ds(tech, rows, stride=techs), :] = dispatch_new
            continue
        gives["dispatch"][tech] = dispatch_new
        avail = given["availability"][tech]
        cap_rows = dispatch_bar - avail * capacity_bar[tech : tech + 1]
        if first:
            primal_acc = primal_acc + dispatch_new * dispatch_new
            duals_new = jnp.maximum(half_weight * cap_rows, 0.0)
            dual_acc = dual_acc + duals_new * duals_new
        else:
            primal_acc = primal_acc + (dispatch_new - dispatch) ** 2
            duals_new = jnp.maximum(duals + half_weight * cap_rows, 0.0)
            dual_acc = dual_acc + (duals_new - duals) ** 2
        gives["cap_duals"][tech] = duals_new
        gives["sums"][tech : tech + 1, :] = row_sum(avail * duals_new)

    step_up = weight / (techs + 8.0) * balance
    if last:
        gives["prices"][...] = prices + step_up
        tech_hot, node_hot = owned_one_hots(given["owner"], techs, nodes)
        chosen = dot3(capacity_new, node_hot, False)
        gives["capacity"][...] = row_sum(jnp.where(tech_hot, chosen, 0.0))
        return
    gives["region"][:rows, :] = prices + step_up
    gives["weight"][...] = jnp.broadcast_to(weight, (1, LANES))
    gives["capacity"][...] = capacity_new
    dual_row = row_sum(dual_acc + step_up * step_up)
    primal_row = primal_row + row_sum(primal_acc)
    primal_row = primal_row + jnp.where(hour_index == 0, row_sum(capacity_change**2), 0.0)

    discharge_bar = flows_bar[1]
    if first:
        store_step = weight / 3.0 * discharge_bar
        store_new = store_step
    else:
        charge_bar = 2.0 * charge_new - charge
        before_new = jnp.clip(
            charge_before - primal_step * (prev_row - store_duals[0:1]), 0.0, energy
        )
        gives["charge_before"][...] = before_new
        before_bar = 2.0 * before_new - charge_before
        shifted = jnp.where(row_id == 0, before_bar, pltpu.roll(charge_bar, 1, 0))
        store_step = weight / 3.0 * (charge_bar - shifted + discharge_bar)
        store_new = store_duals + store_step
        primal_row = primal_row + fold_lanes(row_sum((charge_new - charge) ** 2))
    gives["store_duals"][...] = store_new
    dual_row = dual_row + fold_lanes(row_sum(store_step * store_step))
    gives["region"][rows : rows + 8, :] = jnp.concatenate(
        [primal_row, dual_row, jnp.zeros((6, LANES), jnp.float32)], axis=0
    )
    halo = techs + 2
    span = units // LANES
    gives["sums"][techs:halo, :] = jnp.concatenate([primal_row, dual_row], axis=0)
    for i in range(span):
        gives["sums"][halo + i : halo + i + 1, :] = store_new[:1, i * LANES : (i + 1) * LANES]
        gives["sums"][halo + span + i : halo + span + i + 1, :] = store_new[
            rows - 1 :, i * LANES : (i + 1) * LANES
        ]
    for row in range(halo + 2 * span, gives["sums"].shape[0]):
        gives["sums"][row : row + 1, :] = jnp.zeros((1, LANES), jnp.float32)


def sizes_lines(maps_ref, regions, slots, units):
    return maps_ref.shape[1] - units - regions * slots


def call(kernel, arguments, shapes, in_smem=()):
    return pl.pallas_call(
        kernel,
        out_shape=shapes,
        in_specs=[
            pl.BlockSpec(memory_space=pltpu.SMEM if i in in_smem else pltpu.VMEM)
            for i in range(len(arguments))
        ],
        out_specs=[pl.BlockSpec(memory_space=pltpu.VMEM)] * len(shapes),
        compiler_params=pltpu.CompilerParams(vmem_limit_bytes=VMEM_BYTES),
    )(*arguments)


def to_all_hours(message):
    count = lax.axis_size("hours")
    copies = jnp.broadcast_to(message[None], (count, *message.shape))
    return lax.all_to_all(copies, "hours", split_axis=0, concat_axis=0)


def body(
    availability,
    demand,
    gen_cost,
    cap_cost,
    owner_map,
    line_ends,
    line_limit,
    cross_ends,
    cross_limit,
    pair_counts,
    store_node,
    store_energy,
    store_power,
    price_start,
):
    rows, techs, nodes = availability.shape
    hours, regions = lax.axis_size("hours"), lax.axis_size("region")
    slots = cross_limit.shape[1]
    owned = cap_cost.shape[1]
    units, lines = store_node.shape[0], line_limit.shape[0]
    total_flows = lines + units + regions * slots
    info_rows = 8 * (regions * slots // LANES)
    sizes = (hours, regions, rows, techs, nodes, slots)
    owner_rows = owner_map.reshape(hours, owned)
    energy = store_energy[None]

    def shape(*dims, dtype=jnp.float32):
        return jax.ShapeDtypeStruct(dims, dtype)

    avail_t, message, to_regions = call(
        functools.partial(setup_kernel, sizes),
        (
            availability.reshape(rows * techs, nodes),
            price_start,
            cap_cost,
            owner_rows,
            cross_ends[:, 0],
            cross_limit,
            pair_counts,
        ),
        (shape(techs, rows, nodes), shape(2 * techs, nodes), shape(rows + info_rows, nodes)),
        in_smem=(6,),
    )
    gathered = lax.all_gather(to_regions, "region")
    received = to_all_hours(message)
    state = {
        "availability": avail_t,
        "demand": demand,
        "gen_cost": gen_cost,
        "store_energy": energy,
    }
    message_rows = round_up(techs + 2 + 2 * (units // LANES), 8)
    kept = {
        "dispatch": shape(techs, rows, nodes),
        "cap_duals": shape(techs, rows, nodes),
        "flows": shape(rows, total_flows),
        "store_duals": shape(rows, units),
        "capacity": shape(techs, nodes),
        "weight": shape(1, LANES),
        "region": shape(rows + 8, nodes),
        "sums": shape(message_rows, nodes),
    }
    charges = {"charge": shape(rows, units), "charge_before": shape(1, units)}
    for iteration in range(ITERS):
        given = dict(state, received=received, gathered=gathered)
        if iteration == 0:
            given.update(
                line_ends=line_ends,
                line_limit=line_limit[None],
                store_node=store_node[None],
                store_power=store_power[None],
            )
            outs = dict(
                kept,
                col_weight=shape(techs, nodes),
                cost=shape(techs, nodes),
                maps=shape(regions * nodes, total_flows, dtype=jnp.bfloat16),
                limits=shape(1, total_flows),
            )
        elif iteration < ITERS - 1:
            outs = dict(kept, **charges)
        else:
            given["owner"] = owner_rows
            outs = {
                "dispatch": shape(rows * techs, nodes),
                "capacity": shape(1, owned),
                "prices": shape(rows, nodes),
                "charge": shape(rows, units),
            }
        values = call(
            functools.partial(sweep_kernel, sizes, iteration, tuple(given), tuple(outs)),
            tuple(given.values()),
            tuple(outs.values()),
        )
        results = dict(zip(outs, values))
        if iteration == ITERS - 1:
            break
        to_regions, message = results.pop("region"), results.pop("sums")
        gathered = lax.all_gather(to_regions, "region")
        squares = jnp.sum(gathered[:, rows : rows + 2], axis=0)
        received = to_all_hours(message.at[techs : techs + 2].set(squares))
        state.update(results)
    return (
        results["dispatch"].reshape(rows, techs, nodes),
        results["capacity"],
        results["prices"],
        results["charge"],
    )


def solution(mesh):
    placed = (
        P("hours", None, "region"),
        P("hours", "region"),
        P(None, "region"),
        P("region", "hours"),
        P("region", None),
        P(None, "region"),
        P("region"),
        P(None, "region", None),
        P("region", None),
        P("region", None),
        P("region"),
        P("region"),
        P("region"),
        P("hours", "region"),
    )
    return jax.shard_map(
        body,
        mesh=mesh,
        in_specs=placed,
        out_specs=(
            P("hours", None, "region"),
            P("region", "hours"),
            P("hours", "region"),
            P("hours", "region"),
        ),
        check_vma=False,
    )
```

time: 509 us -> 77.5 us (0.15)
  blocking collectives: 323 us -> 53.6 us
  local copies, waits for them, and re-layouts: 85.8 us -> 5.39 us
  between operations: 35.9 us -> 0.77 us
  matrix products: 23.3 us -> 0 us
  other arithmetic: 18.4 us -> 0.03 us
  waiting for transfers between devices: 13.5 us -> 5.23 us
    psum x7 -> x0, blocking collectives: 245 us -> none  [the longest x4 134 us: to_owners(): summed = lax.psum(partial_value, 'hours')]
    gather x7 -> x0, local copies, waits for them, and re-layouts: 82.4 us -> none  [the longest x3 35.3 us: body(): cap_dense = capacity_all[inverse].reshape(tech_count, node_count)]
    all_gather x7 -> x4, blocking collectives: 78.4 us -> 18.7 us  [body(): gathered = lax.all_gather(to_regions, 'region')]
    all_to_all x0 -> x3, blocking collectives: none -> 35 us  [to_all_hours(): return lax.all_to_all(copies, 'hours', split_axis=0, concat_axis=0)]
    dot_general x32 -> x0, matrix products: 23.3 us -> none  [the longest x4 3.97 us: body(): jnp.dot(cross_bar, leave_map, precision=highest)]
    reduce_scatter x4 -> x0, waiting for transfers between devices: 13.4 us -> none  [body(): lax.psum_scatter(per_dest, 'region', scatter_dimension=1, tiled=True)]
    reduce_sum x12 -> x3, other arithmetic: 10 us -> 0.03 us  [body(): squares = jnp.sum(gathered[:, rows:rows + 2], axis=0)]
    ppermute x6 -> x0, starting transfers between devices: 7.57 us -> none  [shifted(): return lax.ppermute(value, axis, pairs)]
  transfers between devices with their start and end apart: 10 -> 1, of which waited for: 3 -> 1; matrix products, arithmetic and copies ran while one was open for 20% -> 0% of each run, Pallas kernels for 0% -> 0%
where the time goes in v1:
time: 77.5 us; the launch traced here: 76.9 us
  blocking collectives  53.6 us (69%)
  starting transfers between devices  7.36 us (9%)
  local copies, waits for them, and re-layouts  5.39 us (7%)
  waiting for transfers between devices  5.23 us (7%)
  Pallas kernels  4.48 us (6%)
    all_to_all x3, blocking collectives, to_all_hours(): return lax.all_to_all(copies, 'hours', split_axis=0, concat_axis=0)  35 us
    all_gather x4, blocking collectives, body(): gathered = lax.all_gather(to_regions, 'region')  18.7 us
    all_to_all x1, starting transfers between devices, to_all_hours(): return lax.all_to_all(copies, 'hours', split_axis=0, concat_axis=0)  7.36 us
    all_to_all x1, waiting for transfers between devices, to_all_hours(): return lax.all_to_all(copies, 'hours', split_axis=0, concat_axis=0)  5.23 us
    unnamed x30, local copies, waits for them, and re-layouts  4.56 us
    pallas_call x5, Pallas kernels, call(): pl.pallas_call(kernel, out_shape=shapes, in_specs=[pl.BlockSpec(memory_sp...  4.48 us
  transfers between devices with their start and end apart: 1, of which 1 were waited for; matrix products, arithmetic and copies ran while one was open for 0% of the time, Pallas kernels for 0%

profile of v1, /device:TPU:0, one launch (start us, length us, event | category | flops | bytes accessed | tf_op | source)
XLA Modules:
  0.0 76.9 jit_solution(1458090282444441727)
XLA Ops:
  0.6 0.0 copy-start.13
  0.6 0.0 copy-start.14
  0.7 0.0 copy-start.11
  0.7 0.0 copy-start.12
  0.7 0.6 copy-done.13
  1.3 0.0 copy-done.14
  1.3 0.0 copy-done.11
  1.3 0.0 copy-done.12
  1.3 0.0 copy-start.1
  1.3 1.0 %copy-done.1 = f32[64,16,128]{2,1,0:T(8,128)S(1)} copy-done((f32[64,16,128]{2,1,0:T(8,128)S(1)}, f32[64,16,128]{2,1,0:T(8,128)}, u32[]{:S(2)}) %copy-start.1) | copy-done | bytes 524312
  2.4 0.0 copy-start.3
  2.4 0.7 copy-done.3
  3.1 0.0 copy-start.5
  3.1 0.8 copy-done.5
  3.8 0.9 %shard_map.165 = (f32[16,64,128]{2,1,0:T(8,128)S(1)}, f32[32,128]{1,0:T(8,128)S(1)}, f32[72,128]{1,0:T(8,128)S(1)}) custom-call(f32[1024,128]{1,0:T(8,128)S(1)} %bitcast.12, f32[64,128]{1,0:T(8,128)S(1)} %copy-done.5, f32[1,128]{1,0:T(1,128)S(1)} %copy-done.12, s32[16,128]{1,0:T(8,128)S(1)} %bitcast.20, s32[2,64]{1,0:T(2,128)S(1)} %bitcast.29, ...), custom_call_target="tpu_custom_call" | custom-call | tf_op jit(solution)/shard_map/pallas_call | solution.py:306
  4.7 0.8 broadcast_in_dim.17
  5.5 7.4 %all-to-all-start = ((f32[16,32,128]{2,1,0:T(8,128)}), f32[16,32,128]{2,1,0:T(8,128)S(1)}, u32[]{:S(2)}, u32[]{:S(2)}) async-start(f32[16,32,128]{2,1,0:T(8,128)} %broadcast_in_dim.17), calls=%async_computation | async-start | bytes 524288 | tf_op jit(solution)/shard_map/all_to_all | solution.py:321
  12.8 0.0 copy-start
  12.8 0.0 copy-start.8
  12.9 0.0 copy-start.9
  12.9 0.0 copy-start.10
  12.9 4.8 %all-gather = f32[144,128]{1,0:T(8,128)S(1)} all-gather(f32[72,128]{1,0:T(8,128)S(1)} %get-tuple-element.81), channel_id=2, replica_groups=mesh['hours'=16,'region'=2] {'region'}, dimensions={0}, use_global_device_ids=true | all-gather | bytes 110592 | tf_op jit(solution)/shard_map/all_gather | solution.py:368
  17.6 0.0 copy-start.2
  17.6 5.2 %all-to-all-done.refs_4_ = f32[16,32,128]{2,1,0:T(8,128)S(1)} async-done(((f32[16,32,128]{2,1,0:T(8,128)}), f32[16,32,128]{2,1,0:T(8,128)S(1)}, u32[]{:S(2)}, u32[]{:S(2)}) %all-to-all-start) | async-done | bytes 262176 | tf_op jit(solution)/shard_map/all_to_all | solution.py:321
  22.9 0.0 copy-start.7
  22.9 0.0 copy-start.6
  22.9 0.0 copy-done
  22.9 0.0 copy-done.8
  22.9 0.0 copy-done.9
  22.9 0.0 copy-done.10
  22.9 0.0 copy-done.2
  22.9 0.6 copy-done.7
  23.6 0.0 copy-done.6
  23.6 0.7 shard_map.166
  24.3 4.6 %all-gather.1 = f32[144,128]{1,0:T(8,128)S(1)} all-gather(f32[72,128]{1,0:T(8,128)S(1)} %get-tuple-element.93), channel_id=3, replica_groups=mesh['hours'=16,'region'=2] {'region'}, dimensions={0}, use_global_device_ids=true | all-gather | bytes 110592 | tf_op jit(solution)/shard_map/all_gather | solution.py:423
  29.0 11.8 %all_to_all.20.refs_14_ = f32[16,24,128]{2,1,0:T(8,128)S(1)} all-to-all(f32[16,24,128]{2,1,0:T(8,128)S(1)} %broadcast_in_dim.41), channel_id=1, replica_groups=mesh['hours'=16,'region'=2] {'hours'}, dimensions={0} | all-to-all | bytes 393216 | tf_op jit(solution)/shard_map/all_to_all | solution.py:321
  40.7 0.8 %shard_map.167 = (f32[16,64,128]{2,1,0:T(8,128)S(1)}, f32[16,64,128]{2,1,0:T(8,128)S(1)}, f32[64,640]{1,0:T(8,128)S(1)}, f32[64,256]{1,0:T(8,128)S(1)}, f32[16,1...) custom-call(f32[16,64,128]{2,1,0:T(8,128)S(1)} %get-tuple-element.79, ...), custom_call_target="tpu_custom_call" | custom-call | tf_op jit(solution)/shard_map/pallas_call | solution.py:306
  41.5 4.6 %all-gather.2 = f32[144,128]{1,0:T(8,128)S(1)} all-gather(f32[72,128]{1,0:T(8,128)S(1)} %get-tuple-element.103), channel_id=4, replica_groups=mesh['hours'=16,'region'=2] {'region'}, dimensions={0}, use_global_device_ids=true | all-gather | bytes 110592 | tf_op jit(solution)/shard_map/all_gather | solution.py:423
  46.2 11.6 %all_to_all.21.refs_16_ = f32[16,24,128]{2,1,0:T(8,128)S(1)} all-to-all(f32[16,24,128]{2,1,0:T(8,128)S(1)} %broadcast_in_dim.42), channel_id=1, replica_groups=mesh['hours'=16,'region'=2] {'hours'}, dimensions={0} | all-to-all | bytes 393216 | tf_op jit(solution)/shard_map/all_to_all | solution.py:321
  57.8 0.8 %shard_map.168 = (f32[16,64,128]{2,1,0:T(8,128)S(1)}, f32[16,64,128]{2,1,0:T(8,128)S(1)}, f32[64,640]{1,0:T(8,128)S(1)}, f32[64,256]{1,0:T(8,128)S(1)}, f32[16,1...) custom-call(f32[16,64,128]{2,1,0:T(8,128)S(1)} %get-tuple-element.79, ...), custom_call_target="tpu_custom_call" | custom-call | tf_op jit(solution)/shard_map/pallas_call | solution.py:306
  58.6 4.6 %all-gather.3 = f32[144,128]{1,0:T(8,128)S(1)} all-gather(f32[72,128]{1,0:T(8,128)S(1)} %get-tuple-element.113), channel_id=5, replica_groups=mesh['hours'=16,'region'=2] {'region'}, dimensions={0}, use_global_device_ids=true | all-gather | bytes 110592 | tf_op jit(solution)/shard_map/all_gather | solution.py:423
  63.2 11.6 %all_to_all.22.refs_16_ = f32[16,24,128]{2,1,0:T(8,128)S(1)} all-to-all(f32[16,24,128]{2,1,0:T(8,128)S(1)} %broadcast_in_dim.43), channel_id=1, replica_groups=mesh['hours'=16,'region'=2] {'hours'}, dimensions={0} | all-to-all | bytes 393216 | tf_op jit(solution)/shard_map/all_to_all | solution.py:321
  74.8 0.0 copy-start.4
  74.8 0.7 copy-done.4
  75.5 1.4 %shard_map.169 = (f32[1024,128]{1,0:T(8,128)}, f32[1,128]{1,0:T(1,128)}, f32[64,128]{1,0:T(8,128)}, f32[64,256]{1,0:T(8,128)}) custom-call(f32[16,64,128]{2,1,0:T(8,128)S(1)} %get-tuple-element.79.refs_0_, f32[64,128]{1,0:T(8,128)S(1)} %copy-done, f32[16,128]{1,0:T(8,128)S(1)} %copy-done.2, f32[1,256]{1,0:T(1,128)S(1)} %bitcast.25, ...), custom_call_target="tpu_custom_call" | custom-call | tf_op jit(solution)/shard_map/pallas_call | solution.py:306
  (9 shorter events, 0.1 us)
Async XLA Ops:
  0.6 0.7 copy-start.13
  0.6 0.7 copy-start.14
  0.7 0.7 copy-start.11
  0.7 0.7 copy-start.12
  1.3 1.0 %copy-start.1 = (f32[64,16,128]{2,1,0:T(8,128)S(1)}, f32[64,16,128]{2,1,0:T(8,128)}, u32[]{:S(2)}) copy-start(f32[64,16,128]{2,1,0:T(8,128)} %param.20) | copy-start | bytes 1572868
  2.4 0.7 copy-start.3
  3.1 0.8 copy-start.5
  5.5 17.4 %all-to-all-start = ((f32[16,32,128]{2,1,0:T(8,128)}), f32[16,32,128]{2,1,0:T(8,128)S(1)}, u32[]{:S(2)}, u32[]{:S(2)}) async-start(f32[16,32,128]{2,1,0:T(8,128)} %broadcast_in_dim.17), calls=%async_computation | async-start | bytes 524288 | tf_op jit(solution)/shard_map/all_to_all | solution.py:321
  12.8 10.1 %copy-start = (f32[64,128]{1,0:T(8,128)S(1)}, f32[64,128]{1,0:T(8,128)}, u32[]{:S(2)}) copy-start(f32[64,128]{1,0:T(8,128)} %refs_1_.7) | copy-start | bytes 98308
  12.8 10.0 %copy-start.8 = (f32[256]{0:T(256)S(1)}, f32[256]{0:T(256)}, u32[]{:S(2)}) copy-start(f32[256]{0:T(256)} %param.26) | copy-start | bytes 3076
  12.9 10.0 %copy-start.9 = (s32[256]{0:T(256)S(1)}, s32[256]{0:T(256)}, u32[]{:S(2)}) copy-start(s32[256]{0:T(256)} %param.30) | copy-start | bytes 3076
  12.9 10.0 %copy-start.10 = (f32[256]{0:T(256)S(1)}, f32[256]{0:T(256)}, u32[]{:S(2)}) copy-start(f32[256]{0:T(256)} %param.32) | copy-start | bytes 3076
  17.6 5.3 %copy-start.2 = (f32[16,128]{1,0:T(8,128)S(1)}, f32[16,128]{1,0:T(8,128)}, u32[]{:S(2)}) copy-start(f32[16,128]{1,0:T(8,128)} %refs_2_.7) | copy-start | bytes 24580
  22.9 0.7 copy-start.7
  22.9 0.7 copy-start.6
  74.8 0.7 copy-start.4

commit v2 on v1

--- a/solution.py
+++ b/solution.py
@@ -11,10 +11,6 @@
 EPSILON = 1e-06
 LANES = 128
 VMEM_BYTES = 24 * 1024 * 1024
-
-
-def round_up(value, multiple):
-    return (value + multiple - 1) // multiple * multiple
 
 
 def split3(value):
@@ -110,11 +106,8 @@
     gives = dict(zip(names_out, refs[len(names_in) :]))
     own = lax.axis_index("region")
     hour_index = lax.axis_index("hours")
-    received, gathered = given["received"], given["gathered"]
-
-    sums = received[0]
-    for sender in range(1, hours):
-        sums = sums + received[sender]
+    gathered = given["gathered"]
+    sums = given["totals"][...]
     if first:
         weight = jnp.ones((1, 1), jnp.float32)
         col_weight, cost = sums[:techs], sums[techs : 2 * techs]
@@ -175,17 +168,9 @@
 
     row_id = lax.broadcasted_iota(jnp.int32, (rows, units), 0)
     if not first:
-        before = lax.rem(hour_index + hours - 1, hours)
-        after = lax.rem(hour_index + 1, hours)
-        halo = techs + 2
         span = units // LANES
-        next_row = jnp.concatenate(
-            [received[after, halo + i : halo + i + 1, :] for i in range(span)], axis=1
-        )
-        prev_row = jnp.concatenate(
-            [received[before, halo + span + i : halo + span + i + 1, :] for i in range(span)],
-            axis=1,
-        )
+        next_row = jnp.concatenate([given["next_row"][i : i + 1, :] for i in range(span)], axis=1)
+        prev_row = jnp.concatenate([given["prev_row"][i : i + 1, :] for i in range(span)], axis=1)
         store_duals = given["store_duals"][...]
         next_duals = jnp.where(row_id == rows - 1, next_row, pltpu.roll(store_duals, rows - 1, 0))
         if iteration == 1:
@@ -286,16 +271,14 @@
     gives["region"][rows : rows + 8, :] = jnp.concatenate(
         [primal_row, dual_row, jnp.zeros((6, LANES), jnp.float32)], axis=0
     )
-    halo = techs + 2
     span = units // LANES
-    gives["sums"][techs:halo, :] = jnp.concatenate([primal_row, dual_row], axis=0)
+    gives["sums"][techs:, :] = jnp.concatenate(
+        [primal_row, dual_row, jnp.zeros((6, LANES), jnp.float32)], axis=0
+    )
     for i in range(span):
-        gives["sums"][halo + i : halo + i + 1, :] = store_new[:1, i * LANES : (i + 1) * LANES]
-        gives["sums"][halo + span + i : halo + span + i + 1, :] = store_new[
-            rows - 1 :, i * LANES : (i + 1) * LANES
-        ]
-    for row in range(halo + 2 * span, gives["sums"].shape[0]):
-        gives["sums"][row : row + 1, :] = jnp.zeros((1, LANES), jnp.float32)
+        part = slice(i * LANES, (i + 1) * LANES)
+        gives["first_row"][i : i + 1, :] = store_new[:1, part]
+        gives["last_row"][i : i + 1, :] = store_new[rows - 1 :, part]
 
 
 def sizes_lines(maps_ref, regions, slots, units):
@@ -315,10 +298,63 @@
     )(*arguments)
 
 
-def to_all_hours(message):
+def swap(value, hour_bit, region_bit):
+    hours, regions = lax.axis_size("hours"), lax.axis_size("region")
+    pairs = [
+        (hour * regions + region, (hour ^ hour_bit) * regions + (region ^ region_bit))
+        for hour in range(hours)
+        for region in range(regions)
+    ]
+    return lax.ppermute(value, ("hours", "region"), pairs)
+
+
+def shifted(value, steps):
     count = lax.axis_size("hours")
-    copies = jnp.broadcast_to(message[None], (count, *message.shape))
-    return lax.all_to_all(copies, "hours", split_axis=0, concat_axis=0)
+    return lax.ppermute(value, "hours", [(i, (i + steps) % count) for i in range(count)])
+
+
+def exchange(to_regions, sums, squares_at=None, first_row=None, last_row=None):
+    hours, regions = lax.axis_size("hours"), lax.axis_size("region")
+    hour, region = lax.axis_index("hours"), lax.axis_index("region")
+    sweeping = squares_at is not None
+    next_row = prev_row = None
+    if regions != 2 or hours < 4 or hours & (hours - 1):
+        gathered = lax.all_gather(to_regions, "region")
+        if sweeping:
+            rows = to_regions.shape[0] - 8
+            squares = jnp.sum(gathered[:, rows : rows + 8], axis=0)
+            sums = sums.at[squares_at:].set(squares)
+            next_row, prev_row = shifted(first_row, -1), shifted(last_row, 1)
+        return gathered, lax.psum(sums, "hours"), next_row, prev_row
+    even = hour % 2 == 0
+    message = sums
+    if sweeping:
+        message = jnp.concatenate([sums, jnp.where(even, last_row, first_row)], axis=0)
+        beside = jnp.where(even, first_row, last_row)
+        across = [
+            (h * regions + r, (h + 1 if h % 2 else h - 1) % hours * regions + r)
+            for h in range(hours)
+            for r in range(regions)
+        ]
+    partner = swap(message, 1, 0)
+    other = swap(to_regions, 0, 1)
+    count = sums.shape[0]
+    totals = sums + partner[:count]
+    if sweeping:
+        rows = to_regions.shape[0] - 8
+        diagonal = swap(sums[squares_at:], 1, 1)
+        arrived = lax.ppermute(beside, ("hours", "region"), across)
+        next_row = jnp.where(even, partner[count:], arrived)
+        prev_row = jnp.where(even, arrived, partner[count:])
+        totals = totals.at[squares_at:].add(other[rows:] + diagonal)
+    bit = 2
+    while bit < hours:
+        totals = totals + swap(totals, bit, 0)
+        bit *= 2
+    gathered = jnp.where(
+        region == 0, jnp.stack([to_regions, other]), jnp.stack([other, to_regions])
+    )
+    return gathered, totals, next_row, prev_row
 
 
 def body(
@@ -365,15 +401,13 @@
         (shape(techs, rows, nodes), shape(2 * techs, nodes), shape(rows + info_rows, nodes)),
         in_smem=(6,),
     )
-    gathered = lax.all_gather(to_regions, "region")
-    received = to_all_hours(message)
+    gathered, totals, next_row, prev_row = exchange(to_regions, message)
     state = {
         "availability": avail_t,
         "demand": demand,
         "gen_cost": gen_cost,
         "store_energy": energy,
     }
-    message_rows = round_up(techs + 2 + 2 * (units // LANES), 8)
     kept = {
         "dispatch": shape(techs, rows, nodes),
         "cap_duals": shape(techs, rows, nodes),
@@ -382,11 +416,13 @@
         "capacity": shape(techs, nodes),
         "weight": shape(1, LANES),
         "region": shape(rows + 8, nodes),
-        "sums": shape(message_rows, nodes),
+        "sums": shape(techs + 8, nodes),
+        "first_row": shape(units // LANES, LANES),
+        "last_row": shape(units // LANES, LANES),
     }
     charges = {"charge": shape(rows, units), "charge_before": shape(1, units)}
     for iteration in range(ITERS):
-        given = dict(state, received=received, gathered=gathered)
+        given = dict(state, totals=totals, gathered=gathered)
         if iteration == 0:
             given.update(
                 line_ends=line_ends,
@@ -401,9 +437,10 @@
                 maps=shape(regions * nodes, total_flows, dtype=jnp.bfloat16),
                 limits=shape(1, total_flows),
             )
-        elif iteration < ITERS - 1:
+        else:
+            given.update(next_row=next_row, prev_row=prev_row)
             outs = dict(kept, **charges)
-        else:
+        if iteration == ITERS - 1:
             given["owner"] = owner_rows
             outs = {
                 "dispatch": shape(rows * techs, nodes),
@@ -419,10 +456,13 @@
         results = dict(zip(outs, values))
         if iteration == ITERS - 1:
             break
-        to_regions, message = results.pop("region"), results.pop("sums")
-        gathered = lax.all_gather(to_regions, "region")
-        squares = jnp.sum(gathered[:, rows : rows + 2], axis=0)
-        received = to_all_hours(message.at[techs : techs + 2].set(squares))
+        gathered, totals, next_row, prev_row = exchange(
+            results.pop("region"),
+            results.pop("sums"),
+            techs,
+            results.pop("first_row"),
+            results.pop("last_row"),
+        )
         state.update(results)
     return (
         results["dispatch"].reshape(rows, techs, nodes),

time: 77.5 us -> 77 us (level)
  blocking collectives: 53.6 us -> 0 us
  starting transfers between devices: 7.36 us -> 38.2 us
  waiting for transfers between devices: 5.23 us -> 28.4 us
  local copies, waits for them, and re-layouts: 5.39 us -> 4.6 us
    ppermute x0 -> x26, starting transfers between devices: none -> 38.2 us  [the longest x23 32.5 us: swap(): return lax.ppermute(value, ('hours', 'region'), pairs)]
    all_to_all x3 -> x0, blocking collectives: 35 us -> none  [to_all_hours(): return lax.all_to_all(copies, 'hours', split_axis=0, concat_axis=0)]
    ppermute x0 -> x26, waiting for transfers between devices: none -> 28.4 us  [the longest x23 22.6 us: swap(): return lax.ppermute(value, ('hours', 'region'), pairs)]
    all_gather x4 -> x0, blocking collectives: 18.7 us -> none  [body(): gathered = lax.all_gather(to_regions, 'region')]
    all_to_all x1 -> x0, starting transfers between devices: 7.36 us -> none  [to_all_hours(): return lax.all_to_all(copies, 'hours', split_axis=0, concat_axis=0)]
    all_to_all x1 -> x0, waiting for transfers between devices: 5.23 us -> none  [to_all_hours(): return lax.all_to_all(copies, 'hours', split_axis=0, concat_axis=0)]
    broadcast_in_dim x4 -> x0, local copies, waits for them, and re-layouts: 0.8 us -> none  [to_all_hours(): copies = jnp.broadcast_to(message[None], (count, *message.shape))]
  transfers between devices with their start and end apart: 1 -> 26, of which waited for: 1 -> 21; matrix products, arithmetic and copies ran while one was open for 0% -> 0% of each run, Pallas kernels for 0% -> 0%
where the time goes in v2:
time: 77 us; the launch traced here: 76.6 us
  starting transfers between devices  38.2 us (50%)
  waiting for transfers between devices  28.4 us (37%)
  local copies, waits for them, and re-layouts  4.6 us (6%)
  Pallas kernels  4.4 us (6%)
  between operations  0.88 us (1%)
    ppermute x23, starting transfers between devices, swap(): return lax.ppermute(value, ('hours', 'region'), pairs)  32.5 us
    ppermute x23, waiting for transfers between devices, swap(): return lax.ppermute(value, ('hours', 'region'), pairs)  22.6 us
    ppermute x3, waiting for transfers between devices, exchange(): arrived = lax.ppermute(beside, ('hours', 'region'), across)  5.72 us
    ppermute x3, starting transfers between devices, exchange(): arrived = lax.ppermute(beside, ('hours', 'region'), across)  5.7 us
    unnamed x30, local copies, waits for them, and re-layouts  4.6 us
    pallas_call x5, Pallas kernels, call(): pl.pallas_call(kernel, out_shape=shapes, in_specs=[pl.BlockSpec(memory_sp...  4.4 us
  transfers between devices with their start and end apart: 26, of which 21 were waited for; matrix products, arithmetic and copies ran while one was open for 0% of the time, Pallas kernels for 0%

profile of v2, /device:TPU:0, one launch (start us, length us, event | category | flops | bytes accessed | tf_op | source)
XLA Modules:
  0.0 76.6 jit_solution(8600563179284262697)
XLA Ops:
  0.7 0.6 copy-done.13
  1.3 0.0 copy-done.14
  1.3 0.0 copy-done.11
  1.3 1.0 %copy-done.1 = f32[64,16,128]{2,1,0:T(8,128)S(1)} copy-done((f32[64,16,128]{2,1,0:T(8,128)S(1)}, f32[64,16,128]{2,1,0:T(8,128)}, u32[]{:S(2)}) %copy-start.1) | copy-done | bytes 524312
  2.4 0.7 copy-done.3
  3.1 0.8 copy-done.5
  3.8 0.9 %shard_map.165 = (f32[16,64,128]{2,1,0:T(8,128)S(1)}, f32[32,128]{1,0:T(8,128)S(1)}, f32[72,128]{1,0:T(8,128)S(1)}) custom-call(f32[1024,128]{1,0:T(8,128)S(1)} %bitcast.16, f32[64,128]{1,0:T(8,128)S(1)} %copy-done.5, f32[1,128]{1,0:T(1,128)S(1)} %copy-done.12, s32[16,128]{1,0:T(8,128)S(1)} %bitcast.21, s32[2,64]{1,0:T(2,128)S(1)} %bitcast.30, ...), custom_call_target="tpu_custom_call" | custom-call | tf_op jit(solution)/shard_map/pallas_call | solution.py:289
  4.7 0.5 collective-permute-start
  5.2 2.5 %collective-permute-start.4 = (f32[72,128]{1,0:T(8,128)S(1)}, f32[72,128]{1,0:T(8,128)S(1)}, u32[]{:S(2)}, u32[]{:S(2)}) collective-permute-start(f32[72,128]{1,0:T(8,128)S(1)} %get-tuple-element.87), channel_id=1, source_target_pairs={{0,1},{1,0},{2,3},{3,2},{4,5},{5,4},{6,7},{7,6},{8,9},{9,8},{10,11... | collective-permute-start | bytes 110600 | tf_op jit(solution)/shard_map/ppermute | solution.py:308
  7.7 1.6 %collective-permute-start.1 = (f32[32,128]{1,0:T(8,128)S(1)}, f32[32,128]{1,0:T(8,128)S(1)}, u32[]{:S(2)}, u32[]{:S(2)}) collective-permute-start(f32[32,128]{1,0:T(8,128)S(1)} %add.84), channel_id=1, source_target_pairs={{0,4},{1,5},{2,6},{3,7},{4,0},{5,1},{6,2},{7,3},{8,12},{9,13},{10,... | collective-permute-start | bytes 49160 | tf_op jit(solution)/shard_map/ppermute | solution.py:308
  9.3 2.2 %collective-permute-done.1 = f32[32,128]{1,0:T(8,128)S(1)} collective-permute-done((f32[32,128]{1,0:T(8,128)S(1)}, f32[32,128]{1,0:T(8,128)S(1)}, u32[]{:S(2)}, u32[]{:S(2)}) %collective-permute-start.1) | collective-permute-done | bytes 16416 | tf_op jit(solution)/shard_map/ppermute | solution.py:308
  11.5 1.6 %collective-permute-start.2 = (f32[32,128]{1,0:T(8,128)S(1)}, f32[32,128]{1,0:T(8,128)S(1)}, u32[]{:S(2)}, u32[]{:S(2)}) collective-permute-start(f32[32,128]{1,0:T(8,128)S(1)} %add.85), channel_id=1, source_target_pairs={{0,8},{1,9},{2,10},{3,11},{4,12},{5,13},{6,14},{7,15},{8,0},{9,1},... | collective-permute-start | bytes 49160 | tf_op jit(solution)/shard_map/ppermute | solution.py:308
  13.1 2.2 %collective-permute-done.2 = f32[32,128]{1,0:T(8,128)S(1)} collective-permute-done((f32[32,128]{1,0:T(8,128)S(1)}, f32[32,128]{1,0:T(8,128)S(1)}, u32[]{:S(2)}, u32[]{:S(2)}) %collective-permute-start.2) | collective-permute-done | bytes 16416 | tf_op jit(solution)/shard_map/ppermute | solution.py:308
  15.3 2.6 %collective-permute-start.3 = (f32[32,128]{1,0:T(8,128)S(1)}, f32[32,128]{1,0:T(8,128)S(1)}, u32[]{:S(2)}, u32[]{:S(2)}) collective-permute-start(f32[32,128]{1,0:T(8,128)S(1)} %add.86), channel_id=1, source_target_pairs={{0,16},{1,17},{2,18},{3,19},{4,20},{5,21},{6,22},{7,23},{8,24},{9,... | collective-permute-start | bytes 49160 | tf_op jit(solution)/shard_map/ppermute | solution.py:308
  17.9 2.0 %collective-permute-done.3 = f32[32,128]{1,0:T(8,128)S(1)} collective-permute-done((f32[32,128]{1,0:T(8,128)S(1)}, f32[32,128]{1,0:T(8,128)S(1)}, u32[]{:S(2)}, u32[]{:S(2)}) %collective-permute-start.3) | collective-permute-done | bytes 16416 | tf_op jit(solution)/shard_map/ppermute | solution.py:308
  20.0 0.6 copy-done.7
  20.6 0.0 copy-done.8
  20.6 0.0 copy-done.9
  20.6 0.0 copy-done.10
  20.6 0.0 copy-done.2
  20.7 0.7 shard_map.166
  21.4 0.1 collective-permute-start.5
  21.5 1.2 %collective-permute-start.7 = (f32[8,128]{1,0:T(8,128)S(1)}, f32[8,128]{1,0:T(8,128)S(1)}, u32[]{:S(2)}, u32[]{:S(2)}) collective-permute-start(f32[8,128]{1,0:T(8,128)S(1)} %slice.99), channel_id=1, source_target_pairs={{0,3},{1,2},{2,1},{3,0},{4,7},{5,6},{6,5},{7,4},{8,11},{9,10},{10,... | collective-permute-start | bytes 12296 | tf_op jit(solution)/shard_map/ppermute | solution.py:308
  22.7 0.9 %collective-permute-start.6 = (f32[72,128]{1,0:T(8,128)S(1)}, f32[72,128]{1,0:T(8,128)S(1)}, u32[]{:S(2)}, u32[]{:S(2)}) collective-permute-start(f32[72,128]{1,0:T(8,128)S(1)} %get-tuple-element.101), channel_id=1, source_target_pairs={{0,1},{1,0},{2,3},{3,2},{4,5},{5,4},{6,7},{7,6},{8,9},{9,8},{10,11... | collective-permute-start | bytes 110600 | tf_op jit(solution)/shard_map/ppermute | solution.py:308
  23.6 1.0 %collective-permute-done.7 = f32[8,128]{1,0:T(8,128)S(1)} collective-permute-done((f32[8,128]{1,0:T(8,128)S(1)}, f32[8,128]{1,0:T(8,128)S(1)}, u32[]{:S(2)}, u32[]{:S(2)}) %collective-permute-start.7) | collective-permute-done | bytes 4128 | tf_op jit(solution)/shard_map/ppermute | solution.py:308
  24.6 2.1 %collective-permute-done.6 = f32[72,128]{1,0:T(8,128)S(1)} collective-permute-done((f32[72,128]{1,0:T(8,128)S(1)}, f32[72,128]{1,0:T(8,128)S(1)}, u32[]{:S(2)}, u32[]{:S(2)}) %collective-permute-start.6) | collective-permute-done | bytes 36896 | tf_op jit(solution)/shard_map/ppermute | solution.py:308
  26.7 1.5 %collective-permute-start.8 = (f32[24,128]{1,0:T(8,128)S(1)}, f32[24,128]{1,0:T(8,128)S(1)}, u32[]{:S(2)}, u32[]{:S(2)}) collective-permute-start(f32[24,128]{1,0:T(8,128)S(1)} %fusion.5), channel_id=1, source_target_pairs={{0,4},{1,5},{2,6},{3,7},{4,0},{5,1},{6,2},{7,3},{8,12},{9,13},{10,... | collective-permute-start | bytes 36872 | tf_op jit(solution)/shard_map/ppermute | solution.py:308
  28.2 1.9 %collective-permute-start.11 = (f32[2,128]{1,0:T(2,128)S(1)}, f32[2,128]{1,0:T(2,128)S(1)}, u32[]{:S(2)}, u32[]{:S(2)}) collective-permute-start(f32[2,128]{1,0:T(2,128)S(1)} %get-tuple-element.140), channel_id=1, source_target_pairs={{0,30},{1,31},{2,4},{3,5},{4,2},{5,3},{6,8},{7,9},{8,6},{9,7},{10,... | collective-permute-start | bytes 3080 | tf_op jit(solution)/shard_map/ppermute | solution.py:346
  30.0 0.3 collective-permute-done.8
  30.4 1.6 %collective-permute-start.9 = (f32[24,128]{1,0:T(8,128)S(1)}, f32[24,128]{1,0:T(8,128)S(1)}, u32[]{:S(2)}, u32[]{:S(2)}) collective-permute-start(f32[24,128]{1,0:T(8,128)S(1)} %add.92), channel_id=1, source_target_pairs={{0,8},{1,9},{2,10},{3,11},{4,12},{5,13},{6,14},{7,15},{8,0},{9,1},... | collective-permute-start | bytes 36872 | tf_op jit(solution)/shard_map/ppermute | solution.py:308
  31.9 1.9 %collective-permute-done.11 = f32[2,128]{1,0:T(2,128)S(1)} collective-permute-done((f32[2,128]{1,0:T(2,128)S(1)}, f32[2,128]{1,0:T(2,128)S(1)}, u32[]{:S(2)}, u32[]{:S(2)}) %collective-permute-start.11) | collective-permute-done | bytes 1056 | tf_op jit(solution)/shard_map/ppermute | solution.py:346
  33.9 0.2 collective-permute-done.9
  34.1 2.6 %collective-permute-start.10 = (f32[24,128]{1,0:T(8,128)S(1)}, f32[24,128]{1,0:T(8,128)S(1)}, u32[]{:S(2)}, u32[]{:S(2)}) collective-permute-start(f32[24,128]{1,0:T(8,128)S(1)} %add.93), channel_id=1, source_target_pairs={{0,16},{1,17},{2,18},{3,19},{4,20},{5,21},{6,22},{7,23},{8,24},{9,... | collective-permute-start | bytes 36872 | tf_op jit(solution)/shard_map/ppermute | solution.py:308
  36.7 1.9 %collective-permute-done.10 = f32[24,128]{1,0:T(8,128)S(1)} collective-permute-done((f32[24,128]{1,0:T(8,128)S(1)}, f32[24,128]{1,0:T(8,128)S(1)}, u32[]{:S(2)}, u32[]{:S(2)}) %collective-permute-start.10) | collective-permute-done | bytes 12320 | tf_op jit(solution)/shard_map/ppermute | solution.py:308
  38.7 0.8 shard_map.167
  39.4 0.1 collective-permute-start.12
  39.5 1.0 %collective-permute-start.14 = (f32[8,128]{1,0:T(8,128)S(1)}, f32[8,128]{1,0:T(8,128)S(1)}, u32[]{:S(2)}, u32[]{:S(2)}) collective-permute-start(f32[8,128]{1,0:T(8,128)S(1)} %slice.104), channel_id=1, source_target_pairs={{0,3},{1,2},{2,1},{3,0},{4,7},{5,6},{6,5},{7,4},{8,11},{9,10},{10,... | collective-permute-start | bytes 12296 | tf_op jit(solution)/shard_map/ppermute | solution.py:308
  40.6 1.1 %collective-permute-start.13 = (f32[72,128]{1,0:T(8,128)S(1)}, f32[72,128]{1,0:T(8,128)S(1)}, u32[]{:S(2)}, u32[]{:S(2)}) collective-permute-start(f32[72,128]{1,0:T(8,128)S(1)} %get-tuple-element.113), channel_id=1, source_target_pairs={{0,1},{1,0},{2,3},{3,2},{4,5},{5,4},{6,7},{7,6},{8,9},{9,8},{10,11... | collective-permute-start | bytes 110600 | tf_op jit(solution)/shard_map/ppermute | solution.py:308
  41.7 1.0 %collective-permute-done.14 = f32[8,128]{1,0:T(8,128)S(1)} collective-permute-done((f32[8,128]{1,0:T(8,128)S(1)}, f32[8,128]{1,0:T(8,128)S(1)}, u32[]{:S(2)}, u32[]{:S(2)}) %collective-permute-start.14) | collective-permute-done | bytes 4128 | tf_op jit(solution)/shard_map/ppermute | solution.py:308
  42.6 1.9 %collective-permute-done.13 = f32[72,128]{1,0:T(8,128)S(1)} collective-permute-done((f32[72,128]{1,0:T(8,128)S(1)}, f32[72,128]{1,0:T(8,128)S(1)}, u32[]{:S(2)}, u32[]{:S(2)}) %collective-permute-start.13) | collective-permute-done | bytes 36896 | tf_op jit(solution)/shard_map/ppermute | solution.py:308
  44.5 1.5 %collective-permute-start.15 = (f32[24,128]{1,0:T(8,128)S(1)}, f32[24,128]{1,0:T(8,128)S(1)}, u32[]{:S(2)}, u32[]{:S(2)}) collective-permute-start(f32[24,128]{1,0:T(8,128)S(1)} %fusion.3), channel_id=1, source_target_pairs={{0,4},{1,5},{2,6},{3,7},{4,0},{5,1},{6,2},{7,3},{8,12},{9,13},{10,... | collective-permute-start | bytes 36872 | tf_op jit(solution)/shard_map/ppermute | solution.py:308
  46.0 1.9 %collective-permute-start.18 = (f32[2,128]{1,0:T(2,128)S(1)}, f32[2,128]{1,0:T(2,128)S(1)}, u32[]{:S(2)}, u32[]{:S(2)}) collective-permute-start(f32[2,128]{1,0:T(2,128)S(1)} %get-tuple-element.138), channel_id=1, source_target_pairs={{0,30},{1,31},{2,4},{3,5},{4,2},{5,3},{6,8},{7,9},{8,6},{9,7},{10,... | collective-permute-start | bytes 3080 | tf_op jit(solution)/shard_map/ppermute | solution.py:346
  47.9 0.3 collective-permute-done.15
  48.2 1.6 %collective-permute-start.16 = (f32[24,128]{1,0:T(8,128)S(1)}, f32[24,128]{1,0:T(8,128)S(1)}, u32[]{:S(2)}, u32[]{:S(2)}) collective-permute-start(f32[24,128]{1,0:T(8,128)S(1)} %add.98), channel_id=1, source_target_pairs={{0,8},{1,9},{2,10},{3,11},{4,12},{5,13},{6,14},{7,15},{8,0},{9,1},... | collective-permute-start | bytes 36872 | tf_op jit(solution)/shard_map/ppermute | solution.py:308
  49.8 1.9 %collective-permute-done.18 = f32[2,128]{1,0:T(2,128)S(1)} collective-permute-done((f32[2,128]{1,0:T(2,128)S(1)}, f32[2,128]{1,0:T(2,128)S(1)}, u32[]{:S(2)}, u32[]{:S(2)}) %collective-permute-start.18) | collective-permute-done | bytes 1056 | tf_op jit(solution)/shard_map/ppermute | solution.py:346
  51.7 0.2 collective-permute-done.16
  51.9 2.7 %collective-permute-start.17 = (f32[24,128]{1,0:T(8,128)S(1)}, f32[24,128]{1,0:T(8,128)S(1)}, u32[]{:S(2)}, u32[]{:S(2)}) collective-permute-start(f32[24,128]{1,0:T(8,128)S(1)} %add.99), channel_id=1, source_target_pairs={{0,16},{1,17},{2,18},{3,19},{4,20},{5,21},{6,22},{7,23},{8,24},{9,... | collective-permute-start | bytes 36872 | tf_op jit(solution)/shard_map/ppermute | solution.py:308
  54.6 1.9 %collective-permute-done.17 = f32[24,128]{1,0:T(8,128)S(1)} collective-permute-done((f32[24,128]{1,0:T(8,128)S(1)}, f32[24,128]{1,0:T(8,128)S(1)}, u32[]{:S(2)}, u32[]{:S(2)}) %collective-permute-start.17) | collective-permute-done | bytes 12320 | tf_op jit(solution)/shard_map/ppermute | solution.py:308
  56.5 0.8 %shard_map.168 = (f32[16,64,128]{2,1,0:T(8,128)S(1)}, f32[16,64,128]{2,1,0:T(8,128)S(1)}, f32[64,640]{1,0:T(8,128)S(1)}, f32[64,256]{1,0:T(8,128)S(1)}, f32[16,1...) custom-call(f32[16,64,128]{2,1,0:T(8,128)S(1)} %get-tuple-element.85, ...), custom_call_target="tpu_custom_call" | custom-call | tf_op jit(solution)/shard_map/pallas_call | solution.py:289
  57.3 0.1 collective-permute-start.19
  57.4 1.2 %collective-permute-start.21 = (f32[8,128]{1,0:T(8,128)S(1)}, f32[8,128]{1,0:T(8,128)S(1)}, u32[]{:S(2)}, u32[]{:S(2)}) collective-permute-start(f32[8,128]{1,0:T(8,128)S(1)} %slice.109), channel_id=1, source_target_pairs={{0,3},{1,2},{2,1},{3,0},{4,7},{5,6},{6,5},{7,4},{8,11},{9,10},{10,... | collective-permute-start | bytes 12296 | tf_op jit(solution)/shard_map/ppermute | solution.py:308
  58.6 0.9 %collective-permute-start.20 = (f32[72,128]{1,0:T(8,128)S(1)}, f32[72,128]{1,0:T(8,128)S(1)}, u32[]{:S(2)}, u32[]{:S(2)}) collective-permute-start(f32[72,128]{1,0:T(8,128)S(1)} %get-tuple-element.125), channel_id=1, source_target_pairs={{0,1},{1,0},{2,3},{3,2},{4,5},{5,4},{6,7},{7,6},{8,9},{9,8},{10,11... | collective-permute-start | bytes 110600 | tf_op jit(solution)/shard_map/ppermute | solution.py:308
  59.6 1.0 %collective-permute-done.21 = f32[8,128]{1,0:T(8,128)S(1)} collective-permute-done((f32[8,128]{1,0:T(8,128)S(1)}, f32[8,128]{1,0:T(8,128)S(1)}, u32[]{:S(2)}, u32[]{:S(2)}) %collective-permute-start.21) | collective-permute-done | bytes 4128 | tf_op jit(solution)/shard_map/ppermute | solution.py:308
  60.5 2.1 %collective-permute-done.20 = f32[72,128]{1,0:T(8,128)S(1)} collective-permute-done((f32[72,128]{1,0:T(8,128)S(1)}, f32[72,128]{1,0:T(8,128)S(1)}, u32[]{:S(2)}, u32[]{:S(2)}) %collective-permute-start.20) | collective-permute-done | bytes 36896 | tf_op jit(solution)/shard_map/ppermute | solution.py:308
  62.6 1.5 %collective-permute-start.22 = (f32[24,128]{1,0:T(8,128)S(1)}, f32[24,128]{1,0:T(8,128)S(1)}, u32[]{:S(2)}, u32[]{:S(2)}) collective-permute-start(f32[24,128]{1,0:T(8,128)S(1)} %fusion.1), channel_id=1, source_target_pairs={{0,4},{1,5},{2,6},{3,7},{4,0},{5,1},{6,2},{7,3},{8,12},{9,13},{10,... | collective-permute-start | bytes 36872 | tf_op jit(solution)/shard_map/ppermute | solution.py:308
  64.1 1.9 %collective-permute-start.25 = (f32[2,128]{1,0:T(2,128)S(1)}, f32[2,128]{1,0:T(2,128)S(1)}, u32[]{:S(2)}, u32[]{:S(2)}) collective-permute-start(f32[2,128]{1,0:T(2,128)S(1)} %get-tuple-element.136), channel_id=1, source_target_pairs={{0,30},{1,31},{2,4},{3,5},{4,2},{5,3},{6,8},{7,9},{8,6},{9,7},{10,... | collective-permute-start | bytes 3080 | tf_op jit(solution)/shard_map/ppermute | solution.py:346
  66.0 0.3 collective-permute-done.22
  66.3 1.6 %collective-permute-start.23 = (f32[24,128]{1,0:T(8,128)S(1)}, f32[24,128]{1,0:T(8,128)S(1)}, u32[]{:S(2)}, u32[]{:S(2)}) collective-permute-start(f32[24,128]{1,0:T(8,128)S(1)} %add.104), channel_id=1, source_target_pairs={{0,8},{1,9},{2,10},{3,11},{4,12},{5,13},{6,14},{7,15},{8,0},{9,1},... | collective-permute-start | bytes 36872 | tf_op jit(solution)/shard_map/ppermute | solution.py:308
  67.9 1.9 %collective-permute-done.25 = f32[2,128]{1,0:T(2,128)S(1)} collective-permute-done((f32[2,128]{1,0:T(2,128)S(1)}, f32[2,128]{1,0:T(2,128)S(1)}, u32[]{:S(2)}, u32[]{:S(2)}) %collective-permute-start.25) | collective-permute-done | bytes 1056 | tf_op jit(solution)/shard_map/ppermute | solution.py:346
  69.8 0.2 collective-permute-done.23
  70.0 2.7 %collective-permute-start.24 = (f32[24,128]{1,0:T(8,128)S(1)}, f32[24,128]{1,0:T(8,128)S(1)}, u32[]{:S(2)}, u32[]{:S(2)}) collective-permute-start(f32[24,128]{1,0:T(8,128)S(1)} %add.105), channel_id=1, source_target_pairs={{0,16},{1,17},{2,18},{3,19},{4,20},{5,21},{6,22},{7,23},{8,24},{9,... | collective-permute-start | bytes 36872 | tf_op jit(solution)/shard_map/ppermute | solution.py:308
  72.7 1.9 %collective-permute-done.24 = f32[24,128]{1,0:T(8,128)S(1)} collective-permute-done((f32[24,128]{1,0:T(8,128)S(1)}, f32[24,128]{1,0:T(8,128)S(1)}, u32[]{:S(2)}, u32[]{:S(2)}) %collective-permute-start.24) | collective-permute-done | bytes 12320 | tf_op jit(solution)/shard_map/ppermute | solution.py:308
  74.6 0.7 copy-done.4
  75.3 1.3 %shard_map.169 = (f32[1024,128]{1,0:T(8,128)}, f32[1,128]{1,0:T(1,128)}, f32[64,128]{1,0:T(8,128)}, f32[64,256]{1,0:T(8,128)}) custom-call(f32[16,64,128]{2,1,0:T(8,128)S(1)} %get-tuple-element.85.refs_0_, f32[64,128]{1,0:T(8,128)S(1)} %copy-done, f32[16,128]{1,0:T(8,128)S(1)} %copy-done.2, f32[1,256]{1,0:T(1,128)S(1)} %bitcast.26, ...), custom_call_target="tpu_custom_call" | custom-call | tf_op jit(solution)/shard_map/pallas_call | solution.py:289
  (58 shorter events, 0.2 us)
Async XLA Ops:
  0.6 0.7 copy-start.13
  0.6 0.7 copy-start.14
  0.7 0.7 copy-start.11
  0.7 0.7 copy-start.12
  1.3 1.0 %copy-start.1 = (f32[64,16,128]{2,1,0:T(8,128)S(1)}, f32[64,16,128]{2,1,0:T(8,128)}, u32[]{:S(2)}) copy-start(f32[64,16,128]{2,1,0:T(8,128)} %param.20) | copy-start | bytes 1572868
  2.4 0.7 copy-start.3
  3.1 0.8 copy-start.5
  4.7 3.0 %collective-permute-start = (f32[32,128]{1,0:T(8,128)S(1)}, f32[32,128]{1,0:T(8,128)S(1)}, u32[]{:S(2)}, u32[]{:S(2)}) collective-permute-start(f32[32,128]{1,0:T(8,128)S(1)} %get-tuple-element.86), channel_id=1, source_target_pairs={{0,2},{1,3},{2,0},{3,1},{4,6},{5,7},{6,4},{7,5},{8,10},{9,11},{10,... | collective-permute-start | bytes 49160 | tf_op jit(solution)/shard_map/ppermute | solution.py:308
  5.2 12.7 %collective-permute-start.4 = (f32[72,128]{1,0:T(8,128)S(1)}, f32[72,128]{1,0:T(8,128)S(1)}, u32[]{:S(2)}, u32[]{:S(2)}) collective-permute-start(f32[72,128]{1,0:T(8,128)S(1)} %get-tuple-element.87), channel_id=1, source_target_pairs={{0,1},{1,0},{2,3},{3,2},{4,5},{5,4},{6,7},{7,6},{8,9},{9,8},{10,11... | collective-permute-start | bytes 110600 | tf_op jit(solution)/shard_map/ppermute | solution.py:308
  7.7 3.8 %collective-permute-start.1 = (f32[32,128]{1,0:T(8,128)S(1)}, f32[32,128]{1,0:T(8,128)S(1)}, u32[]{:S(2)}, u32[]{:S(2)}) collective-permute-start(f32[32,128]{1,0:T(8,128)S(1)} %add.84), channel_id=1, source_target_pairs={{0,4},{1,5},{2,6},{3,7},{4,0},{5,1},{6,2},{7,3},{8,12},{9,13},{10,... | collective-permute-start | bytes 49160 | tf_op jit(solution)/shard_map/ppermute | solution.py:308
  11.5 3.7 %collective-permute-start.2 = (f32[32,128]{1,0:T(8,128)S(1)}, f32[32,128]{1,0:T(8,128)S(1)}, u32[]{:S(2)}, u32[]{:S(2)}) collective-permute-start(f32[32,128]{1,0:T(8,128)S(1)} %add.85), channel_id=1, source_target_pairs={{0,8},{1,9},{2,10},{3,11},{4,12},{5,13},{6,14},{7,15},{8,0},{9,1},... | collective-permute-start | bytes 49160 | tf_op jit(solution)/shard_map/ppermute | solution.py:308
  15.3 4.6 %collective-permute-start.3 = (f32[32,128]{1,0:T(8,128)S(1)}, f32[32,128]{1,0:T(8,128)S(1)}, u32[]{:S(2)}, u32[]{:S(2)}) collective-permute-start(f32[32,128]{1,0:T(8,128)S(1)} %add.86), channel_id=1, source_target_pairs={{0,16},{1,17},{2,18},{3,19},{4,20},{5,21},{6,22},{7,23},{8,24},{9,... | collective-permute-start | bytes 49160 | tf_op jit(solution)/shard_map/ppermute | solution.py:308
  17.9 2.1 %copy-start = (f32[64,128]{1,0:T(8,128)S(1)}, f32[64,128]{1,0:T(8,128)}, u32[]{:S(2)}) copy-start(f32[64,128]{1,0:T(8,128)} %refs_1_.7) | copy-start | bytes 98308
  19.9 0.7 copy-start.7
  19.9 0.7 copy-start.8
  19.9 0.7 copy-start.9
  19.9 0.7 copy-start.10
  19.9 0.7 copy-start.2
  20.0 0.7 copy-start.6
  21.4 2.2 %collective-permute-start.5 = (f32[26,128]{1,0:T(8,128)S(1)}, f32[26,128]{1,0:T(8,128)S(1)}, u32[]{:S(2)}, u32[]{:S(2)}) collective-permute-start(f32[26,128]{1,0:T(8,128)S(1)} %pad_maximum_fusion), channel_id=1, source_target_pairs={{0,2},{1,3},{2,0},{3,1},{4,6},{5,7},{6,4},{7,5},{8,10},{9,11},{10,... | collective-permute-start | bytes 39944 | tf_op jit(solution)/shard_map/ppermute | solution.py:308
  21.5 3.1 %collective-permute-start.7 = (f32[8,128]{1,0:T(8,128)S(1)}, f32[8,128]{1,0:T(8,128)S(1)}, u32[]{:S(2)}, u32[]{:S(2)}) collective-permute-start(f32[8,128]{1,0:T(8,128)S(1)} %slice.99), channel_id=1, source_target_pairs={{0,3},{1,2},{2,1},{3,0},{4,7},{5,6},{6,5},{7,4},{8,11},{9,10},{10,... | collective-permute-start | bytes 12296 | tf_op jit(solution)/shard_map/ppermute | solution.py:308
  22.7 4.0 %collective-permute-start.6 = (f32[72,128]{1,0:T(8,128)S(1)}, f32[72,128]{1,0:T(8,128)S(1)}, u32[]{:S(2)}, u32[]{:S(2)}) collective-permute-start(f32[72,128]{1,0:T(8,128)S(1)} %get-tuple-element.101), channel_id=1, source_target_pairs={{0,1},{1,0},{2,3},{3,2},{4,5},{5,4},{6,7},{7,6},{8,9},{9,8},{10,11... | collective-permute-start | bytes 110600 | tf_op jit(solution)/shard_map/ppermute | solution.py:308
  26.7 3.7 %collective-permute-start.8 = (f32[24,128]{1,0:T(8,128)S(1)}, f32[24,128]{1,0:T(8,128)S(1)}, u32[]{:S(2)}, u32[]{:S(2)}) collective-permute-start(f32[24,128]{1,0:T(8,128)S(1)} %fusion.5), channel_id=1, source_target_pairs={{0,4},{1,5},{2,6},{3,7},{4,0},{5,1},{6,2},{7,3},{8,12},{9,13},{10,... | collective-permute-start | bytes 36872 | tf_op jit(solution)/shard_map/ppermute | solution.py:308
  28.2 5.7 %collective-permute-start.11 = (f32[2,128]{1,0:T(2,128)S(1)}, f32[2,128]{1,0:T(2,128)S(1)}, u32[]{:S(2)}, u32[]{:S(2)}) collective-permute-start(f32[2,128]{1,0:T(2,128)S(1)} %get-tuple-element.140), channel_id=1, source_target_pairs={{0,30},{1,31},{2,4},{3,5},{4,2},{5,3},{6,8},{7,9},{8,6},{9,7},{10,... | collective-permute-start | bytes 3080 | tf_op jit(solution)/shard_map/ppermute | solution.py:346
  30.4 3.7 %collective-permute-start.9 = (f32[24,128]{1,0:T(8,128)S(1)}, f32[24,128]{1,0:T(8,128)S(1)}, u32[]{:S(2)}, u32[]{:S(2)}) collective-permute-start(f32[24,128]{1,0:T(8,128)S(1)} %add.92), channel_id=1, source_target_pairs={{0,8},{1,9},{2,10},{3,11},{4,12},{5,13},{6,14},{7,15},{8,0},{9,1},... | collective-permute-start | bytes 36872 | tf_op jit(solution)/shard_map/ppermute | solution.py:308
  34.1 4.6 %collective-permute-start.10 = (f32[24,128]{1,0:T(8,128)S(1)}, f32[24,128]{1,0:T(8,128)S(1)}, u32[]{:S(2)}, u32[]{:S(2)}) collective-permute-start(f32[24,128]{1,0:T(8,128)S(1)} %add.93), channel_id=1, source_target_pairs={{0,16},{1,17},{2,18},{3,19},{4,20},{5,21},{6,22},{7,23},{8,24},{9,... | collective-permute-start | bytes 36872 | tf_op jit(solution)/shard_map/ppermute | solution.py:308
  39.4 2.2 %collective-permute-start.12 = (f32[26,128]{1,0:T(8,128)S(1)}, f32[26,128]{1,0:T(8,128)S(1)}, u32[]{:S(2)}, u32[]{:S(2)}) collective-permute-start(f32[26,128]{1,0:T(8,128)S(1)} %pad_maximum_fusion.1), channel_id=1, source_target_pairs={{0,2},{1,3},{2,0},{3,1},{4,6},{5,7},{6,4},{7,5},{8,10},{9,11},{10,... | collective-permute-start | bytes 39944 | tf_op jit(solution)/shard_map/ppermute | solution.py:308
  39.5 3.1 %collective-permute-start.14 = (f32[8,128]{1,0:T(8,128)S(1)}, f32[8,128]{1,0:T(8,128)S(1)}, u32[]{:S(2)}, u32[]{:S(2)}) collective-permute-start(f32[8,128]{1,0:T(8,128)S(1)} %slice.104), channel_id=1, source_target_pairs={{0,3},{1,2},{2,1},{3,0},{4,7},{5,6},{6,5},{7,4},{8,11},{9,10},{10,... | collective-permute-start | bytes 12296 | tf_op jit(solution)/shard_map/ppermute | solution.py:308
  40.6 4.0 %collective-permute-start.13 = (f32[72,128]{1,0:T(8,128)S(1)}, f32[72,128]{1,0:T(8,128)S(1)}, u32[]{:S(2)}, u32[]{:S(2)}) collective-permute-start(f32[72,128]{1,0:T(8,128)S(1)} %get-tuple-element.113), channel_id=1, source_target_pairs={{0,1},{1,0},{2,3},{3,2},{4,5},{5,4},{6,7},{7,6},{8,9},{9,8},{10,11... | collective-permute-start | bytes 110600 | tf_op jit(solution)/shard_map/ppermute | solution.py:308
  44.5 3.7 %collective-permute-start.15 = (f32[24,128]{1,0:T(8,128)S(1)}, f32[24,128]{1,0:T(8,128)S(1)}, u32[]{:S(2)}, u32[]{:S(2)}) collective-permute-start(f32[24,128]{1,0:T(8,128)S(1)} %fusion.3), channel_id=1, source_target_pairs={{0,4},{1,5},{2,6},{3,7},{4,0},{5,1},{6,2},{7,3},{8,12},{9,13},{10,... | collective-permute-start | bytes 36872 | tf_op jit(solution)/shard_map/ppermute | solution.py:308
  46.0 5.7 %collective-permute-start.18 = (f32[2,128]{1,0:T(2,128)S(1)}, f32[2,128]{1,0:T(2,128)S(1)}, u32[]{:S(2)}, u32[]{:S(2)}) collective-permute-start(f32[2,128]{1,0:T(2,128)S(1)} %get-tuple-element.138), channel_id=1, source_target_pairs={{0,30},{1,31},{2,4},{3,5},{4,2},{5,3},{6,8},{7,9},{8,6},{9,7},{10,... | collective-permute-start | bytes 3080 | tf_op jit(solution)/shard_map/ppermute | solution.py:346
  48.2 3.7 %collective-permute-start.16 = (f32[24,128]{1,0:T(8,128)S(1)}, f32[24,128]{1,0:T(8,128)S(1)}, u32[]{:S(2)}, u32[]{:S(2)}) collective-permute-start(f32[24,128]{1,0:T(8,128)S(1)} %add.98), channel_id=1, source_target_pairs={{0,8},{1,9},{2,10},{3,11},{4,12},{5,13},{6,14},{7,15},{8,0},{9,1},... | collective-permute-start | bytes 36872 | tf_op jit(solution)/shard_map/ppermute | solution.py:308
  51.9 4.6 %collective-permute-start.17 = (f32[24,128]{1,0:T(8,128)S(1)}, f32[24,128]{1,0:T(8,128)S(1)}, u32[]{:S(2)}, u32[]{:S(2)}) collective-permute-start(f32[24,128]{1,0:T(8,128)S(1)} %add.99), channel_id=1, source_target_pairs={{0,16},{1,17},{2,18},{3,19},{4,20},{5,21},{6,22},{7,23},{8,24},{9,... | collective-permute-start | bytes 36872 | tf_op jit(solution)/shard_map/ppermute | solution.py:308
  57.3 2.2 %collective-permute-start.19 = (f32[26,128]{1,0:T(8,128)S(1)}, f32[26,128]{1,0:T(8,128)S(1)}, u32[]{:S(2)}, u32[]{:S(2)}) collective-permute-start(f32[26,128]{1,0:T(8,128)S(1)} %pad_maximum_fusion.2), channel_id=1, source_target_pairs={{0,2},{1,3},{2,0},{3,1},{4,6},{5,7},{6,4},{7,5},{8,10},{9,11},{10,... | collective-permute-start | bytes 39944 | tf_op jit(solution)/shard_map/ppermute | solution.py:308
  57.4 3.1 %collective-permute-start.21 = (f32[8,128]{1,0:T(8,128)S(1)}, f32[8,128]{1,0:T(8,128)S(1)}, u32[]{:S(2)}, u32[]{:S(2)}) collective-permute-start(f32[8,128]{1,0:T(8,128)S(1)} %slice.109), channel_id=1, source_target_pairs={{0,3},{1,2},{2,1},{3,0},{4,7},{5,6},{6,5},{7,4},{8,11},{9,10},{10,... | collective-permute-start | bytes 12296 | tf_op jit(solution)/shard_map/ppermute | solution.py:308
  58.6 4.0 %collective-permute-start.20 = (f32[72,128]{1,0:T(8,128)S(1)}, f32[72,128]{1,0:T(8,128)S(1)}, u32[]{:S(2)}, u32[]{:S(2)}) collective-permute-start(f32[72,128]{1,0:T(8,128)S(1)} %get-tuple-element.125), channel_id=1, source_target_pairs={{0,1},{1,0},{2,3},{3,2},{4,5},{5,4},{6,7},{7,6},{8,9},{9,8},{10,11... | collective-permute-start | bytes 110600 | tf_op jit(solution)/shard_map/ppermute | solution.py:308
  62.6 3.7 %collective-permute-start.22 = (f32[24,128]{1,0:T(8,128)S(1)}, f32[24,128]{1,0:T(8,128)S(1)}, u32[]{:S(2)}, u32[]{:S(2)}) collective-permute-start(f32[24,128]{1,0:T(8,128)S(1)} %fusion.1), channel_id=1, source_target_pairs={{0,4},{1,5},{2,6},{3,7},{4,0},{5,1},{6,2},{7,3},{8,12},{9,13},{10,... | collective-permute-start | bytes 36872 | tf_op jit(solution)/shard_map/ppermute | solution.py:308
  64.1 5.7 %collective-permute-start.25 = (f32[2,128]{1,0:T(2,128)S(1)}, f32[2,128]{1,0:T(2,128)S(1)}, u32[]{:S(2)}, u32[]{:S(2)}) collective-permute-start(f32[2,128]{1,0:T(2,128)S(1)} %get-tuple-element.136), channel_id=1, source_target_pairs={{0,30},{1,31},{2,4},{3,5},{4,2},{5,3},{6,8},{7,9},{8,6},{9,7},{10,... | collective-permute-start | bytes 3080 | tf_op jit(solution)/shard_map/ppermute | solution.py:346
  66.3 3.7 %collective-permute-start.23 = (f32[24,128]{1,0:T(8,128)S(1)}, f32[24,128]{1,0:T(8,128)S(1)}, u32[]{:S(2)}, u32[]{:S(2)}) collective-permute-start(f32[24,128]{1,0:T(8,128)S(1)} %add.104), channel_id=1, source_target_pairs={{0,8},{1,9},{2,10},{3,11},{4,12},{5,13},{6,14},{7,15},{8,0},{9,1},... | collective-permute-start | bytes 36872 | tf_op jit(solution)/shard_map/ppermute | solution.py:308
  70.0 4.6 %collective-permute-start.24 = (f32[24,128]{1,0:T(8,128)S(1)}, f32[24,128]{1,0:T(8,128)S(1)}, u32[]{:S(2)}, u32[]{:S(2)}) collective-permute-start(f32[24,128]{1,0:T(8,128)S(1)} %add.105), channel_id=1, source_target_pairs={{0,16},{1,17},{2,18},{3,19},{4,20},{5,21},{6,22},{7,23},{8,24},{9,... | collective-permute-start | bytes 36872 | tf_op jit(solution)/shard_map/ppermute | solution.py:308
  74.6 0.7 copy-start.4

commit v3 on v2

--- a/solution.py
+++ b/solution.py
@@ -98,6 +98,25 @@
         ]
 
 
+def neighbour_rows(given, hour_index, halo, span):
+    def row_of(name, offset):
+        return jnp.concatenate(
+            [given[name][offset + i : offset + i + 1, :] for i in range(span)], axis=1
+        )
+
+    if "totals" in given:
+        return row_of("next_row", 0), row_of("prev_row", 0)
+    first, last = halo, halo + span
+    core, x_place, slab = hour_index % 2, hour_index // 2 % 2, hour_index // 4 % 2
+    next_row = jnp.where(slab == 0, row_of("near", first), row_of("far", first))
+    prev_row = jnp.where(slab == 0, row_of("far", last), row_of("near", last))
+    next_row = jnp.where(x_place == 0, row_of("across", first), next_row)
+    prev_row = jnp.where(x_place == 0, prev_row, row_of("across", last))
+    next_row = jnp.where(core == 0, row_of("partner", first), next_row)
+    prev_row = jnp.where(core == 0, prev_row, row_of("partner", last))
+    return next_row, prev_row
+
+
 def sweep_kernel(sizes, iteration, names_in, names_out, *refs):
     hours, regions, rows, techs, nodes, slots = sizes
     first = iteration == 0
@@ -107,7 +126,12 @@
     own = lax.axis_index("region")
     hour_index = lax.axis_index("hours")
     gathered = given["gathered"]
-    sums = given["totals"][...]
+    if "totals" in given:
+        sums = given["totals"][...]
+    else:
+        sums = (given["slab"][...] + given["near"][...]) + (
+            given["middle"][...] + given["far"][...]
+        )
     if first:
         weight = jnp.ones((1, 1), jnp.float32)
         col_weight, cost = sums[:techs], sums[techs : 2 * techs]
@@ -169,8 +193,7 @@
     row_id = lax.broadcasted_iota(jnp.int32, (rows, units), 0)
     if not first:
         span = units // LANES
-        next_row = jnp.concatenate([given["next_row"][i : i + 1, :] for i in range(span)], axis=1)
-        prev_row = jnp.concatenate([given["prev_row"][i : i + 1, :] for i in range(span)], axis=1)
+        next_row, prev_row = neighbour_rows(given, hour_index, techs + 2, span)
         store_duals = given["store_duals"][...]
         next_duals = jnp.where(row_id == rows - 1, next_row, pltpu.roll(store_duals, rows - 1, 0))
         if iteration == 1:
@@ -271,14 +294,15 @@
     gives["region"][rows : rows + 8, :] = jnp.concatenate(
         [primal_row, dual_row, jnp.zeros((6, LANES), jnp.float32)], axis=0
     )
-    span = units // LANES
-    gives["sums"][techs:, :] = jnp.concatenate(
-        [primal_row, dual_row, jnp.zeros((6, LANES), jnp.float32)], axis=0
-    )
+    halo, span = techs + 2, units // LANES
+    gives["sums"][techs:halo, :] = jnp.concatenate([primal_row, dual_row], axis=0)
     for i in range(span):
         part = slice(i * LANES, (i + 1) * LANES)
-        gives["first_row"][i : i + 1, :] = store_new[:1, part]
-        gives["last_row"][i : i + 1, :] = store_new[rows - 1 :, part]
+        gives["sums"][halo + i : halo + i + 1, :] = store_new[:1, part]
+        gives["sums"][halo + span + i : halo + span + i + 1, :] = store_new[rows - 1 :, part]
+    used = halo + 2 * span
+    total_rows = gives["sums"].shape[0]
+    gives["sums"][used:, :] = jnp.zeros((total_rows - used, LANES), jnp.float32)
 
 
 def sizes_lines(maps_ref, regions, slots, units):
@@ -313,48 +337,51 @@
     return lax.ppermute(value, "hours", [(i, (i + steps) % count) for i in range(count)])
 
 
-def exchange(to_regions, sums, squares_at=None, first_row=None, last_row=None):
+def exchange(to_regions, sums, techs, span):
     hours, regions = lax.axis_size("hours"), lax.axis_size("region")
-    hour, region = lax.axis_index("hours"), lax.axis_index("region")
-    sweeping = squares_at is not None
-    next_row = prev_row = None
-    if regions != 2 or hours < 4 or hours & (hours - 1):
+    region = lax.axis_index("region")
+    sweeping = span > 0
+    halo = techs + 2
+    if regions != 2 or hours != 16:
         gathered = lax.all_gather(to_regions, "region")
-        if sweeping:
-            rows = to_regions.shape[0] - 8
-            squares = jnp.sum(gathered[:, rows : rows + 8], axis=0)
-            sums = sums.at[squares_at:].set(squares)
-            next_row, prev_row = shifted(first_row, -1), shifted(last_row, 1)
-        return gathered, lax.psum(sums, "hours"), next_row, prev_row
-    even = hour % 2 == 0
-    message = sums
-    if sweeping:
-        message = jnp.concatenate([sums, jnp.where(even, last_row, first_row)], axis=0)
-        beside = jnp.where(even, first_row, last_row)
-        across = [
-            (h * regions + r, (h + 1 if h % 2 else h - 1) % hours * regions + r)
-            for h in range(hours)
-            for r in range(regions)
-        ]
-    partner = swap(message, 1, 0)
-    other = swap(to_regions, 0, 1)
-    count = sums.shape[0]
-    totals = sums + partner[:count]
+        if not sweeping:
+            return gathered, {"totals": lax.psum(sums, "hours")}
+        rows = to_regions.shape[0] - 8
+        squares = jnp.sum(gathered[:, rows : rows + 2], axis=0)
+        totals = lax.psum(sums.at[techs:halo].set(squares)[:halo], "hours")
+        next_row = shifted(sums[halo : halo + span], -1)
+        prev_row = shifted(sums[halo + span : halo + 2 * span], 1)
+        return gathered, {"totals": totals, "next_row": next_row, "prev_row": prev_row}
+
+    def merged(mine, yours, mine_first):
+        total = mine + yours
+        if not sweeping:
+            return total
+        edge = lax.broadcasted_iota(jnp.int32, total.shape, 0)
+        keep = jnp.where(edge < halo + span, mine_first, jnp.logical_not(mine_first))
+        return jnp.where(edge < halo, total, jnp.where(keep, mine, yours))
+
+    hour = lax.axis_index("hours")
+    partner = swap(sums, 1, 0)
+    chip = merged(sums, partner, hour % 2 == 0)
+    across = swap(chip, 2, 0)
     if sweeping:
         rows = to_regions.shape[0] - 8
-        diagonal = swap(sums[squares_at:], 1, 1)
-        arrived = lax.ppermute(beside, ("hours", "region"), across)
-        next_row = jnp.where(even, partner[count:], arrived)
-        prev_row = jnp.where(even, arrived, partner[count:])
-        totals = totals.at[squares_at:].add(other[rows:] + diagonal)
-    bit = 2
-    while bit < hours:
-        totals = totals + swap(totals, bit, 0)
-        bit *= 2
+        other = swap(to_regions.at[rows : rows + 2].set(chip[techs:halo]), 0, 1)
+        diagonal = swap(chip[techs:halo], 2, 1)
+    else:
+        other = swap(to_regions, 0, 1)
+    slab = merged(chip, across, hour // 2 % 2 == 0)
+    if sweeping:
+        slab = slab.at[techs:halo].add(other[rows : rows + 2] + diagonal)
+    near, middle, far = [swap(slab, 4 * step, 0) for step in (1, 2, 3)]
     gathered = jnp.where(
         region == 0, jnp.stack([to_regions, other]), jnp.stack([other, to_regions])
     )
-    return gathered, totals, next_row, prev_row
+    parts = {"slab": slab, "near": near, "middle": middle, "far": far}
+    if sweeping:
+        parts.update(partner=partner, across=across)
+    return gathered, parts
 
 
 def body(
@@ -401,13 +428,14 @@
         (shape(techs, rows, nodes), shape(2 * techs, nodes), shape(rows + info_rows, nodes)),
         in_smem=(6,),
     )
-    gathered, totals, next_row, prev_row = exchange(to_regions, message)
+    gathered, parts = exchange(to_regions, message, techs, 0)
     state = {
         "availability": avail_t,
         "demand": demand,
         "gen_cost": gen_cost,
         "store_energy": energy,
     }
+    span = units // LANES
     kept = {
         "dispatch": shape(techs, rows, nodes),
         "cap_duals": shape(techs, rows, nodes),
@@ -416,13 +444,11 @@
         "capacity": shape(techs, nodes),
         "weight": shape(1, LANES),
         "region": shape(rows + 8, nodes),
-        "sums": shape(techs + 8, nodes),
-        "first_row": shape(units // LANES, LANES),
-        "last_row": shape(units // LANES, LANES),
+        "sums": shape((techs + 2 + 2 * span) // 8 * 8 + 8, nodes),
     }
     charges = {"charge": shape(rows, units), "charge_before": shape(1, units)}
     for iteration in range(ITERS):
-        given = dict(state, totals=totals, gathered=gathered)
+        given = dict(state, **parts, gathered=gathered)
         if iteration == 0:
             given.update(
                 line_ends=line_ends,
@@ -438,7 +464,6 @@
                 limits=shape(1, total_flows),
             )
         else:
-            given.update(next_row=next_row, prev_row=prev_row)
             outs = dict(kept, **charges)
         if iteration == ITERS - 1:
             given["owner"] = owner_rows
@@ -456,13 +481,7 @@
         results = dict(zip(outs, values))
         if iteration == ITERS - 1:
             break
-        gathered, totals, next_row, prev_row = exchange(
-            results.pop("region"),
-            results.pop("sums"),
-            techs,
-            results.pop("first_row"),
-            results.pop("last_row"),
-        )
+        gathered, parts = exchange(results.pop("region"), results.pop("sums"), techs, span)
         state.update(results)
     return (
         results["dispatch"].reshape(rows, techs, nodes),

time: 77 us -> 67.2 us (0.87)
  starting transfers between devices: 38.2 us -> 32.8 us
  waiting for transfers between devices: 28.4 us -> 24.4 us
    ppermute x3 -> x0, waiting for transfers between devices: 5.72 us -> none  [exchange(): arrived = lax.ppermute(beside, ('hours', 'region'), across)]
    ppermute x3 -> x0, starting transfers between devices: 5.7 us -> none  [exchange(): arrived = lax.ppermute(beside, ('hours', 'region'), across)]
    ppermute x23 -> x27, waiting for transfers between devices: 22.6 us -> 24.4 us  [swap(): return lax.ppermute(value, ('hours', 'region'), pairs)]
    unnamed x30 -> x33, local copies, waits for them, and re-layouts: 4.6 us -> 3.85 us
    ppermute x23 -> x27, starting transfers between devices: 32.5 us -> 32.8 us  [swap(): return lax.ppermute(value, ('hours', 'region'), pairs)]
  transfers between devices with their start and end apart: 26 -> 27, of which waited for: 21 -> 24; matrix products, arithmetic and copies ran while one was open for 0% -> 0% of each run, Pallas kernels for 0% -> 0%
where the time goes in v3:
time: 67.2 us; the launch traced here: 66.9 us
  starting transfers between devices  32.8 us (49%)
  waiting for transfers between devices  24.4 us (36%)
  Pallas kernels  4.41 us (7%)
  local copies, waits for them, and re-layouts  3.87 us (6%)
  between operations  0.87 us (1%)
    ppermute x27, starting transfers between devices, swap(): return lax.ppermute(value, ('hours', 'region'), pairs)  32.8 us
    ppermute x27, waiting for transfers between devices, swap(): return lax.ppermute(value, ('hours', 'region'), pairs)  24.4 us
    pallas_call x5, Pallas kernels, call(): pl.pallas_call(kernel, out_shape=shapes, in_specs=[pl.BlockSpec(memory_sp...  4.41 us
    unnamed x33, local copies, waits for them, and re-layouts  3.85 us
  transfers between devices with their start and end apart: 27, of which 24 were waited for; matrix products, arithmetic and copies ran while one was open for 0% of the time, Pallas kernels for 0%

profile of v3, /device:TPU:0, one launch (start us, length us, event | category | flops | bytes accessed | tf_op | source)
XLA Modules:
  0.0 66.9 jit_solution(7322445907967714136)
XLA Ops:
  0.7 0.6 copy-done.13
  1.3 1.0 %copy-done.1 = f32[64,16,128]{2,1,0:T(8,128)S(1)} copy-done((f32[64,16,128]{2,1,0:T(8,128)S(1)}, f32[64,16,128]{2,1,0:T(8,128)}, u32[]{:S(2)}) %copy-start.1) | copy-done | bytes 524312
  2.4 0.7 %copy-done.3 = s32[1,2048]{1,0:T(1,128)S(1)} copy-done((s32[1,2048]{1,0:T(1,128)S(1)}, s32[1,2048]{1,0:T(1,128)}, u32[]{:S(2)}) %copy-start.3) | copy-done | bytes 8216
  3.1 0.8 %copy-done.5 = f32[64,128]{1,0:T(8,128)S(1)} copy-done((f32[64,128]{1,0:T(8,128)S(1)}, f32[64,128]{1,0:T(8,128)}, u32[]{:S(2)}) %copy-start.5) | copy-done | bytes 32792
  3.8 0.9 %shard_map.165 = (f32[16,64,128]{2,1,0:T(8,128)S(1)}, f32[32,128]{1,0:T(8,128)S(1)}, f32[72,128]{1,0:T(8,128)S(1)}) custom-call(f32[1024,128]{1,0:T(8,128)S(1)} %bitcast.16, f32[64,128]{1,0:T(8,128)S(1)} %copy-done.5, f32[1,128]{1,0:T(1,128)S(1)} %copy-done.12, s32[16,128]{1,0:T(8,128)S(1)} %bitcast.21, s32[2,64]{1,0:T(2,128)S(1)} %bitcast.30, ...), custom_call_target="tpu_custom_call" | custom-call | tf_op jit(solution)/shard_map/pallas_call | solution.py:313
  4.7 0.5 collective-permute-start
  5.2 2.5 %collective-permute-start.5 = (f32[72,128]{1,0:T(8,128)S(1)}, f32[72,128]{1,0:T(8,128)S(1)}, u32[]{:S(2)}, u32[]{:S(2)}) collective-permute-start(f32[72,128]{1,0:T(8,128)S(1)} %get-tuple-element.117), channel_id=1, source_target_pairs={{0,1},{1,0},{2,3},{3,2},{4,5},{5,4},{6,7},{7,6},{8,9},{9,8},{10,11... | collective-permute-start | bytes 110600 | tf_op jit(solution)/shard_map/ppermute | solution.py:332
  7.7 1.6 %collective-permute-start.1 = (f32[32,128]{1,0:T(8,128)S(1)}, f32[32,128]{1,0:T(8,128)S(1)}, u32[]{:S(2)}, u32[]{:S(2)}) collective-permute-start(f32[32,128]{1,0:T(8,128)S(1)} %add.72), channel_id=1, source_target_pairs={{0,4},{1,5},{2,6},{3,7},{4,0},{5,1},{6,2},{7,3},{8,12},{9,13},{10,... | collective-permute-start | bytes 49160 | tf_op jit(solution)/shard_map/ppermute | solution.py:332
  9.3 2.2 %collective-permute-done.1 = f32[32,128]{1,0:T(8,128)S(1)} collective-permute-done((f32[32,128]{1,0:T(8,128)S(1)}, f32[32,128]{1,0:T(8,128)S(1)}, u32[]{:S(2)}, u32[]{:S(2)}) %collective-permute-start.1) | collective-permute-done | bytes 16416 | tf_op jit(solution)/shard_map/ppermute | solution.py:332
  11.5 3.6 %collective-permute-start.4 = (f32[32,128]{1,0:T(8,128)S(1)}, f32[32,128]{1,0:T(8,128)S(1)}, u32[]{:S(2)}, u32[]{:S(2)}) collective-permute-start(f32[32,128]{1,0:T(8,128)S(1)} %add.73.refs_4_), channel_id=1, source_target_pairs={{0,24},{1,25},{2,26},{3,27},{4,28},{5,29},{6,30},{7,31},{8,16},{9,... | collective-permute-start | bytes 49160 | tf_op jit(solution)/shard_map/ppermute | solution.py:332
  15.1 0.8 %collective-permute-start.2 = (f32[32,128]{1,0:T(8,128)S(1)}, f32[32,128]{1,0:T(8,128)S(1)}, u32[]{:S(2)}, u32[]{:S(2)}) collective-permute-start(f32[32,128]{1,0:T(8,128)S(1)} %add.73.refs_4_), channel_id=1, source_target_pairs={{0,8},{1,9},{2,10},{3,11},{4,12},{5,13},{6,14},{7,15},{8,0},{9,1},... | collective-permute-start | bytes 49160 | tf_op jit(solution)/shard_map/ppermute | solution.py:332
  16.0 1.1 %collective-permute-done.4.refs_7_ = f32[32,128]{1,0:T(8,128)S(1)} collective-permute-done((f32[32,128]{1,0:T(8,128)S(1)}, f32[32,128]{1,0:T(8,128)S(1)}, u32[]{:S(2)}, u32[]{:S(2)}) %collective-permute-start.4) | collective-permute-done | bytes 16416 | tf_op jit(solution)/shard_map/ppermute | solution.py:332
  17.1 2.7 %collective-permute-done.3.refs_6_ = f32[32,128]{1,0:T(8,128)S(1)} collective-permute-done((f32[32,128]{1,0:T(8,128)S(1)}, f32[32,128]{1,0:T(8,128)S(1)}, u32[]{:S(2)}, u32[]{:S(2)}) %collective-permute-start.3) | collective-permute-done | bytes 16416 | tf_op jit(solution)/shard_map/ppermute | solution.py:332
  19.8 0.6 copy-done.6
  20.5 0.7 %shard_map.166 = (f32[16,64,128]{2,1,0:T(8,128)S(1)}, f32[16,64,128]{2,1,0:T(8,128)S(1)}, f32[64,640]{1,0:T(8,128)S(1)}, f32[64,256]{1,0:T(8,128)S(1)}, f32[16,1...) custom-call(f32[16,64,128]{2,1,0:T(8,128)S(1)} %get-tuple-element.11, ...), custom_call_target="tpu_custom_call" | custom-call | tf_op jit(solution)/shard_map/pallas_call | solution.py:313
  21.2 0.1 collective-permute-start.6
  21.3 1.1 %collective-permute-done.6.refs_18_ = f32[24,128]{1,0:T(8,128)S(1)} collective-permute-done((f32[24,128]{1,0:T(8,128)S(1)}, f32[24,128]{1,0:T(8,128)S(1)}, u32[]{:S(2)}, u32[]{:S(2)}) %collective-permute-start.6) | collective-permute-done | bytes 12320 | tf_op jit(solution)/shard_map/ppermute | solution.py:332
  22.4 0.1 select_select_fusion.5
  22.5 1.5 %collective-permute-start.7 = (f32[24,128]{1,0:T(8,128)S(1)}, f32[24,128]{1,0:T(8,128)S(1)}, u32[]{:S(2)}, u32[]{:S(2)}) collective-permute-start(f32[24,128]{1,0:T(8,128)S(1)} %select_select_fusion.5), channel_id=1, source_target_pairs={{0,4},{1,5},{2,6},{3,7},{4,0},{5,1},{6,2},{7,3},{8,12},{9,13},{10,... | collective-permute-start | bytes 36872 | tf_op jit(solution)/shard_map/ppermute | solution.py:332
  24.0 1.1 %collective-permute-start.9 = (f32[2,128]{1,0:T(2,128)S(1)}, f32[2,128]{1,0:T(2,128)S(1)}, u32[]{:S(2)}, u32[]{:S(2)}) collective-permute-start(f32[2,128]{1,0:T(2,128)S(1)} %get-tuple-element.159), channel_id=1, source_target_pairs={{0,5},{1,4},{2,7},{3,6},{4,1},{5,0},{6,3},{7,2},{8,13},{9,12},{10,... | collective-permute-start | bytes 3080 | tf_op jit(solution)/shard_map/ppermute | solution.py:332
  25.1 0.9 %collective-permute-start.8 = (f32[72,128]{1,0:T(8,128)S(1)}, f32[72,128]{1,0:T(8,128)S(1)}, u32[]{:S(2)}, u32[]{:S(2)}) collective-permute-start(f32[72,128]{1,0:T(8,128)S(1)} %get-tuple-element.158), channel_id=1, source_target_pairs={{0,1},{1,0},{2,3},{3,2},{4,5},{5,4},{6,7},{7,6},{8,9},{9,8},{10,11... | collective-permute-start | bytes 110600 | tf_op jit(solution)/shard_map/ppermute | solution.py:332
  26.0 0.2 collective-permute-done.7.refs_19_
  26.2 0.1 select_select_fusion.4
  26.3 2.2 %collective-permute-done.9 = f32[2,128]{1,0:T(2,128)S(1)} collective-permute-done((f32[2,128]{1,0:T(2,128)S(1)}, f32[2,128]{1,0:T(2,128)S(1)}, u32[]{:S(2)}, u32[]{:S(2)}) %collective-permute-start.9) | collective-permute-done | bytes 1056 | tf_op jit(solution)/shard_map/ppermute | solution.py:332
  28.5 0.6 collective-permute-done.8
  29.0 1.5 %collective-permute-start.12 = (f32[24,128]{1,0:T(8,128)S(1)}, f32[24,128]{1,0:T(8,128)S(1)}, u32[]{:S(2)}, u32[]{:S(2)}) collective-permute-start(f32[24,128]{1,0:T(8,128)S(1)} %constant_dynamic-update-slice_fusion.4.refs_14_), channel_id=1, source_target_pairs={{0,24},{1,25},{2,26},{3,27},{4,28},{5,29},{6,30},{7,31},{8,16},{9,... | collective-permute-start | bytes 36872 | tf_op jit(solution)/shard_map/ppermute | solution.py:332
  30.5 0.6 collective-permute-start.11
  31.1 2.3 %collective-permute-start.10 = (f32[24,128]{1,0:T(8,128)S(1)}, f32[24,128]{1,0:T(8,128)S(1)}, u32[]{:S(2)}, u32[]{:S(2)}) collective-permute-start(f32[24,128]{1,0:T(8,128)S(1)} %constant_dynamic-update-slice_fusion.4.refs_14_), channel_id=1, source_target_pairs={{0,8},{1,9},{2,10},{3,11},{4,12},{5,13},{6,14},{7,15},{8,0},{9,1},... | collective-permute-start | bytes 36872 | tf_op jit(solution)/shard_map/ppermute | solution.py:332
  33.4 1.1 %collective-permute-done.12.refs_17_ = f32[24,128]{1,0:T(8,128)S(1)} collective-permute-done((f32[24,128]{1,0:T(8,128)S(1)}, f32[24,128]{1,0:T(8,128)S(1)}, u32[]{:S(2)}, u32[]{:S(2)}) %collective-permute-start.12) | collective-permute-done | bytes 12320 | tf_op jit(solution)/shard_map/ppermute | solution.py:332
  34.5 0.6 collective-permute-done.11.refs_16_
  35.1 0.1 collective-permute-done.10.refs_15_
  35.2 0.8 %shard_map.167 = (f32[16,64,128]{2,1,0:T(8,128)S(1)}, f32[16,64,128]{2,1,0:T(8,128)S(1)}, f32[64,640]{1,0:T(8,128)S(1)}, f32[64,256]{1,0:T(8,128)S(1)}, f32[16,1...) custom-call(f32[16,64,128]{2,1,0:T(8,128)S(1)} %get-tuple-element.11, ...), custom_call_target="tpu_custom_call" | custom-call | tf_op jit(solution)/shard_map/pallas_call | solution.py:313
  36.1 1.2 %collective-permute-done.13.refs_20_ = f32[24,128]{1,0:T(8,128)S(1)} collective-permute-done((f32[24,128]{1,0:T(8,128)S(1)}, f32[24,128]{1,0:T(8,128)S(1)}, u32[]{:S(2)}, u32[]{:S(2)}) %collective-permute-start.13) | collective-permute-done | bytes 12320 | tf_op jit(solution)/shard_map/ppermute | solution.py:332
  37.2 0.1 select_select_fusion.3
  37.3 1.5 %collective-permute-start.14 = (f32[24,128]{1,0:T(8,128)S(1)}, f32[24,128]{1,0:T(8,128)S(1)}, u32[]{:S(2)}, u32[]{:S(2)}) collective-permute-start(f32[24,128]{1,0:T(8,128)S(1)} %select_select_fusion.3), channel_id=1, source_target_pairs={{0,4},{1,5},{2,6},{3,7},{4,0},{5,1},{6,2},{7,3},{8,12},{9,13},{10,... | collective-permute-start | bytes 36872 | tf_op jit(solution)/shard_map/ppermute | solution.py:332
  38.8 0.9 %collective-permute-start.16 = (f32[2,128]{1,0:T(2,128)S(1)}, f32[2,128]{1,0:T(2,128)S(1)}, u32[]{:S(2)}, u32[]{:S(2)}) collective-permute-start(f32[2,128]{1,0:T(2,128)S(1)} %get-tuple-element.157), channel_id=1, source_target_pairs={{0,5},{1,4},{2,7},{3,6},{4,1},{5,0},{6,3},{7,2},{8,13},{9,12},{10,... | collective-permute-start | bytes 3080 | tf_op jit(solution)/shard_map/ppermute | solution.py:332
  39.7 1.1 %collective-permute-start.15 = (f32[72,128]{1,0:T(8,128)S(1)}, f32[72,128]{1,0:T(8,128)S(1)}, u32[]{:S(2)}, u32[]{:S(2)}) collective-permute-start(f32[72,128]{1,0:T(8,128)S(1)} %get-tuple-element.156), channel_id=1, source_target_pairs={{0,1},{1,0},{2,3},{3,2},{4,5},{5,4},{6,7},{7,6},{8,9},{9,8},{10,11... | collective-permute-start | bytes 110600 | tf_op jit(solution)/shard_map/ppermute | solution.py:332
  40.8 0.2 collective-permute-done.14.refs_21_
  41.0 0.1 select_select_fusion.2
  41.1 2.2 %collective-permute-done.16 = f32[2,128]{1,0:T(2,128)S(1)} collective-permute-done((f32[2,128]{1,0:T(2,128)S(1)}, f32[2,128]{1,0:T(2,128)S(1)}, u32[]{:S(2)}, u32[]{:S(2)}) %collective-permute-start.16) | collective-permute-done | bytes 1056 | tf_op jit(solution)/shard_map/ppermute | solution.py:332
  43.3 0.4 collective-permute-done.15
  43.7 2.5 %collective-permute-start.19 = (f32[24,128]{1,0:T(8,128)S(1)}, f32[24,128]{1,0:T(8,128)S(1)}, u32[]{:S(2)}, u32[]{:S(2)}) collective-permute-start(f32[24,128]{1,0:T(8,128)S(1)} %constant_dynamic-update-slice_fusion.2.refs_16_), channel_id=1, source_target_pairs={{0,24},{1,25},{2,26},{3,27},{4,28},{5,29},{6,30},{7,31},{8,16},{9,... | collective-permute-start | bytes 36872 | tf_op jit(solution)/shard_map/ppermute | solution.py:332
  46.1 0.9 %collective-permute-start.18 = (f32[24,128]{1,0:T(8,128)S(1)}, f32[24,128]{1,0:T(8,128)S(1)}, u32[]{:S(2)}, u32[]{:S(2)}) collective-permute-start(f32[24,128]{1,0:T(8,128)S(1)} %constant_dynamic-update-slice_fusion.2.refs_16_), channel_id=1, source_target_pairs={{0,16},{1,17},{2,18},{3,19},{4,20},{5,21},{6,22},{7,23},{8,24},{9,... | collective-permute-start | bytes 36872 | tf_op jit(solution)/shard_map/ppermute | solution.py:332
  47.0 1.0 %collective-permute-start.17 = (f32[24,128]{1,0:T(8,128)S(1)}, f32[24,128]{1,0:T(8,128)S(1)}, u32[]{:S(2)}, u32[]{:S(2)}) collective-permute-start(f32[24,128]{1,0:T(8,128)S(1)} %constant_dynamic-update-slice_fusion.2.refs_16_), channel_id=1, source_target_pairs={{0,8},{1,9},{2,10},{3,11},{4,12},{5,13},{6,14},{7,15},{8,0},{9,1},... | collective-permute-start | bytes 36872 | tf_op jit(solution)/shard_map/ppermute | solution.py:332
  48.1 1.2 %collective-permute-done.19.refs_19_ = f32[24,128]{1,0:T(8,128)S(1)} collective-permute-done((f32[24,128]{1,0:T(8,128)S(1)}, f32[24,128]{1,0:T(8,128)S(1)}, u32[]{:S(2)}, u32[]{:S(2)}) %collective-permute-start.19) | collective-permute-done | bytes 12320 | tf_op jit(solution)/shard_map/ppermute | solution.py:332
  49.3 1.5 %collective-permute-done.18.refs_18_ = f32[24,128]{1,0:T(8,128)S(1)} collective-permute-done((f32[24,128]{1,0:T(8,128)S(1)}, f32[24,128]{1,0:T(8,128)S(1)}, u32[]{:S(2)}, u32[]{:S(2)}) %collective-permute-start.18) | collective-permute-done | bytes 12320 | tf_op jit(solution)/shard_map/ppermute | solution.py:332
  50.7 0.1 collective-permute-done.17.refs_17_
  50.9 0.8 %shard_map.168 = (f32[16,64,128]{2,1,0:T(8,128)S(1)}, f32[16,64,128]{2,1,0:T(8,128)S(1)}, f32[64,640]{1,0:T(8,128)S(1)}, f32[64,256]{1,0:T(8,128)S(1)}, f32[16,1...) custom-call(f32[16,64,128]{2,1,0:T(8,128)S(1)} %get-tuple-element.11, ...), custom_call_target="tpu_custom_call" | custom-call | tf_op jit(solution)/shard_map/pallas_call | solution.py:313
  51.7 1.2 %collective-permute-done.20.refs_20_ = f32[24,128]{1,0:T(8,128)S(1)} collective-permute-done((f32[24,128]{1,0:T(8,128)S(1)}, f32[24,128]{1,0:T(8,128)S(1)}, u32[]{:S(2)}, u32[]{:S(2)}) %collective-permute-start.20) | collective-permute-done | bytes 12320 | tf_op jit(solution)/shard_map/ppermute | solution.py:332
  52.9 0.1 select_select_fusion.1
  52.9 1.5 %collective-permute-start.21 = (f32[24,128]{1,0:T(8,128)S(1)}, f32[24,128]{1,0:T(8,128)S(1)}, u32[]{:S(2)}, u32[]{:S(2)}) collective-permute-start(f32[24,128]{1,0:T(8,128)S(1)} %select_select_fusion.1), channel_id=1, source_target_pairs={{0,4},{1,5},{2,6},{3,7},{4,0},{5,1},{6,2},{7,3},{8,12},{9,13},{10,... | collective-permute-start | bytes 36872 | tf_op jit(solution)/shard_map/ppermute | solution.py:332
  54.4 1.1 %collective-permute-start.23 = (f32[2,128]{1,0:T(2,128)S(1)}, f32[2,128]{1,0:T(2,128)S(1)}, u32[]{:S(2)}, u32[]{:S(2)}) collective-permute-start(f32[2,128]{1,0:T(2,128)S(1)} %get-tuple-element.155), channel_id=1, source_target_pairs={{0,5},{1,4},{2,7},{3,6},{4,1},{5,0},{6,3},{7,2},{8,13},{9,12},{10,... | collective-permute-start | bytes 3080 | tf_op jit(solution)/shard_map/ppermute | solution.py:332
  55.5 0.9 %collective-permute-start.22 = (f32[72,128]{1,0:T(8,128)S(1)}, f32[72,128]{1,0:T(8,128)S(1)}, u32[]{:S(2)}, u32[]{:S(2)}) collective-permute-start(f32[72,128]{1,0:T(8,128)S(1)} %get-tuple-element.154), channel_id=1, source_target_pairs={{0,1},{1,0},{2,3},{3,2},{4,5},{5,4},{6,7},{7,6},{8,9},{9,8},{10,11... | collective-permute-start | bytes 110600 | tf_op jit(solution)/shard_map/ppermute | solution.py:332
  56.4 0.2 collective-permute-done.21.refs_21_
  56.6 0.1 select_select_fusion
  56.7 2.2 %collective-permute-done.23 = f32[2,128]{1,0:T(2,128)S(1)} collective-permute-done((f32[2,128]{1,0:T(2,128)S(1)}, f32[2,128]{1,0:T(2,128)S(1)}, u32[]{:S(2)}, u32[]{:S(2)}) %collective-permute-start.23) | collective-permute-done | bytes 1056 | tf_op jit(solution)/shard_map/ppermute | solution.py:332
  58.9 0.6 collective-permute-done.22
  59.5 1.4 %collective-permute-start.26 = (f32[24,128]{1,0:T(8,128)S(1)}, f32[24,128]{1,0:T(8,128)S(1)}, u32[]{:S(2)}, u32[]{:S(2)}) collective-permute-start(f32[24,128]{1,0:T(8,128)S(1)} %constant_dynamic-update-slice_fusion.refs_16_), channel_id=1, source_target_pairs={{0,24},{1,25},{2,26},{3,27},{4,28},{5,29},{6,30},{7,31},{8,16},{9,... | collective-permute-start | bytes 36872 | tf_op jit(solution)/shard_map/ppermute | solution.py:332
  60.8 1.0 %collective-permute-start.25 = (f32[24,128]{1,0:T(8,128)S(1)}, f32[24,128]{1,0:T(8,128)S(1)}, u32[]{:S(2)}, u32[]{:S(2)}) collective-permute-start(f32[24,128]{1,0:T(8,128)S(1)} %constant_dynamic-update-slice_fusion.refs_16_), channel_id=1, source_target_pairs={{0,16},{1,17},{2,18},{3,19},{4,20},{5,21},{6,22},{7,23},{8,24},{9,... | collective-permute-start | bytes 36872 | tf_op jit(solution)/shard_map/ppermute | solution.py:332
  61.8 2.0 %collective-permute-start.24 = (f32[24,128]{1,0:T(8,128)S(1)}, f32[24,128]{1,0:T(8,128)S(1)}, u32[]{:S(2)}, u32[]{:S(2)}) collective-permute-start(f32[24,128]{1,0:T(8,128)S(1)} %constant_dynamic-update-slice_fusion.refs_16_), channel_id=1, source_target_pairs={{0,8},{1,9},{2,10},{3,11},{4,12},{5,13},{6,14},{7,15},{8,0},{9,1},... | collective-permute-start | bytes 36872 | tf_op jit(solution)/shard_map/ppermute | solution.py:332
  63.9 1.1 %collective-permute-done.26.refs_19_ = f32[24,128]{1,0:T(8,128)S(1)} collective-permute-done((f32[24,128]{1,0:T(8,128)S(1)}, f32[24,128]{1,0:T(8,128)S(1)}, u32[]{:S(2)}, u32[]{:S(2)}) %collective-permute-start.26) | collective-permute-done | bytes 12320 | tf_op jit(solution)/shard_map/ppermute | solution.py:332
  65.0 0.5 collective-permute-done.25.refs_18_
  65.4 0.1 collective-permute-done.24.refs_17_
  65.6 1.3 %shard_map.169 = (f32[1024,128]{1,0:T(8,128)}, f32[1,128]{1,0:T(1,128)}, f32[64,128]{1,0:T(8,128)}, f32[64,256]{1,0:T(8,128)}) custom-call(f32[16,64,128]{2,1,0:T(8,128)S(1)} %get-tuple-element.115.refs_0_, f32[64,128]{1,0:T(8,128)S(1)} %copy-done, f32[16,128]{1,0:T(8,128)S(1)} %copy-done.2, f32[1,256]{1,0:T(1,128)S(1)} %bitcast.26, ...), custom_call_target="tpu_custom_call" | custom-call | tf_op jit(solution)/shard_map/pallas_call | solution.py:313
  (48 shorter events, 0.4 us)
Async XLA Ops:
  0.6 0.7 copy-start.13
  0.6 0.7 copy-start.14
  0.7 0.7 %copy-start.11 = (s32[2,1,64]{2,1,0:T(1,128)S(1)}, s32[2,1,64]{2,1,0:T(1,128)}, u32[]{:S(2)}) copy-start(s32[2,1,64]{2,1,0:T(1,128)} %param.33) | copy-start | bytes 1540
  0.7 0.7 %copy-start.12 = (f32[1,128]{1,0:T(1,128)S(1)}, f32[1,128]{1,0:T(1,128)}, u32[]{:S(2)}) copy-start(f32[1,128]{1,0:T(1,128)} %cost_ref.1) | copy-start | bytes 1540
  1.3 1.0 %copy-start.1 = (f32[64,16,128]{2,1,0:T(8,128)S(1)}, f32[64,16,128]{2,1,0:T(8,128)}, u32[]{:S(2)}) copy-start(f32[64,16,128]{2,1,0:T(8,128)} %param.26) | copy-start | bytes 1572868
  2.4 0.7 %copy-start.3 = (s32[1,2048]{1,0:T(1,128)S(1)}, s32[1,2048]{1,0:T(1,128)}, u32[]{:S(2)}) copy-start(s32[1,2048]{1,0:T(1,128)} %param.30) | copy-start | bytes 24580
  3.1 0.8 %copy-start.5 = (f32[64,128]{1,0:T(8,128)S(1)}, f32[64,128]{1,0:T(8,128)}, u32[]{:S(2)}) copy-start(f32[64,128]{1,0:T(8,128)} %price_ref.1) | copy-start | bytes 98308
  4.7 3.0 %collective-permute-start = (f32[32,128]{1,0:T(8,128)S(1)}, f32[32,128]{1,0:T(8,128)S(1)}, u32[]{:S(2)}, u32[]{:S(2)}) collective-permute-start(f32[32,128]{1,0:T(8,128)S(1)} %get-tuple-element.116), channel_id=1, source_target_pairs={{0,2},{1,3},{2,0},{3,1},{4,6},{5,7},{6,4},{7,5},{8,10},{9,11},{10,... | collective-permute-start | bytes 49160 | tf_op jit(solution)/shard_map/ppermute | solution.py:332
  5.2 10.7 %collective-permute-start.5 = (f32[72,128]{1,0:T(8,128)S(1)}, f32[72,128]{1,0:T(8,128)S(1)}, u32[]{:S(2)}, u32[]{:S(2)}) collective-permute-start(f32[72,128]{1,0:T(8,128)S(1)} %get-tuple-element.117), channel_id=1, source_target_pairs={{0,1},{1,0},{2,3},{3,2},{4,5},{5,4},{6,7},{7,6},{8,9},{9,8},{10,11... | collective-permute-start | bytes 110600 | tf_op jit(solution)/shard_map/ppermute | solution.py:332
  7.7 3.8 %collective-permute-start.1 = (f32[32,128]{1,0:T(8,128)S(1)}, f32[32,128]{1,0:T(8,128)S(1)}, u32[]{:S(2)}, u32[]{:S(2)}) collective-permute-start(f32[32,128]{1,0:T(8,128)S(1)} %add.72), channel_id=1, source_target_pairs={{0,4},{1,5},{2,6},{3,7},{4,0},{5,1},{6,2},{7,3},{8,12},{9,13},{10,... | collective-permute-start | bytes 49160 | tf_op jit(solution)/shard_map/ppermute | solution.py:332
  11.5 5.5 %collective-permute-start.4 = (f32[32,128]{1,0:T(8,128)S(1)}, f32[32,128]{1,0:T(8,128)S(1)}, u32[]{:S(2)}, u32[]{:S(2)}) collective-permute-start(f32[32,128]{1,0:T(8,128)S(1)} %add.73.refs_4_), channel_id=1, source_target_pairs={{0,24},{1,25},{2,26},{3,27},{4,28},{5,29},{6,30},{7,31},{8,16},{9,... | collective-permute-start | bytes 49160 | tf_op jit(solution)/shard_map/ppermute | solution.py:332
  15.1 4.6 %collective-permute-start.3 = (f32[32,128]{1,0:T(8,128)S(1)}, f32[32,128]{1,0:T(8,128)S(1)}, u32[]{:S(2)}, u32[]{:S(2)}) collective-permute-start(f32[32,128]{1,0:T(8,128)S(1)} %add.73.refs_4_), channel_id=1, source_target_pairs={{0,16},{1,17},{2,18},{3,19},{4,20},{5,21},{6,22},{7,23},{8,24},{9,... | collective-permute-start | bytes 49160 | tf_op jit(solution)/shard_map/ppermute | solution.py:332
  15.1 4.6 %collective-permute-start.2 = (f32[32,128]{1,0:T(8,128)S(1)}, f32[32,128]{1,0:T(8,128)S(1)}, u32[]{:S(2)}, u32[]{:S(2)}) collective-permute-start(f32[32,128]{1,0:T(8,128)S(1)} %add.73.refs_4_), channel_id=1, source_target_pairs={{0,8},{1,9},{2,10},{3,11},{4,12},{5,13},{6,14},{7,15},{8,0},{9,1},... | collective-permute-start | bytes 49160 | tf_op jit(solution)/shard_map/ppermute | solution.py:332
  15.9 3.9 %copy-start = (f32[64,128]{1,0:T(8,128)S(1)}, f32[64,128]{1,0:T(8,128)}, u32[]{:S(2)}) copy-start(f32[64,128]{1,0:T(8,128)} %refs_1_.7) | copy-start | bytes 98308
  15.9 3.9 %copy-start.7 = (s32[2,256]{1,0:T(2,128)S(1)}, s32[2,256]{1,0:T(2,128)}, u32[]{:S(2)}) copy-start(s32[2,256]{1,0:T(2,128)} %refs_9_.1) | copy-start | bytes 6148
  15.9 3.9 %copy-start.8 = (f32[256]{0:T(256)S(1)}, f32[256]{0:T(256)}, u32[]{:S(2)}) copy-start(f32[256]{0:T(256)} %param.32) | copy-start | bytes 3076
  15.9 3.9 %copy-start.9 = (s32[256]{0:T(256)S(1)}, s32[256]{0:T(256)}, u32[]{:S(2)}) copy-start(s32[256]{0:T(256)} %param.36) | copy-start | bytes 3076
  16.0 3.9 %copy-start.10 = (f32[256]{0:T(256)S(1)}, f32[256]{0:T(256)}, u32[]{:S(2)}) copy-start(f32[256]{0:T(256)} %param.38) | copy-start | bytes 3076
  16.0 3.8 %copy-start.2 = (f32[16,128]{1,0:T(8,128)S(1)}, f32[16,128]{1,0:T(8,128)}, u32[]{:S(2)}) copy-start(f32[16,128]{1,0:T(8,128)} %refs_2_.7) | copy-start | bytes 24580
  19.8 0.7 %copy-start.6 = (f32[256]{0:T(256)S(1)}, f32[256]{0:T(256)}, u32[]{:S(2)}) copy-start(f32[256]{0:T(256)} %param.37) | copy-start | bytes 3076
  21.2 1.2 %collective-permute-start.6 = (f32[24,128]{1,0:T(8,128)S(1)}, f32[24,128]{1,0:T(8,128)S(1)}, u32[]{:S(2)}, u32[]{:S(2)}) collective-permute-start(f32[24,128]{1,0:T(8,128)S(1)} %get-tuple-element.128), channel_id=1, source_target_pairs={{0,2},{1,3},{2,0},{3,1},{4,6},{5,7},{6,4},{7,5},{8,10},{9,11},{10,... | collective-permute-start | bytes 36872 | tf_op jit(solution)/shard_map/ppermute | solution.py:332
  22.5 3.7 %collective-permute-start.7 = (f32[24,128]{1,0:T(8,128)S(1)}, f32[24,128]{1,0:T(8,128)S(1)}, u32[]{:S(2)}, u32[]{:S(2)}) collective-permute-start(f32[24,128]{1,0:T(8,128)S(1)} %select_select_fusion.5), channel_id=1, source_target_pairs={{0,4},{1,5},{2,6},{3,7},{4,0},{5,1},{6,2},{7,3},{8,12},{9,13},{10,... | collective-permute-start | bytes 36872 | tf_op jit(solution)/shard_map/ppermute | solution.py:332
  24.0 4.5 %collective-permute-start.9 = (f32[2,128]{1,0:T(2,128)S(1)}, f32[2,128]{1,0:T(2,128)S(1)}, u32[]{:S(2)}, u32[]{:S(2)}) collective-permute-start(f32[2,128]{1,0:T(2,128)S(1)} %get-tuple-element.159), channel_id=1, source_target_pairs={{0,5},{1,4},{2,7},{3,6},{4,1},{5,0},{6,3},{7,2},{8,13},{9,12},{10,... | collective-permute-start | bytes 3080 | tf_op jit(solution)/shard_map/ppermute | solution.py:332
  25.1 4.0 %collective-permute-start.8 = (f32[72,128]{1,0:T(8,128)S(1)}, f32[72,128]{1,0:T(8,128)S(1)}, u32[]{:S(2)}, u32[]{:S(2)}) collective-permute-start(f32[72,128]{1,0:T(8,128)S(1)} %get-tuple-element.158), channel_id=1, source_target_pairs={{0,1},{1,0},{2,3},{3,2},{4,5},{5,4},{6,7},{7,6},{8,9},{9,8},{10,11... | collective-permute-start | bytes 110600 | tf_op jit(solution)/shard_map/ppermute | solution.py:332
  29.0 5.5 %collective-permute-start.12 = (f32[24,128]{1,0:T(8,128)S(1)}, f32[24,128]{1,0:T(8,128)S(1)}, u32[]{:S(2)}, u32[]{:S(2)}) collective-permute-start(f32[24,128]{1,0:T(8,128)S(1)} %constant_dynamic-update-slice_fusion.4.refs_14_), channel_id=1, source_target_pairs={{0,24},{1,25},{2,26},{3,27},{4,28},{5,29},{6,30},{7,31},{8,16},{9,... | collective-permute-start | bytes 36872 | tf_op jit(solution)/shard_map/ppermute | solution.py:332
  30.5 4.6 %collective-permute-start.11 = (f32[24,128]{1,0:T(8,128)S(1)}, f32[24,128]{1,0:T(8,128)S(1)}, u32[]{:S(2)}, u32[]{:S(2)}) collective-permute-start(f32[24,128]{1,0:T(8,128)S(1)} %constant_dynamic-update-slice_fusion.4.refs_14_), channel_id=1, source_target_pairs={{0,16},{1,17},{2,18},{3,19},{4,20},{5,21},{6,22},{7,23},{8,24},{9,... | collective-permute-start | bytes 36872 | tf_op jit(solution)/shard_map/ppermute | solution.py:332
  31.1 4.1 %collective-permute-start.10 = (f32[24,128]{1,0:T(8,128)S(1)}, f32[24,128]{1,0:T(8,128)S(1)}, u32[]{:S(2)}, u32[]{:S(2)}) collective-permute-start(f32[24,128]{1,0:T(8,128)S(1)} %constant_dynamic-update-slice_fusion.4.refs_14_), channel_id=1, source_target_pairs={{0,8},{1,9},{2,10},{3,11},{4,12},{5,13},{6,14},{7,15},{8,0},{9,1},... | collective-permute-start | bytes 36872 | tf_op jit(solution)/shard_map/ppermute | solution.py:332
  36.0 1.2 %collective-permute-start.13 = (f32[24,128]{1,0:T(8,128)S(1)}, f32[24,128]{1,0:T(8,128)S(1)}, u32[]{:S(2)}, u32[]{:S(2)}) collective-permute-start(f32[24,128]{1,0:T(8,128)S(1)} %get-tuple-element.138), channel_id=1, source_target_pairs={{0,2},{1,3},{2,0},{3,1},{4,6},{5,7},{6,4},{7,5},{8,10},{9,11},{10,... | collective-permute-start | bytes 36872 | tf_op jit(solution)/shard_map/ppermute | solution.py:332
  37.3 3.7 %collective-permute-start.14 = (f32[24,128]{1,0:T(8,128)S(1)}, f32[24,128]{1,0:T(8,128)S(1)}, u32[]{:S(2)}, u32[]{:S(2)}) collective-permute-start(f32[24,128]{1,0:T(8,128)S(1)} %select_select_fusion.3), channel_id=1, source_target_pairs={{0,4},{1,5},{2,6},{3,7},{4,0},{5,1},{6,2},{7,3},{8,12},{9,13},{10,... | collective-permute-start | bytes 36872 | tf_op jit(solution)/shard_map/ppermute | solution.py:332
  38.8 4.5 %collective-permute-start.16 = (f32[2,128]{1,0:T(2,128)S(1)}, f32[2,128]{1,0:T(2,128)S(1)}, u32[]{:S(2)}, u32[]{:S(2)}) collective-permute-start(f32[2,128]{1,0:T(2,128)S(1)} %get-tuple-element.157), channel_id=1, source_target_pairs={{0,5},{1,4},{2,7},{3,6},{4,1},{5,0},{6,3},{7,2},{8,13},{9,12},{10,... | collective-permute-start | bytes 3080 | tf_op jit(solution)/shard_map/ppermute | solution.py:332
  39.7 4.0 %collective-permute-start.15 = (f32[72,128]{1,0:T(8,128)S(1)}, f32[72,128]{1,0:T(8,128)S(1)}, u32[]{:S(2)}, u32[]{:S(2)}) collective-permute-start(f32[72,128]{1,0:T(8,128)S(1)} %get-tuple-element.156), channel_id=1, source_target_pairs={{0,1},{1,0},{2,3},{3,2},{4,5},{5,4},{6,7},{7,6},{8,9},{9,8},{10,11... | collective-permute-start | bytes 110600 | tf_op jit(solution)/shard_map/ppermute | solution.py:332
  43.7 5.6 %collective-permute-start.19 = (f32[24,128]{1,0:T(8,128)S(1)}, f32[24,128]{1,0:T(8,128)S(1)}, u32[]{:S(2)}, u32[]{:S(2)}) collective-permute-start(f32[24,128]{1,0:T(8,128)S(1)} %constant_dynamic-update-slice_fusion.2.refs_16_), channel_id=1, source_target_pairs={{0,24},{1,25},{2,26},{3,27},{4,28},{5,29},{6,30},{7,31},{8,16},{9,... | collective-permute-start | bytes 36872 | tf_op jit(solution)/shard_map/ppermute | solution.py:332
  46.1 4.6 %collective-permute-start.18 = (f32[24,128]{1,0:T(8,128)S(1)}, f32[24,128]{1,0:T(8,128)S(1)}, u32[]{:S(2)}, u32[]{:S(2)}) collective-permute-start(f32[24,128]{1,0:T(8,128)S(1)} %constant_dynamic-update-slice_fusion.2.refs_16_), channel_id=1, source_target_pairs={{0,16},{1,17},{2,18},{3,19},{4,20},{5,21},{6,22},{7,23},{8,24},{9,... | collective-permute-start | bytes 36872 | tf_op jit(solution)/shard_map/ppermute | solution.py:332
  47.0 3.8 %collective-permute-start.17 = (f32[24,128]{1,0:T(8,128)S(1)}, f32[24,128]{1,0:T(8,128)S(1)}, u32[]{:S(2)}, u32[]{:S(2)}) collective-permute-start(f32[24,128]{1,0:T(8,128)S(1)} %constant_dynamic-update-slice_fusion.2.refs_16_), channel_id=1, source_target_pairs={{0,8},{1,9},{2,10},{3,11},{4,12},{5,13},{6,14},{7,15},{8,0},{9,1},... | collective-permute-start | bytes 36872 | tf_op jit(solution)/shard_map/ppermute | solution.py:332
  51.6 1.2 %collective-permute-start.20 = (f32[24,128]{1,0:T(8,128)S(1)}, f32[24,128]{1,0:T(8,128)S(1)}, u32[]{:S(2)}, u32[]{:S(2)}) collective-permute-start(f32[24,128]{1,0:T(8,128)S(1)} %get-tuple-element.148), channel_id=1, source_target_pairs={{0,2},{1,3},{2,0},{3,1},{4,6},{5,7},{6,4},{7,5},{8,10},{9,11},{10,... | collective-permute-start | bytes 36872 | tf_op jit(solution)/shard_map/ppermute | solution.py:332
  52.9 3.7 %collective-permute-start.21 = (f32[24,128]{1,0:T(8,128)S(1)}, f32[24,128]{1,0:T(8,128)S(1)}, u32[]{:S(2)}, u32[]{:S(2)}) collective-permute-start(f32[24,128]{1,0:T(8,128)S(1)} %select_select_fusion.1), channel_id=1, source_target_pairs={{0,4},{1,5},{2,6},{3,7},{4,0},{5,1},{6,2},{7,3},{8,12},{9,13},{10,... | collective-permute-start | bytes 36872 | tf_op jit(solution)/shard_map/ppermute | solution.py:332
  54.4 4.5 %collective-permute-start.23 = (f32[2,128]{1,0:T(2,128)S(1)}, f32[2,128]{1,0:T(2,128)S(1)}, u32[]{:S(2)}, u32[]{:S(2)}) collective-permute-start(f32[2,128]{1,0:T(2,128)S(1)} %get-tuple-element.155), channel_id=1, source_target_pairs={{0,5},{1,4},{2,7},{3,6},{4,1},{5,0},{6,3},{7,2},{8,13},{9,12},{10,... | collective-permute-start | bytes 3080 | tf_op jit(solution)/shard_map/ppermute | solution.py:332
  55.5 4.0 %collective-permute-start.22 = (f32[72,128]{1,0:T(8,128)S(1)}, f32[72,128]{1,0:T(8,128)S(1)}, u32[]{:S(2)}, u32[]{:S(2)}) collective-permute-start(f32[72,128]{1,0:T(8,128)S(1)} %get-tuple-element.154), channel_id=1, source_target_pairs={{0,1},{1,0},{2,3},{3,2},{4,5},{5,4},{6,7},{7,6},{8,9},{9,8},{10,11... | collective-permute-start | bytes 110600 | tf_op jit(solution)/shard_map/ppermute | solution.py:332
  59.5 5.5 %collective-permute-start.26 = (f32[24,128]{1,0:T(8,128)S(1)}, f32[24,128]{1,0:T(8,128)S(1)}, u32[]{:S(2)}, u32[]{:S(2)}) collective-permute-start(f32[24,128]{1,0:T(8,128)S(1)} %constant_dynamic-update-slice_fusion.refs_16_), channel_id=1, source_target_pairs={{0,24},{1,25},{2,26},{3,27},{4,28},{5,29},{6,30},{7,31},{8,16},{9,... | collective-permute-start | bytes 36872 | tf_op jit(solution)/shard_map/ppermute | solution.py:332
  60.8 4.6 %collective-permute-start.25 = (f32[24,128]{1,0:T(8,128)S(1)}, f32[24,128]{1,0:T(8,128)S(1)}, u32[]{:S(2)}, u32[]{:S(2)}) collective-permute-start(f32[24,128]{1,0:T(8,128)S(1)} %constant_dynamic-update-slice_fusion.refs_16_), channel_id=1, source_target_pairs={{0,16},{1,17},{2,18},{3,19},{4,20},{5,21},{6,22},{7,23},{8,24},{9,... | collective-permute-start | bytes 36872 | tf_op jit(solution)/shard_map/ppermute | solution.py:332
  61.8 3.7 %collective-permute-start.24 = (f32[24,128]{1,0:T(8,128)S(1)}, f32[24,128]{1,0:T(8,128)S(1)}, u32[]{:S(2)}, u32[]{:S(2)}) collective-permute-start(f32[24,128]{1,0:T(8,128)S(1)} %constant_dynamic-update-slice_fusion.refs_16_), channel_id=1, source_target_pairs={{0,8},{1,9},{2,10},{3,11},{4,12},{5,13},{6,14},{7,15},{8,0},{9,1},... | collective-permute-start | bytes 36872 | tf_op jit(solution)/shard_map/ppermute | solution.py:332
  63.9 1.7 %copy-start.4 = (s32[1,2048]{1,0:T(1,128)S(1)}, s32[1,2048]{1,0:T(1,128)}, u32[]{:S(2)}) copy-start(s32[1,2048]{1,0:T(1,128)} %param.30) | copy-start | bytes 24580

commit v4 on v3

--- a/solution.py
+++ b/solution.py
@@ -99,21 +99,27 @@
 
 
 def neighbour_rows(given, hour_index, halo, span):
-    def row_of(name, offset):
+    def row_of(ref, *place):
+        start = place[-1]
         return jnp.concatenate(
-            [given[name][offset + i : offset + i + 1, :] for i in range(span)], axis=1
+            [ref[(*place[:-1], slice(start + i, start + i + 1))] for i in range(span)], axis=1
         )
 
     if "totals" in given:
-        return row_of("next_row", 0), row_of("prev_row", 0)
-    first, last = halo, halo + span
-    core, x_place, slab = hour_index % 2, hour_index // 2 % 2, hour_index // 4 % 2
-    next_row = jnp.where(slab == 0, row_of("near", first), row_of("far", first))
-    prev_row = jnp.where(slab == 0, row_of("far", last), row_of("near", last))
-    next_row = jnp.where(x_place == 0, row_of("across", first), next_row)
-    prev_row = jnp.where(x_place == 0, prev_row, row_of("across", last))
-    next_row = jnp.where(core == 0, row_of("partner", first), next_row)
-    prev_row = jnp.where(core == 0, prev_row, row_of("partner", last))
+        return row_of(given["next_row"], 0), row_of(given["prev_row"], 0)
+    places, slabs = given["places"], given["slabs"]
+    inner, outer = places.shape[0], slabs.shape[0]
+    place, slab = hour_index % inner, hour_index // inner
+    next_row = jnp.where(
+        place == inner - 1,
+        row_of(slabs, (slab + 1) % outer, halo),
+        row_of(places, (place + 1) % inner, halo),
+    )
+    prev_row = jnp.where(
+        place == 0,
+        row_of(slabs, (slab + outer - 1) % outer, halo + span),
+        row_of(places, (place + inner - 1) % inner, halo + span),
+    )
     return next_row, prev_row
 
 
@@ -129,9 +135,7 @@
     if "totals" in given:
         sums = given["totals"][...]
     else:
-        sums = (given["slab"][...] + given["near"][...]) + (
-            given["middle"][...] + given["far"][...]
-        )
+        sums = jnp.sum(given["slabs"][...], axis=0)
     if first:
         weight = jnp.ones((1, 1), jnp.float32)
         col_weight, cost = sums[:techs], sums[techs : 2 * techs]
@@ -332,6 +336,13 @@
     return lax.ppermute(value, ("hours", "region"), pairs)
 
 
+def to_all(message, groups):
+    copies = jnp.broadcast_to(message[None], (len(groups[0]), *message.shape))
+    return lax.all_to_all(
+        copies, ("hours", "region"), split_axis=0, concat_axis=0, axis_index_groups=groups
+    )
+
+
 def shifted(value, steps):
     count = lax.axis_size("hours")
     return lax.ppermute(value, "hours", [(i, (i + steps) % count) for i in range(count)])
@@ -353,34 +364,40 @@
         prev_row = shifted(sums[halo + span : halo + 2 * span], 1)
         return gathered, {"totals": totals, "next_row": next_row, "prev_row": prev_row}
 
-    def merged(mine, yours, mine_first):
-        total = mine + yours
-        if not sweeping:
-            return total
-        edge = lax.broadcasted_iota(jnp.int32, total.shape, 0)
-        keep = jnp.where(edge < halo + span, mine_first, jnp.logical_not(mine_first))
-        return jnp.where(edge < halo, total, jnp.where(keep, mine, yours))
-
-    hour = lax.axis_index("hours")
-    partner = swap(sums, 1, 0)
-    chip = merged(sums, partner, hour % 2 == 0)
-    across = swap(chip, 2, 0)
+    near = [
+        [(z * 4 + place) * regions + side for place in range(4) for side in range(regions)]
+        for z in range(hours // 4)
+    ]
+    far = [
+        [(z * 4 + place) * regions + side for z in range(hours // 4)]
+        for place in range(4)
+        for side in range(regions)
+    ]
+    other = swap(to_regions, 0, 1)
+    slab = to_all(sums, near)
     if sweeping:
-        rows = to_regions.shape[0] - 8
-        other = swap(to_regions.at[rows : rows + 2].set(chip[techs:halo]), 0, 1)
-        diagonal = swap(chip[techs:halo], 2, 1)
-    else:
-        other = swap(to_regions, 0, 1)
-    slab = merged(chip, across, hour // 2 % 2 == 0)
+        squares = jnp.sum(slab[:, techs:halo], axis=0)
+    mine = slab.reshape(4, regions, *sums.shape)
+    mine = jnp.where(region == 0, mine[:, 0], mine[:, 1])
+    message = jnp.sum(mine, axis=0)
     if sweeping:
-        slab = slab.at[techs:halo].add(other[rows : rows + 2] + diagonal)
-    near, middle, far = [swap(slab, 4 * step, 0) for step in (1, 2, 3)]
+        message = jnp.concatenate(
+            [
+                message[:techs],
+                squares,
+                mine[0, halo : halo + span],
+                mine[-1, halo + span : halo + 2 * span],
+                message[halo + 2 * span :],
+            ],
+            axis=0,
+        )
+    slabs = to_all(message, far)
     gathered = jnp.where(
         region == 0, jnp.stack([to_regions, other]), jnp.stack([other, to_regions])
     )
-    parts = {"slab": slab, "near": near, "middle": middle, "far": far}
+    parts = {"slabs": slabs}
     if sweeping:
-        parts.update(partner=partner, across=across)
+        parts["places"] = mine
     return gathered, parts
 
 

time: 67.2 us -> 98 us (1.46)
  local copies, waits for them, and re-layouts: 3.87 us -> 19.5 us
  waiting for transfers between devices: 24.4 us -> 33.9 us
  starting transfers between devices: 32.8 us -> 37.7 us
    all_to_all x0 -> x8, waiting for transfers between devices: none -> 33.9 us  [to_all(): lax.all_to_all(copies, ('hours', 'region'), split_axis=0, concat_axis=0,...]
    all_to_all x0 -> x8, starting transfers between devices: none -> 29.9 us  [to_all(): lax.all_to_all(copies, ('hours', 'region'), split_axis=0, concat_axis=0,...]
    ppermute x27 -> x4, starting transfers between devices: 32.8 us -> 7.78 us  [swap(): return lax.ppermute(value, ('hours', 'region'), pairs)]
    ppermute x27 -> x4, waiting for transfers between devices: 24.4 us -> 0.01 us  [swap(): return lax.ppermute(value, ('hours', 'region'), pairs)]
    unnamed x33 -> x74, local copies, waits for them, and re-layouts: 3.85 us -> 14.3 us
    broadcast_in_dim x0 -> x8, local copies, waits for them, and re-layouts: none -> 5.15 us  [to_all(): copies = jnp.broadcast_to(message[None], (len(groups[0]), *message.shape))]
  transfers between devices with their start and end apart: 27 -> 12, of which waited for: 24 -> 8; matrix products, arithmetic and copies ran while one was open for 0% -> 3% of each run, Pallas kernels for 0% -> 0%
where the time goes in v4:
time: 98 us; the launch traced here: 96.7 us
  starting transfers between devices  37.7 us (38%)
  waiting for transfers between devices  33.9 us (35%)
  local copies, waits for them, and re-layouts  19.5 us (20%)
  Pallas kernels  4.4 us (4%)
  between operations  1.04 us (1%)
    all_to_all x8, waiting for transfers between devices, to_all(): lax.all_to_all(copies, ('hours', 'region'), split_axis=0, concat_axis=0,...  33.9 us
    all_to_all x8, starting transfers between devices, to_all(): lax.all_to_all(copies, ('hours', 'region'), split_axis=0, concat_axis=0,...  29.9 us
    unnamed x74, local copies, waits for them, and re-layouts  14.3 us
    ppermute x4, starting transfers between devices, swap(): return lax.ppermute(value, ('hours', 'region'), pairs)  7.78 us
    broadcast_in_dim x8, local copies, waits for them, and re-layouts, to_all(): copies = jnp.broadcast_to(message[None], (len(groups[0]), *message.shape))  5.15 us
    pallas_call x5, Pallas kernels, call(): pl.pallas_call(kernel, out_shape=shapes, in_specs=[pl.BlockSpec(memory_sp...  4.4 us
  transfers between devices with their start and end apart: 12, of which 8 were waited for; matrix products, arithmetic and copies ran while one was open for 3% of the time, Pallas kernels for 0%

profile of v4, /device:TPU:0, one launch (start us, length us, event | category | flops | bytes accessed | tf_op | source)
XLA Modules:
  0.0 96.7 jit_solution(2622851552534023272)
XLA Ops:
  0.7 0.6 copy-done.35
  1.3 0.0 copy-done.36
  1.3 0.0 copy-done.29
  1.3 1.0 %copy-done.1 = f32[64,16,128]{2,1,0:T(8,128)S(1)} copy-done((f32[64,16,128]{2,1,0:T(8,128)S(1)}, f32[64,16,128]{2,1,0:T(8,128)}, u32[]{:S(2)}) %copy-start.1) | copy-done | bytes 524312
  2.4 0.7 copy-done.13
  3.1 0.8 copy-done.15
  3.8 0.9 shard_map.165
  4.7 0.7 broadcast_in_dim.25
  5.4 5.2 %all-to-all-start = ((f32[8,32,128]{2,1,0:T(8,128)}), f32[8,32,128]{2,1,0:T(8,128)S(1)}, u32[]{:S(2)}, u32[]{:S(2)}) async-start(f32[8,32,128]{2,1,0:T(8,128)} %broadcast_in_dim.25), calls=%async_computation | async-start | bytes 262144 | tf_op jit(solution)/shard_map/all_to_all | solution.py:341
  10.6 2.0 %collective-permute-start = (f32[72,128]{1,0:T(8,128)S(1)}, f32[72,128]{1,0:T(8,128)S(1)}, u32[]{:S(2)}, u32[]{:S(2)}) collective-permute-start(f32[72,128]{1,0:T(8,128)S(1)} %get-tuple-element.45), channel_id=1, source_target_pairs={{0,1},{1,0},{2,3},{3,2},{4,5},{5,4},{6,7},{7,6},{8,9},{9,8},{10,11... | collective-permute-start | bytes 110600 | tf_op jit(solution)/shard_map/ppermute | solution.py:336
  12.6 2.9 %all-to-all-done = f32[8,32,128]{2,1,0:T(8,128)S(1)} async-done(((f32[8,32,128]{2,1,0:T(8,128)}), f32[8,32,128]{2,1,0:T(8,128)S(1)}, u32[]{:S(2)}, u32[]{:S(2)}) %all-to-all-start) | async-done | bytes 131104 | tf_op jit(solution)/shard_map/all_to_all | solution.py:341
  15.5 0.6 broadcast_in_dim.26
  16.2 4.9 %all-to-all-start.1 = ((f32[4,32,128]{2,1,0:T(8,128)}), f32[4,32,128]{2,1,0:T(8,128)S(1)}, u32[]{:S(2)}, u32[]{:S(2)}) async-start(f32[4,32,128]{2,1,0:T(8,128)} %broadcast_in_dim.26), calls=%async_computation.1 | async-start | bytes 131072 | tf_op jit(solution)/shard_map/all_to_all | solution.py:341
  21.1 0.0 copy-start.24
  21.1 0.0 copy-start.25
  21.1 0.0 copy-start.26
  21.1 0.0 copy-start.2
  21.1 5.7 %all-to-all-done.1.refs_4_ = f32[4,32,128]{2,1,0:T(8,128)S(1)} async-done(((f32[4,32,128]{2,1,0:T(8,128)}), f32[4,32,128]{2,1,0:T(8,128)S(1)}, u32[]{:S(2)}, u32[]{:S(2)}) %all-to-all-start.1) | async-done | bytes 65568 | tf_op jit(solution)/shard_map/all_to_all | solution.py:341
  26.8 0.6 copy-done.16
  27.5 0.7 shard_map.166
  28.2 0.0 copy-start.11
  28.2 0.6 copy-done.11
  28.8 0.7 broadcast_in_dim.30
  29.5 3.4 %all-to-all-start.2 = ((f32[8,24,128]{2,1,0:T(8,128)}), f32[8,24,128]{2,1,0:T(8,128)S(1)}, u32[]{:S(2)}, u32[]{:S(2)}) async-start(f32[8,24,128]{2,1,0:T(8,128)} %broadcast_in_dim.30), calls=%async_computation.2 | async-start | bytes 196608 | tf_op jit(solution)/shard_map/all_to_all | solution.py:341
  32.8 1.9 %collective-permute-start.1 = (f32[72,128]{1,0:T(8,128)S(1)}, f32[72,128]{1,0:T(8,128)S(1)}, u32[]{:S(2)}, u32[]{:S(2)}) collective-permute-start(f32[72,128]{1,0:T(8,128)S(1)} %get-tuple-element.57), channel_id=1, source_target_pairs={{0,1},{1,0},{2,3},{3,2},{4,5},{5,4},{6,7},{7,6},{8,9},{9,8},{10,11... | collective-permute-start | bytes 110600 | tf_op jit(solution)/shard_map/ppermute | solution.py:336
  34.7 2.8 %all-to-all-done.2 = f32[8,24,128]{2,1,0:T(8,128)S(1)} async-done(((f32[8,24,128]{2,1,0:T(8,128)}), f32[8,24,128]{2,1,0:T(8,128)S(1)}, u32[]{:S(2)}, u32[]{:S(2)}) %all-to-all-start.2) | async-done | bytes 98336 | tf_op jit(solution)/shard_map/all_to_all | solution.py:341
  37.6 0.6 broadcast_in_dim.31
  38.3 3.3 %all-to-all-start.3 = ((f32[4,24,128]{2,1,0:T(8,128)}), f32[4,24,128]{2,1,0:T(8,128)S(1)}, u32[]{:S(2)}, u32[]{:S(2)}) async-start(f32[4,24,128]{2,1,0:T(8,128)} %broadcast_in_dim.31), calls=%async_computation.3 | async-start | bytes 98304 | tf_op jit(solution)/shard_map/all_to_all | solution.py:341
  41.6 5.6 %all-to-all-done.3.refs_14_ = f32[4,24,128]{2,1,0:T(8,128)S(1)} async-done(((f32[4,24,128]{2,1,0:T(8,128)}), f32[4,24,128]{2,1,0:T(8,128)S(1)}, u32[]{:S(2)}, u32[]{:S(2)}) %all-to-all-start.3) | async-done | bytes 49184 | tf_op jit(solution)/shard_map/all_to_all | solution.py:341
  47.2 0.7 copy-done.22
  47.9 0.8 copy-done.12
  48.8 0.8 shard_map.167
  49.5 0.0 copy-start.7
  49.5 0.6 copy-done.7
  50.2 0.6 copy-done.9
  50.8 0.6 copy-done.19
  51.4 0.5 copy-done.27
  51.9 0.5 copy-done.32
  52.4 0.6 broadcast_in_dim.32
  53.1 3.4 %all-to-all-start.4 = ((f32[8,24,128]{2,1,0:T(8,128)}), f32[8,24,128]{2,1,0:T(8,128)S(1)}, u32[]{:S(2)}, u32[]{:S(2)}) async-start(f32[8,24,128]{2,1,0:T(8,128)} %broadcast_in_dim.32), calls=%async_computation.4 | async-start | bytes 196608 | tf_op jit(solution)/shard_map/all_to_all | solution.py:341
  56.4 1.9 %collective-permute-start.2 = (f32[72,128]{1,0:T(8,128)S(1)}, f32[72,128]{1,0:T(8,128)S(1)}, u32[]{:S(2)}, u32[]{:S(2)}) collective-permute-start(f32[72,128]{1,0:T(8,128)S(1)} %get-tuple-element.67), channel_id=1, source_target_pairs={{0,1},{1,0},{2,3},{3,2},{4,5},{5,4},{6,7},{7,6},{8,9},{9,8},{10,11... | collective-permute-start | bytes 110600 | tf_op jit(solution)/shard_map/ppermute | solution.py:336
  58.4 2.8 %all-to-all-done.4 = f32[8,24,128]{2,1,0:T(8,128)S(1)} async-done(((f32[8,24,128]{2,1,0:T(8,128)}), f32[8,24,128]{2,1,0:T(8,128)S(1)}, u32[]{:S(2)}, u32[]{:S(2)}) %all-to-all-start.4) | async-done | bytes 98336 | tf_op jit(solution)/shard_map/all_to_all | solution.py:341
  61.3 0.6 broadcast_in_dim.33
  61.9 3.3 %all-to-all-start.5 = ((f32[4,24,128]{2,1,0:T(8,128)}), f32[4,24,128]{2,1,0:T(8,128)S(1)}, u32[]{:S(2)}, u32[]{:S(2)}) async-start(f32[4,24,128]{2,1,0:T(8,128)} %broadcast_in_dim.33), calls=%async_computation.5 | async-start | bytes 98304 | tf_op jit(solution)/shard_map/all_to_all | solution.py:341
  65.2 5.6 %all-to-all-done.5.refs_16_ = f32[4,24,128]{2,1,0:T(8,128)S(1)} async-done(((f32[4,24,128]{2,1,0:T(8,128)}), f32[4,24,128]{2,1,0:T(8,128)S(1)}, u32[]{:S(2)}, u32[]{:S(2)}) %all-to-all-start.5) | async-done | bytes 49184 | tf_op jit(solution)/shard_map/all_to_all | solution.py:341
  70.9 0.7 copy-done.20
  71.6 0.8 copy-done.8
  72.4 0.8 copy-done.10
  73.2 0.8 shard_map.168
  74.0 0.6 copy-done.3
  74.6 0.6 copy-done.5
  75.3 0.6 copy-done.17
  75.9 0.5 copy-done.30
  76.4 0.6 broadcast_in_dim.34
  77.0 3.4 %all-to-all-start.6 = ((f32[8,24,128]{2,1,0:T(8,128)}), f32[8,24,128]{2,1,0:T(8,128)S(1)}, u32[]{:S(2)}, u32[]{:S(2)}) async-start(f32[8,24,128]{2,1,0:T(8,128)} %broadcast_in_dim.34), calls=%async_computation.6 | async-start | bytes 196608 | tf_op jit(solution)/shard_map/all_to_all | solution.py:341
  80.4 1.9 %collective-permute-start.3 = (f32[72,128]{1,0:T(8,128)S(1)}, f32[72,128]{1,0:T(8,128)S(1)}, u32[]{:S(2)}, u32[]{:S(2)}) collective-permute-start(f32[72,128]{1,0:T(8,128)S(1)} %get-tuple-element.77), channel_id=1, source_target_pairs={{0,1},{1,0},{2,3},{3,2},{4,5},{5,4},{6,7},{7,6},{8,9},{9,8},{10,11... | collective-permute-start | bytes 110600 | tf_op jit(solution)/shard_map/ppermute | solution.py:336
  82.3 2.8 %all-to-all-done.6 = f32[8,24,128]{2,1,0:T(8,128)S(1)} async-done(((f32[8,24,128]{2,1,0:T(8,128)}), f32[8,24,128]{2,1,0:T(8,128)S(1)}, u32[]{:S(2)}, u32[]{:S(2)}) %all-to-all-start.6) | async-done | bytes 98336 | tf_op jit(solution)/shard_map/all_to_all | solution.py:341
  85.2 0.6 broadcast_in_dim.35
  85.8 3.3 %all-to-all-start.7 = ((f32[4,24,128]{2,1,0:T(8,128)}), f32[4,24,128]{2,1,0:T(8,128)S(1)}, u32[]{:S(2)}, u32[]{:S(2)}) async-start(f32[4,24,128]{2,1,0:T(8,128)} %broadcast_in_dim.35), calls=%async_computation.7 | async-start | bytes 98304 | tf_op jit(solution)/shard_map/all_to_all | solution.py:341
  89.1 0.0 copy-start.4
  89.2 0.0 copy-start.14
  89.2 5.6 %all-to-all-done.7.refs_16_ = f32[4,24,128]{2,1,0:T(8,128)S(1)} async-done(((f32[4,24,128]{2,1,0:T(8,128)}), f32[4,24,128]{2,1,0:T(8,128)S(1)}, u32[]{:S(2)}, u32[]{:S(2)}) %all-to-all-start.7) | async-done | bytes 49184 | tf_op jit(solution)/shard_map/all_to_all | solution.py:341
  94.8 0.6 copy-done.31
  95.4 1.3 %shard_map.169 = (f32[1024,128]{1,0:T(8,128)}, f32[1,128]{1,0:T(1,128)}, f32[64,128]{1,0:T(8,128)}, f32[64,256]{1,0:T(8,128)}) custom-call(f32[16,64,128]{2,1,0:T(8,128)S(1)} %get-tuple-element.43.refs_0_, f32[64,128]{1,0:T(8,128)S(1)} %copy-done, f32[16,128]{1,0:T(8,128)S(1)} %copy-done.2, f32[1,256]{1,0:T(1,128)S(1)} %bitcast.96, ...), custom_call_target="tpu_custom_call" | custom-call | tf_op jit(solution)/shard_map/pallas_call | solution.py:317
  (70 shorter events, 0.3 us)
Async XLA Ops:
  0.6 0.7 copy-start.35
  0.6 0.7 copy-start.36
  0.7 0.7 copy-start.29
  0.7 0.7 copy-start.34
  1.3 1.0 %copy-start.1 = (f32[64,16,128]{2,1,0:T(8,128)S(1)}, f32[64,16,128]{2,1,0:T(8,128)}, u32[]{:S(2)}) copy-start(f32[64,16,128]{2,1,0:T(8,128)} %param.14) | copy-start | bytes 1572868
  2.4 0.7 copy-start.13
  3.1 0.8 copy-start.15
  5.4 10.1 %all-to-all-start = ((f32[8,32,128]{2,1,0:T(8,128)}), f32[8,32,128]{2,1,0:T(8,128)S(1)}, u32[]{:S(2)}, u32[]{:S(2)}) async-start(f32[8,32,128]{2,1,0:T(8,128)} %broadcast_in_dim.25), calls=%async_computation | async-start | bytes 262144 | tf_op jit(solution)/shard_map/all_to_all | solution.py:341
  10.6 10.5 %collective-permute-start = (f32[72,128]{1,0:T(8,128)S(1)}, f32[72,128]{1,0:T(8,128)S(1)}, u32[]{:S(2)}, u32[]{:S(2)}) collective-permute-start(f32[72,128]{1,0:T(8,128)S(1)} %get-tuple-element.45), channel_id=1, source_target_pairs={{0,1},{1,0},{2,3},{3,2},{4,5},{5,4},{6,7},{7,6},{8,9},{9,8},{10,11... | collective-permute-start | bytes 110600 | tf_op jit(solution)/shard_map/ppermute | solution.py:336
  16.2 10.6 %all-to-all-start.1 = ((f32[4,32,128]{2,1,0:T(8,128)}), f32[4,32,128]{2,1,0:T(8,128)S(1)}, u32[]{:S(2)}, u32[]{:S(2)}) async-start(f32[4,32,128]{2,1,0:T(8,128)} %broadcast_in_dim.26), calls=%async_computation.1 | async-start | bytes 131072 | tf_op jit(solution)/shard_map/all_to_all | solution.py:341
  21.0 5.7 %copy-start = (f32[64,128]{1,0:T(8,128)S(1)}, f32[64,128]{1,0:T(8,128)}, u32[]{:S(2)}) copy-start(f32[64,128]{1,0:T(8,128)} %refs_1_.7) | copy-start | bytes 98308
  21.0 5.7 %copy-start.23 = (s32[2,256]{1,0:T(2,128)S(1)}, s32[2,256]{1,0:T(2,128)}, u32[]{:S(2)}) copy-start(s32[2,256]{1,0:T(2,128)} %refs_6_.1) | copy-start | bytes 6148
  21.1 5.7 %copy-start.24 = (f32[256]{0:T(256)S(1)}, f32[256]{0:T(256)}, u32[]{:S(2)}) copy-start(f32[256]{0:T(256)} %param.20) | copy-start | bytes 3076
  21.1 5.7 %copy-start.25 = (s32[256]{0:T(256)S(1)}, s32[256]{0:T(256)}, u32[]{:S(2)}) copy-start(s32[256]{0:T(256)} %param.24) | copy-start | bytes 3076
  21.1 5.7 %copy-start.26 = (f32[256]{0:T(256)S(1)}, f32[256]{0:T(256)}, u32[]{:S(2)}) copy-start(f32[256]{0:T(256)} %param.26) | copy-start | bytes 3076
  21.1 5.7 %copy-start.2 = (f32[16,128]{1,0:T(8,128)S(1)}, f32[16,128]{1,0:T(8,128)}, u32[]{:S(2)}) copy-start(f32[16,128]{1,0:T(8,128)} %refs_2_.7) | copy-start | bytes 24580
  26.8 0.7 copy-start.16
  28.2 0.6 copy-start.11
  28.8 0.7 copy-start.21
  29.5 8.1 %all-to-all-start.2 = ((f32[8,24,128]{2,1,0:T(8,128)}), f32[8,24,128]{2,1,0:T(8,128)S(1)}, u32[]{:S(2)}, u32[]{:S(2)}) async-start(f32[8,24,128]{2,1,0:T(8,128)} %broadcast_in_dim.30), calls=%async_computation.2 | async-start | bytes 196608 | tf_op jit(solution)/shard_map/all_to_all | solution.py:341
  32.8 8.7 %collective-permute-start.1 = (f32[72,128]{1,0:T(8,128)S(1)}, f32[72,128]{1,0:T(8,128)S(1)}, u32[]{:S(2)}, u32[]{:S(2)}) collective-permute-start(f32[72,128]{1,0:T(8,128)S(1)} %get-tuple-element.57), channel_id=1, source_target_pairs={{0,1},{1,0},{2,3},{3,2},{4,5},{5,4},{6,7},{7,6},{8,9},{9,8},{10,11... | collective-permute-start | bytes 110600 | tf_op jit(solution)/shard_map/ppermute | solution.py:336
  38.3 8.9 %all-to-all-start.3 = ((f32[4,24,128]{2,1,0:T(8,128)}), f32[4,24,128]{2,1,0:T(8,128)S(1)}, u32[]{:S(2)}, u32[]{:S(2)}) async-start(f32[4,24,128]{2,1,0:T(8,128)} %broadcast_in_dim.31), calls=%async_computation.3 | async-start | bytes 98304 | tf_op jit(solution)/shard_map/all_to_all | solution.py:341
  47.2 0.7 copy-start.22
  47.9 0.8 copy-start.12
  49.5 0.6 copy-start.7
  50.2 0.6 copy-start.9
  50.8 0.6 copy-start.19
  51.4 0.5 copy-start.27
  51.9 0.5 copy-start.32
  53.1 8.1 %all-to-all-start.4 = ((f32[8,24,128]{2,1,0:T(8,128)}), f32[8,24,128]{2,1,0:T(8,128)S(1)}, u32[]{:S(2)}, u32[]{:S(2)}) async-start(f32[8,24,128]{2,1,0:T(8,128)} %broadcast_in_dim.32), calls=%async_computation.4 | async-start | bytes 196608 | tf_op jit(solution)/shard_map/all_to_all | solution.py:341
  56.4 8.7 %collective-permute-start.2 = (f32[72,128]{1,0:T(8,128)S(1)}, f32[72,128]{1,0:T(8,128)S(1)}, u32[]{:S(2)}, u32[]{:S(2)}) collective-permute-start(f32[72,128]{1,0:T(8,128)S(1)} %get-tuple-element.67), channel_id=1, source_target_pairs={{0,1},{1,0},{2,3},{3,2},{4,5},{5,4},{6,7},{7,6},{8,9},{9,8},{10,11... | collective-permute-start | bytes 110600 | tf_op jit(solution)/shard_map/ppermute | solution.py:336
  61.9 8.9 %all-to-all-start.5 = ((f32[4,24,128]{2,1,0:T(8,128)}), f32[4,24,128]{2,1,0:T(8,128)S(1)}, u32[]{:S(2)}, u32[]{:S(2)}) async-start(f32[4,24,128]{2,1,0:T(8,128)} %broadcast_in_dim.33), calls=%async_computation.5 | async-start | bytes 98304 | tf_op jit(solution)/shard_map/all_to_all | solution.py:341
  70.8 0.7 copy-start.20
  70.8 0.7 copy-start.28
  70.9 0.7 copy-start.33
  71.5 0.8 copy-start.8
  72.4 0.8 copy-start.10
  74.0 0.6 copy-start.3
  74.6 0.6 copy-start.5
  75.3 0.6 copy-start.17
  75.9 0.5 copy-start.30
  77.0 8.1 %all-to-all-start.6 = ((f32[8,24,128]{2,1,0:T(8,128)}), f32[8,24,128]{2,1,0:T(8,128)S(1)}, u32[]{:S(2)}, u32[]{:S(2)}) async-start(f32[8,24,128]{2,1,0:T(8,128)} %broadcast_in_dim.34), calls=%async_computation.6 | async-start | bytes 196608 | tf_op jit(solution)/shard_map/all_to_all | solution.py:341
  80.4 8.7 %collective-permute-start.3 = (f32[72,128]{1,0:T(8,128)S(1)}, f32[72,128]{1,0:T(8,128)S(1)}, u32[]{:S(2)}, u32[]{:S(2)}) collective-permute-start(f32[72,128]{1,0:T(8,128)S(1)} %get-tuple-element.77), channel_id=1, source_target_pairs={{0,1},{1,0},{2,3},{3,2},{4,5},{5,4},{6,7},{7,6},{8,9},{9,8},{10,11... | collective-permute-start | bytes 110600 | tf_op jit(solution)/shard_map/ppermute | solution.py:336
  85.8 8.9 %all-to-all-start.7 = ((f32[4,24,128]{2,1,0:T(8,128)}), f32[4,24,128]{2,1,0:T(8,128)S(1)}, u32[]{:S(2)}, u32[]{:S(2)}) async-start(f32[4,24,128]{2,1,0:T(8,128)} %broadcast_in_dim.35), calls=%async_computation.7 | async-start | bytes 98304 | tf_op jit(solution)/shard_map/all_to_all | solution.py:341
  89.1 5.7 %copy-start.4 = (f32[64,256]{1,0:T(8,128)S(1)}, f32[64,256]{1,0:T(8,128)}, u32[]{:S(2)}) copy-start(f32[64,256]{1,0:T(8,128)} %copy-done.3) | copy-start | bytes 196612
  89.1 5.7 %copy-start.6 = (f32[64,256]{1,0:T(8,128)S(1)}, f32[64,256]{1,0:T(8,128)}, u32[]{:S(2)}) copy-start(f32[64,256]{1,0:T(8,128)} %copy-done.5) | copy-start | bytes 196612
  89.1 5.6 %copy-start.18 = (f32[16,128]{1,0:T(8,128)S(1)}, f32[16,128]{1,0:T(8,128)}, u32[]{:S(2)}) copy-start(f32[16,128]{1,0:T(8,128)} %copy-done.17) | copy-start | bytes 24580
  89.2 5.6 %copy-start.14 = (s32[1,2048]{1,0:T(1,128)S(1)}, s32[1,2048]{1,0:T(1,128)}, u32[]{:S(2)}) copy-start(s32[1,2048]{1,0:T(1,128)} %param.18) | copy-start | bytes 24580
  94.8 0.7 copy-start.31

commit v5 on v3

v5 whole, which is shorter than its diff:
```python
import functools

import jax
import jax.numpy as jnp
from jax import lax
from jax.experimental import pallas as pl
from jax.experimental.pallas import tpu as pltpu
from jax.sharding import PartitionSpec as P

ITERS = 4
EPSILON = 1e-06
LANES = 128
VMEM_BYTES = 24 * 1024 * 1024
SQUARES = 3


def split3(value):
    high = value.astype(jnp.bfloat16)
    rest = value - high.astype(jnp.float32)
    middle = rest.astype(jnp.bfloat16)
    low = (rest - middle.astype(jnp.float32)).astype(jnp.bfloat16)
    return jnp.concatenate([high, middle, low], axis=0)


def dot3(value, matrix, transposed):
    rows = value.shape[0]
    contract = ((1,), (1 if transposed else 0,))
    product = lax.dot_general(
        split3(value), matrix, (contract, ((), ())), preferred_element_type=jnp.float32
    )
    return product[:rows] + product[rows : 2 * rows] + product[2 * rows :]


def row_sum(value):
    return jnp.sum(value, axis=0, keepdims=True)


def fold_lanes(row):
    total = row[:, :LANES]
    for start in range(LANES, row.shape[1], LANES):
        total = total + row[:, start : start + LANES]
    return total


def owned_one_hots(owner_ref, tech_count, node_count):
    owned = owner_ref[pl.ds(lax.axis_index("hours"), 1), :]
    shape_t = (tech_count, owned.shape[1])
    shape_n = (node_count, owned.shape[1])
    tech = lax.broadcasted_iota(jnp.int32, shape_t, 0) == owned // node_count
    node = lax.broadcasted_iota(jnp.int32, shape_n, 0) == owned % node_count
    return tech, node.astype(jnp.float32).astype(jnp.bfloat16)


def incidence(start, end, count):
    node = lax.broadcasted_iota(jnp.int32, (count, start.shape[1]), 0)
    maps = (node == end).astype(jnp.float32) - (node == start).astype(jnp.float32)
    return maps.astype(jnp.bfloat16)


def halo_at(sizes):
    return sizes["techs"] + SQUARES


def sums_rows(sizes):
    return (halo_at(sizes) + 2 * sizes["units"] // LANES + 7) // 8 * 8


def write_halo(sizes, sums_ref, store_new):
    halo, span, rows = halo_at(sizes), sizes["units"] // LANES, sizes["rows"]
    for i in range(span):
        part = slice(i * LANES, (i + 1) * LANES)
        sums_ref[halo + i : halo + i + 1, :] = store_new[:1, part]
        sums_ref[halo + span + i : halo + span + i + 1, :] = store_new[rows - 1 :, part]
    used, end = halo + 2 * span, sums_rows(sizes)
    if used < end:
        sums_ref[used:end, :] = jnp.zeros((end - used, LANES), jnp.float32)


def regions_kernel(sizes, price, ends, limit, pairs_ref, region_ref, ends_ref, limit_ref, sems):
    rows, nodes, slots, regions = (sizes[name] for name in ("rows", "nodes", "slots", "regions"))
    copies = [
        pltpu.make_async_copy(ends, ends_ref, sems.at[0]),
        pltpu.make_async_copy(limit, limit_ref, sems.at[1]),
        pltpu.make_async_copy(price, region_ref.at[pl.ds(0, rows)], sems.at[2]),
    ]
    for copy in copies:
        copy.start()
    own = lax.axis_index("region")
    width = slots // regions
    slot = lax.broadcasted_iota(jnp.int32, (1, slots), 1)
    pair = slot // width
    in_use = jnp.zeros((1, slots), jnp.int32)
    for target in range(regions):
        in_use = jnp.where(pair == target, pairs_ref[0, target], in_use)
    place = lax.broadcasted_iota(jnp.int32, (slots, regions * slots), 1) == (
        own * slots + lax.broadcasted_iota(jnp.int32, (slots, regions * slots), 0)
    )
    place = place.astype(jnp.float32).astype(jnp.bfloat16)
    copies[0].wait()
    copies[1].wait()
    bound = jnp.where(slot % width < in_use, limit_ref[...], 0.0)
    start = ends_ref[0:1, :] + own * nodes
    end = ends_ref[1:2, :] + pair * nodes
    info = jnp.concatenate(
        [start.astype(jnp.float32), end.astype(jnp.float32), bound, jnp.zeros((13, slots), jnp.float32)],
        axis=0,
    )
    info = dot3(info, place, False)
    for chunk in range(regions * slots // LANES):
        region_ref[rows + 8 * chunk : rows + 8 * chunk + 8, :] = info[
            :8, chunk * LANES : (chunk + 1) * LANES
        ]
    copies[2].wait()


def start_kernel(sizes, sources, outs, *refs):
    given = dict(zip(sources, refs[: len(sources)]))
    gives = dict(zip(outs, refs[len(sources) : len(sources) + len(outs)]))
    held = dict(zip(START_SCRATCH, refs[len(sources) + len(outs) : -1]))
    sems = refs[-1]
    targets = {name: gives[name] if name in gives else held[name] for name in sources}
    copies = {
        name: pltpu.make_async_copy(given[name], targets[name], sems.at[i])
        for i, name in enumerate(sources)
    }
    for copy in copies.values():
        copy.start()
    rows, techs, nodes = sizes["rows"], sizes["techs"], sizes["nodes"]
    lines = sizes["lines"]
    for name in ("line_ends", "store_node", "line_limit", "store_power", "price"):
        copies[name].wait()
    line_ends, stores = held["line_ends"][...], held["store_node"][...]
    start = jnp.concatenate([line_ends[0:1], jnp.full_like(stores, -1)], axis=1)
    end = jnp.concatenate([line_ends[1:2], stores], axis=1)
    maps = incidence(start, end, nodes)
    limits = jnp.concatenate([held["line_limit"][...], held["store_power"][...]], axis=1)
    gives["maps_local"][...] = maps
    gives["limits_local"][...] = limits
    prices = held["price"][...]
    flows = jnp.clip(-0.5 * dot3(prices, maps, False), -limits, limits)
    gives["flows_local"][...] = flows
    store_new = (1.0 / 3.0) * (2.0 * flows[:, lines:])
    gives["store_duals"][...] = store_new
    primal_row = fold_lanes(row_sum(flows * flows))
    dual_row = fold_lanes(row_sum(store_new * store_new))
    balance = dot3(2.0 * flows, maps, True)
    copies["demand"].wait()
    balance = balance - gives["demand"][...]
    copies["gen_cost"].wait()
    gen_cost = gives["gen_cost"][...]
    copies["availability"].wait()
    acc = jnp.zeros((rows, nodes), jnp.float32)
    weights = jnp.zeros((techs, nodes), jnp.float32)
    for hour in range(rows):
        weights = weights + held["availability"][hour * techs : (hour + 1) * techs, :]
    for tech in range(techs):
        avail = held["availability"][pl.ds(tech, rows, stride=techs), :]
        gives["available"][tech] = avail
        dispatch = jnp.maximum(-0.5 * (gen_cost[tech : tech + 1] + prices), 0.0)
        gives["dispatch"][tech] = dispatch
        dispatch_bar = 2.0 * dispatch
        balance = balance + dispatch_bar
        duals = jnp.maximum(0.5 * dispatch_bar, 0.0)
        acc = acc + dispatch * dispatch
        gives["sums"][tech : tech + 1, :] = row_sum(avail * duals)
    gives["balance"][...] = balance
    squares = row_sum(acc)
    copies["cap_cost"].wait()
    copies["owner"].wait()
    cost = held["cap_cost"][...]
    negative = jnp.sum((cost < 0.0).astype(jnp.float32), axis=1, keepdims=True)
    write_halo(sizes, gives["sums"], store_new)
    gives["sums"][techs : techs + SQUARES, :] = jnp.concatenate(
        [primal_row + squares, dual_row + squares, jnp.broadcast_to(negative, (1, LANES))], axis=0
    )
    tech_hot, node_hot = owned_one_hots(gives["owner"], techs, nodes)
    first = sums_rows(sizes)
    gives["sums"][first : first + techs, :] = weights
    gives["sums"][first + techs : first + 2 * techs, :] = dot3(
        jnp.where(tech_hot, cost, 0.0), node_hot, True
    )
    for name in ("store_energy",):
        copies[name].wait()


START_SCRATCH = (
    "availability",
    "price",
    "cap_cost",
    "line_ends",
    "line_limit",
    "store_node",
    "store_power",
)


def close_kernel(
    sizes,
    gathered,
    balance_ref,
    sums_in_ref,
    maps_ref,
    limits_ref,
    flows_ref,
    region_ref,
    sums_ref,
):
    rows, techs, nodes, slots, regions = (
        sizes[name] for name in ("rows", "techs", "nodes", "slots", "regions")
    )
    own = lax.axis_index("region")
    chunks = []
    for chunk in range(regions * slots // LANES):
        at = slice(rows + 8 * chunk, rows + 8 * chunk + 8)
        part = gathered[0, at, :]
        for region in range(1, regions):
            part = part + gathered[region, at, :]
        chunks.append(part)
    info = jnp.concatenate(chunks, axis=1) if len(chunks) > 1 else chunks[0]
    maps_ref[...] = incidence(
        info[0:1].astype(jnp.int32), info[1:2].astype(jnp.int32), regions * nodes
    )
    limits = info[2:3]
    limits_ref[...] = limits
    prices_all = jnp.concatenate([gathered[region, :rows, :] for region in range(regions)], axis=1)
    flows = jnp.clip(-0.5 * dot3(prices_all, maps_ref[...], False), -limits, limits)
    flows_ref[...] = flows
    maps_own = maps_ref[pl.ds(pl.multiple_of(own * nodes, nodes), nodes), :]
    balance = balance_ref[...] + dot3(2.0 * flows, maps_own, True)
    step_up = (1.0 / (techs + 8.0)) * balance
    region_ref[:rows, :] = gathered[own, :rows, :] + step_up
    change = row_sum(flows * flows)
    slot = lax.broadcasted_iota(jnp.int32, change.shape, 1)
    primal = fold_lanes(jnp.where(slot // slots == own, change, 0.0))
    more = jnp.concatenate(
        [primal, row_sum(step_up * step_up), jnp.zeros((SQUARES - 2, LANES), jnp.float32)], axis=0
    )
    sums_ref[...] = sums_in_ref[...]
    squares = sums_in_ref[techs : techs + SQUARES, :] + more
    sums_ref[techs : techs + SQUARES, :] = squares
    region_ref[rows:, :] = jnp.concatenate(
        [squares, jnp.zeros((8 - SQUARES, LANES), jnp.float32)], axis=0
    )


def neighbour_rows(sizes, given, hour_index):
    span = sizes["units"] // LANES

    def row_of(name, offset):
        return jnp.concatenate(
            [given[name][offset + i : offset + i + 1, :] for i in range(span)], axis=1
        )

    if "totals" in given:
        return row_of("next_row", 0), row_of("prev_row", 0)
    first = halo_at(sizes)
    last = first + span
    core, x_place, slab = hour_index % 2, hour_index // 2 % 2, hour_index // 4 % 2
    next_row = jnp.where(slab == 0, row_of("near", first), row_of("far", first))
    prev_row = jnp.where(slab == 0, row_of("far", last), row_of("near", last))
    next_row = jnp.where(x_place == 0, row_of("across", first), next_row)
    prev_row = jnp.where(x_place == 0, prev_row, row_of("across", last))
    next_row = jnp.where(core == 0, row_of("partner", first), next_row)
    prev_row = jnp.where(core == 0, prev_row, row_of("partner", last))
    return next_row, prev_row


def total_of(parts):
    if "totals" in parts:
        return parts["totals"][...]
    return (parts["slab"][...] + parts["near"][...]) + (parts["middle"][...] + parts["far"][...])


def sweep_kernel(sizes, iteration, names_in, names_out, *refs):
    rows, techs, nodes, slots, regions, lines, units = (
        sizes[name] for name in ("rows", "techs", "nodes", "slots", "regions", "lines", "units")
    )
    second = iteration == 1
    last = iteration == ITERS - 1
    given = dict(zip(names_in, refs[: len(names_in)]))
    gives = dict(zip(names_out, refs[len(names_in) :]))
    own = lax.axis_index("region")
    hour_index = lax.axis_index("hours")
    gathered = given["gathered"]

    sums = total_of(given)
    squares = jnp.sum(sums[techs : techs + 2], axis=1, keepdims=True)
    old_weight = jnp.ones((1, 1), jnp.float32) if second else given["weight"][...][:, :1]
    weight = jnp.sqrt(
        old_weight * jnp.sqrt((squares[1:2] + EPSILON) / (squares[0:1] + EPSILON))
    )
    primal_step = 0.5 / weight
    if second:
        first = sums_rows(sizes)
        col_weight, cost = sums[first : first + techs], sums[first + techs : first + 2 * techs]
        gives["col_weight"][...] = col_weight
        gives["cost"][...] = cost
        capacity = jnp.maximum(-cost / col_weight, 0.0)
        first_bar = 2.0 * capacity
    else:
        col_weight, cost = given["col_weight"][...], given["cost"][...]
        capacity = given["capacity"][...]
    capacity_new = jnp.maximum(capacity - (cost - sums[:techs]) / (weight * col_weight), 0.0)
    capacity_bar = 2.0 * capacity_new - capacity

    prices_all = jnp.concatenate([gathered[region, :rows, :] for region in range(regions)], axis=1)
    prices = gathered[own, :rows, :]
    maps_local = given["maps_local"][...]
    slope_local = dot3(prices, maps_local, False)
    slope_cross = dot3(prices_all, given["maps_cross"][...], False)

    energy = given["store_energy"][...]
    row_id = lax.broadcasted_iota(jnp.int32, (rows, units), 0)
    next_row, prev_row = neighbour_rows(sizes, given, hour_index)
    store_duals = given["store_duals"][...]
    next_duals = jnp.where(row_id == rows - 1, next_row, pltpu.roll(store_duals, rows - 1, 0))
    if second:
        charge = jnp.zeros((rows, units), jnp.float32)
        charge_before = jnp.zeros((1, units), jnp.float32)
    else:
        charge = given["charge"][...]
        charge_before = given["charge_before"][...]
    charge_new = jnp.clip(charge - primal_step * (store_duals - next_duals), 0.0, energy)
    gives["charge"][...] = charge_new

    primal_row = jnp.zeros((1, LANES), jnp.float32)
    bars = []
    for name, slope, low, high in (
        ("flows_local", slope_local, 0, lines),
        ("flows_local", slope_local, lines, lines + units),
        ("flows_cross", slope_cross, 0, regions * slots),
    ):
        slope = slope[:, low:high]
        if low:
            slope = slope + store_duals
        bound = given[name.replace("flows", "limits")][:, low:high]
        old = given[name][:, low:high]
        new = jnp.clip(old - primal_step * slope, -bound, bound)
        bars.append(2.0 * new - old)
        if not last:
            gives[name][:, low:high] = new
            change = row_sum((new - old) ** 2)
            if name == "flows_cross":
                slot = lax.broadcasted_iota(jnp.int32, change.shape, 1)
                change = jnp.where(slot // slots == own, change, 0.0)
            primal_row = primal_row + fold_lanes(change)
    maps_own = given["maps_cross"][pl.ds(pl.multiple_of(own * nodes, nodes), nodes), :]
    balance = dot3(jnp.concatenate(bars[:2], axis=1), maps_local, True) - given["demand"][...]
    balance = balance + dot3(bars[2], maps_own, True)

    gen_cost = given["gen_cost"][...]
    half_weight = weight / 2.0
    primal_acc = jnp.zeros((rows, nodes), jnp.float32)
    dual_acc = jnp.zeros((rows, nodes), jnp.float32)
    for tech in range(techs):
        slope = gen_cost[tech : tech + 1] + prices
        dispatch = given["dispatch"][tech]
        avail = given["available"][tech]
        if second:
            duals = jnp.maximum(0.5 * (2.0 * dispatch - avail * first_bar[tech : tech + 1]), 0.0)
        else:
            duals = given["cap_duals"][tech]
        dispatch_new = jnp.maximum(dispatch - primal_step * (slope + duals), 0.0)
        dispatch_bar = 2.0 * dispatch_new - dispatch
        balance = balance + dispatch_bar
        if last:
            gives["dispatch"][pl.ds(tech, rows, stride=techs), :] = dispatch_new
            continue
        gives["dispatch"][tech] = dispatch_new
        cap_rows = dispatch_bar - avail * capacity_bar[tech : tech + 1]
        primal_acc = primal_acc + (dispatch_new - dispatch) ** 2
        duals_new = jnp.maximum(duals + half_weight * cap_rows, 0.0)
        dual_acc = dual_acc + (duals_new - duals) ** 2
        gives["cap_duals"][tech] = duals_new
        gives["sums"][tech : tech + 1, :] = row_sum(avail * duals_new)

    step_up = weight / (techs + 8.0) * balance
    if last:
        gives["prices"][...] = prices + step_up
        tech_hot, node_hot = owned_one_hots(given["owner"], techs, nodes)
        chosen = dot3(capacity_new, node_hot, False)
        gives["capacity"][...] = row_sum(jnp.where(tech_hot, chosen, 0.0))
        return
    gives["region"][:rows, :] = prices + step_up
    gives["weight"][...] = jnp.broadcast_to(weight, (1, LANES))
    gives["capacity"][...] = capacity_new
    charge_bar = 2.0 * charge_new - charge
    before_new = jnp.clip(charge_before - primal_step * (prev_row - store_duals[0:1]), 0.0, energy)
    gives["charge_before"][...] = before_new
    before_bar = 2.0 * before_new - charge_before
    shifted_bar = jnp.where(row_id == 0, before_bar, pltpu.roll(charge_bar, 1, 0))
    store_step = weight / 3.0 * (charge_bar - shifted_bar + bars[1])
    store_new = store_duals + store_step
    gives["store_duals"][...] = store_new
    primal_row = primal_row + row_sum(primal_acc) + fold_lanes(row_sum((charge_new - charge) ** 2))
    primal_row = primal_row + jnp.where(
        hour_index == 0, row_sum((capacity_new - capacity) ** 2), 0.0
    )
    dual_row = row_sum(dual_acc + step_up * step_up) + fold_lanes(row_sum(store_step * store_step))
    squares = jnp.concatenate(
        [primal_row, dual_row, jnp.zeros((SQUARES - 2, LANES), jnp.float32)], axis=0
    )
    gives["region"][rows:, :] = jnp.concatenate(
        [squares, jnp.zeros((8 - SQUARES, LANES), jnp.float32)], axis=0
    )
    gives["sums"][techs : techs + SQUARES, :] = squares
    write_halo(sizes, gives["sums"], store_new)


def call(kernel, arguments, shapes, scratch=(), spaces=None, cost=None):
    spaces = spaces or [pltpu.VMEM] * len(arguments)
    return pl.pallas_call(
        kernel,
        out_shape=shapes,
        in_specs=[pl.BlockSpec(memory_space=space) for space in spaces],
        out_specs=[pl.BlockSpec(memory_space=pltpu.VMEM)] * len(shapes),
        scratch_shapes=scratch,
        cost_estimate=cost,
        compiler_params=pltpu.CompilerParams(vmem_limit_bytes=VMEM_BYTES),
    )(*arguments)


def swap(value, hour_bit, region_bit):
    hours, regions = lax.axis_size("hours"), lax.axis_size("region")
    pairs = [
        (hour * regions + region, (hour ^ hour_bit) * regions + (region ^ region_bit))
        for hour in range(hours)
        for region in range(regions)
    ]
    return lax.ppermute(value, ("hours", "region"), pairs)


def shifted(value, steps):
    count = lax.axis_size("hours")
    return lax.ppermute(value, "hours", [(i, (i + steps) % count) for i in range(count)])


def both_regions(block):
    if lax.axis_size("region") != 2:
        return lax.all_gather(block, "region")
    return in_order(block, swap(block, 0, 1))


def in_order(block, other):
    return jnp.where(
        lax.axis_index("region") == 0, jnp.stack([block, other]), jnp.stack([other, block])
    )


def exchange(sizes, block, sums):
    hours, regions = lax.axis_size("hours"), lax.axis_size("region")
    techs, rows, span = sizes["techs"], sizes["rows"], sizes["units"] // LANES
    halo = halo_at(sizes)
    if regions != 2 or hours != 16:
        gathered = lax.all_gather(block, "region")
        squares = jnp.sum(gathered[:, rows : rows + SQUARES], axis=0)
        totals = lax.psum(sums.at[techs:halo].set(squares), "hours")
        next_row = shifted(sums[halo : halo + span], -1)
        prev_row = shifted(sums[halo + span : halo + 2 * span], 1)
        return gathered, {"totals": totals, "next_row": next_row, "prev_row": prev_row}

    def merged(mine, yours, mine_first):
        row = lax.broadcasted_iota(jnp.int32, mine.shape, 0)
        keep = jnp.where(row < halo + span, mine_first, jnp.logical_not(mine_first))
        edge = (row >= halo) & (row < halo + 2 * span)
        return jnp.where(edge, jnp.where(keep, mine, yours), mine + yours)

    hour = lax.axis_index("hours")
    partner = swap(sums, 1, 0)
    chip = merged(sums, partner, hour % 2 == 0)
    across = swap(chip, 2, 0)
    other = swap(block.at[rows : rows + SQUARES].set(chip[techs:halo]), 0, 1)
    diagonal = swap(chip[techs:halo], 2, 1)
    slab = merged(chip, across, hour // 2 % 2 == 0)
    slab = slab.at[techs:halo].add(other[rows : rows + SQUARES] + diagonal)
    near, middle, far = [swap(slab, 4 * step, 0) for step in (1, 2, 3)]
    parts = {"slab": slab, "near": near, "middle": middle, "far": far}
    parts.update(partner=partner, across=across)
    return in_order(block, other), parts


def body(
    availability,
    demand,
    gen_cost,
    cap_cost,
    owner_map,
    line_ends,
    line_limit,
    cross_ends,
    cross_limit,
    pair_counts,
    store_node,
    store_energy,
    store_power,
    price_start,
):
    rows, techs, nodes = availability.shape
    hours, regions = lax.axis_size("hours"), lax.axis_size("region")
    slots, owned = cross_limit.shape[1], cap_cost.shape[1]
    units, lines = store_node.shape[0], line_limit.shape[0]
    sizes = dict(
        rows=rows, techs=techs, nodes=nodes, regions=regions, slots=slots, lines=lines, units=units
    )
    cross = regions * slots
    info_rows = 8 * (cross // LANES)

    def shape(*dims, dtype=jnp.float32):
        return jax.ShapeDtypeStruct(dims, dtype)

    def scratch_like(array):
        return pltpu.VMEM(array.shape, array.dtype)

    ends = cross_ends[:, 0]
    (block,) = call(
        functools.partial(regions_kernel, sizes),
        (price_start, ends, cross_limit, pair_counts),
        (shape(rows + info_rows, nodes),),
        scratch=[scratch_like(ends), scratch_like(cross_limit), pltpu.SemaphoreType.DMA((3,))],
        spaces=[pltpu.HBM] * 3 + [pltpu.SMEM],
    )
    gathered = both_regions(block)

    sources = {
        "line_ends": line_ends,
        "store_node": store_node[None],
        "line_limit": line_limit[None],
        "store_power": store_power[None],
        "price": price_start,
        "demand": demand,
        "gen_cost": gen_cost,
        "availability": availability.reshape(rows * techs, nodes),
        "cap_cost": cap_cost,
        "owner": owner_map.reshape(hours, owned),
        "store_energy": store_energy[None],
    }
    outs = {
        "demand": shape(rows, nodes),
        "gen_cost": shape(techs, nodes),
        "owner": shape(hours, owned, dtype=jnp.int32),
        "store_energy": shape(1, units),
        "available": shape(techs, rows, nodes),
        "maps_local": shape(nodes, lines + units, dtype=jnp.bfloat16),
        "limits_local": shape(1, lines + units),
        "flows_local": shape(rows, lines + units),
        "store_duals": shape(rows, units),
        "dispatch": shape(techs, rows, nodes),
        "balance": shape(rows, nodes),
        "sums": shape(sums_rows(sizes) + 2 * techs, nodes),
    }
    values = call(
        functools.partial(start_kernel, sizes, tuple(sources), tuple(outs)),
        tuple(sources.values()),
        tuple(outs.values()),
        scratch=[scratch_like(sources[name]) for name in START_SCRATCH]
        + [pltpu.SemaphoreType.DMA((len(sources),))],
        spaces=[pltpu.HBM] * len(sources),
        cost=pl.CostEstimate(flops=10**7, bytes_accessed=4 * 10**6, transcendentals=0),
    )
    state = dict(zip(outs, values))
    sums = state.pop("sums")
    closed = call(
        functools.partial(close_kernel, sizes),
        (gathered, state.pop("balance"), sums),
        (
            shape(regions * nodes, cross, dtype=jnp.bfloat16),
            shape(1, cross),
            shape(rows, cross),
            shape(rows + 8, nodes),
            shape(*sums.shape),
        ),
    )
    state.update(zip(("maps_cross", "limits_cross", "flows_cross"), closed))
    block, sums = closed[3:]
    gathered, parts = exchange(sizes, block, sums)

    def again(parts):
        totals = total_of(parts)
        first = sums_rows(sizes)
        col_weight, cost = totals[first : first + techs], totals[first + techs :]
        capacity = jnp.maximum(-cost / col_weight, 0.0)
        taken = state["dispatch"]
        rows_of = 2.0 * taken - state["available"] * (2.0 * capacity)[:, None, :]
        duals = jnp.maximum(0.5 * rows_of, 0.0)
        own = jnp.where(lax.axis_index("hours") == 0, jnp.sum(capacity**2, axis=0), 0.0)
        fixed = sums.at[:techs].set(jnp.sum(state["available"] * duals, axis=1))
        fixed = fixed.at[techs].add(own)
        fixed = fixed.at[techs + 1].add(jnp.sum(duals**2 - taken**2, axis=(0, 1)))
        blocks = block.at[rows : rows + SQUARES].set(fixed[techs : techs + SQUARES])
        return exchange(sizes, blocks, fixed)[1]

    negative = total_of(parts)[techs + 2, 0]
    parts = lax.cond(negative > 0.0, again, lambda parts: parts, parts)

    for iteration in range(1, ITERS):
        given = dict(state, **parts, gathered=gathered)
        if iteration < ITERS - 1:
            given.pop("owner")
            outs = {
                "dispatch": shape(techs, rows, nodes),
                "cap_duals": shape(techs, rows, nodes),
                "flows_local": shape(rows, lines + units),
                "flows_cross": shape(rows, cross),
                "store_duals": shape(rows, units),
                "capacity": shape(techs, nodes),
                "weight": shape(1, LANES),
                "charge": shape(rows, units),
                "charge_before": shape(1, units),
                "region": shape(rows + 8, nodes),
                "sums": shape(sums_rows(sizes), nodes),
            }
            if iteration == 1:
                outs.update(col_weight=shape(techs, nodes), cost=shape(techs, nodes))
        else:
            outs = {
                "dispatch": shape(rows * techs, nodes),
                "capacity": shape(1, owned),
                "prices": shape(rows, nodes),
                "charge": shape(rows, units),
            }
        values = call(
            functools.partial(sweep_kernel, sizes, iteration, tuple(given), tuple(outs)),
            tuple(given.values()),
            tuple(outs.values()),
        )
        results = dict(zip(outs, values))
        if iteration < ITERS - 1:
            gathered, parts = exchange(sizes, results.pop("region"), results.pop("sums"))
            state.update(results)
    return (
        results["dispatch"].reshape(rows, techs, nodes),
        results["capacity"],
        results["prices"],
        results["charge"],
    )


def solution(mesh):
    placed = (
        P("hours", None, "region"),
        P("hours", "region"),
        P(None, "region"),
        P("region", "hours"),
        P("region", None),
        P(None, "region"),
        P("region"),
        P(None, "region", None),
        P("region", None),
        P("region", None),
        P("region"),
        P("region"),
        P("region"),
        P("hours", "region"),
    )
    return jax.shard_map(
        body,
        mesh=mesh,
        in_specs=placed,
        out_specs=(
            P("hours", None, "region"),
            P("region", "hours"),
            P("hours", "region"),
            P("hours", "region"),
        ),
        check_vma=False,
    )
```

time: 67.2 us -> 69.7 us (1.037)
  waiting for transfers between devices: 24.4 us -> 17 us
  local copies, waits for them, and re-layouts: 3.87 us -> 10.2 us
  starting transfers between devices: 32.8 us -> 27.4 us
  Pallas kernels: 4.41 us -> 8.17 us
  between operations: 0.87 us -> 3.6 us
  other arithmetic: 0.53 us -> 2.58 us
    ppermute x27 -> x22, waiting for transfers between devices: 24.4 us -> 17 us  [swap(): return lax.ppermute(value, ('hours', 'region'), pairs)]
    ppermute x27 -> x22, starting transfers between devices: 32.8 us -> 27.4 us  [swap(): return lax.ppermute(value, ('hours', 'region'), pairs)]
    slice x0 -> x7, local copies, waits for them, and re-layouts: none -> 4.79 us  [the longest x4 4.78 us: body(): negative = total_of(parts)[techs + 2, 0]]
    pallas_call x5 -> x6, Pallas kernels: 4.41 us -> 8.17 us  [call(): pl.pallas_call(kernel, out_shape=shapes, in_specs=[pl.BlockSpec(memory_sp...]
    scatter-add x0 -> x3, local copies, waits for them, and re-layouts: none -> 1.42 us  [exchange(): slab = slab.at[techs:halo].add(other[rows:rows + SQUARES] + diagonal)]
    select_n x12 -> x13, other arithmetic: 0.49 us -> 1.86 us  [the longest x6 1.81 us: merged(): return jnp.where(edge, jnp.where(keep, mine, yours), mine + yours)]
    unnamed x33 -> x35, local copies, waits for them, and re-layouts: 3.85 us -> 3.83 us
  transfers between devices with their start and end apart: 27 -> 22, of which waited for: 24 -> 18; matrix products, arithmetic and copies ran while one was open for 0% -> 8% of each run, Pallas kernels for 0% -> 2%
where the time goes in v5:
time: 69.7 us; the launch traced here: 68.9 us
  starting transfers between devices  27.4 us (39%)
  waiting for transfers between devices  17 us (24%)
  local copies, waits for them, and re-layouts  10.2 us (15%)
  Pallas kernels  8.17 us (12%)
  between operations  3.6 us (5%)
  other arithmetic  2.58 us (4%)
    ppermute x22, starting transfers between devices, swap(): return lax.ppermute(value, ('hours', 'region'), pairs)  27.4 us
    ppermute x22, waiting for transfers between devices, swap(): return lax.ppermute(value, ('hours', 'region'), pairs)  17 us
    pallas_call x6, Pallas kernels, call(): pl.pallas_call(kernel, out_shape=shapes, in_specs=[pl.BlockSpec(memory_sp...  8.17 us
    slice x4, local copies, waits for them, and re-layouts, body(): negative = total_of(parts)[techs + 2, 0]  4.78 us
    unnamed x35, local copies, waits for them, and re-layouts  3.83 us
    select_n x6, other arithmetic, merged(): return jnp.where(edge, jnp.where(keep, mine, yours), mine + yours)  1.81 us
    scatter-add x3, local copies, waits for them, and re-layouts, exchange(): slab = slab.at[techs:halo].add(other[rows:rows + SQUARES] + diagonal)  1.42 us
  transfers between devices with their start and end apart: 22, of which 18 were waited for; matrix products, arithmetic and copies ran while one was open for 8% of the time, Pallas kernels for 2%

profile of v5, /device:TPU:0, one launch (start us, length us, event | category | flops | bytes accessed | tf_op | source)
XLA Modules:
  0.0 68.9 jit_solution(14581028909741839255)
XLA Ops:
  0.7 0.6 copy-done.12
  1.3 0.8 %copy-done.1 = f32[64,128]{1,0:T(8,128)S(1)} copy-done((f32[64,128]{1,0:T(8,128)S(1)}, f32[64,128]{1,0:T(8,128)}, u32[]{:S(2)}) %copy-start.1) | copy-done | bytes 32792
  2.1 0.7 copy-done.13
  2.8 0.8 %shard_map.166 = f32[72,128]{1,0:T(8,128)S(1)} custom-call(f32[64,128]{1,0:T(8,128)S(1)} %copy-done.1, s32[2,64]{1,0:T(2,128)S(1)} %bitcast.28, f32[1,64]{1,0:T(1,128)S(1)} %copy-done.12, s32[1,2]{1,0:T(1,128)S(1)} %copy-done.13), custom_call_target="tpu_custom_call" | custom-call | tf_op jit(solution)/shard_map/pallas_call | solution.py:412
  3.5 3.0 %collective-permute-start.7 = (f32[72,128]{1,0:T(8,128)S(1)}, f32[72,128]{1,0:T(8,128)S(1)}, u32[]{:S(2)}, u32[]{:S(2)}) collective-permute-start(f32[72,128]{1,0:T(8,128)S(1)} %shard_map.166), channel_id=1, source_target_pairs={{0,1},{1,0},{2,3},{3,2},{4,5},{5,4},{6,7},{7,6},{8,9},{9,8},{10,11... | collective-permute-start | bytes 110600 | tf_op jit(solution)/shard_map/ppermute | solution.py:430
  6.7 0.6 copy-done.14
  7.3 1.0 %copy-done = f32[64,16,128]{2,1,0:T(8,128)S(1)} copy-done((f32[64,16,128]{2,1,0:T(8,128)S(1)}, f32[64,16,128]{2,1,0:T(8,128)}, u32[]{:S(2)}) %copy-start) | copy-done | bytes 524312
  8.4 1.2 %shard_map.165 = (f32[64,128]{1,0:T(8,128)S(1)}, f32[16,128]{1,0:T(8,128)S(1)}, s32[16,128]{1,0:T(8,128)S(1)}, f32[1,256]{1,0:T(1,128)S(1)}, f32[16,64,128]{2,1,...) custom-call(s32[2,256]{1,0:T(2,128)S(1)} %copy-done.6, ...), custom_call_target="tpu_custom_call" | custom-call | flops 10000000 | bytes 4000000 | tf_op jit(solution)/shard_map/pallas_call | solution.py:412
  9.6 0.4 shard_map.167
  9.9 0.1 collective-permute-start.8
  10.1 1.1 %collective-permute-done.8 = f32[56,128]{1,0:T(8,128)S(1)} collective-permute-done((f32[56,128]{1,0:T(8,128)S(1)}, f32[56,128]{1,0:T(8,128)S(1)}, u32[]{:S(2)}, u32[]{:S(2)}) %collective-permute-start.8) | collective-permute-done | bytes 28704 | tf_op jit(solution)/shard_map/ppermute | solution.py:430
  11.2 0.1 add_select_fusion.3
  11.3 1.6 %collective-permute-start.9 = (f32[56,128]{1,0:T(8,128)S(1)}, f32[56,128]{1,0:T(8,128)}, u32[]{:S(2)}, u32[]{:S(2)}) collective-permute-start(f32[56,128]{1,0:T(8,128)S(1)} %add_select_fusion.3), channel_id=1, source_target_pairs={{0,4},{1,5},{2,6},{3,7},{4,0},{5,1},{6,2},{7,3},{8,12},{9,13},{10,... | collective-permute-start | bytes 86024 | tf_op jit(solution)/shard_map/ppermute | solution.py:430
  12.9 1.0 %collective-permute-start.11 = (f32[3,128]{1,0:T(4,128)S(1)}, f32[3,128]{1,0:T(4,128)S(1)}, u32[]{:S(2)}, u32[]{:S(2)}) collective-permute-start(f32[3,128]{1,0:T(4,128)S(1)} %slice.271), channel_id=1, source_target_pairs={{0,5},{1,4},{2,7},{3,6},{4,1},{5,0},{6,3},{7,2},{8,13},{9,12},{10,... | collective-permute-start | bytes 4616 | tf_op jit(solution)/shard_map/ppermute | solution.py:430
  13.9 0.1 scatter.23
  13.9 1.1 %collective-permute-start.10 = (f32[72,128]{1,0:T(8,128)S(1)}, f32[72,128]{1,0:T(8,128)S(1)}, u32[]{:S(2)}, u32[]{:S(2)}) collective-permute-start(f32[72,128]{1,0:T(8,128)S(1)} %scatter.23), channel_id=1, source_target_pairs={{0,1},{1,0},{2,3},{3,2},{4,5},{5,4},{6,7},{7,6},{8,9},{9,8},{10,11... | collective-permute-start | bytes 110600 | tf_op jit(solution)/shard_map/ppermute | solution.py:430
  15.1 0.3 collective-permute-done.9
  15.3 1.4 %add_select_fusion.2 = f32[56,128]{1,0:T(8,128)} fusion(f32[56,128]{1,0:T(8,128)S(1)} %add_select_fusion.3, f32[56,128]{1,0:T(8,128)} %collective-permute-done.9, pred[56]{0:T(512)(128)(4,1)S(1)} %compare_select_fusion.5, pred[56]{0:T(512)(128)(4,1)S(1)} %get-tuple-element.292), kind=kLoop, calls=%fused_computation.25 | loop fusion | flops 21504 | bytes 86128 | tf_op jit(solution)/shard_map/jit(_where)/select_n | solution.py:466
  16.8 0.6 collective-permute-done.11
  17.4 0.5 collective-permute-done.10
  18.0 0.7 %fusion.6 = f32[3,128]{1,0:T(4,128)S(1)} fusion(f32[3,128]{1,0:T(4,128)S(1)} %collective-permute-done.11, f32[72,128]{1,0:T(8,128)S(1)} %collective-permute-done.10, f32[56,128]{1,0:T(8,128)} %add_select_fusion.2), kind=kLoop, calls=%fused_computation.36 | loop fusion | flops 768 | bytes 6144 | tf_op jit(solution)/shard_map/add | solution.py:475
  18.7 1.3 %scatter-add.23 = f32[56,128]{1,0:T(8,128)} dynamic-update-slice(f32[56,128]{1,0:T(8,128)} %add_select_fusion.2, f32[3,128]{1,0:T(4,128)S(1)} %fusion.6, s32[]{:T(128)} %constant.398.clone.1, s32[]{:T(128)} %constant.389.clone.1) | dynamic-update-slice | bytes 3076 | tf_op jit(solution)/shard_map/scatter-add | solution.py:475
  20.0 3.6 %collective-permute-start.14 = (f32[56,128]{1,0:T(8,128)}, f32[56,128]{1,0:T(8,128)}, u32[]{:S(2)}, u32[]{:S(2)}) collective-permute-start(f32[56,128]{1,0:T(8,128)} %scatter-add.23), channel_id=1, source_target_pairs={{0,24},{1,25},{2,26},{3,27},{4,28},{5,29},{6,30},{7,31},{8,16},{9,... | collective-permute-start | bytes 86024 | tf_op jit(solution)/shard_map/ppermute | solution.py:430
  23.6 0.8 %collective-permute-start.12 = (f32[56,128]{1,0:T(8,128)}, f32[56,128]{1,0:T(8,128)}, u32[]{:S(2)}, u32[]{:S(2)}) collective-permute-start(f32[56,128]{1,0:T(8,128)} %scatter-add.23), channel_id=1, source_target_pairs={{0,8},{1,9},{2,10},{3,11},{4,12},{5,13},{6,14},{7,15},{8,0},{9,1},... | collective-permute-start | bytes 86024 | tf_op jit(solution)/shard_map/ppermute | solution.py:430
  24.4 1.2 %slice.273 = f32[1,1]{1,0:T(1,128)} slice(f32[56,128]{1,0:T(8,128)} %scatter-add.23), slice={[18:19], [0:1]} | slice | bytes 8 | tf_op jit(solution)/shard_map/slice | solution.py:592
  25.6 0.5 collective-permute-done.14
  26.1 1.2 %slice.276 = f32[1,1]{1,0:T(1,128)} slice(f32[56,128]{1,0:T(8,128)} %collective-permute-done.14), slice={[18:19], [0:1]} | slice | bytes 8 | tf_op jit(solution)/shard_map/slice | solution.py:592
  27.2 1.4 %collective-permute-done.13 = f32[56,128]{1,0:T(8,128)} collective-permute-done((f32[56,128]{1,0:T(8,128)}, f32[56,128]{1,0:T(8,128)}, u32[]{:S(2)}, u32[]{:S(2)}) %collective-permute-start.13) | collective-permute-done | bytes 28704 | tf_op jit(solution)/shard_map/ppermute | solution.py:430
  28.7 1.2 %slice.275 = f32[1,1]{1,0:T(1,128)} slice(f32[56,128]{1,0:T(8,128)} %collective-permute-done.13), slice={[18:19], [0:1]} | slice | bytes 8 | tf_op jit(solution)/shard_map/slice | solution.py:592
  31.1 1.2 %slice.274 = f32[1,1]{1,0:T(1,128)} slice(f32[56,128]{1,0:T(8,128)} %collective-permute-done.12), slice={[18:19], [0:1]} | slice | bytes 8 | tf_op jit(solution)/shard_map/slice | solution.py:592
  33.7 1.7 %shard_map.168 = (f32[16,64,128]{2,1,0:T(8,128)S(1)}, f32[16,64,128]{2,1,0:T(8,128)S(1)}, f32[64,512]{1,0:T(8,128)S(1)}, f32[64,128]{1,0:T(8,128)S(1)}, f32[64,2...) custom-call(f32[64,128]{1,0:T(8,128)S(1)} %get-tuple-element.235.ref, ...), custom_call_target="tpu_custom_call" | custom-call | tf_op jit(solution)/shard_map/pallas_call | solution.py:412
  35.3 0.1 collective-permute-start.15
  35.4 1.1 %collective-permute-done.15.refs_23_ = f32[24,128]{1,0:T(8,128)S(1)} collective-permute-done((f32[24,128]{1,0:T(8,128)S(1)}, f32[24,128]{1,0:T(8,128)S(1)}, u32[]{:S(2)}, u32[]{:S(2)}) %collective-permute-start.15) | collective-permute-done | bytes 12320 | tf_op jit(solution)/shard_map/ppermute | solution.py:430
  36.6 0.1 add_select_fusion.7
  36.7 1.5 %collective-permute-start.16 = (f32[24,128]{1,0:T(8,128)S(1)}, f32[24,128]{1,0:T(8,128)S(1)}, u32[]{:S(2)}, u32[]{:S(2)}) collective-permute-start(f32[24,128]{1,0:T(8,128)S(1)} %add_select_fusion.7), channel_id=1, source_target_pairs={{0,4},{1,5},{2,6},{3,7},{4,0},{5,1},{6,2},{7,3},{8,12},{9,13},{10,... | collective-permute-start | bytes 36872 | tf_op jit(solution)/shard_map/ppermute | solution.py:430
  38.2 1.1 %collective-permute-start.18 = (f32[3,128]{1,0:T(4,128)S(1)}, f32[3,128]{1,0:T(4,128)S(1)}, u32[]{:S(2)}, u32[]{:S(2)}) collective-permute-start(f32[3,128]{1,0:T(4,128)S(1)} %slice.278), channel_id=1, source_target_pairs={{0,5},{1,4},{2,7},{3,6},{4,1},{5,0},{6,3},{7,2},{8,13},{9,12},{10,... | collective-permute-start | bytes 4616 | tf_op jit(solution)/shard_map/ppermute | solution.py:430
  39.3 1.0 %collective-permute-start.17 = (f32[72,128]{1,0:T(8,128)S(1)}, f32[72,128]{1,0:T(8,128)S(1)}, u32[]{:S(2)}, u32[]{:S(2)}) collective-permute-start(f32[72,128]{1,0:T(8,128)S(1)} %scatter.24), channel_id=1, source_target_pairs={{0,1},{1,0},{2,3},{3,2},{4,5},{5,4},{6,7},{7,6},{8,9},{9,8},{10,11... | collective-permute-start | bytes 110600 | tf_op jit(solution)/shard_map/ppermute | solution.py:430
  40.4 0.1 add_select_fusion.6
  40.5 2.3 %collective-permute-done.18 = f32[3,128]{1,0:T(4,128)S(1)} collective-permute-done((f32[3,128]{1,0:T(4,128)S(1)}, f32[3,128]{1,0:T(4,128)S(1)}, u32[]{:S(2)}, u32[]{:S(2)}) %collective-permute-start.18) | collective-permute-done | bytes 1568 | tf_op jit(solution)/shard_map/ppermute | solution.py:430
  42.7 0.6 collective-permute-done.17
  43.4 0.1 scatter-add.24.refs_19_
  43.4 2.2 %collective-permute-start.21 = (f32[24,128]{1,0:T(8,128)S(1)}, f32[24,128]{1,0:T(8,128)S(1)}, u32[]{:S(2)}, u32[]{:S(2)}) collective-permute-start(f32[24,128]{1,0:T(8,128)S(1)} %scatter-add.24.refs_19_), channel_id=1, source_target_pairs={{0,24},{1,25},{2,26},{3,27},{4,28},{5,29},{6,30},{7,31},{8,16},{9,... | collective-permute-start | bytes 36872 | tf_op jit(solution)/shard_map/ppermute | solution.py:430
  45.6 2.3 %collective-permute-start.19 = (f32[24,128]{1,0:T(8,128)S(1)}, f32[24,128]{1,0:T(8,128)S(1)}, u32[]{:S(2)}, u32[]{:S(2)}) collective-permute-start(f32[24,128]{1,0:T(8,128)S(1)} %scatter-add.24.refs_19_), channel_id=1, source_target_pairs={{0,8},{1,9},{2,10},{3,11},{4,12},{5,13},{6,14},{7,15},{8,0},{9,1},... | collective-permute-start | bytes 36872 | tf_op jit(solution)/shard_map/ppermute | solution.py:430
  47.9 1.1 %collective-permute-done.21.refs_22_ = f32[24,128]{1,0:T(8,128)S(1)} collective-permute-done((f32[24,128]{1,0:T(8,128)S(1)}, f32[24,128]{1,0:T(8,128)S(1)}, u32[]{:S(2)}, u32[]{:S(2)}) %collective-permute-start.21) | collective-permute-done | bytes 12320 | tf_op jit(solution)/shard_map/ppermute | solution.py:430
  49.0 1.2 %collective-permute-done.20.refs_21_ = f32[24,128]{1,0:T(8,128)S(1)} collective-permute-done((f32[24,128]{1,0:T(8,128)S(1)}, f32[24,128]{1,0:T(8,128)S(1)}, u32[]{:S(2)}, u32[]{:S(2)}) %collective-permute-start.20) | collective-permute-done | bytes 12320 | tf_op jit(solution)/shard_map/ppermute | solution.py:430
  50.2 1.8 %shard_map.169 = (f32[16,64,128]{2,1,0:T(8,128)S(1)}, f32[16,64,128]{2,1,0:T(8,128)S(1)}, f32[64,512]{1,0:T(8,128)S(1)}, f32[64,128]{1,0:T(8,128)S(1)}, f32[64,2...) custom-call(f32[64,128]{1,0:T(8,128)S(1)} %get-tuple-element.235.ref, ...), custom_call_target="tpu_custom_call" | custom-call | tf_op jit(solution)/shard_map/pallas_call | solution.py:412
  52.0 0.1 collective-permute-start.22
  52.1 1.2 %collective-permute-done.22.refs_24_ = f32[24,128]{1,0:T(8,128)S(1)} collective-permute-done((f32[24,128]{1,0:T(8,128)S(1)}, f32[24,128]{1,0:T(8,128)S(1)}, u32[]{:S(2)}, u32[]{:S(2)}) %collective-permute-start.22) | collective-permute-done | bytes 12320 | tf_op jit(solution)/shard_map/ppermute | solution.py:430
  53.3 0.1 add_select_fusion.5
  53.3 1.5 %collective-permute-start.23 = (f32[24,128]{1,0:T(8,128)S(1)}, f32[24,128]{1,0:T(8,128)S(1)}, u32[]{:S(2)}, u32[]{:S(2)}) collective-permute-start(f32[24,128]{1,0:T(8,128)S(1)} %add_select_fusion.5), channel_id=1, source_target_pairs={{0,4},{1,5},{2,6},{3,7},{4,0},{5,1},{6,2},{7,3},{8,12},{9,13},{10,... | collective-permute-start | bytes 36872 | tf_op jit(solution)/shard_map/ppermute | solution.py:430
  54.8 0.9 %collective-permute-start.25 = (f32[3,128]{1,0:T(4,128)S(1)}, f32[3,128]{1,0:T(4,128)S(1)}, u32[]{:S(2)}, u32[]{:S(2)}) collective-permute-start(f32[3,128]{1,0:T(4,128)S(1)} %slice.281), channel_id=1, source_target_pairs={{0,5},{1,4},{2,7},{3,6},{4,1},{5,0},{6,3},{7,2},{8,13},{9,12},{10,... | collective-permute-start | bytes 4616 | tf_op jit(solution)/shard_map/ppermute | solution.py:430
  55.8 1.1 %collective-permute-start.24 = (f32[72,128]{1,0:T(8,128)S(1)}, f32[72,128]{1,0:T(8,128)S(1)}, u32[]{:S(2)}, u32[]{:S(2)}) collective-permute-start(f32[72,128]{1,0:T(8,128)S(1)} %scatter.27), channel_id=1, source_target_pairs={{0,1},{1,0},{2,3},{3,2},{4,5},{5,4},{6,7},{7,6},{8,9},{9,8},{10,11... | collective-permute-start | bytes 110600 | tf_op jit(solution)/shard_map/ppermute | solution.py:430
  57.0 0.1 collective-permute-done.23.refs_25_
  57.0 0.1 add_select_fusion.4
  57.1 2.2 %collective-permute-done.25 = f32[3,128]{1,0:T(4,128)S(1)} collective-permute-done((f32[3,128]{1,0:T(4,128)S(1)}, f32[3,128]{1,0:T(4,128)S(1)}, u32[]{:S(2)}, u32[]{:S(2)}) %collective-permute-start.25) | collective-permute-done | bytes 1568 | tf_op jit(solution)/shard_map/ppermute | solution.py:430
  59.3 0.5 collective-permute-done.24
  59.9 0.1 scatter-add.27.refs_20_
  59.9 1.8 %collective-permute-start.28 = (f32[24,128]{1,0:T(8,128)S(1)}, f32[24,128]{1,0:T(8,128)S(1)}, u32[]{:S(2)}, u32[]{:S(2)}) collective-permute-start(f32[24,128]{1,0:T(8,128)S(1)} %scatter-add.27.refs_20_), channel_id=1, source_target_pairs={{0,24},{1,25},{2,26},{3,27},{4,28},{5,29},{6,30},{7,31},{8,16},{9,... | collective-permute-start | bytes 36872 | tf_op jit(solution)/shard_map/ppermute | solution.py:430
  61.7 1.1 %collective-permute-start.27 = (f32[24,128]{1,0:T(8,128)S(1)}, f32[24,128]{1,0:T(8,128)S(1)}, u32[]{:S(2)}, u32[]{:S(2)}) collective-permute-start(f32[24,128]{1,0:T(8,128)S(1)} %scatter-add.27.refs_20_), channel_id=1, source_target_pairs={{0,16},{1,17},{2,18},{3,19},{4,20},{5,21},{6,22},{7,23},{8,24},{9,... | collective-permute-start | bytes 36872 | tf_op jit(solution)/shard_map/ppermute | solution.py:430
  62.9 1.5 %collective-permute-start.26 = (f32[24,128]{1,0:T(8,128)S(1)}, f32[24,128]{1,0:T(8,128)S(1)}, u32[]{:S(2)}, u32[]{:S(2)}) collective-permute-start(f32[24,128]{1,0:T(8,128)S(1)} %scatter-add.27.refs_20_), channel_id=1, source_target_pairs={{0,8},{1,9},{2,10},{3,11},{4,12},{5,13},{6,14},{7,15},{8,0},{9,1},... | collective-permute-start | bytes 36872 | tf_op jit(solution)/shard_map/ppermute | solution.py:430
  64.4 1.1 %collective-permute-done.28.refs_23_ = f32[24,128]{1,0:T(8,128)S(1)} collective-permute-done((f32[24,128]{1,0:T(8,128)S(1)}, f32[24,128]{1,0:T(8,128)S(1)}, u32[]{:S(2)}, u32[]{:S(2)}) %collective-permute-start.28) | collective-permute-done | bytes 12320 | tf_op jit(solution)/shard_map/ppermute | solution.py:430
  65.5 0.8 %collective-permute-done.27.refs_22_ = f32[24,128]{1,0:T(8,128)S(1)} collective-permute-done((f32[24,128]{1,0:T(8,128)S(1)}, f32[24,128]{1,0:T(8,128)S(1)}, u32[]{:S(2)}, u32[]{:S(2)}) %collective-permute-start.27) | collective-permute-done | bytes 12320 | tf_op jit(solution)/shard_map/ppermute | solution.py:430
  66.3 0.2 collective-permute-done.26.refs_21_
  66.5 2.4 %shard_map.170 = (f32[1024,128]{1,0:T(8,128)}, f32[1,128]{1,0:T(1,128)}, f32[64,128]{1,0:T(8,128)}, f32[64,256]{1,0:T(8,128)}) custom-call(f32[64,128]{1,0:T(8,128)S(1)} %get-tuple-element.235.refs_0_, f32[16,128]{1,0:T(8,128)S(1)} %get-tuple-element.236.refs_1_, s32[16,128]{1,0:T(8,128)S(1)} %get-tuple-element.237.refs_2_, ...), custom_call_target="tpu_custom_call" | custom-call | tf_op jit(solution)/shard_map/pallas_call | solution.py:412
  (53 shorter events, 0.4 us)
Async XLA Ops:
  0.6 0.7 copy-start.12
  0.6 0.7 copy-start.7
  1.3 0.8 %copy-start.1 = (f32[64,128]{1,0:T(8,128)S(1)}, f32[64,128]{1,0:T(8,128)}, u32[]{:S(2)}) copy-start(f32[64,128]{1,0:T(8,128)} %price.1) | copy-start | bytes 98308
  2.1 0.7 copy-start.13
  2.7 3.9 %copy-start.3 = (f32[64,128]{1,0:T(8,128)S(1)}, f32[64,128]{1,0:T(8,128)}, u32[]{:S(2)}) copy-start(f32[64,128]{1,0:T(8,128)} %refs_5_.1) | copy-start | bytes 98308
  2.7 3.9 %copy-start.9 = (f32[256]{0:T(256)S(1)}, f32[256]{0:T(256)}, u32[]{:S(2)}) copy-start(f32[256]{0:T(256)} %param.46) | copy-start | bytes 3076
  2.7 3.9 %copy-start.10 = (f32[256]{0:T(256)S(1)}, f32[256]{0:T(256)}, u32[]{:S(2)}) copy-start(f32[256]{0:T(256)} %param.52) | copy-start | bytes 3076
  2.8 3.9 %copy-start.11 = (f32[256]{0:T(256)S(1)}, f32[256]{0:T(256)}, u32[]{:S(2)}) copy-start(f32[256]{0:T(256)} %param.51) | copy-start | bytes 3076
  3.5 3.1 %copy-start.2 = (f32[64,128]{1,0:T(8,128)S(1)}, f32[64,128]{1,0:T(8,128)}, u32[]{:S(2)}) copy-start(f32[64,128]{1,0:T(8,128)} %price.1) | copy-start | bytes 98308
  3.5 6.0 %collective-permute-start.7 = (f32[72,128]{1,0:T(8,128)S(1)}, f32[72,128]{1,0:T(8,128)S(1)}, u32[]{:S(2)}, u32[]{:S(2)}) collective-permute-start(f32[72,128]{1,0:T(8,128)S(1)} %shard_map.166), channel_id=1, source_target_pairs={{0,1},{1,0},{2,3},{3,2},{4,5},{5,4},{6,7},{7,6},{8,9},{9,8},{10,11... | collective-permute-start | bytes 110600 | tf_op jit(solution)/shard_map/ppermute | solution.py:430
  6.6 0.7 copy-start.14
  6.6 0.7 %copy-start.6 = (s32[2,256]{1,0:T(2,128)S(1)}, s32[2,256]{1,0:T(2,128)}, u32[]{:S(2)}) copy-start(s32[2,256]{1,0:T(2,128)} %refs_0_.1) | copy-start | bytes 6148
  6.6 0.7 %copy-start.5 = (s32[1,2048]{1,0:T(1,128)S(1)}, s32[1,2048]{1,0:T(1,128)}, u32[]{:S(2)}) copy-start(s32[1,2048]{1,0:T(1,128)} %param.44) | copy-start | bytes 24580
  6.6 0.7 %copy-start.4 = (f32[16,128]{1,0:T(8,128)S(1)}, f32[16,128]{1,0:T(8,128)}, u32[]{:S(2)}) copy-start(f32[16,128]{1,0:T(8,128)} %refs_6_.1) | copy-start | bytes 24580
  6.6 0.7 %copy-start.8 = (s32[256]{0:T(256)S(1)}, s32[256]{0:T(256)}, u32[]{:S(2)}) copy-start(s32[256]{0:T(256)} %param.50) | copy-start | bytes 3076
  7.3 1.0 %copy-start = (f32[64,16,128]{2,1,0:T(8,128)S(1)}, f32[64,16,128]{2,1,0:T(8,128)}, u32[]{:S(2)}) copy-start(f32[64,16,128]{2,1,0:T(8,128)} %param.40) | copy-start | bytes 1572868
  9.5 24.1 %copy-start.15 = (f32[16,64,128]{2,1,0:T(8,128)}, f32[16,64,128]{2,1,0:T(8,128)S(1)}, u32[]{:S(2)}) copy-start(f32[16,64,128]{2,1,0:T(8,128)S(1)} %get-tuple-element.239.refs_3_.refs_4_) | copy-start | bytes 1572868
  9.9 1.3 %collective-permute-start.8 = (f32[56,128]{1,0:T(8,128)S(1)}, f32[56,128]{1,0:T(8,128)S(1)}, u32[]{:S(2)}, u32[]{:S(2)}) collective-permute-start(f32[56,128]{1,0:T(8,128)S(1)} %get-tuple-element.250), channel_id=1, source_target_pairs={{0,2},{1,3},{2,0},{3,1},{4,6},{5,7},{6,4},{7,5},{8,10},{9,11},{10,... | collective-permute-start | bytes 86024 | tf_op jit(solution)/shard_map/ppermute | solution.py:430
  11.3 4.0 %collective-permute-start.9 = (f32[56,128]{1,0:T(8,128)S(1)}, f32[56,128]{1,0:T(8,128)}, u32[]{:S(2)}, u32[]{:S(2)}) collective-permute-start(f32[56,128]{1,0:T(8,128)S(1)} %add_select_fusion.3), channel_id=1, source_target_pairs={{0,4},{1,5},{2,6},{3,7},{4,0},{5,1},{6,2},{7,3},{8,12},{9,13},{10,... | collective-permute-start | bytes 86024 | tf_op jit(solution)/shard_map/ppermute | solution.py:430
  12.9 4.5 %collective-permute-start.11 = (f32[3,128]{1,0:T(4,128)S(1)}, f32[3,128]{1,0:T(4,128)S(1)}, u32[]{:S(2)}, u32[]{:S(2)}) collective-permute-start(f32[3,128]{1,0:T(4,128)S(1)} %slice.271), channel_id=1, source_target_pairs={{0,5},{1,4},{2,7},{3,6},{4,1},{5,0},{6,3},{7,2},{8,13},{9,12},{10,... | collective-permute-start | bytes 4616 | tf_op jit(solution)/shard_map/ppermute | solution.py:430
  13.9 4.0 %collective-permute-start.10 = (f32[72,128]{1,0:T(8,128)S(1)}, f32[72,128]{1,0:T(8,128)S(1)}, u32[]{:S(2)}, u32[]{:S(2)}) collective-permute-start(f32[72,128]{1,0:T(8,128)S(1)} %scatter.23), channel_id=1, source_target_pairs={{0,1},{1,0},{2,3},{3,2},{4,5},{5,4},{6,7},{7,6},{8,9},{9,8},{10,11... | collective-permute-start | bytes 110600 | tf_op jit(solution)/shard_map/ppermute | solution.py:430
  20.0 6.1 %collective-permute-start.14 = (f32[56,128]{1,0:T(8,128)}, f32[56,128]{1,0:T(8,128)}, u32[]{:S(2)}, u32[]{:S(2)}) collective-permute-start(f32[56,128]{1,0:T(8,128)} %scatter-add.23), channel_id=1, source_target_pairs={{0,24},{1,25},{2,26},{3,27},{4,28},{5,29},{6,30},{7,31},{8,16},{9,... | collective-permute-start | bytes 86024 | tf_op jit(solution)/shard_map/ppermute | solution.py:430
  23.6 5.1 %collective-permute-start.13 = (f32[56,128]{1,0:T(8,128)}, f32[56,128]{1,0:T(8,128)}, u32[]{:S(2)}, u32[]{:S(2)}) collective-permute-start(f32[56,128]{1,0:T(8,128)} %scatter-add.23), channel_id=1, source_target_pairs={{0,16},{1,17},{2,18},{3,19},{4,20},{5,21},{6,22},{7,23},{8,24},{9,... | collective-permute-start | bytes 86024 | tf_op jit(solution)/shard_map/ppermute | solution.py:430
  23.6 7.6 %collective-permute-start.12 = (f32[56,128]{1,0:T(8,128)}, f32[56,128]{1,0:T(8,128)}, u32[]{:S(2)}, u32[]{:S(2)}) collective-permute-start(f32[56,128]{1,0:T(8,128)} %scatter-add.23), channel_id=1, source_target_pairs={{0,8},{1,9},{2,10},{3,11},{4,12},{5,13},{6,14},{7,15},{8,0},{9,1},... | collective-permute-start | bytes 86024 | tf_op jit(solution)/shard_map/ppermute | solution.py:430
  35.3 1.2 %collective-permute-start.15 = (f32[24,128]{1,0:T(8,128)S(1)}, f32[24,128]{1,0:T(8,128)S(1)}, u32[]{:S(2)}, u32[]{:S(2)}) collective-permute-start(f32[24,128]{1,0:T(8,128)S(1)} %get-tuple-element.269), channel_id=1, source_target_pairs={{0,2},{1,3},{2,0},{3,1},{4,6},{5,7},{6,4},{7,5},{8,10},{9,11},{10,... | collective-permute-start | bytes 36872 | tf_op jit(solution)/shard_map/ppermute | solution.py:430
  36.7 3.7 %collective-permute-start.16 = (f32[24,128]{1,0:T(8,128)S(1)}, f32[24,128]{1,0:T(8,128)S(1)}, u32[]{:S(2)}, u32[]{:S(2)}) collective-permute-start(f32[24,128]{1,0:T(8,128)S(1)} %add_select_fusion.7), channel_id=1, source_target_pairs={{0,4},{1,5},{2,6},{3,7},{4,0},{5,1},{6,2},{7,3},{8,12},{9,13},{10,... | collective-permute-start | bytes 36872 | tf_op jit(solution)/shard_map/ppermute | solution.py:430
  38.2 4.5 %collective-permute-start.18 = (f32[3,128]{1,0:T(4,128)S(1)}, f32[3,128]{1,0:T(4,128)S(1)}, u32[]{:S(2)}, u32[]{:S(2)}) collective-permute-start(f32[3,128]{1,0:T(4,128)S(1)} %slice.278), channel_id=1, source_target_pairs={{0,5},{1,4},{2,7},{3,6},{4,1},{5,0},{6,3},{7,2},{8,13},{9,12},{10,... | collective-permute-start | bytes 4616 | tf_op jit(solution)/shard_map/ppermute | solution.py:430
  39.3 4.0 %collective-permute-start.17 = (f32[72,128]{1,0:T(8,128)S(1)}, f32[72,128]{1,0:T(8,128)S(1)}, u32[]{:S(2)}, u32[]{:S(2)}) collective-permute-start(f32[72,128]{1,0:T(8,128)S(1)} %scatter.24), channel_id=1, source_target_pairs={{0,1},{1,0},{2,3},{3,2},{4,5},{5,4},{6,7},{7,6},{8,9},{9,8},{10,11... | collective-permute-start | bytes 110600 | tf_op jit(solution)/shard_map/ppermute | solution.py:430
  43.4 5.6 %collective-permute-start.21 = (f32[24,128]{1,0:T(8,128)S(1)}, f32[24,128]{1,0:T(8,128)S(1)}, u32[]{:S(2)}, u32[]{:S(2)}) collective-permute-start(f32[24,128]{1,0:T(8,128)S(1)} %scatter-add.24.refs_19_), channel_id=1, source_target_pairs={{0,24},{1,25},{2,26},{3,27},{4,28},{5,29},{6,30},{7,31},{8,16},{9,... | collective-permute-start | bytes 36872 | tf_op jit(solution)/shard_map/ppermute | solution.py:430
  45.6 4.6 %collective-permute-start.20 = (f32[24,128]{1,0:T(8,128)S(1)}, f32[24,128]{1,0:T(8,128)S(1)}, u32[]{:S(2)}, u32[]{:S(2)}) collective-permute-start(f32[24,128]{1,0:T(8,128)S(1)} %scatter-add.24.refs_19_), channel_id=1, source_target_pairs={{0,16},{1,17},{2,18},{3,19},{4,20},{5,21},{6,22},{7,23},{8,24},{9,... | collective-permute-start | bytes 36872 | tf_op jit(solution)/shard_map/ppermute | solution.py:430
  45.6 4.6 %collective-permute-start.19 = (f32[24,128]{1,0:T(8,128)S(1)}, f32[24,128]{1,0:T(8,128)S(1)}, u32[]{:S(2)}, u32[]{:S(2)}) collective-permute-start(f32[24,128]{1,0:T(8,128)S(1)} %scatter-add.24.refs_19_), channel_id=1, source_target_pairs={{0,8},{1,9},{2,10},{3,11},{4,12},{5,13},{6,14},{7,15},{8,0},{9,1},... | collective-permute-start | bytes 36872 | tf_op jit(solution)/shard_map/ppermute | solution.py:430
  52.0 1.2 %collective-permute-start.22 = (f32[24,128]{1,0:T(8,128)S(1)}, f32[24,128]{1,0:T(8,128)S(1)}, u32[]{:S(2)}, u32[]{:S(2)}) collective-permute-start(f32[24,128]{1,0:T(8,128)S(1)} %get-tuple-element.280), channel_id=1, source_target_pairs={{0,2},{1,3},{2,0},{3,1},{4,6},{5,7},{6,4},{7,5},{8,10},{9,11},{10,... | collective-permute-start | bytes 36872 | tf_op jit(solution)/shard_map/ppermute | solution.py:430
  53.3 3.7 %collective-permute-start.23 = (f32[24,128]{1,0:T(8,128)S(1)}, f32[24,128]{1,0:T(8,128)S(1)}, u32[]{:S(2)}, u32[]{:S(2)}) collective-permute-start(f32[24,128]{1,0:T(8,128)S(1)} %add_select_fusion.5), channel_id=1, source_target_pairs={{0,4},{1,5},{2,6},{3,7},{4,0},{5,1},{6,2},{7,3},{8,12},{9,13},{10,... | collective-permute-start | bytes 36872 | tf_op jit(solution)/shard_map/ppermute | solution.py:430
  54.8 4.5 %collective-permute-start.25 = (f32[3,128]{1,0:T(4,128)S(1)}, f32[3,128]{1,0:T(4,128)S(1)}, u32[]{:S(2)}, u32[]{:S(2)}) collective-permute-start(f32[3,128]{1,0:T(4,128)S(1)} %slice.281), channel_id=1, source_target_pairs={{0,5},{1,4},{2,7},{3,6},{4,1},{5,0},{6,3},{7,2},{8,13},{9,12},{10,... | collective-permute-start | bytes 4616 | tf_op jit(solution)/shard_map/ppermute | solution.py:430
  55.8 4.0 %collective-permute-start.24 = (f32[72,128]{1,0:T(8,128)S(1)}, f32[72,128]{1,0:T(8,128)S(1)}, u32[]{:S(2)}, u32[]{:S(2)}) collective-permute-start(f32[72,128]{1,0:T(8,128)S(1)} %scatter.27), channel_id=1, source_target_pairs={{0,1},{1,0},{2,3},{3,2},{4,5},{5,4},{6,7},{7,6},{8,9},{9,8},{10,11... | collective-permute-start | bytes 110600 | tf_op jit(solution)/shard_map/ppermute | solution.py:430
  59.9 5.6 %collective-permute-start.28 = (f32[24,128]{1,0:T(8,128)S(1)}, f32[24,128]{1,0:T(8,128)S(1)}, u32[]{:S(2)}, u32[]{:S(2)}) collective-permute-start(f32[24,128]{1,0:T(8,128)S(1)} %scatter-add.27.refs_20_), channel_id=1, source_target_pairs={{0,24},{1,25},{2,26},{3,27},{4,28},{5,29},{6,30},{7,31},{8,16},{9,... | collective-permute-start | bytes 36872 | tf_op jit(solution)/shard_map/ppermute | solution.py:430
  61.7 4.6 %collective-permute-start.27 = (f32[24,128]{1,0:T(8,128)S(1)}, f32[24,128]{1,0:T(8,128)S(1)}, u32[]{:S(2)}, u32[]{:S(2)}) collective-permute-start(f32[24,128]{1,0:T(8,128)S(1)} %scatter-add.27.refs_20_), channel_id=1, source_target_pairs={{0,16},{1,17},{2,18},{3,19},{4,20},{5,21},{6,22},{7,23},{8,24},{9,... | collective-permute-start | bytes 36872 | tf_op jit(solution)/shard_map/ppermute | solution.py:430
  62.9 3.7 %collective-permute-start.26 = (f32[24,128]{1,0:T(8,128)S(1)}, f32[24,128]{1,0:T(8,128)S(1)}, u32[]{:S(2)}, u32[]{:S(2)}) collective-permute-start(f32[24,128]{1,0:T(8,128)S(1)} %scatter-add.27.refs_20_), channel_id=1, source_target_pairs={{0,8},{1,9},{2,10},{3,11},{4,12},{5,13},{6,14},{7,15},{8,0},{9,1},... | collective-permute-start | bytes 36872 | tf_op jit(solution)/shard_map/ppermute | solution.py:430

commit v6 on v5

v6 whole, which is shorter than its diff:
```python
import functools
from types import SimpleNamespace as Bag

import jax
import jax.numpy as jnp
from jax import lax
from jax.experimental import pallas as pl
from jax.experimental.pallas import tpu as pltpu
from jax.sharding import PartitionSpec as P

ITERS = 4
EPSILON = 1e-06
LANES = 128
VMEM_BYTES = 24 * 1024 * 1024
SQUARES = 3


def split3(value):
    high = value.astype(jnp.bfloat16)
    rest = value - high.astype(jnp.float32)
    middle = rest.astype(jnp.bfloat16)
    low = (rest - middle.astype(jnp.float32)).astype(jnp.bfloat16)
    return jnp.concatenate([high, middle, low], axis=0)


def dot3(value, matrix, transposed):
    rows = value.shape[0]
    contract = ((1,), (1 if transposed else 0,))
    product = lax.dot_general(
        split3(value), matrix, (contract, ((), ())), preferred_element_type=jnp.float32
    )
    return product[:rows] + product[rows : 2 * rows] + product[2 * rows :]


def row_sum(value):
    return jnp.sum(value, axis=0, keepdims=True)


def fold_lanes(row):
    total = row[:, :LANES]
    for start in range(LANES, row.shape[1], LANES):
        total = total + row[:, start : start + LANES]
    return total


def owned_one_hots(owner_ref, tech_count, node_count):
    owned = owner_ref[pl.ds(lax.axis_index("hours"), 1), :]
    shape_t = (tech_count, owned.shape[1])
    shape_n = (node_count, owned.shape[1])
    tech = lax.broadcasted_iota(jnp.int32, shape_t, 0) == owned // node_count
    node = lax.broadcasted_iota(jnp.int32, shape_n, 0) == owned % node_count
    return tech, node.astype(jnp.float32).astype(jnp.bfloat16)


def incidence(start, end, count):
    node = lax.broadcasted_iota(jnp.int32, (count, start.shape[1]), 0)
    maps = (node == end).astype(jnp.float32) - (node == start).astype(jnp.float32)
    return maps.astype(jnp.bfloat16)


def halo_at(sizes):
    return sizes.techs + SQUARES


def sums_rows(sizes):
    return (halo_at(sizes) + 2 * sizes.units // LANES + 7) // 8 * 8


def write_halo(sizes, sums_ref, store_new):
    halo, span, rows = halo_at(sizes), sizes.units // LANES, sizes.rows
    for i in range(span):
        part = slice(i * LANES, (i + 1) * LANES)
        sums_ref[halo + i : halo + i + 1, :] = store_new[:1, part]
        sums_ref[halo + span + i : halo + span + i + 1, :] = store_new[rows - 1 :, part]
    used, end = halo + 2 * span, sums_rows(sizes)
    if used < end:
        sums_ref[used:end, :] = jnp.zeros((end - used, LANES), jnp.float32)


def slots_kernel(sizes, ends_ref, limit_ref, pairs_ref, info_ref):
    nodes, slots, regions = sizes.nodes, sizes.slots, sizes.regions
    own = lax.axis_index("region")
    width = slots // regions
    slot = lax.broadcasted_iota(jnp.int32, (1, slots), 1)
    pair = slot // width
    in_use = jnp.zeros((1, slots), jnp.int32)
    for target in range(regions):
        in_use = jnp.where(pair == target, pairs_ref[0, target], in_use)
    place = lax.broadcasted_iota(jnp.int32, (slots, regions * slots), 1) == (
        own * slots + lax.broadcasted_iota(jnp.int32, (slots, regions * slots), 0)
    )
    place = place.astype(jnp.float32).astype(jnp.bfloat16)
    bound = jnp.where(slot % width < in_use, limit_ref[...], 0.0)
    start = (ends_ref[0:1, :] + own * nodes).astype(jnp.float32)
    end = (ends_ref[1:2, :] + pair * nodes).astype(jnp.float32)
    rest = jnp.zeros((13, slots), jnp.float32)
    info = dot3(jnp.concatenate([start, end, bound, rest], axis=0), place, False)
    for chunk in range(regions * slots // LANES):
        info_ref[8 * chunk : 8 * chunk + 8, :] = info[:8, chunk * LANES : (chunk + 1) * LANES]


def start_kernel(sizes, names_in, names_out, *refs):
    given = Bag(**dict(zip(names_in, refs[: len(names_in)])))
    gives = Bag(**dict(zip(names_out, refs[len(names_in) :])))
    rows, techs, nodes, lines = sizes.rows, sizes.techs, sizes.nodes, sizes.lines
    gives.demand[...] = given.demand[...]
    gives.gen_cost[...] = given.gen_cost[...]
    gives.owner[...] = given.owner[...]
    gives.store_energy[...] = given.store_energy[...]
    line_ends, stores = given.line_ends[...], given.store_node[...]
    start = jnp.concatenate([line_ends[0:1], jnp.full_like(stores, -1)], axis=1)
    end = jnp.concatenate([line_ends[1:2], stores], axis=1)
    maps = incidence(start, end, nodes)
    limits = jnp.concatenate([given.line_limit[...], given.store_power[...]], axis=1)
    gives.maps_local[...] = maps
    gives.limits_local[...] = limits
    prices = given.price[...]
    flows = jnp.clip(-0.5 * dot3(prices, maps, False), -limits, limits)
    gives.flows_local[...] = flows
    store_new = (1.0 / 3.0) * (2.0 * flows[:, lines:])
    gives.store_duals[...] = store_new
    primal_row = fold_lanes(row_sum(flows * flows))
    dual_row = fold_lanes(row_sum(store_new * store_new))
    balance = dot3(2.0 * flows, maps, True) - given.demand[...]
    gen_cost = given.gen_cost[...]
    acc = jnp.zeros((rows, nodes), jnp.float32)
    weights = jnp.zeros((techs, nodes), jnp.float32)
    for hour in range(rows):
        weights = weights + given.availability[hour * techs : (hour + 1) * techs, :]
    for tech in range(techs):
        avail = given.availability[pl.ds(tech, rows, stride=techs), :]
        gives.available[tech] = avail
        dispatch = jnp.maximum(-0.5 * (gen_cost[tech : tech + 1] + prices), 0.0)
        gives.dispatch[tech] = dispatch
        dispatch_bar = 2.0 * dispatch
        balance = balance + dispatch_bar
        duals = jnp.maximum(0.5 * dispatch_bar, 0.0)
        acc = acc + dispatch * dispatch
        gives.sums[tech : tech + 1, :] = row_sum(avail * duals)
    gives.balance[...] = balance
    squares = row_sum(acc)
    cost = given.cap_cost[...]
    negative = jnp.sum((cost < 0.0).astype(jnp.float32), axis=1, keepdims=True)
    write_halo(sizes, gives.sums, store_new)
    gives.sums[techs : techs + SQUARES, :] = jnp.concatenate(
        [primal_row + squares, dual_row + squares, jnp.broadcast_to(negative, (1, LANES))], axis=0
    )
    tech_hot, node_hot = owned_one_hots(given.owner, techs, nodes)
    first = sums_rows(sizes)
    gives.sums[first : first + techs, :] = weights
    gives.sums[first + techs : first + 2 * techs, :] = dot3(
        jnp.where(tech_hot, cost, 0.0), node_hot, True
    )


def close_kernel(
    sizes,
    gathered,
    info_ref,
    balance_ref,
    sums_in_ref,
    maps_ref,
    limits_ref,
    flows_ref,
    region_ref,
    sums_ref,
):
    rows, techs, nodes = sizes.rows, sizes.techs, sizes.nodes
    slots, regions = sizes.slots, sizes.regions
    own = lax.axis_index("region")
    chunks = []
    for chunk in range(regions * slots // LANES):
        at = slice(8 * chunk, 8 * chunk + 8)
        part = info_ref[0, at, :]
        for region in range(1, regions):
            part = part + info_ref[region, at, :]
        chunks.append(part)
    info = jnp.concatenate(chunks, axis=1) if len(chunks) > 1 else chunks[0]
    maps_ref[...] = incidence(
        info[0:1].astype(jnp.int32), info[1:2].astype(jnp.int32), regions * nodes
    )
    limits = info[2:3]
    limits_ref[...] = limits
    prices_all = jnp.concatenate([gathered[region, :rows, :] for region in range(regions)], axis=1)
    flows = jnp.clip(-0.5 * dot3(prices_all, maps_ref[...], False), -limits, limits)
    flows_ref[...] = flows
    maps_own = maps_ref[pl.ds(pl.multiple_of(own * nodes, nodes), nodes), :]
    balance = balance_ref[...] + dot3(2.0 * flows, maps_own, True)
    step_up = (1.0 / (techs + 8.0)) * balance
    region_ref[:rows, :] = gathered[own, :rows, :] + step_up
    change = row_sum(flows * flows)
    slot = lax.broadcasted_iota(jnp.int32, change.shape, 1)
    primal = fold_lanes(jnp.where(slot // slots == own, change, 0.0))
    more = jnp.concatenate(
        [primal, row_sum(step_up * step_up), jnp.zeros((SQUARES - 2, LANES), jnp.float32)], axis=0
    )
    sums_ref[...] = sums_in_ref[...]
    squares = sums_in_ref[techs : techs + SQUARES, :] + more
    sums_ref[techs : techs + SQUARES, :] = squares
    region_ref[rows:, :] = jnp.concatenate(
        [squares, jnp.zeros((8 - SQUARES, LANES), jnp.float32)], axis=0
    )


def neighbour_rows(sizes, given, hour_index):
    span = sizes.units // LANES

    def row_of(ref, offset):
        return jnp.concatenate([ref[offset + i : offset + i + 1, :] for i in range(span)], axis=1)

    if hasattr(given, "totals"):
        return row_of(given.next_row, 0), row_of(given.prev_row, 0)
    first = halo_at(sizes)
    last = first + span
    core, x_place, slab = hour_index % 2, hour_index // 2 % 2, hour_index // 4 % 2
    next_row = jnp.where(slab == 0, row_of(given.near, first), row_of(given.far, first))
    prev_row = jnp.where(slab == 0, row_of(given.far, last), row_of(given.near, last))
    next_row = jnp.where(x_place == 0, row_of(given.across, first), next_row)
    prev_row = jnp.where(x_place == 0, prev_row, row_of(given.across, last))
    next_row = jnp.where(core == 0, row_of(given.partner, first), next_row)
    prev_row = jnp.where(core == 0, prev_row, row_of(given.partner, last))
    return next_row, prev_row


def total_of(parts):
    if hasattr(parts, "totals"):
        return parts.totals[...]
    return (parts.slab[...] + parts.near[...]) + (parts.middle[...] + parts.far[...])


def sweep_kernel(sizes, iteration, names_in, names_out, *refs):
    rows, techs, nodes = sizes.rows, sizes.techs, sizes.nodes
    slots, regions, lines, units = sizes.slots, sizes.regions, sizes.lines, sizes.units
    second = iteration == 1
    last = iteration == ITERS - 1
    given = Bag(**dict(zip(names_in, refs[: len(names_in)])))
    gives = Bag(**dict(zip(names_out, refs[len(names_in) :])))
    own = lax.axis_index("region")
    hour_index = lax.axis_index("hours")
    gathered = given.gathered

    sums = total_of(given)
    squares = jnp.sum(sums[techs : techs + 2], axis=1, keepdims=True)
    old_weight = jnp.ones((1, 1), jnp.float32) if second else given.weight[...][:, :1]
    weight = jnp.sqrt(
        old_weight * jnp.sqrt((squares[1:2] + EPSILON) / (squares[0:1] + EPSILON))
    )
    primal_step = 0.5 / weight
    if second:
        first = sums_rows(sizes)
        col_weight, cost = sums[first : first + techs], sums[first + techs : first + 2 * techs]
        gives.col_weight[...] = col_weight
        gives.cost[...] = cost
        gives.negative[...] = sums[techs + 2 : techs + 3]
        capacity = jnp.maximum(-cost / col_weight, 0.0)
        first_bar = 2.0 * capacity
    else:
        col_weight, cost = given.col_weight[...], given.cost[...]
        capacity = given.capacity[...]
    capacity_new = jnp.maximum(capacity - (cost - sums[:techs]) / (weight * col_weight), 0.0)
    capacity_bar = 2.0 * capacity_new - capacity

    prices_all = jnp.concatenate([gathered[region, :rows, :] for region in range(regions)], axis=1)
    prices = gathered[own, :rows, :]
    maps_local = given.maps_local[...]
    slope_local = dot3(prices, maps_local, False)
    slope_cross = dot3(prices_all, given.maps_cross[...], False)

    energy = given.store_energy[...]
    row_id = lax.broadcasted_iota(jnp.int32, (rows, units), 0)
    next_row, prev_row = neighbour_rows(sizes, given, hour_index)
    store_duals = given.store_duals[...]
    next_duals = jnp.where(row_id == rows - 1, next_row, pltpu.roll(store_duals, rows - 1, 0))
    if second:
        charge = jnp.zeros((rows, units), jnp.float32)
        charge_before = jnp.zeros((1, units), jnp.float32)
    else:
        charge = given.charge[...]
        charge_before = given.charge_before[...]
    charge_new = jnp.clip(charge - primal_step * (store_duals - next_duals), 0.0, energy)
    gives.charge[...] = charge_new

    primal_row = jnp.zeros((1, LANES), jnp.float32)
    bars = []
    local_out = None if last else gives.flows_local
    cross_out = None if last else gives.flows_cross
    for flows, out, limits, slope, low, high in (
        (given.flows_local, local_out, given.limits_local, slope_local, 0, lines),
        (given.flows_local, local_out, given.limits_local, slope_local, lines, lines + units),
        (given.flows_cross, cross_out, given.limits_cross, slope_cross, 0, regions * slots),
    ):
        slope = slope[:, low:high]
        if low:
            slope = slope + store_duals
        bound = limits[:, low:high]
        old = flows[:, low:high]
        new = jnp.clip(old - primal_step * slope, -bound, bound)
        bars.append(2.0 * new - old)
        if not last:
            out[:, low:high] = new
            change = row_sum((new - old) ** 2)
            if out is cross_out:
                slot = lax.broadcasted_iota(jnp.int32, change.shape, 1)
                change = jnp.where(slot // slots == own, change, 0.0)
            primal_row = primal_row + fold_lanes(change)
    maps_own = given.maps_cross[pl.ds(pl.multiple_of(own * nodes, nodes), nodes), :]
    balance = dot3(jnp.concatenate(bars[:2], axis=1), maps_local, True) - given.demand[...]
    balance = balance + dot3(bars[2], maps_own, True)

    gen_cost = given.gen_cost[...]
    half_weight = weight / 2.0
    primal_acc = jnp.zeros((rows, nodes), jnp.float32)
    dual_acc = jnp.zeros((rows, nodes), jnp.float32)
    for tech in range(techs):
        slope = gen_cost[tech : tech + 1] + prices
        dispatch = given.dispatch[tech]
        avail = given.available[tech]
        if second:
            duals = jnp.maximum(0.5 * (2.0 * dispatch - avail * first_bar[tech : tech + 1]), 0.0)
        else:
            duals = given.cap_duals[tech]
        dispatch_new = jnp.maximum(dispatch - primal_step * (slope + duals), 0.0)
        dispatch_bar = 2.0 * dispatch_new - dispatch
        balance = balance + dispatch_bar
        if last:
            gives.dispatch[pl.ds(tech, rows, stride=techs), :] = dispatch_new
            continue
        gives.dispatch[tech] = dispatch_new
        cap_rows = dispatch_bar - avail * capacity_bar[tech : tech + 1]
        primal_acc = primal_acc + (dispatch_new - dispatch) ** 2
        duals_new = jnp.maximum(duals + half_weight * cap_rows, 0.0)
        dual_acc = dual_acc + (duals_new - duals) ** 2
        gives.cap_duals[tech] = duals_new
        gives.sums[tech : tech + 1, :] = row_sum(avail * duals_new)

    step_up = weight / (techs + 8.0) * balance
    if last:
        gives.prices[...] = prices + step_up
        tech_hot, node_hot = owned_one_hots(given.owner, techs, nodes)
        chosen = dot3(capacity_new, node_hot, False)
        gives.capacity[...] = row_sum(jnp.where(tech_hot, chosen, 0.0))
        return
    gives.block[:rows, :] = prices + step_up
    gives.weight[...] = jnp.broadcast_to(weight, (1, LANES))
    gives.capacity[...] = capacity_new
    charge_bar = 2.0 * charge_new - charge
    before_new = jnp.clip(charge_before - primal_step * (prev_row - store_duals[0:1]), 0.0, energy)
    gives.charge_before[...] = before_new
    before_bar = 2.0 * before_new - charge_before
    shifted_bar = jnp.where(row_id == 0, before_bar, pltpu.roll(charge_bar, 1, 0))
    store_step = weight / 3.0 * (charge_bar - shifted_bar + bars[1])
    store_new = store_duals + store_step
    gives.store_duals[...] = store_new
    primal_row = primal_row + row_sum(primal_acc) + fold_lanes(row_sum((charge_new - charge) ** 2))
    primal_row = primal_row + jnp.where(
        hour_index == 0, row_sum((capacity_new - capacity) ** 2), 0.0
    )
    dual_row = row_sum(dual_acc + step_up * step_up) + fold_lanes(row_sum(store_step * store_step))
    squares = jnp.concatenate(
        [primal_row, dual_row, jnp.zeros((SQUARES - 2, LANES), jnp.float32)], axis=0
    )
    gives.block[rows:, :] = jnp.concatenate(
        [squares, jnp.zeros((8 - SQUARES, LANES), jnp.float32)], axis=0
    )
    gives.sums[techs : techs + SQUARES, :] = squares
    write_halo(sizes, gives.sums, store_new)


def call(kernel, given, outs, flops=0, smem=()):
    names_in, names_out = tuple(vars(given)), tuple(vars(outs))
    values = pl.pallas_call(
        functools.partial(kernel, names_in, names_out),
        out_shape=tuple(vars(outs).values()),
        in_specs=[
            pl.BlockSpec(memory_space=pltpu.SMEM if i in smem else pltpu.VMEM)
            for i in range(len(names_in))
        ],
        out_specs=[pl.BlockSpec(memory_space=pltpu.VMEM)] * len(names_out),
        cost_estimate=pl.CostEstimate(flops=flops, bytes_accessed=4 * flops, transcendentals=0),
        compiler_params=pltpu.CompilerParams(vmem_limit_bytes=VMEM_BYTES),
    )(*vars(given).values())
    return Bag(**dict(zip(names_out, values)))


def swap(value, hour_bit, region_bit):
    hours, regions = lax.axis_size("hours"), lax.axis_size("region")
    pairs = [
        (hour * regions + region, (hour ^ hour_bit) * regions + (region ^ region_bit))
        for hour in range(hours)
        for region in range(regions)
    ]
    return lax.ppermute(value, ("hours", "region"), pairs)


def shifted(value, steps):
    count = lax.axis_size("hours")
    return lax.ppermute(value, "hours", [(i, (i + steps) % count) for i in range(count)])


def both_regions(block):
    if lax.axis_size("region") != 2:
        return lax.all_gather(block, "region")
    return in_order(block, swap(block, 0, 1))


def in_order(block, other):
    return jnp.where(
        lax.axis_index("region") == 0, jnp.stack([block, other]), jnp.stack([other, block])
    )


def exchange(sizes, block, sums):
    hours, regions = lax.axis_size("hours"), lax.axis_size("region")
    techs, rows, span = sizes.techs, sizes.rows, sizes.units // LANES
    halo = halo_at(sizes)
    if regions != 2 or hours != 16:
        gathered = lax.all_gather(block, "region")
        squares = jnp.sum(gathered[:, rows : rows + SQUARES], axis=0)
        totals = lax.psum(sums.at[techs:halo].set(squares), "hours")
        next_row = shifted(sums[halo : halo + span], -1)
        prev_row = shifted(sums[halo + span : halo + 2 * span], 1)
        return gathered, Bag(totals=totals, next_row=next_row, prev_row=prev_row)

    def merged(mine, yours, mine_first):
        row = lax.broadcasted_iota(jnp.int32, mine.shape, 0)
        keep = jnp.where(row < halo + span, mine_first, jnp.logical_not(mine_first))
        edge = (row >= halo) & (row < halo + 2 * span)
        return jnp.where(edge, jnp.where(keep, mine, yours), mine + yours)

    hour = lax.axis_index("hours")
    partner = swap(sums, 1, 0)
    chip = merged(sums, partner, hour % 2 == 0)
    across = swap(chip, 2, 0)
    other = swap(block.at[rows : rows + SQUARES].set(chip[techs:halo]), 0, 1)
    diagonal = swap(chip[techs:halo], 2, 1)
    slab = merged(chip, across, hour // 2 % 2 == 0)
    slab = slab.at[techs:halo].add(other[rows : rows + SQUARES] + diagonal)
    near, middle, far = [swap(slab, 4 * step, 0) for step in (1, 2, 3)]
    parts = Bag(slab=slab, near=near, middle=middle, far=far, partner=partner, across=across)
    return in_order(block, other), parts


def shape(*dims, dtype=jnp.float32):
    return jax.ShapeDtypeStruct(dims, dtype)


def corrected(sizes, state, block, sums, parts):
    techs, rows = sizes.techs, sizes.rows
    totals = total_of(parts)
    first = sums_rows(sizes)
    col_weight, cost = totals[first : first + techs], totals[first + techs :]
    capacity = jnp.maximum(-cost / col_weight, 0.0)
    taken = state.dispatch
    rows_of = 2.0 * taken - state.available * (2.0 * capacity)[:, None, :]
    duals = jnp.maximum(0.5 * rows_of, 0.0)
    own = jnp.where(lax.axis_index("hours") == 0, jnp.sum(capacity**2, axis=0), 0.0)
    fixed = sums.at[:techs].set(jnp.sum(state.available * duals, axis=1))
    fixed = fixed.at[techs].add(own)
    fixed = fixed.at[techs + 1].add(jnp.sum(duals**2 - taken**2, axis=(0, 1)))
    block = block.at[rows : rows + SQUARES].set(fixed[techs : techs + SQUARES])
    return exchange(sizes, block, fixed)[1]


def run(args, exact):
    rows, techs, nodes = args.availability.shape
    hours, regions = lax.axis_size("hours"), lax.axis_size("region")
    slots, owned = args.cross_limit.shape[1], args.cap_cost.shape[1]
    units, lines = args.store_node.shape[0], args.line_limit.shape[0]
    sizes = Bag(
        rows=rows, techs=techs, nodes=nodes, regions=regions, slots=slots, lines=lines, units=units
    )
    cross = regions * slots

    gathered = both_regions(args.price_start)
    info = call(
        lambda names_in, names_out, *refs: slots_kernel(sizes, *refs),
        Bag(ends=args.cross_ends[:, 0], limit=args.cross_limit, pairs=args.pair_counts),
        Bag(info=shape(8 * (cross // LANES), nodes)),
        smem=(2,),
    ).info
    info = both_regions(info)
    state = call(
        functools.partial(start_kernel, sizes),
        Bag(
            availability=args.availability.reshape(rows * techs, nodes),
            price=args.price_start,
            demand=args.demand,
            gen_cost=args.gen_cost,
            cap_cost=args.cap_cost,
            owner=args.owner_map.reshape(hours, owned),
            line_ends=args.line_ends,
            line_limit=args.line_limit[None],
            store_node=args.store_node[None],
            store_power=args.store_power[None],
            store_energy=args.store_energy[None],
        ),
        Bag(
            demand=shape(rows, nodes),
            gen_cost=shape(techs, nodes),
            owner=shape(hours, owned, dtype=jnp.int32),
            store_energy=shape(1, units),
            available=shape(techs, rows, nodes),
            maps_local=shape(nodes, lines + units, dtype=jnp.bfloat16),
            limits_local=shape(1, lines + units),
            flows_local=shape(rows, lines + units),
            store_duals=shape(rows, units),
            dispatch=shape(techs, rows, nodes),
            balance=shape(rows, nodes),
            sums=shape(sums_rows(sizes) + 2 * techs, nodes),
        ),
        flops=10**6,
    )
    closed = call(
        lambda names_in, names_out, *refs: close_kernel(sizes, *refs),
        Bag(gathered=gathered, info=info, balance=state.balance, sums=state.sums),
        Bag(
            maps=shape(regions * nodes, cross, dtype=jnp.bfloat16),
            limits=shape(1, cross),
            flows=shape(rows, cross),
            block=shape(rows + 8, nodes),
            sums=shape(*state.sums.shape),
        ),
    )
    del state.sums, state.balance
    state.maps_cross, state.limits_cross = closed.maps, closed.limits
    state.flows_cross = closed.flows
    gathered, parts = exchange(sizes, closed.block, closed.sums)
    if exact:
        parts = corrected(sizes, state, closed.block, closed.sums, parts)

    negative = None
    for iteration in range(1, ITERS):
        given = Bag(**vars(state), **vars(parts), gathered=gathered)
        if iteration < ITERS - 1:
            del given.owner
            outs = Bag(
                dispatch=shape(techs, rows, nodes),
                cap_duals=shape(techs, rows, nodes),
                flows_local=shape(rows, lines + units),
                flows_cross=shape(rows, cross),
                store_duals=shape(rows, units),
                capacity=shape(techs, nodes),
                weight=shape(1, LANES),
                charge=shape(rows, units),
                charge_before=shape(1, units),
                block=shape(rows + 8, nodes),
                sums=shape(sums_rows(sizes), nodes),
            )
            if iteration == 1:
                outs.col_weight, outs.cost = shape(techs, nodes), shape(techs, nodes)
                outs.negative = shape(1, LANES)
        else:
            outs = Bag(
                dispatch=shape(rows * techs, nodes),
                capacity=shape(1, owned),
                prices=shape(rows, nodes),
                charge=shape(rows, units),
            )
        results = call(functools.partial(sweep_kernel, sizes, iteration), given, outs)
        if iteration == 1:
            negative = results.negative[0, 0]
            del results.negative
        if iteration < ITERS - 1:
            gathered, parts = exchange(sizes, results.block, results.sums)
            del results.block, results.sums
            vars(state).update(vars(results))
    dispatch = results.dispatch.reshape(rows, techs, nodes)
    return (dispatch, results.capacity, results.prices, results.charge), negative


def body(
    availability,
    demand,
    gen_cost,
    cap_cost,
    owner_map,
    line_ends,
    line_limit,
    cross_ends,
    cross_limit,
    pair_counts,
    store_node,
    store_energy,
    store_power,
    price_start,
):
    args = Bag(**locals())
    outputs, negative = run(args, False)
    return lax.cond(negative > 0.0, lambda: run(args, True)[0], lambda: outputs)


def solution(mesh):
    placed = (
        P("hours", None, "region"),
        P("hours", "region"),
        P(None, "region"),
        P("region", "hours"),
        P("region", None),
        P(None, "region"),
        P("region"),
        P(None, "region", None),
        P("region", None),
        P("region", None),
        P("region"),
        P("region"),
        P("region"),
        P("hours", "region"),
    )
    return jax.shard_map(
        body,
        mesh=mesh,
        in_specs=placed,
        out_specs=(
            P("hours", None, "region"),
            P("region", "hours"),
            P("hours", "region"),
            P("hours", "region"),
        ),
        check_vma=False,
    )
```

time: 69.7 us -> 64.3 us (0.923)
  waiting for transfers between devices: 17 us -> 21.7 us
  local copies, waits for them, and re-layouts: 10.2 us -> 6.82 us
  Pallas kernels: 8.17 us -> 5.82 us
  between operations: 3.6 us -> 1.3 us
  other arithmetic: 2.58 us -> 0.54 us
    slice x4 -> x0, local copies, waits for them, and re-layouts: 4.78 us -> none  [body(): negative = total_of(parts)[techs + 2, 0]]
    ppermute x22 -> x23, waiting for transfers between devices: 17 us -> 21.7 us  [swap(): return lax.ppermute(value, ('hours', 'region'), pairs)]
    unnamed x35 -> x103, local copies, waits for them, and re-layouts: 3.83 us -> 6.43 us
    pallas_call x6, Pallas kernels: 8.17 us -> 5.82 us  [call(): pl.pallas_call(functools.partial(kernel, names_in, names_out), out_shape=...]
    select_n x6, other arithmetic: 1.81 us -> 0.45 us  [merged(): return jnp.where(edge, jnp.where(keep, mine, yours), mine + yours)]
    scatter-add x3, local copies, waits for them, and re-layouts: 1.42 us -> 0.22 us  [exchange(): slab = slab.at[techs:halo].add(other[rows:rows + SQUARES] + diagonal)]
    ppermute x22 -> x23, starting transfers between devices: 27.4 us -> 27.6 us  [swap(): return lax.ppermute(value, ('hours', 'region'), pairs)]
  transfers between devices with their start and end apart: 22 -> 23, of which waited for: 18 -> 18; matrix products, arithmetic and copies ran while one was open for 8% -> 1% of each run, Pallas kernels for 2% -> 3%
where the time goes in v6:
time: 64.3 us; the launch traced here: 64 us
  starting transfers between devices  27.6 us (43%)
  waiting for transfers between devices  21.7 us (34%)
  local copies, waits for them, and re-layouts  6.82 us (11%)
  Pallas kernels  5.82 us (9%)
  between operations  1.3 us (2%)
    ppermute x23, starting transfers between devices, swap(): return lax.ppermute(value, ('hours', 'region'), pairs)  27.6 us
    ppermute x23, waiting for transfers between devices, swap(): return lax.ppermute(value, ('hours', 'region'), pairs)  21.7 us
    unnamed x103, local copies, waits for them, and re-layouts  6.43 us
    pallas_call x6, Pallas kernels, call(): pl.pallas_call(functools.partial(kernel, names_in, names_out), out_shape=...  5.82 us
  transfers between devices with their start and end apart: 23, of which 18 were waited for; matrix products, arithmetic and copies ran while one was open for 1% of the time, Pallas kernels for 3%

profile of v6, /device:TPU:0, one launch (start us, length us, event | category | flops | bytes accessed | tf_op | source)
XLA Modules:
  0.0 64.0 jit_solution(11199925400067930080)
XLA Ops:
  0.7 0.6 copy-done.64
  1.3 0.8 %shard_map.166 = f32[8,128]{1,0:T(8,128)S(1)} custom-call(s32[2,64]{1,0:T(2,128)S(1)} %bitcast.77, f32[1,64]{1,0:T(1,128)S(1)} %copy-done.64, s32[1,2]{1,0:T(1,128)} %refs_2_.3), custom_call_target="tpu_custom_call" | custom-call | tf_op jit(solution)/shard_map/pallas_call | solution.py:371
  2.1 3.0 %collective-permute-start.31 = (f32[8,128]{1,0:T(8,128)S(1)}, f32[8,128]{1,0:T(8,128)S(1)}, u32[]{:S(2)}, u32[]{:S(2)}) collective-permute-start(f32[8,128]{1,0:T(8,128)S(1)} %shard_map.166), channel_id=1, source_target_pairs={{0,1},{1,0},{2,3},{3,2},{4,5},{5,4},{6,7},{7,6},{8,9},{9,8},{10,11... | collective-permute-start | bytes 12296 | tf_op jit(solution)/shard_map/ppermute | solution.py:392
  5.2 0.6 copy-done.50
  5.9 1.7 %shard_map.165 = (f32[64,128]{1,0:T(8,128)S(1)}, f32[16,128]{1,0:T(8,128)S(1)}, s32[16,128]{1,0:T(8,128)S(1)}, f32[1,256]{1,0:T(1,128)S(1)}, f32[16,64,128]{2,1,...) custom-call(f32[1024,128]{1,0:T(8,128)} %bitcast.53, ...), custom_call_target="tpu_custom_call" | custom-call | flops 1000000 | bytes 4000000 | tf_op jit(solution)/shard_map/pallas_call | solution.py:371
  7.7 1.5 %collective-permute-done.30 = f32[64,128]{1,0:T(8,128)S(1)} collective-permute-done((f32[64,128]{1,0:T(8,128)}, f32[64,128]{1,0:T(8,128)S(1)}, u32[]{:S(2)}, u32[]{:S(2)}) %collective-permute-start.30) | collective-permute-done | bytes 32800 | tf_op jit(solution)/shard_map/ppermute | solution.py:392
  9.2 0.4 shard_map.167
  9.6 0.1 collective-permute-start.32
  9.8 1.1 %collective-permute-done.32.refs_16_ = f32[56,128]{1,0:T(8,128)S(1)} collective-permute-done((f32[56,128]{1,0:T(8,128)S(1)}, f32[56,128]{1,0:T(8,128)S(1)}, u32[]{:S(2)}, u32[]{:S(2)}) %collective-permute-start.32) | collective-permute-done | bytes 28704 | tf_op jit(solution)/shard_map/ppermute | solution.py:392
  10.9 0.1 add_select_fusion.9
  11.0 1.6 %collective-permute-start.33 = (f32[56,128]{1,0:T(8,128)S(1)}, f32[56,128]{1,0:T(8,128)S(1)}, u32[]{:S(2)}, u32[]{:S(2)}) collective-permute-start(f32[56,128]{1,0:T(8,128)S(1)} %add_select_fusion.9), channel_id=1, source_target_pairs={{0,4},{1,5},{2,6},{3,7},{4,0},{5,1},{6,2},{7,3},{8,12},{9,13},{10,... | collective-permute-start | bytes 86024 | tf_op jit(solution)/shard_map/ppermute | solution.py:392
  12.6 0.5 collective-permute-start.35
  13.1 1.6 %collective-permute-start.34 = (f32[72,128]{1,0:T(8,128)S(1)}, f32[72,128]{1,0:T(8,128)S(1)}, u32[]{:S(2)}, u32[]{:S(2)}) collective-permute-start(f32[72,128]{1,0:T(8,128)S(1)} %scatter.30), channel_id=1, source_target_pairs={{0,1},{1,0},{2,3},{3,2},{4,5},{5,4},{6,7},{7,6},{8,9},{9,8},{10,11... | collective-permute-start | bytes 110600 | tf_op jit(solution)/shard_map/ppermute | solution.py:392
  14.7 0.2 collective-permute-done.33.refs_17_
  14.9 0.1 add_select_fusion.8
  15.0 2.2 %collective-permute-done.35 = f32[3,128]{1,0:T(4,128)S(1)} collective-permute-done((f32[3,128]{1,0:T(4,128)S(1)}, f32[3,128]{1,0:T(4,128)S(1)}, u32[]{:S(2)}, u32[]{:S(2)}) %collective-permute-start.35) | collective-permute-done | bytes 1568 | tf_op jit(solution)/shard_map/ppermute | solution.py:392
  17.2 0.1 scatter-add.30.refs_12_
  17.3 3.7 %collective-permute-start.38 = (f32[56,128]{1,0:T(8,128)S(1)}, f32[56,128]{1,0:T(8,128)S(1)}, u32[]{:S(2)}, u32[]{:S(2)}) collective-permute-start(f32[56,128]{1,0:T(8,128)S(1)} %scatter-add.30.refs_12_), channel_id=1, source_target_pairs={{0,24},{1,25},{2,26},{3,27},{4,28},{5,29},{6,30},{7,31},{8,16},{9,... | collective-permute-start | bytes 86024 | tf_op jit(solution)/shard_map/ppermute | solution.py:392
  21.0 0.8 %collective-permute-start.36 = (f32[56,128]{1,0:T(8,128)S(1)}, f32[56,128]{1,0:T(8,128)S(1)}, u32[]{:S(2)}, u32[]{:S(2)}) collective-permute-start(f32[56,128]{1,0:T(8,128)S(1)} %scatter-add.30.refs_12_), channel_id=1, source_target_pairs={{0,8},{1,9},{2,10},{3,11},{4,12},{5,13},{6,14},{7,15},{8,0},{9,1},... | collective-permute-start | bytes 86024 | tf_op jit(solution)/shard_map/ppermute | solution.py:392
  21.8 1.3 %collective-permute-done.38.refs_15_ = f32[56,128]{1,0:T(8,128)S(1)} collective-permute-done((f32[56,128]{1,0:T(8,128)S(1)}, f32[56,128]{1,0:T(8,128)S(1)}, u32[]{:S(2)}, u32[]{:S(2)}) %collective-permute-start.38) | collective-permute-done | bytes 28704 | tf_op jit(solution)/shard_map/ppermute | solution.py:392
  23.0 2.7 %collective-permute-done.37.refs_14_ = f32[56,128]{1,0:T(8,128)S(1)} collective-permute-done((f32[56,128]{1,0:T(8,128)S(1)}, f32[56,128]{1,0:T(8,128)S(1)}, u32[]{:S(2)}, u32[]{:S(2)}) %collective-permute-start.37) | collective-permute-done | bytes 28704 | tf_op jit(solution)/shard_map/ppermute | solution.py:392
  25.8 0.8 %shard_map.168 = (f32[16,64,128]{2,1,0:T(8,128)S(1)}, f32[16,64,128]{2,1,0:T(8,128)S(1)}, f32[64,512]{1,0:T(8,128)S(1)}, f32[64,128]{1,0:T(8,128)S(1)}, f32[64,2...) custom-call(f32[64,128]{1,0:T(8,128)S(1)} %get-tuple-element.366.ref, ...), custom_call_target="tpu_custom_call" | custom-call | tf_op jit(solution)/shard_map/pallas_call | solution.py:371
  26.6 0.6 copy-done.18
  27.1 0.6 copy-done.26
  27.7 0.5 copy-done.30
  28.2 1.2 %collective-permute-done.39.refs_23_ = f32[24,128]{1,0:T(8,128)S(1)} collective-permute-done((f32[24,128]{1,0:T(8,128)S(1)}, f32[24,128]{1,0:T(8,128)S(1)}, u32[]{:S(2)}, u32[]{:S(2)}) %collective-permute-start.39) | collective-permute-done | bytes 12320 | tf_op jit(solution)/shard_map/ppermute | solution.py:392
  29.4 0.1 add_select_fusion.13
  29.5 1.5 %collective-permute-start.40 = (f32[24,128]{1,0:T(8,128)S(1)}, f32[24,128]{1,0:T(8,128)S(1)}, u32[]{:S(2)}, u32[]{:S(2)}) collective-permute-start(f32[24,128]{1,0:T(8,128)S(1)} %add_select_fusion.13), channel_id=1, source_target_pairs={{0,4},{1,5},{2,6},{3,7},{4,0},{5,1},{6,2},{7,3},{8,12},{9,13},{10,... | collective-permute-start | bytes 36872 | tf_op jit(solution)/shard_map/ppermute | solution.py:392
  31.0 1.6 %collective-permute-start.42 = (f32[3,128]{1,0:T(4,128)S(1)}, f32[3,128]{1,0:T(4,128)S(1)}, u32[]{:S(2)}, u32[]{:S(2)}) collective-permute-start(f32[3,128]{1,0:T(4,128)S(1)} %slice.411), channel_id=1, source_target_pairs={{0,5},{1,4},{2,7},{3,6},{4,1},{5,0},{6,3},{7,2},{8,13},{9,12},{10,... | collective-permute-start | bytes 4616 | tf_op jit(solution)/shard_map/ppermute | solution.py:392
  32.6 0.6 collective-permute-start.41
  33.3 0.1 add_select_fusion.12
  33.3 2.2 %collective-permute-done.42 = f32[3,128]{1,0:T(4,128)S(1)} collective-permute-done((f32[3,128]{1,0:T(4,128)S(1)}, f32[3,128]{1,0:T(4,128)S(1)}, u32[]{:S(2)}, u32[]{:S(2)}) %collective-permute-start.42) | collective-permute-done | bytes 1568 | tf_op jit(solution)/shard_map/ppermute | solution.py:392
  35.6 1.1 %collective-permute-done.41 = f32[72,128]{1,0:T(8,128)S(1)} collective-permute-done((f32[72,128]{1,0:T(8,128)S(1)}, f32[72,128]{1,0:T(8,128)S(1)}, u32[]{:S(2)}, u32[]{:S(2)}) %collective-permute-start.41) | collective-permute-done | bytes 36896 | tf_op jit(solution)/shard_map/ppermute | solution.py:392
  36.7 0.1 scatter-add.31.refs_19_
  36.7 1.5 %collective-permute-start.45 = (f32[24,128]{1,0:T(8,128)S(1)}, f32[24,128]{1,0:T(8,128)S(1)}, u32[]{:S(2)}, u32[]{:S(2)}) collective-permute-start(f32[24,128]{1,0:T(8,128)S(1)} %scatter-add.31.refs_19_), channel_id=1, source_target_pairs={{0,24},{1,25},{2,26},{3,27},{4,28},{5,29},{6,30},{7,31},{8,16},{9,... | collective-permute-start | bytes 36872 | tf_op jit(solution)/shard_map/ppermute | solution.py:392
  38.2 0.6 collective-permute-start.44
  38.9 2.3 %collective-permute-start.43 = (f32[24,128]{1,0:T(8,128)S(1)}, f32[24,128]{1,0:T(8,128)S(1)}, u32[]{:S(2)}, u32[]{:S(2)}) collective-permute-start(f32[24,128]{1,0:T(8,128)S(1)} %scatter-add.31.refs_19_), channel_id=1, source_target_pairs={{0,8},{1,9},{2,10},{3,11},{4,12},{5,13},{6,14},{7,15},{8,0},{9,1},... | collective-permute-start | bytes 36872 | tf_op jit(solution)/shard_map/ppermute | solution.py:392
  41.2 1.1 %collective-permute-done.45.refs_22_ = f32[24,128]{1,0:T(8,128)S(1)} collective-permute-done((f32[24,128]{1,0:T(8,128)S(1)}, f32[24,128]{1,0:T(8,128)S(1)}, u32[]{:S(2)}, u32[]{:S(2)}) %collective-permute-start.45) | collective-permute-done | bytes 12320 | tf_op jit(solution)/shard_map/ppermute | solution.py:392
  42.3 0.6 collective-permute-done.44.refs_21_
  42.9 0.1 collective-permute-done.43.refs_20_
  43.0 0.7 %copy-done.5 = f32[16,128]{1,0:T(8,128)S(1)} copy-done((f32[16,128]{1,0:T(8,128)S(1)}, f32[16,128]{1,0:T(8,128)}, u32[]{:S(2)}) %copy-start.5) | copy-done | bytes 8216
  43.7 0.8 %shard_map.169 = (f32[16,64,128]{2,1,0:T(8,128)S(1)}, f32[16,64,128]{2,1,0:T(8,128)S(1)}, f32[64,512]{1,0:T(8,128)S(1)}, f32[64,128]{1,0:T(8,128)S(1)}, f32[64,2...) custom-call(f32[64,128]{1,0:T(8,128)S(1)} %get-tuple-element.366.ref, ...), custom_call_target="tpu_custom_call" | custom-call | tf_op jit(solution)/shard_map/pallas_call | solution.py:371
  44.5 0.6 copy-done.22
  45.1 0.1 collective-permute-start.46
  45.1 1.2 %collective-permute-done.46.refs_24_ = f32[24,128]{1,0:T(8,128)S(1)} collective-permute-done((f32[24,128]{1,0:T(8,128)S(1)}, f32[24,128]{1,0:T(8,128)S(1)}, u32[]{:S(2)}, u32[]{:S(2)}) %collective-permute-start.46) | collective-permute-done | bytes 12320 | tf_op jit(solution)/shard_map/ppermute | solution.py:392
  46.3 0.1 add_select_fusion.11
  46.4 1.6 %collective-permute-start.47 = (f32[24,128]{1,0:T(8,128)S(1)}, f32[24,128]{1,0:T(8,128)S(1)}, u32[]{:S(2)}, u32[]{:S(2)}) collective-permute-start(f32[24,128]{1,0:T(8,128)S(1)} %add_select_fusion.11), channel_id=1, source_target_pairs={{0,4},{1,5},{2,6},{3,7},{4,0},{5,1},{6,2},{7,3},{8,12},{9,13},{10,... | collective-permute-start | bytes 36872 | tf_op jit(solution)/shard_map/ppermute | solution.py:392
  48.0 0.7 %copy-done.31 = f32[1,128]{1,0:T(1,128)S(1)} copy-done((f32[1,128]{1,0:T(1,128)S(1)}, f32[1,128]{1,0:T(1,128)}, u32[]{:S(2)}) %copy-start.31) | copy-done | bytes 536
  48.7 0.6 collective-permute-start.49
  49.4 1.5 %collective-permute-start.48 = (f32[72,128]{1,0:T(8,128)S(1)}, f32[72,128]{1,0:T(8,128)S(1)}, u32[]{:S(2)}, u32[]{:S(2)}) collective-permute-start(f32[72,128]{1,0:T(8,128)S(1)} %scatter.34), channel_id=1, source_target_pairs={{0,1},{1,0},{2,3},{3,2},{4,5},{5,4},{6,7},{7,6},{8,9},{9,8},{10,11... | collective-permute-start | bytes 110600 | tf_op jit(solution)/shard_map/ppermute | solution.py:392
  50.9 0.1 add_select_fusion.10
  51.0 2.4 %collective-permute-done.49 = f32[3,128]{1,0:T(4,128)S(1)} collective-permute-done((f32[3,128]{1,0:T(4,128)S(1)}, f32[3,128]{1,0:T(4,128)S(1)}, u32[]{:S(2)}, u32[]{:S(2)}) %collective-permute-start.49) | collective-permute-done | bytes 1568 | tf_op jit(solution)/shard_map/ppermute | solution.py:392
  53.3 0.1 collective-permute-done.48
  53.5 2.5 %collective-permute-start.52 = (f32[24,128]{1,0:T(8,128)S(1)}, f32[24,128]{1,0:T(8,128)S(1)}, u32[]{:S(2)}, u32[]{:S(2)}) collective-permute-start(f32[24,128]{1,0:T(8,128)S(1)} %scatter-add.34.refs_20_), channel_id=1, source_target_pairs={{0,24},{1,25},{2,26},{3,27},{4,28},{5,29},{6,30},{7,31},{8,16},{9,... | collective-permute-start | bytes 36872 | tf_op jit(solution)/shard_map/ppermute | solution.py:392
  56.0 0.9 %collective-permute-start.51 = (f32[24,128]{1,0:T(8,128)S(1)}, f32[24,128]{1,0:T(8,128)S(1)}, u32[]{:S(2)}, u32[]{:S(2)}) collective-permute-start(f32[24,128]{1,0:T(8,128)S(1)} %scatter-add.34.refs_20_), channel_id=1, source_target_pairs={{0,16},{1,17},{2,18},{3,19},{4,20},{5,21},{6,22},{7,23},{8,24},{9,... | collective-permute-start | bytes 36872 | tf_op jit(solution)/shard_map/ppermute | solution.py:392
  56.9 1.0 %collective-permute-start.50 = (f32[24,128]{1,0:T(8,128)S(1)}, f32[24,128]{1,0:T(8,128)S(1)}, u32[]{:S(2)}, u32[]{:S(2)}) collective-permute-start(f32[24,128]{1,0:T(8,128)S(1)} %scatter-add.34.refs_20_), channel_id=1, source_target_pairs={{0,8},{1,9},{2,10},{3,11},{4,12},{5,13},{6,14},{7,15},{8,0},{9,1},... | collective-permute-start | bytes 36872 | tf_op jit(solution)/shard_map/ppermute | solution.py:392
  58.0 1.1 %collective-permute-done.52.refs_23_ = f32[24,128]{1,0:T(8,128)S(1)} collective-permute-done((f32[24,128]{1,0:T(8,128)S(1)}, f32[24,128]{1,0:T(8,128)S(1)}, u32[]{:S(2)}, u32[]{:S(2)}) %collective-permute-start.52) | collective-permute-done | bytes 12320 | tf_op jit(solution)/shard_map/ppermute | solution.py:392
  59.1 1.5 %collective-permute-done.51.refs_22_ = f32[24,128]{1,0:T(8,128)S(1)} collective-permute-done((f32[24,128]{1,0:T(8,128)S(1)}, f32[24,128]{1,0:T(8,128)S(1)}, u32[]{:S(2)}, u32[]{:S(2)}) %collective-permute-start.51) | collective-permute-done | bytes 12320 | tf_op jit(solution)/shard_map/ppermute | solution.py:392
  60.6 0.1 collective-permute-done.50.refs_21_
  60.7 0.7 %copy-done.1 = f32[16,128]{1,0:T(8,128)S(1)} copy-done((f32[16,128]{1,0:T(8,128)S(1)}, f32[16,128]{1,0:T(8,128)}, u32[]{:S(2)}) %copy-start.1) | copy-done | bytes 8216
  61.6 1.4 %shard_map.170 = (f32[1024,128]{1,0:T(8,128)}, f32[1,128]{1,0:T(1,128)S(1)}, f32[64,128]{1,0:T(8,128)S(1)}, f32[64,256]{1,0:T(8,128)}) custom-call(f32[64,128]{1,0:T(8,128)S(1)} %get-tuple-element.366.refs_0_, f32[16,128]{1,0:T(8,128)S(1)} %get-tuple-element.367.refs_1_, s32[16,128]{1,0:T(8,128)S(1)} %get-tuple-element.383.refs_2_, ...), custom_call_target="tpu_custom_call" | custom-call | tf_op jit(solution)/shard_map/pallas_call | solution.py:371
  63.1 0.2 conditional.1
  63.3 0.5 copy-done.70
  63.8 0.1 copy-done.69
  (120 shorter events, 0.8 us)
Async XLA Ops:
  0.6 0.7 %copy-start.54 = (s32[2,1,64]{2,1,0:T(1,128)S(1)}, s32[2,1,64]{2,1,0:T(1,128)}, u32[]{:S(2)}) copy-start(s32[2,1,64]{2,1,0:T(1,128)} %param.59) | copy-start | bytes 1540
  0.7 4.6 %copy-start.33 = (f32[64,128]{1,0:T(8,128)S(1)}, f32[64,128]{1,0:T(8,128)}, u32[]{:S(2)}) copy-start(f32[64,128]{1,0:T(8,128)} %refs_1_.2) | copy-start | bytes 98308
  2.1 5.6 %collective-permute-start.31 = (f32[8,128]{1,0:T(8,128)S(1)}, f32[8,128]{1,0:T(8,128)S(1)}, u32[]{:S(2)}, u32[]{:S(2)}) collective-permute-start(f32[8,128]{1,0:T(8,128)S(1)} %shard_map.166), channel_id=1, source_target_pairs={{0,1},{1,0},{2,3},{3,2},{4,5},{5,4},{6,7},{7,6},{8,9},{9,8},{10,11... | collective-permute-start | bytes 12296 | tf_op jit(solution)/shard_map/ppermute | solution.py:392
  5.1 4.1 %collective-permute-start.30 = (f32[64,128]{1,0:T(8,128)}, f32[64,128]{1,0:T(8,128)S(1)}, u32[]{:S(2)}, u32[]{:S(2)}) collective-permute-start(f32[64,128]{1,0:T(8,128)} %refs_1_.2), channel_id=1, source_target_pairs={{0,1},{1,0},{2,3},{3,2},{4,5},{5,4},{6,7},{7,6},{8,9},{9,8},{10,11... | collective-permute-start | bytes 98312 | tf_op jit(solution)/shard_map/ppermute | solution.py:392
  5.1 0.7 %copy-start.52 = (f32[256]{0:T(256)S(1)}, f32[256]{0:T(256)}, u32[]{:S(2)}) copy-start(f32[256]{0:T(256)} %param.63) | copy-start | bytes 3076
  5.1 0.7 %copy-start.48 = (s32[256]{0:T(256)S(1)}, s32[256]{0:T(256)}, u32[]{:S(2)}) copy-start(s32[256]{0:T(256)} %param.62) | copy-start | bytes 3076
  5.1 0.7 %copy-start.67 = (f32[1,128]{1,0:T(1,128)S(1)}, f32[1,128]{1,0:T(1,128)}, u32[]{:S(2)}) copy-start(f32[1,128]{1,0:T(1,128)} %refs_4_.1) | copy-start | bytes 1540
  5.2 0.7 %copy-start.40 = (s32[2,256]{1,0:T(2,128)S(1)}, s32[2,256]{1,0:T(2,128)}, u32[]{:S(2)}) copy-start(s32[2,256]{1,0:T(2,128)} %refs_6_.1) | copy-start | bytes 6148
  5.2 0.7 %copy-start.38 = (s32[1,2048]{1,0:T(1,128)S(1)}, s32[1,2048]{1,0:T(1,128)}, u32[]{:S(2)}) copy-start(s32[1,2048]{1,0:T(1,128)} %param.56) | copy-start | bytes 24580
  5.2 0.7 %copy-start.36 = (f32[16,128]{1,0:T(8,128)S(1)}, f32[16,128]{1,0:T(8,128)}, u32[]{:S(2)}) copy-start(f32[16,128]{1,0:T(8,128)} %refs_3_.1) | copy-start | bytes 24580
  5.2 0.7 %copy-start.46 = (f32[256]{0:T(256)S(1)}, f32[256]{0:T(256)}, u32[]{:S(2)}) copy-start(f32[256]{0:T(256)} %param.58) | copy-start | bytes 3076
  9.6 16.2 %copy-start.11 = (f32[1,128]{1,0:T(1,128)}, f32[1,128]{1,0:T(1,128)S(1)}, u32[]{:S(2)}) copy-start(f32[1,128]{1,0:T(1,128)S(1)} %get-tuple-element.378.refs_10_.refs_11_) | copy-start | bytes 1540
  9.6 1.3 %collective-permute-start.32 = (f32[56,128]{1,0:T(8,128)S(1)}, f32[56,128]{1,0:T(8,128)S(1)}, u32[]{:S(2)}, u32[]{:S(2)}) collective-permute-start(f32[56,128]{1,0:T(8,128)S(1)} %get-tuple-element.380), channel_id=1, source_target_pairs={{0,2},{1,3},{2,0},{3,1},{4,6},{5,7},{6,4},{7,5},{8,10},{9,11},{10,... | collective-permute-start | bytes 86024 | tf_op jit(solution)/shard_map/ppermute | solution.py:392
  9.7 23.6 %copy-start.42 = (pred[24]{0:T(512)(128)(4,1)}, pred[24]{0:T(512)(128)(4,1)S(1)}, u32[]{:S(2)}) copy-start(pred[24]{0:T(512)(128)(4,1)S(1)} %compare_and_fusion.2) | copy-start | bytes 76
  11.0 3.9 %collective-permute-start.33 = (f32[56,128]{1,0:T(8,128)S(1)}, f32[56,128]{1,0:T(8,128)S(1)}, u32[]{:S(2)}, u32[]{:S(2)}) collective-permute-start(f32[56,128]{1,0:T(8,128)S(1)} %add_select_fusion.9), channel_id=1, source_target_pairs={{0,4},{1,5},{2,6},{3,7},{4,0},{5,1},{6,2},{7,3},{8,12},{9,13},{10,... | collective-permute-start | bytes 86024 | tf_op jit(solution)/shard_map/ppermute | solution.py:392
  12.6 4.6 %collective-permute-start.35 = (f32[3,128]{1,0:T(4,128)S(1)}, f32[3,128]{1,0:T(4,128)S(1)}, u32[]{:S(2)}, u32[]{:S(2)}) collective-permute-start(f32[3,128]{1,0:T(4,128)S(1)} %slice.408), channel_id=1, source_target_pairs={{0,5},{1,4},{2,7},{3,6},{4,1},{5,0},{6,3},{7,2},{8,13},{9,12},{10,... | collective-permute-start | bytes 4616 | tf_op jit(solution)/shard_map/ppermute | solution.py:392
  13.1 4.0 %collective-permute-start.34 = (f32[72,128]{1,0:T(8,128)S(1)}, f32[72,128]{1,0:T(8,128)S(1)}, u32[]{:S(2)}, u32[]{:S(2)}) collective-permute-start(f32[72,128]{1,0:T(8,128)S(1)} %scatter.30), channel_id=1, source_target_pairs={{0,1},{1,0},{2,3},{3,2},{4,5},{5,4},{6,7},{7,6},{8,9},{9,8},{10,11... | collective-permute-start | bytes 110600 | tf_op jit(solution)/shard_map/ppermute | solution.py:392
  17.3 5.8 %collective-permute-start.38 = (f32[56,128]{1,0:T(8,128)S(1)}, f32[56,128]{1,0:T(8,128)S(1)}, u32[]{:S(2)}, u32[]{:S(2)}) collective-permute-start(f32[56,128]{1,0:T(8,128)S(1)} %scatter-add.30.refs_12_), channel_id=1, source_target_pairs={{0,24},{1,25},{2,26},{3,27},{4,28},{5,29},{6,30},{7,31},{8,16},{9,... | collective-permute-start | bytes 86024 | tf_op jit(solution)/shard_map/ppermute | solution.py:392
  21.0 4.8 %collective-permute-start.37 = (f32[56,128]{1,0:T(8,128)S(1)}, f32[56,128]{1,0:T(8,128)S(1)}, u32[]{:S(2)}, u32[]{:S(2)}) collective-permute-start(f32[56,128]{1,0:T(8,128)S(1)} %scatter-add.30.refs_12_), channel_id=1, source_target_pairs={{0,16},{1,17},{2,18},{3,19},{4,20},{5,21},{6,22},{7,23},{8,24},{9,... | collective-permute-start | bytes 86024 | tf_op jit(solution)/shard_map/ppermute | solution.py:392
  21.0 4.8 %collective-permute-start.36 = (f32[56,128]{1,0:T(8,128)S(1)}, f32[56,128]{1,0:T(8,128)S(1)}, u32[]{:S(2)}, u32[]{:S(2)}) collective-permute-start(f32[56,128]{1,0:T(8,128)S(1)} %scatter-add.30.refs_12_), channel_id=1, source_target_pairs={{0,8},{1,9},{2,10},{3,11},{4,12},{5,13},{6,14},{7,15},{8,0},{9,1},... | collective-permute-start | bytes 86024 | tf_op jit(solution)/shard_map/ppermute | solution.py:392
  28.2 1.3 %copy-start.4 = (f32[16,128]{1,0:T(8,128)}, f32[16,128]{1,0:T(8,128)S(1)}, u32[]{:S(2)}) copy-start(f32[16,128]{1,0:T(8,128)S(1)} %get-tuple-element.389.refs_13_) | copy-start | bytes 24580
  28.2 1.2 %collective-permute-start.39 = (f32[24,128]{1,0:T(8,128)S(1)}, f32[24,128]{1,0:T(8,128)S(1)}, u32[]{:S(2)}, u32[]{:S(2)}) collective-permute-start(f32[24,128]{1,0:T(8,128)S(1)} %get-tuple-element.395), channel_id=1, source_target_pairs={{0,2},{1,3},{2,0},{3,1},{4,6},{5,7},{6,4},{7,5},{8,10},{9,11},{10,... | collective-permute-start | bytes 36872 | tf_op jit(solution)/shard_map/ppermute | solution.py:392
  28.2 1.2 %copy-start.62 = (pred[24]{0:T(512)(128)(4,1)}, pred[24]{0:T(512)(128)(4,1)S(1)}, u32[]{:S(2)}) copy-start(pred[24]{0:T(512)(128)(4,1)S(1)} %compare_select_fusion.4) | copy-start | bytes 76
  29.5 3.8 %collective-permute-start.40 = (f32[24,128]{1,0:T(8,128)S(1)}, f32[24,128]{1,0:T(8,128)S(1)}, u32[]{:S(2)}, u32[]{:S(2)}) collective-permute-start(f32[24,128]{1,0:T(8,128)S(1)} %add_select_fusion.13), channel_id=1, source_target_pairs={{0,4},{1,5},{2,6},{3,7},{4,0},{5,1},{6,2},{7,3},{8,12},{9,13},{10,... | collective-permute-start | bytes 36872 | tf_op jit(solution)/shard_map/ppermute | solution.py:392
  31.0 2.3 %copy-start.56 = (pred[24]{0:T(512)(128)(4,1)}, pred[24]{0:T(512)(128)(4,1)S(1)}, u32[]{:S(2)}) copy-start(pred[24]{0:T(512)(128)(4,1)S(1)} %compare_select_fusion.5) | copy-start | bytes 76
  31.0 4.5 %collective-permute-start.42 = (f32[3,128]{1,0:T(4,128)S(1)}, f32[3,128]{1,0:T(4,128)S(1)}, u32[]{:S(2)}, u32[]{:S(2)}) collective-permute-start(f32[3,128]{1,0:T(4,128)S(1)} %slice.411), channel_id=1, source_target_pairs={{0,5},{1,4},{2,7},{3,6},{4,1},{5,0},{6,3},{7,2},{8,13},{9,12},{10,... | collective-permute-start | bytes 4616 | tf_op jit(solution)/shard_map/ppermute | solution.py:392
  32.6 4.0 %collective-permute-start.41 = (f32[72,128]{1,0:T(8,128)S(1)}, f32[72,128]{1,0:T(8,128)S(1)}, u32[]{:S(2)}, u32[]{:S(2)}) collective-permute-start(f32[72,128]{1,0:T(8,128)S(1)} %scatter.31), channel_id=1, source_target_pairs={{0,1},{1,0},{2,3},{3,2},{4,5},{5,4},{6,7},{7,6},{8,9},{9,8},{10,11... | collective-permute-start | bytes 110600 | tf_op jit(solution)/shard_map/ppermute | solution.py:392
  36.7 5.6 %collective-permute-start.45 = (f32[24,128]{1,0:T(8,128)S(1)}, f32[24,128]{1,0:T(8,128)S(1)}, u32[]{:S(2)}, u32[]{:S(2)}) collective-permute-start(f32[24,128]{1,0:T(8,128)S(1)} %scatter-add.31.refs_19_), channel_id=1, source_target_pairs={{0,24},{1,25},{2,26},{3,27},{4,28},{5,29},{6,30},{7,31},{8,16},{9,... | collective-permute-start | bytes 36872 | tf_op jit(solution)/shard_map/ppermute | solution.py:392
  38.2 4.6 %collective-permute-start.44 = (f32[24,128]{1,0:T(8,128)S(1)}, f32[24,128]{1,0:T(8,128)S(1)}, u32[]{:S(2)}, u32[]{:S(2)}) collective-permute-start(f32[24,128]{1,0:T(8,128)S(1)} %scatter-add.31.refs_19_), channel_id=1, source_target_pairs={{0,16},{1,17},{2,18},{3,19},{4,20},{5,21},{6,22},{7,23},{8,24},{9,... | collective-permute-start | bytes 36872 | tf_op jit(solution)/shard_map/ppermute | solution.py:392
  38.9 4.1 %collective-permute-start.43 = (f32[24,128]{1,0:T(8,128)S(1)}, f32[24,128]{1,0:T(8,128)S(1)}, u32[]{:S(2)}, u32[]{:S(2)}) collective-permute-start(f32[24,128]{1,0:T(8,128)S(1)} %scatter-add.31.refs_19_), channel_id=1, source_target_pairs={{0,8},{1,9},{2,10},{3,11},{4,12},{5,13},{6,14},{7,15},{8,0},{9,1},... | collective-permute-start | bytes 36872 | tf_op jit(solution)/shard_map/ppermute | solution.py:392
  43.0 0.7 %copy-start.5 = (f32[16,128]{1,0:T(8,128)S(1)}, f32[16,128]{1,0:T(8,128)}, u32[]{:S(2)}) copy-start(f32[16,128]{1,0:T(8,128)} %copy-done.4) | copy-start | bytes 24580
  43.0 0.7 %copy-start.27 = (f32[1,128]{1,0:T(1,128)S(1)}, f32[1,128]{1,0:T(1,128)}, u32[]{:S(2)}) copy-start(f32[1,128]{1,0:T(1,128)} %copy-done.26) | copy-start | bytes 1540
  43.0 0.7 %copy-start.12 = (f32[1,128]{1,0:T(1,128)S(1)}, f32[1,128]{1,0:T(1,128)}, u32[]{:S(2)}) copy-start(f32[1,128]{1,0:T(1,128)} %copy-done.11) | copy-start | bytes 1540
  43.0 0.7 %copy-start.19 = (f32[1,256]{1,0:T(1,128)S(1)}, f32[1,256]{1,0:T(1,128)}, u32[]{:S(2)}) copy-start(f32[1,256]{1,0:T(1,128)} %copy-done.18) | copy-start | bytes 3076
  45.0 1.3 %copy-start = (f32[16,128]{1,0:T(8,128)}, f32[16,128]{1,0:T(8,128)S(1)}, u32[]{:S(2)}) copy-start(f32[16,128]{1,0:T(8,128)S(1)} %get-tuple-element.402.refs_14_) | copy-start | bytes 24580
  45.1 1.3 %copy-start.14 = (f32[1,256]{1,0:T(1,128)}, f32[1,256]{1,0:T(1,128)S(1)}, u32[]{:S(2)}) copy-start(f32[1,256]{1,0:T(1,128)S(1)} %get-tuple-element.405.refs_17_) | copy-start | bytes 3076
  45.1 1.3 %copy-start.43 = (pred[24]{0:T(512)(128)(4,1)S(1)}, pred[24]{0:T(512)(128)(4,1)}, u32[]{:S(2)}) copy-start(pred[24]{0:T(512)(128)(4,1)} %copy-done.42) | copy-start | bytes 76
  45.1 1.3 %copy-start.63 = (pred[24]{0:T(512)(128)(4,1)S(1)}, pred[24]{0:T(512)(128)(4,1)}, u32[]{:S(2)}) copy-start(pred[24]{0:T(512)(128)(4,1)} %copy-done.62) | copy-start | bytes 76
  45.1 1.2 %collective-permute-start.46 = (f32[24,128]{1,0:T(8,128)S(1)}, f32[24,128]{1,0:T(8,128)S(1)}, u32[]{:S(2)}, u32[]{:S(2)}) collective-permute-start(f32[24,128]{1,0:T(8,128)S(1)} %get-tuple-element.406), channel_id=1, source_target_pairs={{0,2},{1,3},{2,0},{3,1},{4,6},{5,7},{6,4},{7,5},{8,10},{9,11},{10,... | collective-permute-start | bytes 36872 | tf_op jit(solution)/shard_map/ppermute | solution.py:392
  46.4 4.5 %collective-permute-start.47 = (f32[24,128]{1,0:T(8,128)S(1)}, f32[24,128]{1,0:T(8,128)S(1)}, u32[]{:S(2)}, u32[]{:S(2)}) collective-permute-start(f32[24,128]{1,0:T(8,128)S(1)} %add_select_fusion.11), channel_id=1, source_target_pairs={{0,4},{1,5},{2,6},{3,7},{4,0},{5,1},{6,2},{7,3},{8,12},{9,13},{10,... | collective-permute-start | bytes 36872 | tf_op jit(solution)/shard_map/ppermute | solution.py:392
  48.7 2.2 %copy-start.57 = (pred[24]{0:T(512)(128)(4,1)S(1)}, pred[24]{0:T(512)(128)(4,1)}, u32[]{:S(2)}) copy-start(pred[24]{0:T(512)(128)(4,1)} %copy-done.56) | copy-start | bytes 76
  48.7 4.7 %collective-permute-start.49 = (f32[3,128]{1,0:T(4,128)S(1)}, f32[3,128]{1,0:T(4,128)S(1)}, u32[]{:S(2)}, u32[]{:S(2)}) collective-permute-start(f32[3,128]{1,0:T(4,128)S(1)} %slice.414), channel_id=1, source_target_pairs={{0,5},{1,4},{2,7},{3,6},{4,1},{5,0},{6,3},{7,2},{8,13},{9,12},{10,... | collective-permute-start | bytes 4616 | tf_op jit(solution)/shard_map/ppermute | solution.py:392
  49.4 4.0 %collective-permute-start.48 = (f32[72,128]{1,0:T(8,128)S(1)}, f32[72,128]{1,0:T(8,128)S(1)}, u32[]{:S(2)}, u32[]{:S(2)}) collective-permute-start(f32[72,128]{1,0:T(8,128)S(1)} %scatter.34), channel_id=1, source_target_pairs={{0,1},{1,0},{2,3},{3,2},{4,5},{5,4},{6,7},{7,6},{8,9},{9,8},{10,11... | collective-permute-start | bytes 110600 | tf_op jit(solution)/shard_map/ppermute | solution.py:392
  53.5 5.6 %collective-permute-start.52 = (f32[24,128]{1,0:T(8,128)S(1)}, f32[24,128]{1,0:T(8,128)S(1)}, u32[]{:S(2)}, u32[]{:S(2)}) collective-permute-start(f32[24,128]{1,0:T(8,128)S(1)} %scatter-add.34.refs_20_), channel_id=1, source_target_pairs={{0,24},{1,25},{2,26},{3,27},{4,28},{5,29},{6,30},{7,31},{8,16},{9,... | collective-permute-start | bytes 36872 | tf_op jit(solution)/shard_map/ppermute | solution.py:392
  56.0 4.6 %collective-permute-start.51 = (f32[24,128]{1,0:T(8,128)S(1)}, f32[24,128]{1,0:T(8,128)S(1)}, u32[]{:S(2)}, u32[]{:S(2)}) collective-permute-start(f32[24,128]{1,0:T(8,128)S(1)} %scatter-add.34.refs_20_), channel_id=1, source_target_pairs={{0,16},{1,17},{2,18},{3,19},{4,20},{5,21},{6,22},{7,23},{8,24},{9,... | collective-permute-start | bytes 36872 | tf_op jit(solution)/shard_map/ppermute | solution.py:392
  56.9 3.8 %collective-permute-start.50 = (f32[24,128]{1,0:T(8,128)S(1)}, f32[24,128]{1,0:T(8,128)S(1)}, u32[]{:S(2)}, u32[]{:S(2)}) collective-permute-start(f32[24,128]{1,0:T(8,128)S(1)} %scatter-add.34.refs_20_), channel_id=1, source_target_pairs={{0,8},{1,9},{2,10},{3,11},{4,12},{5,13},{6,14},{7,15},{8,0},{9,1},... | collective-permute-start | bytes 36872 | tf_op jit(solution)/shard_map/ppermute | solution.py:392
  60.7 0.7 %copy-start.1 = (f32[16,128]{1,0:T(8,128)S(1)}, f32[16,128]{1,0:T(8,128)}, u32[]{:S(2)}) copy-start(f32[16,128]{1,0:T(8,128)} %copy-done) | copy-start | bytes 24580
  60.7 0.7 %copy-start.23 = (f32[1,128]{1,0:T(1,128)S(1)}, f32[1,128]{1,0:T(1,128)}, u32[]{:S(2)}) copy-start(f32[1,128]{1,0:T(1,128)} %copy-done.22) | copy-start | bytes 1540
  60.7 0.7 %copy-start.13 = (f32[1,128]{1,0:T(1,128)S(1)}, f32[1,128]{1,0:T(1,128)}, u32[]{:S(2)}) copy-start(f32[1,128]{1,0:T(1,128)} %copy-done.11) | copy-start | bytes 1540
  60.7 0.7 %copy-start.15 = (f32[1,256]{1,0:T(1,128)S(1)}, f32[1,256]{1,0:T(1,128)}, u32[]{:S(2)}) copy-start(f32[1,256]{1,0:T(1,128)} %copy-done.14) | copy-start | bytes 3076
  61.5 1.5 %copy-start.32 = (f32[64,16,128]{2,1,0:T(8,128)S(1)}, f32[64,16,128]{2,1,0:T(8,128)}, u32[]{:S(2)}) copy-start(f32[64,16,128]{2,1,0:T(8,128)} %param.52) | copy-start | bytes 1572868
  61.5 1.5 %copy-start.34 = (f32[64,128]{1,0:T(8,128)S(1)}, f32[64,128]{1,0:T(8,128)}, u32[]{:S(2)}) copy-start(f32[64,128]{1,0:T(8,128)} %refs_1_.2) | copy-start | bytes 98308
  61.5 1.5 %copy-start.35 = (f32[64,128]{1,0:T(8,128)S(1)}, f32[64,128]{1,0:T(8,128)}, u32[]{:S(2)}) copy-start(f32[64,128]{1,0:T(8,128)} %refs_2_.2) | copy-start | bytes 98308
  61.5 1.5 %copy-start.37 = (f32[16,128]{1,0:T(8,128)S(1)}, f32[16,128]{1,0:T(8,128)}, u32[]{:S(2)}) copy-start(f32[16,128]{1,0:T(8,128)} %refs_3_.1) | copy-start | bytes 24580
  61.5 1.5 %copy-start.39 = (s32[1,2048]{1,0:T(1,128)S(1)}, s32[1,2048]{1,0:T(1,128)}, u32[]{:S(2)}) copy-start(s32[1,2048]{1,0:T(1,128)} %param.56) | copy-start | bytes 24580
  61.5 1.5 %copy-start.41 = (s32[2,256]{1,0:T(2,128)S(1)}, s32[2,256]{1,0:T(2,128)}, u32[]{:S(2)}) copy-start(s32[2,256]{1,0:T(2,128)} %refs_6_.1) | copy-start | bytes 6148
  61.5 1.5 %copy-start.47 = (f32[256]{0:T(256)S(1)}, f32[256]{0:T(256)}, u32[]{:S(2)}) copy-start(f32[256]{0:T(256)} %param.58) | copy-start | bytes 3076
  61.5 1.5 %copy-start.49 = (s32[256]{0:T(256)S(1)}, s32[256]{0:T(256)}, u32[]{:S(2)}) copy-start(s32[256]{0:T(256)} %param.62) | copy-start | bytes 3076
  61.5 1.5 %copy-start.51 = (f32[256]{0:T(256)S(1)}, f32[256]{0:T(256)}, u32[]{:S(2)}) copy-start(f32[256]{0:T(256)} %param.64) | copy-start | bytes 3076
  61.5 1.5 %copy-start.53 = (f32[256]{0:T(256)S(1)}, f32[256]{0:T(256)}, u32[]{:S(2)}) copy-start(f32[256]{0:T(256)} %param.63) | copy-start | bytes 3076
  61.6 1.5 %copy-start.55 = (s32[2,1,64]{2,1,0:T(1,128)S(1)}, s32[2,1,64]{2,1,0:T(1,128)}, u32[]{:S(2)}) copy-start(s32[2,1,64]{2,1,0:T(1,128)} %param.59) | copy-start | bytes 1540
  61.6 1.5 %copy-start.65 = (f32[1,64]{1,0:T(1,128)S(1)}, f32[1,64]{1,0:T(1,128)}, u32[]{:S(2)}) copy-start(f32[1,64]{1,0:T(1,128)} %refs_1_.3) | copy-start | bytes 772
  61.6 1.5 %copy-start.66 = (s32[1,2]{1,0:T(1,128)S(1)}, s32[1,2]{1,0:T(1,128)}, u32[]{:S(2)}) copy-start(s32[1,2]{1,0:T(1,128)} %refs_2_.3) | copy-start | bytes 28
  61.6 1.5 %copy-start.68 = (f32[1,128]{1,0:T(1,128)S(1)}, f32[1,128]{1,0:T(1,128)}, u32[]{:S(2)}) copy-start(f32[1,128]{1,0:T(1,128)} %refs_4_.1) | copy-start | bytes 1540
  (9 other events, 5.4 us)

commit v7 on v6

--- a/solution.py
+++ b/solution.py
@@ -43,8 +43,7 @@
     return total
 
 
-def owned_one_hots(owner_ref, tech_count, node_count):
-    owned = owner_ref[pl.ds(lax.axis_index("hours"), 1), :]
+def owned_one_hots(owned, tech_count, node_count):
     shape_t = (tech_count, owned.shape[1])
     shape_n = (node_count, owned.shape[1])
     tech = lax.broadcasted_iota(jnp.int32, shape_t, 0) == owned // node_count
@@ -68,13 +67,36 @@
 
 def write_halo(sizes, sums_ref, store_new):
     halo, span, rows = halo_at(sizes), sizes.units // LANES, sizes.rows
-    for i in range(span):
-        part = slice(i * LANES, (i + 1) * LANES)
-        sums_ref[halo + i : halo + i + 1, :] = store_new[:1, part]
-        sums_ref[halo + span + i : halo + span + i + 1, :] = store_new[rows - 1 :, part]
+    write_lanes(sums_ref, halo, store_new[:1])
+    write_lanes(sums_ref, halo + span, store_new[rows - 1 :])
     used, end = halo + 2 * span, sums_rows(sizes)
     if used < end:
         sums_ref[used:end, :] = jnp.zeros((end - used, LANES), jnp.float32)
+
+
+def write_lanes(ref, start, row):
+    for i in range(row.shape[1] // LANES):
+        ref[start + i : start + i + 1, :] = row[:, i * LANES : (i + 1) * LANES]
+
+
+def read_lanes(ref, start, length):
+    return jnp.concatenate(
+        [ref[start + i : start + i + 1, :] for i in range(length // LANES)], axis=1
+    )
+
+
+def places(sizes):
+    span = sizes.units // LANES
+    limits = sizes.techs
+    energy = limits + (sizes.lines + sizes.units) // LANES
+    return Bag(
+        limits=limits,
+        energy=energy,
+        owned=energy + span,
+        weight=sizes.techs,
+        before=sizes.techs + 1,
+        negative=sizes.techs + 1 + span,
+    )
 
 
 def slots_kernel(sizes, ends_ref, limit_ref, pairs_ref, info_ref):
@@ -103,17 +125,20 @@
     given = Bag(**dict(zip(names_in, refs[: len(names_in)])))
     gives = Bag(**dict(zip(names_out, refs[len(names_in) :])))
     rows, techs, nodes, lines = sizes.rows, sizes.techs, sizes.nodes, sizes.lines
-    gives.demand[...] = given.demand[...]
-    gives.gen_cost[...] = given.gen_cost[...]
-    gives.owner[...] = given.owner[...]
-    gives.store_energy[...] = given.store_energy[...]
+    at = places(sizes)
+    fixed = gives.available.at[techs + 1]
+    gives.available[techs] = given.demand[...]
+    fixed[:techs, :] = given.gen_cost[...]
+    write_lanes(fixed, at.energy, given.store_energy[...])
+    owned = given.owner[pl.ds(lax.axis_index("hours"), 1), :]
+    fixed[at.owned : at.owned + 1, : owned.shape[1]] = owned.astype(jnp.float32)
     line_ends, stores = given.line_ends[...], given.store_node[...]
     start = jnp.concatenate([line_ends[0:1], jnp.full_like(stores, -1)], axis=1)
     end = jnp.concatenate([line_ends[1:2], stores], axis=1)
     maps = incidence(start, end, nodes)
     limits = jnp.concatenate([given.line_limit[...], given.store_power[...]], axis=1)
     gives.maps_local[...] = maps
-    gives.limits_local[...] = limits
+    write_lanes(fixed, at.limits, limits)
     prices = given.price[...]
     flows = jnp.clip(-0.5 * dot3(prices, maps, False), -limits, limits)
     gives.flows_local[...] = flows
@@ -145,7 +170,7 @@
     gives.sums[techs : techs + SQUARES, :] = jnp.concatenate(
         [primal_row + squares, dual_row + squares, jnp.broadcast_to(negative, (1, LANES))], axis=0
     )
-    tech_hot, node_hot = owned_one_hots(given.owner, techs, nodes)
+    tech_hot, node_hot = owned_one_hots(owned, techs, nodes)
     first = sums_rows(sizes)
     gives.sums[first : first + techs, :] = weights
     gives.sums[first + techs : first + 2 * techs, :] = dot3(
@@ -160,7 +185,6 @@
     balance_ref,
     sums_in_ref,
     maps_ref,
-    limits_ref,
     flows_ref,
     region_ref,
     sums_ref,
@@ -180,10 +204,10 @@
         info[0:1].astype(jnp.int32), info[1:2].astype(jnp.int32), regions * nodes
     )
     limits = info[2:3]
-    limits_ref[...] = limits
     prices_all = jnp.concatenate([gathered[region, :rows, :] for region in range(regions)], axis=1)
     flows = jnp.clip(-0.5 * dot3(prices_all, maps_ref[...], False), -limits, limits)
-    flows_ref[...] = flows
+    flows_ref[:rows, :] = flows
+    flows_ref[rows : rows + 1, :] = limits
     maps_own = maps_ref[pl.ds(pl.multiple_of(own * nodes, nodes), nodes), :]
     balance = balance_ref[...] + dot3(2.0 * flows, maps_own, True)
     step_up = (1.0 / (techs + 8.0)) * balance
@@ -203,29 +227,26 @@
 
 
 def neighbour_rows(sizes, given, hour_index):
-    span = sizes.units // LANES
-
-    def row_of(ref, offset):
-        return jnp.concatenate([ref[offset + i : offset + i + 1, :] for i in range(span)], axis=1)
-
+    units = sizes.units
     if hasattr(given, "totals"):
-        return row_of(given.next_row, 0), row_of(given.prev_row, 0)
+        return read_lanes(given.next_row, 0, units), read_lanes(given.prev_row, 0, units)
     first = halo_at(sizes)
-    last = first + span
-    core, x_place, slab = hour_index % 2, hour_index // 2 % 2, hour_index // 4 % 2
-    next_row = jnp.where(slab == 0, row_of(given.near, first), row_of(given.far, first))
-    prev_row = jnp.where(slab == 0, row_of(given.far, last), row_of(given.near, last))
-    next_row = jnp.where(x_place == 0, row_of(given.across, first), next_row)
-    prev_row = jnp.where(x_place == 0, prev_row, row_of(given.across, last))
-    next_row = jnp.where(core == 0, row_of(given.partner, first), next_row)
-    prev_row = jnp.where(core == 0, prev_row, row_of(given.partner, last))
+    last = first + units // LANES
+    count = given.slabs.shape[0]
+    core, x_place, slab = hour_index % 2, hour_index // 2 % 2, hour_index // 4
+    next_row = read_lanes(given.slabs.at[(slab + 1) % count], first, units)
+    prev_row = read_lanes(given.slabs.at[(slab + count - 1) % count], last, units)
+    next_row = jnp.where(x_place == 0, read_lanes(given.across, first, units), next_row)
+    prev_row = jnp.where(x_place == 0, prev_row, read_lanes(given.across, last, units))
+    next_row = jnp.where(core == 0, read_lanes(given.partner, first, units), next_row)
+    prev_row = jnp.where(core == 0, prev_row, read_lanes(given.partner, last, units))
     return next_row, prev_row
 
 
 def total_of(parts):
     if hasattr(parts, "totals"):
         return parts.totals[...]
-    return (parts.slab[...] + parts.near[...]) + (parts.middle[...] + parts.far[...])
+    return jnp.sum(parts.slabs[...], axis=0)
 
 
 def sweep_kernel(sizes, iteration, names_in, names_out, *refs):
@@ -239,9 +260,12 @@
     hour_index = lax.axis_index("hours")
     gathered = given.gathered
 
+    at = places(sizes)
+    fixed = given.available.at[techs + 1]
+    small = given.dispatch.at[techs]
     sums = total_of(given)
     squares = jnp.sum(sums[techs : techs + 2], axis=1, keepdims=True)
-    old_weight = jnp.ones((1, 1), jnp.float32) if second else given.weight[...][:, :1]
+    old_weight = jnp.ones((1, 1), jnp.float32) if second else small[at.weight : at.weight + 1, :1]
     weight = jnp.sqrt(
         old_weight * jnp.sqrt((squares[1:2] + EPSILON) / (squares[0:1] + EPSILON))
     )
@@ -249,14 +273,14 @@
     if second:
         first = sums_rows(sizes)
         col_weight, cost = sums[first : first + techs], sums[first + techs : first + 2 * techs]
-        gives.col_weight[...] = col_weight
-        gives.cost[...] = cost
-        gives.negative[...] = sums[techs + 2 : techs + 3]
+        negative = sums[techs + 2 : techs + 3]
         capacity = jnp.maximum(-cost / col_weight, 0.0)
         first_bar = 2.0 * capacity
     else:
-        col_weight, cost = given.col_weight[...], given.cost[...]
-        capacity = given.capacity[...]
+        col_weight = given.cap_duals[techs, :techs, :]
+        cost = given.cap_duals[techs, techs : 2 * techs, :]
+        capacity = small[:techs, :]
+        negative = small[at.negative : at.negative + 1, :]
     capacity_new = jnp.maximum(capacity - (cost - sums[:techs]) / (weight * col_weight), 0.0)
     capacity_bar = 2.0 * capacity_new - capacity
 
@@ -266,7 +290,7 @@
     slope_local = dot3(prices, maps_local, False)
     slope_cross = dot3(prices_all, given.maps_cross[...], False)
 
-    energy = given.store_energy[...]
+    energy = read_lanes(fixed, at.energy, units)
     row_id = lax.broadcasted_iota(jnp.int32, (rows, units), 0)
     next_row, prev_row = neighbour_rows(sizes, given, hour_index)
     store_duals = given.store_duals[...]
@@ -276,7 +300,7 @@
         charge_before = jnp.zeros((1, units), jnp.float32)
     else:
         charge = given.charge[...]
-        charge_before = given.charge_before[...]
+        charge_before = read_lanes(small, at.before, units)
     charge_new = jnp.clip(charge - primal_step * (store_duals - next_duals), 0.0, energy)
     gives.charge[...] = charge_new
 
@@ -284,30 +308,32 @@
     bars = []
     local_out = None if last else gives.flows_local
     cross_out = None if last else gives.flows_cross
+    local_limits = read_lanes(fixed, at.limits, lines + units)
+    cross_limits = given.flows_cross[rows : rows + 1, :]
     for flows, out, limits, slope, low, high in (
-        (given.flows_local, local_out, given.limits_local, slope_local, 0, lines),
-        (given.flows_local, local_out, given.limits_local, slope_local, lines, lines + units),
-        (given.flows_cross, cross_out, given.limits_cross, slope_cross, 0, regions * slots),
+        (given.flows_local, local_out, local_limits, slope_local, 0, lines),
+        (given.flows_local, local_out, local_limits, slope_local, lines, lines + units),
+        (given.flows_cross, cross_out, cross_limits, slope_cross, 0, regions * slots),
     ):
         slope = slope[:, low:high]
         if low:
             slope = slope + store_duals
         bound = limits[:, low:high]
-        old = flows[:, low:high]
+        old = flows[:rows, low:high]
         new = jnp.clip(old - primal_step * slope, -bound, bound)
         bars.append(2.0 * new - old)
         if not last:
-            out[:, low:high] = new
+            out[:rows, low:high] = new
             change = row_sum((new - old) ** 2)
             if out is cross_out:
                 slot = lax.broadcasted_iota(jnp.int32, change.shape, 1)
                 change = jnp.where(slot // slots == own, change, 0.0)
             primal_row = primal_row + fold_lanes(change)
     maps_own = given.maps_cross[pl.ds(pl.multiple_of(own * nodes, nodes), nodes), :]
-    balance = dot3(jnp.concatenate(bars[:2], axis=1), maps_local, True) - given.demand[...]
+    balance = dot3(jnp.concatenate(bars[:2], axis=1), maps_local, True) - given.available[techs]
     balance = balance + dot3(bars[2], maps_own, True)
 
-    gen_cost = given.gen_cost[...]
+    gen_cost = fixed[:techs, :]
     half_weight = weight / 2.0
     primal_acc = jnp.zeros((rows, nodes), jnp.float32)
     dual_acc = jnp.zeros((rows, nodes), jnp.float32)
@@ -336,16 +362,23 @@
     step_up = weight / (techs + 8.0) * balance
     if last:
         gives.prices[...] = prices + step_up
-        tech_hot, node_hot = owned_one_hots(given.owner, techs, nodes)
+        owned = fixed[at.owned : at.owned + 1, : gives.capacity.shape[1]].astype(jnp.int32)
+        tech_hot, node_hot = owned_one_hots(owned, techs, nodes)
         chosen = dot3(capacity_new, node_hot, False)
         gives.capacity[...] = row_sum(jnp.where(tech_hot, chosen, 0.0))
+        gives.negative[...] = negative
         return
     gives.block[:rows, :] = prices + step_up
-    gives.weight[...] = jnp.broadcast_to(weight, (1, LANES))
-    gives.capacity[...] = capacity_new
+    gives.flows_cross[rows : rows + 1, :] = cross_limits
+    gives.cap_duals[techs, :techs, :] = col_weight
+    gives.cap_duals[techs, techs : 2 * techs, :] = cost
+    small_new = gives.dispatch.at[techs]
+    small_new[:techs, :] = capacity_new
+    small_new[at.weight : at.weight + 1, :] = jnp.broadcast_to(weight, (1, LANES))
+    small_new[at.negative : at.negative + 1, :] = negative
     charge_bar = 2.0 * charge_new - charge
     before_new = jnp.clip(charge_before - primal_step * (prev_row - store_duals[0:1]), 0.0, energy)
-    gives.charge_before[...] = before_new
+    write_lanes(small_new, at.before, before_new)
     before_bar = 2.0 * before_new - charge_before
     shifted_bar = jnp.where(row_id == 0, before_bar, pltpu.roll(charge_bar, 1, 0))
     store_step = weight / 3.0 * (charge_bar - shifted_bar + bars[1])
@@ -422,22 +455,44 @@
         return gathered, Bag(totals=totals, next_row=next_row, prev_row=prev_row)
 
     def merged(mine, yours, mine_first):
-        row = lax.broadcasted_iota(jnp.int32, mine.shape, 0)
-        keep = jnp.where(row < halo + span, mine_first, jnp.logical_not(mine_first))
-        edge = (row >= halo) & (row < halo + 2 * span)
-        return jnp.where(edge, jnp.where(keep, mine, yours), mine + yours)
-
-    hour = lax.axis_index("hours")
+        last = halo + span
+        edges = [
+            jnp.where(mine_first, mine[halo:last], yours[halo:last]),
+            jnp.where(mine_first, yours[last : last + span], mine[last : last + span]),
+        ]
+        total = mine + yours
+        return jnp.concatenate([total[:halo], *edges, total[last + span :]], axis=0)
+
+    hour, region = lax.axis_index("hours"), lax.axis_index("region")
     partner = swap(sums, 1, 0)
+    other = swap(block[:rows], 0, 1)
     chip = merged(sums, partner, hour % 2 == 0)
-    across = swap(chip, 2, 0)
-    other = swap(block.at[rows : rows + SQUARES].set(chip[techs:halo]), 0, 1)
-    diagonal = swap(chip[techs:halo], 2, 1)
-    slab = merged(chip, across, hour // 2 % 2 == 0)
-    slab = slab.at[techs:halo].add(other[rows : rows + SQUARES] + diagonal)
-    near, middle, far = [swap(slab, 4 * step, 0) for step in (1, 2, 3)]
-    parts = Bag(slab=slab, near=near, middle=middle, far=far, partner=partner, across=across)
-    return in_order(block, other), parts
+    square = gather_from(
+        chip,
+        [
+            [(4 * z + 2 * x + core) * regions + side for x in range(2) for side in range(regions)]
+            for z in range(hours // 4)
+            for core in range(2)
+        ],
+    )
+    left = jnp.where(region == 0, square[0], square[1])
+    right = jnp.where(region == 0, square[2], square[3])
+    across = jnp.where(hour // 2 % 2 == 0, right, left)
+    slab = merged(left, right, True)
+    slab = slab.at[techs:halo].set(jnp.sum(square[:, techs:halo], axis=0))
+    slabs = gather_from(
+        slab,
+        [
+            [(4 * z + place) * regions + side for z in range(hours // 4)]
+            for place in range(4)
+            for side in range(regions)
+        ],
+    )
+    return in_order(block[:rows], other), Bag(slabs=slabs, partner=partner, across=across)
+
+
+def gather_from(value, groups):
+    return lax.all_gather(value, ("hours", "region"), axis_index_groups=groups)
 
 
 def shape(*dims, dtype=jnp.float32):
@@ -450,11 +505,11 @@
     first = sums_rows(sizes)
     col_weight, cost = totals[first : first + techs], totals[first + techs :]
     capacity = jnp.maximum(-cost / col_weight, 0.0)
-    taken = state.dispatch
-    rows_of = 2.0 * taken - state.available * (2.0 * capacity)[:, None, :]
+    taken = state.dispatch[:techs]
+    rows_of = 2.0 * taken - state.available[:techs] * (2.0 * capacity)[:, None, :]
     duals = jnp.maximum(0.5 * rows_of, 0.0)
     own = jnp.where(lax.axis_index("hours") == 0, jnp.sum(capacity**2, axis=0), 0.0)
-    fixed = sums.at[:techs].set(jnp.sum(state.available * duals, axis=1))
+    fixed = sums.at[:techs].set(jnp.sum(state.available[:techs] * duals, axis=1))
     fixed = fixed.at[techs].add(own)
     fixed = fixed.at[techs + 1].add(jnp.sum(duals**2 - taken**2, axis=(0, 1)))
     block = block.at[rows : rows + SQUARES].set(fixed[techs : techs + SQUARES])
@@ -495,16 +550,11 @@
             store_energy=args.store_energy[None],
         ),
         Bag(
-            demand=shape(rows, nodes),
-            gen_cost=shape(techs, nodes),
-            owner=shape(hours, owned, dtype=jnp.int32),
-            store_energy=shape(1, units),
-            available=shape(techs, rows, nodes),
+            available=shape(techs + 2, rows, nodes),
             maps_local=shape(nodes, lines + units, dtype=jnp.bfloat16),
-            limits_local=shape(1, lines + units),
             flows_local=shape(rows, lines + units),
             store_duals=shape(rows, units),
-            dispatch=shape(techs, rows, nodes),
+            dispatch=shape(techs + 1, rows, nodes),
             balance=shape(rows, nodes),
             sums=shape(sums_rows(sizes) + 2 * techs, nodes),
         ),
@@ -515,57 +565,46 @@
         Bag(gathered=gathered, info=info, balance=state.balance, sums=state.sums),
         Bag(
             maps=shape(regions * nodes, cross, dtype=jnp.bfloat16),
-            limits=shape(1, cross),
-            flows=shape(rows, cross),
+            flows=shape(rows + 8, cross),
             block=shape(rows + 8, nodes),
             sums=shape(*state.sums.shape),
         ),
     )
     del state.sums, state.balance
-    state.maps_cross, state.limits_cross = closed.maps, closed.limits
-    state.flows_cross = closed.flows
+    state.maps_cross, state.flows_cross = closed.maps, closed.flows
     gathered, parts = exchange(sizes, closed.block, closed.sums)
     if exact:
         parts = corrected(sizes, state, closed.block, closed.sums, parts)
 
-    negative = None
     for iteration in range(1, ITERS):
         given = Bag(**vars(state), **vars(parts), gathered=gathered)
         if iteration < ITERS - 1:
-            del given.owner
             outs = Bag(
-                dispatch=shape(techs, rows, nodes),
-                cap_duals=shape(techs, rows, nodes),
+                dispatch=shape(techs + 1, rows, nodes),
+                cap_duals=shape(techs + 1, rows, nodes),
                 flows_local=shape(rows, lines + units),
-                flows_cross=shape(rows, cross),
+                flows_cross=shape(rows + 8, cross),
                 store_duals=shape(rows, units),
-                capacity=shape(techs, nodes),
-                weight=shape(1, LANES),
                 charge=shape(rows, units),
-                charge_before=shape(1, units),
                 block=shape(rows + 8, nodes),
                 sums=shape(sums_rows(sizes), nodes),
             )
-            if iteration == 1:
-                outs.col_weight, outs.cost = shape(techs, nodes), shape(techs, nodes)
-                outs.negative = shape(1, LANES)
         else:
             outs = Bag(
                 dispatch=shape(rows * techs, nodes),
                 capacity=shape(1, owned),
                 prices=shape(rows, nodes),
                 charge=shape(rows, units),
+                negative=shape(1, LANES),
             )
         results = call(functools.partial(sweep_kernel, sizes, iteration), given, outs)
-        if iteration == 1:
-            negative = results.negative[0, 0]
-            del results.negative
         if iteration < ITERS - 1:
             gathered, parts = exchange(sizes, results.block, results.sums)
             del results.block, results.sums
             vars(state).update(vars(results))
     dispatch = results.dispatch.reshape(rows, techs, nodes)
-    return (dispatch, results.capacity, results.prices, results.charge), negative
+    outputs = (dispatch, results.capacity, results.prices, results.charge)
+    return outputs, results.negative[0, 0]
 
 
 def body(

time: 64.3 us -> 85.7 us (1.33)
  blocking collectives: 0 us -> 64 us
  starting transfers between devices: 27.6 us -> 5.75 us
  waiting for transfers between devices: 21.7 us -> 1.97 us
  local copies, waits for them, and re-layouts: 6.82 us -> 5.76 us
    all_gather x0 -> x6, blocking collectives: none -> 64 us  [gather_from(): return lax.all_gather(value, ('hours', 'region'), axis_index_groups=groups)]
    ppermute x23 -> x8, starting transfers between devices: 27.6 us -> 5.75 us  [swap(): return lax.ppermute(value, ('hours', 'region'), pairs)]
    ppermute x23 -> x8, waiting for transfers between devices: 21.7 us -> 1.97 us  [swap(): return lax.ppermute(value, ('hours', 'region'), pairs)]
    unnamed x103 -> x66, local copies, waits for them, and re-layouts: 6.43 us -> 5.3 us
  transfers between devices with their start and end apart: 23 -> 8, of which waited for: 18 -> 2; matrix products, arithmetic and copies ran while one was open for 1% -> 1% of each run, Pallas kernels for 3% -> 2%
where the time goes in v7:
time: 85.7 us; the launch traced here: 85.2 us
  blocking collectives  64 us (75%)
  local copies, waits for them, and re-layouts  5.76 us (7%)
  starting transfers between devices  5.75 us (7%)
  Pallas kernels  5.68 us (7%)
  waiting for transfers between devices  1.97 us (2%)
  between operations  1.26 us (1%)
    all_gather x6, blocking collectives, gather_from(): return lax.all_gather(value, ('hours', 'region'), axis_index_groups=groups)  64 us
    ppermute x8, starting transfers between devices, swap(): return lax.ppermute(value, ('hours', 'region'), pairs)  5.75 us
    pallas_call x6, Pallas kernels, call(): pl.pallas_call(functools.partial(kernel, names_in, names_out), out_shape=...  5.68 us
    unnamed x66, local copies, waits for them, and re-layouts  5.3 us
    ppermute x8, waiting for transfers between devices, swap(): return lax.ppermute(value, ('hours', 'region'), pairs)  1.97 us
  transfers between devices with their start and end apart: 8, of which 2 were waited for; matrix products, arithmetic and copies ran while one was open for 1% of the time, Pallas kernels for 2%

profile of v7, /device:TPU:0, one launch (start us, length us, event | category | flops | bytes accessed | tf_op | source)
XLA Modules:
  0.0 85.2 jit_solution(5479326085794487567)
XLA Ops:
  0.6 0.0 copy-start.30
  0.6 0.0 copy-start.28
  0.7 0.6 copy-done.30
  1.3 0.0 copy-done.28
  1.3 0.8 shard_map.166
  2.1 3.0 %collective-permute-start.10 = (f32[8,128]{1,0:T(8,128)S(1)}, f32[8,128]{1,0:T(8,128)S(1)}, u32[]{:S(2)}, u32[]{:S(2)}) collective-permute-start(f32[8,128]{1,0:T(8,128)S(1)} %shard_map.166), channel_id=1, source_target_pairs={{0,1},{1,0},{2,3},{3,2},{4,5},{5,4},{6,7},{7,6},{8,9},{9,8},{10,11... | collective-permute-start | bytes 12296 | tf_op jit(solution)/shard_map/ppermute | solution.py:425
  5.1 0.0 collective-permute-start.9
  5.1 0.0 copy-start.22
  5.2 0.0 copy-start.19
  5.2 0.0 copy-start.17
  5.2 0.0 copy-start.15
  5.2 0.0 copy-start.13
  5.2 0.0 copy-start.11
  5.3 0.5 copy-done.33
  5.8 0.0 copy-done.24
  5.8 0.0 copy-done.26
  5.8 0.0 copy-done.20
  5.9 0.0 copy-done.22
  5.9 0.0 copy-done.19
  5.9 0.0 copy-done.17
  5.9 0.0 copy-done.15
  5.9 0.1 copy-done.13
  6.0 0.0 copy-done.11
  6.0 1.7 %shard_map.165 = (f32[18,64,128]{2,1,0:T(8,128)S(1)}, bf16[128,512]{1,0:T(8,128)(2,1)S(1)}, f32[64,512]{1,0:T(8,128)S(1)}, f32[64,256]{1,0:T(8,128)S(1)}, f32[17...) custom-call(f32[1024,128]{1,0:T(8,128)} %bitcast.195, f32[64,128]{1,0:T(8,128)S(1)} %copy-done.11, ...), custom_call_target="tpu_custom_call" | custom-call | flops 1000000 | bytes 4000000 | tf_op jit(solution)/shard_map/pallas_call | solution.py:404
  7.8 1.4 %collective-permute-done.9 = f32[64,128]{1,0:T(8,128)S(1)} collective-permute-done((f32[64,128]{1,0:T(8,128)}, f32[64,128]{1,0:T(8,128)S(1)}, u32[]{:S(2)}, u32[]{:S(2)}) %collective-permute-start.9) | collective-permute-done | bytes 32800 | tf_op jit(solution)/shard_map/ppermute | solution.py:425
  9.2 0.4 shard_map.167
  9.6 0.1 collective-permute-start.11
  9.7 0.6 collective-permute-start.12
  10.3 0.5 collective-permute-done.11.refs_8_
  10.9 8.4 %all-gather.4 = f32[224,128]{1,0:T(8,128)S(1)} all-gather(f32[56,128]{1,0:T(8,128)S(1)} %pad_maximum_fusion.4), channel_id=6, replica_groups={{0,1,4,5},{2,3,6,7},{8,9,12,13},{10,11,14,15},{16,17,20,21},{18,19,22,2..., dimensions={0}, use_global_device_ids=true | all-gather | bytes 143360 | tf_op jit(solution)/shard_map/all_gather | solution.py:495
  19.5 0.1 scatter.26
  19.6 13.6 %all_gather.102.refs_7_ = f32[4,56,128]{2,1,0:T(8,128)S(1)} all-gather(f32[1,56,128]{2,1,0:T(8,128)S(1)} %scatter.26), channel_id=1, replica_groups={{0,8,16,24},{1,9,17,25},{2,10,18,26},{3,11,19,27},{4,12,20,28},{5,13,21..., dimensions={0}, use_global_device_ids=true | all-gather | bytes 143360 | tf_op jit(solution)/shard_map/all_gather | solution.py:495
  33.2 0.8 shard_map.168
  34.0 0.0 copy-start.6
  34.1 0.1 collective-permute-start.13
  34.2 0.5 copy-done.6
  34.7 0.9 %collective-permute-start.14 = (f32[64,128]{1,0:T(8,128)S(1)}, f32[64,128]{1,0:T(8,128)S(1)}, u32[]{:S(2)}, u32[]{:S(2)}) collective-permute-start(f32[64,128]{1,0:T(8,128)S(1)} %get-tuple-element.356), channel_id=1, source_target_pairs={{0,1},{1,0},{2,3},{3,2},{4,5},{5,4},{6,7},{7,6},{8,9},{9,8},{10,11... | collective-permute-start | bytes 98312 | tf_op jit(solution)/shard_map/ppermute | solution.py:425
  35.6 7.8 %all-gather.5 = f32[96,128]{1,0:T(8,128)S(1)} all-gather(f32[24,128]{1,0:T(8,128)S(1)} %pad_maximum_fusion.5), channel_id=7, replica_groups={{0,1,4,5},{2,3,6,7},{8,9,12,13},{10,11,14,15},{16,17,20,21},{18,19,22,2..., dimensions={0}, use_global_device_ids=true | all-gather | bytes 61440 | tf_op jit(solution)/shard_map/all_gather | solution.py:495
  43.5 0.6 select_bitcast_fusion.5
  44.1 0.1 scatter.29
  44.3 13.1 %all_gather.107.refs_9_ = f32[4,24,128]{2,1,0:T(8,128)S(1)} all-gather(f32[1,24,128]{2,1,0:T(8,128)S(1)} %scatter.29), channel_id=1, replica_groups={{0,8,16,24},{1,9,17,25},{2,10,18,26},{3,11,19,27},{4,12,20,28},{5,13,21..., dimensions={0}, use_global_device_ids=true | all-gather | bytes 61440 | tf_op jit(solution)/shard_map/all_gather | solution.py:495
  57.4 0.0 copy-start
  57.4 0.7 copy-done.7
  58.2 0.7 shard_map.169
  58.9 0.0 copy-start.4
  58.9 0.1 collective-permute-start.15
  59.0 0.5 copy-done.4
  59.5 0.9 %collective-permute-start.16 = (f32[64,128]{1,0:T(8,128)S(1)}, f32[64,128]{1,0:T(8,128)S(1)}, u32[]{:S(2)}, u32[]{:S(2)}) collective-permute-start(f32[64,128]{1,0:T(8,128)S(1)} %get-tuple-element.354), channel_id=1, source_target_pairs={{0,1},{1,0},{2,3},{3,2},{4,5},{5,4},{6,7},{7,6},{8,9},{9,8},{10,11... | collective-permute-start | bytes 98312 | tf_op jit(solution)/shard_map/ppermute | solution.py:425
  60.5 7.8 %all-gather.6 = f32[96,128]{1,0:T(8,128)S(1)} all-gather(f32[24,128]{1,0:T(8,128)S(1)} %pad_maximum_fusion.6), channel_id=8, replica_groups={{0,1,4,5},{2,3,6,7},{8,9,12,13},{10,11,14,15},{16,17,20,21},{18,19,22,2..., dimensions={0}, use_global_device_ids=true | all-gather | bytes 61440 | tf_op jit(solution)/shard_map/all_gather | solution.py:495
  68.4 0.1 scatter.30
  68.6 13.1 %all_gather.112.refs_9_ = f32[4,24,128]{2,1,0:T(8,128)S(1)} all-gather(f32[1,24,128]{2,1,0:T(8,128)S(1)} %scatter.30), channel_id=1, replica_groups={{0,8,16,24},{1,9,17,25},{2,10,18,26},{3,11,19,27},{4,12,20,28},{5,13,21..., dimensions={0}, use_global_device_ids=true | all-gather | bytes 61440 | tf_op jit(solution)/shard_map/all_gather | solution.py:495
  81.7 0.8 copy-done.5
  82.5 0.0 copy-start.25
  82.5 0.0 copy-start.27
  82.5 0.0 copy-start.29
  82.5 0.0 copy-start.32
  82.5 0.0 copy-start.34
  82.6 1.3 %shard_map.170 = (f32[1024,128]{1,0:T(8,128)}, f32[1,128]{1,0:T(1,128)S(1)}, f32[64,128]{1,0:T(8,128)S(1)}, f32[64,256]{1,0:T(8,128)S(1)}, f32[1,128]{1,0:T(1,128)S(1)}) custom-call(f32[18,64,128]{2,1,0:T(8,128)S(1)} %get-tuple-element.246.refs_0_, bf16[128,512]{1,0:T(8,128)(2,1)S(1)} %get-tuple-element.247.refs_1_, ...), custom_call_target="tpu_custom_call" | custom-call | tf_op jit(solution)/shard_map/pallas_call | solution.py:404
  84.0 0.5 copy-done.18
  84.5 0.0 copy-done.16
  84.5 0.0 copy-done.21
  84.6 0.5 copy-done.37
  85.1 0.1 copy-done.35
  85.2 0.0 copy-done.36
  (78 shorter events, 0.4 us)
Async XLA Ops:
  0.6 0.7 copy-start.30
  0.6 0.7 copy-start.28
  2.1 5.7 %collective-permute-start.10 = (f32[8,128]{1,0:T(8,128)S(1)}, f32[8,128]{1,0:T(8,128)S(1)}, u32[]{:S(2)}, u32[]{:S(2)}) collective-permute-start(f32[8,128]{1,0:T(8,128)S(1)} %shard_map.166), channel_id=1, source_target_pairs={{0,1},{1,0},{2,3},{3,2},{4,5},{5,4},{6,7},{7,6},{8,9},{9,8},{10,11... | collective-permute-start | bytes 12296 | tf_op jit(solution)/shard_map/ppermute | solution.py:425
  5.1 4.1 %collective-permute-start.9 = (f32[64,128]{1,0:T(8,128)}, f32[64,128]{1,0:T(8,128)S(1)}, u32[]{:S(2)}, u32[]{:S(2)}) collective-permute-start(f32[64,128]{1,0:T(8,128)} %refs_1_.2), channel_id=1, source_target_pairs={{0,1},{1,0},{2,3},{3,2},{4,5},{5,4},{6,7},{7,6},{8,9},{9,8},{10,11... | collective-permute-start | bytes 98312 | tf_op jit(solution)/shard_map/ppermute | solution.py:425
  5.1 0.7 copy-start.33
  5.1 0.7 copy-start.24
  5.1 0.7 copy-start.26
  5.1 0.7 copy-start.20
  5.1 0.7 copy-start.22
  5.2 0.7 copy-start.19
  5.2 0.8 copy-start.17
  5.2 0.8 copy-start.15
  5.2 0.8 copy-start.13
  5.2 0.8 copy-start.11
  9.6 1.3 %collective-permute-start.11 = (f32[56,128]{1,0:T(8,128)S(1)}, f32[56,128]{1,0:T(8,128)S(1)}, u32[]{:S(2)}, u32[]{:S(2)}) collective-permute-start(f32[56,128]{1,0:T(8,128)S(1)} %get-tuple-element.255), channel_id=1, source_target_pairs={{0,2},{1,3},{2,0},{3,1},{4,6},{5,7},{6,4},{7,5},{8,10},{9,11},{10,... | collective-permute-start | bytes 86024 | tf_op jit(solution)/shard_map/ppermute | solution.py:425
  9.7 23.5 %collective-permute-start.12 = (f32[64,128]{1,0:T(8,128)S(1)}, f32[64,128]{1,0:T(8,128)S(1)}, u32[]{:S(2)}, u32[]{:S(2)}) collective-permute-start(f32[64,128]{1,0:T(8,128)S(1)} %get-tuple-element.358), channel_id=1, source_target_pairs={{0,1},{1,0},{2,3},{3,2},{4,5},{5,4},{6,7},{7,6},{8,9},{9,8},{10,11... | collective-permute-start | bytes 98312 | tf_op jit(solution)/shard_map/ppermute | solution.py:425
  34.0 0.6 copy-start.6
  34.1 1.5 %collective-permute-start.13 = (f32[24,128]{1,0:T(8,128)S(1)}, f32[24,128]{1,0:T(8,128)S(1)}, u32[]{:S(2)}, u32[]{:S(2)}) collective-permute-start(f32[24,128]{1,0:T(8,128)S(1)} %get-tuple-element.263), channel_id=1, source_target_pairs={{0,2},{1,3},{2,0},{3,1},{4,6},{5,7},{6,4},{7,5},{8,10},{9,11},{10,... | collective-permute-start | bytes 36872 | tf_op jit(solution)/shard_map/ppermute | solution.py:425
  34.7 22.7 %collective-permute-start.14 = (f32[64,128]{1,0:T(8,128)S(1)}, f32[64,128]{1,0:T(8,128)S(1)}, u32[]{:S(2)}, u32[]{:S(2)}) collective-permute-start(f32[64,128]{1,0:T(8,128)S(1)} %get-tuple-element.356), channel_id=1, source_target_pairs={{0,1},{1,0},{2,3},{3,2},{4,5},{5,4},{6,7},{7,6},{8,9},{9,8},{10,11... | collective-permute-start | bytes 98312 | tf_op jit(solution)/shard_map/ppermute | solution.py:425
  57.4 0.8 copy-start.7
  57.4 0.8 copy-start
  58.9 0.6 copy-start.4
  58.9 1.6 %collective-permute-start.15 = (f32[24,128]{1,0:T(8,128)S(1)}, f32[24,128]{1,0:T(8,128)S(1)}, u32[]{:S(2)}, u32[]{:S(2)}) collective-permute-start(f32[24,128]{1,0:T(8,128)S(1)} %get-tuple-element.271), channel_id=1, source_target_pairs={{0,2},{1,3},{2,0},{3,1},{4,6},{5,7},{6,4},{7,5},{8,10},{9,11},{10,... | collective-permute-start | bytes 36872 | tf_op jit(solution)/shard_map/ppermute | solution.py:425
  59.5 22.2 %collective-permute-start.16 = (f32[64,128]{1,0:T(8,128)S(1)}, f32[64,128]{1,0:T(8,128)S(1)}, u32[]{:S(2)}, u32[]{:S(2)}) collective-permute-start(f32[64,128]{1,0:T(8,128)S(1)} %get-tuple-element.354), channel_id=1, source_target_pairs={{0,1},{1,0},{2,3},{3,2},{4,5},{5,4},{6,7},{7,6},{8,9},{9,8},{10,11... | collective-permute-start | bytes 98312 | tf_op jit(solution)/shard_map/ppermute | solution.py:425
  81.7 0.8 copy-start.5
  82.5 1.4 %copy-start.10 = (f32[64,16,128]{2,1,0:T(8,128)S(1)}, f32[64,16,128]{2,1,0:T(8,128)}, u32[]{:S(2)}) copy-start(f32[64,16,128]{2,1,0:T(8,128)} %param.36) | copy-start | bytes 1572868
  82.5 1.4 %copy-start.12 = (f32[64,128]{1,0:T(8,128)S(1)}, f32[64,128]{1,0:T(8,128)}, u32[]{:S(2)}) copy-start(f32[64,128]{1,0:T(8,128)} %refs_1_.2) | copy-start | bytes 98308
  82.5 1.4 %copy-start.14 = (f32[64,128]{1,0:T(8,128)S(1)}, f32[64,128]{1,0:T(8,128)}, u32[]{:S(2)}) copy-start(f32[64,128]{1,0:T(8,128)} %refs_2_.2) | copy-start | bytes 98308
  82.5 1.4 %copy-start.23 = (s32[256]{0:T(256)S(1)}, s32[256]{0:T(256)}, u32[]{:S(2)}) copy-start(s32[256]{0:T(256)} %param.46) | copy-start | bytes 3076
  82.5 1.4 %copy-start.25 = (f32[256]{0:T(256)S(1)}, f32[256]{0:T(256)}, u32[]{:S(2)}) copy-start(f32[256]{0:T(256)} %param.48) | copy-start | bytes 3076
  82.5 1.4 %copy-start.27 = (f32[256]{0:T(256)S(1)}, f32[256]{0:T(256)}, u32[]{:S(2)}) copy-start(f32[256]{0:T(256)} %param.47) | copy-start | bytes 3076
  82.5 1.4 %copy-start.29 = (s32[2,1,64]{2,1,0:T(1,128)S(1)}, s32[2,1,64]{2,1,0:T(1,128)}, u32[]{:S(2)}) copy-start(s32[2,1,64]{2,1,0:T(1,128)} %param.43) | copy-start | bytes 1540
  82.5 1.4 %copy-start.31 = (f32[1,64]{1,0:T(1,128)S(1)}, f32[1,64]{1,0:T(1,128)}, u32[]{:S(2)}) copy-start(f32[1,64]{1,0:T(1,128)} %refs_1_.3) | copy-start | bytes 772
  82.5 1.4 %copy-start.32 = (s32[1,2]{1,0:T(1,128)S(1)}, s32[1,2]{1,0:T(1,128)}, u32[]{:S(2)}) copy-start(s32[1,2]{1,0:T(1,128)} %refs_2_.3) | copy-start | bytes 28
  82.5 1.4 %copy-start.34 = (f32[1,128]{1,0:T(1,128)S(1)}, f32[1,128]{1,0:T(1,128)}, u32[]{:S(2)}) copy-start(f32[1,128]{1,0:T(1,128)} %refs_4_.1) | copy-start | bytes 1540
  83.8 0.7 copy-start.18
  83.8 0.7 copy-start.16
  83.9 0.7 copy-start.21
  84.6 0.5 copy-start.37
  84.6 0.6 copy-start.35
  84.6 0.6 copy-start.36

commit v8 on v7

--- a/solution.py
+++ b/solution.py
@@ -226,29 +226,6 @@
     )
 
 
-def neighbour_rows(sizes, given, hour_index):
-    units = sizes.units
-    if hasattr(given, "totals"):
-        return read_lanes(given.next_row, 0, units), read_lanes(given.prev_row, 0, units)
-    first = halo_at(sizes)
-    last = first + units // LANES
-    count = given.slabs.shape[0]
-    core, x_place, slab = hour_index % 2, hour_index // 2 % 2, hour_index // 4
-    next_row = read_lanes(given.slabs.at[(slab + 1) % count], first, units)
-    prev_row = read_lanes(given.slabs.at[(slab + count - 1) % count], last, units)
-    next_row = jnp.where(x_place == 0, read_lanes(given.across, first, units), next_row)
-    prev_row = jnp.where(x_place == 0, prev_row, read_lanes(given.across, last, units))
-    next_row = jnp.where(core == 0, read_lanes(given.partner, first, units), next_row)
-    prev_row = jnp.where(core == 0, prev_row, read_lanes(given.partner, last, units))
-    return next_row, prev_row
-
-
-def total_of(parts):
-    if hasattr(parts, "totals"):
-        return parts.totals[...]
-    return jnp.sum(parts.slabs[...], axis=0)
-
-
 def sweep_kernel(sizes, iteration, names_in, names_out, *refs):
     rows, techs, nodes = sizes.rows, sizes.techs, sizes.nodes
     slots, regions, lines, units = sizes.slots, sizes.regions, sizes.lines, sizes.units
@@ -263,8 +240,8 @@
     at = places(sizes)
     fixed = given.available.at[techs + 1]
     small = given.dispatch.at[techs]
-    sums = total_of(given)
-    squares = jnp.sum(sums[techs : techs + 2], axis=1, keepdims=True)
+    sums = given.totals
+    squares = jnp.sum(sums[techs : techs + 2, :], axis=1, keepdims=True)
     old_weight = jnp.ones((1, 1), jnp.float32) if second else small[at.weight : at.weight + 1, :1]
     weight = jnp.sqrt(
         old_weight * jnp.sqrt((squares[1:2] + EPSILON) / (squares[0:1] + EPSILON))
@@ -272,8 +249,8 @@
     primal_step = 0.5 / weight
     if second:
         first = sums_rows(sizes)
-        col_weight, cost = sums[first : first + techs], sums[first + techs : first + 2 * techs]
-        negative = sums[techs + 2 : techs + 3]
+        col_weight, cost = sums[first : first + techs, :], sums[first + techs :, :]
+        negative = sums[techs + 2 : techs + 3, :]
         capacity = jnp.maximum(-cost / col_weight, 0.0)
         first_bar = 2.0 * capacity
     else:
@@ -281,7 +258,7 @@
         cost = given.cap_duals[techs, techs : 2 * techs, :]
         capacity = small[:techs, :]
         negative = small[at.negative : at.negative + 1, :]
-    capacity_new = jnp.maximum(capacity - (cost - sums[:techs]) / (weight * col_weight), 0.0)
+    capacity_new = jnp.maximum(capacity - (cost - sums[:techs, :]) / (weight * col_weight), 0.0)
     capacity_bar = 2.0 * capacity_new - capacity
 
     prices_all = jnp.concatenate([gathered[region, :rows, :] for region in range(regions)], axis=1)
@@ -292,7 +269,9 @@
 
     energy = read_lanes(fixed, at.energy, units)
     row_id = lax.broadcasted_iota(jnp.int32, (rows, units), 0)
-    next_row, prev_row = neighbour_rows(sizes, given, hour_index)
+    halo = halo_at(sizes)
+    next_row = read_lanes(sums, halo, units)
+    prev_row = read_lanes(sums, halo + units // LANES, units)
     store_duals = given.store_duals[...]
     next_duals = jnp.where(row_id == rows - 1, next_row, pltpu.roll(store_duals, rows - 1, 0))
     if second:
@@ -415,14 +394,27 @@
     return Bag(**dict(zip(names_out, values)))
 
 
-def swap(value, hour_bit, region_bit):
+def permute(value, target, takes_part=lambda hour: True):
     hours, regions = lax.axis_size("hours"), lax.axis_size("region")
-    pairs = [
-        (hour * regions + region, (hour ^ hour_bit) * regions + (region ^ region_bit))
-        for hour in range(hours)
-        for region in range(regions)
-    ]
+    pairs = []
+    for hour in range(hours):
+        for region in range(regions):
+            if takes_part(hour):
+                to_hour, to_region = target(hour, region)
+                pairs.append((hour * regions + region, to_hour * regions + to_region))
     return lax.ppermute(value, ("hours", "region"), pairs)
+
+
+def other_region(hour, region):
+    return hour, region ^ 1
+
+
+def core_of(hour):
+    return hour % 2
+
+
+def first_core(hour):
+    return hour % 2 == 0
 
 
 def shifted(value, steps):
@@ -433,7 +425,7 @@
 def both_regions(block):
     if lax.axis_size("region") != 2:
         return lax.all_gather(block, "region")
-    return in_order(block, swap(block, 0, 1))
+    return in_order(block, permute(block, other_region))
 
 
 def in_order(block, other):
@@ -446,62 +438,64 @@
     hours, regions = lax.axis_size("hours"), lax.axis_size("region")
     techs, rows, span = sizes.techs, sizes.rows, sizes.units // LANES
     halo = halo_at(sizes)
+    last, end = halo + span, halo + 2 * span
+
+    def with_edges(total, first_rows, last_rows):
+        return jnp.concatenate([total[:halo], first_rows, last_rows, total[end:]], axis=0)
+
     if regions != 2 or hours != 16:
         gathered = lax.all_gather(block, "region")
         squares = jnp.sum(gathered[:, rows : rows + SQUARES], axis=0)
         totals = lax.psum(sums.at[techs:halo].set(squares), "hours")
-        next_row = shifted(sums[halo : halo + span], -1)
-        prev_row = shifted(sums[halo + span : halo + 2 * span], 1)
-        return gathered, Bag(totals=totals, next_row=next_row, prev_row=prev_row)
-
-    def merged(mine, yours, mine_first):
-        last = halo + span
-        edges = [
-            jnp.where(mine_first, mine[halo:last], yours[halo:last]),
-            jnp.where(mine_first, yours[last : last + span], mine[last : last + span]),
-        ]
-        total = mine + yours
-        return jnp.concatenate([total[:halo], *edges, total[last + span :]], axis=0)
-
-    hour, region = lax.axis_index("hours"), lax.axis_index("region")
-    partner = swap(sums, 1, 0)
-    other = swap(block[:rows], 0, 1)
-    chip = merged(sums, partner, hour % 2 == 0)
-    square = gather_from(
-        chip,
-        [
-            [(4 * z + 2 * x + core) * regions + side for x in range(2) for side in range(regions)]
-            for z in range(hours // 4)
-            for core in range(2)
-        ],
-    )
-    left = jnp.where(region == 0, square[0], square[1])
-    right = jnp.where(region == 0, square[2], square[3])
-    across = jnp.where(hour // 2 % 2 == 0, right, left)
-    slab = merged(left, right, True)
-    slab = slab.at[techs:halo].set(jnp.sum(square[:, techs:halo], axis=0))
-    slabs = gather_from(
+        return gathered, with_edges(
+            totals, shifted(sums[halo:last], -1), shifted(sums[last:end], 1)
+        )
+
+    hour = lax.axis_index("hours")
+    prices = block[:rows]
+    lower = permute(sums, lambda h, r: (h + 1, r), first_core)
+    upper_prices = permute(prices, lambda h, r: (h - 1, r), core_of)
+    far_prices = permute(
+        jnp.concatenate([prices, upper_prices], axis=0), other_region, first_core
+    )
+    given_prices = permute(far_prices[rows:], lambda h, r: (h + 1, r), first_core)
+    other = jnp.where(core_of(hour) == 0, far_prices[:rows], given_prices)
+
+    chip = with_edges(sums + lower, lower[halo:last], sums[last:end])
+    across = permute(chip, lambda h, r: (h ^ 2, r), core_of)
+    squares = chip[techs:halo]
+    diagonal = permute(squares, lambda h, r: (h ^ 2, r ^ 1), core_of)
+    beside = permute(squares, other_region, core_of)
+    on_left = hour // 2 % 2 == 0
+    slab = chip + across
+    slab = slab.at[techs:halo].add(diagonal + beside)
+    slab = with_edges(
         slab,
-        [
-            [(4 * z + place) * regions + side for z in range(hours // 4)]
-            for place in range(4)
-            for side in range(regions)
-        ],
-    )
-    return in_order(block[:rows], other), Bag(slabs=slabs, partner=partner, across=across)
-
-
-def gather_from(value, groups):
-    return lax.all_gather(value, ("hours", "region"), axis_index_groups=groups)
+        jnp.where(on_left, chip[halo:last], across[halo:last]),
+        jnp.where(on_left, across[last:end], chip[last:end]),
+    )
+    near, middle, far = [
+        permute(slab, lambda h, r, step=step: (h ^ 4 * step, r), core_of) for step in (1, 2, 3)
+    ]
+    even = hour // 4 % 2 == 0
+    totals = (slab + near) + (middle + far)
+    next_rows = jnp.where(even, near[halo:last], far[halo:last])
+    next_rows = jnp.where(on_left, across[halo:last], next_rows)
+    prev_rows = jnp.where(even, far[last:end], near[last:end])
+    prev_rows = jnp.where(on_left, prev_rows, across[last:end])
+    mine = with_edges(totals, next_rows, lower[last:end])
+    down = permute(
+        with_edges(totals, sums[halo:last], prev_rows), lambda h, r: (h - 1, r), core_of
+    )
+    return in_order(prices, other), jnp.where(core_of(hour) == 0, down, mine)
 
 
 def shape(*dims, dtype=jnp.float32):
     return jax.ShapeDtypeStruct(dims, dtype)
 
 
-def corrected(sizes, state, block, sums, parts):
+def corrected(sizes, state, block, sums, totals):
     techs, rows = sizes.techs, sizes.rows
-    totals = total_of(parts)
     first = sums_rows(sizes)
     col_weight, cost = totals[first : first + techs], totals[first + techs :]
     capacity = jnp.maximum(-cost / col_weight, 0.0)
@@ -572,12 +566,12 @@
     )
     del state.sums, state.balance
     state.maps_cross, state.flows_cross = closed.maps, closed.flows
-    gathered, parts = exchange(sizes, closed.block, closed.sums)
+    gathered, totals = exchange(sizes, closed.block, closed.sums)
     if exact:
-        parts = corrected(sizes, state, closed.block, closed.sums, parts)
+        totals = corrected(sizes, state, closed.block, closed.sums, totals)
 
     for iteration in range(1, ITERS):
-        given = Bag(**vars(state), **vars(parts), gathered=gathered)
+        given = Bag(**vars(state), totals=totals, gathered=gathered)
         if iteration < ITERS - 1:
             outs = Bag(
                 dispatch=shape(techs + 1, rows, nodes),
@@ -599,7 +593,7 @@
             )
         results = call(functools.partial(sweep_kernel, sizes, iteration), given, outs)
         if iteration < ITERS - 1:
-            gathered, parts = exchange(sizes, results.block, results.sums)
+            gathered, totals = exchange(sizes, results.block, results.sums)
             del results.block, results.sums
             vars(state).update(vars(results))
     dispatch = results.dispatch.reshape(rows, techs, nodes)

time: 85.7 us -> 108 us (1.26); the launches traced: 85.2 us -> 106 us
  starting transfers between devices: 5.75 us -> 81.4 us
  blocking collectives: 64 us -> 0 us
  waiting for transfers between devices: 1.97 us -> 12.3 us
  local copies, waits for them, and re-layouts: 5.76 us -> 4.65 us
    ppermute x8 -> x35, starting transfers between devices: 5.75 us -> 81.4 us  [permute(): return lax.ppermute(value, ('hours', 'region'), pairs)]
    all_gather x6 -> x0, blocking collectives: 64 us -> none  [gather_from(): return lax.all_gather(value, ('hours', 'region'), axis_index_groups=groups)]
    ppermute x8 -> x35, waiting for transfers between devices: 1.97 us -> 12.3 us  [permute(): return lax.ppermute(value, ('hours', 'region'), pairs)]
    unnamed x66 -> x60, local copies, waits for them, and re-layouts: 5.3 us -> 4.16 us
  transfers between devices with their start and end apart: 8 -> 35, of which waited for: 2 -> 10; matrix products, arithmetic and copies ran while one was open for 1% -> 1% of each run, Pallas kernels for 2% -> 2%
where the time goes in v8:
time: 108 us; the launch traced here: 106 us
  starting transfers between devices  81.4 us (75%)
  waiting for transfers between devices  12.3 us (11%)
  Pallas kernels  5.82 us (5%)
  local copies, waits for them, and re-layouts  4.65 us (4%)
  between operations  1.84 us (2%)
    ppermute x35, starting transfers between devices, permute(): return lax.ppermute(value, ('hours', 'region'), pairs)  81.4 us
    ppermute x35, waiting for transfers between devices, permute(): return lax.ppermute(value, ('hours', 'region'), pairs)  12.3 us
    pallas_call x6, Pallas kernels, call(): pl.pallas_call(functools.partial(kernel, names_in, names_out), out_shape=...  5.82 us
    unnamed x60, local copies, waits for them, and re-layouts  4.16 us
  transfers between devices with their start and end apart: 35, of which 10 were waited for; matrix products, arithmetic and copies ran while one was open for 1% of the time, Pallas kernels for 2%

profile of v8, /device:TPU:0, one launch (start us, length us, event | category | flops | bytes accessed | tf_op | source)
XLA Modules:
  0.0 106.4 jit_solution(5463699242264142784)
XLA Ops:
  0.7 0.6 copy-done.27
  1.3 0.0 copy-done.25
  1.3 0.9 shard_map.166
  2.3 3.0 %collective-permute-start.44 = (f32[8,128]{1,0:T(8,128)S(1)}, f32[8,128]{1,0:T(8,128)S(1)}, u32[]{:S(2)}, u32[]{:S(2)}) collective-permute-start(f32[8,128]{1,0:T(8,128)S(1)} %shard_map.166), channel_id=1, source_target_pairs={{0,1},{1,0},{2,3},{3,2},{4,5},{5,4},{6,7},{7,6},{8,9},{9,8},{10,11... | collective-permute-start | bytes 12296 | tf_op jit(solution)/shard_map/ppermute | solution.py:405
  5.2 0.0 collective-permute-start.43
  5.3 0.6 copy-done.16
  6.0 0.0 copy-done.14
  6.0 1.8 %shard_map.165 = (f32[18,64,128]{2,1,0:T(8,128)S(1)}, bf16[128,512]{1,0:T(8,128)(2,1)S(1)}, f32[64,512]{1,0:T(8,128)S(1)}, f32[64,256]{1,0:T(8,128)S(1)}, f32[17...) custom-call(f32[1024,128]{1,0:T(8,128)} %bitcast.71, f32[64,128]{1,0:T(8,128)} %refs_1_.2, ...), custom_call_target="tpu_custom_call" | custom-call | flops 1000000 | bytes 4000000 | tf_op jit(solution)/shard_map/pallas_call | solution.py:383
  7.8 1.6 %collective-permute-done.43 = f32[64,128]{1,0:T(8,128)S(1)} collective-permute-done((f32[64,128]{1,0:T(8,128)}, f32[64,128]{1,0:T(8,128)S(1)}, u32[]{:S(2)}, u32[]{:S(2)}) %collective-permute-start.43) | collective-permute-done | bytes 32800 | tf_op jit(solution)/shard_map/ppermute | solution.py:405
  9.4 0.4 shard_map.167
  9.8 1.3 %collective-permute-start.45 = (f32[56,128]{1,0:T(8,128)S(1)}, f32[56,128]{1,0:T(8,128)S(1)}, u32[]{:S(2)}, u32[]{:S(2)}) collective-permute-start(f32[56,128]{1,0:T(8,128)S(1)} %get-tuple-element.255), channel_id=1, source_target_pairs={{0,2},{1,3},{4,6},{5,7},{8,10},{9,11},{12,14},{13,15},{16,18},{17,... | collective-permute-start | bytes 86024 | tf_op jit(solution)/shard_map/ppermute | solution.py:405
  11.1 0.8 collective-permute-done.45
  11.9 0.7 collective-permute-start.46
  12.6 1.3 %collective-permute-start.53 = (f32[64,128]{1,0:T(8,128)S(1)}, f32[64,128]{1,0:T(8,128)S(1)}, u32[]{:S(2)}, u32[]{:S(2)}) collective-permute-start(f32[64,128]{1,0:T(8,128)S(1)} %get-tuple-element.341), channel_id=1, source_target_pairs={{2,0},{3,1},{6,4},{7,5},{10,8},{11,9},{14,12},{15,13},{18,16},{19,... | collective-permute-start | bytes 98312 | tf_op jit(solution)/shard_map/ppermute | solution.py:405
  13.9 0.7 collective-permute-start.48
  14.6 0.7 collective-permute-start.47
  15.3 0.1 scatter-add.30
  15.5 0.7 collective-permute-start.50
  16.2 0.7 collective-permute-start.51
  16.9 0.7 collective-permute-start.49
  17.6 2.4 %collective-permute-start.54 = (f32[128,128]{1,0:T(8,128)S(1)}, f32[128,128]{1,0:T(8,128)S(1)}, u32[]{:S(2)}, u32[]{:S(2)}) collective-permute-start(f32[128,128]{1,0:T(8,128)S(1)} %pad_maximum_fusion.23), channel_id=1, source_target_pairs={{0,1},{1,0},{4,5},{5,4},{8,9},{9,8},{12,13},{13,12},{16,17},{17,16... | collective-permute-start | bytes 196616 | tf_op jit(solution)/shard_map/ppermute | solution.py:405
  20.0 1.3 %collective-permute-start.52 = (f32[56,128]{1,0:T(8,128)S(1)}, f32[56,128]{1,0:T(8,128)S(1)}, u32[]{:S(2)}, u32[]{:S(2)}) collective-permute-start(f32[56,128]{1,0:T(8,128)S(1)} %pad_maximum_fusion.29), channel_id=1, source_target_pairs={{2,0},{3,1},{6,4},{7,5},{10,8},{11,9},{14,12},{15,13},{18,16},{19,... | collective-permute-start | bytes 86024 | tf_op jit(solution)/shard_map/ppermute | solution.py:405
  21.4 2.4 %collective-permute-done.54 = f32[128,128]{1,0:T(8,128)S(1)} collective-permute-done((f32[128,128]{1,0:T(8,128)S(1)}, f32[128,128]{1,0:T(8,128)S(1)}, u32[]{:S(2)}, u32[]{:S(2)}) %collective-permute-start.54) | collective-permute-done | bytes 65568 | tf_op jit(solution)/shard_map/ppermute | solution.py:405
  23.7 15.7 %collective-permute-start.55 = (f32[64,128]{1,0:T(8,128)S(1)}, f32[64,128]{1,0:T(8,128)S(1)}, u32[]{:S(2)}, u32[]{:S(2)}) collective-permute-start(f32[64,128]{1,0:T(8,128)S(1)} %slice.803), channel_id=1, source_target_pairs={{0,2},{1,3},{4,6},{5,7},{8,10},{9,11},{12,14},{13,15},{16,18},{17,... | collective-permute-start | bytes 98312 | tf_op jit(solution)/shard_map/ppermute | solution.py:405
  39.4 0.8 collective-permute-done.55
  40.3 0.8 shard_map.168
  41.1 2.2 %collective-permute-start.56 = (f32[24,128]{1,0:T(8,128)S(1)}, f32[24,128]{1,0:T(8,128)S(1)}, u32[]{:S(2)}, u32[]{:S(2)}) collective-permute-start(f32[24,128]{1,0:T(8,128)S(1)} %get-tuple-element.263), channel_id=1, source_target_pairs={{0,2},{1,3},{4,6},{5,7},{8,10},{9,11},{12,14},{13,15},{16,18},{17,... | collective-permute-start | bytes 36872 | tf_op jit(solution)/shard_map/ppermute | solution.py:405
  43.3 0.8 collective-permute-done.56
  44.2 0.7 collective-permute-start.57
  44.9 1.3 %collective-permute-start.64 = (f32[64,128]{1,0:T(8,128)S(1)}, f32[64,128]{1,0:T(8,128)S(1)}, u32[]{:S(2)}, u32[]{:S(2)}) collective-permute-start(f32[64,128]{1,0:T(8,128)S(1)} %get-tuple-element.337), channel_id=1, source_target_pairs={{2,0},{3,1},{6,4},{7,5},{10,8},{11,9},{14,12},{15,13},{18,16},{19,... | collective-permute-start | bytes 98312 | tf_op jit(solution)/shard_map/ppermute | solution.py:405
  46.2 0.7 collective-permute-start.59
  46.8 0.7 collective-permute-start.58
  47.6 0.1 scatter-add.31
  47.8 0.7 collective-permute-start.62
  48.4 0.7 collective-permute-start.61
  49.1 0.7 collective-permute-start.60
  49.8 3.4 %collective-permute-start.65 = (f32[128,128]{1,0:T(8,128)S(1)}, f32[128,128]{1,0:T(8,128)S(1)}, u32[]{:S(2)}, u32[]{:S(2)}) collective-permute-start(f32[128,128]{1,0:T(8,128)S(1)} %pad_maximum_fusion.24), channel_id=1, source_target_pairs={{0,1},{1,0},{4,5},{5,4},{8,9},{9,8},{12,13},{13,12},{16,17},{17,16... | collective-permute-start | bytes 196616 | tf_op jit(solution)/shard_map/ppermute | solution.py:405
  53.3 1.3 %collective-permute-start.63 = (f32[24,128]{1,0:T(8,128)S(1)}, f32[24,128]{1,0:T(8,128)S(1)}, u32[]{:S(2)}, u32[]{:S(2)}) collective-permute-start(f32[24,128]{1,0:T(8,128)S(1)} %pad_maximum_fusion.33), channel_id=1, source_target_pairs={{2,0},{3,1},{6,4},{7,5},{10,8},{11,9},{14,12},{15,13},{18,16},{19,... | collective-permute-start | bytes 36872 | tf_op jit(solution)/shard_map/ppermute | solution.py:405
  54.6 1.3 %collective-permute-done.65 = f32[128,128]{1,0:T(8,128)S(1)} collective-permute-done((f32[128,128]{1,0:T(8,128)S(1)}, f32[128,128]{1,0:T(8,128)S(1)}, u32[]{:S(2)}, u32[]{:S(2)}) %collective-permute-start.65) | collective-permute-done | bytes 65568 | tf_op jit(solution)/shard_map/ppermute | solution.py:405
  56.0 14.3 %collective-permute-start.66 = (f32[64,128]{1,0:T(8,128)S(1)}, f32[64,128]{1,0:T(8,128)S(1)}, u32[]{:S(2)}, u32[]{:S(2)}) collective-permute-start(f32[64,128]{1,0:T(8,128)S(1)} %slice.821), channel_id=1, source_target_pairs={{0,2},{1,3},{4,6},{5,7},{8,10},{9,11},{12,14},{13,15},{16,18},{17,... | collective-permute-start | bytes 98312 | tf_op jit(solution)/shard_map/ppermute | solution.py:405
  70.3 0.8 collective-permute-done.66
  71.1 0.8 copy-done.5
  71.9 0.7 shard_map.169
  72.6 2.3 %collective-permute-start.67 = (f32[24,128]{1,0:T(8,128)S(1)}, f32[24,128]{1,0:T(8,128)S(1)}, u32[]{:S(2)}, u32[]{:S(2)}) collective-permute-start(f32[24,128]{1,0:T(8,128)S(1)} %get-tuple-element.271), channel_id=1, source_target_pairs={{0,2},{1,3},{4,6},{5,7},{8,10},{9,11},{12,14},{13,15},{16,18},{17,... | collective-permute-start | bytes 36872 | tf_op jit(solution)/shard_map/ppermute | solution.py:405
  74.9 0.8 collective-permute-done.67
  75.8 0.7 collective-permute-start.68
  76.4 1.3 %collective-permute-start.75 = (f32[64,128]{1,0:T(8,128)S(1)}, f32[64,128]{1,0:T(8,128)S(1)}, u32[]{:S(2)}, u32[]{:S(2)}) collective-permute-start(f32[64,128]{1,0:T(8,128)S(1)} %get-tuple-element.333), channel_id=1, source_target_pairs={{2,0},{3,1},{6,4},{7,5},{10,8},{11,9},{14,12},{15,13},{18,16},{19,... | collective-permute-start | bytes 98312 | tf_op jit(solution)/shard_map/ppermute | solution.py:405
  77.7 0.7 collective-permute-start.70
  78.4 0.7 collective-permute-start.69
  79.1 0.1 scatter-add.34
  79.3 0.7 collective-permute-start.73
  80.0 0.7 collective-permute-start.72
  80.7 0.7 collective-permute-start.71
  81.4 2.6 %collective-permute-start.76 = (f32[128,128]{1,0:T(8,128)S(1)}, f32[128,128]{1,0:T(8,128)S(1)}, u32[]{:S(2)}, u32[]{:S(2)}) collective-permute-start(f32[128,128]{1,0:T(8,128)S(1)} %pad_maximum_fusion.25), channel_id=1, source_target_pairs={{0,1},{1,0},{4,5},{5,4},{8,9},{9,8},{12,13},{13,12},{16,17},{17,16... | collective-permute-start | bytes 196616 | tf_op jit(solution)/shard_map/ppermute | solution.py:405
  84.1 1.3 %collective-permute-start.74 = (f32[24,128]{1,0:T(8,128)S(1)}, f32[24,128]{1,0:T(8,128)S(1)}, u32[]{:S(2)}, u32[]{:S(2)}) collective-permute-start(f32[24,128]{1,0:T(8,128)S(1)} %pad_maximum_fusion.35), channel_id=1, source_target_pairs={{2,0},{3,1},{6,4},{7,5},{10,8},{11,9},{14,12},{15,13},{18,16},{19,... | collective-permute-start | bytes 36872 | tf_op jit(solution)/shard_map/ppermute | solution.py:405
  85.4 2.1 %collective-permute-done.76 = f32[128,128]{1,0:T(8,128)S(1)} collective-permute-done((f32[128,128]{1,0:T(8,128)S(1)}, f32[128,128]{1,0:T(8,128)S(1)}, u32[]{:S(2)}, u32[]{:S(2)}) %collective-permute-start.76) | collective-permute-done | bytes 65568 | tf_op jit(solution)/shard_map/ppermute | solution.py:405
  87.5 14.6 %collective-permute-start.77 = (f32[64,128]{1,0:T(8,128)S(1)}, f32[64,128]{1,0:T(8,128)S(1)}, u32[]{:S(2)}, u32[]{:S(2)}) collective-permute-start(f32[64,128]{1,0:T(8,128)S(1)} %slice.839), channel_id=1, source_target_pairs={{0,2},{1,3},{4,6},{5,7},{8,10},{9,11},{12,14},{13,15},{16,18},{17,... | collective-permute-start | bytes 98312 | tf_op jit(solution)/shard_map/ppermute | solution.py:405
  102.1 0.8 collective-permute-done.77
  103.0 0.8 copy-done.3
  103.8 1.3 %shard_map.170 = (f32[1024,128]{1,0:T(8,128)}, f32[1,128]{1,0:T(1,128)S(1)}, f32[64,128]{1,0:T(8,128)S(1)}, f32[64,256]{1,0:T(8,128)}, f32[1,128]{1,0:T(1,128)S(1)}) custom-call(f32[18,64,128]{2,1,0:T(8,128)S(1)} %get-tuple-element.246.refs_0_, bf16[128,512]{1,0:T(8,128)(2,1)S(1)} %get-tuple-element.247.refs_1_, f32[64,512]{1,0:T(8,128)S(1)} %get-tuple-element.265.refs_2_, ...), custom_call_target="tpu_custom_call" | custom-call | tf_op jit(solution)/shard_map/pallas_call | solution.py:383
  105.2 0.5 copy-done.15
  105.8 0.0 copy-done.18
  105.8 0.5 copy-done.33
  106.3 0.1 copy-done.32
  (144 shorter events, 0.7 us)
Async XLA Ops:
  0.6 0.7 copy-start.27
  0.6 0.7 copy-start.25
  1.3 4.0 %copy-start.17 = (f32[256]{0:T(256)S(1)}, f32[256]{0:T(256)}, u32[]{:S(2)}) copy-start(f32[256]{0:T(256)} %param.42) | copy-start | bytes 3076
  1.3 4.0 %copy-start.19 = (s32[256]{0:T(256)S(1)}, s32[256]{0:T(256)}, u32[]{:S(2)}) copy-start(s32[256]{0:T(256)} %param.46) | copy-start | bytes 3076
  1.3 4.0 %copy-start.21 = (f32[256]{0:T(256)S(1)}, f32[256]{0:T(256)}, u32[]{:S(2)}) copy-start(f32[256]{0:T(256)} %param.48) | copy-start | bytes 3076
  1.3 4.0 %copy-start.23 = (f32[256]{0:T(256)S(1)}, f32[256]{0:T(256)}, u32[]{:S(2)}) copy-start(f32[256]{0:T(256)} %param.47) | copy-start | bytes 3076
  2.3 5.5 %collective-permute-start.44 = (f32[8,128]{1,0:T(8,128)S(1)}, f32[8,128]{1,0:T(8,128)S(1)}, u32[]{:S(2)}, u32[]{:S(2)}) collective-permute-start(f32[8,128]{1,0:T(8,128)S(1)} %shard_map.166), channel_id=1, source_target_pairs={{0,1},{1,0},{2,3},{3,2},{4,5},{5,4},{6,7},{7,6},{8,9},{9,8},{10,11... | collective-permute-start | bytes 12296 | tf_op jit(solution)/shard_map/ppermute | solution.py:405
  5.2 4.1 %collective-permute-start.43 = (f32[64,128]{1,0:T(8,128)}, f32[64,128]{1,0:T(8,128)S(1)}, u32[]{:S(2)}, u32[]{:S(2)}) collective-permute-start(f32[64,128]{1,0:T(8,128)} %refs_1_.2), channel_id=1, source_target_pairs={{0,1},{1,0},{2,3},{3,2},{4,5},{5,4},{6,7},{7,6},{8,9},{9,8},{10,11... | collective-permute-start | bytes 98312 | tf_op jit(solution)/shard_map/ppermute | solution.py:405
  5.3 0.7 copy-start.16
  5.3 0.7 copy-start.14
  5.3 0.7 copy-start.12
  5.3 0.7 copy-start.30
  6.0 3.4 %copy-start.9 = (f32[64,128]{1,0:T(8,128)S(1)}, f32[64,128]{1,0:T(8,128)}, u32[]{:S(2)}) copy-start(f32[64,128]{1,0:T(8,128)} %refs_1_.2) | copy-start | bytes 98308
  9.8 2.1 %collective-permute-start.45 = (f32[56,128]{1,0:T(8,128)S(1)}, f32[56,128]{1,0:T(8,128)S(1)}, u32[]{:S(2)}, u32[]{:S(2)}) collective-permute-start(f32[56,128]{1,0:T(8,128)S(1)} %get-tuple-element.255), channel_id=1, source_target_pairs={{0,2},{1,3},{4,6},{5,7},{8,10},{9,11},{12,14},{13,15},{16,18},{17,... | collective-permute-start | bytes 86024 | tf_op jit(solution)/shard_map/ppermute | solution.py:405
  11.9 3.3 %collective-permute-start.46 = (f32[56,128]{1,0:T(8,128)S(1)}, f32[56,128]{1,0:T(8,128)S(1)}, u32[]{:S(2)}, u32[]{:S(2)}) collective-permute-start(f32[56,128]{1,0:T(8,128)S(1)} %pad_maximum_fusion.30), channel_id=1, source_target_pairs={{2,6},{3,7},{6,2},{7,3},{10,14},{11,15},{14,10},{15,11},{18,22},{1... | collective-permute-start | bytes 86024 | tf_op jit(solution)/shard_map/ppermute | solution.py:405
  12.6 4.9 %collective-permute-start.53 = (f32[64,128]{1,0:T(8,128)S(1)}, f32[64,128]{1,0:T(8,128)S(1)}, u32[]{:S(2)}, u32[]{:S(2)}) collective-permute-start(f32[64,128]{1,0:T(8,128)S(1)} %get-tuple-element.341), channel_id=1, source_target_pairs={{2,0},{3,1},{6,4},{7,5},{10,8},{11,9},{14,12},{15,13},{18,16},{19,... | collective-permute-start | bytes 98312 | tf_op jit(solution)/shard_map/ppermute | solution.py:405
  13.9 1.4 %collective-permute-start.48 = (f32[3,128]{1,0:T(4,128)S(1)}, f32[3,128]{1,0:T(4,128)S(1)}, u32[]{:S(2)}, u32[]{:S(2)}) collective-permute-start(f32[3,128]{1,0:T(4,128)S(1)} %slice.790), channel_id=1, source_target_pairs={{2,3},{3,2},{6,7},{7,6},{10,11},{11,10},{14,15},{15,14},{18,19},{1... | collective-permute-start | bytes 4616 | tf_op jit(solution)/shard_map/ppermute | solution.py:405
  14.6 0.7 collective-permute-start.47
  15.5 4.4 %collective-permute-start.50 = (f32[56,128]{1,0:T(8,128)S(1)}, f32[56,128]{1,0:T(8,128)S(1)}, u32[]{:S(2)}, u32[]{:S(2)}) collective-permute-start(f32[56,128]{1,0:T(8,128)S(1)} %pad_maximum_fusion.31), channel_id=1, source_target_pairs={{2,18},{3,19},{6,22},{7,23},{10,26},{11,27},{14,30},{15,31},{18,2}... | collective-permute-start | bytes 86024 | tf_op jit(solution)/shard_map/ppermute | solution.py:405
  16.2 3.7 %collective-permute-start.51 = (f32[56,128]{1,0:T(8,128)S(1)}, f32[56,128]{1,0:T(8,128)S(1)}, u32[]{:S(2)}, u32[]{:S(2)}) collective-permute-start(f32[56,128]{1,0:T(8,128)S(1)} %pad_maximum_fusion.31), channel_id=1, source_target_pairs={{2,26},{3,27},{6,30},{7,31},{10,18},{11,19},{14,22},{15,23},{18,10... | collective-permute-start | bytes 86024 | tf_op jit(solution)/shard_map/ppermute | solution.py:405
  16.9 3.1 %collective-permute-start.49 = (f32[56,128]{1,0:T(8,128)S(1)}, f32[56,128]{1,0:T(8,128)S(1)}, u32[]{:S(2)}, u32[]{:S(2)}) collective-permute-start(f32[56,128]{1,0:T(8,128)S(1)} %pad_maximum_fusion.31), channel_id=1, source_target_pairs={{2,10},{3,11},{6,14},{7,15},{10,2},{11,3},{14,6},{15,7},{18,26},{1... | collective-permute-start | bytes 86024 | tf_op jit(solution)/shard_map/ppermute | solution.py:405
  17.6 6.2 %collective-permute-start.54 = (f32[128,128]{1,0:T(8,128)S(1)}, f32[128,128]{1,0:T(8,128)S(1)}, u32[]{:S(2)}, u32[]{:S(2)}) collective-permute-start(f32[128,128]{1,0:T(8,128)S(1)} %pad_maximum_fusion.23), channel_id=1, source_target_pairs={{0,1},{1,0},{4,5},{5,4},{8,9},{9,8},{12,13},{13,12},{16,17},{17,16... | collective-permute-start | bytes 196616 | tf_op jit(solution)/shard_map/ppermute | solution.py:405
  20.0 19.4 %collective-permute-start.52 = (f32[56,128]{1,0:T(8,128)S(1)}, f32[56,128]{1,0:T(8,128)S(1)}, u32[]{:S(2)}, u32[]{:S(2)}) collective-permute-start(f32[56,128]{1,0:T(8,128)S(1)} %pad_maximum_fusion.29), channel_id=1, source_target_pairs={{2,0},{3,1},{6,4},{7,5},{10,8},{11,9},{14,12},{15,13},{18,16},{19,... | collective-permute-start | bytes 86024 | tf_op jit(solution)/shard_map/ppermute | solution.py:405
  23.7 16.5 %collective-permute-start.55 = (f32[64,128]{1,0:T(8,128)S(1)}, f32[64,128]{1,0:T(8,128)S(1)}, u32[]{:S(2)}, u32[]{:S(2)}) collective-permute-start(f32[64,128]{1,0:T(8,128)S(1)} %slice.803), channel_id=1, source_target_pairs={{0,2},{1,3},{4,6},{5,7},{8,10},{9,11},{12,14},{13,15},{16,18},{17,... | collective-permute-start | bytes 98312 | tf_op jit(solution)/shard_map/ppermute | solution.py:405
  41.1 3.1 %copy-start.4 = (f32[72,128]{1,0:T(8,128)}, f32[72,128]{1,0:T(8,128)S(1)}, u32[]{:S(2)}) copy-start(f32[72,128]{1,0:T(8,128)S(1)} %get-tuple-element.260.refs_6_) | copy-start | bytes 110596
  41.1 3.1 %collective-permute-start.56 = (f32[24,128]{1,0:T(8,128)S(1)}, f32[24,128]{1,0:T(8,128)S(1)}, u32[]{:S(2)}, u32[]{:S(2)}) collective-permute-start(f32[24,128]{1,0:T(8,128)S(1)} %get-tuple-element.263), channel_id=1, source_target_pairs={{0,2},{1,3},{4,6},{5,7},{8,10},{9,11},{12,14},{13,15},{16,18},{17,... | collective-permute-start | bytes 36872 | tf_op jit(solution)/shard_map/ppermute | solution.py:405
  44.2 3.3 %collective-permute-start.57 = (f32[24,128]{1,0:T(8,128)S(1)}, f32[24,128]{1,0:T(8,128)S(1)}, u32[]{:S(2)}, u32[]{:S(2)}) collective-permute-start(f32[24,128]{1,0:T(8,128)S(1)} %pad_maximum_fusion.36), channel_id=1, source_target_pairs={{2,6},{3,7},{6,2},{7,3},{10,14},{11,15},{14,10},{15,11},{18,22},{1... | collective-permute-start | bytes 36872 | tf_op jit(solution)/shard_map/ppermute | solution.py:405
  44.9 4.9 %collective-permute-start.64 = (f32[64,128]{1,0:T(8,128)S(1)}, f32[64,128]{1,0:T(8,128)S(1)}, u32[]{:S(2)}, u32[]{:S(2)}) collective-permute-start(f32[64,128]{1,0:T(8,128)S(1)} %get-tuple-element.337), channel_id=1, source_target_pairs={{2,0},{3,1},{6,4},{7,5},{10,8},{11,9},{14,12},{15,13},{18,16},{19,... | collective-permute-start | bytes 98312 | tf_op jit(solution)/shard_map/ppermute | solution.py:405
  46.2 1.4 %collective-permute-start.59 = (f32[3,128]{1,0:T(4,128)S(1)}, f32[3,128]{1,0:T(4,128)S(1)}, u32[]{:S(2)}, u32[]{:S(2)}) collective-permute-start(f32[3,128]{1,0:T(4,128)S(1)} %slice.808), channel_id=1, source_target_pairs={{2,3},{3,2},{6,7},{7,6},{10,11},{11,10},{14,15},{15,14},{18,19},{1... | collective-permute-start | bytes 4616 | tf_op jit(solution)/shard_map/ppermute | solution.py:405
  46.8 0.7 collective-permute-start.58
  47.8 5.5 %collective-permute-start.62 = (f32[24,128]{1,0:T(8,128)S(1)}, f32[24,128]{1,0:T(8,128)S(1)}, u32[]{:S(2)}, u32[]{:S(2)}) collective-permute-start(f32[24,128]{1,0:T(8,128)S(1)} %pad_maximum_fusion.37), channel_id=1, source_target_pairs={{2,26},{3,27},{6,30},{7,31},{10,18},{11,19},{14,22},{15,23},{18,10... | collective-permute-start | bytes 36872 | tf_op jit(solution)/shard_map/ppermute | solution.py:405
  48.4 4.8 %collective-permute-start.61 = (f32[24,128]{1,0:T(8,128)S(1)}, f32[24,128]{1,0:T(8,128)S(1)}, u32[]{:S(2)}, u32[]{:S(2)}) collective-permute-start(f32[24,128]{1,0:T(8,128)S(1)} %pad_maximum_fusion.37), channel_id=1, source_target_pairs={{2,18},{3,19},{6,22},{7,23},{10,26},{11,27},{14,30},{15,31},{18,2}... | collective-permute-start | bytes 36872 | tf_op jit(solution)/shard_map/ppermute | solution.py:405
  49.1 4.2 %collective-permute-start.60 = (f32[24,128]{1,0:T(8,128)S(1)}, f32[24,128]{1,0:T(8,128)S(1)}, u32[]{:S(2)}, u32[]{:S(2)}) collective-permute-start(f32[24,128]{1,0:T(8,128)S(1)} %pad_maximum_fusion.37), channel_id=1, source_target_pairs={{2,10},{3,11},{6,14},{7,15},{10,2},{11,3},{14,6},{15,7},{18,26},{1... | collective-permute-start | bytes 36872 | tf_op jit(solution)/shard_map/ppermute | solution.py:405
  49.8 6.2 %collective-permute-start.65 = (f32[128,128]{1,0:T(8,128)S(1)}, f32[128,128]{1,0:T(8,128)S(1)}, u32[]{:S(2)}, u32[]{:S(2)}) collective-permute-start(f32[128,128]{1,0:T(8,128)S(1)} %pad_maximum_fusion.24), channel_id=1, source_target_pairs={{0,1},{1,0},{4,5},{5,4},{8,9},{9,8},{12,13},{13,12},{16,17},{17,16... | collective-permute-start | bytes 196616 | tf_op jit(solution)/shard_map/ppermute | solution.py:405
  53.3 17.0 %collective-permute-start.63 = (f32[24,128]{1,0:T(8,128)S(1)}, f32[24,128]{1,0:T(8,128)S(1)}, u32[]{:S(2)}, u32[]{:S(2)}) collective-permute-start(f32[24,128]{1,0:T(8,128)S(1)} %pad_maximum_fusion.33), channel_id=1, source_target_pairs={{2,0},{3,1},{6,4},{7,5},{10,8},{11,9},{14,12},{15,13},{18,16},{19,... | collective-permute-start | bytes 36872 | tf_op jit(solution)/shard_map/ppermute | solution.py:405
  56.0 15.2 %collective-permute-start.66 = (f32[64,128]{1,0:T(8,128)S(1)}, f32[64,128]{1,0:T(8,128)S(1)}, u32[]{:S(2)}, u32[]{:S(2)}) collective-permute-start(f32[64,128]{1,0:T(8,128)S(1)} %slice.821), channel_id=1, source_target_pairs={{0,2},{1,3},{4,6},{5,7},{8,10},{9,11},{12,14},{13,15},{16,18},{17,... | collective-permute-start | bytes 98312 | tf_op jit(solution)/shard_map/ppermute | solution.py:405
  71.1 0.8 copy-start.5
  72.6 3.1 %copy-start.2 = (f32[72,128]{1,0:T(8,128)}, f32[72,128]{1,0:T(8,128)S(1)}, u32[]{:S(2)}) copy-start(f32[72,128]{1,0:T(8,128)S(1)} %get-tuple-element.268.refs_6_) | copy-start | bytes 110596
  72.6 3.1 %collective-permute-start.67 = (f32[24,128]{1,0:T(8,128)S(1)}, f32[24,128]{1,0:T(8,128)S(1)}, u32[]{:S(2)}, u32[]{:S(2)}) collective-permute-start(f32[24,128]{1,0:T(8,128)S(1)} %get-tuple-element.271), channel_id=1, source_target_pairs={{0,2},{1,3},{4,6},{5,7},{8,10},{9,11},{12,14},{13,15},{16,18},{17,... | collective-permute-start | bytes 36872 | tf_op jit(solution)/shard_map/ppermute | solution.py:405
  75.8 3.3 %collective-permute-start.68 = (f32[24,128]{1,0:T(8,128)S(1)}, f32[24,128]{1,0:T(8,128)S(1)}, u32[]{:S(2)}, u32[]{:S(2)}) collective-permute-start(f32[24,128]{1,0:T(8,128)S(1)} %pad_maximum_fusion.38), channel_id=1, source_target_pairs={{2,6},{3,7},{6,2},{7,3},{10,14},{11,15},{14,10},{15,11},{18,22},{1... | collective-permute-start | bytes 36872 | tf_op jit(solution)/shard_map/ppermute | solution.py:405
  76.4 4.9 %collective-permute-start.75 = (f32[64,128]{1,0:T(8,128)S(1)}, f32[64,128]{1,0:T(8,128)S(1)}, u32[]{:S(2)}, u32[]{:S(2)}) collective-permute-start(f32[64,128]{1,0:T(8,128)S(1)} %get-tuple-element.333), channel_id=1, source_target_pairs={{2,0},{3,1},{6,4},{7,5},{10,8},{11,9},{14,12},{15,13},{18,16},{19,... | collective-permute-start | bytes 98312 | tf_op jit(solution)/shard_map/ppermute | solution.py:405
  77.7 1.4 %collective-permute-start.70 = (f32[3,128]{1,0:T(4,128)S(1)}, f32[3,128]{1,0:T(4,128)S(1)}, u32[]{:S(2)}, u32[]{:S(2)}) collective-permute-start(f32[3,128]{1,0:T(4,128)S(1)} %slice.826), channel_id=1, source_target_pairs={{2,3},{3,2},{6,7},{7,6},{10,11},{11,10},{14,15},{15,14},{18,19},{1... | collective-permute-start | bytes 4616 | tf_op jit(solution)/shard_map/ppermute | solution.py:405
  78.4 0.7 collective-permute-start.69
  79.3 4.7 %collective-permute-start.73 = (f32[24,128]{1,0:T(8,128)S(1)}, f32[24,128]{1,0:T(8,128)S(1)}, u32[]{:S(2)}, u32[]{:S(2)}) collective-permute-start(f32[24,128]{1,0:T(8,128)S(1)} %pad_maximum_fusion.39), channel_id=1, source_target_pairs={{2,26},{3,27},{6,30},{7,31},{10,18},{11,19},{14,22},{15,23},{18,10... | collective-permute-start | bytes 36872 | tf_op jit(solution)/shard_map/ppermute | solution.py:405
  80.0 4.0 %collective-permute-start.72 = (f32[24,128]{1,0:T(8,128)S(1)}, f32[24,128]{1,0:T(8,128)S(1)}, u32[]{:S(2)}, u32[]{:S(2)}) collective-permute-start(f32[24,128]{1,0:T(8,128)S(1)} %pad_maximum_fusion.39), channel_id=1, source_target_pairs={{2,18},{3,19},{6,22},{7,23},{10,26},{11,27},{14,30},{15,31},{18,2}... | collective-permute-start | bytes 36872 | tf_op jit(solution)/shard_map/ppermute | solution.py:405
  80.7 3.3 %collective-permute-start.71 = (f32[24,128]{1,0:T(8,128)S(1)}, f32[24,128]{1,0:T(8,128)S(1)}, u32[]{:S(2)}, u32[]{:S(2)}) collective-permute-start(f32[24,128]{1,0:T(8,128)S(1)} %pad_maximum_fusion.39), channel_id=1, source_target_pairs={{2,10},{3,11},{6,14},{7,15},{10,2},{11,3},{14,6},{15,7},{18,26},{1... | collective-permute-start | bytes 36872 | tf_op jit(solution)/shard_map/ppermute | solution.py:405
  81.4 6.2 %collective-permute-start.76 = (f32[128,128]{1,0:T(8,128)S(1)}, f32[128,128]{1,0:T(8,128)S(1)}, u32[]{:S(2)}, u32[]{:S(2)}) collective-permute-start(f32[128,128]{1,0:T(8,128)S(1)} %pad_maximum_fusion.25), channel_id=1, source_target_pairs={{0,1},{1,0},{4,5},{5,4},{8,9},{9,8},{12,13},{13,12},{16,17},{17,16... | collective-permute-start | bytes 196616 | tf_op jit(solution)/shard_map/ppermute | solution.py:405
  84.1 18.0 %collective-permute-start.74 = (f32[24,128]{1,0:T(8,128)S(1)}, f32[24,128]{1,0:T(8,128)S(1)}, u32[]{:S(2)}, u32[]{:S(2)}) collective-permute-start(f32[24,128]{1,0:T(8,128)S(1)} %pad_maximum_fusion.35), channel_id=1, source_target_pairs={{2,0},{3,1},{6,4},{7,5},{10,8},{11,9},{14,12},{15,13},{18,16},{19,... | collective-permute-start | bytes 36872 | tf_op jit(solution)/shard_map/ppermute | solution.py:405
  87.5 15.4 %collective-permute-start.77 = (f32[64,128]{1,0:T(8,128)S(1)}, f32[64,128]{1,0:T(8,128)S(1)}, u32[]{:S(2)}, u32[]{:S(2)}) collective-permute-start(f32[64,128]{1,0:T(8,128)S(1)} %slice.839), channel_id=1, source_target_pairs={{0,2},{1,3},{4,6},{5,7},{8,10},{9,11},{12,14},{13,15},{16,18},{17,... | collective-permute-start | bytes 98312 | tf_op jit(solution)/shard_map/ppermute | solution.py:405
  103.0 0.8 copy-start.3
  103.7 1.4 %copy-start.8 = (f32[64,16,128]{2,1,0:T(8,128)S(1)}, f32[64,16,128]{2,1,0:T(8,128)}, u32[]{:S(2)}) copy-start(f32[64,16,128]{2,1,0:T(8,128)} %param.36) | copy-start | bytes 1572868
  103.7 1.4 %copy-start.10 = (f32[64,128]{1,0:T(8,128)S(1)}, f32[64,128]{1,0:T(8,128)}, u32[]{:S(2)}) copy-start(f32[64,128]{1,0:T(8,128)} %refs_1_.2) | copy-start | bytes 98308
  103.7 1.4 %copy-start.11 = (f32[64,128]{1,0:T(8,128)S(1)}, f32[64,128]{1,0:T(8,128)}, u32[]{:S(2)}) copy-start(f32[64,128]{1,0:T(8,128)} %refs_2_.2) | copy-start | bytes 98308
  103.7 1.4 %copy-start.20 = (s32[256]{0:T(256)S(1)}, s32[256]{0:T(256)}, u32[]{:S(2)}) copy-start(s32[256]{0:T(256)} %param.46) | copy-start | bytes 3076
  103.7 1.4 %copy-start.22 = (f32[256]{0:T(256)S(1)}, f32[256]{0:T(256)}, u32[]{:S(2)}) copy-start(f32[256]{0:T(256)} %param.48) | copy-start | bytes 3076
  103.7 1.4 %copy-start.24 = (f32[256]{0:T(256)S(1)}, f32[256]{0:T(256)}, u32[]{:S(2)}) copy-start(f32[256]{0:T(256)} %param.47) | copy-start | bytes 3076
  103.8 1.4 %copy-start.26 = (s32[2,1,64]{2,1,0:T(1,128)S(1)}, s32[2,1,64]{2,1,0:T(1,128)}, u32[]{:S(2)}) copy-start(s32[2,1,64]{2,1,0:T(1,128)} %param.43) | copy-start | bytes 1540
  103.8 1.4 %copy-start.28 = (f32[1,64]{1,0:T(1,128)S(1)}, f32[1,64]{1,0:T(1,128)}, u32[]{:S(2)}) copy-start(f32[1,64]{1,0:T(1,128)} %refs_1_.3) | copy-start | bytes 772
  103.8 1.4 %copy-start.29 = (s32[1,2]{1,0:T(1,128)S(1)}, s32[1,2]{1,0:T(1,128)}, u32[]{:S(2)}) copy-start(s32[1,2]{1,0:T(1,128)} %refs_2_.3) | copy-start | bytes 28
  103.8 1.4 %copy-start.31 = (f32[1,128]{1,0:T(1,128)S(1)}, f32[1,128]{1,0:T(1,128)}, u32[]{:S(2)}) copy-start(f32[1,128]{1,0:T(1,128)} %refs_4_.1) | copy-start | bytes 1540
  105.1 0.7 copy-start.15
  105.1 0.7 copy-start.13
  105.1 0.7 copy-start.18
  105.8 0.6 copy-start.32
  (1 other events, 0.5 us)

commit v9 on v8

--- a/solution.py
+++ b/solution.py
@@ -186,8 +186,7 @@
     sums_in_ref,
     maps_ref,
     flows_ref,
-    region_ref,
-    sums_ref,
+    block_ref,
 ):
     rows, techs, nodes = sizes.rows, sizes.techs, sizes.nodes
     slots, regions = sizes.slots, sizes.regions
@@ -211,18 +210,16 @@
     maps_own = maps_ref[pl.ds(pl.multiple_of(own * nodes, nodes), nodes), :]
     balance = balance_ref[...] + dot3(2.0 * flows, maps_own, True)
     step_up = (1.0 / (techs + 8.0)) * balance
-    region_ref[:rows, :] = gathered[own, :rows, :] + step_up
+    block_ref[:rows, :] = gathered[own, :rows, :] + step_up
     change = row_sum(flows * flows)
     slot = lax.broadcasted_iota(jnp.int32, change.shape, 1)
     primal = fold_lanes(jnp.where(slot // slots == own, change, 0.0))
     more = jnp.concatenate(
         [primal, row_sum(step_up * step_up), jnp.zeros((SQUARES - 2, LANES), jnp.float32)], axis=0
     )
-    sums_ref[...] = sums_in_ref[...]
-    squares = sums_in_ref[techs : techs + SQUARES, :] + more
-    sums_ref[techs : techs + SQUARES, :] = squares
-    region_ref[rows:, :] = jnp.concatenate(
-        [squares, jnp.zeros((8 - SQUARES, LANES), jnp.float32)], axis=0
+    block_ref[rows:, :] = sums_in_ref[...]
+    block_ref[rows + techs : rows + techs + SQUARES, :] = (
+        sums_in_ref[techs : techs + SQUARES, :] + more
     )
 
 
@@ -240,6 +237,7 @@
     at = places(sizes)
     fixed = given.available.at[techs + 1]
     small = given.dispatch.at[techs]
+    out_sums = None if last else gives.block.at[pl.ds(rows, sums_rows(sizes))]
     sums = given.totals
     squares = jnp.sum(sums[techs : techs + 2, :], axis=1, keepdims=True)
     old_weight = jnp.ones((1, 1), jnp.float32) if second else small[at.weight : at.weight + 1, :1]
@@ -336,7 +334,7 @@
         duals_new = jnp.maximum(duals + half_weight * cap_rows, 0.0)
         dual_acc = dual_acc + (duals_new - duals) ** 2
         gives.cap_duals[tech] = duals_new
-        gives.sums[tech : tech + 1, :] = row_sum(avail * duals_new)
+        out_sums[tech : tech + 1, :] = row_sum(avail * duals_new)
 
     step_up = weight / (techs + 8.0) * balance
     if last:
@@ -371,11 +369,8 @@
     squares = jnp.concatenate(
         [primal_row, dual_row, jnp.zeros((SQUARES - 2, LANES), jnp.float32)], axis=0
     )
-    gives.block[rows:, :] = jnp.concatenate(
-        [squares, jnp.zeros((8 - SQUARES, LANES), jnp.float32)], axis=0
-    )
-    gives.sums[techs : techs + SQUARES, :] = squares
-    write_halo(sizes, gives.sums, store_new)
+    out_sums[techs : techs + SQUARES, :] = squares
+    write_halo(sizes, out_sums, store_new)
 
 
 def call(kernel, given, outs, flops=0, smem=()):
@@ -394,27 +389,15 @@
     return Bag(**dict(zip(names_out, values)))
 
 
-def permute(value, target, takes_part=lambda hour: True):
+def swap(value, hour_bit, region_bit, core=None):
     hours, regions = lax.axis_size("hours"), lax.axis_size("region")
     pairs = []
     for hour in range(hours):
         for region in range(regions):
-            if takes_part(hour):
-                to_hour, to_region = target(hour, region)
-                pairs.append((hour * regions + region, to_hour * regions + to_region))
+            here = hour * regions + region
+            there = (hour ^ hour_bit) * regions + (region ^ region_bit)
+            pairs.append((here, there if core in (None, hour % 2) else here))
     return lax.ppermute(value, ("hours", "region"), pairs)
-
-
-def other_region(hour, region):
-    return hour, region ^ 1
-
-
-def core_of(hour):
-    return hour % 2
-
-
-def first_core(hour):
-    return hour % 2 == 0
 
 
 def shifted(value, steps):
@@ -425,7 +408,7 @@
 def both_regions(block):
     if lax.axis_size("region") != 2:
         return lax.all_gather(block, "region")
-    return in_order(block, permute(block, other_region))
+    return in_order(block, swap(block, 0, 1))
 
 
 def in_order(block, other):
@@ -434,39 +417,36 @@
     )
 
 
-def exchange(sizes, block, sums):
+def exchange(sizes, block):
     hours, regions = lax.axis_size("hours"), lax.axis_size("region")
     techs, rows, span = sizes.techs, sizes.rows, sizes.units // LANES
     halo = halo_at(sizes)
     last, end = halo + span, halo + 2 * span
+    prices, sums = block[:rows], block[rows:]
 
     def with_edges(total, first_rows, last_rows):
         return jnp.concatenate([total[:halo], first_rows, last_rows, total[end:]], axis=0)
 
     if regions != 2 or hours != 16:
-        gathered = lax.all_gather(block, "region")
-        squares = jnp.sum(gathered[:, rows : rows + SQUARES], axis=0)
+        gathered = lax.all_gather(block[: rows + halo], "region")
+        squares = jnp.sum(gathered[:, rows + techs :], axis=0)
+        gathered = gathered[:, :rows]
         totals = lax.psum(sums.at[techs:halo].set(squares), "hours")
         return gathered, with_edges(
             totals, shifted(sums[halo:last], -1), shifted(sums[last:end], 1)
         )
 
-    hour = lax.axis_index("hours")
-    prices = block[:rows]
-    lower = permute(sums, lambda h, r: (h + 1, r), first_core)
-    upper_prices = permute(prices, lambda h, r: (h - 1, r), core_of)
-    far_prices = permute(
-        jnp.concatenate([prices, upper_prices], axis=0), other_region, first_core
-    )
-    given_prices = permute(far_prices[rows:], lambda h, r: (h + 1, r), first_core)
-    other = jnp.where(core_of(hour) == 0, far_prices[:rows], given_prices)
-
+    core = lax.axis_index("hours") % 2
+    on_left = lax.axis_index("hours") // 2 % 2 == 0
+    even = lax.axis_index("hours") // 4 % 2 == 0
+    partner = swap(block, 1, 0)
+    lower = partner[rows:]
+    far_prices = swap(jnp.concatenate([prices, partner[:rows]], axis=0), 0, 1, core=0)
     chip = with_edges(sums + lower, lower[halo:last], sums[last:end])
-    across = permute(chip, lambda h, r: (h ^ 2, r), core_of)
+    across = swap(chip, 2, 0, core=1)
     squares = chip[techs:halo]
-    diagonal = permute(squares, lambda h, r: (h ^ 2, r ^ 1), core_of)
-    beside = permute(squares, other_region, core_of)
-    on_left = hour // 2 % 2 == 0
+    diagonal = swap(squares, 2, 1, core=1)
+    beside = swap(squares, 0, 1, core=1)
     slab = chip + across
     slab = slab.at[techs:halo].add(diagonal + beside)
     slab = with_edges(
@@ -474,27 +454,25 @@
         jnp.where(on_left, chip[halo:last], across[halo:last]),
         jnp.where(on_left, across[last:end], chip[last:end]),
     )
-    near, middle, far = [
-        permute(slab, lambda h, r, step=step: (h ^ 4 * step, r), core_of) for step in (1, 2, 3)
-    ]
-    even = hour // 4 % 2 == 0
+    near, middle, far = [swap(slab, 4 * step, 0, core=1) for step in (1, 2, 3)]
     totals = (slab + near) + (middle + far)
     next_rows = jnp.where(even, near[halo:last], far[halo:last])
     next_rows = jnp.where(on_left, across[halo:last], next_rows)
     prev_rows = jnp.where(even, far[last:end], near[last:end])
     prev_rows = jnp.where(on_left, prev_rows, across[last:end])
     mine = with_edges(totals, next_rows, lower[last:end])
-    down = permute(
-        with_edges(totals, sums[halo:last], prev_rows), lambda h, r: (h - 1, r), core_of
-    )
-    return in_order(prices, other), jnp.where(core_of(hour) == 0, down, mine)
+    message = with_edges(totals, sums[halo:last], prev_rows)
+    message = jnp.pad(message, ((0, rows - message.shape[0]), (0, 0)))
+    arrived = swap(jnp.where(core == 0, far_prices[rows:], message), 1, 0)
+    other = jnp.where(core == 0, far_prices[:rows], arrived)
+    return in_order(prices, other), jnp.where(core == 0, arrived[: sums.shape[0]], mine)
 
 
 def shape(*dims, dtype=jnp.float32):
     return jax.ShapeDtypeStruct(dims, dtype)
 
 
-def corrected(sizes, state, block, sums, totals):
+def corrected(sizes, state, block, totals):
     techs, rows = sizes.techs, sizes.rows
     first = sums_rows(sizes)
     col_weight, cost = totals[first : first + techs], totals[first + techs :]
@@ -503,11 +481,11 @@
     rows_of = 2.0 * taken - state.available[:techs] * (2.0 * capacity)[:, None, :]
     duals = jnp.maximum(0.5 * rows_of, 0.0)
     own = jnp.where(lax.axis_index("hours") == 0, jnp.sum(capacity**2, axis=0), 0.0)
-    fixed = sums.at[:techs].set(jnp.sum(state.available[:techs] * duals, axis=1))
-    fixed = fixed.at[techs].add(own)
-    fixed = fixed.at[techs + 1].add(jnp.sum(duals**2 - taken**2, axis=(0, 1)))
-    block = block.at[rows : rows + SQUARES].set(fixed[techs : techs + SQUARES])
-    return exchange(sizes, block, fixed)[1]
+    at = rows + techs
+    block = block.at[rows:at].set(jnp.sum(state.available[:techs] * duals, axis=1))
+    block = block.at[at].add(own)
+    block = block.at[at + 1].add(jnp.sum(duals**2 - taken**2, axis=(0, 1)))
+    return exchange(sizes, block)[1]
 
 
 def run(args, exact):
@@ -560,15 +538,14 @@
         Bag(
             maps=shape(regions * nodes, cross, dtype=jnp.bfloat16),
             flows=shape(rows + 8, cross),
-            block=shape(rows + 8, nodes),
-            sums=shape(*state.sums.shape),
+            block=shape(rows + state.sums.shape[0], nodes),
         ),
     )
     del state.sums, state.balance
     state.maps_cross, state.flows_cross = closed.maps, closed.flows
-    gathered, totals = exchange(sizes, closed.block, closed.sums)
+    gathered, totals = exchange(sizes, closed.block)
     if exact:
-        totals = corrected(sizes, state, closed.block, closed.sums, totals)
+        totals = corrected(sizes, state, closed.block, totals)
 
     for iteration in range(1, ITERS):
         given = Bag(**vars(state), totals=totals, gathered=gathered)
@@ -580,8 +557,7 @@
                 flows_cross=shape(rows + 8, cross),
                 store_duals=shape(rows, units),
                 charge=shape(rows, units),
-                block=shape(rows + 8, nodes),
-                sums=shape(sums_rows(sizes), nodes),
+                block=shape(rows + sums_rows(sizes), nodes),
             )
         else:
             outs = Bag(
@@ -593,8 +569,8 @@
             )
         results = call(functools.partial(sweep_kernel, sizes, iteration), given, outs)
         if iteration < ITERS - 1:
-            gathered, totals = exchange(sizes, results.block, results.sums)
-            del results.block, results.sums
+            gathered, totals = exchange(sizes, results.block)
+            del results.block
             vars(state).update(vars(results))
     dispatch = results.dispatch.reshape(rows, techs, nodes)
     outputs = (dispatch, results.capacity, results.prices, results.charge)

time: 108 us -> 91.2 us (0.84)
  starting transfers between devices: 81.4 us -> 59.2 us
  waiting for transfers between devices: 12.3 us -> 16.9 us
    ppermute x35 -> x29, starting transfers between devices: 81.4 us -> 59.2 us  [swap(): return lax.ppermute(value, ('hours', 'region'), pairs)]
    ppermute x35 -> x29, waiting for transfers between devices: 12.3 us -> 16.9 us  [swap(): return lax.ppermute(value, ('hours', 'region'), pairs)]
    unnamed x60 -> x66, local copies, waits for them, and re-layouts: 4.16 us -> 4.73 us
  transfers between devices with their start and end apart: 35 -> 29, of which waited for: 10 -> 10; matrix products, arithmetic and copies ran while one was open for 1% -> 0% of each run, Pallas kernels for 2% -> 2%
where the time goes in v9:
time: 91.2 us; the launch traced here: 90.1 us
  starting transfers between devices  59.2 us (65%)
  waiting for transfers between devices  16.9 us (19%)
  Pallas kernels  5.82 us (6%)
  local copies, waits for them, and re-layouts  5.23 us (6%)
  between operations  1.82 us (2%)
  other arithmetic  1.16 us (1%)
    ppermute x29, starting transfers between devices, swap(): return lax.ppermute(value, ('hours', 'region'), pairs)  59.2 us
    ppermute x29, waiting for transfers between devices, swap(): return lax.ppermute(value, ('hours', 'region'), pairs)  16.9 us
    pallas_call x6, Pallas kernels, call(): pl.pallas_call(functools.partial(kernel, names_in, names_out), out_shape=...  5.82 us
    unnamed x66, local copies, waits for them, and re-layouts  4.73 us
  transfers between devices with their start and end apart: 29, of which 10 were waited for; matrix products, arithmetic and copies ran while one was open for 0% of the time, Pallas kernels for 2%

profile of v9, /device:TPU:0, one launch (start us, length us, event | category | flops | bytes accessed | tf_op | source)
XLA Modules:
  0.0 90.1 jit_solution(6757229691495514876)
XLA Ops:
  0.6 0.0 copy-start.35
  0.7 0.6 copy-done.35
  1.3 0.0 copy-done.33
  1.3 0.9 %shard_map.166 = f32[8,128]{1,0:T(8,128)S(1)} custom-call(s32[2,64]{1,0:T(2,128)S(1)} %bitcast.109, f32[1,64]{1,0:T(1,128)S(1)} %copy-done.35, s32[1,2]{1,0:T(1,128)} %refs_2_.3), custom_call_target="tpu_custom_call" | custom-call | tf_op jit(solution)/shard_map/pallas_call | solution.py:378
  2.3 3.0 %collective-permute-start.39 = (f32[8,128]{1,0:T(8,128)S(1)}, f32[8,128]{1,0:T(8,128)S(1)}, u32[]{:S(2)}, u32[]{:S(2)}) collective-permute-start(f32[8,128]{1,0:T(8,128)S(1)} %shard_map.166), channel_id=1, source_target_pairs={{0,1},{1,0},{2,3},{3,2},{4,5},{5,4},{6,7},{7,6},{8,9},{9,8},{10,11... | collective-permute-start | bytes 12296 | tf_op jit(solution)/shard_map/ppermute | solution.py:400
  5.2 0.0 collective-permute-start.38
  5.3 0.6 copy-done.23
  6.0 0.0 copy-done.22
  6.0 0.0 copy-done.21
  6.0 1.8 %shard_map.165 = (f32[18,64,128]{2,1,0:T(8,128)S(1)}, bf16[128,512]{1,0:T(8,128)(2,1)S(1)}, f32[64,512]{1,0:T(8,128)S(1)}, f32[64,256]{1,0:T(8,128)S(1)}, f32[17...) custom-call(f32[1024,128]{1,0:T(8,128)} %bitcast.71, f32[64,128]{1,0:T(8,128)} %refs_1_.2, ...), custom_call_target="tpu_custom_call" | custom-call | flops 1000000 | bytes 4000000 | tf_op jit(solution)/shard_map/pallas_call | solution.py:378
  7.8 1.6 %collective-permute-done.38 = f32[64,128]{1,0:T(8,128)S(1)} collective-permute-done((f32[64,128]{1,0:T(8,128)}, f32[64,128]{1,0:T(8,128)S(1)}, u32[]{:S(2)}, u32[]{:S(2)}) %collective-permute-start.38) | collective-permute-done | bytes 32800 | tf_op jit(solution)/shard_map/ppermute | solution.py:400
  9.4 0.4 shard_map.167
  9.8 0.1 collective-permute-start.40
  9.9 1.2 %collective-permute-done.40 = f32[120,128]{1,0:T(8,128)S(1)} collective-permute-done((f32[120,128]{1,0:T(8,128)S(1)}, f32[120,128]{1,0:T(8,128)S(1)}, u32[]{:S(2)}, u32[]{:S(2)}) %collective-permute-start.40) | collective-permute-done | bytes 61472 | tf_op jit(solution)/shard_map/ppermute | solution.py:400
  11.1 0.7 collective-permute-start.42
  11.8 0.7 collective-permute-start.44
  12.5 0.7 collective-permute-start.43
  13.2 0.1 scatter-add.30
  13.5 0.7 collective-permute-start.46
  14.1 0.7 collective-permute-start.47
  14.8 0.7 collective-permute-start.45
  15.5 2.4 %collective-permute-start.41 = (f32[128,128]{1,0:T(8,128)S(1)}, f32[128,128]{1,0:T(8,128)S(1)}, u32[]{:S(2)}, u32[]{:S(2)}) collective-permute-start(f32[128,128]{1,0:T(8,128)S(1)} %pad_maximum_fusion.24), channel_id=1, source_target_pairs={{0,1},{1,0},{2,2},{3,3},{4,5},{5,4},{6,6},{7,7},{8,9},{9,8},{10,10... | collective-permute-start | bytes 196616 | tf_op jit(solution)/shard_map/ppermute | solution.py:400
  18.0 3.7 %collective-permute-done.41 = f32[128,128]{1,0:T(8,128)S(1)} collective-permute-done((f32[128,128]{1,0:T(8,128)S(1)}, f32[128,128]{1,0:T(8,128)S(1)}, u32[]{:S(2)}, u32[]{:S(2)}) %collective-permute-start.41) | collective-permute-done | bytes 65568 | tf_op jit(solution)/shard_map/ppermute | solution.py:400
  21.7 12.3 %collective-permute-start.48 = (f32[64,128]{1,0:T(8,128)S(1)}, f32[64,128]{1,0:T(8,128)S(1)}, u32[]{:S(2)}, u32[]{:S(2)}) collective-permute-start(f32[64,128]{1,0:T(8,128)S(1)} %slice_select_fusion.20), channel_id=1, source_target_pairs={{0,2},{1,3},{2,0},{3,1},{4,6},{5,7},{6,4},{7,5},{8,10},{9,11},{10,... | collective-permute-start | bytes 98312 | tf_op jit(solution)/shard_map/ppermute | solution.py:400
  34.0 0.9 collective-permute-done.48
  34.9 0.8 shard_map.168
  35.7 0.4 collective-permute-start.49
  36.1 0.9 collective-permute-done.49
  37.0 0.7 collective-permute-start.51
  37.7 0.7 collective-permute-start.53
  38.4 0.7 collective-permute-start.52
  39.1 0.1 scatter-add.31
  39.3 0.0 slice-start.2
  39.3 0.7 collective-permute-start.56
  40.0 0.7 collective-permute-start.55
  40.7 0.7 collective-permute-start.54
  41.4 3.4 %collective-permute-start.50 = (f32[128,128]{1,0:T(8,128)S(1)}, f32[128,128]{1,0:T(8,128)S(1)}, u32[]{:S(2)}, u32[]{:S(2)}) collective-permute-start(f32[128,128]{1,0:T(8,128)S(1)} %pad_maximum_fusion.25), channel_id=1, source_target_pairs={{0,1},{1,0},{2,2},{3,3},{4,5},{5,4},{6,6},{7,7},{8,9},{9,8},{10,10... | collective-permute-start | bytes 196616 | tf_op jit(solution)/shard_map/ppermute | solution.py:400
  44.9 2.6 %collective-permute-done.50 = f32[128,128]{1,0:T(8,128)S(1)} collective-permute-done((f32[128,128]{1,0:T(8,128)S(1)}, f32[128,128]{1,0:T(8,128)S(1)}, u32[]{:S(2)}, u32[]{:S(2)}) %collective-permute-start.50) | collective-permute-done | bytes 65568 | tf_op jit(solution)/shard_map/ppermute | solution.py:400
  47.5 11.2 %collective-permute-start.57 = (f32[64,128]{1,0:T(8,128)S(1)}, f32[64,128]{1,0:T(8,128)S(1)}, u32[]{:S(2)}, u32[]{:S(2)}) collective-permute-start(f32[64,128]{1,0:T(8,128)S(1)} %slice_select_fusion.18), channel_id=1, source_target_pairs={{0,2},{1,3},{2,0},{3,1},{4,6},{5,7},{6,4},{7,5},{8,10},{9,11},{10,... | collective-permute-start | bytes 98312 | tf_op jit(solution)/shard_map/ppermute | solution.py:400
  58.7 0.9 collective-permute-done.57
  59.6 0.0 copy-start.7
  59.6 0.7 copy-done.7
  60.4 0.7 shard_map.169
  61.1 0.6 copy-done.4
  61.7 0.3 collective-permute-start.58
  62.0 0.9 collective-permute-done.58
  63.0 0.7 collective-permute-start.60
  63.7 0.7 collective-permute-start.62
  64.3 0.7 collective-permute-start.61
  65.1 0.1 scatter-add.34
  65.2 0.8 fusion.47
  66.0 0.7 collective-permute-start.65
  66.7 0.7 collective-permute-start.64
  67.4 0.7 collective-permute-start.63
  68.0 2.6 %collective-permute-start.59 = (f32[128,128]{1,0:T(8,128)S(1)}, f32[128,128]{1,0:T(8,128)S(1)}, u32[]{:S(2)}, u32[]{:S(2)}) collective-permute-start(f32[128,128]{1,0:T(8,128)S(1)} %pad_maximum_fusion.26), channel_id=1, source_target_pairs={{0,1},{1,0},{2,2},{3,3},{4,5},{5,4},{6,6},{7,7},{8,9},{9,8},{10,10... | collective-permute-start | bytes 196616 | tf_op jit(solution)/shard_map/ppermute | solution.py:400
  70.8 3.5 %collective-permute-done.59 = f32[128,128]{1,0:T(8,128)S(1)} collective-permute-done((f32[128,128]{1,0:T(8,128)S(1)}, f32[128,128]{1,0:T(8,128)S(1)}, u32[]{:S(2)}, u32[]{:S(2)}) %collective-permute-start.59) | collective-permute-done | bytes 65568 | tf_op jit(solution)/shard_map/ppermute | solution.py:400
  74.2 11.5 %collective-permute-start.66 = (f32[64,128]{1,0:T(8,128)S(1)}, f32[64,128]{1,0:T(8,128)S(1)}, u32[]{:S(2)}, u32[]{:S(2)}) collective-permute-start(f32[64,128]{1,0:T(8,128)S(1)} %slice_select_fusion.16), channel_id=1, source_target_pairs={{0,2},{1,3},{2,0},{3,1},{4,6},{5,7},{6,4},{7,5},{8,10},{9,11},{10,... | collective-permute-start | bytes 98312 | tf_op jit(solution)/shard_map/ppermute | solution.py:400
  85.8 0.9 collective-permute-done.66
  86.7 0.7 copy-done.5
  87.5 1.3 %shard_map.170 = (f32[1024,128]{1,0:T(8,128)}, f32[1,128]{1,0:T(1,128)S(1)}, f32[64,128]{1,0:T(8,128)S(1)}, f32[64,256]{1,0:T(8,128)}, f32[1,128]{1,0:T(1,128)S(1)}) custom-call(f32[18,64,128]{2,1,0:T(8,128)S(1)} %get-tuple-element.240.refs_0_, bf16[128,512]{1,0:T(8,128)(2,1)S(1)} %get-tuple-element.241.refs_1_, f32[64,512]{1,0:T(8,128)S(1)} %get-tuple-element.257.refs_2_, ...), custom_call_target="tpu_custom_call" | custom-call | tf_op jit(solution)/shard_map/pallas_call | solution.py:378
  88.9 0.6 copy-done.24
  89.5 0.0 copy-done.26
  89.5 0.5 copy-done.41
  90.0 0.1 copy-done.40
  (147 shorter events, 0.7 us)
Async XLA Ops:
  0.6 0.7 copy-start.35
  0.6 0.7 copy-start.33
  1.3 4.0 %copy-start.25 = (f32[256]{0:T(256)S(1)}, f32[256]{0:T(256)}, u32[]{:S(2)}) copy-start(f32[256]{0:T(256)} %param.42) | copy-start | bytes 3076
  1.3 4.0 %copy-start.27 = (s32[256]{0:T(256)S(1)}, s32[256]{0:T(256)}, u32[]{:S(2)}) copy-start(s32[256]{0:T(256)} %param.46) | copy-start | bytes 3076
  1.3 4.0 %copy-start.29 = (f32[256]{0:T(256)S(1)}, f32[256]{0:T(256)}, u32[]{:S(2)}) copy-start(f32[256]{0:T(256)} %param.48) | copy-start | bytes 3076
  1.3 4.0 %copy-start.31 = (f32[256]{0:T(256)S(1)}, f32[256]{0:T(256)}, u32[]{:S(2)}) copy-start(f32[256]{0:T(256)} %param.47) | copy-start | bytes 3076
  2.3 5.5 %collective-permute-start.39 = (f32[8,128]{1,0:T(8,128)S(1)}, f32[8,128]{1,0:T(8,128)S(1)}, u32[]{:S(2)}, u32[]{:S(2)}) collective-permute-start(f32[8,128]{1,0:T(8,128)S(1)} %shard_map.166), channel_id=1, source_target_pairs={{0,1},{1,0},{2,3},{3,2},{4,5},{5,4},{6,7},{7,6},{8,9},{9,8},{10,11... | collective-permute-start | bytes 12296 | tf_op jit(solution)/shard_map/ppermute | solution.py:400
  5.2 4.1 %collective-permute-start.38 = (f32[64,128]{1,0:T(8,128)}, f32[64,128]{1,0:T(8,128)S(1)}, u32[]{:S(2)}, u32[]{:S(2)}) collective-permute-start(f32[64,128]{1,0:T(8,128)} %refs_1_.2), channel_id=1, source_target_pairs={{0,1},{1,0},{2,3},{3,2},{4,5},{5,4},{6,7},{7,6},{8,9},{9,8},{10,11... | collective-permute-start | bytes 98312 | tf_op jit(solution)/shard_map/ppermute | solution.py:400
  5.3 0.7 copy-start.23
  5.3 0.7 copy-start.22
  5.3 0.7 copy-start.21
  5.3 0.7 copy-start.38
  6.0 3.4 %copy-start.11 = (f32[64,128]{1,0:T(8,128)S(1)}, f32[64,128]{1,0:T(8,128)}, u32[]{:S(2)}) copy-start(f32[64,128]{1,0:T(8,128)} %refs_1_.2) | copy-start | bytes 98308
  9.8 1.3 %collective-permute-start.40 = (f32[120,128]{1,0:T(8,128)S(1)}, f32[120,128]{1,0:T(8,128)S(1)}, u32[]{:S(2)}, u32[]{:S(2)}) collective-permute-start(f32[120,128]{1,0:T(8,128)S(1)} %get-tuple-element.249), channel_id=1, source_target_pairs={{0,2},{1,3},{2,0},{3,1},{4,6},{5,7},{6,4},{7,5},{8,10},{9,11},{10,... | collective-permute-start | bytes 184328 | tf_op jit(solution)/shard_map/ppermute | solution.py:400
  11.1 2.3 %copy-start.18 = (f32[120,128]{1,0:T(8,128)}, f32[120,128]{1,0:T(8,128)S(1)}, u32[]{:S(2)}) copy-start(f32[120,128]{1,0:T(8,128)S(1)} %collective-permute-done.40) | copy-start | bytes 184324
  11.1 2.0 %collective-permute-start.42 = (f32[56,128]{1,0:T(8,128)S(1)}, f32[56,128]{1,0:T(8,128)S(1)}, u32[]{:S(2)}, u32[]{:S(2)}) collective-permute-start(f32[56,128]{1,0:T(8,128)S(1)} %pad_maximum_fusion.31), channel_id=1, source_target_pairs={{0,0},{1,1},{2,6},{3,7},{4,4},{5,5},{6,2},{7,3},{8,8},{9,9},{10,14... | collective-permute-start | bytes 86024 | tf_op jit(solution)/shard_map/ppermute | solution.py:400
  11.8 1.4 %collective-permute-start.44 = (f32[3,128]{1,0:T(4,128)S(1)}, f32[3,128]{1,0:T(4,128)S(1)}, u32[]{:S(2)}, u32[]{:S(2)}) collective-permute-start(f32[3,128]{1,0:T(4,128)S(1)} %slice.938), channel_id=1, source_target_pairs={{0,0},{1,1},{2,3},{3,2},{4,4},{5,5},{6,7},{7,6},{8,8},{9,9},{10,11... | collective-permute-start | bytes 4616 | tf_op jit(solution)/shard_map/ppermute | solution.py:400
  12.5 0.7 collective-permute-start.43
  13.4 2.0 %slice-start.4 = ((f32[120,128]{1,0:T(8,128)}), f32[64,128]{1,0:T(8,128)S(1)}, s32[]{:S(2)}) async-start(f32[120,128]{1,0:T(8,128)} %copy-done.18), calls=%async_computation.4 | async-start | bytes 65536 | tf_op jit(solution)/shard_map/slice | solution.py:444
  13.5 4.4 %collective-permute-start.46 = (f32[56,128]{1,0:T(8,128)S(1)}, f32[56,128]{1,0:T(8,128)S(1)}, u32[]{:S(2)}, u32[]{:S(2)}) collective-permute-start(f32[56,128]{1,0:T(8,128)S(1)} %pad_maximum_fusion.32), channel_id=1, source_target_pairs={{0,0},{1,1},{2,18},{3,19},{4,4},{5,5},{6,22},{7,23},{8,8},{9,9},{1... | collective-permute-start | bytes 86024 | tf_op jit(solution)/shard_map/ppermute | solution.py:400
  14.1 3.7 %collective-permute-start.47 = (f32[56,128]{1,0:T(8,128)S(1)}, f32[56,128]{1,0:T(8,128)S(1)}, u32[]{:S(2)}, u32[]{:S(2)}) collective-permute-start(f32[56,128]{1,0:T(8,128)S(1)} %pad_maximum_fusion.32), channel_id=1, source_target_pairs={{0,0},{1,1},{2,26},{3,27},{4,4},{5,5},{6,30},{7,31},{8,8},{9,9},{1... | collective-permute-start | bytes 86024 | tf_op jit(solution)/shard_map/ppermute | solution.py:400
  14.8 3.1 %collective-permute-start.45 = (f32[56,128]{1,0:T(8,128)S(1)}, f32[56,128]{1,0:T(8,128)S(1)}, u32[]{:S(2)}, u32[]{:S(2)}) collective-permute-start(f32[56,128]{1,0:T(8,128)S(1)} %pad_maximum_fusion.32), channel_id=1, source_target_pairs={{0,0},{1,1},{2,10},{3,11},{4,4},{5,5},{6,14},{7,15},{8,8},{9,9},{1... | collective-permute-start | bytes 86024 | tf_op jit(solution)/shard_map/ppermute | solution.py:400
  15.5 6.2 %collective-permute-start.41 = (f32[128,128]{1,0:T(8,128)S(1)}, f32[128,128]{1,0:T(8,128)S(1)}, u32[]{:S(2)}, u32[]{:S(2)}) collective-permute-start(f32[128,128]{1,0:T(8,128)S(1)} %pad_maximum_fusion.24), channel_id=1, source_target_pairs={{0,1},{1,0},{2,2},{3,3},{4,5},{5,4},{6,6},{7,7},{8,9},{9,8},{10,10... | collective-permute-start | bytes 196616 | tf_op jit(solution)/shard_map/ppermute | solution.py:400
  21.7 13.2 %collective-permute-start.48 = (f32[64,128]{1,0:T(8,128)S(1)}, f32[64,128]{1,0:T(8,128)S(1)}, u32[]{:S(2)}, u32[]{:S(2)}) collective-permute-start(f32[64,128]{1,0:T(8,128)S(1)} %slice_select_fusion.20), channel_id=1, source_target_pairs={{0,2},{1,3},{2,0},{3,1},{4,6},{5,7},{6,4},{7,5},{8,10},{9,11},{10,... | collective-permute-start | bytes 98312 | tf_op jit(solution)/shard_map/ppermute | solution.py:400
  35.7 1.3 %copy-start.6 = (f32[72,128]{1,0:T(8,128)}, f32[72,128]{1,0:T(8,128)S(1)}, u32[]{:S(2)}) copy-start(f32[72,128]{1,0:T(8,128)S(1)} %get-tuple-element.253.refs_6_) | copy-start | bytes 110596
  35.7 1.3 %collective-permute-start.49 = (f32[88,128]{1,0:T(8,128)S(1)}, f32[88,128]{1,0:T(8,128)S(1)}, u32[]{:S(2)}, u32[]{:S(2)}) collective-permute-start(f32[88,128]{1,0:T(8,128)S(1)} %get-tuple-element.256), channel_id=1, source_target_pairs={{0,2},{1,3},{2,0},{3,1},{4,6},{5,7},{6,4},{7,5},{8,10},{9,11},{10,... | collective-permute-start | bytes 135176 | tf_op jit(solution)/shard_map/ppermute | solution.py:400
  37.0 2.3 %copy-start.16 = (f32[88,128]{1,0:T(8,128)}, f32[88,128]{1,0:T(8,128)S(1)}, u32[]{:S(2)}) copy-start(f32[88,128]{1,0:T(8,128)S(1)} %collective-permute-done.49) | copy-start | bytes 135172
  37.0 2.0 %collective-permute-start.51 = (f32[24,128]{1,0:T(8,128)S(1)}, f32[24,128]{1,0:T(8,128)S(1)}, u32[]{:S(2)}, u32[]{:S(2)}) collective-permute-start(f32[24,128]{1,0:T(8,128)S(1)} %pad_maximum_fusion.37), channel_id=1, source_target_pairs={{0,0},{1,1},{2,6},{3,7},{4,4},{5,5},{6,2},{7,3},{8,8},{9,9},{10,14... | collective-permute-start | bytes 36872 | tf_op jit(solution)/shard_map/ppermute | solution.py:400
  37.7 1.4 %collective-permute-start.53 = (f32[3,128]{1,0:T(4,128)S(1)}, f32[3,128]{1,0:T(4,128)S(1)}, u32[]{:S(2)}, u32[]{:S(2)}) collective-permute-start(f32[3,128]{1,0:T(4,128)S(1)} %slice.959), channel_id=1, source_target_pairs={{0,0},{1,1},{2,3},{3,2},{4,4},{5,5},{6,7},{7,6},{8,8},{9,9},{10,11... | collective-permute-start | bytes 4616 | tf_op jit(solution)/shard_map/ppermute | solution.py:400
  38.4 0.7 collective-permute-start.52
  39.3 2.0 %slice-start.2 = ((f32[88,128]{1,0:T(8,128)}), f32[64,128]{1,0:T(8,128)S(1)}, s32[]{:S(2)}) async-start(f32[88,128]{1,0:T(8,128)} %copy-done.16), calls=%async_computation.2 | async-start | bytes 65536 | tf_op jit(solution)/shard_map/slice | solution.py:444
  39.3 5.5 %collective-permute-start.56 = (f32[24,128]{1,0:T(8,128)S(1)}, f32[24,128]{1,0:T(8,128)S(1)}, u32[]{:S(2)}, u32[]{:S(2)}) collective-permute-start(f32[24,128]{1,0:T(8,128)S(1)} %pad_maximum_fusion.38), channel_id=1, source_target_pairs={{0,0},{1,1},{2,26},{3,27},{4,4},{5,5},{6,30},{7,31},{8,8},{9,9},{1... | collective-permute-start | bytes 36872 | tf_op jit(solution)/shard_map/ppermute | solution.py:400
  40.0 4.8 %collective-permute-start.55 = (f32[24,128]{1,0:T(8,128)S(1)}, f32[24,128]{1,0:T(8,128)S(1)}, u32[]{:S(2)}, u32[]{:S(2)}) collective-permute-start(f32[24,128]{1,0:T(8,128)S(1)} %pad_maximum_fusion.38), channel_id=1, source_target_pairs={{0,0},{1,1},{2,18},{3,19},{4,4},{5,5},{6,22},{7,23},{8,8},{9,9},{1... | collective-permute-start | bytes 36872 | tf_op jit(solution)/shard_map/ppermute | solution.py:400
  40.7 4.2 %collective-permute-start.54 = (f32[24,128]{1,0:T(8,128)S(1)}, f32[24,128]{1,0:T(8,128)S(1)}, u32[]{:S(2)}, u32[]{:S(2)}) collective-permute-start(f32[24,128]{1,0:T(8,128)S(1)} %pad_maximum_fusion.38), channel_id=1, source_target_pairs={{0,0},{1,1},{2,10},{3,11},{4,4},{5,5},{6,14},{7,15},{8,8},{9,9},{1... | collective-permute-start | bytes 36872 | tf_op jit(solution)/shard_map/ppermute | solution.py:400
  41.4 6.2 %collective-permute-start.50 = (f32[128,128]{1,0:T(8,128)S(1)}, f32[128,128]{1,0:T(8,128)S(1)}, u32[]{:S(2)}, u32[]{:S(2)}) collective-permute-start(f32[128,128]{1,0:T(8,128)S(1)} %pad_maximum_fusion.25), channel_id=1, source_target_pairs={{0,1},{1,0},{2,2},{3,3},{4,5},{5,4},{6,6},{7,7},{8,9},{9,8},{10,10... | collective-permute-start | bytes 196616 | tf_op jit(solution)/shard_map/ppermute | solution.py:400
  47.5 12.0 %collective-permute-start.57 = (f32[64,128]{1,0:T(8,128)S(1)}, f32[64,128]{1,0:T(8,128)S(1)}, u32[]{:S(2)}, u32[]{:S(2)}) collective-permute-start(f32[64,128]{1,0:T(8,128)S(1)} %slice_select_fusion.18), channel_id=1, source_target_pairs={{0,2},{1,3},{2,0},{3,1},{4,6},{5,7},{6,4},{7,5},{8,10},{9,11},{10,... | collective-permute-start | bytes 98312 | tf_op jit(solution)/shard_map/ppermute | solution.py:400
  59.6 0.8 copy-start.7
  61.1 0.6 copy-start.4
  61.7 2.0 %copy-start = (f32[88,128]{1,0:T(8,128)}, f32[88,128]{1,0:T(8,128)S(1)}, u32[]{:S(2)}) copy-start(f32[88,128]{1,0:T(8,128)S(1)} %get-tuple-element.263) | copy-start | bytes 135172
  61.7 1.2 %collective-permute-start.58 = (f32[88,128]{1,0:T(8,128)S(1)}, f32[88,128]{1,0:T(8,128)S(1)}, u32[]{:S(2)}, u32[]{:S(2)}) collective-permute-start(f32[88,128]{1,0:T(8,128)S(1)} %get-tuple-element.263), channel_id=1, source_target_pairs={{0,2},{1,3},{2,0},{3,1},{4,6},{5,7},{6,4},{7,5},{8,10},{9,11},{10,... | collective-permute-start | bytes 135176 | tf_op jit(solution)/shard_map/ppermute | solution.py:400
  62.9 3.1 %copy-start.14 = (f32[88,128]{1,0:T(8,128)}, f32[88,128]{1,0:T(8,128)S(1)}, u32[]{:S(2)}) copy-start(f32[88,128]{1,0:T(8,128)S(1)} %collective-permute-done.58) | copy-start | bytes 135172
  63.0 2.0 %collective-permute-start.60 = (f32[24,128]{1,0:T(8,128)S(1)}, f32[24,128]{1,0:T(8,128)S(1)}, u32[]{:S(2)}, u32[]{:S(2)}) collective-permute-start(f32[24,128]{1,0:T(8,128)S(1)} %pad_maximum_fusion.39), channel_id=1, source_target_pairs={{0,0},{1,1},{2,6},{3,7},{4,4},{5,5},{6,2},{7,3},{8,8},{9,9},{10,14... | collective-permute-start | bytes 36872 | tf_op jit(solution)/shard_map/ppermute | solution.py:400
  63.7 1.4 %collective-permute-start.62 = (f32[3,128]{1,0:T(4,128)S(1)}, f32[3,128]{1,0:T(4,128)S(1)}, u32[]{:S(2)}, u32[]{:S(2)}) collective-permute-start(f32[3,128]{1,0:T(4,128)S(1)} %slice.980), channel_id=1, source_target_pairs={{0,0},{1,1},{2,3},{3,2},{4,4},{5,5},{6,7},{7,6},{8,8},{9,9},{10,11... | collective-permute-start | bytes 4616 | tf_op jit(solution)/shard_map/ppermute | solution.py:400
  64.3 0.7 collective-permute-start.61
  66.0 2.0 %slice-start = ((f32[88,128]{1,0:T(8,128)}), f32[64,128]{1,0:T(8,128)S(1)}, s32[]{:S(2)}) async-start(f32[88,128]{1,0:T(8,128)} %copy-done.14), calls=%async_computation | async-start | bytes 65536 | tf_op jit(solution)/shard_map/slice | solution.py:444
  66.0 4.7 %collective-permute-start.65 = (f32[24,128]{1,0:T(8,128)S(1)}, f32[24,128]{1,0:T(8,128)S(1)}, u32[]{:S(2)}, u32[]{:S(2)}) collective-permute-start(f32[24,128]{1,0:T(8,128)S(1)} %pad_maximum_fusion.40), channel_id=1, source_target_pairs={{0,0},{1,1},{2,26},{3,27},{4,4},{5,5},{6,30},{7,31},{8,8},{9,9},{1... | collective-permute-start | bytes 36872 | tf_op jit(solution)/shard_map/ppermute | solution.py:400
  66.7 4.0 %collective-permute-start.64 = (f32[24,128]{1,0:T(8,128)S(1)}, f32[24,128]{1,0:T(8,128)S(1)}, u32[]{:S(2)}, u32[]{:S(2)}) collective-permute-start(f32[24,128]{1,0:T(8,128)S(1)} %pad_maximum_fusion.40), channel_id=1, source_target_pairs={{0,0},{1,1},{2,18},{3,19},{4,4},{5,5},{6,22},{7,23},{8,8},{9,9},{1... | collective-permute-start | bytes 36872 | tf_op jit(solution)/shard_map/ppermute | solution.py:400
  67.4 3.3 %collective-permute-start.63 = (f32[24,128]{1,0:T(8,128)S(1)}, f32[24,128]{1,0:T(8,128)S(1)}, u32[]{:S(2)}, u32[]{:S(2)}) collective-permute-start(f32[24,128]{1,0:T(8,128)S(1)} %pad_maximum_fusion.40), channel_id=1, source_target_pairs={{0,0},{1,1},{2,10},{3,11},{4,4},{5,5},{6,14},{7,15},{8,8},{9,9},{1... | collective-permute-start | bytes 36872 | tf_op jit(solution)/shard_map/ppermute | solution.py:400
  68.0 6.2 %collective-permute-start.59 = (f32[128,128]{1,0:T(8,128)S(1)}, f32[128,128]{1,0:T(8,128)S(1)}, u32[]{:S(2)}, u32[]{:S(2)}) collective-permute-start(f32[128,128]{1,0:T(8,128)S(1)} %pad_maximum_fusion.26), channel_id=1, source_target_pairs={{0,1},{1,0},{2,2},{3,3},{4,5},{5,4},{6,6},{7,7},{8,9},{9,8},{10,10... | collective-permute-start | bytes 196616 | tf_op jit(solution)/shard_map/ppermute | solution.py:400
  74.2 12.4 %collective-permute-start.66 = (f32[64,128]{1,0:T(8,128)S(1)}, f32[64,128]{1,0:T(8,128)S(1)}, u32[]{:S(2)}, u32[]{:S(2)}) collective-permute-start(f32[64,128]{1,0:T(8,128)S(1)} %slice_select_fusion.16), channel_id=1, source_target_pairs={{0,2},{1,3},{2,0},{3,1},{4,6},{5,7},{6,4},{7,5},{8,10},{9,11},{10,... | collective-permute-start | bytes 98312 | tf_op jit(solution)/shard_map/ppermute | solution.py:400
  86.6 0.8 copy-start.5
  87.4 1.4 %copy-start.10 = (f32[64,16,128]{2,1,0:T(8,128)S(1)}, f32[64,16,128]{2,1,0:T(8,128)}, u32[]{:S(2)}) copy-start(f32[64,16,128]{2,1,0:T(8,128)} %param.36) | copy-start | bytes 1572868
  87.4 1.4 %copy-start.12 = (f32[64,128]{1,0:T(8,128)S(1)}, f32[64,128]{1,0:T(8,128)}, u32[]{:S(2)}) copy-start(f32[64,128]{1,0:T(8,128)} %refs_1_.2) | copy-start | bytes 98308
  87.4 1.4 %copy-start.13 = (f32[64,128]{1,0:T(8,128)S(1)}, f32[64,128]{1,0:T(8,128)}, u32[]{:S(2)}) copy-start(f32[64,128]{1,0:T(8,128)} %refs_2_.2) | copy-start | bytes 98308
  87.4 1.4 %copy-start.28 = (s32[256]{0:T(256)S(1)}, s32[256]{0:T(256)}, u32[]{:S(2)}) copy-start(s32[256]{0:T(256)} %param.46) | copy-start | bytes 3076
  87.4 1.4 %copy-start.30 = (f32[256]{0:T(256)S(1)}, f32[256]{0:T(256)}, u32[]{:S(2)}) copy-start(f32[256]{0:T(256)} %param.48) | copy-start | bytes 3076
  87.4 1.4 %copy-start.32 = (f32[256]{0:T(256)S(1)}, f32[256]{0:T(256)}, u32[]{:S(2)}) copy-start(f32[256]{0:T(256)} %param.47) | copy-start | bytes 3076
  87.4 1.4 %copy-start.34 = (s32[2,1,64]{2,1,0:T(1,128)S(1)}, s32[2,1,64]{2,1,0:T(1,128)}, u32[]{:S(2)}) copy-start(s32[2,1,64]{2,1,0:T(1,128)} %param.43) | copy-start | bytes 1540
  87.5 1.4 %copy-start.37 = (s32[1,2]{1,0:T(1,128)S(1)}, s32[1,2]{1,0:T(1,128)}, u32[]{:S(2)}) copy-start(s32[1,2]{1,0:T(1,128)} %refs_2_.3) | copy-start | bytes 28
  87.5 1.4 %copy-start.39 = (f32[1,128]{1,0:T(1,128)S(1)}, f32[1,128]{1,0:T(1,128)}, u32[]{:S(2)}) copy-start(f32[1,128]{1,0:T(1,128)} %refs_4_.1) | copy-start | bytes 1540
  88.8 0.7 copy-start.24
  88.8 0.7 copy-start.26
  88.8 0.7 copy-start.36
  89.5 0.6 copy-start.40
  (1 other events, 0.5 us)

commit v10 on v7

--- a/solution.py
+++ b/solution.py
@@ -107,7 +107,7 @@
     pair = slot // width
     in_use = jnp.zeros((1, slots), jnp.int32)
     for target in range(regions):
-        in_use = jnp.where(pair == target, pairs_ref[0, target], in_use)
+        in_use = jnp.where(pair == target, pairs_ref[0:1, target : target + 1], in_use)
     place = lax.broadcasted_iota(jnp.int32, (slots, regions * slots), 1) == (
         own * slots + lax.broadcasted_iota(jnp.int32, (slots, regions * slots), 0)
     )
@@ -186,7 +186,7 @@
     sums_in_ref,
     maps_ref,
     flows_ref,
-    region_ref,
+    prices_ref,
     sums_ref,
 ):
     rows, techs, nodes = sizes.rows, sizes.techs, sizes.nodes
@@ -211,7 +211,7 @@
     maps_own = maps_ref[pl.ds(pl.multiple_of(own * nodes, nodes), nodes), :]
     balance = balance_ref[...] + dot3(2.0 * flows, maps_own, True)
     step_up = (1.0 / (techs + 8.0)) * balance
-    region_ref[:rows, :] = gathered[own, :rows, :] + step_up
+    prices_ref[...] = gathered[own, :rows, :] + step_up
     change = row_sum(flows * flows)
     slot = lax.broadcasted_iota(jnp.int32, change.shape, 1)
     primal = fold_lanes(jnp.where(slot // slots == own, change, 0.0))
@@ -221,9 +221,6 @@
     sums_ref[...] = sums_in_ref[...]
     squares = sums_in_ref[techs : techs + SQUARES, :] + more
     sums_ref[techs : techs + SQUARES, :] = squares
-    region_ref[rows:, :] = jnp.concatenate(
-        [squares, jnp.zeros((8 - SQUARES, LANES), jnp.float32)], axis=0
-    )
 
 
 def neighbour_rows(sizes, given, hour_index):
@@ -232,10 +229,13 @@
         return read_lanes(given.next_row, 0, units), read_lanes(given.prev_row, 0, units)
     first = halo_at(sizes)
     last = first + units // LANES
-    count = given.slabs.shape[0]
-    core, x_place, slab = hour_index % 2, hour_index // 2 % 2, hour_index // 4
-    next_row = read_lanes(given.slabs.at[(slab + 1) % count], first, units)
-    prev_row = read_lanes(given.slabs.at[(slab + count - 1) % count], last, units)
+    core, x_place, odd = hour_index % 2, hour_index // 2 % 2, hour_index // 4 % 2
+    next_row = jnp.where(
+        odd == 0, read_lanes(given.near, first, units), read_lanes(given.far, first, units)
+    )
+    prev_row = jnp.where(
+        odd == 0, read_lanes(given.far, last, units), read_lanes(given.near, last, units)
+    )
     next_row = jnp.where(x_place == 0, read_lanes(given.across, first, units), next_row)
     prev_row = jnp.where(x_place == 0, prev_row, read_lanes(given.across, last, units))
     next_row = jnp.where(core == 0, read_lanes(given.partner, first, units), next_row)
@@ -246,7 +246,7 @@
 def total_of(parts):
     if hasattr(parts, "totals"):
         return parts.totals[...]
-    return jnp.sum(parts.slabs[...], axis=0)
+    return (parts.slab[...] + parts.near[...]) + (parts.middle[...] + parts.far[...])
 
 
 def sweep_kernel(sizes, iteration, names_in, names_out, *refs):
@@ -368,7 +368,7 @@
         gives.capacity[...] = row_sum(jnp.where(tech_hot, chosen, 0.0))
         gives.negative[...] = negative
         return
-    gives.block[:rows, :] = prices + step_up
+    gives.prices[...] = prices + step_up
     gives.flows_cross[rows : rows + 1, :] = cross_limits
     gives.cap_duals[techs, :techs, :] = col_weight
     gives.cap_duals[techs, techs : 2 * techs, :] = cost
@@ -392,9 +392,6 @@
     squares = jnp.concatenate(
         [primal_row, dual_row, jnp.zeros((SQUARES - 2, LANES), jnp.float32)], axis=0
     )
-    gives.block[rows:, :] = jnp.concatenate(
-        [squares, jnp.zeros((8 - SQUARES, LANES), jnp.float32)], axis=0
-    )
     gives.sums[techs : techs + SQUARES, :] = squares
     write_halo(sizes, gives.sums, store_new)
 
@@ -442,14 +439,14 @@
     )
 
 
-def exchange(sizes, block, sums):
+def exchange(sizes, prices, sums):
     hours, regions = lax.axis_size("hours"), lax.axis_size("region")
-    techs, rows, span = sizes.techs, sizes.rows, sizes.units // LANES
+    techs, span = sizes.techs, sizes.units // LANES
     halo = halo_at(sizes)
     if regions != 2 or hours != 16:
-        gathered = lax.all_gather(block, "region")
-        squares = jnp.sum(gathered[:, rows : rows + SQUARES], axis=0)
-        totals = lax.psum(sums.at[techs:halo].set(squares), "hours")
+        gathered = lax.all_gather(prices, "region")
+        totals = lax.psum(sums, "hours")
+        totals = totals.at[techs:halo].set(lax.psum(totals[techs:halo], "region"))
         next_row = shifted(sums[halo : halo + span], -1)
         prev_row = shifted(sums[halo + span : halo + 2 * span], 1)
         return gathered, Bag(totals=totals, next_row=next_row, prev_row=prev_row)
@@ -463,44 +460,26 @@
         total = mine + yours
         return jnp.concatenate([total[:halo], *edges, total[last + span :]], axis=0)
 
-    hour, region = lax.axis_index("hours"), lax.axis_index("region")
+    hour = lax.axis_index("hours")
     partner = swap(sums, 1, 0)
-    other = swap(block[:rows], 0, 1)
     chip = merged(sums, partner, hour % 2 == 0)
-    square = gather_from(
-        chip,
-        [
-            [(4 * z + 2 * x + core) * regions + side for x in range(2) for side in range(regions)]
-            for z in range(hours // 4)
-            for core in range(2)
-        ],
-    )
-    left = jnp.where(region == 0, square[0], square[1])
-    right = jnp.where(region == 0, square[2], square[3])
-    across = jnp.where(hour // 2 % 2 == 0, right, left)
-    slab = merged(left, right, True)
-    slab = slab.at[techs:halo].set(jnp.sum(square[:, techs:halo], axis=0))
-    slabs = gather_from(
-        slab,
-        [
-            [(4 * z + place) * regions + side for z in range(hours // 4)]
-            for place in range(4)
-            for side in range(regions)
-        ],
-    )
-    return in_order(block[:rows], other), Bag(slabs=slabs, partner=partner, across=across)
-
-
-def gather_from(value, groups):
-    return lax.all_gather(value, ("hours", "region"), axis_index_groups=groups)
+    across = swap(chip, 2, 0)
+    diagonal = swap(chip[techs:halo], 2, 1)
+    beside = swap(jnp.concatenate([prices, chip[techs:halo]], axis=0), 0, 1)
+    other, squares = beside[: sizes.rows], beside[sizes.rows :]
+    slab = merged(chip, across, hour // 2 % 2 == 0)
+    slab = slab.at[techs:halo].add(squares + diagonal)
+    near, middle, far = [swap(slab, 4 * step, 0) for step in (1, 2, 3)]
+    parts = Bag(slab=slab, near=near, middle=middle, far=far, partner=partner, across=across)
+    return in_order(prices, other), parts
 
 
 def shape(*dims, dtype=jnp.float32):
     return jax.ShapeDtypeStruct(dims, dtype)
 
 
-def corrected(sizes, state, block, sums, parts):
-    techs, rows = sizes.techs, sizes.rows
+def corrected(sizes, state, prices, sums, parts):
+    techs = sizes.techs
     totals = total_of(parts)
     first = sums_rows(sizes)
     col_weight, cost = totals[first : first + techs], totals[first + techs :]
@@ -512,8 +491,7 @@
     fixed = sums.at[:techs].set(jnp.sum(state.available[:techs] * duals, axis=1))
     fixed = fixed.at[techs].add(own)
     fixed = fixed.at[techs + 1].add(jnp.sum(duals**2 - taken**2, axis=(0, 1)))
-    block = block.at[rows : rows + SQUARES].set(fixed[techs : techs + SQUARES])
-    return exchange(sizes, block, fixed)[1]
+    return exchange(sizes, prices, fixed)[1]
 
 
 def run(args, exact):
@@ -531,7 +509,6 @@
         lambda names_in, names_out, *refs: slots_kernel(sizes, *refs),
         Bag(ends=args.cross_ends[:, 0], limit=args.cross_limit, pairs=args.pair_counts),
         Bag(info=shape(8 * (cross // LANES), nodes)),
-        smem=(2,),
     ).info
     info = both_regions(info)
     state = call(
@@ -566,15 +543,15 @@
         Bag(
             maps=shape(regions * nodes, cross, dtype=jnp.bfloat16),
             flows=shape(rows + 8, cross),
-            block=shape(rows + 8, nodes),
+            prices=shape(rows, nodes),
             sums=shape(*state.sums.shape),
         ),
     )
     del state.sums, state.balance
     state.maps_cross, state.flows_cross = closed.maps, closed.flows
-    gathered, parts = exchange(sizes, closed.block, closed.sums)
+    gathered, parts = exchange(sizes, closed.prices, closed.sums)
     if exact:
-        parts = corrected(sizes, state, closed.block, closed.sums, parts)
+        parts = corrected(sizes, state, closed.prices, closed.sums, parts)
 
     for iteration in range(1, ITERS):
         given = Bag(**vars(state), **vars(parts), gathered=gathered)
@@ -586,7 +563,7 @@
                 flows_cross=shape(rows + 8, cross),
                 store_duals=shape(rows, units),
                 charge=shape(rows, units),
-                block=shape(rows + 8, nodes),
+                prices=shape(rows, nodes),
                 sums=shape(sums_rows(sizes), nodes),
             )
         else:
@@ -599,8 +576,8 @@
             )
         results = call(functools.partial(sweep_kernel, sizes, iteration), given, outs)
         if iteration < ITERS - 1:
-            gathered, parts = exchange(sizes, results.block, results.sums)
-            del results.block, results.sums
+            gathered, parts = exchange(sizes, results.prices, results.sums)
+            del results.prices, results.sums
             vars(state).update(vars(results))
     dispatch = results.dispatch.reshape(rows, techs, nodes)
     outputs = (dispatch, results.capacity, results.prices, results.charge)

time: 85.7 us -> 60.1 us (0.70)
  blocking collectives: 64 us -> 0 us
  starting transfers between devices: 5.75 us -> 27.5 us
  waiting for transfers between devices: 1.97 us -> 21.7 us
  local copies, waits for them, and re-layouts: 5.76 us -> 3.5 us
    all_gather x6 -> x0, blocking collectives: 64 us -> none  [gather_from(): return lax.all_gather(value, ('hours', 'region'), axis_index_groups=groups)]
    ppermute x8 -> x23, starting transfers between devices: 5.75 us -> 27.5 us  [swap(): return lax.ppermute(value, ('hours', 'region'), pairs)]
    ppermute x8 -> x23, waiting for transfers between devices: 1.97 us -> 21.7 us  [swap(): return lax.ppermute(value, ('hours', 'region'), pairs)]
    unnamed x66 -> x62, local copies, waits for them, and re-layouts: 5.3 us -> 3.26 us
  transfers between devices with their start and end apart: 8 -> 23, of which waited for: 2 -> 18; matrix products, arithmetic and copies ran while one was open for 1% -> 0% of each run, Pallas kernels for 2% -> 3%
where the time goes in v10:
time: 60.1 us; the launch traced here: 59.9 us
  starting transfers between devices  27.5 us (46%)
  waiting for transfers between devices  21.7 us (36%)
  Pallas kernels  5.82 us (10%)
  local copies, waits for them, and re-layouts  3.5 us (6%)
  between operations  1.17 us (2%)
    ppermute x23, starting transfers between devices, swap(): return lax.ppermute(value, ('hours', 'region'), pairs)  27.5 us
    ppermute x23, waiting for transfers between devices, swap(): return lax.ppermute(value, ('hours', 'region'), pairs)  21.7 us
    pallas_call x6, Pallas kernels, call(): pl.pallas_call(functools.partial(kernel, names_in, names_out), out_shape=...  5.82 us
    unnamed x62, local copies, waits for them, and re-layouts  3.26 us
  transfers between devices with their start and end apart: 23, of which 18 were waited for; matrix products, arithmetic and copies ran while one was open for 0% of the time, Pallas kernels for 3%

profile of v10, /device:TPU:0, one launch (start us, length us, event | category | flops | bytes accessed | tf_op | source)
XLA Modules:
  0.0 59.9 jit_solution(5804935197679937097)
XLA Ops:
  0.6 0.0 copy-start.30
  0.6 0.0 copy-start.28
  0.7 0.6 %copy-done.30 = f32[1,64]{1,0:T(1,128)S(1)} copy-done((f32[1,64]{1,0:T(1,128)S(1)}, f32[1,64]{1,0:T(1,128)}, u32[]{:S(2)}) %copy-start.30) | copy-done | bytes 280
  1.3 0.0 copy-done.28
  1.3 0.9 %shard_map.166 = f32[8,128]{1,0:T(8,128)S(1)} custom-call(s32[2,64]{1,0:T(2,128)S(1)} %bitcast.97, f32[1,64]{1,0:T(1,128)S(1)} %copy-done.30, s32[1,2]{1,0:T(1,128)} %refs_2_.3), custom_call_target="tpu_custom_call" | custom-call | tf_op jit(solution)/shard_map/pallas_call | solution.py:401
  2.2 3.0 %collective-permute-start.31 = (f32[8,128]{1,0:T(8,128)S(1)}, f32[8,128]{1,0:T(8,128)S(1)}, u32[]{:S(2)}, u32[]{:S(2)}) collective-permute-start(f32[8,128]{1,0:T(8,128)S(1)} %shard_map.166), channel_id=1, source_target_pairs={{0,1},{1,0},{2,3},{3,2},{4,5},{5,4},{6,7},{7,6},{8,9},{9,8},{10,11... | collective-permute-start | bytes 12296 | tf_op jit(solution)/shard_map/ppermute | solution.py:422
  5.2 0.1 collective-permute-start.30
  5.3 0.6 %copy-done.19 = s32[2,256]{1,0:T(2,128)S(1)} copy-done((s32[2,256]{1,0:T(2,128)S(1)}, s32[2,256]{1,0:T(2,128)}, u32[]{:S(2)}) %copy-start.19) | copy-done | bytes 2072
  5.9 0.0 copy-done.17
  6.0 0.0 copy-done.16
  6.0 1.8 %shard_map.165 = (f32[18,64,128]{2,1,0:T(8,128)S(1)}, bf16[128,512]{1,0:T(8,128)(2,1)S(1)}, f32[64,512]{1,0:T(8,128)S(1)}, f32[64,256]{1,0:T(8,128)S(1)}, f32[17...) custom-call(f32[1024,128]{1,0:T(8,128)} %bitcast.67, f32[64,128]{1,0:T(8,128)} %refs_1_.2, ...), custom_call_target="tpu_custom_call" | custom-call | flops 1000000 | bytes 4000000 | tf_op jit(solution)/shard_map/pallas_call | solution.py:401
  7.8 1.6 %collective-permute-done.30 = f32[64,128]{1,0:T(8,128)S(1)} collective-permute-done((f32[64,128]{1,0:T(8,128)}, f32[64,128]{1,0:T(8,128)S(1)}, u32[]{:S(2)}, u32[]{:S(2)}) %collective-permute-start.30) | collective-permute-done | bytes 32800 | tf_op jit(solution)/shard_map/ppermute | solution.py:422
  9.4 0.4 shard_map.167
  9.7 0.1 collective-permute-start.32
  9.8 1.2 %collective-permute-done.32.refs_11_ = f32[56,128]{1,0:T(8,128)S(1)} collective-permute-done((f32[56,128]{1,0:T(8,128)S(1)}, f32[56,128]{1,0:T(8,128)S(1)}, u32[]{:S(2)}, u32[]{:S(2)}) %collective-permute-start.32) | collective-permute-done | bytes 28704 | tf_op jit(solution)/shard_map/ppermute | solution.py:422
  11.0 1.5 %collective-permute-start.35 = (f32[3,128]{1,0:T(4,128)S(1)}, f32[3,128]{1,0:T(4,128)S(1)}, u32[]{:S(2)}, u32[]{:S(2)}) collective-permute-start(f32[3,128]{1,0:T(4,128)S(1)} %slice.603), channel_id=1, source_target_pairs={{0,5},{1,4},{2,7},{3,6},{4,1},{5,0},{6,3},{7,2},{8,13},{9,12},{10,... | collective-permute-start | bytes 4616 | tf_op jit(solution)/shard_map/ppermute | solution.py:422
  12.5 0.5 collective-permute-start.33
  13.1 1.6 %collective-permute-start.34 = (f32[67,128]{1,0:T(8,128)S(1)}, f32[67,128]{1,0:T(8,128)S(1)}, u32[]{:S(2)}, u32[]{:S(2)}) collective-permute-start(f32[67,128]{1,0:T(8,128)S(1)} %pad_maximum_fusion.12), channel_id=1, source_target_pairs={{0,1},{1,0},{2,3},{3,2},{4,5},{5,4},{6,7},{7,6},{8,9},{9,8},{10,11... | collective-permute-start | bytes 102920 | tf_op jit(solution)/shard_map/ppermute | solution.py:422
  14.7 1.8 %collective-permute-done.33.refs_12_ = f32[56,128]{1,0:T(8,128)S(1)} collective-permute-done((f32[56,128]{1,0:T(8,128)S(1)}, f32[56,128]{1,0:T(8,128)S(1)}, u32[]{:S(2)}, u32[]{:S(2)}) %collective-permute-start.33) | collective-permute-done | bytes 28704 | tf_op jit(solution)/shard_map/ppermute | solution.py:422
  16.6 0.5 collective-permute-done.34
  17.1 0.1 scatter-add.30.refs_7_
  17.1 3.7 %collective-permute-start.38 = (f32[56,128]{1,0:T(8,128)S(1)}, f32[56,128]{1,0:T(8,128)S(1)}, u32[]{:S(2)}, u32[]{:S(2)}) collective-permute-start(f32[56,128]{1,0:T(8,128)S(1)} %scatter-add.30.refs_7_), channel_id=1, source_target_pairs={{0,24},{1,25},{2,26},{3,27},{4,28},{5,29},{6,30},{7,31},{8,16},{9,... | collective-permute-start | bytes 86024 | tf_op jit(solution)/shard_map/ppermute | solution.py:422
  20.9 0.7 %collective-permute-start.36 = (f32[56,128]{1,0:T(8,128)S(1)}, f32[56,128]{1,0:T(8,128)S(1)}, u32[]{:S(2)}, u32[]{:S(2)}) collective-permute-start(f32[56,128]{1,0:T(8,128)S(1)} %scatter-add.30.refs_7_), channel_id=1, source_target_pairs={{0,8},{1,9},{2,10},{3,11},{4,12},{5,13},{6,14},{7,15},{8,0},{9,1},... | collective-permute-start | bytes 86024 | tf_op jit(solution)/shard_map/ppermute | solution.py:422
  21.6 1.3 %collective-permute-done.38.refs_10_ = f32[56,128]{1,0:T(8,128)S(1)} collective-permute-done((f32[56,128]{1,0:T(8,128)S(1)}, f32[56,128]{1,0:T(8,128)S(1)}, u32[]{:S(2)}, u32[]{:S(2)}) %collective-permute-start.38) | collective-permute-done | bytes 28704 | tf_op jit(solution)/shard_map/ppermute | solution.py:422
  22.9 2.8 %collective-permute-done.37.refs_9_ = f32[56,128]{1,0:T(8,128)S(1)} collective-permute-done((f32[56,128]{1,0:T(8,128)S(1)}, f32[56,128]{1,0:T(8,128)S(1)}, u32[]{:S(2)}, u32[]{:S(2)}) %collective-permute-start.37) | collective-permute-done | bytes 28704 | tf_op jit(solution)/shard_map/ppermute | solution.py:422
  25.6 0.8 %shard_map.168 = (f32[17,64,128]{2,1,0:T(8,128)S(1)}, f32[17,64,128]{2,1,0:T(8,128)S(1)}, f32[64,512]{1,0:T(8,128)S(1)}, f32[72,128]{1,0:T(8,128)S(1)}, f32[64,2...) custom-call(f32[18,64,128]{2,1,0:T(8,128)S(1)} %get-tuple-element.246.refs_0_, ...), custom_call_target="tpu_custom_call" | custom-call | tf_op jit(solution)/shard_map/pallas_call | solution.py:401
  26.4 0.6 %copy-done.8 = f32[72,128]{1,0:T(8,128)} copy-done((f32[72,128]{1,0:T(8,128)}, f32[72,128]{1,0:T(8,128)S(1)}, u32[]{:S(2)}) %copy-start.8) | copy-done | bytes 36888
  27.1 1.2 %collective-permute-done.39.refs_13_ = f32[24,128]{1,0:T(8,128)S(1)} collective-permute-done((f32[24,128]{1,0:T(8,128)S(1)}, f32[24,128]{1,0:T(8,128)S(1)}, u32[]{:S(2)}, u32[]{:S(2)}) %collective-permute-start.39) | collective-permute-done | bytes 12320 | tf_op jit(solution)/shard_map/ppermute | solution.py:422
  28.2 2.5 %collective-permute-start.42 = (f32[3,128]{1,0:T(4,128)S(1)}, f32[3,128]{1,0:T(4,128)S(1)}, u32[]{:S(2)}, u32[]{:S(2)}) collective-permute-start(f32[3,128]{1,0:T(4,128)S(1)} %slice.615), channel_id=1, source_target_pairs={{0,5},{1,4},{2,7},{3,6},{4,1},{5,0},{6,3},{7,2},{8,13},{9,12},{10,... | collective-permute-start | bytes 4616 | tf_op jit(solution)/shard_map/ppermute | solution.py:422
  30.8 0.6 %collective-permute-start.40 = (f32[24,128]{1,0:T(8,128)S(1)}, f32[24,128]{1,0:T(8,128)S(1)}, u32[]{:S(2)}, u32[]{:S(2)}) collective-permute-start(f32[24,128]{1,0:T(8,128)S(1)} %pad_maximum_fusion.17), channel_id=1, source_target_pairs={{0,4},{1,5},{2,6},{3,7},{4,0},{5,1},{6,2},{7,3},{8,12},{9,13},{10,... | collective-permute-start | bytes 36872 | tf_op jit(solution)/shard_map/ppermute | solution.py:422
  31.4 0.6 collective-permute-start.41
  32.0 2.6 %collective-permute-done.40.refs_14_ = f32[24,128]{1,0:T(8,128)S(1)} collective-permute-done((f32[24,128]{1,0:T(8,128)S(1)}, f32[24,128]{1,0:T(8,128)S(1)}, u32[]{:S(2)}, u32[]{:S(2)}) %collective-permute-start.40) | collective-permute-done | bytes 12320 | tf_op jit(solution)/shard_map/ppermute | solution.py:422
  34.6 0.8 %collective-permute-done.41 = f32[67,128]{1,0:T(8,128)S(1)} collective-permute-done((f32[67,128]{1,0:T(8,128)S(1)}, f32[67,128]{1,0:T(8,128)S(1)}, u32[]{:S(2)}, u32[]{:S(2)}) %collective-permute-start.41) | collective-permute-done | bytes 34336 | tf_op jit(solution)/shard_map/ppermute | solution.py:422
  35.4 0.1 scatter-add.31.refs_9_
  35.5 1.5 %collective-permute-start.45 = (f32[24,128]{1,0:T(8,128)S(1)}, f32[24,128]{1,0:T(8,128)S(1)}, u32[]{:S(2)}, u32[]{:S(2)}) collective-permute-start(f32[24,128]{1,0:T(8,128)S(1)} %scatter-add.31.refs_9_), channel_id=1, source_target_pairs={{0,24},{1,25},{2,26},{3,27},{4,28},{5,29},{6,30},{7,31},{8,16},{9,... | collective-permute-start | bytes 36872 | tf_op jit(solution)/shard_map/ppermute | solution.py:422
  37.0 0.6 %collective-permute-start.44 = (f32[24,128]{1,0:T(8,128)S(1)}, f32[24,128]{1,0:T(8,128)S(1)}, u32[]{:S(2)}, u32[]{:S(2)}) collective-permute-start(f32[24,128]{1,0:T(8,128)S(1)} %scatter-add.31.refs_9_), channel_id=1, source_target_pairs={{0,16},{1,17},{2,18},{3,19},{4,20},{5,21},{6,22},{7,23},{8,24},{9,... | collective-permute-start | bytes 36872 | tf_op jit(solution)/shard_map/ppermute | solution.py:422
  37.6 2.3 %collective-permute-start.43 = (f32[24,128]{1,0:T(8,128)S(1)}, f32[24,128]{1,0:T(8,128)S(1)}, u32[]{:S(2)}, u32[]{:S(2)}) collective-permute-start(f32[24,128]{1,0:T(8,128)S(1)} %scatter-add.31.refs_9_), channel_id=1, source_target_pairs={{0,8},{1,9},{2,10},{3,11},{4,12},{5,13},{6,14},{7,15},{8,0},{9,1},... | collective-permute-start | bytes 36872 | tf_op jit(solution)/shard_map/ppermute | solution.py:422
  40.0 1.1 %collective-permute-done.45.refs_12_ = f32[24,128]{1,0:T(8,128)S(1)} collective-permute-done((f32[24,128]{1,0:T(8,128)S(1)}, f32[24,128]{1,0:T(8,128)S(1)}, u32[]{:S(2)}, u32[]{:S(2)}) %collective-permute-start.45) | collective-permute-done | bytes 12320 | tf_op jit(solution)/shard_map/ppermute | solution.py:422
  41.0 0.6 collective-permute-done.44.refs_11_
  41.6 0.1 collective-permute-done.43.refs_10_
  41.7 0.7 %shard_map.169 = (f32[17,64,128]{2,1,0:T(8,128)S(1)}, f32[17,64,128]{2,1,0:T(8,128)S(1)}, f32[64,512]{1,0:T(8,128)S(1)}, f32[72,128]{1,0:T(8,128)S(1)}, f32[64,2...) custom-call(f32[18,64,128]{2,1,0:T(8,128)S(1)} %get-tuple-element.246.refs_0_, ...), custom_call_target="tpu_custom_call" | custom-call | tf_op jit(solution)/shard_map/pallas_call | solution.py:401
  42.5 0.0 copy-start.6
  42.5 0.1 collective-permute-start.46
  42.6 1.2 %collective-permute-done.46.refs_13_ = f32[24,128]{1,0:T(8,128)S(1)} collective-permute-done((f32[24,128]{1,0:T(8,128)S(1)}, f32[24,128]{1,0:T(8,128)S(1)}, u32[]{:S(2)}, u32[]{:S(2)}) %collective-permute-start.46) | collective-permute-done | bytes 12320 | tf_op jit(solution)/shard_map/ppermute | solution.py:422
  43.7 1.5 %collective-permute-start.49 = (f32[3,128]{1,0:T(4,128)S(1)}, f32[3,128]{1,0:T(4,128)S(1)}, u32[]{:S(2)}, u32[]{:S(2)}) collective-permute-start(f32[3,128]{1,0:T(4,128)S(1)} %slice.627), channel_id=1, source_target_pairs={{0,5},{1,4},{2,7},{3,6},{4,1},{5,0},{6,3},{7,2},{8,13},{9,12},{10,... | collective-permute-start | bytes 4616 | tf_op jit(solution)/shard_map/ppermute | solution.py:422
  45.3 0.6 %collective-permute-start.47 = (f32[24,128]{1,0:T(8,128)S(1)}, f32[24,128]{1,0:T(8,128)S(1)}, u32[]{:S(2)}, u32[]{:S(2)}) collective-permute-start(f32[24,128]{1,0:T(8,128)S(1)} %pad_maximum_fusion.19), channel_id=1, source_target_pairs={{0,4},{1,5},{2,6},{3,7},{4,0},{5,1},{6,2},{7,3},{8,12},{9,13},{10,... | collective-permute-start | bytes 36872 | tf_op jit(solution)/shard_map/ppermute | solution.py:422
  45.9 1.5 %collective-permute-start.48 = (f32[67,128]{1,0:T(8,128)S(1)}, f32[67,128]{1,0:T(8,128)S(1)}, u32[]{:S(2)}, u32[]{:S(2)}) collective-permute-start(f32[67,128]{1,0:T(8,128)S(1)} %pad_maximum_fusion.14), channel_id=1, source_target_pairs={{0,1},{1,0},{2,3},{3,2},{4,5},{5,4},{6,7},{7,6},{8,9},{9,8},{10,11... | collective-permute-start | bytes 102920 | tf_op jit(solution)/shard_map/ppermute | solution.py:422
  47.4 1.6 %collective-permute-done.47.refs_14_ = f32[24,128]{1,0:T(8,128)S(1)} collective-permute-done((f32[24,128]{1,0:T(8,128)S(1)}, f32[24,128]{1,0:T(8,128)S(1)}, u32[]{:S(2)}, u32[]{:S(2)}) %collective-permute-start.47) | collective-permute-done | bytes 12320 | tf_op jit(solution)/shard_map/ppermute | solution.py:422
  49.1 0.7 %collective-permute-done.48 = f32[67,128]{1,0:T(8,128)S(1)} collective-permute-done((f32[67,128]{1,0:T(8,128)S(1)}, f32[67,128]{1,0:T(8,128)S(1)}, u32[]{:S(2)}, u32[]{:S(2)}) %collective-permute-start.48) | collective-permute-done | bytes 34336 | tf_op jit(solution)/shard_map/ppermute | solution.py:422
  49.8 0.1 scatter-add.34.refs_9_
  49.9 2.5 %collective-permute-start.52 = (f32[24,128]{1,0:T(8,128)S(1)}, f32[24,128]{1,0:T(8,128)S(1)}, u32[]{:S(2)}, u32[]{:S(2)}) collective-permute-start(f32[24,128]{1,0:T(8,128)S(1)} %scatter-add.34.refs_9_), channel_id=1, source_target_pairs={{0,24},{1,25},{2,26},{3,27},{4,28},{5,29},{6,30},{7,31},{8,16},{9,... | collective-permute-start | bytes 36872 | tf_op jit(solution)/shard_map/ppermute | solution.py:422
  52.4 0.9 %collective-permute-start.51 = (f32[24,128]{1,0:T(8,128)S(1)}, f32[24,128]{1,0:T(8,128)S(1)}, u32[]{:S(2)}, u32[]{:S(2)}) collective-permute-start(f32[24,128]{1,0:T(8,128)S(1)} %scatter-add.34.refs_9_), channel_id=1, source_target_pairs={{0,16},{1,17},{2,18},{3,19},{4,20},{5,21},{6,22},{7,23},{8,24},{9,... | collective-permute-start | bytes 36872 | tf_op jit(solution)/shard_map/ppermute | solution.py:422
  53.3 1.0 %collective-permute-start.50 = (f32[24,128]{1,0:T(8,128)S(1)}, f32[24,128]{1,0:T(8,128)S(1)}, u32[]{:S(2)}, u32[]{:S(2)}) collective-permute-start(f32[24,128]{1,0:T(8,128)S(1)} %scatter-add.34.refs_9_), channel_id=1, source_target_pairs={{0,8},{1,9},{2,10},{3,11},{4,12},{5,13},{6,14},{7,15},{8,0},{9,1},... | collective-permute-start | bytes 36872 | tf_op jit(solution)/shard_map/ppermute | solution.py:422
  54.4 1.2 %collective-permute-done.52.refs_12_ = f32[24,128]{1,0:T(8,128)S(1)} collective-permute-done((f32[24,128]{1,0:T(8,128)S(1)}, f32[24,128]{1,0:T(8,128)S(1)}, u32[]{:S(2)}, u32[]{:S(2)}) %collective-permute-start.52) | collective-permute-done | bytes 12320 | tf_op jit(solution)/shard_map/ppermute | solution.py:422
  55.5 1.5 %collective-permute-done.51.refs_11_ = f32[24,128]{1,0:T(8,128)S(1)} collective-permute-done((f32[24,128]{1,0:T(8,128)S(1)}, f32[24,128]{1,0:T(8,128)S(1)}, u32[]{:S(2)}, u32[]{:S(2)}) %collective-permute-start.51) | collective-permute-done | bytes 12320 | tf_op jit(solution)/shard_map/ppermute | solution.py:422
  57.0 0.1 collective-permute-done.50.refs_10_
  57.2 0.0 copy-start.27
  57.2 0.0 copy-start.29
  57.2 0.0 copy-start.34
  57.2 1.3 %shard_map.170 = (f32[1024,128]{1,0:T(8,128)}, f32[1,128]{1,0:T(1,128)S(1)}, f32[64,128]{1,0:T(8,128)S(1)}, f32[64,256]{1,0:T(8,128)}, f32[1,128]{1,0:T(1,128)S(1)}) custom-call(f32[18,64,128]{2,1,0:T(8,128)S(1)} %get-tuple-element.246.refs_0_, bf16[128,512]{1,0:T(8,128)(2,1)S(1)} %get-tuple-element.247.refs_1_, f32[64,512]{1,0:T(8,128)S(1)} %get-tuple-element.265.refs_2_, ...), custom_call_target="tpu_custom_call" | custom-call | tf_op jit(solution)/shard_map/pallas_call | solution.py:401
  58.7 0.5 copy-done.18
  59.2 0.0 copy-done.21
  59.3 0.5 copy-done.36
  59.8 0.1 copy-done.35
  (97 shorter events, 0.4 us)
Async XLA Ops:
  0.6 0.7 %copy-start.30 = (f32[1,64]{1,0:T(1,128)S(1)}, f32[1,64]{1,0:T(1,128)}, u32[]{:S(2)}) copy-start(f32[1,64]{1,0:T(1,128)} %refs_1_.3) | copy-start | bytes 772
  0.6 0.7 %copy-start.28 = (s32[2,1,64]{2,1,0:T(1,128)S(1)}, s32[2,1,64]{2,1,0:T(1,128)}, u32[]{:S(2)}) copy-start(s32[2,1,64]{2,1,0:T(1,128)} %param.43) | copy-start | bytes 1540
  1.3 4.0 %copy-start.20 = (f32[256]{0:T(256)S(1)}, f32[256]{0:T(256)}, u32[]{:S(2)}) copy-start(f32[256]{0:T(256)} %param.42) | copy-start | bytes 3076
  1.3 4.0 %copy-start.22 = (s32[256]{0:T(256)S(1)}, s32[256]{0:T(256)}, u32[]{:S(2)}) copy-start(s32[256]{0:T(256)} %param.46) | copy-start | bytes 3076
  1.3 4.0 %copy-start.24 = (f32[256]{0:T(256)S(1)}, f32[256]{0:T(256)}, u32[]{:S(2)}) copy-start(f32[256]{0:T(256)} %param.48) | copy-start | bytes 3076
  1.3 4.0 %copy-start.26 = (f32[256]{0:T(256)S(1)}, f32[256]{0:T(256)}, u32[]{:S(2)}) copy-start(f32[256]{0:T(256)} %param.47) | copy-start | bytes 3076
  2.2 5.5 %collective-permute-start.31 = (f32[8,128]{1,0:T(8,128)S(1)}, f32[8,128]{1,0:T(8,128)S(1)}, u32[]{:S(2)}, u32[]{:S(2)}) collective-permute-start(f32[8,128]{1,0:T(8,128)S(1)} %shard_map.166), channel_id=1, source_target_pairs={{0,1},{1,0},{2,3},{3,2},{4,5},{5,4},{6,7},{7,6},{8,9},{9,8},{10,11... | collective-permute-start | bytes 12296 | tf_op jit(solution)/shard_map/ppermute | solution.py:422
  5.2 4.1 %collective-permute-start.30 = (f32[64,128]{1,0:T(8,128)}, f32[64,128]{1,0:T(8,128)S(1)}, u32[]{:S(2)}, u32[]{:S(2)}) collective-permute-start(f32[64,128]{1,0:T(8,128)} %refs_1_.2), channel_id=1, source_target_pairs={{0,1},{1,0},{2,3},{3,2},{4,5},{5,4},{6,7},{7,6},{8,9},{9,8},{10,11... | collective-permute-start | bytes 98312 | tf_op jit(solution)/shard_map/ppermute | solution.py:422
  5.3 0.7 %copy-start.19 = (s32[2,256]{1,0:T(2,128)S(1)}, s32[2,256]{1,0:T(2,128)}, u32[]{:S(2)}) copy-start(s32[2,256]{1,0:T(2,128)} %refs_6_.1) | copy-start | bytes 6148
  5.3 0.7 %copy-start.17 = (s32[1,2048]{1,0:T(1,128)S(1)}, s32[1,2048]{1,0:T(1,128)}, u32[]{:S(2)}) copy-start(s32[1,2048]{1,0:T(1,128)} %param.40) | copy-start | bytes 24580
  5.3 0.7 %copy-start.16 = (f32[16,128]{1,0:T(8,128)S(1)}, f32[16,128]{1,0:T(8,128)}, u32[]{:S(2)}) copy-start(f32[16,128]{1,0:T(8,128)} %refs_3_.1) | copy-start | bytes 24580
  5.3 0.7 %copy-start.33 = (f32[1,128]{1,0:T(1,128)S(1)}, f32[1,128]{1,0:T(1,128)}, u32[]{:S(2)}) copy-start(f32[1,128]{1,0:T(1,128)} %refs_4_.1) | copy-start | bytes 1540
  6.0 3.3 %copy-start.13 = (f32[64,128]{1,0:T(8,128)S(1)}, f32[64,128]{1,0:T(8,128)}, u32[]{:S(2)}) copy-start(f32[64,128]{1,0:T(8,128)} %refs_1_.2) | copy-start | bytes 98308
  9.7 1.3 %collective-permute-start.32 = (f32[56,128]{1,0:T(8,128)S(1)}, f32[56,128]{1,0:T(8,128)S(1)}, u32[]{:S(2)}, u32[]{:S(2)}) collective-permute-start(f32[56,128]{1,0:T(8,128)S(1)} %get-tuple-element.255), channel_id=1, source_target_pairs={{0,2},{1,3},{2,0},{3,1},{4,6},{5,7},{6,4},{7,5},{8,10},{9,11},{10,... | collective-permute-start | bytes 86024 | tf_op jit(solution)/shard_map/ppermute | solution.py:422
  11.0 5.5 %collective-permute-start.35 = (f32[3,128]{1,0:T(4,128)S(1)}, f32[3,128]{1,0:T(4,128)S(1)}, u32[]{:S(2)}, u32[]{:S(2)}) collective-permute-start(f32[3,128]{1,0:T(4,128)S(1)} %slice.603), channel_id=1, source_target_pairs={{0,5},{1,4},{2,7},{3,6},{4,1},{5,0},{6,3},{7,2},{8,13},{9,12},{10,... | collective-permute-start | bytes 4616 | tf_op jit(solution)/shard_map/ppermute | solution.py:422
  12.5 3.9 %collective-permute-start.33 = (f32[56,128]{1,0:T(8,128)S(1)}, f32[56,128]{1,0:T(8,128)S(1)}, u32[]{:S(2)}, u32[]{:S(2)}) collective-permute-start(f32[56,128]{1,0:T(8,128)S(1)} %pad_maximum_fusion.15), channel_id=1, source_target_pairs={{0,4},{1,5},{2,6},{3,7},{4,0},{5,1},{6,2},{7,3},{8,12},{9,13},{10,... | collective-permute-start | bytes 86024 | tf_op jit(solution)/shard_map/ppermute | solution.py:422
  13.1 4.0 %collective-permute-start.34 = (f32[67,128]{1,0:T(8,128)S(1)}, f32[67,128]{1,0:T(8,128)S(1)}, u32[]{:S(2)}, u32[]{:S(2)}) collective-permute-start(f32[67,128]{1,0:T(8,128)S(1)} %pad_maximum_fusion.12), channel_id=1, source_target_pairs={{0,1},{1,0},{2,3},{3,2},{4,5},{5,4},{6,7},{7,6},{8,9},{9,8},{10,11... | collective-permute-start | bytes 102920 | tf_op jit(solution)/shard_map/ppermute | solution.py:422
  17.1 5.8 %collective-permute-start.38 = (f32[56,128]{1,0:T(8,128)S(1)}, f32[56,128]{1,0:T(8,128)S(1)}, u32[]{:S(2)}, u32[]{:S(2)}) collective-permute-start(f32[56,128]{1,0:T(8,128)S(1)} %scatter-add.30.refs_7_), channel_id=1, source_target_pairs={{0,24},{1,25},{2,26},{3,27},{4,28},{5,29},{6,30},{7,31},{8,16},{9,... | collective-permute-start | bytes 86024 | tf_op jit(solution)/shard_map/ppermute | solution.py:422
  20.9 4.8 %collective-permute-start.37 = (f32[56,128]{1,0:T(8,128)S(1)}, f32[56,128]{1,0:T(8,128)S(1)}, u32[]{:S(2)}, u32[]{:S(2)}) collective-permute-start(f32[56,128]{1,0:T(8,128)S(1)} %scatter-add.30.refs_7_), channel_id=1, source_target_pairs={{0,16},{1,17},{2,18},{3,19},{4,20},{5,21},{6,22},{7,23},{8,24},{9,... | collective-permute-start | bytes 86024 | tf_op jit(solution)/shard_map/ppermute | solution.py:422
  20.9 4.8 %collective-permute-start.36 = (f32[56,128]{1,0:T(8,128)S(1)}, f32[56,128]{1,0:T(8,128)S(1)}, u32[]{:S(2)}, u32[]{:S(2)}) collective-permute-start(f32[56,128]{1,0:T(8,128)S(1)} %scatter-add.30.refs_7_), channel_id=1, source_target_pairs={{0,8},{1,9},{2,10},{3,11},{4,12},{5,13},{6,14},{7,15},{8,0},{9,1},... | collective-permute-start | bytes 86024 | tf_op jit(solution)/shard_map/ppermute | solution.py:422
  26.4 0.6 %copy-start.8 = (f32[72,128]{1,0:T(8,128)}, f32[72,128]{1,0:T(8,128)S(1)}, u32[]{:S(2)}) copy-start(f32[72,128]{1,0:T(8,128)S(1)} %get-tuple-element.260.refs_6_) | copy-start | bytes 110596
  27.1 4.3 %copy-start = (f32[64,256]{1,0:T(8,128)}, f32[64,256]{1,0:T(8,128)S(1)}, u32[]{:S(2)}) copy-start(f32[64,256]{1,0:T(8,128)S(1)} %get-tuple-element.262.refs_8_) | copy-start | bytes 196612
  27.1 1.2 %collective-permute-start.39 = (f32[24,128]{1,0:T(8,128)S(1)}, f32[24,128]{1,0:T(8,128)S(1)}, u32[]{:S(2)}, u32[]{:S(2)}) collective-permute-start(f32[24,128]{1,0:T(8,128)S(1)} %get-tuple-element.263), channel_id=1, source_target_pairs={{0,2},{1,3},{2,0},{3,1},{4,6},{5,7},{6,4},{7,5},{8,10},{9,11},{10,... | collective-permute-start | bytes 36872 | tf_op jit(solution)/shard_map/ppermute | solution.py:422
  28.2 6.3 %collective-permute-start.42 = (f32[3,128]{1,0:T(4,128)S(1)}, f32[3,128]{1,0:T(4,128)S(1)}, u32[]{:S(2)}, u32[]{:S(2)}) collective-permute-start(f32[3,128]{1,0:T(4,128)S(1)} %slice.615), channel_id=1, source_target_pairs={{0,5},{1,4},{2,7},{3,6},{4,1},{5,0},{6,3},{7,2},{8,13},{9,12},{10,... | collective-permute-start | bytes 4616 | tf_op jit(solution)/shard_map/ppermute | solution.py:422
  30.8 3.8 %collective-permute-start.40 = (f32[24,128]{1,0:T(8,128)S(1)}, f32[24,128]{1,0:T(8,128)S(1)}, u32[]{:S(2)}, u32[]{:S(2)}) collective-permute-start(f32[24,128]{1,0:T(8,128)S(1)} %pad_maximum_fusion.17), channel_id=1, source_target_pairs={{0,4},{1,5},{2,6},{3,7},{4,0},{5,1},{6,2},{7,3},{8,12},{9,13},{10,... | collective-permute-start | bytes 36872 | tf_op jit(solution)/shard_map/ppermute | solution.py:422
  31.4 4.0 %collective-permute-start.41 = (f32[67,128]{1,0:T(8,128)S(1)}, f32[67,128]{1,0:T(8,128)S(1)}, u32[]{:S(2)}, u32[]{:S(2)}) collective-permute-start(f32[67,128]{1,0:T(8,128)S(1)} %pad_maximum_fusion.13), channel_id=1, source_target_pairs={{0,1},{1,0},{2,3},{3,2},{4,5},{5,4},{6,7},{7,6},{8,9},{9,8},{10,11... | collective-permute-start | bytes 102920 | tf_op jit(solution)/shard_map/ppermute | solution.py:422
  35.5 5.6 %collective-permute-start.45 = (f32[24,128]{1,0:T(8,128)S(1)}, f32[24,128]{1,0:T(8,128)S(1)}, u32[]{:S(2)}, u32[]{:S(2)}) collective-permute-start(f32[24,128]{1,0:T(8,128)S(1)} %scatter-add.31.refs_9_), channel_id=1, source_target_pairs={{0,24},{1,25},{2,26},{3,27},{4,28},{5,29},{6,30},{7,31},{8,16},{9,... | collective-permute-start | bytes 36872 | tf_op jit(solution)/shard_map/ppermute | solution.py:422
  37.0 4.6 %collective-permute-start.44 = (f32[24,128]{1,0:T(8,128)S(1)}, f32[24,128]{1,0:T(8,128)S(1)}, u32[]{:S(2)}, u32[]{:S(2)}) collective-permute-start(f32[24,128]{1,0:T(8,128)S(1)} %scatter-add.31.refs_9_), channel_id=1, source_target_pairs={{0,16},{1,17},{2,18},{3,19},{4,20},{5,21},{6,22},{7,23},{8,24},{9,... | collective-permute-start | bytes 36872 | tf_op jit(solution)/shard_map/ppermute | solution.py:422
  37.6 4.1 %collective-permute-start.43 = (f32[24,128]{1,0:T(8,128)S(1)}, f32[24,128]{1,0:T(8,128)S(1)}, u32[]{:S(2)}, u32[]{:S(2)}) collective-permute-start(f32[24,128]{1,0:T(8,128)S(1)} %scatter-add.31.refs_9_), channel_id=1, source_target_pairs={{0,8},{1,9},{2,10},{3,11},{4,12},{5,13},{6,14},{7,15},{8,0},{9,1},... | collective-permute-start | bytes 36872 | tf_op jit(solution)/shard_map/ppermute | solution.py:422
  39.9 1.8 %copy-start.1 = (f32[64,256]{1,0:T(8,128)S(1)}, f32[64,256]{1,0:T(8,128)}, u32[]{:S(2)}) copy-start(f32[64,256]{1,0:T(8,128)} %copy-done) | copy-start | bytes 196612
  39.9 1.8 %copy-start.9 = (f32[72,128]{1,0:T(8,128)S(1)}, f32[72,128]{1,0:T(8,128)}, u32[]{:S(2)}) copy-start(f32[72,128]{1,0:T(8,128)} %copy-done.8) | copy-start | bytes 110596
  42.5 2.8 %copy-start.6 = (f32[72,128]{1,0:T(8,128)}, f32[72,128]{1,0:T(8,128)S(1)}, u32[]{:S(2)}) copy-start(f32[72,128]{1,0:T(8,128)S(1)} %get-tuple-element.268.refs_6_) | copy-start | bytes 110596
  42.5 1.2 %collective-permute-start.46 = (f32[24,128]{1,0:T(8,128)S(1)}, f32[24,128]{1,0:T(8,128)S(1)}, u32[]{:S(2)}, u32[]{:S(2)}) collective-permute-start(f32[24,128]{1,0:T(8,128)S(1)} %get-tuple-element.271), channel_id=1, source_target_pairs={{0,2},{1,3},{2,0},{3,1},{4,6},{5,7},{6,4},{7,5},{8,10},{9,11},{10,... | collective-permute-start | bytes 36872 | tf_op jit(solution)/shard_map/ppermute | solution.py:422
  43.7 5.3 %collective-permute-start.49 = (f32[3,128]{1,0:T(4,128)S(1)}, f32[3,128]{1,0:T(4,128)S(1)}, u32[]{:S(2)}, u32[]{:S(2)}) collective-permute-start(f32[3,128]{1,0:T(4,128)S(1)} %slice.627), channel_id=1, source_target_pairs={{0,5},{1,4},{2,7},{3,6},{4,1},{5,0},{6,3},{7,2},{8,13},{9,12},{10,... | collective-permute-start | bytes 4616 | tf_op jit(solution)/shard_map/ppermute | solution.py:422
  45.3 3.8 %collective-permute-start.47 = (f32[24,128]{1,0:T(8,128)S(1)}, f32[24,128]{1,0:T(8,128)S(1)}, u32[]{:S(2)}, u32[]{:S(2)}) collective-permute-start(f32[24,128]{1,0:T(8,128)S(1)} %pad_maximum_fusion.19), channel_id=1, source_target_pairs={{0,4},{1,5},{2,6},{3,7},{4,0},{5,1},{6,2},{7,3},{8,12},{9,13},{10,... | collective-permute-start | bytes 36872 | tf_op jit(solution)/shard_map/ppermute | solution.py:422
  45.9 4.0 %collective-permute-start.48 = (f32[67,128]{1,0:T(8,128)S(1)}, f32[67,128]{1,0:T(8,128)S(1)}, u32[]{:S(2)}, u32[]{:S(2)}) collective-permute-start(f32[67,128]{1,0:T(8,128)S(1)} %pad_maximum_fusion.14), channel_id=1, source_target_pairs={{0,1},{1,0},{2,3},{3,2},{4,5},{5,4},{6,7},{7,6},{8,9},{9,8},{10,11... | collective-permute-start | bytes 102920 | tf_op jit(solution)/shard_map/ppermute | solution.py:422
  49.9 5.6 %collective-permute-start.52 = (f32[24,128]{1,0:T(8,128)S(1)}, f32[24,128]{1,0:T(8,128)S(1)}, u32[]{:S(2)}, u32[]{:S(2)}) collective-permute-start(f32[24,128]{1,0:T(8,128)S(1)} %scatter-add.34.refs_9_), channel_id=1, source_target_pairs={{0,24},{1,25},{2,26},{3,27},{4,28},{5,29},{6,30},{7,31},{8,16},{9,... | collective-permute-start | bytes 36872 | tf_op jit(solution)/shard_map/ppermute | solution.py:422
  52.4 4.6 %collective-permute-start.51 = (f32[24,128]{1,0:T(8,128)S(1)}, f32[24,128]{1,0:T(8,128)S(1)}, u32[]{:S(2)}, u32[]{:S(2)}) collective-permute-start(f32[24,128]{1,0:T(8,128)S(1)} %scatter-add.34.refs_9_), channel_id=1, source_target_pairs={{0,16},{1,17},{2,18},{3,19},{4,20},{5,21},{6,22},{7,23},{8,24},{9,... | collective-permute-start | bytes 36872 | tf_op jit(solution)/shard_map/ppermute | solution.py:422
  53.3 3.8 %collective-permute-start.50 = (f32[24,128]{1,0:T(8,128)S(1)}, f32[24,128]{1,0:T(8,128)S(1)}, u32[]{:S(2)}, u32[]{:S(2)}) collective-permute-start(f32[24,128]{1,0:T(8,128)S(1)} %scatter-add.34.refs_9_), channel_id=1, source_target_pairs={{0,8},{1,9},{2,10},{3,11},{4,12},{5,13},{6,14},{7,15},{8,0},{9,1},... | collective-permute-start | bytes 36872 | tf_op jit(solution)/shard_map/ppermute | solution.py:422
  54.4 2.8 %copy-start.7 = (f32[72,128]{1,0:T(8,128)S(1)}, f32[72,128]{1,0:T(8,128)}, u32[]{:S(2)}) copy-start(f32[72,128]{1,0:T(8,128)} %copy-done.6) | copy-start | bytes 110596
  57.2 1.4 %copy-start.12 = (f32[64,16,128]{2,1,0:T(8,128)S(1)}, f32[64,16,128]{2,1,0:T(8,128)}, u32[]{:S(2)}) copy-start(f32[64,16,128]{2,1,0:T(8,128)} %param.36) | copy-start | bytes 1572868
  57.2 1.4 %copy-start.14 = (f32[64,128]{1,0:T(8,128)S(1)}, f32[64,128]{1,0:T(8,128)}, u32[]{:S(2)}) copy-start(f32[64,128]{1,0:T(8,128)} %refs_1_.2) | copy-start | bytes 98308
  57.2 1.4 %copy-start.15 = (f32[64,128]{1,0:T(8,128)S(1)}, f32[64,128]{1,0:T(8,128)}, u32[]{:S(2)}) copy-start(f32[64,128]{1,0:T(8,128)} %refs_2_.2) | copy-start | bytes 98308
  57.2 1.5 %copy-start.23 = (s32[256]{0:T(256)S(1)}, s32[256]{0:T(256)}, u32[]{:S(2)}) copy-start(s32[256]{0:T(256)} %param.46) | copy-start | bytes 3076
  57.2 1.4 %copy-start.25 = (f32[256]{0:T(256)S(1)}, f32[256]{0:T(256)}, u32[]{:S(2)}) copy-start(f32[256]{0:T(256)} %param.48) | copy-start | bytes 3076
  57.2 1.4 %copy-start.27 = (f32[256]{0:T(256)S(1)}, f32[256]{0:T(256)}, u32[]{:S(2)}) copy-start(f32[256]{0:T(256)} %param.47) | copy-start | bytes 3076
  57.2 1.4 %copy-start.29 = (s32[2,1,64]{2,1,0:T(1,128)S(1)}, s32[2,1,64]{2,1,0:T(1,128)}, u32[]{:S(2)}) copy-start(s32[2,1,64]{2,1,0:T(1,128)} %param.43) | copy-start | bytes 1540
  57.2 1.4 %copy-start.32 = (s32[1,2]{1,0:T(1,128)S(1)}, s32[1,2]{1,0:T(1,128)}, u32[]{:S(2)}) copy-start(s32[1,2]{1,0:T(1,128)} %refs_2_.3) | copy-start | bytes 28
  57.2 1.4 %copy-start.34 = (f32[1,128]{1,0:T(1,128)S(1)}, f32[1,128]{1,0:T(1,128)}, u32[]{:S(2)}) copy-start(f32[1,128]{1,0:T(1,128)} %refs_4_.1) | copy-start | bytes 1540
  58.5 0.7 %copy-start.18 = (s32[1,2048]{1,0:T(1,128)S(1)}, s32[1,2048]{1,0:T(1,128)}, u32[]{:S(2)}) copy-start(s32[1,2048]{1,0:T(1,128)} %param.40) | copy-start | bytes 24580
  58.6 0.7 %copy-start.21 = (f32[256]{0:T(256)S(1)}, f32[256]{0:T(256)}, u32[]{:S(2)}) copy-start(f32[256]{0:T(256)} %param.42) | copy-start | bytes 3076
  58.6 0.7 %copy-start.31 = (f32[1,64]{1,0:T(1,128)S(1)}, f32[1,64]{1,0:T(1,128)}, u32[]{:S(2)}) copy-start(f32[1,64]{1,0:T(1,128)} %refs_1_.3) | copy-start | bytes 772
  59.2 0.5 copy-start.36
  59.2 0.6 %copy-start.35 = (f32[64,128]{1,0:T(8,128)}, f32[64,128]{1,0:T(8,128)S(1)}, u32[]{:S(2)}) copy-start(f32[64,128]{1,0:T(8,128)S(1)} %get-tuple-element.279) | copy-start | bytes 98308

commit v11 on v10

--- a/solution.py
+++ b/solution.py
@@ -463,13 +463,13 @@
     hour = lax.axis_index("hours")
     partner = swap(sums, 1, 0)
     chip = merged(sums, partner, hour % 2 == 0)
-    across = swap(chip, 2, 0)
-    diagonal = swap(chip[techs:halo], 2, 1)
+    across = swap(chip, 2 + 1, 0)
+    diagonal = swap(chip[techs:halo], 2 + 1, 1)
     beside = swap(jnp.concatenate([prices, chip[techs:halo]], axis=0), 0, 1)
     other, squares = beside[: sizes.rows], beside[sizes.rows :]
     slab = merged(chip, across, hour // 2 % 2 == 0)
     slab = slab.at[techs:halo].add(squares + diagonal)
-    near, middle, far = [swap(slab, 4 * step, 0) for step in (1, 2, 3)]
+    near, middle, far = [swap(slab, 4 * step + 1, 0) for step in (1, 2, 3)]
     parts = Bag(slab=slab, near=near, middle=middle, far=far, partner=partner, across=across)
     return in_order(prices, other), parts
 

time: 60.1 us -> 56.6 us (0.942)
  starting transfers between devices: 27.5 us -> 25.4 us
  waiting for transfers between devices: 21.7 us -> 20.3 us
    ppermute x23, starting transfers between devices: 27.5 us -> 25.4 us  [swap(): return lax.ppermute(value, ('hours', 'region'), pairs)]
    ppermute x23, waiting for transfers between devices: 21.7 us -> 20.3 us  [swap(): return lax.ppermute(value, ('hours', 'region'), pairs)]
  transfers between devices with their start and end apart: 23 -> 23, of which waited for: 18 -> 16; matrix products, arithmetic and copies ran while one was open for 0% -> 0% of each run, Pallas kernels for 3% -> 3%
where the time goes in v11:
time: 56.6 us; the launch traced here: 56.4 us
  starting transfers between devices  25.4 us (45%)
  waiting for transfers between devices  20.3 us (36%)
  Pallas kernels  5.82 us (10%)
  local copies, waits for them, and re-layouts  3.5 us (6%)
  between operations  1.18 us (2%)
    ppermute x23, starting transfers between devices, swap(): return lax.ppermute(value, ('hours', 'region'), pairs)  25.4 us
    ppermute x23, waiting for transfers between devices, swap(): return lax.ppermute(value, ('hours', 'region'), pairs)  20.3 us
    pallas_call x6, Pallas kernels, call(): pl.pallas_call(functools.partial(kernel, names_in, names_out), out_shape=...  5.82 us
    unnamed x62, local copies, waits for them, and re-layouts  3.26 us
  transfers between devices with their start and end apart: 23, of which 16 were waited for; matrix products, arithmetic and copies ran while one was open for 0% of the time, Pallas kernels for 3%

profile of v11, /device:TPU:0, one launch (start us, length us, event | category | flops | bytes accessed | tf_op | source)
XLA Modules:
  0.0 56.4 jit_solution(9763136724759034294)
XLA Ops:
  0.6 0.0 copy-start.30
  0.7 0.6 %copy-done.30 = f32[1,64]{1,0:T(1,128)S(1)} copy-done((f32[1,64]{1,0:T(1,128)S(1)}, f32[1,64]{1,0:T(1,128)}, u32[]{:S(2)}) %copy-start.30) | copy-done | bytes 280
  1.3 0.0 copy-done.28
  1.3 0.9 %shard_map.166 = f32[8,128]{1,0:T(8,128)S(1)} custom-call(s32[2,64]{1,0:T(2,128)S(1)} %bitcast.97, f32[1,64]{1,0:T(1,128)S(1)} %copy-done.30, s32[1,2]{1,0:T(1,128)} %refs_2_.3), custom_call_target="tpu_custom_call" | custom-call | tf_op jit(solution)/shard_map/pallas_call | solution.py:401
  2.2 3.0 %collective-permute-start.31 = (f32[8,128]{1,0:T(8,128)S(1)}, f32[8,128]{1,0:T(8,128)S(1)}, u32[]{:S(2)}, u32[]{:S(2)}) collective-permute-start(f32[8,128]{1,0:T(8,128)S(1)} %shard_map.166), channel_id=1, source_target_pairs={{0,1},{1,0},{2,3},{3,2},{4,5},{5,4},{6,7},{7,6},{8,9},{9,8},{10,11... | collective-permute-start | bytes 12296 | tf_op jit(solution)/shard_map/ppermute | solution.py:422
  5.2 0.1 collective-permute-start.30
  5.3 0.6 %copy-done.19 = s32[2,256]{1,0:T(2,128)S(1)} copy-done((s32[2,256]{1,0:T(2,128)S(1)}, s32[2,256]{1,0:T(2,128)}, u32[]{:S(2)}) %copy-start.19) | copy-done | bytes 2072
  5.9 0.0 copy-done.17
  6.0 0.0 copy-done.16
  6.0 1.8 %shard_map.165 = (f32[18,64,128]{2,1,0:T(8,128)S(1)}, bf16[128,512]{1,0:T(8,128)(2,1)S(1)}, f32[64,512]{1,0:T(8,128)S(1)}, f32[64,256]{1,0:T(8,128)S(1)}, f32[17...) custom-call(f32[1024,128]{1,0:T(8,128)} %bitcast.67, f32[64,128]{1,0:T(8,128)} %refs_1_.2, ...), custom_call_target="tpu_custom_call" | custom-call | flops 1000000 | bytes 4000000 | tf_op jit(solution)/shard_map/pallas_call | solution.py:401
  7.8 1.6 %collective-permute-done.30 = f32[64,128]{1,0:T(8,128)S(1)} collective-permute-done((f32[64,128]{1,0:T(8,128)}, f32[64,128]{1,0:T(8,128)S(1)}, u32[]{:S(2)}, u32[]{:S(2)}) %collective-permute-start.30) | collective-permute-done | bytes 32800 | tf_op jit(solution)/shard_map/ppermute | solution.py:422
  9.4 0.4 shard_map.167
  9.7 0.1 collective-permute-start.32
  9.8 1.2 %collective-permute-done.32.refs_11_ = f32[56,128]{1,0:T(8,128)S(1)} collective-permute-done((f32[56,128]{1,0:T(8,128)S(1)}, f32[56,128]{1,0:T(8,128)S(1)}, u32[]{:S(2)}, u32[]{:S(2)}) %collective-permute-start.32) | collective-permute-done | bytes 28704 | tf_op jit(solution)/shard_map/ppermute | solution.py:422
  11.0 1.3 %collective-permute-start.35 = (f32[3,128]{1,0:T(4,128)S(1)}, f32[3,128]{1,0:T(4,128)S(1)}, u32[]{:S(2)}, u32[]{:S(2)}) collective-permute-start(f32[3,128]{1,0:T(4,128)S(1)} %slice.603), channel_id=1, source_target_pairs={{0,7},{1,6},{2,5},{3,4},{4,3},{5,2},{6,1},{7,0},{8,15},{9,14},{10,... | collective-permute-start | bytes 4616 | tf_op jit(solution)/shard_map/ppermute | solution.py:422
  12.3 0.5 collective-permute-start.33
  12.8 1.6 %collective-permute-start.34 = (f32[67,128]{1,0:T(8,128)S(1)}, f32[67,128]{1,0:T(8,128)S(1)}, u32[]{:S(2)}, u32[]{:S(2)}) collective-permute-start(f32[67,128]{1,0:T(8,128)S(1)} %pad_maximum_fusion.12), channel_id=1, source_target_pairs={{0,1},{1,0},{2,3},{3,2},{4,5},{5,4},{6,7},{7,6},{8,9},{9,8},{10,11... | collective-permute-start | bytes 102920 | tf_op jit(solution)/shard_map/ppermute | solution.py:422
  14.4 1.3 %collective-permute-done.33.refs_12_ = f32[56,128]{1,0:T(8,128)S(1)} collective-permute-done((f32[56,128]{1,0:T(8,128)S(1)}, f32[56,128]{1,0:T(8,128)S(1)}, u32[]{:S(2)}, u32[]{:S(2)}) %collective-permute-start.33) | collective-permute-done | bytes 28704 | tf_op jit(solution)/shard_map/ppermute | solution.py:422
  15.7 1.0 %collective-permute-done.34 = f32[67,128]{1,0:T(8,128)S(1)} collective-permute-done((f32[67,128]{1,0:T(8,128)S(1)}, f32[67,128]{1,0:T(8,128)S(1)}, u32[]{:S(2)}, u32[]{:S(2)}) %collective-permute-start.34) | collective-permute-done | bytes 34336 | tf_op jit(solution)/shard_map/ppermute | solution.py:422
  16.8 0.1 scatter-add.30.refs_7_
  16.8 2.7 %collective-permute-start.38 = (f32[56,128]{1,0:T(8,128)S(1)}, f32[56,128]{1,0:T(8,128)S(1)}, u32[]{:S(2)}, u32[]{:S(2)}) collective-permute-start(f32[56,128]{1,0:T(8,128)S(1)} %scatter-add.30.refs_7_), channel_id=1, source_target_pairs={{0,26},{1,27},{2,24},{3,25},{4,30},{5,31},{6,28},{7,29},{8,18},{9,... | collective-permute-start | bytes 86024 | tf_op jit(solution)/shard_map/ppermute | solution.py:422
  19.5 0.2 collective-permute-start.37
  19.7 1.2 %collective-permute-start.36 = (f32[56,128]{1,0:T(8,128)S(1)}, f32[56,128]{1,0:T(8,128)S(1)}, u32[]{:S(2)}, u32[]{:S(2)}) collective-permute-start(f32[56,128]{1,0:T(8,128)S(1)} %scatter-add.30.refs_7_), channel_id=1, source_target_pairs={{0,10},{1,11},{2,8},{3,9},{4,14},{5,15},{6,12},{7,13},{8,2},{9,3},... | collective-permute-start | bytes 86024 | tf_op jit(solution)/shard_map/ppermute | solution.py:422
  21.0 1.0 %collective-permute-done.38.refs_10_ = f32[56,128]{1,0:T(8,128)S(1)} collective-permute-done((f32[56,128]{1,0:T(8,128)S(1)}, f32[56,128]{1,0:T(8,128)S(1)}, u32[]{:S(2)}, u32[]{:S(2)}) %collective-permute-start.38) | collective-permute-done | bytes 28704 | tf_op jit(solution)/shard_map/ppermute | solution.py:422
  22.0 1.7 %collective-permute-done.37.refs_9_ = f32[56,128]{1,0:T(8,128)S(1)} collective-permute-done((f32[56,128]{1,0:T(8,128)S(1)}, f32[56,128]{1,0:T(8,128)S(1)}, u32[]{:S(2)}, u32[]{:S(2)}) %collective-permute-start.37) | collective-permute-done | bytes 28704 | tf_op jit(solution)/shard_map/ppermute | solution.py:422
  23.7 0.8 %shard_map.168 = (f32[17,64,128]{2,1,0:T(8,128)S(1)}, f32[17,64,128]{2,1,0:T(8,128)S(1)}, f32[64,512]{1,0:T(8,128)S(1)}, f32[72,128]{1,0:T(8,128)S(1)}, f32[64,2...) custom-call(f32[18,64,128]{2,1,0:T(8,128)S(1)} %get-tuple-element.246.refs_0_, ...), custom_call_target="tpu_custom_call" | custom-call | tf_op jit(solution)/shard_map/pallas_call | solution.py:401
  24.5 0.0 copy-start.8
  24.5 0.6 %copy-done.8 = f32[72,128]{1,0:T(8,128)} copy-done((f32[72,128]{1,0:T(8,128)}, f32[72,128]{1,0:T(8,128)S(1)}, u32[]{:S(2)}) %copy-start.8) | copy-done | bytes 36888
  25.2 1.2 %collective-permute-start.39 = (f32[24,128]{1,0:T(8,128)S(1)}, f32[24,128]{1,0:T(8,128)S(1)}, u32[]{:S(2)}, u32[]{:S(2)}) collective-permute-start(f32[24,128]{1,0:T(8,128)S(1)} %get-tuple-element.263), channel_id=1, source_target_pairs={{0,2},{1,3},{2,0},{3,1},{4,6},{5,7},{6,4},{7,5},{8,10},{9,11},{10,... | collective-permute-start | bytes 36872 | tf_op jit(solution)/shard_map/ppermute | solution.py:422
  26.3 0.8 %collective-permute-done.39.refs_13_ = f32[24,128]{1,0:T(8,128)S(1)} collective-permute-done((f32[24,128]{1,0:T(8,128)S(1)}, f32[24,128]{1,0:T(8,128)S(1)}, u32[]{:S(2)}, u32[]{:S(2)}) %collective-permute-start.39) | collective-permute-done | bytes 12320 | tf_op jit(solution)/shard_map/ppermute | solution.py:422
  27.2 2.5 %collective-permute-start.42 = (f32[3,128]{1,0:T(4,128)S(1)}, f32[3,128]{1,0:T(4,128)S(1)}, u32[]{:S(2)}, u32[]{:S(2)}) collective-permute-start(f32[3,128]{1,0:T(4,128)S(1)} %slice.615), channel_id=1, source_target_pairs={{0,7},{1,6},{2,5},{3,4},{4,3},{5,2},{6,1},{7,0},{8,15},{9,14},{10,... | collective-permute-start | bytes 4616 | tf_op jit(solution)/shard_map/ppermute | solution.py:422
  29.6 0.4 collective-permute-start.40
  30.0 0.6 %collective-permute-start.41 = (f32[67,128]{1,0:T(8,128)S(1)}, f32[67,128]{1,0:T(8,128)S(1)}, u32[]{:S(2)}, u32[]{:S(2)}) collective-permute-start(f32[67,128]{1,0:T(8,128)S(1)} %pad_maximum_fusion.13), channel_id=1, source_target_pairs={{0,1},{1,0},{2,3},{3,2},{4,5},{5,4},{6,7},{7,6},{8,9},{9,8},{10,11... | collective-permute-start | bytes 102920 | tf_op jit(solution)/shard_map/ppermute | solution.py:422
  30.6 2.2 %collective-permute-done.40.refs_14_ = f32[24,128]{1,0:T(8,128)S(1)} collective-permute-done((f32[24,128]{1,0:T(8,128)S(1)}, f32[24,128]{1,0:T(8,128)S(1)}, u32[]{:S(2)}, u32[]{:S(2)}) %collective-permute-start.40) | collective-permute-done | bytes 12320 | tf_op jit(solution)/shard_map/ppermute | solution.py:422
  32.9 1.2 %collective-permute-done.41 = f32[67,128]{1,0:T(8,128)S(1)} collective-permute-done((f32[67,128]{1,0:T(8,128)S(1)}, f32[67,128]{1,0:T(8,128)S(1)}, u32[]{:S(2)}, u32[]{:S(2)}) %collective-permute-start.41) | collective-permute-done | bytes 34336 | tf_op jit(solution)/shard_map/ppermute | solution.py:422
  34.0 0.1 scatter-add.31.refs_9_
  34.1 0.5 collective-permute-start.45
  34.6 0.9 %collective-permute-start.44 = (f32[24,128]{1,0:T(8,128)S(1)}, f32[24,128]{1,0:T(8,128)S(1)}, u32[]{:S(2)}, u32[]{:S(2)}) collective-permute-start(f32[24,128]{1,0:T(8,128)S(1)} %scatter-add.31.refs_9_), channel_id=1, source_target_pairs={{0,18},{1,19},{2,16},{3,17},{4,22},{5,23},{6,20},{7,21},{8,26},{9,... | collective-permute-start | bytes 36872 | tf_op jit(solution)/shard_map/ppermute | solution.py:422
  35.6 1.5 %collective-permute-start.43 = (f32[24,128]{1,0:T(8,128)S(1)}, f32[24,128]{1,0:T(8,128)S(1)}, u32[]{:S(2)}, u32[]{:S(2)}) collective-permute-start(f32[24,128]{1,0:T(8,128)S(1)} %scatter-add.31.refs_9_), channel_id=1, source_target_pairs={{0,10},{1,11},{2,8},{3,9},{4,14},{5,15},{6,12},{7,13},{8,2},{9,3},... | collective-permute-start | bytes 36872 | tf_op jit(solution)/shard_map/ppermute | solution.py:422
  37.1 2.0 %collective-permute-done.45.refs_12_ = f32[24,128]{1,0:T(8,128)S(1)} collective-permute-done((f32[24,128]{1,0:T(8,128)S(1)}, f32[24,128]{1,0:T(8,128)S(1)}, u32[]{:S(2)}, u32[]{:S(2)}) %collective-permute-start.45) | collective-permute-done | bytes 12320 | tf_op jit(solution)/shard_map/ppermute | solution.py:422
  39.1 0.7 %shard_map.169 = (f32[17,64,128]{2,1,0:T(8,128)S(1)}, f32[17,64,128]{2,1,0:T(8,128)S(1)}, f32[64,512]{1,0:T(8,128)S(1)}, f32[72,128]{1,0:T(8,128)S(1)}, f32[64,2...) custom-call(f32[18,64,128]{2,1,0:T(8,128)S(1)} %get-tuple-element.246.refs_0_, ...), custom_call_target="tpu_custom_call" | custom-call | tf_op jit(solution)/shard_map/pallas_call | solution.py:401
  39.9 0.9 %collective-permute-start.46 = (f32[24,128]{1,0:T(8,128)S(1)}, f32[24,128]{1,0:T(8,128)S(1)}, u32[]{:S(2)}, u32[]{:S(2)}) collective-permute-start(f32[24,128]{1,0:T(8,128)S(1)} %get-tuple-element.271), channel_id=1, source_target_pairs={{0,2},{1,3},{2,0},{3,1},{4,6},{5,7},{6,4},{7,5},{8,10},{9,11},{10,... | collective-permute-start | bytes 36872 | tf_op jit(solution)/shard_map/ppermute | solution.py:422
  40.8 0.8 %collective-permute-done.46.refs_13_ = f32[24,128]{1,0:T(8,128)S(1)} collective-permute-done((f32[24,128]{1,0:T(8,128)S(1)}, f32[24,128]{1,0:T(8,128)S(1)}, u32[]{:S(2)}, u32[]{:S(2)}) %collective-permute-start.46) | collective-permute-done | bytes 12320 | tf_op jit(solution)/shard_map/ppermute | solution.py:422
  41.7 1.5 %collective-permute-start.49 = (f32[3,128]{1,0:T(4,128)S(1)}, f32[3,128]{1,0:T(4,128)S(1)}, u32[]{:S(2)}, u32[]{:S(2)}) collective-permute-start(f32[3,128]{1,0:T(4,128)S(1)} %slice.627), channel_id=1, source_target_pairs={{0,7},{1,6},{2,5},{3,4},{4,3},{5,2},{6,1},{7,0},{8,15},{9,14},{10,... | collective-permute-start | bytes 4616 | tf_op jit(solution)/shard_map/ppermute | solution.py:422
  43.2 0.3 collective-permute-start.47
  43.5 1.5 %collective-permute-start.48 = (f32[67,128]{1,0:T(8,128)S(1)}, f32[67,128]{1,0:T(8,128)S(1)}, u32[]{:S(2)}, u32[]{:S(2)}) collective-permute-start(f32[67,128]{1,0:T(8,128)S(1)} %pad_maximum_fusion.14), channel_id=1, source_target_pairs={{0,1},{1,0},{2,3},{3,2},{4,5},{5,4},{6,7},{7,6},{8,9},{9,8},{10,11... | collective-permute-start | bytes 102920 | tf_op jit(solution)/shard_map/ppermute | solution.py:422
  45.0 1.3 %collective-permute-done.47.refs_14_ = f32[24,128]{1,0:T(8,128)S(1)} collective-permute-done((f32[24,128]{1,0:T(8,128)S(1)}, f32[24,128]{1,0:T(8,128)S(1)}, u32[]{:S(2)}, u32[]{:S(2)}) %collective-permute-start.47) | collective-permute-done | bytes 12320 | tf_op jit(solution)/shard_map/ppermute | solution.py:422
  46.4 1.0 %collective-permute-done.48 = f32[67,128]{1,0:T(8,128)S(1)} collective-permute-done((f32[67,128]{1,0:T(8,128)S(1)}, f32[67,128]{1,0:T(8,128)S(1)}, u32[]{:S(2)}, u32[]{:S(2)}) %collective-permute-start.48) | collective-permute-done | bytes 34336 | tf_op jit(solution)/shard_map/ppermute | solution.py:422
  47.5 0.1 scatter-add.34.refs_9_
  47.5 1.1 %collective-permute-start.52 = (f32[24,128]{1,0:T(8,128)S(1)}, f32[24,128]{1,0:T(8,128)S(1)}, u32[]{:S(2)}, u32[]{:S(2)}) collective-permute-start(f32[24,128]{1,0:T(8,128)S(1)} %scatter-add.34.refs_9_), channel_id=1, source_target_pairs={{0,26},{1,27},{2,24},{3,25},{4,30},{5,31},{6,28},{7,29},{8,18},{9,... | collective-permute-start | bytes 36872 | tf_op jit(solution)/shard_map/ppermute | solution.py:422
  48.6 1.9 %collective-permute-start.51 = (f32[24,128]{1,0:T(8,128)S(1)}, f32[24,128]{1,0:T(8,128)S(1)}, u32[]{:S(2)}, u32[]{:S(2)}) collective-permute-start(f32[24,128]{1,0:T(8,128)S(1)} %scatter-add.34.refs_9_), channel_id=1, source_target_pairs={{0,18},{1,19},{2,16},{3,17},{4,22},{5,23},{6,20},{7,21},{8,26},{9,... | collective-permute-start | bytes 36872 | tf_op jit(solution)/shard_map/ppermute | solution.py:422
  50.6 1.9 %collective-permute-done.52.refs_12_ = f32[24,128]{1,0:T(8,128)S(1)} collective-permute-done((f32[24,128]{1,0:T(8,128)S(1)}, f32[24,128]{1,0:T(8,128)S(1)}, u32[]{:S(2)}, u32[]{:S(2)}) %collective-permute-start.52) | collective-permute-done | bytes 12320 | tf_op jit(solution)/shard_map/ppermute | solution.py:422
  52.5 0.1 collective-permute-done.51.refs_11_
  52.7 1.0 %collective-permute-done.50.refs_10_ = f32[24,128]{1,0:T(8,128)S(1)} collective-permute-done((f32[24,128]{1,0:T(8,128)S(1)}, f32[24,128]{1,0:T(8,128)S(1)}, u32[]{:S(2)}, u32[]{:S(2)}) %collective-permute-start.50) | collective-permute-done | bytes 12320 | tf_op jit(solution)/shard_map/ppermute | solution.py:422
  53.7 0.0 copy-start.23
  53.7 0.0 copy-start.25
  53.7 0.0 copy-start.32
  53.7 0.0 copy-start.34
  53.8 1.3 %shard_map.170 = (f32[1024,128]{1,0:T(8,128)}, f32[1,128]{1,0:T(1,128)S(1)}, f32[64,128]{1,0:T(8,128)S(1)}, f32[64,256]{1,0:T(8,128)}, f32[1,128]{1,0:T(1,128)S(1)}) custom-call(f32[18,64,128]{2,1,0:T(8,128)S(1)} %get-tuple-element.246.refs_0_, bf16[128,512]{1,0:T(8,128)(2,1)S(1)} %get-tuple-element.247.refs_1_, f32[64,512]{1,0:T(8,128)S(1)} %get-tuple-element.265.refs_2_, ...), custom_call_target="tpu_custom_call" | custom-call | tf_op jit(solution)/shard_map/pallas_call | solution.py:401
  55.1 0.0 copy-start.31
  55.2 0.5 copy-done.18
  55.7 0.0 copy-done.21
  55.8 0.5 copy-done.36
  56.3 0.1 copy-done.35
  (97 shorter events, 0.4 us)
Async XLA Ops:
  0.6 0.7 %copy-start.30 = (f32[1,64]{1,0:T(1,128)S(1)}, f32[1,64]{1,0:T(1,128)}, u32[]{:S(2)}) copy-start(f32[1,64]{1,0:T(1,128)} %refs_1_.3) | copy-start | bytes 772
  0.6 0.7 %copy-start.28 = (s32[2,1,64]{2,1,0:T(1,128)S(1)}, s32[2,1,64]{2,1,0:T(1,128)}, u32[]{:S(2)}) copy-start(s32[2,1,64]{2,1,0:T(1,128)} %param.43) | copy-start | bytes 1540
  1.3 4.0 %copy-start.20 = (f32[256]{0:T(256)S(1)}, f32[256]{0:T(256)}, u32[]{:S(2)}) copy-start(f32[256]{0:T(256)} %param.42) | copy-start | bytes 3076
  1.3 4.0 %copy-start.22 = (s32[256]{0:T(256)S(1)}, s32[256]{0:T(256)}, u32[]{:S(2)}) copy-start(s32[256]{0:T(256)} %param.46) | copy-start | bytes 3076
  1.3 4.0 %copy-start.24 = (f32[256]{0:T(256)S(1)}, f32[256]{0:T(256)}, u32[]{:S(2)}) copy-start(f32[256]{0:T(256)} %param.48) | copy-start | bytes 3076
  1.3 4.0 %copy-start.26 = (f32[256]{0:T(256)S(1)}, f32[256]{0:T(256)}, u32[]{:S(2)}) copy-start(f32[256]{0:T(256)} %param.47) | copy-start | bytes 3076
  2.2 5.5 %collective-permute-start.31 = (f32[8,128]{1,0:T(8,128)S(1)}, f32[8,128]{1,0:T(8,128)S(1)}, u32[]{:S(2)}, u32[]{:S(2)}) collective-permute-start(f32[8,128]{1,0:T(8,128)S(1)} %shard_map.166), channel_id=1, source_target_pairs={{0,1},{1,0},{2,3},{3,2},{4,5},{5,4},{6,7},{7,6},{8,9},{9,8},{10,11... | collective-permute-start | bytes 12296 | tf_op jit(solution)/shard_map/ppermute | solution.py:422
  5.2 4.1 %collective-permute-start.30 = (f32[64,128]{1,0:T(8,128)}, f32[64,128]{1,0:T(8,128)S(1)}, u32[]{:S(2)}, u32[]{:S(2)}) collective-permute-start(f32[64,128]{1,0:T(8,128)} %refs_1_.2), channel_id=1, source_target_pairs={{0,1},{1,0},{2,3},{3,2},{4,5},{5,4},{6,7},{7,6},{8,9},{9,8},{10,11... | collective-permute-start | bytes 98312 | tf_op jit(solution)/shard_map/ppermute | solution.py:422
  5.3 0.7 %copy-start.19 = (s32[2,256]{1,0:T(2,128)S(1)}, s32[2,256]{1,0:T(2,128)}, u32[]{:S(2)}) copy-start(s32[2,256]{1,0:T(2,128)} %refs_6_.1) | copy-start | bytes 6148
  5.3 0.7 %copy-start.17 = (s32[1,2048]{1,0:T(1,128)S(1)}, s32[1,2048]{1,0:T(1,128)}, u32[]{:S(2)}) copy-start(s32[1,2048]{1,0:T(1,128)} %param.40) | copy-start | bytes 24580
  5.3 0.7 %copy-start.16 = (f32[16,128]{1,0:T(8,128)S(1)}, f32[16,128]{1,0:T(8,128)}, u32[]{:S(2)}) copy-start(f32[16,128]{1,0:T(8,128)} %refs_3_.1) | copy-start | bytes 24580
  5.3 0.7 %copy-start.33 = (f32[1,128]{1,0:T(1,128)S(1)}, f32[1,128]{1,0:T(1,128)}, u32[]{:S(2)}) copy-start(f32[1,128]{1,0:T(1,128)} %refs_4_.1) | copy-start | bytes 1540
  6.0 3.3 %copy-start.13 = (f32[64,128]{1,0:T(8,128)S(1)}, f32[64,128]{1,0:T(8,128)}, u32[]{:S(2)}) copy-start(f32[64,128]{1,0:T(8,128)} %refs_1_.2) | copy-start | bytes 98308
  9.7 1.3 %collective-permute-start.32 = (f32[56,128]{1,0:T(8,128)S(1)}, f32[56,128]{1,0:T(8,128)S(1)}, u32[]{:S(2)}, u32[]{:S(2)}) collective-permute-start(f32[56,128]{1,0:T(8,128)S(1)} %get-tuple-element.255), channel_id=1, source_target_pairs={{0,2},{1,3},{2,0},{3,1},{4,6},{5,7},{6,4},{7,5},{8,10},{9,11},{10,... | collective-permute-start | bytes 86024 | tf_op jit(solution)/shard_map/ppermute | solution.py:422
  11.0 4.7 %collective-permute-start.35 = (f32[3,128]{1,0:T(4,128)S(1)}, f32[3,128]{1,0:T(4,128)S(1)}, u32[]{:S(2)}, u32[]{:S(2)}) collective-permute-start(f32[3,128]{1,0:T(4,128)S(1)} %slice.603), channel_id=1, source_target_pairs={{0,7},{1,6},{2,5},{3,4},{4,3},{5,2},{6,1},{7,0},{8,15},{9,14},{10,... | collective-permute-start | bytes 4616 | tf_op jit(solution)/shard_map/ppermute | solution.py:422
  12.3 3.4 %collective-permute-start.33 = (f32[56,128]{1,0:T(8,128)S(1)}, f32[56,128]{1,0:T(8,128)S(1)}, u32[]{:S(2)}, u32[]{:S(2)}) collective-permute-start(f32[56,128]{1,0:T(8,128)S(1)} %pad_maximum_fusion.15), channel_id=1, source_target_pairs={{0,6},{1,7},{2,4},{3,5},{4,2},{5,3},{6,0},{7,1},{8,14},{9,15},{10,... | collective-permute-start | bytes 86024 | tf_op jit(solution)/shard_map/ppermute | solution.py:422
  12.8 4.0 %collective-permute-start.34 = (f32[67,128]{1,0:T(8,128)S(1)}, f32[67,128]{1,0:T(8,128)S(1)}, u32[]{:S(2)}, u32[]{:S(2)}) collective-permute-start(f32[67,128]{1,0:T(8,128)S(1)} %pad_maximum_fusion.12), channel_id=1, source_target_pairs={{0,1},{1,0},{2,3},{3,2},{4,5},{5,4},{6,7},{7,6},{8,9},{9,8},{10,11... | collective-permute-start | bytes 102920 | tf_op jit(solution)/shard_map/ppermute | solution.py:422
  16.8 5.2 %collective-permute-start.38 = (f32[56,128]{1,0:T(8,128)S(1)}, f32[56,128]{1,0:T(8,128)S(1)}, u32[]{:S(2)}, u32[]{:S(2)}) collective-permute-start(f32[56,128]{1,0:T(8,128)S(1)} %scatter-add.30.refs_7_), channel_id=1, source_target_pairs={{0,26},{1,27},{2,24},{3,25},{4,30},{5,31},{6,28},{7,29},{8,18},{9,... | collective-permute-start | bytes 86024 | tf_op jit(solution)/shard_map/ppermute | solution.py:422
  19.5 4.2 %collective-permute-start.37 = (f32[56,128]{1,0:T(8,128)S(1)}, f32[56,128]{1,0:T(8,128)S(1)}, u32[]{:S(2)}, u32[]{:S(2)}) collective-permute-start(f32[56,128]{1,0:T(8,128)S(1)} %scatter-add.30.refs_7_), channel_id=1, source_target_pairs={{0,18},{1,19},{2,16},{3,17},{4,22},{5,23},{6,20},{7,21},{8,26},{9,... | collective-permute-start | bytes 86024 | tf_op jit(solution)/shard_map/ppermute | solution.py:422
  19.7 4.0 %collective-permute-start.36 = (f32[56,128]{1,0:T(8,128)S(1)}, f32[56,128]{1,0:T(8,128)S(1)}, u32[]{:S(2)}, u32[]{:S(2)}) collective-permute-start(f32[56,128]{1,0:T(8,128)S(1)} %scatter-add.30.refs_7_), channel_id=1, source_target_pairs={{0,10},{1,11},{2,8},{3,9},{4,14},{5,15},{6,12},{7,13},{8,2},{9,3},... | collective-permute-start | bytes 86024 | tf_op jit(solution)/shard_map/ppermute | solution.py:422
  24.5 0.6 %copy-start.8 = (f32[72,128]{1,0:T(8,128)}, f32[72,128]{1,0:T(8,128)S(1)}, u32[]{:S(2)}) copy-start(f32[72,128]{1,0:T(8,128)S(1)} %get-tuple-element.260.refs_6_) | copy-start | bytes 110596
  25.2 4.9 %copy-start = (f32[64,256]{1,0:T(8,128)}, f32[64,256]{1,0:T(8,128)S(1)}, u32[]{:S(2)}) copy-start(f32[64,256]{1,0:T(8,128)S(1)} %get-tuple-element.262.refs_8_) | copy-start | bytes 196612
  25.2 2.0 %collective-permute-start.39 = (f32[24,128]{1,0:T(8,128)S(1)}, f32[24,128]{1,0:T(8,128)S(1)}, u32[]{:S(2)}, u32[]{:S(2)}) collective-permute-start(f32[24,128]{1,0:T(8,128)S(1)} %get-tuple-element.263), channel_id=1, source_target_pairs={{0,2},{1,3},{2,0},{3,1},{4,6},{5,7},{6,4},{7,5},{8,10},{9,11},{10,... | collective-permute-start | bytes 36872 | tf_op jit(solution)/shard_map/ppermute | solution.py:422
  27.2 5.7 %collective-permute-start.42 = (f32[3,128]{1,0:T(4,128)S(1)}, f32[3,128]{1,0:T(4,128)S(1)}, u32[]{:S(2)}, u32[]{:S(2)}) collective-permute-start(f32[3,128]{1,0:T(4,128)S(1)} %slice.615), channel_id=1, source_target_pairs={{0,7},{1,6},{2,5},{3,4},{4,3},{5,2},{6,1},{7,0},{8,15},{9,14},{10,... | collective-permute-start | bytes 4616 | tf_op jit(solution)/shard_map/ppermute | solution.py:422
  29.6 3.2 %collective-permute-start.40 = (f32[24,128]{1,0:T(8,128)S(1)}, f32[24,128]{1,0:T(8,128)S(1)}, u32[]{:S(2)}, u32[]{:S(2)}) collective-permute-start(f32[24,128]{1,0:T(8,128)S(1)} %pad_maximum_fusion.17), channel_id=1, source_target_pairs={{0,6},{1,7},{2,4},{3,5},{4,2},{5,3},{6,0},{7,1},{8,14},{9,15},{10,... | collective-permute-start | bytes 36872 | tf_op jit(solution)/shard_map/ppermute | solution.py:422
  30.0 4.0 %collective-permute-start.41 = (f32[67,128]{1,0:T(8,128)S(1)}, f32[67,128]{1,0:T(8,128)S(1)}, u32[]{:S(2)}, u32[]{:S(2)}) collective-permute-start(f32[67,128]{1,0:T(8,128)S(1)} %pad_maximum_fusion.13), channel_id=1, source_target_pairs={{0,1},{1,0},{2,3},{3,2},{4,5},{5,4},{6,7},{7,6},{8,9},{9,8},{10,11... | collective-permute-start | bytes 102920 | tf_op jit(solution)/shard_map/ppermute | solution.py:422
  34.1 5.0 %collective-permute-start.45 = (f32[24,128]{1,0:T(8,128)S(1)}, f32[24,128]{1,0:T(8,128)S(1)}, u32[]{:S(2)}, u32[]{:S(2)}) collective-permute-start(f32[24,128]{1,0:T(8,128)S(1)} %scatter-add.31.refs_9_), channel_id=1, source_target_pairs={{0,26},{1,27},{2,24},{3,25},{4,30},{5,31},{6,28},{7,29},{8,18},{9,... | collective-permute-start | bytes 36872 | tf_op jit(solution)/shard_map/ppermute | solution.py:422
  34.6 4.5 %collective-permute-start.44 = (f32[24,128]{1,0:T(8,128)S(1)}, f32[24,128]{1,0:T(8,128)S(1)}, u32[]{:S(2)}, u32[]{:S(2)}) collective-permute-start(f32[24,128]{1,0:T(8,128)S(1)} %scatter-add.31.refs_9_), channel_id=1, source_target_pairs={{0,18},{1,19},{2,16},{3,17},{4,22},{5,23},{6,20},{7,21},{8,26},{9,... | collective-permute-start | bytes 36872 | tf_op jit(solution)/shard_map/ppermute | solution.py:422
  35.6 3.5 %collective-permute-start.43 = (f32[24,128]{1,0:T(8,128)S(1)}, f32[24,128]{1,0:T(8,128)S(1)}, u32[]{:S(2)}, u32[]{:S(2)}) collective-permute-start(f32[24,128]{1,0:T(8,128)S(1)} %scatter-add.31.refs_9_), channel_id=1, source_target_pairs={{0,10},{1,11},{2,8},{3,9},{4,14},{5,15},{6,12},{7,13},{8,2},{9,3},... | collective-permute-start | bytes 36872 | tf_op jit(solution)/shard_map/ppermute | solution.py:422
  37.1 2.0 %copy-start.1 = (f32[64,256]{1,0:T(8,128)S(1)}, f32[64,256]{1,0:T(8,128)}, u32[]{:S(2)}) copy-start(f32[64,256]{1,0:T(8,128)} %copy-done) | copy-start | bytes 196612
  37.1 2.0 %copy-start.9 = (f32[72,128]{1,0:T(8,128)S(1)}, f32[72,128]{1,0:T(8,128)}, u32[]{:S(2)}) copy-start(f32[72,128]{1,0:T(8,128)} %copy-done.8) | copy-start | bytes 110596
  39.9 3.3 %copy-start.6 = (f32[72,128]{1,0:T(8,128)}, f32[72,128]{1,0:T(8,128)S(1)}, u32[]{:S(2)}) copy-start(f32[72,128]{1,0:T(8,128)S(1)} %get-tuple-element.268.refs_6_) | copy-start | bytes 110596
  39.9 1.8 %collective-permute-start.46 = (f32[24,128]{1,0:T(8,128)S(1)}, f32[24,128]{1,0:T(8,128)S(1)}, u32[]{:S(2)}, u32[]{:S(2)}) collective-permute-start(f32[24,128]{1,0:T(8,128)S(1)} %get-tuple-element.271), channel_id=1, source_target_pairs={{0,2},{1,3},{2,0},{3,1},{4,6},{5,7},{6,4},{7,5},{8,10},{9,11},{10,... | collective-permute-start | bytes 36872 | tf_op jit(solution)/shard_map/ppermute | solution.py:422
  41.7 4.8 %collective-permute-start.49 = (f32[3,128]{1,0:T(4,128)S(1)}, f32[3,128]{1,0:T(4,128)S(1)}, u32[]{:S(2)}, u32[]{:S(2)}) collective-permute-start(f32[3,128]{1,0:T(4,128)S(1)} %slice.627), channel_id=1, source_target_pairs={{0,7},{1,6},{2,5},{3,4},{4,3},{5,2},{6,1},{7,0},{8,15},{9,14},{10,... | collective-permute-start | bytes 4616 | tf_op jit(solution)/shard_map/ppermute | solution.py:422
  43.2 3.2 %collective-permute-start.47 = (f32[24,128]{1,0:T(8,128)S(1)}, f32[24,128]{1,0:T(8,128)S(1)}, u32[]{:S(2)}, u32[]{:S(2)}) collective-permute-start(f32[24,128]{1,0:T(8,128)S(1)} %pad_maximum_fusion.19), channel_id=1, source_target_pairs={{0,6},{1,7},{2,4},{3,5},{4,2},{5,3},{6,0},{7,1},{8,14},{9,15},{10,... | collective-permute-start | bytes 36872 | tf_op jit(solution)/shard_map/ppermute | solution.py:422
  43.5 4.0 %collective-permute-start.48 = (f32[67,128]{1,0:T(8,128)S(1)}, f32[67,128]{1,0:T(8,128)S(1)}, u32[]{:S(2)}, u32[]{:S(2)}) collective-permute-start(f32[67,128]{1,0:T(8,128)S(1)} %pad_maximum_fusion.14), channel_id=1, source_target_pairs={{0,1},{1,0},{2,3},{3,2},{4,5},{5,4},{6,7},{7,6},{8,9},{9,8},{10,11... | collective-permute-start | bytes 102920 | tf_op jit(solution)/shard_map/ppermute | solution.py:422
  47.5 5.0 %collective-permute-start.52 = (f32[24,128]{1,0:T(8,128)S(1)}, f32[24,128]{1,0:T(8,128)S(1)}, u32[]{:S(2)}, u32[]{:S(2)}) collective-permute-start(f32[24,128]{1,0:T(8,128)S(1)} %scatter-add.34.refs_9_), channel_id=1, source_target_pairs={{0,26},{1,27},{2,24},{3,25},{4,30},{5,31},{6,28},{7,29},{8,18},{9,... | collective-permute-start | bytes 36872 | tf_op jit(solution)/shard_map/ppermute | solution.py:422
  48.6 4.0 %collective-permute-start.51 = (f32[24,128]{1,0:T(8,128)S(1)}, f32[24,128]{1,0:T(8,128)S(1)}, u32[]{:S(2)}, u32[]{:S(2)}) collective-permute-start(f32[24,128]{1,0:T(8,128)S(1)} %scatter-add.34.refs_9_), channel_id=1, source_target_pairs={{0,18},{1,19},{2,16},{3,17},{4,22},{5,23},{6,20},{7,21},{8,26},{9,... | collective-permute-start | bytes 36872 | tf_op jit(solution)/shard_map/ppermute | solution.py:422
  50.5 3.1 %collective-permute-start.50 = (f32[24,128]{1,0:T(8,128)S(1)}, f32[24,128]{1,0:T(8,128)S(1)}, u32[]{:S(2)}, u32[]{:S(2)}) collective-permute-start(f32[24,128]{1,0:T(8,128)S(1)} %scatter-add.34.refs_9_), channel_id=1, source_target_pairs={{0,10},{1,11},{2,8},{3,9},{4,14},{5,15},{6,12},{7,13},{8,2},{9,3},... | collective-permute-start | bytes 36872 | tf_op jit(solution)/shard_map/ppermute | solution.py:422
  50.6 3.1 %copy-start.7 = (f32[72,128]{1,0:T(8,128)S(1)}, f32[72,128]{1,0:T(8,128)}, u32[]{:S(2)}) copy-start(f32[72,128]{1,0:T(8,128)} %copy-done.6) | copy-start | bytes 110596
  53.7 1.4 %copy-start.12 = (f32[64,16,128]{2,1,0:T(8,128)S(1)}, f32[64,16,128]{2,1,0:T(8,128)}, u32[]{:S(2)}) copy-start(f32[64,16,128]{2,1,0:T(8,128)} %param.36) | copy-start | bytes 1572868
  53.7 1.4 %copy-start.14 = (f32[64,128]{1,0:T(8,128)S(1)}, f32[64,128]{1,0:T(8,128)}, u32[]{:S(2)}) copy-start(f32[64,128]{1,0:T(8,128)} %refs_1_.2) | copy-start | bytes 98308
  53.7 1.4 %copy-start.15 = (f32[64,128]{1,0:T(8,128)S(1)}, f32[64,128]{1,0:T(8,128)}, u32[]{:S(2)}) copy-start(f32[64,128]{1,0:T(8,128)} %refs_2_.2) | copy-start | bytes 98308
  53.7 1.5 %copy-start.23 = (s32[256]{0:T(256)S(1)}, s32[256]{0:T(256)}, u32[]{:S(2)}) copy-start(s32[256]{0:T(256)} %param.46) | copy-start | bytes 3076
  53.7 1.5 %copy-start.25 = (f32[256]{0:T(256)S(1)}, f32[256]{0:T(256)}, u32[]{:S(2)}) copy-start(f32[256]{0:T(256)} %param.48) | copy-start | bytes 3076
  53.7 1.4 %copy-start.27 = (f32[256]{0:T(256)S(1)}, f32[256]{0:T(256)}, u32[]{:S(2)}) copy-start(f32[256]{0:T(256)} %param.47) | copy-start | bytes 3076
  53.7 1.4 %copy-start.29 = (s32[2,1,64]{2,1,0:T(1,128)S(1)}, s32[2,1,64]{2,1,0:T(1,128)}, u32[]{:S(2)}) copy-start(s32[2,1,64]{2,1,0:T(1,128)} %param.43) | copy-start | bytes 1540
  53.7 1.4 %copy-start.32 = (s32[1,2]{1,0:T(1,128)S(1)}, s32[1,2]{1,0:T(1,128)}, u32[]{:S(2)}) copy-start(s32[1,2]{1,0:T(1,128)} %refs_2_.3) | copy-start | bytes 28
  53.7 1.4 %copy-start.34 = (f32[1,128]{1,0:T(1,128)S(1)}, f32[1,128]{1,0:T(1,128)}, u32[]{:S(2)}) copy-start(f32[1,128]{1,0:T(1,128)} %refs_4_.1) | copy-start | bytes 1540
  55.0 0.7 %copy-start.18 = (s32[1,2048]{1,0:T(1,128)S(1)}, s32[1,2048]{1,0:T(1,128)}, u32[]{:S(2)}) copy-start(s32[1,2048]{1,0:T(1,128)} %param.40) | copy-start | bytes 24580
  55.1 0.7 %copy-start.21 = (f32[256]{0:T(256)S(1)}, f32[256]{0:T(256)}, u32[]{:S(2)}) copy-start(f32[256]{0:T(256)} %param.42) | copy-start | bytes 3076
  55.1 0.7 %copy-start.31 = (f32[1,64]{1,0:T(1,128)S(1)}, f32[1,64]{1,0:T(1,128)}, u32[]{:S(2)}) copy-start(f32[1,64]{1,0:T(1,128)} %refs_1_.3) | copy-start | bytes 772
  55.8 0.5 copy-start.36
  55.8 0.6 %copy-start.35 = (f32[64,128]{1,0:T(8,128)}, f32[64,128]{1,0:T(8,128)S(1)}, u32[]{:S(2)}) copy-start(f32[64,128]{1,0:T(8,128)S(1)} %get-tuple-element.279) | copy-start | bytes 98308

commit v12 on v11

--- a/solution.py
+++ b/solution.py
@@ -99,12 +99,22 @@
     )
 
 
-def slots_kernel(sizes, ends_ref, limit_ref, pairs_ref, info_ref):
+def first_kernel(sizes, sources, block_ref, ends_ref, limit_ref, pairs_ref, sems):
+    rows = sizes.rows
+    targets = (block_ref.at[pl.ds(0, rows)], ends_ref, limit_ref, pairs_ref)
+    copies = [
+        pltpu.make_async_copy(source, target, sems.at[i])
+        for i, (source, target) in enumerate(zip(sources, targets))
+    ]
+    for copy in copies:
+        copy.start()
     nodes, slots, regions = sizes.nodes, sizes.slots, sizes.regions
     own = lax.axis_index("region")
     width = slots // regions
     slot = lax.broadcasted_iota(jnp.int32, (1, slots), 1)
     pair = slot // width
+    for copy in copies[1:]:
+        copy.wait()
     in_use = jnp.zeros((1, slots), jnp.int32)
     for target in range(regions):
         in_use = jnp.where(pair == target, pairs_ref[0:1, target : target + 1], in_use)
@@ -118,12 +128,18 @@
     rest = jnp.zeros((13, slots), jnp.float32)
     info = dot3(jnp.concatenate([start, end, bound, rest], axis=0), place, False)
     for chunk in range(regions * slots // LANES):
-        info_ref[8 * chunk : 8 * chunk + 8, :] = info[:8, chunk * LANES : (chunk + 1) * LANES]
+        block_ref[rows + 8 * chunk : rows + 8 * chunk + 8, :] = info[
+            :8, chunk * LANES : (chunk + 1) * LANES
+        ]
+    copies[0].wait()
 
 
 def start_kernel(sizes, names_in, names_out, *refs):
     given = Bag(**dict(zip(names_in, refs[: len(names_in)])))
-    gives = Bag(**dict(zip(names_out, refs[len(names_in) :])))
+    gives = Bag(**dict(zip(names_out, refs[len(names_in) : -2])))
+    availability, sem = refs[-2:]
+    copy = pltpu.make_async_copy(given.availability, availability, sem)
+    copy.start()
     rows, techs, nodes, lines = sizes.rows, sizes.techs, sizes.nodes, sizes.lines
     at = places(sizes)
     fixed = gives.available.at[techs + 1]
@@ -148,12 +164,13 @@
     dual_row = fold_lanes(row_sum(store_new * store_new))
     balance = dot3(2.0 * flows, maps, True) - given.demand[...]
     gen_cost = given.gen_cost[...]
+    copy.wait()
     acc = jnp.zeros((rows, nodes), jnp.float32)
     weights = jnp.zeros((techs, nodes), jnp.float32)
     for hour in range(rows):
-        weights = weights + given.availability[hour * techs : (hour + 1) * techs, :]
+        weights = weights + availability[hour * techs : (hour + 1) * techs, :]
     for tech in range(techs):
-        avail = given.availability[pl.ds(tech, rows, stride=techs), :]
+        avail = availability[pl.ds(tech, rows, stride=techs), :]
         gives.available[tech] = avail
         dispatch = jnp.maximum(-0.5 * (gen_cost[tech : tech + 1] + prices), 0.0)
         gives.dispatch[tech] = dispatch
@@ -181,7 +198,7 @@
 def close_kernel(
     sizes,
     gathered,
-    info_ref,
+    local_ref,
     balance_ref,
     sums_in_ref,
     maps_ref,
@@ -194,10 +211,10 @@
     own = lax.axis_index("region")
     chunks = []
     for chunk in range(regions * slots // LANES):
-        at = slice(8 * chunk, 8 * chunk + 8)
-        part = info_ref[0, at, :]
+        at = slice(rows + 8 * chunk, rows + 8 * chunk + 8)
+        part = gathered[0, at, :]
         for region in range(1, regions):
-            part = part + info_ref[region, at, :]
+            part = part + gathered[region, at, :]
         chunks.append(part)
     info = jnp.concatenate(chunks, axis=1) if len(chunks) > 1 else chunks[0]
     maps_ref[...] = incidence(
@@ -206,8 +223,10 @@
     limits = info[2:3]
     prices_all = jnp.concatenate([gathered[region, :rows, :] for region in range(regions)], axis=1)
     flows = jnp.clip(-0.5 * dot3(prices_all, maps_ref[...], False), -limits, limits)
-    flows_ref[:rows, :] = flows
-    flows_ref[rows : rows + 1, :] = limits
+    local = local_ref.shape[1]
+    flows_ref[:rows, :local] = local_ref[...]
+    flows_ref[:rows, local:] = flows
+    flows_ref[rows : rows + 1, local:] = limits
     maps_own = maps_ref[pl.ds(pl.multiple_of(own * nodes, nodes), nodes), :]
     balance = balance_ref[...] + dot3(2.0 * flows, maps_own, True)
     step_up = (1.0 / (techs + 8.0)) * balance
@@ -306,26 +325,21 @@
 
     primal_row = jnp.zeros((1, LANES), jnp.float32)
     bars = []
-    local_out = None if last else gives.flows_local
-    cross_out = None if last else gives.flows_cross
-    local_limits = read_lanes(fixed, at.limits, lines + units)
-    cross_limits = given.flows_cross[rows : rows + 1, :]
-    for flows, out, limits, slope, low, high in (
-        (given.flows_local, local_out, local_limits, slope_local, 0, lines),
-        (given.flows_local, local_out, local_limits, slope_local, lines, lines + units),
-        (given.flows_cross, cross_out, cross_limits, slope_cross, 0, regions * slots),
+    local, total_flows = lines + units, lines + units + regions * slots
+    local_limits = read_lanes(fixed, at.limits, local)
+    cross_limits = given.flows[rows : rows + 1, local:]
+    for bound, slope, low, high in (
+        (local_limits[:, :lines], slope_local[:, :lines], 0, lines),
+        (local_limits[:, lines:], slope_local[:, lines:] + store_duals, lines, local),
+        (cross_limits, slope_cross, local, total_flows),
     ):
-        slope = slope[:, low:high]
-        if low:
-            slope = slope + store_duals
-        bound = limits[:, low:high]
-        old = flows[:rows, low:high]
+        old = given.flows[:rows, low:high]
         new = jnp.clip(old - primal_step * slope, -bound, bound)
         bars.append(2.0 * new - old)
         if not last:
-            out[:rows, low:high] = new
+            gives.flows[:rows, low:high] = new
             change = row_sum((new - old) ** 2)
-            if out is cross_out:
+            if low == local:
                 slot = lax.broadcasted_iota(jnp.int32, change.shape, 1)
                 change = jnp.where(slot // slots == own, change, 0.0)
             primal_row = primal_row + fold_lanes(change)
@@ -369,7 +383,7 @@
         gives.negative[...] = negative
         return
     gives.prices[...] = prices + step_up
-    gives.flows_cross[rows : rows + 1, :] = cross_limits
+    gives.flows[rows : rows + 1, local:] = cross_limits
     gives.cap_duals[techs, :techs, :] = col_weight
     gives.cap_duals[techs, techs : 2 * techs, :] = cost
     small_new = gives.dispatch.at[techs]
@@ -396,18 +410,19 @@
     write_halo(sizes, gives.sums, store_new)
 
 
-def call(kernel, given, outs, flops=0, smem=()):
+def call(kernel, given, outs, flops=0, left=(), scratch=(), limit=VMEM_BYTES):
     names_in, names_out = tuple(vars(given)), tuple(vars(outs))
     values = pl.pallas_call(
         functools.partial(kernel, names_in, names_out),
         out_shape=tuple(vars(outs).values()),
         in_specs=[
-            pl.BlockSpec(memory_space=pltpu.SMEM if i in smem else pltpu.VMEM)
+            pl.BlockSpec(memory_space=pl.ANY if i in left else pltpu.VMEM)
             for i in range(len(names_in))
         ],
         out_specs=[pl.BlockSpec(memory_space=pltpu.VMEM)] * len(names_out),
+        scratch_shapes=scratch,
         cost_estimate=pl.CostEstimate(flops=flops, bytes_accessed=4 * flops, transcendentals=0),
-        compiler_params=pltpu.CompilerParams(vmem_limit_bytes=VMEM_BYTES),
+        compiler_params=pltpu.CompilerParams(vmem_limit_bytes=limit),
     )(*vars(given).values())
     return Bag(**dict(zip(names_out, values)))
 
@@ -478,23 +493,69 @@
     return jax.ShapeDtypeStruct(dims, dtype)
 
 
-def corrected(sizes, state, prices, sums, parts):
-    techs = sizes.techs
-    totals = total_of(parts)
-    first = sums_rows(sizes)
-    col_weight, cost = totals[first : first + techs], totals[first + techs :]
+def restarted(sizes, kept, price_start):
+    rows, techs, nodes, lines = sizes.rows, sizes.techs, sizes.nodes, sizes.lines
+    local, cross = lines + sizes.units, sizes.regions * sizes.slots
+    at, own = places(sizes), lax.axis_index("region")
+    first_hour = lax.axis_index("hours") == 0
+    fixed, available = kept.available[techs + 1], kept.available[:techs]
+    col_weight, cost = kept.cap_duals[techs, :techs], kept.cap_duals[techs, techs : 2 * techs]
+    local_limits = fixed[at.limits : at.energy].reshape(1, local)
+    cross_limits = kept.flows[rows : rows + 1, local:]
+    maps_local = kept.maps_local.astype(jnp.float32)
+    maps_cross = kept.maps_cross.astype(jnp.float32)
+    maps_own = lax.dynamic_slice_in_dim(maps_cross, own * nodes, nodes)
+    prices_all = jnp.concatenate(list(both_regions(price_start)), axis=1)
+    highest = lax.Precision.HIGHEST
+
     capacity = jnp.maximum(-cost / col_weight, 0.0)
-    taken = state.dispatch[:techs]
-    rows_of = 2.0 * taken - state.available[:techs] * (2.0 * capacity)[:, None, :]
-    duals = jnp.maximum(0.5 * rows_of, 0.0)
-    own = jnp.where(lax.axis_index("hours") == 0, jnp.sum(capacity**2, axis=0), 0.0)
-    fixed = sums.at[:techs].set(jnp.sum(state.available[:techs] * duals, axis=1))
-    fixed = fixed.at[techs].add(own)
-    fixed = fixed.at[techs + 1].add(jnp.sum(duals**2 - taken**2, axis=(0, 1)))
-    return exchange(sizes, prices, fixed)[1]
-
-
-def run(args, exact):
+    slopes = fixed[:techs][:, None, :] + price_start[None]
+    dispatch = jnp.maximum(-0.5 * slopes, 0.0)
+    slope = jnp.dot(price_start, maps_local, precision=highest)
+    flows_local = jnp.clip(-0.5 * slope, -local_limits, local_limits)
+    slope = jnp.dot(prices_all, maps_cross, precision=highest)
+    flows_cross = jnp.clip(-0.5 * slope, -cross_limits, cross_limits)
+    balance = (
+        jnp.sum(2.0 * dispatch, axis=0)
+        + jnp.dot(2.0 * flows_local, maps_local.T, precision=highest)
+        + jnp.dot(2.0 * flows_cross, maps_own.T, precision=highest)
+        - kept.available[techs]
+    )
+    step_up = balance / (techs + 8.0)
+    duals = jnp.maximum(0.5 * (2.0 * dispatch - available * (2.0 * capacity)[:, None, :]), 0.0)
+    store_duals = 2.0 * flows_local[:, lines:] / 3.0
+    slot = lax.broadcasted_iota(jnp.int32, (1, cross), 1) // sizes.slots
+    primal = (
+        jnp.sum(dispatch**2)
+        + jnp.sum(flows_local**2)
+        + jnp.sum(jnp.where(slot == own, flows_cross**2, 0.0))
+        + jnp.where(first_hour, jnp.sum(capacity**2), 0.0)
+    )
+    dual = jnp.sum(step_up**2) + jnp.sum(duals**2) + jnp.sum(store_duals**2)
+    rows_of = [
+        jnp.sum(available * duals, axis=1),
+        jnp.zeros((SQUARES, nodes)).at[0, 0].set(primal).at[1, 0].set(dual),
+        store_duals[:1].reshape(-1, LANES),
+        store_duals[rows - 1 :].reshape(-1, LANES),
+    ]
+    used = halo_at(sizes) + 2 * sizes.units // LANES
+    rows_of.append(jnp.zeros((sums_rows(sizes) - used, nodes)))
+    rows_of += [jnp.where(first_hour, part, 0.0) for part in (col_weight, cost)]
+    gathered, parts = exchange(sizes, price_start + step_up, jnp.concatenate(rows_of, axis=0))
+    flows = jnp.concatenate([flows_local, flows_cross], axis=1)
+    limits = jnp.concatenate([local_limits, cross_limits], axis=1)
+    state = Bag(
+        available=kept.available,
+        maps_local=kept.maps_local,
+        maps_cross=kept.maps_cross,
+        store_duals=store_duals,
+        dispatch=jnp.concatenate([dispatch, jnp.zeros((1, rows, nodes))], axis=0),
+        flows=jnp.concatenate([flows, jnp.broadcast_to(limits, (8, local + cross))], axis=0),
+    )
+    return state, gathered, parts
+
+
+def run(args):
     rows, techs, nodes = args.availability.shape
     hours, regions = lax.axis_size("hours"), lax.axis_size("region")
     slots, owned = args.cross_limit.shape[1], args.cap_cost.shape[1]
@@ -504,13 +565,26 @@
     )
     cross = regions * slots
 
-    gathered = both_regions(args.price_start)
-    info = call(
-        lambda names_in, names_out, *refs: slots_kernel(sizes, *refs),
-        Bag(ends=args.cross_ends[:, 0], limit=args.cross_limit, pairs=args.pair_counts),
-        Bag(info=shape(8 * (cross // LANES), nodes)),
-    ).info
-    info = both_regions(info)
+    gathered = both_regions(
+        call(
+            lambda names_in, names_out, *refs: first_kernel(sizes, refs[:4], *refs[4:]),
+            Bag(
+                price=args.price_start,
+                ends=args.cross_ends[:, 0],
+                limit=args.cross_limit,
+                pairs=args.pair_counts,
+            ),
+            Bag(block=shape(rows + 8 * (cross // LANES), nodes)),
+            left=(0, 1, 2, 3),
+            scratch=[
+                pltpu.VMEM((2, slots), jnp.int32),
+                pltpu.VMEM((1, slots), jnp.float32),
+                pltpu.VMEM((1, regions), jnp.int32),
+                pltpu.SemaphoreType.DMA((4,)),
+            ],
+            limit=None,
+        ).block
+    )
     state = call(
         functools.partial(start_kernel, sizes),
         Bag(
@@ -536,31 +610,51 @@
             sums=shape(sums_rows(sizes) + 2 * techs, nodes),
         ),
         flops=10**6,
+        left=(0,),
+        scratch=[pltpu.VMEM((rows * techs, nodes), jnp.float32), pltpu.SemaphoreType.DMA],
     )
     closed = call(
         lambda names_in, names_out, *refs: close_kernel(sizes, *refs),
-        Bag(gathered=gathered, info=info, balance=state.balance, sums=state.sums),
+        Bag(
+            gathered=gathered,
+            flows_local=state.flows_local,
+            balance=state.balance,
+            sums=state.sums,
+        ),
         Bag(
             maps=shape(regions * nodes, cross, dtype=jnp.bfloat16),
-            flows=shape(rows + 8, cross),
+            flows=shape(rows + 8, lines + units + cross),
             prices=shape(rows, nodes),
             sums=shape(*state.sums.shape),
         ),
     )
-    del state.sums, state.balance
-    state.maps_cross, state.flows_cross = closed.maps, closed.flows
+    del state.sums, state.balance, state.flows_local
+    state.maps_cross, state.flows = closed.maps, closed.flows
     gathered, parts = exchange(sizes, closed.prices, closed.sums)
-    if exact:
-        parts = corrected(sizes, state, closed.prices, closed.sums, parts)
-
+    outputs, kept, negative = sweeps(sizes, owned, state, gathered, parts)
+
+    def again():
+        return sweeps(sizes, owned, *restarted(sizes, kept, args.price_start))[0]
+
+    return lax.cond(negative > 0.0, again, lambda: outputs)
+
+
+def sweeps(sizes, owned, state, gathered, parts):
+    rows, techs, nodes, lines, units = (
+        sizes.rows,
+        sizes.techs,
+        sizes.nodes,
+        sizes.lines,
+        sizes.units,
+    )
+    state = Bag(**vars(state))
     for iteration in range(1, ITERS):
         given = Bag(**vars(state), **vars(parts), gathered=gathered)
         if iteration < ITERS - 1:
             outs = Bag(
                 dispatch=shape(techs + 1, rows, nodes),
                 cap_duals=shape(techs + 1, rows, nodes),
-                flows_local=shape(rows, lines + units),
-                flows_cross=shape(rows + 8, cross),
+                flows=shape(rows + 8, lines + units + sizes.regions * sizes.slots),
                 store_duals=shape(rows, units),
                 charge=shape(rows, units),
                 prices=shape(rows, nodes),
@@ -581,7 +675,7 @@
             vars(state).update(vars(results))
     dispatch = results.dispatch.reshape(rows, techs, nodes)
     outputs = (dispatch, results.capacity, results.prices, results.charge)
-    return outputs, results.negative[0, 0]
+    return outputs, state, results.negative[0, 0]
 
 
 def body(
@@ -601,8 +695,7 @@
     price_start,
 ):
     args = Bag(**locals())
-    outputs, negative = run(args, False)
-    return lax.cond(negative > 0.0, lambda: run(args, True)[0], lambda: outputs)
+    return run(args)
 
 
 def solution(mesh):

time: 56.6 us -> 56.8 us (level)
  Pallas kernels: 5.82 us -> 7.52 us
  local copies, waits for them, and re-layouts: 3.5 us -> 2.6 us
    pallas_call x6, Pallas kernels: 5.82 us -> 7.52 us  [call(): pl.pallas_call(functools.partial(kernel, names_in, names_out), out_shape=...]
    unnamed x62 -> x30, local copies, waits for them, and re-layouts: 3.26 us -> 2.36 us
    ppermute x23 -> x22, waiting for transfers between devices: 20.3 us -> 19.8 us  [swap(): return lax.ppermute(value, ('hours', 'region'), pairs)]
    ppermute x23 -> x22, starting transfers between devices: 25.4 us -> 25.2 us  [swap(): return lax.ppermute(value, ('hours', 'region'), pairs)]
  transfers between devices with their start and end apart: 23 -> 22, of which waited for: 16 -> 15; matrix products, arithmetic and copies ran while one was open for 0% -> 0% of each run, Pallas kernels for 3% -> 2%
where the time goes in v12:
time: 56.8 us; the launch traced here: 56.4 us
  starting transfers between devices  25.2 us (44%)
  waiting for transfers between devices  19.8 us (35%)
  Pallas kernels  7.52 us (13%)
  local copies, waits for them, and re-layouts  2.6 us (5%)
  between operations  1.08 us (2%)
    ppermute x22, starting transfers between devices, swap(): return lax.ppermute(value, ('hours', 'region'), pairs)  25.2 us
    ppermute x22, waiting for transfers between devices, swap(): return lax.ppermute(value, ('hours', 'region'), pairs)  19.8 us
    pallas_call x6, Pallas kernels, call(): pl.pallas_call(functools.partial(kernel, names_in, names_out), out_shape=...  7.52 us
    unnamed x30, local copies, waits for them, and re-layouts  2.36 us
  transfers between devices with their start and end apart: 22, of which 15 were waited for; matrix products, arithmetic and copies ran while one was open for 0% of the time, Pallas kernels for 2%

profile of v12, /device:TPU:0, one launch (start us, length us, event | category | flops | bytes accessed | tf_op | source)
XLA Modules:
  0.0 56.4 jit_solution(3510171946214524329)
XLA Ops:
  0.6 0.0 copy-start.1
  0.7 1.6 %shard_map.166 = f32[72,128]{1,0:T(8,128)} custom-call(f32[64,128]{1,0:T(8,128)} %refs_0_.1, s32[2,64]{1,0:T(2,128)} %bitcast.104, f32[1,64]{1,0:T(1,128)} %refs_2_.3, s32[1,2]{1,0:T(1,128)} %refs_3_.3), custom_call_target="tpu_custom_call" | custom-call | tf_op jit(solution)/shard_map/pallas_call | solution.py:415
  2.3 3.0 %collective-permute-start.22 = (f32[72,128]{1,0:T(8,128)}, f32[72,128]{1,0:T(8,128)S(1)}, u32[]{:S(2)}, u32[]{:S(2)}) collective-permute-start(f32[72,128]{1,0:T(8,128)} %shard_map.166), channel_id=1, source_target_pairs={{0,1},{1,0},{2,3},{3,2},{4,5},{5,4},{6,7},{7,6},{8,9},{9,8},{10,11... | collective-permute-start | bytes 110600 | tf_op jit(solution)/shard_map/ppermute | solution.py:437
  5.4 0.6 %copy-done.4 = s32[2,256]{1,0:T(2,128)S(1)} copy-done((s32[2,256]{1,0:T(2,128)S(1)}, s32[2,256]{1,0:T(2,128)}, u32[]{:S(2)}) %copy-start.4) | copy-done | bytes 2072
  6.0 0.0 copy-done.3
  6.0 0.0 copy-done.2
  6.1 1.0 %copy-done = f32[64,16,128]{2,1,0:T(8,128)S(1)} copy-done((f32[64,16,128]{2,1,0:T(8,128)S(1)}, f32[64,16,128]{2,1,0:T(8,128)}, u32[]{:S(2)}) %copy-start) | copy-done | bytes 524312
  7.1 0.9 %shard_map.165 = (f32[18,64,128]{2,1,0:T(8,128)S(1)}, bf16[128,512]{1,0:T(8,128)(2,1)S(1)}, f32[64,512]{1,0:T(8,128)S(1)}, f32[64,256]{1,0:T(8,128)S(1)}, f32[17...) custom-call(f32[1024,128]{1,0:T(8,128)S(1)} %bitcast.70, f32[64,128]{1,0:T(8,128)S(1)} %copy-done.16, ...), custom_call_target="tpu_custom_call" | custom-call | flops 1000000 | bytes 4000000 | tf_op jit(solution)/shard_map/pallas_call | solution.py:415
  8.0 0.0 collective-permute-done.22
  8.0 0.4 shard_map.167
  8.4 0.1 collective-permute-start.23
  8.5 1.2 %collective-permute-done.23.refs_10_ = f32[56,128]{1,0:T(8,128)S(1)} collective-permute-done((f32[56,128]{1,0:T(8,128)S(1)}, f32[56,128]{1,0:T(8,128)S(1)}, u32[]{:S(2)}, u32[]{:S(2)}) %collective-permute-start.23) | collective-permute-done | bytes 28704 | tf_op jit(solution)/shard_map/ppermute | solution.py:437
  9.7 2.2 %collective-permute-start.26 = (f32[3,128]{1,0:T(4,128)S(1)}, f32[3,128]{1,0:T(4,128)S(1)}, u32[]{:S(2)}, u32[]{:S(2)}) collective-permute-start(f32[3,128]{1,0:T(4,128)S(1)} %slice.530), channel_id=1, source_target_pairs={{0,7},{1,6},{2,5},{3,4},{4,3},{5,2},{6,1},{7,0},{8,15},{9,14},{10,... | collective-permute-start | bytes 4616 | tf_op jit(solution)/shard_map/ppermute | solution.py:437
  12.0 0.6 collective-permute-start.24
  12.5 0.6 collective-permute-start.25
  13.1 2.2 %collective-permute-done.24.refs_11_ = f32[56,128]{1,0:T(8,128)S(1)} collective-permute-done((f32[56,128]{1,0:T(8,128)S(1)}, f32[56,128]{1,0:T(8,128)S(1)}, u32[]{:S(2)}, u32[]{:S(2)}) %collective-permute-start.24) | collective-permute-done | bytes 28704 | tf_op jit(solution)/shard_map/ppermute | solution.py:437
  15.4 0.0 collective-permute-done.26
  15.4 1.1 %collective-permute-done.25 = f32[67,128]{1,0:T(8,128)S(1)} collective-permute-done((f32[67,128]{1,0:T(8,128)S(1)}, f32[67,128]{1,0:T(8,128)S(1)}, u32[]{:S(2)}, u32[]{:S(2)}) %collective-permute-start.25) | collective-permute-done | bytes 34336 | tf_op jit(solution)/shard_map/ppermute | solution.py:437
  16.5 0.1 scatter-add.20.refs_6_
  16.6 2.6 %collective-permute-start.29 = (f32[56,128]{1,0:T(8,128)S(1)}, f32[56,128]{1,0:T(8,128)S(1)}, u32[]{:S(2)}, u32[]{:S(2)}) collective-permute-start(f32[56,128]{1,0:T(8,128)S(1)} %scatter-add.20.refs_6_), channel_id=1, source_target_pairs={{0,26},{1,27},{2,24},{3,25},{4,30},{5,31},{6,28},{7,29},{8,18},{9,... | collective-permute-start | bytes 86024 | tf_op jit(solution)/shard_map/ppermute | solution.py:437
  19.2 0.2 collective-permute-start.28
  19.4 1.2 %collective-permute-start.27 = (f32[56,128]{1,0:T(8,128)S(1)}, f32[56,128]{1,0:T(8,128)S(1)}, u32[]{:S(2)}, u32[]{:S(2)}) collective-permute-start(f32[56,128]{1,0:T(8,128)S(1)} %scatter-add.20.refs_6_), channel_id=1, source_target_pairs={{0,10},{1,11},{2,8},{3,9},{4,14},{5,15},{6,12},{7,13},{8,2},{9,3},... | collective-permute-start | bytes 86024 | tf_op jit(solution)/shard_map/ppermute | solution.py:437
  20.6 1.1 %collective-permute-done.29.refs_9_ = f32[56,128]{1,0:T(8,128)S(1)} collective-permute-done((f32[56,128]{1,0:T(8,128)S(1)}, f32[56,128]{1,0:T(8,128)S(1)}, u32[]{:S(2)}, u32[]{:S(2)}) %collective-permute-start.29) | collective-permute-done | bytes 28704 | tf_op jit(solution)/shard_map/ppermute | solution.py:437
  21.7 1.7 %collective-permute-done.28.refs_8_ = f32[56,128]{1,0:T(8,128)S(1)} collective-permute-done((f32[56,128]{1,0:T(8,128)S(1)}, f32[56,128]{1,0:T(8,128)S(1)}, u32[]{:S(2)}, u32[]{:S(2)}) %collective-permute-start.28) | collective-permute-done | bytes 28704 | tf_op jit(solution)/shard_map/ppermute | solution.py:437
  23.4 0.0 collective-permute-done.27.refs_7_
  23.4 0.8 %shard_map.168 = (f32[17,64,128]{2,1,0:T(8,128)S(1)}, f32[17,64,128]{2,1,0:T(8,128)S(1)}, f32[72,640]{1,0:T(8,128)S(1)}, f32[64,256]{1,0:T(8,128)S(1)}, f32[64,2...) custom-call(f32[18,64,128]{2,1,0:T(8,128)S(1)} %get-tuple-element.183.refs_0_, ...), custom_call_target="tpu_custom_call" | custom-call | tf_op jit(solution)/shard_map/pallas_call | solution.py:415
  24.2 1.2 %collective-permute-start.30 = (f32[24,128]{1,0:T(8,128)S(1)}, f32[24,128]{1,0:T(8,128)S(1)}, u32[]{:S(2)}, u32[]{:S(2)}) collective-permute-start(f32[24,128]{1,0:T(8,128)S(1)} %get-tuple-element.199), channel_id=1, source_target_pairs={{0,2},{1,3},{2,0},{3,1},{4,6},{5,7},{6,4},{7,5},{8,10},{9,11},{10,... | collective-permute-start | bytes 36872 | tf_op jit(solution)/shard_map/ppermute | solution.py:437
  25.4 0.8 %collective-permute-done.30.refs_12_ = f32[24,128]{1,0:T(8,128)S(1)} collective-permute-done((f32[24,128]{1,0:T(8,128)S(1)}, f32[24,128]{1,0:T(8,128)S(1)}, u32[]{:S(2)}, u32[]{:S(2)}) %collective-permute-start.30) | collective-permute-done | bytes 12320 | tf_op jit(solution)/shard_map/ppermute | solution.py:437
  26.3 1.5 %collective-permute-start.33 = (f32[3,128]{1,0:T(4,128)S(1)}, f32[3,128]{1,0:T(4,128)S(1)}, u32[]{:S(2)}, u32[]{:S(2)}) collective-permute-start(f32[3,128]{1,0:T(4,128)S(1)} %slice.542), channel_id=1, source_target_pairs={{0,7},{1,6},{2,5},{3,4},{4,3},{5,2},{6,1},{7,0},{8,15},{9,14},{10,... | collective-permute-start | bytes 4616 | tf_op jit(solution)/shard_map/ppermute | solution.py:437
  27.8 0.4 collective-permute-start.31
  28.1 1.5 %collective-permute-start.32 = (f32[67,128]{1,0:T(8,128)S(1)}, f32[67,128]{1,0:T(8,128)S(1)}, u32[]{:S(2)}, u32[]{:S(2)}) collective-permute-start(f32[67,128]{1,0:T(8,128)S(1)} %pad_maximum_fusion.11), channel_id=1, source_target_pairs={{0,1},{1,0},{2,3},{3,2},{4,5},{5,4},{6,7},{7,6},{8,9},{9,8},{10,11... | collective-permute-start | bytes 102920 | tf_op jit(solution)/shard_map/ppermute | solution.py:437
  29.6 1.3 %collective-permute-done.31.refs_13_ = f32[24,128]{1,0:T(8,128)S(1)} collective-permute-done((f32[24,128]{1,0:T(8,128)S(1)}, f32[24,128]{1,0:T(8,128)S(1)}, u32[]{:S(2)}, u32[]{:S(2)}) %collective-permute-start.31) | collective-permute-done | bytes 12320 | tf_op jit(solution)/shard_map/ppermute | solution.py:437
  31.0 0.0 collective-permute-done.33
  31.0 1.1 %collective-permute-done.32 = f32[67,128]{1,0:T(8,128)S(1)} collective-permute-done((f32[67,128]{1,0:T(8,128)S(1)}, f32[67,128]{1,0:T(8,128)S(1)}, u32[]{:S(2)}, u32[]{:S(2)}) %collective-permute-start.32) | collective-permute-done | bytes 34336 | tf_op jit(solution)/shard_map/ppermute | solution.py:437
  32.1 0.1 scatter-add.21.refs_8_
  32.2 0.6 collective-permute-start.36
  32.7 0.9 %collective-permute-start.35 = (f32[24,128]{1,0:T(8,128)S(1)}, f32[24,128]{1,0:T(8,128)S(1)}, u32[]{:S(2)}, u32[]{:S(2)}) collective-permute-start(f32[24,128]{1,0:T(8,128)S(1)} %scatter-add.21.refs_8_), channel_id=1, source_target_pairs={{0,18},{1,19},{2,16},{3,17},{4,22},{5,23},{6,20},{7,21},{8,26},{9,... | collective-permute-start | bytes 36872 | tf_op jit(solution)/shard_map/ppermute | solution.py:437
  33.7 1.5 %collective-permute-start.34 = (f32[24,128]{1,0:T(8,128)S(1)}, f32[24,128]{1,0:T(8,128)S(1)}, u32[]{:S(2)}, u32[]{:S(2)}) collective-permute-start(f32[24,128]{1,0:T(8,128)S(1)} %scatter-add.21.refs_8_), channel_id=1, source_target_pairs={{0,10},{1,11},{2,8},{3,9},{4,14},{5,15},{6,12},{7,13},{8,2},{9,3},... | collective-permute-start | bytes 36872 | tf_op jit(solution)/shard_map/ppermute | solution.py:437
  35.2 2.0 %collective-permute-done.36.refs_11_ = f32[24,128]{1,0:T(8,128)S(1)} collective-permute-done((f32[24,128]{1,0:T(8,128)S(1)}, f32[24,128]{1,0:T(8,128)S(1)}, u32[]{:S(2)}, u32[]{:S(2)}) %collective-permute-start.36) | collective-permute-done | bytes 12320 | tf_op jit(solution)/shard_map/ppermute | solution.py:437
  37.2 0.0 collective-permute-done.35.refs_10_
  37.2 0.0 collective-permute-done.34.refs_9_
  37.2 1.5 %shard_map.169 = (f32[17,64,128]{2,1,0:T(8,128)S(1)}, f32[17,64,128]{2,1,0:T(8,128)}, f32[72,640]{1,0:T(8,128)S(1)}, f32[64,256]{1,0:T(8,128)S(1)}, f32[64,256]{...) custom-call(f32[18,64,128]{2,1,0:T(8,128)S(1)} %get-tuple-element.183.refs_0_, ...), custom_call_target="tpu_custom_call" | custom-call | tf_op jit(solution)/shard_map/pallas_call | solution.py:415
  38.7 0.9 %collective-permute-start.37 = (f32[24,128]{1,0:T(8,128)S(1)}, f32[24,128]{1,0:T(8,128)S(1)}, u32[]{:S(2)}, u32[]{:S(2)}) collective-permute-start(f32[24,128]{1,0:T(8,128)S(1)} %get-tuple-element.206), channel_id=1, source_target_pairs={{0,2},{1,3},{2,0},{3,1},{4,6},{5,7},{6,4},{7,5},{8,10},{9,11},{10,... | collective-permute-start | bytes 36872 | tf_op jit(solution)/shard_map/ppermute | solution.py:437
  39.6 0.8 %collective-permute-done.37.refs_12_ = f32[24,128]{1,0:T(8,128)S(1)} collective-permute-done((f32[24,128]{1,0:T(8,128)S(1)}, f32[24,128]{1,0:T(8,128)S(1)}, u32[]{:S(2)}, u32[]{:S(2)}) %collective-permute-start.37) | collective-permute-done | bytes 12320 | tf_op jit(solution)/shard_map/ppermute | solution.py:437
  40.4 2.4 %collective-permute-start.40 = (f32[3,128]{1,0:T(4,128)S(1)}, f32[3,128]{1,0:T(4,128)S(1)}, u32[]{:S(2)}, u32[]{:S(2)}) collective-permute-start(f32[3,128]{1,0:T(4,128)S(1)} %slice.554), channel_id=1, source_target_pairs={{0,7},{1,6},{2,5},{3,4},{4,3},{5,2},{6,1},{7,0},{8,15},{9,14},{10,... | collective-permute-start | bytes 4616 | tf_op jit(solution)/shard_map/ppermute | solution.py:437
  42.9 0.3 collective-permute-start.38
  43.2 0.6 %collective-permute-start.39 = (f32[67,128]{1,0:T(8,128)S(1)}, f32[67,128]{1,0:T(8,128)S(1)}, u32[]{:S(2)}, u32[]{:S(2)}) collective-permute-start(f32[67,128]{1,0:T(8,128)S(1)} %pad_maximum_fusion.12), channel_id=1, source_target_pairs={{0,1},{1,0},{2,3},{3,2},{4,5},{5,4},{6,7},{7,6},{8,9},{9,8},{10,11... | collective-permute-start | bytes 102920 | tf_op jit(solution)/shard_map/ppermute | solution.py:437
  43.8 2.3 %collective-permute-done.38.refs_13_ = f32[24,128]{1,0:T(8,128)S(1)} collective-permute-done((f32[24,128]{1,0:T(8,128)S(1)}, f32[24,128]{1,0:T(8,128)S(1)}, u32[]{:S(2)}, u32[]{:S(2)}) %collective-permute-start.38) | collective-permute-done | bytes 12320 | tf_op jit(solution)/shard_map/ppermute | solution.py:437
  46.1 0.0 collective-permute-done.40
  46.1 1.0 %collective-permute-done.39 = f32[67,128]{1,0:T(8,128)S(1)} collective-permute-done((f32[67,128]{1,0:T(8,128)S(1)}, f32[67,128]{1,0:T(8,128)S(1)}, u32[]{:S(2)}, u32[]{:S(2)}) %collective-permute-start.39) | collective-permute-done | bytes 34336 | tf_op jit(solution)/shard_map/ppermute | solution.py:437
  47.2 0.1 scatter-add.24.refs_8_
  47.3 1.1 %collective-permute-start.43 = (f32[24,128]{1,0:T(8,128)S(1)}, f32[24,128]{1,0:T(8,128)S(1)}, u32[]{:S(2)}, u32[]{:S(2)}) collective-permute-start(f32[24,128]{1,0:T(8,128)S(1)} %scatter-add.24.refs_8_), channel_id=1, source_target_pairs={{0,26},{1,27},{2,24},{3,25},{4,30},{5,31},{6,28},{7,29},{8,18},{9,... | collective-permute-start | bytes 36872 | tf_op jit(solution)/shard_map/ppermute | solution.py:437
  48.4 1.9 %collective-permute-start.42 = (f32[24,128]{1,0:T(8,128)S(1)}, f32[24,128]{1,0:T(8,128)S(1)}, u32[]{:S(2)}, u32[]{:S(2)}) collective-permute-start(f32[24,128]{1,0:T(8,128)S(1)} %scatter-add.24.refs_8_), channel_id=1, source_target_pairs={{0,18},{1,19},{2,16},{3,17},{4,22},{5,23},{6,20},{7,21},{8,26},{9,... | collective-permute-start | bytes 36872 | tf_op jit(solution)/shard_map/ppermute | solution.py:437
  50.3 0.0 collective-permute-start.41
  50.3 1.9 %collective-permute-done.43.refs_11_ = f32[24,128]{1,0:T(8,128)S(1)} collective-permute-done((f32[24,128]{1,0:T(8,128)S(1)}, f32[24,128]{1,0:T(8,128)S(1)}, u32[]{:S(2)}, u32[]{:S(2)}) %collective-permute-start.43) | collective-permute-done | bytes 12320 | tf_op jit(solution)/shard_map/ppermute | solution.py:437
  52.2 0.1 collective-permute-done.42.refs_10_
  52.4 1.0 %collective-permute-done.41.refs_9_ = f32[24,128]{1,0:T(8,128)S(1)} collective-permute-done((f32[24,128]{1,0:T(8,128)S(1)}, f32[24,128]{1,0:T(8,128)S(1)}, u32[]{:S(2)}, u32[]{:S(2)}) %collective-permute-start.41) | collective-permute-done | bytes 12320 | tf_op jit(solution)/shard_map/ppermute | solution.py:437
  53.4 2.3 %shard_map.170 = (f32[1024,128]{1,0:T(8,128)}, f32[1,128]{1,0:T(1,128)S(1)}, f32[64,128]{1,0:T(8,128)S(1)}, f32[64,256]{1,0:T(8,128)S(1)}, f32[1,128]{1,0:T(1,128)S(1)}) custom-call(f32[18,64,128]{2,1,0:T(8,128)S(1)} %get-tuple-element.183.refs_0_, bf16[128,512]{1,0:T(8,128)(2,1)S(1)} %get-tuple-element.184.refs_1_, ...), custom_call_target="tpu_custom_call" | custom-call | tf_op jit(solution)/shard_map/pallas_call | solution.py:415
  55.8 0.0 copy-start.20
  55.8 0.0 copy-start.18
  55.8 0.0 copy-start.19
  55.8 0.5 copy-done.20
  56.3 0.1 copy-done.18
  56.4 0.0 copy-done.19
  (62 shorter events, 0.3 us)
Async XLA Ops:
  0.6 4.7 %copy-start.1 = (f32[64,128]{1,0:T(8,128)S(1)}, f32[64,128]{1,0:T(8,128)}, u32[]{:S(2)}) copy-start(f32[64,128]{1,0:T(8,128)} %refs_2_.2) | copy-start | bytes 98308
  0.6 4.7 %copy-start.5 = (f32[256]{0:T(256)S(1)}, f32[256]{0:T(256)}, u32[]{:S(2)}) copy-start(f32[256]{0:T(256)} %param.38) | copy-start | bytes 3076
  0.7 4.7 %copy-start.6 = (s32[256]{0:T(256)S(1)}, s32[256]{0:T(256)}, u32[]{:S(2)}) copy-start(s32[256]{0:T(256)} %param.42) | copy-start | bytes 3076
  0.7 4.7 %copy-start.7 = (f32[256]{0:T(256)S(1)}, f32[256]{0:T(256)}, u32[]{:S(2)}) copy-start(f32[256]{0:T(256)} %param.44) | copy-start | bytes 3076
  0.7 4.7 %copy-start.8 = (f32[256]{0:T(256)S(1)}, f32[256]{0:T(256)}, u32[]{:S(2)}) copy-start(f32[256]{0:T(256)} %param.43) | copy-start | bytes 3076
  0.7 4.7 %copy-start.16 = (f32[64,128]{1,0:T(8,128)S(1)}, f32[64,128]{1,0:T(8,128)}, u32[]{:S(2)}) copy-start(f32[64,128]{1,0:T(8,128)} %refs_0_.1) | copy-start | bytes 98308
  2.3 5.7 %collective-permute-start.22 = (f32[72,128]{1,0:T(8,128)}, f32[72,128]{1,0:T(8,128)S(1)}, u32[]{:S(2)}, u32[]{:S(2)}) collective-permute-start(f32[72,128]{1,0:T(8,128)} %shard_map.166), channel_id=1, source_target_pairs={{0,1},{1,0},{2,3},{3,2},{4,5},{5,4},{6,7},{7,6},{8,9},{9,8},{10,11... | collective-permute-start | bytes 110600 | tf_op jit(solution)/shard_map/ppermute | solution.py:437
  5.3 0.7 %copy-start.4 = (s32[2,256]{1,0:T(2,128)S(1)}, s32[2,256]{1,0:T(2,128)}, u32[]{:S(2)}) copy-start(s32[2,256]{1,0:T(2,128)} %refs_6_.1) | copy-start | bytes 6148
  5.3 0.7 %copy-start.3 = (s32[1,2048]{1,0:T(1,128)S(1)}, s32[1,2048]{1,0:T(1,128)}, u32[]{:S(2)}) copy-start(s32[1,2048]{1,0:T(1,128)} %param.36) | copy-start | bytes 24580
  5.3 0.7 %copy-start.2 = (f32[16,128]{1,0:T(8,128)S(1)}, f32[16,128]{1,0:T(8,128)}, u32[]{:S(2)}) copy-start(f32[16,128]{1,0:T(8,128)} %refs_3_.2) | copy-start | bytes 24580
  5.3 0.7 %copy-start.9 = (f32[1,128]{1,0:T(1,128)S(1)}, f32[1,128]{1,0:T(1,128)}, u32[]{:S(2)}) copy-start(f32[1,128]{1,0:T(1,128)} %refs_4_.1) | copy-start | bytes 1540
  6.1 1.0 %copy-start = (f32[64,16,128]{2,1,0:T(8,128)S(1)}, f32[64,16,128]{2,1,0:T(8,128)}, u32[]{:S(2)}) copy-start(f32[64,16,128]{2,1,0:T(8,128)} %param.32) | copy-start | bytes 1572868
  7.1 0.9 %copy-start.17 = (f32[72,128]{1,0:T(8,128)S(1)}, f32[72,128]{1,0:T(8,128)}, u32[]{:S(2)}) copy-start(f32[72,128]{1,0:T(8,128)} %shard_map.166) | copy-start | bytes 110596
  8.4 1.3 %collective-permute-start.23 = (f32[56,128]{1,0:T(8,128)S(1)}, f32[56,128]{1,0:T(8,128)S(1)}, u32[]{:S(2)}, u32[]{:S(2)}) collective-permute-start(f32[56,128]{1,0:T(8,128)S(1)} %get-tuple-element.192), channel_id=1, source_target_pairs={{0,2},{1,3},{2,0},{3,1},{4,6},{5,7},{6,4},{7,5},{8,10},{9,11},{10,... | collective-permute-start | bytes 86024 | tf_op jit(solution)/shard_map/ppermute | solution.py:437
  9.7 5.7 %collective-permute-start.26 = (f32[3,128]{1,0:T(4,128)S(1)}, f32[3,128]{1,0:T(4,128)S(1)}, u32[]{:S(2)}, u32[]{:S(2)}) collective-permute-start(f32[3,128]{1,0:T(4,128)S(1)} %slice.530), channel_id=1, source_target_pairs={{0,7},{1,6},{2,5},{3,4},{4,3},{5,2},{6,1},{7,0},{8,15},{9,14},{10,... | collective-permute-start | bytes 4616 | tf_op jit(solution)/shard_map/ppermute | solution.py:437
  12.0 3.4 %collective-permute-start.24 = (f32[56,128]{1,0:T(8,128)S(1)}, f32[56,128]{1,0:T(8,128)S(1)}, u32[]{:S(2)}, u32[]{:S(2)}) collective-permute-start(f32[56,128]{1,0:T(8,128)S(1)} %pad_maximum_fusion.13), channel_id=1, source_target_pairs={{0,6},{1,7},{2,4},{3,5},{4,2},{5,3},{6,0},{7,1},{8,14},{9,15},{10,... | collective-permute-start | bytes 86024 | tf_op jit(solution)/shard_map/ppermute | solution.py:437
  12.5 4.0 %collective-permute-start.25 = (f32[67,128]{1,0:T(8,128)S(1)}, f32[67,128]{1,0:T(8,128)S(1)}, u32[]{:S(2)}, u32[]{:S(2)}) collective-permute-start(f32[67,128]{1,0:T(8,128)S(1)} %pad_maximum_fusion.10), channel_id=1, source_target_pairs={{0,1},{1,0},{2,3},{3,2},{4,5},{5,4},{6,7},{7,6},{8,9},{9,8},{10,11... | collective-permute-start | bytes 102920 | tf_op jit(solution)/shard_map/ppermute | solution.py:437
  16.6 5.2 %collective-permute-start.29 = (f32[56,128]{1,0:T(8,128)S(1)}, f32[56,128]{1,0:T(8,128)S(1)}, u32[]{:S(2)}, u32[]{:S(2)}) collective-permute-start(f32[56,128]{1,0:T(8,128)S(1)} %scatter-add.20.refs_6_), channel_id=1, source_target_pairs={{0,26},{1,27},{2,24},{3,25},{4,30},{5,31},{6,28},{7,29},{8,18},{9,... | collective-permute-start | bytes 86024 | tf_op jit(solution)/shard_map/ppermute | solution.py:437
  19.2 4.2 %collective-permute-start.28 = (f32[56,128]{1,0:T(8,128)S(1)}, f32[56,128]{1,0:T(8,128)S(1)}, u32[]{:S(2)}, u32[]{:S(2)}) collective-permute-start(f32[56,128]{1,0:T(8,128)S(1)} %scatter-add.20.refs_6_), channel_id=1, source_target_pairs={{0,18},{1,19},{2,16},{3,17},{4,22},{5,23},{6,20},{7,21},{8,26},{9,... | collective-permute-start | bytes 86024 | tf_op jit(solution)/shard_map/ppermute | solution.py:437
  19.4 4.0 %collective-permute-start.27 = (f32[56,128]{1,0:T(8,128)S(1)}, f32[56,128]{1,0:T(8,128)S(1)}, u32[]{:S(2)}, u32[]{:S(2)}) collective-permute-start(f32[56,128]{1,0:T(8,128)S(1)} %scatter-add.20.refs_6_), channel_id=1, source_target_pairs={{0,10},{1,11},{2,8},{3,9},{4,14},{5,15},{6,12},{7,13},{8,2},{9,3},... | collective-permute-start | bytes 86024 | tf_op jit(solution)/shard_map/ppermute | solution.py:437
  24.2 2.1 %collective-permute-start.30 = (f32[24,128]{1,0:T(8,128)S(1)}, f32[24,128]{1,0:T(8,128)S(1)}, u32[]{:S(2)}, u32[]{:S(2)}) collective-permute-start(f32[24,128]{1,0:T(8,128)S(1)} %get-tuple-element.199), channel_id=1, source_target_pairs={{0,2},{1,3},{2,0},{3,1},{4,6},{5,7},{6,4},{7,5},{8,10},{9,11},{10,... | collective-permute-start | bytes 36872 | tf_op jit(solution)/shard_map/ppermute | solution.py:437
  26.3 4.8 %collective-permute-start.33 = (f32[3,128]{1,0:T(4,128)S(1)}, f32[3,128]{1,0:T(4,128)S(1)}, u32[]{:S(2)}, u32[]{:S(2)}) collective-permute-start(f32[3,128]{1,0:T(4,128)S(1)} %slice.542), channel_id=1, source_target_pairs={{0,7},{1,6},{2,5},{3,4},{4,3},{5,2},{6,1},{7,0},{8,15},{9,14},{10,... | collective-permute-start | bytes 4616 | tf_op jit(solution)/shard_map/ppermute | solution.py:437
  27.8 3.2 %collective-permute-start.31 = (f32[24,128]{1,0:T(8,128)S(1)}, f32[24,128]{1,0:T(8,128)S(1)}, u32[]{:S(2)}, u32[]{:S(2)}) collective-permute-start(f32[24,128]{1,0:T(8,128)S(1)} %pad_maximum_fusion.15), channel_id=1, source_target_pairs={{0,6},{1,7},{2,4},{3,5},{4,2},{5,3},{6,0},{7,1},{8,14},{9,15},{10,... | collective-permute-start | bytes 36872 | tf_op jit(solution)/shard_map/ppermute | solution.py:437
  28.1 4.0 %collective-permute-start.32 = (f32[67,128]{1,0:T(8,128)S(1)}, f32[67,128]{1,0:T(8,128)S(1)}, u32[]{:S(2)}, u32[]{:S(2)}) collective-permute-start(f32[67,128]{1,0:T(8,128)S(1)} %pad_maximum_fusion.11), channel_id=1, source_target_pairs={{0,1},{1,0},{2,3},{3,2},{4,5},{5,4},{6,7},{7,6},{8,9},{9,8},{10,11... | collective-permute-start | bytes 102920 | tf_op jit(solution)/shard_map/ppermute | solution.py:437
  32.2 5.0 %collective-permute-start.36 = (f32[24,128]{1,0:T(8,128)S(1)}, f32[24,128]{1,0:T(8,128)S(1)}, u32[]{:S(2)}, u32[]{:S(2)}) collective-permute-start(f32[24,128]{1,0:T(8,128)S(1)} %scatter-add.21.refs_8_), channel_id=1, source_target_pairs={{0,26},{1,27},{2,24},{3,25},{4,30},{5,31},{6,28},{7,29},{8,18},{9,... | collective-permute-start | bytes 36872 | tf_op jit(solution)/shard_map/ppermute | solution.py:437
  32.7 4.4 %collective-permute-start.35 = (f32[24,128]{1,0:T(8,128)S(1)}, f32[24,128]{1,0:T(8,128)S(1)}, u32[]{:S(2)}, u32[]{:S(2)}) collective-permute-start(f32[24,128]{1,0:T(8,128)S(1)} %scatter-add.21.refs_8_), channel_id=1, source_target_pairs={{0,18},{1,19},{2,16},{3,17},{4,22},{5,23},{6,20},{7,21},{8,26},{9,... | collective-permute-start | bytes 36872 | tf_op jit(solution)/shard_map/ppermute | solution.py:437
  33.7 3.5 %collective-permute-start.34 = (f32[24,128]{1,0:T(8,128)S(1)}, f32[24,128]{1,0:T(8,128)S(1)}, u32[]{:S(2)}, u32[]{:S(2)}) collective-permute-start(f32[24,128]{1,0:T(8,128)S(1)} %scatter-add.21.refs_8_), channel_id=1, source_target_pairs={{0,10},{1,11},{2,8},{3,9},{4,14},{5,15},{6,12},{7,13},{8,2},{9,3},... | collective-permute-start | bytes 36872 | tf_op jit(solution)/shard_map/ppermute | solution.py:437
  38.7 1.7 %collective-permute-start.37 = (f32[24,128]{1,0:T(8,128)S(1)}, f32[24,128]{1,0:T(8,128)S(1)}, u32[]{:S(2)}, u32[]{:S(2)}) collective-permute-start(f32[24,128]{1,0:T(8,128)S(1)} %get-tuple-element.206), channel_id=1, source_target_pairs={{0,2},{1,3},{2,0},{3,1},{4,6},{5,7},{6,4},{7,5},{8,10},{9,11},{10,... | collective-permute-start | bytes 36872 | tf_op jit(solution)/shard_map/ppermute | solution.py:437
  40.4 5.7 %collective-permute-start.40 = (f32[3,128]{1,0:T(4,128)S(1)}, f32[3,128]{1,0:T(4,128)S(1)}, u32[]{:S(2)}, u32[]{:S(2)}) collective-permute-start(f32[3,128]{1,0:T(4,128)S(1)} %slice.554), channel_id=1, source_target_pairs={{0,7},{1,6},{2,5},{3,4},{4,3},{5,2},{6,1},{7,0},{8,15},{9,14},{10,... | collective-permute-start | bytes 4616 | tf_op jit(solution)/shard_map/ppermute | solution.py:437
  42.9 3.2 %collective-permute-start.38 = (f32[24,128]{1,0:T(8,128)S(1)}, f32[24,128]{1,0:T(8,128)S(1)}, u32[]{:S(2)}, u32[]{:S(2)}) collective-permute-start(f32[24,128]{1,0:T(8,128)S(1)} %pad_maximum_fusion.17), channel_id=1, source_target_pairs={{0,6},{1,7},{2,4},{3,5},{4,2},{5,3},{6,0},{7,1},{8,14},{9,15},{10,... | collective-permute-start | bytes 36872 | tf_op jit(solution)/shard_map/ppermute | solution.py:437
  43.2 4.0 %collective-permute-start.39 = (f32[67,128]{1,0:T(8,128)S(1)}, f32[67,128]{1,0:T(8,128)S(1)}, u32[]{:S(2)}, u32[]{:S(2)}) collective-permute-start(f32[67,128]{1,0:T(8,128)S(1)} %pad_maximum_fusion.12), channel_id=1, source_target_pairs={{0,1},{1,0},{2,3},{3,2},{4,5},{5,4},{6,7},{7,6},{8,9},{9,8},{10,11... | collective-permute-start | bytes 102920 | tf_op jit(solution)/shard_map/ppermute | solution.py:437
  47.3 5.0 %collective-permute-start.43 = (f32[24,128]{1,0:T(8,128)S(1)}, f32[24,128]{1,0:T(8,128)S(1)}, u32[]{:S(2)}, u32[]{:S(2)}) collective-permute-start(f32[24,128]{1,0:T(8,128)S(1)} %scatter-add.24.refs_8_), channel_id=1, source_target_pairs={{0,26},{1,27},{2,24},{3,25},{4,30},{5,31},{6,28},{7,29},{8,18},{9,... | collective-permute-start | bytes 36872 | tf_op jit(solution)/shard_map/ppermute | solution.py:437
  48.4 4.0 %collective-permute-start.42 = (f32[24,128]{1,0:T(8,128)S(1)}, f32[24,128]{1,0:T(8,128)S(1)}, u32[]{:S(2)}, u32[]{:S(2)}) collective-permute-start(f32[24,128]{1,0:T(8,128)S(1)} %scatter-add.24.refs_8_), channel_id=1, source_target_pairs={{0,18},{1,19},{2,16},{3,17},{4,22},{5,23},{6,20},{7,21},{8,26},{9,... | collective-permute-start | bytes 36872 | tf_op jit(solution)/shard_map/ppermute | solution.py:437
  50.3 3.1 %collective-permute-start.41 = (f32[24,128]{1,0:T(8,128)S(1)}, f32[24,128]{1,0:T(8,128)S(1)}, u32[]{:S(2)}, u32[]{:S(2)}) collective-permute-start(f32[24,128]{1,0:T(8,128)S(1)} %scatter-add.24.refs_8_), channel_id=1, source_target_pairs={{0,10},{1,11},{2,8},{3,9},{4,14},{5,15},{6,12},{7,13},{8,2},{9,3},... | collective-permute-start | bytes 36872 | tf_op jit(solution)/shard_map/ppermute | solution.py:437
  55.8 0.5 copy-start.20
  55.8 0.6 %copy-start.18 = (f32[64,256]{1,0:T(8,128)}, f32[64,256]{1,0:T(8,128)S(1)}, u32[]{:S(2)}) copy-start(f32[64,256]{1,0:T(8,128)S(1)} %get-tuple-element.215) | copy-start | bytes 196612
  55.8 0.6 %copy-start.19 = (f32[64,128]{1,0:T(8,128)}, f32[64,128]{1,0:T(8,128)S(1)}, u32[]{:S(2)}) copy-start(f32[64,128]{1,0:T(8,128)S(1)} %get-tuple-element.214) | copy-start | bytes 98308

commit v13 on v12

--- a/solution.py
+++ b/solution.py
@@ -493,69 +493,23 @@
     return jax.ShapeDtypeStruct(dims, dtype)
 
 
-def restarted(sizes, kept, price_start):
-    rows, techs, nodes, lines = sizes.rows, sizes.techs, sizes.nodes, sizes.lines
-    local, cross = lines + sizes.units, sizes.regions * sizes.slots
-    at, own = places(sizes), lax.axis_index("region")
-    first_hour = lax.axis_index("hours") == 0
-    fixed, available = kept.available[techs + 1], kept.available[:techs]
-    col_weight, cost = kept.cap_duals[techs, :techs], kept.cap_duals[techs, techs : 2 * techs]
-    local_limits = fixed[at.limits : at.energy].reshape(1, local)
-    cross_limits = kept.flows[rows : rows + 1, local:]
-    maps_local = kept.maps_local.astype(jnp.float32)
-    maps_cross = kept.maps_cross.astype(jnp.float32)
-    maps_own = lax.dynamic_slice_in_dim(maps_cross, own * nodes, nodes)
-    prices_all = jnp.concatenate(list(both_regions(price_start)), axis=1)
-    highest = lax.Precision.HIGHEST
-
+def corrected(sizes, state, prices, sums, parts):
+    techs = sizes.techs
+    totals = total_of(parts)
+    first = sums_rows(sizes)
+    col_weight, cost = totals[first : first + techs], totals[first + techs :]
     capacity = jnp.maximum(-cost / col_weight, 0.0)
-    slopes = fixed[:techs][:, None, :] + price_start[None]
-    dispatch = jnp.maximum(-0.5 * slopes, 0.0)
-    slope = jnp.dot(price_start, maps_local, precision=highest)
-    flows_local = jnp.clip(-0.5 * slope, -local_limits, local_limits)
-    slope = jnp.dot(prices_all, maps_cross, precision=highest)
-    flows_cross = jnp.clip(-0.5 * slope, -cross_limits, cross_limits)
-    balance = (
-        jnp.sum(2.0 * dispatch, axis=0)
-        + jnp.dot(2.0 * flows_local, maps_local.T, precision=highest)
-        + jnp.dot(2.0 * flows_cross, maps_own.T, precision=highest)
-        - kept.available[techs]
-    )
-    step_up = balance / (techs + 8.0)
-    duals = jnp.maximum(0.5 * (2.0 * dispatch - available * (2.0 * capacity)[:, None, :]), 0.0)
-    store_duals = 2.0 * flows_local[:, lines:] / 3.0
-    slot = lax.broadcasted_iota(jnp.int32, (1, cross), 1) // sizes.slots
-    primal = (
-        jnp.sum(dispatch**2)
-        + jnp.sum(flows_local**2)
-        + jnp.sum(jnp.where(slot == own, flows_cross**2, 0.0))
-        + jnp.where(first_hour, jnp.sum(capacity**2), 0.0)
-    )
-    dual = jnp.sum(step_up**2) + jnp.sum(duals**2) + jnp.sum(store_duals**2)
-    rows_of = [
-        jnp.sum(available * duals, axis=1),
-        jnp.zeros((SQUARES, nodes)).at[0, 0].set(primal).at[1, 0].set(dual),
-        store_duals[:1].reshape(-1, LANES),
-        store_duals[rows - 1 :].reshape(-1, LANES),
-    ]
-    used = halo_at(sizes) + 2 * sizes.units // LANES
-    rows_of.append(jnp.zeros((sums_rows(sizes) - used, nodes)))
-    rows_of += [jnp.where(first_hour, part, 0.0) for part in (col_weight, cost)]
-    gathered, parts = exchange(sizes, price_start + step_up, jnp.concatenate(rows_of, axis=0))
-    flows = jnp.concatenate([flows_local, flows_cross], axis=1)
-    limits = jnp.concatenate([local_limits, cross_limits], axis=1)
-    state = Bag(
-        available=kept.available,
-        maps_local=kept.maps_local,
-        maps_cross=kept.maps_cross,
-        store_duals=store_duals,
-        dispatch=jnp.concatenate([dispatch, jnp.zeros((1, rows, nodes))], axis=0),
-        flows=jnp.concatenate([flows, jnp.broadcast_to(limits, (8, local + cross))], axis=0),
-    )
-    return state, gathered, parts
-
-
-def run(args):
+    taken = state.dispatch[:techs]
+    rows_of = 2.0 * taken - state.available[:techs] * (2.0 * capacity)[:, None, :]
+    duals = jnp.maximum(0.5 * rows_of, 0.0)
+    own = jnp.where(lax.axis_index("hours") == 0, jnp.sum(capacity**2, axis=0), 0.0)
+    fixed = sums.at[:techs].set(jnp.sum(state.available[:techs] * duals, axis=1))
+    fixed = fixed.at[techs].add(own)
+    fixed = fixed.at[techs + 1].add(jnp.sum(duals**2 - taken**2, axis=(0, 1)))
+    return exchange(sizes, prices, fixed)[1]
+
+
+def run(args, exact):
     rows, techs, nodes = args.availability.shape
     hours, regions = lax.axis_size("hours"), lax.axis_size("region")
     slots, owned = args.cross_limit.shape[1], args.cap_cost.shape[1]
@@ -631,12 +585,9 @@
     del state.sums, state.balance, state.flows_local
     state.maps_cross, state.flows = closed.maps, closed.flows
     gathered, parts = exchange(sizes, closed.prices, closed.sums)
-    outputs, kept, negative = sweeps(sizes, owned, state, gathered, parts)
-
-    def again():
-        return sweeps(sizes, owned, *restarted(sizes, kept, args.price_start))[0]
-
-    return lax.cond(negative > 0.0, again, lambda: outputs)
+    if exact:
+        parts = corrected(sizes, state, closed.prices, closed.sums, parts)
+    return sweeps(sizes, owned, state, gathered, parts)
 
 
 def sweeps(sizes, owned, state, gathered, parts):
@@ -675,7 +626,7 @@
             vars(state).update(vars(results))
     dispatch = results.dispatch.reshape(rows, techs, nodes)
     outputs = (dispatch, results.capacity, results.prices, results.charge)
-    return outputs, state, results.negative[0, 0]
+    return outputs, results.negative[0, 0]
 
 
 def body(
@@ -695,7 +646,8 @@
     price_start,
 ):
     args = Bag(**locals())
-    return run(args)
+    outputs, negative = run(args, False)
+    return lax.cond(negative > 0.0, lambda: run(args, True)[0], lambda: outputs)
 
 
 def solution(mesh):

time: 56.8 us -> 57.8 us (1.018)
  local copies, waits for them, and re-layouts: 2.6 us -> 4.77 us
  Pallas kernels: 7.52 us -> 6.48 us
  waiting for transfers between devices: 19.8 us -> 19.2 us
    unnamed x30 -> x76, local copies, waits for them, and re-layouts: 2.36 us -> 4.54 us
    pallas_call x6, Pallas kernels: 7.52 us -> 6.48 us  [call(): pl.pallas_call(functools.partial(kernel, names_in, names_out), out_shape=...]
  transfers between devices with their start and end apart: 22 -> 22, of which waited for: 15 -> 16; matrix products, arithmetic and copies ran while one was open for 0% -> 0% of each run, Pallas kernels for 2% -> 3%
where the time goes in v13:
time: 57.8 us; the launch traced here: 57.5 us
  starting transfers between devices  25.6 us (44%)
  waiting for transfers between devices  19.2 us (33%)
  Pallas kernels  6.48 us (11%)
  local copies, waits for them, and re-layouts  4.77 us (8%)
  between operations  1.25 us (2%)
    ppermute x22, starting transfers between devices, swap(): return lax.ppermute(value, ('hours', 'region'), pairs)  25.6 us
    ppermute x22, waiting for transfers between devices, swap(): return lax.ppermute(value, ('hours', 'region'), pairs)  19.2 us
    pallas_call x6, Pallas kernels, call(): pl.pallas_call(functools.partial(kernel, names_in, names_out), out_shape=...  6.48 us
    unnamed x76, local copies, waits for them, and re-layouts  4.54 us
  transfers between devices with their start and end apart: 22, of which 16 were waited for; matrix products, arithmetic and copies ran while one was open for 0% of the time, Pallas kernels for 3%

profile of v13, /device:TPU:0, one launch (start us, length us, event | category | flops | bytes accessed | tf_op | source)
XLA Modules:
  0.0 57.5 jit_solution(12902516996892583911)
XLA Ops:
  0.7 0.6 %copy-done.42 = f32[1,64]{1,0:T(1,128)S(1)} copy-done((f32[1,64]{1,0:T(1,128)S(1)}, f32[1,64]{1,0:T(1,128)}, u32[]{:S(2)}) %copy-start.42) | copy-done | bytes 280
  1.3 0.0 copy-done.40
  1.3 0.0 copy-start.36
  1.4 1.6 %shard_map.166 = f32[72,128]{1,0:T(8,128)} custom-call(f32[64,128]{1,0:T(8,128)} %refs_0_.1, s32[2,64]{1,0:T(2,128)S(1)} %bitcast.89, f32[1,64]{1,0:T(1,128)S(1)} %copy-done.42, s32[1,2]{1,0:T(1,128)} %refs_3_.3), custom_call_target="tpu_custom_call" | custom-call | tf_op jit(solution)/shard_map/pallas_call | solution.py:415
  3.0 3.0 %collective-permute-start.29 = (f32[72,128]{1,0:T(8,128)}, f32[72,128]{1,0:T(8,128)S(1)}, u32[]{:S(2)}, u32[]{:S(2)}) collective-permute-start(f32[72,128]{1,0:T(8,128)} %shard_map.166), channel_id=1, source_target_pairs={{0,1},{1,0},{2,3},{3,2},{4,5},{5,4},{6,7},{7,6},{8,9},{9,8},{10,11... | collective-permute-start | bytes 110600 | tf_op jit(solution)/shard_map/ppermute | solution.py:437
  6.1 0.6 %copy-done.30 = s32[2,256]{1,0:T(2,128)S(1)} copy-done((s32[2,256]{1,0:T(2,128)S(1)}, s32[2,256]{1,0:T(2,128)}, u32[]{:S(2)}) %copy-start.30) | copy-done | bytes 2072
  6.7 0.0 copy-done.28
  6.7 0.0 copy-done.27
  6.7 1.7 %shard_map.165 = (f32[18,64,128]{2,1,0:T(8,128)S(1)}, bf16[128,512]{1,0:T(8,128)(2,1)S(1)}, f32[64,512]{1,0:T(8,128)S(1)}, f32[64,256]{1,0:T(8,128)S(1)}, f32[17...) custom-call(f32[1024,128]{1,0:T(8,128)} %bitcast.61, f32[64,128]{1,0:T(8,128)S(1)} %copy-done.21, ...), custom_call_target="tpu_custom_call" | custom-call | flops 1000000 | bytes 4000000 | tf_op jit(solution)/shard_map/pallas_call | solution.py:415
  8.5 0.4 shard_map.167
  8.9 0.1 collective-permute-start.30
  9.0 1.2 %collective-permute-done.30.refs_10_ = f32[56,128]{1,0:T(8,128)S(1)} collective-permute-done((f32[56,128]{1,0:T(8,128)S(1)}, f32[56,128]{1,0:T(8,128)S(1)}, u32[]{:S(2)}, u32[]{:S(2)}) %collective-permute-start.30) | collective-permute-done | bytes 28704 | tf_op jit(solution)/shard_map/ppermute | solution.py:437
  10.2 2.4 %collective-permute-start.33 = (f32[3,128]{1,0:T(4,128)S(1)}, f32[3,128]{1,0:T(4,128)S(1)}, u32[]{:S(2)}, u32[]{:S(2)}) collective-permute-start(f32[3,128]{1,0:T(4,128)S(1)} %slice.603), channel_id=1, source_target_pairs={{0,7},{1,6},{2,5},{3,4},{4,3},{5,2},{6,1},{7,0},{8,15},{9,14},{10,... | collective-permute-start | bytes 4616 | tf_op jit(solution)/shard_map/ppermute | solution.py:437
  12.6 0.6 collective-permute-start.31
  13.2 0.3 collective-permute-start.32
  13.5 2.4 %collective-permute-done.31.refs_11_ = f32[56,128]{1,0:T(8,128)S(1)} collective-permute-done((f32[56,128]{1,0:T(8,128)S(1)}, f32[56,128]{1,0:T(8,128)S(1)}, u32[]{:S(2)}, u32[]{:S(2)}) %collective-permute-start.31) | collective-permute-done | bytes 28704 | tf_op jit(solution)/shard_map/ppermute | solution.py:437
  16.1 1.1 %collective-permute-done.32 = f32[67,128]{1,0:T(8,128)S(1)} collective-permute-done((f32[67,128]{1,0:T(8,128)S(1)}, f32[67,128]{1,0:T(8,128)S(1)}, u32[]{:S(2)}, u32[]{:S(2)}) %collective-permute-start.32) | collective-permute-done | bytes 34336 | tf_op jit(solution)/shard_map/ppermute | solution.py:437
  17.1 0.1 scatter-add.30.refs_6_
  17.2 2.6 %collective-permute-start.36 = (f32[56,128]{1,0:T(8,128)S(1)}, f32[56,128]{1,0:T(8,128)S(1)}, u32[]{:S(2)}, u32[]{:S(2)}) collective-permute-start(f32[56,128]{1,0:T(8,128)S(1)} %scatter-add.30.refs_6_), channel_id=1, source_target_pairs={{0,26},{1,27},{2,24},{3,25},{4,30},{5,31},{6,28},{7,29},{8,18},{9,... | collective-permute-start | bytes 86024 | tf_op jit(solution)/shard_map/ppermute | solution.py:437
  19.8 0.2 collective-permute-start.35
  20.0 1.2 %collective-permute-start.34 = (f32[56,128]{1,0:T(8,128)S(1)}, f32[56,128]{1,0:T(8,128)S(1)}, u32[]{:S(2)}, u32[]{:S(2)}) collective-permute-start(f32[56,128]{1,0:T(8,128)S(1)} %scatter-add.30.refs_6_), channel_id=1, source_target_pairs={{0,10},{1,11},{2,8},{3,9},{4,14},{5,15},{6,12},{7,13},{8,2},{9,3},... | collective-permute-start | bytes 86024 | tf_op jit(solution)/shard_map/ppermute | solution.py:437
  21.3 1.1 %collective-permute-done.36.refs_9_ = f32[56,128]{1,0:T(8,128)S(1)} collective-permute-done((f32[56,128]{1,0:T(8,128)S(1)}, f32[56,128]{1,0:T(8,128)S(1)}, u32[]{:S(2)}, u32[]{:S(2)}) %collective-permute-start.36) | collective-permute-done | bytes 28704 | tf_op jit(solution)/shard_map/ppermute | solution.py:437
  22.4 1.7 %collective-permute-done.35.refs_8_ = f32[56,128]{1,0:T(8,128)S(1)} collective-permute-done((f32[56,128]{1,0:T(8,128)S(1)}, f32[56,128]{1,0:T(8,128)S(1)}, u32[]{:S(2)}, u32[]{:S(2)}) %collective-permute-start.35) | collective-permute-done | bytes 28704 | tf_op jit(solution)/shard_map/ppermute | solution.py:437
  24.0 0.8 %shard_map.168 = (f32[17,64,128]{2,1,0:T(8,128)S(1)}, f32[17,64,128]{2,1,0:T(8,128)S(1)}, f32[72,640]{1,0:T(8,128)S(1)}, f32[64,256]{1,0:T(8,128)S(1)}, f32[64,2...) custom-call(f32[18,64,128]{2,1,0:T(8,128)S(1)} %get-tuple-element.242.refs_0_, ...), custom_call_target="tpu_custom_call" | custom-call | tf_op jit(solution)/shard_map/pallas_call | solution.py:415
  24.9 1.2 %collective-permute-start.37 = (f32[24,128]{1,0:T(8,128)S(1)}, f32[24,128]{1,0:T(8,128)S(1)}, u32[]{:S(2)}, u32[]{:S(2)}) collective-permute-start(f32[24,128]{1,0:T(8,128)S(1)} %get-tuple-element.258), channel_id=1, source_target_pairs={{0,2},{1,3},{2,0},{3,1},{4,6},{5,7},{6,4},{7,5},{8,10},{9,11},{10,... | collective-permute-start | bytes 36872 | tf_op jit(solution)/shard_map/ppermute | solution.py:437
  26.1 0.8 %collective-permute-done.37.refs_12_ = f32[24,128]{1,0:T(8,128)S(1)} collective-permute-done((f32[24,128]{1,0:T(8,128)S(1)}, f32[24,128]{1,0:T(8,128)S(1)}, u32[]{:S(2)}, u32[]{:S(2)}) %collective-permute-start.37) | collective-permute-done | bytes 12320 | tf_op jit(solution)/shard_map/ppermute | solution.py:437
  26.9 1.4 %collective-permute-start.40 = (f32[3,128]{1,0:T(4,128)S(1)}, f32[3,128]{1,0:T(4,128)S(1)}, u32[]{:S(2)}, u32[]{:S(2)}) collective-permute-start(f32[3,128]{1,0:T(4,128)S(1)} %slice.615), channel_id=1, source_target_pairs={{0,7},{1,6},{2,5},{3,4},{4,3},{5,2},{6,1},{7,0},{8,15},{9,14},{10,... | collective-permute-start | bytes 4616 | tf_op jit(solution)/shard_map/ppermute | solution.py:437
  28.4 0.6 %copy-done.12 = f32[24,128]{1,0:T(8,128)} copy-done((f32[24,128]{1,0:T(8,128)}, f32[24,128]{1,0:T(8,128)S(1)}, u32[]{:S(2)}) %copy-start.12) | copy-done | bytes 12312
  29.0 0.4 collective-permute-start.38
  29.4 1.6 %collective-permute-start.39 = (f32[67,128]{1,0:T(8,128)S(1)}, f32[67,128]{1,0:T(8,128)S(1)}, u32[]{:S(2)}, u32[]{:S(2)}) collective-permute-start(f32[67,128]{1,0:T(8,128)S(1)} %pad_maximum_fusion.13), channel_id=1, source_target_pairs={{0,1},{1,0},{2,3},{3,2},{4,5},{5,4},{6,7},{7,6},{8,9},{9,8},{10,11... | collective-permute-start | bytes 102920 | tf_op jit(solution)/shard_map/ppermute | solution.py:437
  31.0 1.2 %collective-permute-done.38.refs_13_ = f32[24,128]{1,0:T(8,128)S(1)} collective-permute-done((f32[24,128]{1,0:T(8,128)S(1)}, f32[24,128]{1,0:T(8,128)S(1)}, u32[]{:S(2)}, u32[]{:S(2)}) %collective-permute-start.38) | collective-permute-done | bytes 12320 | tf_op jit(solution)/shard_map/ppermute | solution.py:437
  32.2 0.6 copy-done.8
  32.8 0.6 %collective-permute-done.39 = f32[67,128]{1,0:T(8,128)S(1)} collective-permute-done((f32[67,128]{1,0:T(8,128)S(1)}, f32[67,128]{1,0:T(8,128)S(1)}, u32[]{:S(2)}, u32[]{:S(2)}) %collective-permute-start.39) | collective-permute-done | bytes 34336 | tf_op jit(solution)/shard_map/ppermute | solution.py:437
  33.4 0.1 scatter-add.31.refs_8_
  33.5 0.0 copy-start.16
  33.5 1.0 %collective-permute-start.43 = (f32[24,128]{1,0:T(8,128)S(1)}, f32[24,128]{1,0:T(8,128)S(1)}, u32[]{:S(2)}, u32[]{:S(2)}) collective-permute-start(f32[24,128]{1,0:T(8,128)S(1)} %scatter-add.31.refs_8_), channel_id=1, source_target_pairs={{0,26},{1,27},{2,24},{3,25},{4,30},{5,31},{6,28},{7,29},{8,18},{9,... | collective-permute-start | bytes 36872 | tf_op jit(solution)/shard_map/ppermute | solution.py:437
  34.5 0.5 collective-permute-start.42
  35.0 1.9 %collective-permute-start.41 = (f32[24,128]{1,0:T(8,128)S(1)}, f32[24,128]{1,0:T(8,128)S(1)}, u32[]{:S(2)}, u32[]{:S(2)}) collective-permute-start(f32[24,128]{1,0:T(8,128)S(1)} %scatter-add.31.refs_8_), channel_id=1, source_target_pairs={{0,10},{1,11},{2,8},{3,9},{4,14},{5,15},{6,12},{7,13},{8,2},{9,3},... | collective-permute-start | bytes 36872 | tf_op jit(solution)/shard_map/ppermute | solution.py:437
  36.9 0.0 copy-start.3
  37.0 1.6 %collective-permute-done.43.refs_11_ = f32[24,128]{1,0:T(8,128)S(1)} collective-permute-done((f32[24,128]{1,0:T(8,128)S(1)}, f32[24,128]{1,0:T(8,128)S(1)}, u32[]{:S(2)}, u32[]{:S(2)}) %collective-permute-start.43) | collective-permute-done | bytes 12320 | tf_op jit(solution)/shard_map/ppermute | solution.py:437
  38.5 0.1 collective-permute-done.42.refs_10_
  38.7 0.0 collective-permute-done.41.refs_9_
  38.7 0.7 %copy-done.17 = f32[24,128]{1,0:T(8,128)S(1)} copy-done((f32[24,128]{1,0:T(8,128)S(1)}, f32[24,128]{1,0:T(8,128)}, u32[]{:S(2)}) %copy-start.17) | copy-done | bytes 12312
  39.4 0.7 %shard_map.169 = (f32[17,64,128]{2,1,0:T(8,128)S(1)}, f32[17,64,128]{2,1,0:T(8,128)S(1)}, f32[72,640]{1,0:T(8,128)S(1)}, f32[64,256]{1,0:T(8,128)S(1)}, f32[64,2...) custom-call(f32[18,64,128]{2,1,0:T(8,128)S(1)} %get-tuple-element.242.refs_0_, ...), custom_call_target="tpu_custom_call" | custom-call | tf_op jit(solution)/shard_map/pallas_call | solution.py:415
  40.1 0.7 %collective-permute-start.44 = (f32[24,128]{1,0:T(8,128)S(1)}, f32[24,128]{1,0:T(8,128)S(1)}, u32[]{:S(2)}, u32[]{:S(2)}) collective-permute-start(f32[24,128]{1,0:T(8,128)S(1)} %get-tuple-element.265), channel_id=1, source_target_pairs={{0,2},{1,3},{2,0},{3,1},{4,6},{5,7},{6,4},{7,5},{8,10},{9,11},{10,... | collective-permute-start | bytes 36872 | tf_op jit(solution)/shard_map/ppermute | solution.py:437
  40.8 0.8 %collective-permute-done.44.refs_12_ = f32[24,128]{1,0:T(8,128)S(1)} collective-permute-done((f32[24,128]{1,0:T(8,128)S(1)}, f32[24,128]{1,0:T(8,128)S(1)}, u32[]{:S(2)}, u32[]{:S(2)}) %collective-permute-start.44) | collective-permute-done | bytes 12320 | tf_op jit(solution)/shard_map/ppermute | solution.py:437
  41.7 2.6 %collective-permute-start.47 = (f32[3,128]{1,0:T(4,128)S(1)}, f32[3,128]{1,0:T(4,128)S(1)}, u32[]{:S(2)}, u32[]{:S(2)}) collective-permute-start(f32[3,128]{1,0:T(4,128)S(1)} %slice.627), channel_id=1, source_target_pairs={{0,7},{1,6},{2,5},{3,4},{4,3},{5,2},{6,1},{7,0},{8,15},{9,14},{10,... | collective-permute-start | bytes 4616 | tf_op jit(solution)/shard_map/ppermute | solution.py:437
  44.3 0.3 collective-permute-start.45
  44.6 0.5 collective-permute-start.46
  45.1 2.4 %collective-permute-done.45.refs_13_ = f32[24,128]{1,0:T(8,128)S(1)} collective-permute-done((f32[24,128]{1,0:T(8,128)S(1)}, f32[24,128]{1,0:T(8,128)S(1)}, u32[]{:S(2)}, u32[]{:S(2)}) %collective-permute-start.45) | collective-permute-done | bytes 12320 | tf_op jit(solution)/shard_map/ppermute | solution.py:437
  47.5 1.0 %collective-permute-done.46 = f32[67,128]{1,0:T(8,128)S(1)} collective-permute-done((f32[67,128]{1,0:T(8,128)S(1)}, f32[67,128]{1,0:T(8,128)S(1)}, u32[]{:S(2)}, u32[]{:S(2)}) %collective-permute-start.46) | collective-permute-done | bytes 34336 | tf_op jit(solution)/shard_map/ppermute | solution.py:437
  48.6 0.1 scatter-add.34.refs_8_
  48.6 1.1 %collective-permute-start.50 = (f32[24,128]{1,0:T(8,128)S(1)}, f32[24,128]{1,0:T(8,128)S(1)}, u32[]{:S(2)}, u32[]{:S(2)}) collective-permute-start(f32[24,128]{1,0:T(8,128)S(1)} %scatter-add.34.refs_8_), channel_id=1, source_target_pairs={{0,26},{1,27},{2,24},{3,25},{4,30},{5,31},{6,28},{7,29},{8,18},{9,... | collective-permute-start | bytes 36872 | tf_op jit(solution)/shard_map/ppermute | solution.py:437
  49.7 1.9 %collective-permute-start.49 = (f32[24,128]{1,0:T(8,128)S(1)}, f32[24,128]{1,0:T(8,128)S(1)}, u32[]{:S(2)}, u32[]{:S(2)}) collective-permute-start(f32[24,128]{1,0:T(8,128)S(1)} %scatter-add.34.refs_8_), channel_id=1, source_target_pairs={{0,18},{1,19},{2,16},{3,17},{4,22},{5,23},{6,20},{7,21},{8,26},{9,... | collective-permute-start | bytes 36872 | tf_op jit(solution)/shard_map/ppermute | solution.py:437
  51.7 2.0 %collective-permute-done.50.refs_11_ = f32[24,128]{1,0:T(8,128)S(1)} collective-permute-done((f32[24,128]{1,0:T(8,128)S(1)}, f32[24,128]{1,0:T(8,128)S(1)}, u32[]{:S(2)}, u32[]{:S(2)}) %collective-permute-start.50) | collective-permute-done | bytes 12320 | tf_op jit(solution)/shard_map/ppermute | solution.py:437
  53.6 0.1 collective-permute-done.49.refs_10_
  53.7 1.0 %collective-permute-done.48.refs_9_ = f32[24,128]{1,0:T(8,128)S(1)} collective-permute-done((f32[24,128]{1,0:T(8,128)S(1)}, f32[24,128]{1,0:T(8,128)S(1)}, u32[]{:S(2)}, u32[]{:S(2)}) %collective-permute-start.48) | collective-permute-done | bytes 12320 | tf_op jit(solution)/shard_map/ppermute | solution.py:437
  54.8 0.0 copy-start.39
  54.8 1.3 %shard_map.170 = (f32[1024,128]{1,0:T(8,128)}, f32[1,128]{1,0:T(1,128)S(1)}, f32[64,128]{1,0:T(8,128)S(1)}, f32[64,256]{1,0:T(8,128)}, f32[1,128]{1,0:T(1,128)S(1)}) custom-call(f32[18,64,128]{2,1,0:T(8,128)S(1)} %get-tuple-element.242.refs_0_, bf16[128,512]{1,0:T(8,128)(2,1)S(1)} %get-tuple-element.243.refs_1_, f32[64,256]{1,0:T(8,128)S(1)} %get-tuple-element.260.refs_2_, ...), custom_call_target="tpu_custom_call" | custom-call | tf_op jit(solution)/shard_map/pallas_call | solution.py:415
  56.3 0.5 copy-done.29
  56.8 0.0 copy-done.31
  56.8 0.0 copy-done.33
  56.9 0.5 copy-done.48
  57.4 0.1 copy-done.47
  (108 shorter events, 0.4 us)
Async XLA Ops:
  0.6 0.7 %copy-start.42 = (f32[1,64]{1,0:T(1,128)S(1)}, f32[1,64]{1,0:T(1,128)}, u32[]{:S(2)}) copy-start(f32[1,64]{1,0:T(1,128)} %refs_2_.3) | copy-start | bytes 772
  0.6 0.7 %copy-start.40 = (s32[2,1,64]{2,1,0:T(1,128)S(1)}, s32[2,1,64]{2,1,0:T(1,128)}, u32[]{:S(2)}) copy-start(s32[2,1,64]{2,1,0:T(1,128)} %param.43) | copy-start | bytes 1540
  1.3 4.7 %copy-start.21 = (f32[64,128]{1,0:T(8,128)S(1)}, f32[64,128]{1,0:T(8,128)}, u32[]{:S(2)}) copy-start(f32[64,128]{1,0:T(8,128)} %refs_0_.1) | copy-start | bytes 98308
  1.3 4.7 %copy-start.25 = (f32[64,128]{1,0:T(8,128)S(1)}, f32[64,128]{1,0:T(8,128)}, u32[]{:S(2)}) copy-start(f32[64,128]{1,0:T(8,128)} %refs_2_.2) | copy-start | bytes 98308
  1.3 4.7 %copy-start.32 = (f32[256]{0:T(256)S(1)}, f32[256]{0:T(256)}, u32[]{:S(2)}) copy-start(f32[256]{0:T(256)} %param.42) | copy-start | bytes 3076
  1.3 4.7 %copy-start.34 = (s32[256]{0:T(256)S(1)}, s32[256]{0:T(256)}, u32[]{:S(2)}) copy-start(s32[256]{0:T(256)} %param.46) | copy-start | bytes 3076
  1.3 4.7 %copy-start.36 = (f32[256]{0:T(256)S(1)}, f32[256]{0:T(256)}, u32[]{:S(2)}) copy-start(f32[256]{0:T(256)} %param.48) | copy-start | bytes 3076
  1.4 4.7 %copy-start.38 = (f32[256]{0:T(256)S(1)}, f32[256]{0:T(256)}, u32[]{:S(2)}) copy-start(f32[256]{0:T(256)} %param.47) | copy-start | bytes 3076
  3.0 5.5 %collective-permute-start.29 = (f32[72,128]{1,0:T(8,128)}, f32[72,128]{1,0:T(8,128)S(1)}, u32[]{:S(2)}, u32[]{:S(2)}) collective-permute-start(f32[72,128]{1,0:T(8,128)} %shard_map.166), channel_id=1, source_target_pairs={{0,1},{1,0},{2,3},{3,2},{4,5},{5,4},{6,7},{7,6},{8,9},{9,8},{10,11... | collective-permute-start | bytes 110600 | tf_op jit(solution)/shard_map/ppermute | solution.py:437
  6.0 0.7 %copy-start.30 = (s32[2,256]{1,0:T(2,128)S(1)}, s32[2,256]{1,0:T(2,128)}, u32[]{:S(2)}) copy-start(s32[2,256]{1,0:T(2,128)} %refs_6_.1) | copy-start | bytes 6148
  6.0 0.7 %copy-start.28 = (s32[1,2048]{1,0:T(1,128)S(1)}, s32[1,2048]{1,0:T(1,128)}, u32[]{:S(2)}) copy-start(s32[1,2048]{1,0:T(1,128)} %param.40) | copy-start | bytes 24580
  6.0 0.7 %copy-start.27 = (f32[16,128]{1,0:T(8,128)S(1)}, f32[16,128]{1,0:T(8,128)}, u32[]{:S(2)}) copy-start(f32[16,128]{1,0:T(8,128)} %refs_3_.2) | copy-start | bytes 24580
  6.0 0.7 %copy-start.45 = (f32[1,128]{1,0:T(1,128)S(1)}, f32[1,128]{1,0:T(1,128)}, u32[]{:S(2)}) copy-start(f32[1,128]{1,0:T(1,128)} %refs_4_.1) | copy-start | bytes 1540
  6.7 1.8 %copy-start.23 = (f32[72,128]{1,0:T(8,128)S(1)}, f32[72,128]{1,0:T(8,128)}, u32[]{:S(2)}) copy-start(f32[72,128]{1,0:T(8,128)} %shard_map.166) | copy-start | bytes 110596
  8.9 1.3 %collective-permute-start.30 = (f32[56,128]{1,0:T(8,128)S(1)}, f32[56,128]{1,0:T(8,128)S(1)}, u32[]{:S(2)}, u32[]{:S(2)}) collective-permute-start(f32[56,128]{1,0:T(8,128)S(1)} %get-tuple-element.251), channel_id=1, source_target_pairs={{0,2},{1,3},{2,0},{3,1},{4,6},{5,7},{6,4},{7,5},{8,10},{9,11},{10,... | collective-permute-start | bytes 86024 | tf_op jit(solution)/shard_map/ppermute | solution.py:437
  10.2 5.9 %collective-permute-start.33 = (f32[3,128]{1,0:T(4,128)S(1)}, f32[3,128]{1,0:T(4,128)S(1)}, u32[]{:S(2)}, u32[]{:S(2)}) collective-permute-start(f32[3,128]{1,0:T(4,128)S(1)} %slice.603), channel_id=1, source_target_pairs={{0,7},{1,6},{2,5},{3,4},{4,3},{5,2},{6,1},{7,0},{8,15},{9,14},{10,... | collective-permute-start | bytes 4616 | tf_op jit(solution)/shard_map/ppermute | solution.py:437
  12.6 3.4 %collective-permute-start.31 = (f32[56,128]{1,0:T(8,128)S(1)}, f32[56,128]{1,0:T(8,128)S(1)}, u32[]{:S(2)}, u32[]{:S(2)}) collective-permute-start(f32[56,128]{1,0:T(8,128)S(1)} %pad_maximum_fusion.15), channel_id=1, source_target_pairs={{0,6},{1,7},{2,4},{3,5},{4,2},{5,3},{6,0},{7,1},{8,14},{9,15},{10,... | collective-permute-start | bytes 86024 | tf_op jit(solution)/shard_map/ppermute | solution.py:437
  13.2 4.0 %collective-permute-start.32 = (f32[67,128]{1,0:T(8,128)S(1)}, f32[67,128]{1,0:T(8,128)S(1)}, u32[]{:S(2)}, u32[]{:S(2)}) collective-permute-start(f32[67,128]{1,0:T(8,128)S(1)} %pad_maximum_fusion.12), channel_id=1, source_target_pairs={{0,1},{1,0},{2,3},{3,2},{4,5},{5,4},{6,7},{7,6},{8,9},{9,8},{10,11... | collective-permute-start | bytes 102920 | tf_op jit(solution)/shard_map/ppermute | solution.py:437
  17.2 5.2 %collective-permute-start.36 = (f32[56,128]{1,0:T(8,128)S(1)}, f32[56,128]{1,0:T(8,128)S(1)}, u32[]{:S(2)}, u32[]{:S(2)}) collective-permute-start(f32[56,128]{1,0:T(8,128)S(1)} %scatter-add.30.refs_6_), channel_id=1, source_target_pairs={{0,26},{1,27},{2,24},{3,25},{4,30},{5,31},{6,28},{7,29},{8,18},{9,... | collective-permute-start | bytes 86024 | tf_op jit(solution)/shard_map/ppermute | solution.py:437
  19.8 4.2 %collective-permute-start.35 = (f32[56,128]{1,0:T(8,128)S(1)}, f32[56,128]{1,0:T(8,128)S(1)}, u32[]{:S(2)}, u32[]{:S(2)}) collective-permute-start(f32[56,128]{1,0:T(8,128)S(1)} %scatter-add.30.refs_6_), channel_id=1, source_target_pairs={{0,18},{1,19},{2,16},{3,17},{4,22},{5,23},{6,20},{7,21},{8,26},{9,... | collective-permute-start | bytes 86024 | tf_op jit(solution)/shard_map/ppermute | solution.py:437
  20.0 4.0 %collective-permute-start.34 = (f32[56,128]{1,0:T(8,128)S(1)}, f32[56,128]{1,0:T(8,128)S(1)}, u32[]{:S(2)}, u32[]{:S(2)}) collective-permute-start(f32[56,128]{1,0:T(8,128)S(1)} %scatter-add.30.refs_6_), channel_id=1, source_target_pairs={{0,10},{1,11},{2,8},{3,9},{4,14},{5,15},{6,12},{7,13},{8,2},{9,3},... | collective-permute-start | bytes 86024 | tf_op jit(solution)/shard_map/ppermute | solution.py:437
  24.8 4.5 %copy-start = (f32[64,256]{1,0:T(8,128)}, f32[64,256]{1,0:T(8,128)S(1)}, u32[]{:S(2)}) copy-start(f32[64,256]{1,0:T(8,128)S(1)} %get-tuple-element.253.refs_2_) | copy-start | bytes 196612
  24.9 4.5 %copy-start.2 = (f32[64,256]{1,0:T(8,128)}, f32[64,256]{1,0:T(8,128)S(1)}, u32[]{:S(2)}) copy-start(f32[64,256]{1,0:T(8,128)S(1)} %get-tuple-element.257.refs_7_) | copy-start | bytes 196612
  24.9 2.1 %collective-permute-start.37 = (f32[24,128]{1,0:T(8,128)S(1)}, f32[24,128]{1,0:T(8,128)S(1)}, u32[]{:S(2)}, u32[]{:S(2)}) collective-permute-start(f32[24,128]{1,0:T(8,128)S(1)} %get-tuple-element.258), channel_id=1, source_target_pairs={{0,2},{1,3},{2,0},{3,1},{4,6},{5,7},{6,4},{7,5},{8,10},{9,11},{10,... | collective-permute-start | bytes 36872 | tf_op jit(solution)/shard_map/ppermute | solution.py:437
  26.9 5.9 %collective-permute-start.40 = (f32[3,128]{1,0:T(4,128)S(1)}, f32[3,128]{1,0:T(4,128)S(1)}, u32[]{:S(2)}, u32[]{:S(2)}) collective-permute-start(f32[3,128]{1,0:T(4,128)S(1)} %slice.615), channel_id=1, source_target_pairs={{0,7},{1,6},{2,5},{3,4},{4,3},{5,2},{6,1},{7,0},{8,15},{9,14},{10,... | collective-permute-start | bytes 4616 | tf_op jit(solution)/shard_map/ppermute | solution.py:437
  28.4 0.6 %copy-start.12 = (f32[24,128]{1,0:T(8,128)}, f32[24,128]{1,0:T(8,128)S(1)}, u32[]{:S(2)}) copy-start(f32[24,128]{1,0:T(8,128)S(1)} %collective-permute-done.37.refs_12_) | copy-start | bytes 36868
  29.0 3.2 %collective-permute-start.38 = (f32[24,128]{1,0:T(8,128)S(1)}, f32[24,128]{1,0:T(8,128)S(1)}, u32[]{:S(2)}, u32[]{:S(2)}) collective-permute-start(f32[24,128]{1,0:T(8,128)S(1)} %pad_maximum_fusion.17), channel_id=1, source_target_pairs={{0,6},{1,7},{2,4},{3,5},{4,2},{5,3},{6,0},{7,1},{8,14},{9,15},{10,... | collective-permute-start | bytes 36872 | tf_op jit(solution)/shard_map/ppermute | solution.py:437
  29.4 4.0 %collective-permute-start.39 = (f32[67,128]{1,0:T(8,128)S(1)}, f32[67,128]{1,0:T(8,128)S(1)}, u32[]{:S(2)}, u32[]{:S(2)}) collective-permute-start(f32[67,128]{1,0:T(8,128)S(1)} %pad_maximum_fusion.13), channel_id=1, source_target_pairs={{0,1},{1,0},{2,3},{3,2},{4,5},{5,4},{6,7},{7,6},{8,9},{9,8},{10,11... | collective-permute-start | bytes 102920 | tf_op jit(solution)/shard_map/ppermute | solution.py:437
  32.2 0.6 %copy-start.8 = (f32[24,128]{1,0:T(8,128)}, f32[24,128]{1,0:T(8,128)S(1)}, u32[]{:S(2)}) copy-start(f32[24,128]{1,0:T(8,128)S(1)} %collective-permute-done.38.refs_13_) | copy-start | bytes 36868
  33.5 3.4 %copy-start.16 = (f32[24,128]{1,0:T(8,128)}, f32[24,128]{1,0:T(8,128)S(1)}, u32[]{:S(2)}) copy-start(f32[24,128]{1,0:T(8,128)S(1)} %scatter-add.31.refs_8_) | copy-start | bytes 36868
  33.5 5.0 %collective-permute-start.43 = (f32[24,128]{1,0:T(8,128)S(1)}, f32[24,128]{1,0:T(8,128)S(1)}, u32[]{:S(2)}, u32[]{:S(2)}) collective-permute-start(f32[24,128]{1,0:T(8,128)S(1)} %scatter-add.31.refs_8_), channel_id=1, source_target_pairs={{0,26},{1,27},{2,24},{3,25},{4,30},{5,31},{6,28},{7,29},{8,18},{9,... | collective-permute-start | bytes 36872 | tf_op jit(solution)/shard_map/ppermute | solution.py:437
  34.5 4.1 %collective-permute-start.42 = (f32[24,128]{1,0:T(8,128)S(1)}, f32[24,128]{1,0:T(8,128)S(1)}, u32[]{:S(2)}, u32[]{:S(2)}) collective-permute-start(f32[24,128]{1,0:T(8,128)S(1)} %scatter-add.31.refs_8_), channel_id=1, source_target_pairs={{0,18},{1,19},{2,16},{3,17},{4,22},{5,23},{6,20},{7,21},{8,26},{9,... | collective-permute-start | bytes 36872 | tf_op jit(solution)/shard_map/ppermute | solution.py:437
  35.0 3.6 %collective-permute-start.41 = (f32[24,128]{1,0:T(8,128)S(1)}, f32[24,128]{1,0:T(8,128)S(1)}, u32[]{:S(2)}, u32[]{:S(2)}) collective-permute-start(f32[24,128]{1,0:T(8,128)S(1)} %scatter-add.31.refs_8_), channel_id=1, source_target_pairs={{0,10},{1,11},{2,8},{3,9},{4,14},{5,15},{6,12},{7,13},{8,2},{9,3},... | collective-permute-start | bytes 36872 | tf_op jit(solution)/shard_map/ppermute | solution.py:437
  36.9 1.8 %copy-start.9 = (f32[24,128]{1,0:T(8,128)S(1)}, f32[24,128]{1,0:T(8,128)}, u32[]{:S(2)}) copy-start(f32[24,128]{1,0:T(8,128)} %copy-done.8) | copy-start | bytes 36868
  36.9 1.8 %copy-start.13 = (f32[24,128]{1,0:T(8,128)S(1)}, f32[24,128]{1,0:T(8,128)}, u32[]{:S(2)}) copy-start(f32[24,128]{1,0:T(8,128)} %copy-done.12) | copy-start | bytes 36868
  36.9 1.8 %copy-start.1 = (f32[64,256]{1,0:T(8,128)S(1)}, f32[64,256]{1,0:T(8,128)}, u32[]{:S(2)}) copy-start(f32[64,256]{1,0:T(8,128)} %copy-done) | copy-start | bytes 196612
  36.9 1.8 %copy-start.3 = (f32[64,256]{1,0:T(8,128)S(1)}, f32[64,256]{1,0:T(8,128)}, u32[]{:S(2)}) copy-start(f32[64,256]{1,0:T(8,128)} %copy-done.2) | copy-start | bytes 196612
  38.7 0.7 %copy-start.17 = (f32[24,128]{1,0:T(8,128)S(1)}, f32[24,128]{1,0:T(8,128)}, u32[]{:S(2)}) copy-start(f32[24,128]{1,0:T(8,128)} %copy-done.16) | copy-start | bytes 36868
  40.1 1.5 %collective-permute-start.44 = (f32[24,128]{1,0:T(8,128)S(1)}, f32[24,128]{1,0:T(8,128)S(1)}, u32[]{:S(2)}, u32[]{:S(2)}) collective-permute-start(f32[24,128]{1,0:T(8,128)S(1)} %get-tuple-element.265), channel_id=1, source_target_pairs={{0,2},{1,3},{2,0},{3,1},{4,6},{5,7},{6,4},{7,5},{8,10},{9,11},{10,... | collective-permute-start | bytes 36872 | tf_op jit(solution)/shard_map/ppermute | solution.py:437
  41.7 5.8 %collective-permute-start.47 = (f32[3,128]{1,0:T(4,128)S(1)}, f32[3,128]{1,0:T(4,128)S(1)}, u32[]{:S(2)}, u32[]{:S(2)}) collective-permute-start(f32[3,128]{1,0:T(4,128)S(1)} %slice.627), channel_id=1, source_target_pairs={{0,7},{1,6},{2,5},{3,4},{4,3},{5,2},{6,1},{7,0},{8,15},{9,14},{10,... | collective-permute-start | bytes 4616 | tf_op jit(solution)/shard_map/ppermute | solution.py:437
  44.3 3.2 %collective-permute-start.45 = (f32[24,128]{1,0:T(8,128)S(1)}, f32[24,128]{1,0:T(8,128)S(1)}, u32[]{:S(2)}, u32[]{:S(2)}) collective-permute-start(f32[24,128]{1,0:T(8,128)S(1)} %pad_maximum_fusion.19), channel_id=1, source_target_pairs={{0,6},{1,7},{2,4},{3,5},{4,2},{5,3},{6,0},{7,1},{8,14},{9,15},{10,... | collective-permute-start | bytes 36872 | tf_op jit(solution)/shard_map/ppermute | solution.py:437
  44.6 4.0 %collective-permute-start.46 = (f32[67,128]{1,0:T(8,128)S(1)}, f32[67,128]{1,0:T(8,128)S(1)}, u32[]{:S(2)}, u32[]{:S(2)}) collective-permute-start(f32[67,128]{1,0:T(8,128)S(1)} %pad_maximum_fusion.14), channel_id=1, source_target_pairs={{0,1},{1,0},{2,3},{3,2},{4,5},{5,4},{6,7},{7,6},{8,9},{9,8},{10,11... | collective-permute-start | bytes 102920 | tf_op jit(solution)/shard_map/ppermute | solution.py:437
  48.6 5.0 %collective-permute-start.50 = (f32[24,128]{1,0:T(8,128)S(1)}, f32[24,128]{1,0:T(8,128)S(1)}, u32[]{:S(2)}, u32[]{:S(2)}) collective-permute-start(f32[24,128]{1,0:T(8,128)S(1)} %scatter-add.34.refs_8_), channel_id=1, source_target_pairs={{0,26},{1,27},{2,24},{3,25},{4,30},{5,31},{6,28},{7,29},{8,18},{9,... | collective-permute-start | bytes 36872 | tf_op jit(solution)/shard_map/ppermute | solution.py:437
  49.7 4.0 %collective-permute-start.49 = (f32[24,128]{1,0:T(8,128)S(1)}, f32[24,128]{1,0:T(8,128)S(1)}, u32[]{:S(2)}, u32[]{:S(2)}) collective-permute-start(f32[24,128]{1,0:T(8,128)S(1)} %scatter-add.34.refs_8_), channel_id=1, source_target_pairs={{0,18},{1,19},{2,16},{3,17},{4,22},{5,23},{6,20},{7,21},{8,26},{9,... | collective-permute-start | bytes 36872 | tf_op jit(solution)/shard_map/ppermute | solution.py:437
  51.6 3.1 %collective-permute-start.48 = (f32[24,128]{1,0:T(8,128)S(1)}, f32[24,128]{1,0:T(8,128)S(1)}, u32[]{:S(2)}, u32[]{:S(2)}) collective-permute-start(f32[24,128]{1,0:T(8,128)S(1)} %scatter-add.34.refs_8_), channel_id=1, source_target_pairs={{0,10},{1,11},{2,8},{3,9},{4,14},{5,15},{6,12},{7,13},{8,2},{9,3},... | collective-permute-start | bytes 36872 | tf_op jit(solution)/shard_map/ppermute | solution.py:437
  54.8 1.4 %copy-start.20 = (f32[64,16,128]{2,1,0:T(8,128)S(1)}, f32[64,16,128]{2,1,0:T(8,128)}, u32[]{:S(2)}) copy-start(f32[64,16,128]{2,1,0:T(8,128)} %param.36) | copy-start | bytes 1572868
  54.8 1.4 %copy-start.22 = (f32[64,128]{1,0:T(8,128)S(1)}, f32[64,128]{1,0:T(8,128)}, u32[]{:S(2)}) copy-start(f32[64,128]{1,0:T(8,128)} %refs_0_.1) | copy-start | bytes 98308
  54.8 1.5 %copy-start.26 = (f32[64,128]{1,0:T(8,128)S(1)}, f32[64,128]{1,0:T(8,128)}, u32[]{:S(2)}) copy-start(f32[64,128]{1,0:T(8,128)} %refs_2_.2) | copy-start | bytes 98308
  54.8 1.5 %copy-start.35 = (s32[256]{0:T(256)S(1)}, s32[256]{0:T(256)}, u32[]{:S(2)}) copy-start(s32[256]{0:T(256)} %param.46) | copy-start | bytes 3076
  54.8 1.5 %copy-start.37 = (f32[256]{0:T(256)S(1)}, f32[256]{0:T(256)}, u32[]{:S(2)}) copy-start(f32[256]{0:T(256)} %param.48) | copy-start | bytes 3076
  54.8 1.5 %copy-start.39 = (f32[256]{0:T(256)S(1)}, f32[256]{0:T(256)}, u32[]{:S(2)}) copy-start(f32[256]{0:T(256)} %param.47) | copy-start | bytes 3076
  54.8 1.5 %copy-start.41 = (s32[2,1,64]{2,1,0:T(1,128)S(1)}, s32[2,1,64]{2,1,0:T(1,128)}, u32[]{:S(2)}) copy-start(s32[2,1,64]{2,1,0:T(1,128)} %param.43) | copy-start | bytes 1540
  54.8 1.5 %copy-start.44 = (s32[1,2]{1,0:T(1,128)S(1)}, s32[1,2]{1,0:T(1,128)}, u32[]{:S(2)}) copy-start(s32[1,2]{1,0:T(1,128)} %refs_3_.3) | copy-start | bytes 28
  54.8 1.5 %copy-start.46 = (f32[1,128]{1,0:T(1,128)S(1)}, f32[1,128]{1,0:T(1,128)}, u32[]{:S(2)}) copy-start(f32[1,128]{1,0:T(1,128)} %refs_4_.1) | copy-start | bytes 1540
  56.1 0.7 %copy-start.29 = (s32[1,2048]{1,0:T(1,128)S(1)}, s32[1,2048]{1,0:T(1,128)}, u32[]{:S(2)}) copy-start(s32[1,2048]{1,0:T(1,128)} %param.40) | copy-start | bytes 24580
  56.2 0.7 %copy-start.31 = (s32[2,256]{1,0:T(2,128)S(1)}, s32[2,256]{1,0:T(2,128)}, u32[]{:S(2)}) copy-start(s32[2,256]{1,0:T(2,128)} %refs_6_.1) | copy-start | bytes 6148
  56.2 0.7 %copy-start.33 = (f32[256]{0:T(256)S(1)}, f32[256]{0:T(256)}, u32[]{:S(2)}) copy-start(f32[256]{0:T(256)} %param.42) | copy-start | bytes 3076
  56.2 0.7 %copy-start.43 = (f32[1,64]{1,0:T(1,128)S(1)}, f32[1,64]{1,0:T(1,128)}, u32[]{:S(2)}) copy-start(f32[1,64]{1,0:T(1,128)} %refs_2_.3) | copy-start | bytes 772
  56.9 0.5 copy-start.48
  56.9 0.6 %copy-start.47 = (f32[64,128]{1,0:T(8,128)}, f32[64,128]{1,0:T(8,128)S(1)}, u32[]{:S(2)}) copy-start(f32[64,128]{1,0:T(8,128)S(1)} %get-tuple-element.273) | copy-start | bytes 98308

commit v14 on v13

--- a/solution.py
+++ b/solution.py
@@ -483,7 +483,7 @@
     beside = swap(jnp.concatenate([prices, chip[techs:halo]], axis=0), 0, 1)
     other, squares = beside[: sizes.rows], beside[sizes.rows :]
     slab = merged(chip, across, hour // 2 % 2 == 0)
-    slab = slab.at[techs:halo].add(squares + diagonal)
+    slab = slab + jnp.pad(squares + diagonal, ((techs, slab.shape[0] - halo), (0, 0)))
     near, middle, far = [swap(slab, 4 * step + 1, 0) for step in (1, 2, 3)]
     parts = Bag(slab=slab, near=near, middle=middle, far=far, partner=partner, across=across)
     return in_order(prices, other), parts

time: 57.8 us -> 56 us (0.969)
  local copies, waits for them, and re-layouts: 4.77 us -> 2.69 us
  waiting for transfers between devices: 19.2 us -> 20 us
    unnamed x76 -> x34, local copies, waits for them, and re-layouts: 4.54 us -> 2.63 us
    ppermute x22, waiting for transfers between devices: 19.2 us -> 20 us  [swap(): return lax.ppermute(value, ('hours', 'region'), pairs)]
  transfers between devices with their start and end apart: 22 -> 22, of which waited for: 16 -> 15; matrix products, arithmetic and copies ran while one was open for 0% -> 0% of each run, Pallas kernels for 3% -> 3%
where the time goes in v14:
time: 56 us; the launch traced here: 55.8 us
  starting transfers between devices  25.4 us (45%)
  waiting for transfers between devices  20 us (36%)
  Pallas kernels  6.49 us (12%)
  local copies, waits for them, and re-layouts  2.69 us (5%)
  between operations  1.03 us (2%)
    ppermute x22, starting transfers between devices, swap(): return lax.ppermute(value, ('hours', 'region'), pairs)  25.4 us
    ppermute x22, waiting for transfers between devices, swap(): return lax.ppermute(value, ('hours', 'region'), pairs)  20 us
    pallas_call x6, Pallas kernels, call(): pl.pallas_call(functools.partial(kernel, names_in, names_out), out_shape=...  6.49 us
    unnamed x34, local copies, waits for them, and re-layouts  2.63 us
  transfers between devices with their start and end apart: 22, of which 15 were waited for; matrix products, arithmetic and copies ran while one was open for 0% of the time, Pallas kernels for 3%

profile of v14, /device:TPU:0, one launch (start us, length us, event | category | flops | bytes accessed | tf_op | source)
XLA Modules:
  0.0 55.8 jit_solution(4903160444539102216)
XLA Ops:
  0.6 0.0 copy-start.13
  0.6 0.0 copy-start.12
  0.7 0.6 %copy-done.13 = f32[1,64]{1,0:T(1,128)S(1)} copy-done((f32[1,64]{1,0:T(1,128)S(1)}, f32[1,64]{1,0:T(1,128)}, u32[]{:S(2)}) %copy-start.13) | copy-done | bytes 280
  1.3 0.0 copy-done.12
  1.3 0.0 copy-start.10
  1.4 0.0 copy-start.11
  1.4 1.6 %shard_map.166 = f32[72,128]{1,0:T(8,128)} custom-call(f32[64,128]{1,0:T(8,128)} %refs_0_.1, s32[2,64]{1,0:T(2,128)S(1)} %bitcast.89, f32[1,64]{1,0:T(1,128)S(1)} %copy-done.13, s32[1,2]{1,0:T(1,128)} %refs_3_.3), custom_call_target="tpu_custom_call" | custom-call | tf_op jit(solution)/shard_map/pallas_call | solution.py:415
  3.0 3.0 %collective-permute-start.29 = (f32[72,128]{1,0:T(8,128)}, f32[72,128]{1,0:T(8,128)S(1)}, u32[]{:S(2)}, u32[]{:S(2)}) collective-permute-start(f32[72,128]{1,0:T(8,128)} %shard_map.166), channel_id=1, source_target_pairs={{0,1},{1,0},{2,3},{3,2},{4,5},{5,4},{6,7},{7,6},{8,9},{9,8},{10,11... | collective-permute-start | bytes 110600 | tf_op jit(solution)/shard_map/ppermute | solution.py:437
  6.1 0.6 %copy-done.7 = s32[2,256]{1,0:T(2,128)S(1)} copy-done((s32[2,256]{1,0:T(2,128)S(1)}, s32[2,256]{1,0:T(2,128)}, u32[]{:S(2)}) %copy-start.7) | copy-done | bytes 2072
  6.7 0.0 copy-done.6
  6.7 0.0 copy-done.5
  6.7 1.7 %shard_map.165 = (f32[18,64,128]{2,1,0:T(8,128)S(1)}, bf16[128,512]{1,0:T(8,128)(2,1)S(1)}, f32[64,512]{1,0:T(8,128)S(1)}, f32[64,256]{1,0:T(8,128)S(1)}, f32[17...) custom-call(f32[1024,128]{1,0:T(8,128)} %bitcast.61, f32[64,128]{1,0:T(8,128)S(1)} %copy-done.1, ...), custom_call_target="tpu_custom_call" | custom-call | flops 1000000 | bytes 4000000 | tf_op jit(solution)/shard_map/pallas_call | solution.py:415
  8.5 0.0 collective-permute-done.29
  8.5 0.4 shard_map.167
  8.9 0.1 collective-permute-start.30
  9.0 1.2 %collective-permute-done.30.refs_10_ = f32[56,128]{1,0:T(8,128)S(1)} collective-permute-done((f32[56,128]{1,0:T(8,128)S(1)}, f32[56,128]{1,0:T(8,128)S(1)}, u32[]{:S(2)}, u32[]{:S(2)}) %collective-permute-start.30) | collective-permute-done | bytes 28704 | tf_op jit(solution)/shard_map/ppermute | solution.py:437
  10.2 2.4 %collective-permute-start.33 = (f32[3,128]{1,0:T(4,128)S(1)}, f32[3,128]{1,0:T(4,128)S(1)}, u32[]{:S(2)}, u32[]{:S(2)}) collective-permute-start(f32[3,128]{1,0:T(4,128)S(1)} %slice.448), channel_id=1, source_target_pairs={{0,7},{1,6},{2,5},{3,4},{4,3},{5,2},{6,1},{7,0},{8,15},{9,14},{10,... | collective-permute-start | bytes 4616 | tf_op jit(solution)/shard_map/ppermute | solution.py:437
  12.6 0.6 %collective-permute-start.31 = (f32[56,128]{1,0:T(8,128)S(1)}, f32[56,128]{1,0:T(8,128)S(1)}, u32[]{:S(2)}, u32[]{:S(2)}) collective-permute-start(f32[56,128]{1,0:T(8,128)S(1)} %pad_maximum_fusion.11), channel_id=1, source_target_pairs={{0,6},{1,7},{2,4},{3,5},{4,2},{5,3},{6,0},{7,1},{8,14},{9,15},{10,... | collective-permute-start | bytes 86024 | tf_op jit(solution)/shard_map/ppermute | solution.py:437
  13.2 0.4 collective-permute-start.32
  13.5 2.4 %collective-permute-done.31.refs_11_ = f32[56,128]{1,0:T(8,128)S(1)} collective-permute-done((f32[56,128]{1,0:T(8,128)S(1)}, f32[56,128]{1,0:T(8,128)S(1)}, u32[]{:S(2)}, u32[]{:S(2)}) %collective-permute-start.31) | collective-permute-done | bytes 28704 | tf_op jit(solution)/shard_map/ppermute | solution.py:437
  16.0 0.0 collective-permute-done.33
  16.0 1.1 %collective-permute-done.32 = f32[67,128]{1,0:T(8,128)S(1)} collective-permute-done((f32[67,128]{1,0:T(8,128)S(1)}, f32[67,128]{1,0:T(8,128)S(1)}, u32[]{:S(2)}, u32[]{:S(2)}) %collective-permute-start.32) | collective-permute-done | bytes 34336 | tf_op jit(solution)/shard_map/ppermute | solution.py:437
  17.2 2.6 %collective-permute-start.36 = (f32[56,128]{1,0:T(8,128)S(1)}, f32[56,128]{1,0:T(8,128)S(1)}, u32[]{:S(2)}, u32[]{:S(2)}) collective-permute-start(f32[56,128]{1,0:T(8,128)S(1)} %maximum_add_fusion.4.refs_6_), channel_id=1, source_target_pairs={{0,26},{1,27},{2,24},{3,25},{4,30},{5,31},{6,28},{7,29},{8,18},{9,... | collective-permute-start | bytes 86024 | tf_op jit(solution)/shard_map/ppermute | solution.py:437
  19.7 0.3 collective-permute-start.35
  20.0 1.2 %collective-permute-start.34 = (f32[56,128]{1,0:T(8,128)S(1)}, f32[56,128]{1,0:T(8,128)S(1)}, u32[]{:S(2)}, u32[]{:S(2)}) collective-permute-start(f32[56,128]{1,0:T(8,128)S(1)} %maximum_add_fusion.4.refs_6_), channel_id=1, source_target_pairs={{0,10},{1,11},{2,8},{3,9},{4,14},{5,15},{6,12},{7,13},{8,2},{9,3},... | collective-permute-start | bytes 86024 | tf_op jit(solution)/shard_map/ppermute | solution.py:437
  21.2 1.1 %collective-permute-done.36.refs_9_ = f32[56,128]{1,0:T(8,128)S(1)} collective-permute-done((f32[56,128]{1,0:T(8,128)S(1)}, f32[56,128]{1,0:T(8,128)S(1)}, u32[]{:S(2)}, u32[]{:S(2)}) %collective-permute-start.36) | collective-permute-done | bytes 28704 | tf_op jit(solution)/shard_map/ppermute | solution.py:437
  22.3 1.6 %collective-permute-done.35.refs_8_ = f32[56,128]{1,0:T(8,128)S(1)} collective-permute-done((f32[56,128]{1,0:T(8,128)S(1)}, f32[56,128]{1,0:T(8,128)S(1)}, u32[]{:S(2)}, u32[]{:S(2)}) %collective-permute-start.35) | collective-permute-done | bytes 28704 | tf_op jit(solution)/shard_map/ppermute | solution.py:437
  23.9 0.0 collective-permute-done.34.refs_7_
  23.9 0.8 %shard_map.168 = (f32[17,64,128]{2,1,0:T(8,128)S(1)}, f32[17,64,128]{2,1,0:T(8,128)S(1)}, f32[72,640]{1,0:T(8,128)S(1)}, f32[64,256]{1,0:T(8,128)S(1)}, f32[64,2...) custom-call(f32[18,64,128]{2,1,0:T(8,128)S(1)} %get-tuple-element.158.refs_0_, ...), custom_call_target="tpu_custom_call" | custom-call | tf_op jit(solution)/shard_map/pallas_call | solution.py:415
  24.7 1.3 %collective-permute-start.37 = (f32[24,128]{1,0:T(8,128)S(1)}, f32[24,128]{1,0:T(8,128)S(1)}, u32[]{:S(2)}, u32[]{:S(2)}) collective-permute-start(f32[24,128]{1,0:T(8,128)S(1)} %get-tuple-element.174), channel_id=1, source_target_pairs={{0,2},{1,3},{2,0},{3,1},{4,6},{5,7},{6,4},{7,5},{8,10},{9,11},{10,... | collective-permute-start | bytes 36872 | tf_op jit(solution)/shard_map/ppermute | solution.py:437
  26.0 0.8 %collective-permute-done.37.refs_12_ = f32[24,128]{1,0:T(8,128)S(1)} collective-permute-done((f32[24,128]{1,0:T(8,128)S(1)}, f32[24,128]{1,0:T(8,128)S(1)}, u32[]{:S(2)}, u32[]{:S(2)}) %collective-permute-start.37) | collective-permute-done | bytes 12320 | tf_op jit(solution)/shard_map/ppermute | solution.py:437
  26.9 1.4 %collective-permute-start.40 = (f32[3,128]{1,0:T(4,128)S(1)}, f32[3,128]{1,0:T(4,128)S(1)}, u32[]{:S(2)}, u32[]{:S(2)}) collective-permute-start(f32[3,128]{1,0:T(4,128)S(1)} %slice.459), channel_id=1, source_target_pairs={{0,7},{1,6},{2,5},{3,4},{4,3},{5,2},{6,1},{7,0},{8,15},{9,14},{10,... | collective-permute-start | bytes 4616 | tf_op jit(solution)/shard_map/ppermute | solution.py:437
  28.3 0.4 collective-permute-start.38
  28.7 1.5 %collective-permute-start.39 = (f32[67,128]{1,0:T(8,128)S(1)}, f32[67,128]{1,0:T(8,128)S(1)}, u32[]{:S(2)}, u32[]{:S(2)}) collective-permute-start(f32[67,128]{1,0:T(8,128)S(1)} %pad_maximum_fusion.9), channel_id=1, source_target_pairs={{0,1},{1,0},{2,3},{3,2},{4,5},{5,4},{6,7},{7,6},{8,9},{9,8},{10,11... | collective-permute-start | bytes 102920 | tf_op jit(solution)/shard_map/ppermute | solution.py:437
  30.2 1.3 %collective-permute-done.38.refs_13_ = f32[24,128]{1,0:T(8,128)S(1)} collective-permute-done((f32[24,128]{1,0:T(8,128)S(1)}, f32[24,128]{1,0:T(8,128)S(1)}, u32[]{:S(2)}, u32[]{:S(2)}) %collective-permute-start.38) | collective-permute-done | bytes 12320 | tf_op jit(solution)/shard_map/ppermute | solution.py:437
  31.5 0.0 collective-permute-done.40
  31.6 1.1 %collective-permute-done.39 = f32[67,128]{1,0:T(8,128)S(1)} collective-permute-done((f32[67,128]{1,0:T(8,128)S(1)}, f32[67,128]{1,0:T(8,128)S(1)}, u32[]{:S(2)}, u32[]{:S(2)}) %collective-permute-start.39) | collective-permute-done | bytes 34336 | tf_op jit(solution)/shard_map/ppermute | solution.py:437
  32.7 0.5 collective-permute-start.43
  33.2 0.9 %collective-permute-start.42 = (f32[24,128]{1,0:T(8,128)S(1)}, f32[24,128]{1,0:T(8,128)S(1)}, u32[]{:S(2)}, u32[]{:S(2)}) collective-permute-start(f32[24,128]{1,0:T(8,128)S(1)} %maximum_add_fusion.5.refs_8_), channel_id=1, source_target_pairs={{0,18},{1,19},{2,16},{3,17},{4,22},{5,23},{6,20},{7,21},{8,26},{9,... | collective-permute-start | bytes 36872 | tf_op jit(solution)/shard_map/ppermute | solution.py:437
  34.0 1.6 %collective-permute-start.41 = (f32[24,128]{1,0:T(8,128)S(1)}, f32[24,128]{1,0:T(8,128)S(1)}, u32[]{:S(2)}, u32[]{:S(2)}) collective-permute-start(f32[24,128]{1,0:T(8,128)S(1)} %maximum_add_fusion.5.refs_8_), channel_id=1, source_target_pairs={{0,10},{1,11},{2,8},{3,9},{4,14},{5,15},{6,12},{7,13},{8,2},{9,3},... | collective-permute-start | bytes 36872 | tf_op jit(solution)/shard_map/ppermute | solution.py:437
  35.7 2.0 %collective-permute-done.43.refs_11_ = f32[24,128]{1,0:T(8,128)S(1)} collective-permute-done((f32[24,128]{1,0:T(8,128)S(1)}, f32[24,128]{1,0:T(8,128)S(1)}, u32[]{:S(2)}, u32[]{:S(2)}) %collective-permute-start.43) | collective-permute-done | bytes 12320 | tf_op jit(solution)/shard_map/ppermute | solution.py:437
  37.7 0.0 collective-permute-done.42.refs_10_
  37.7 0.0 collective-permute-done.41.refs_9_
  37.7 0.7 %shard_map.169 = (f32[17,64,128]{2,1,0:T(8,128)S(1)}, f32[17,64,128]{2,1,0:T(8,128)S(1)}, f32[72,640]{1,0:T(8,128)S(1)}, f32[64,256]{1,0:T(8,128)S(1)}, f32[64,2...) custom-call(f32[18,64,128]{2,1,0:T(8,128)S(1)} %get-tuple-element.158.refs_0_, ...), custom_call_target="tpu_custom_call" | custom-call | tf_op jit(solution)/shard_map/pallas_call | solution.py:415
  38.4 0.9 %collective-permute-start.44 = (f32[24,128]{1,0:T(8,128)S(1)}, f32[24,128]{1,0:T(8,128)S(1)}, u32[]{:S(2)}, u32[]{:S(2)}) collective-permute-start(f32[24,128]{1,0:T(8,128)S(1)} %get-tuple-element.181), channel_id=1, source_target_pairs={{0,2},{1,3},{2,0},{3,1},{4,6},{5,7},{6,4},{7,5},{8,10},{9,11},{10,... | collective-permute-start | bytes 36872 | tf_op jit(solution)/shard_map/ppermute | solution.py:437
  39.3 0.8 %collective-permute-done.44.refs_12_ = f32[24,128]{1,0:T(8,128)S(1)} collective-permute-done((f32[24,128]{1,0:T(8,128)S(1)}, f32[24,128]{1,0:T(8,128)S(1)}, u32[]{:S(2)}, u32[]{:S(2)}) %collective-permute-start.44) | collective-permute-done | bytes 12320 | tf_op jit(solution)/shard_map/ppermute | solution.py:437
  40.1 2.5 %collective-permute-start.47 = (f32[3,128]{1,0:T(4,128)S(1)}, f32[3,128]{1,0:T(4,128)S(1)}, u32[]{:S(2)}, u32[]{:S(2)}) collective-permute-start(f32[3,128]{1,0:T(4,128)S(1)} %slice.470), channel_id=1, source_target_pairs={{0,7},{1,6},{2,5},{3,4},{4,3},{5,2},{6,1},{7,0},{8,15},{9,14},{10,... | collective-permute-start | bytes 4616 | tf_op jit(solution)/shard_map/ppermute | solution.py:437
  42.7 0.3 collective-permute-start.45
  43.0 0.5 collective-permute-start.46
  43.5 2.4 %collective-permute-done.45.refs_13_ = f32[24,128]{1,0:T(8,128)S(1)} collective-permute-done((f32[24,128]{1,0:T(8,128)S(1)}, f32[24,128]{1,0:T(8,128)S(1)}, u32[]{:S(2)}, u32[]{:S(2)}) %collective-permute-start.45) | collective-permute-done | bytes 12320 | tf_op jit(solution)/shard_map/ppermute | solution.py:437
  45.9 0.0 collective-permute-done.47
  45.9 1.0 %collective-permute-done.46 = f32[67,128]{1,0:T(8,128)S(1)} collective-permute-done((f32[67,128]{1,0:T(8,128)S(1)}, f32[67,128]{1,0:T(8,128)S(1)}, u32[]{:S(2)}, u32[]{:S(2)}) %collective-permute-start.46) | collective-permute-done | bytes 34336 | tf_op jit(solution)/shard_map/ppermute | solution.py:437
  47.0 1.1 %collective-permute-start.50 = (f32[24,128]{1,0:T(8,128)S(1)}, f32[24,128]{1,0:T(8,128)S(1)}, u32[]{:S(2)}, u32[]{:S(2)}) collective-permute-start(f32[24,128]{1,0:T(8,128)S(1)} %maximum_add_fusion.6.refs_8_), channel_id=1, source_target_pairs={{0,26},{1,27},{2,24},{3,25},{4,30},{5,31},{6,28},{7,29},{8,18},{9,... | collective-permute-start | bytes 36872 | tf_op jit(solution)/shard_map/ppermute | solution.py:437
  48.1 2.0 %collective-permute-start.49 = (f32[24,128]{1,0:T(8,128)S(1)}, f32[24,128]{1,0:T(8,128)S(1)}, u32[]{:S(2)}, u32[]{:S(2)}) collective-permute-start(f32[24,128]{1,0:T(8,128)S(1)} %maximum_add_fusion.6.refs_8_), channel_id=1, source_target_pairs={{0,18},{1,19},{2,16},{3,17},{4,22},{5,23},{6,20},{7,21},{8,26},{9,... | collective-permute-start | bytes 36872 | tf_op jit(solution)/shard_map/ppermute | solution.py:437
  50.0 0.0 collective-permute-start.48
  50.1 1.9 %collective-permute-done.50.refs_11_ = f32[24,128]{1,0:T(8,128)S(1)} collective-permute-done((f32[24,128]{1,0:T(8,128)S(1)}, f32[24,128]{1,0:T(8,128)S(1)}, u32[]{:S(2)}, u32[]{:S(2)}) %collective-permute-start.50) | collective-permute-done | bytes 12320 | tf_op jit(solution)/shard_map/ppermute | solution.py:437
  52.0 0.1 collective-permute-done.49.refs_10_
  52.1 1.1 %collective-permute-done.48.refs_9_ = f32[24,128]{1,0:T(8,128)S(1)} collective-permute-done((f32[24,128]{1,0:T(8,128)S(1)}, f32[24,128]{1,0:T(8,128)S(1)}, u32[]{:S(2)}, u32[]{:S(2)}) %collective-permute-start.48) | collective-permute-done | bytes 12320 | tf_op jit(solution)/shard_map/ppermute | solution.py:437
  53.2 1.3 %shard_map.170 = (f32[1024,128]{1,0:T(8,128)}, f32[1,128]{1,0:T(1,128)S(1)}, f32[64,128]{1,0:T(8,128)S(1)}, f32[64,256]{1,0:T(8,128)}, f32[1,128]{1,0:T(1,128)S(1)}) custom-call(f32[18,64,128]{2,1,0:T(8,128)S(1)} %get-tuple-element.158.refs_0_, bf16[128,512]{1,0:T(8,128)(2,1)S(1)} %get-tuple-element.159.refs_1_, f32[64,256]{1,0:T(8,128)S(1)} %get-tuple-element.176.refs_2_, ...), custom_call_target="tpu_custom_call" | custom-call | tf_op jit(solution)/shard_map/pallas_call | solution.py:415
  54.5 0.0 copy-start.14
  54.5 0.0 copy-done
  54.5 0.6 %copy-done.14 = s32[1,2]{1,0:T(1,128)S(1)} copy-done((s32[1,2]{1,0:T(1,128)S(1)}, s32[1,2]{1,0:T(1,128)}, u32[]{:S(2)}) %copy-start.14) | copy-done | bytes 32
  55.1 0.5 copy-done.17
  55.7 0.1 copy-done.16
  (63 shorter events, 0.3 us)
Async XLA Ops:
  0.6 0.7 %copy-start.13 = (f32[1,64]{1,0:T(1,128)S(1)}, f32[1,64]{1,0:T(1,128)}, u32[]{:S(2)}) copy-start(f32[1,64]{1,0:T(1,128)} %refs_2_.3) | copy-start | bytes 772
  0.6 0.7 %copy-start.12 = (s32[2,1,64]{2,1,0:T(1,128)S(1)}, s32[2,1,64]{2,1,0:T(1,128)}, u32[]{:S(2)}) copy-start(s32[2,1,64]{2,1,0:T(1,128)} %param.29) | copy-start | bytes 1540
  1.3 4.7 %copy-start.1 = (f32[64,128]{1,0:T(8,128)S(1)}, f32[64,128]{1,0:T(8,128)}, u32[]{:S(2)}) copy-start(f32[64,128]{1,0:T(8,128)} %refs_0_.1) | copy-start | bytes 98308
  1.3 4.7 %copy-start.4 = (f32[64,128]{1,0:T(8,128)S(1)}, f32[64,128]{1,0:T(8,128)}, u32[]{:S(2)}) copy-start(f32[64,128]{1,0:T(8,128)} %refs_2_.2) | copy-start | bytes 98308
  1.3 4.7 %copy-start.8 = (f32[256]{0:T(256)S(1)}, f32[256]{0:T(256)}, u32[]{:S(2)}) copy-start(f32[256]{0:T(256)} %param.28) | copy-start | bytes 3076
  1.3 4.7 %copy-start.9 = (s32[256]{0:T(256)S(1)}, s32[256]{0:T(256)}, u32[]{:S(2)}) copy-start(s32[256]{0:T(256)} %param.32) | copy-start | bytes 3076
  1.3 4.7 %copy-start.10 = (f32[256]{0:T(256)S(1)}, f32[256]{0:T(256)}, u32[]{:S(2)}) copy-start(f32[256]{0:T(256)} %param.34) | copy-start | bytes 3076
  1.4 4.7 %copy-start.11 = (f32[256]{0:T(256)S(1)}, f32[256]{0:T(256)}, u32[]{:S(2)}) copy-start(f32[256]{0:T(256)} %param.33) | copy-start | bytes 3076
  3.0 5.5 %collective-permute-start.29 = (f32[72,128]{1,0:T(8,128)}, f32[72,128]{1,0:T(8,128)S(1)}, u32[]{:S(2)}, u32[]{:S(2)}) collective-permute-start(f32[72,128]{1,0:T(8,128)} %shard_map.166), channel_id=1, source_target_pairs={{0,1},{1,0},{2,3},{3,2},{4,5},{5,4},{6,7},{7,6},{8,9},{9,8},{10,11... | collective-permute-start | bytes 110600 | tf_op jit(solution)/shard_map/ppermute | solution.py:437
  6.0 0.7 %copy-start.7 = (s32[2,256]{1,0:T(2,128)S(1)}, s32[2,256]{1,0:T(2,128)}, u32[]{:S(2)}) copy-start(s32[2,256]{1,0:T(2,128)} %refs_6_.1) | copy-start | bytes 6148
  6.0 0.7 %copy-start.6 = (s32[1,2048]{1,0:T(1,128)S(1)}, s32[1,2048]{1,0:T(1,128)}, u32[]{:S(2)}) copy-start(s32[1,2048]{1,0:T(1,128)} %param.26) | copy-start | bytes 24580
  6.0 0.7 %copy-start.5 = (f32[16,128]{1,0:T(8,128)S(1)}, f32[16,128]{1,0:T(8,128)}, u32[]{:S(2)}) copy-start(f32[16,128]{1,0:T(8,128)} %refs_3_.2) | copy-start | bytes 24580
  6.0 0.7 %copy-start.15 = (f32[1,128]{1,0:T(1,128)S(1)}, f32[1,128]{1,0:T(1,128)}, u32[]{:S(2)}) copy-start(f32[1,128]{1,0:T(1,128)} %refs_4_.1) | copy-start | bytes 1540
  6.7 1.8 %copy-start.2 = (f32[72,128]{1,0:T(8,128)S(1)}, f32[72,128]{1,0:T(8,128)}, u32[]{:S(2)}) copy-start(f32[72,128]{1,0:T(8,128)} %shard_map.166) | copy-start | bytes 110596
  8.9 1.3 %collective-permute-start.30 = (f32[56,128]{1,0:T(8,128)S(1)}, f32[56,128]{1,0:T(8,128)S(1)}, u32[]{:S(2)}, u32[]{:S(2)}) collective-permute-start(f32[56,128]{1,0:T(8,128)S(1)} %get-tuple-element.167), channel_id=1, source_target_pairs={{0,2},{1,3},{2,0},{3,1},{4,6},{5,7},{6,4},{7,5},{8,10},{9,11},{10,... | collective-permute-start | bytes 86024 | tf_op jit(solution)/shard_map/ppermute | solution.py:437
  10.2 5.9 %collective-permute-start.33 = (f32[3,128]{1,0:T(4,128)S(1)}, f32[3,128]{1,0:T(4,128)S(1)}, u32[]{:S(2)}, u32[]{:S(2)}) collective-permute-start(f32[3,128]{1,0:T(4,128)S(1)} %slice.448), channel_id=1, source_target_pairs={{0,7},{1,6},{2,5},{3,4},{4,3},{5,2},{6,1},{7,0},{8,15},{9,14},{10,... | collective-permute-start | bytes 4616 | tf_op jit(solution)/shard_map/ppermute | solution.py:437
  12.6 3.4 %collective-permute-start.31 = (f32[56,128]{1,0:T(8,128)S(1)}, f32[56,128]{1,0:T(8,128)S(1)}, u32[]{:S(2)}, u32[]{:S(2)}) collective-permute-start(f32[56,128]{1,0:T(8,128)S(1)} %pad_maximum_fusion.11), channel_id=1, source_target_pairs={{0,6},{1,7},{2,4},{3,5},{4,2},{5,3},{6,0},{7,1},{8,14},{9,15},{10,... | collective-permute-start | bytes 86024 | tf_op jit(solution)/shard_map/ppermute | solution.py:437
  13.2 4.0 %collective-permute-start.32 = (f32[67,128]{1,0:T(8,128)S(1)}, f32[67,128]{1,0:T(8,128)S(1)}, u32[]{:S(2)}, u32[]{:S(2)}) collective-permute-start(f32[67,128]{1,0:T(8,128)S(1)} %pad_maximum_fusion.8), channel_id=1, source_target_pairs={{0,1},{1,0},{2,3},{3,2},{4,5},{5,4},{6,7},{7,6},{8,9},{9,8},{10,11... | collective-permute-start | bytes 102920 | tf_op jit(solution)/shard_map/ppermute | solution.py:437
  17.2 5.2 %collective-permute-start.36 = (f32[56,128]{1,0:T(8,128)S(1)}, f32[56,128]{1,0:T(8,128)S(1)}, u32[]{:S(2)}, u32[]{:S(2)}) collective-permute-start(f32[56,128]{1,0:T(8,128)S(1)} %maximum_add_fusion.4.refs_6_), channel_id=1, source_target_pairs={{0,26},{1,27},{2,24},{3,25},{4,30},{5,31},{6,28},{7,29},{8,18},{9,... | collective-permute-start | bytes 86024 | tf_op jit(solution)/shard_map/ppermute | solution.py:437
  19.7 4.2 %collective-permute-start.35 = (f32[56,128]{1,0:T(8,128)S(1)}, f32[56,128]{1,0:T(8,128)S(1)}, u32[]{:S(2)}, u32[]{:S(2)}) collective-permute-start(f32[56,128]{1,0:T(8,128)S(1)} %maximum_add_fusion.4.refs_6_), channel_id=1, source_target_pairs={{0,18},{1,19},{2,16},{3,17},{4,22},{5,23},{6,20},{7,21},{8,26},{9,... | collective-permute-start | bytes 86024 | tf_op jit(solution)/shard_map/ppermute | solution.py:437
  20.0 3.9 %collective-permute-start.34 = (f32[56,128]{1,0:T(8,128)S(1)}, f32[56,128]{1,0:T(8,128)S(1)}, u32[]{:S(2)}, u32[]{:S(2)}) collective-permute-start(f32[56,128]{1,0:T(8,128)S(1)} %maximum_add_fusion.4.refs_6_), channel_id=1, source_target_pairs={{0,10},{1,11},{2,8},{3,9},{4,14},{5,15},{6,12},{7,13},{8,2},{9,3},... | collective-permute-start | bytes 86024 | tf_op jit(solution)/shard_map/ppermute | solution.py:437
  24.7 2.1 %collective-permute-start.37 = (f32[24,128]{1,0:T(8,128)S(1)}, f32[24,128]{1,0:T(8,128)S(1)}, u32[]{:S(2)}, u32[]{:S(2)}) collective-permute-start(f32[24,128]{1,0:T(8,128)S(1)} %get-tuple-element.174), channel_id=1, source_target_pairs={{0,2},{1,3},{2,0},{3,1},{4,6},{5,7},{6,4},{7,5},{8,10},{9,11},{10,... | collective-permute-start | bytes 36872 | tf_op jit(solution)/shard_map/ppermute | solution.py:437
  26.9 4.7 %collective-permute-start.40 = (f32[3,128]{1,0:T(4,128)S(1)}, f32[3,128]{1,0:T(4,128)S(1)}, u32[]{:S(2)}, u32[]{:S(2)}) collective-permute-start(f32[3,128]{1,0:T(4,128)S(1)} %slice.459), channel_id=1, source_target_pairs={{0,7},{1,6},{2,5},{3,4},{4,3},{5,2},{6,1},{7,0},{8,15},{9,14},{10,... | collective-permute-start | bytes 4616 | tf_op jit(solution)/shard_map/ppermute | solution.py:437
  28.3 3.2 %collective-permute-start.38 = (f32[24,128]{1,0:T(8,128)S(1)}, f32[24,128]{1,0:T(8,128)S(1)}, u32[]{:S(2)}, u32[]{:S(2)}) collective-permute-start(f32[24,128]{1,0:T(8,128)S(1)} %pad_maximum_fusion.12), channel_id=1, source_target_pairs={{0,6},{1,7},{2,4},{3,5},{4,2},{5,3},{6,0},{7,1},{8,14},{9,15},{10,... | collective-permute-start | bytes 36872 | tf_op jit(solution)/shard_map/ppermute | solution.py:437
  28.7 4.0 %collective-permute-start.39 = (f32[67,128]{1,0:T(8,128)S(1)}, f32[67,128]{1,0:T(8,128)S(1)}, u32[]{:S(2)}, u32[]{:S(2)}) collective-permute-start(f32[67,128]{1,0:T(8,128)S(1)} %pad_maximum_fusion.9), channel_id=1, source_target_pairs={{0,1},{1,0},{2,3},{3,2},{4,5},{5,4},{6,7},{7,6},{8,9},{9,8},{10,11... | collective-permute-start | bytes 102920 | tf_op jit(solution)/shard_map/ppermute | solution.py:437
  32.7 5.0 %collective-permute-start.43 = (f32[24,128]{1,0:T(8,128)S(1)}, f32[24,128]{1,0:T(8,128)S(1)}, u32[]{:S(2)}, u32[]{:S(2)}) collective-permute-start(f32[24,128]{1,0:T(8,128)S(1)} %maximum_add_fusion.5.refs_8_), channel_id=1, source_target_pairs={{0,26},{1,27},{2,24},{3,25},{4,30},{5,31},{6,28},{7,29},{8,18},{9,... | collective-permute-start | bytes 36872 | tf_op jit(solution)/shard_map/ppermute | solution.py:437
  33.2 4.5 %collective-permute-start.42 = (f32[24,128]{1,0:T(8,128)S(1)}, f32[24,128]{1,0:T(8,128)S(1)}, u32[]{:S(2)}, u32[]{:S(2)}) collective-permute-start(f32[24,128]{1,0:T(8,128)S(1)} %maximum_add_fusion.5.refs_8_), channel_id=1, source_target_pairs={{0,18},{1,19},{2,16},{3,17},{4,22},{5,23},{6,20},{7,21},{8,26},{9,... | collective-permute-start | bytes 36872 | tf_op jit(solution)/shard_map/ppermute | solution.py:437
  34.0 3.6 %collective-permute-start.41 = (f32[24,128]{1,0:T(8,128)S(1)}, f32[24,128]{1,0:T(8,128)S(1)}, u32[]{:S(2)}, u32[]{:S(2)}) collective-permute-start(f32[24,128]{1,0:T(8,128)S(1)} %maximum_add_fusion.5.refs_8_), channel_id=1, source_target_pairs={{0,10},{1,11},{2,8},{3,9},{4,14},{5,15},{6,12},{7,13},{8,2},{9,3},... | collective-permute-start | bytes 36872 | tf_op jit(solution)/shard_map/ppermute | solution.py:437
  38.4 1.7 %collective-permute-start.44 = (f32[24,128]{1,0:T(8,128)S(1)}, f32[24,128]{1,0:T(8,128)S(1)}, u32[]{:S(2)}, u32[]{:S(2)}) collective-permute-start(f32[24,128]{1,0:T(8,128)S(1)} %get-tuple-element.181), channel_id=1, source_target_pairs={{0,2},{1,3},{2,0},{3,1},{4,6},{5,7},{6,4},{7,5},{8,10},{9,11},{10,... | collective-permute-start | bytes 36872 | tf_op jit(solution)/shard_map/ppermute | solution.py:437
  40.1 5.8 %collective-permute-start.47 = (f32[3,128]{1,0:T(4,128)S(1)}, f32[3,128]{1,0:T(4,128)S(1)}, u32[]{:S(2)}, u32[]{:S(2)}) collective-permute-start(f32[3,128]{1,0:T(4,128)S(1)} %slice.470), channel_id=1, source_target_pairs={{0,7},{1,6},{2,5},{3,4},{4,3},{5,2},{6,1},{7,0},{8,15},{9,14},{10,... | collective-permute-start | bytes 4616 | tf_op jit(solution)/shard_map/ppermute | solution.py:437
  42.7 3.2 %collective-permute-start.45 = (f32[24,128]{1,0:T(8,128)S(1)}, f32[24,128]{1,0:T(8,128)S(1)}, u32[]{:S(2)}, u32[]{:S(2)}) collective-permute-start(f32[24,128]{1,0:T(8,128)S(1)} %pad_maximum_fusion.13), channel_id=1, source_target_pairs={{0,6},{1,7},{2,4},{3,5},{4,2},{5,3},{6,0},{7,1},{8,14},{9,15},{10,... | collective-permute-start | bytes 36872 | tf_op jit(solution)/shard_map/ppermute | solution.py:437
  43.0 4.0 %collective-permute-start.46 = (f32[67,128]{1,0:T(8,128)S(1)}, f32[67,128]{1,0:T(8,128)S(1)}, u32[]{:S(2)}, u32[]{:S(2)}) collective-permute-start(f32[67,128]{1,0:T(8,128)S(1)} %pad_maximum_fusion.10), channel_id=1, source_target_pairs={{0,1},{1,0},{2,3},{3,2},{4,5},{5,4},{6,7},{7,6},{8,9},{9,8},{10,11... | collective-permute-start | bytes 102920 | tf_op jit(solution)/shard_map/ppermute | solution.py:437
  47.0 5.0 %collective-permute-start.50 = (f32[24,128]{1,0:T(8,128)S(1)}, f32[24,128]{1,0:T(8,128)S(1)}, u32[]{:S(2)}, u32[]{:S(2)}) collective-permute-start(f32[24,128]{1,0:T(8,128)S(1)} %maximum_add_fusion.6.refs_8_), channel_id=1, source_target_pairs={{0,26},{1,27},{2,24},{3,25},{4,30},{5,31},{6,28},{7,29},{8,18},{9,... | collective-permute-start | bytes 36872 | tf_op jit(solution)/shard_map/ppermute | solution.py:437
  48.1 4.0 %collective-permute-start.49 = (f32[24,128]{1,0:T(8,128)S(1)}, f32[24,128]{1,0:T(8,128)S(1)}, u32[]{:S(2)}, u32[]{:S(2)}) collective-permute-start(f32[24,128]{1,0:T(8,128)S(1)} %maximum_add_fusion.6.refs_8_), channel_id=1, source_target_pairs={{0,18},{1,19},{2,16},{3,17},{4,22},{5,23},{6,20},{7,21},{8,26},{9,... | collective-permute-start | bytes 36872 | tf_op jit(solution)/shard_map/ppermute | solution.py:437
  50.0 3.1 %collective-permute-start.48 = (f32[24,128]{1,0:T(8,128)S(1)}, f32[24,128]{1,0:T(8,128)S(1)}, u32[]{:S(2)}, u32[]{:S(2)}) collective-permute-start(f32[24,128]{1,0:T(8,128)S(1)} %maximum_add_fusion.6.refs_8_), channel_id=1, source_target_pairs={{0,10},{1,11},{2,8},{3,9},{4,14},{5,15},{6,12},{7,13},{8,2},{9,3},... | collective-permute-start | bytes 36872 | tf_op jit(solution)/shard_map/ppermute | solution.py:437
  53.2 1.3 %copy-start = (f32[64,16,128]{2,1,0:T(8,128)S(1)}, f32[64,16,128]{2,1,0:T(8,128)}, u32[]{:S(2)}) copy-start(f32[64,16,128]{2,1,0:T(8,128)} %param.22) | copy-start | bytes 1572868
  54.5 0.7 %copy-start.14 = (s32[1,2]{1,0:T(1,128)S(1)}, s32[1,2]{1,0:T(1,128)}, u32[]{:S(2)}) copy-start(s32[1,2]{1,0:T(1,128)} %refs_3_.3) | copy-start | bytes 28
  55.1 0.5 copy-start.17
  55.1 0.6 %copy-start.16 = (f32[64,128]{1,0:T(8,128)}, f32[64,128]{1,0:T(8,128)S(1)}, u32[]{:S(2)}) copy-start(f32[64,128]{1,0:T(8,128)S(1)} %get-tuple-element.189) | copy-start | bytes 98308

commit v15 on v12

--- a/solution.py
+++ b/solution.py
@@ -118,19 +118,15 @@
     in_use = jnp.zeros((1, slots), jnp.int32)
     for target in range(regions):
         in_use = jnp.where(pair == target, pairs_ref[0:1, target : target + 1], in_use)
-    place = lax.broadcasted_iota(jnp.int32, (slots, regions * slots), 1) == (
-        own * slots + lax.broadcasted_iota(jnp.int32, (slots, regions * slots), 0)
-    )
-    place = place.astype(jnp.float32).astype(jnp.bfloat16)
     bound = jnp.where(slot % width < in_use, limit_ref[...], 0.0)
     start = (ends_ref[0:1, :] + own * nodes).astype(jnp.float32)
     end = (ends_ref[1:2, :] + pair * nodes).astype(jnp.float32)
-    rest = jnp.zeros((13, slots), jnp.float32)
-    info = dot3(jnp.concatenate([start, end, bound, rest], axis=0), place, False)
-    for chunk in range(regions * slots // LANES):
-        block_ref[rows + 8 * chunk : rows + 8 * chunk + 8, :] = info[
-            :8, chunk * LANES : (chunk + 1) * LANES
-        ]
+    block_ref[rows:, :] = jnp.zeros((block_ref.shape[0] - rows, LANES), jnp.float32)
+    width = min(slots, LANES)
+    for chunk in range(slots // width):
+        at = rows + 8 * chunk
+        for i, row in enumerate((start, end, bound)):
+            block_ref[at + i : at + i + 1, :width] = row[:, chunk * width : (chunk + 1) * width]
     copies[0].wait()
 
 
@@ -209,14 +205,15 @@
     rows, techs, nodes = sizes.rows, sizes.techs, sizes.nodes
     slots, regions = sizes.slots, sizes.regions
     own = lax.axis_index("region")
-    chunks = []
-    for chunk in range(regions * slots // LANES):
-        at = slice(rows + 8 * chunk, rows + 8 * chunk + 8)
-        part = gathered[0, at, :]
-        for region in range(1, regions):
-            part = part + gathered[region, at, :]
-        chunks.append(part)
-    info = jnp.concatenate(chunks, axis=1) if len(chunks) > 1 else chunks[0]
+    width = min(slots, LANES)
+    info = jnp.concatenate(
+        [
+            gathered[region, rows + 8 * chunk : rows + 8 * chunk + 8, :width]
+            for region in range(regions)
+            for chunk in range(slots // width)
+        ],
+        axis=1,
+    )
     maps_ref[...] = incidence(
         info[0:1].astype(jnp.int32), info[1:2].astype(jnp.int32), regions * nodes
     )
@@ -226,7 +223,7 @@
     local = local_ref.shape[1]
     flows_ref[:rows, :local] = local_ref[...]
     flows_ref[:rows, local:] = flows
-    flows_ref[rows : rows + 1, local:] = limits
+    flows_ref[rows:, local:] = info
     maps_own = maps_ref[pl.ds(pl.multiple_of(own * nodes, nodes), nodes), :]
     balance = balance_ref[...] + dot3(2.0 * flows, maps_own, True)
     step_up = (1.0 / (techs + 8.0)) * balance
@@ -327,7 +324,7 @@
     bars = []
     local, total_flows = lines + units, lines + units + regions * slots
     local_limits = read_lanes(fixed, at.limits, local)
-    cross_limits = given.flows[rows : rows + 1, local:]
+    cross_limits = given.flows[rows + 2 : rows + 3, local:]
     for bound, slope, low, high in (
         (local_limits[:, :lines], slope_local[:, :lines], 0, lines),
         (local_limits[:, lines:], slope_local[:, lines:] + store_duals, lines, local),
@@ -381,9 +378,16 @@
         chosen = dot3(capacity_new, node_hot, False)
         gives.capacity[...] = row_sum(jnp.where(tech_hot, chosen, 0.0))
         gives.negative[...] = negative
+        gives.kept[:rows, :] = fixed[...]
+        gives.kept[rows : rows + techs, :] = col_weight
+        gives.kept[rows + techs : rows + 2 * techs, :] = cost
+        for chunk in range(regions * slots // LANES):
+            low = local + chunk * LANES
+            first = rows + 2 * techs + 8 * chunk
+            gives.kept[first : first + 8, :] = given.flows[rows:, low : low + LANES]
         return
     gives.prices[...] = prices + step_up
-    gives.flows[rows : rows + 1, local:] = cross_limits
+    gives.flows[rows:, local:] = given.flows[rows:, local:]
     gives.cap_duals[techs, :techs, :] = col_weight
     gives.cap_duals[techs, techs : 2 * techs, :] = cost
     small_new = gives.dispatch.at[techs]
@@ -483,7 +487,7 @@
     beside = swap(jnp.concatenate([prices, chip[techs:halo]], axis=0), 0, 1)
     other, squares = beside[: sizes.rows], beside[sizes.rows :]
     slab = merged(chip, across, hour // 2 % 2 == 0)
-    slab = slab.at[techs:halo].add(squares + diagonal)
+    slab = slab + jnp.pad(squares + diagonal, ((techs, slab.shape[0] - halo), (0, 0)))
     near, middle, far = [swap(slab, 4 * step + 1, 0) for step in (1, 2, 3)]
     parts = Bag(slab=slab, near=near, middle=middle, far=far, partner=partner, across=across)
     return in_order(prices, other), parts
@@ -493,17 +497,28 @@
     return jax.ShapeDtypeStruct(dims, dtype)
 
 
-def restarted(sizes, kept, price_start):
+def restarted(sizes, kept, args):
     rows, techs, nodes, lines = sizes.rows, sizes.techs, sizes.nodes, sizes.lines
     local, cross = lines + sizes.units, sizes.regions * sizes.slots
     at, own = places(sizes), lax.axis_index("region")
     first_hour = lax.axis_index("hours") == 0
-    fixed, available = kept.available[techs + 1], kept.available[:techs]
-    col_weight, cost = kept.cap_duals[techs, :techs], kept.cap_duals[techs, techs : 2 * techs]
+    price_start = args.price_start
+    available = args.availability.transpose(1, 0, 2)
+    fixed, last = kept[:rows], rows + 2 * techs
+    col_weight, cost = kept[rows : rows + techs], kept[rows + techs : last]
+    info = kept[last:].reshape(-1, 8, LANES).transpose(1, 0, 2).reshape(8, cross)
     local_limits = fixed[at.limits : at.energy].reshape(1, local)
-    cross_limits = kept.flows[rows : rows + 1, local:]
-    maps_local = kept.maps_local.astype(jnp.float32)
-    maps_cross = kept.maps_cross.astype(jnp.float32)
+    cross_limits = info[2:3]
+    ends = info[:2].astype(jnp.int32)
+    maps_cross_low = incidence(ends[:1], ends[1:], sizes.regions * nodes)
+    stores = args.store_node[None]
+    maps_local_low = incidence(
+        jnp.concatenate([args.line_ends[:1], jnp.full_like(stores, -1)], axis=1),
+        jnp.concatenate([args.line_ends[1:], stores], axis=1),
+        nodes,
+    )
+    maps_local = maps_local_low.astype(jnp.float32)
+    maps_cross = maps_cross_low.astype(jnp.float32)
     maps_own = lax.dynamic_slice_in_dim(maps_cross, own * nodes, nodes)
     prices_all = jnp.concatenate(list(both_regions(price_start)), axis=1)
     highest = lax.Precision.HIGHEST
@@ -519,7 +534,7 @@
         jnp.sum(2.0 * dispatch, axis=0)
         + jnp.dot(2.0 * flows_local, maps_local.T, precision=highest)
         + jnp.dot(2.0 * flows_cross, maps_own.T, precision=highest)
-        - kept.available[techs]
+        - args.demand
     )
     step_up = balance / (techs + 8.0)
     duals = jnp.maximum(0.5 * (2.0 * dispatch - available * (2.0 * capacity)[:, None, :]), 0.0)
@@ -543,14 +558,14 @@
     rows_of += [jnp.where(first_hour, part, 0.0) for part in (col_weight, cost)]
     gathered, parts = exchange(sizes, price_start + step_up, jnp.concatenate(rows_of, axis=0))
     flows = jnp.concatenate([flows_local, flows_cross], axis=1)
-    limits = jnp.concatenate([local_limits, cross_limits], axis=1)
+    spare = jnp.concatenate([jnp.zeros((8, local)), info], axis=1)
     state = Bag(
-        available=kept.available,
-        maps_local=kept.maps_local,
-        maps_cross=kept.maps_cross,
+        available=jnp.concatenate([available, args.demand[None], fixed[None]], axis=0),
+        maps_local=maps_local_low,
+        maps_cross=maps_cross_low,
         store_duals=store_duals,
         dispatch=jnp.concatenate([dispatch, jnp.zeros((1, rows, nodes))], axis=0),
-        flows=jnp.concatenate([flows, jnp.broadcast_to(limits, (8, local + cross))], axis=0),
+        flows=jnp.concatenate([flows, spare], axis=0),
     )
     return state, gathered, parts
 
@@ -574,7 +589,7 @@
                 limit=args.cross_limit,
                 pairs=args.pair_counts,
             ),
-            Bag(block=shape(rows + 8 * (cross // LANES), nodes)),
+            Bag(block=shape(rows + 8 * max(1, slots // LANES), nodes)),
             left=(0, 1, 2, 3),
             scratch=[
                 pltpu.VMEM((2, slots), jnp.int32),
@@ -631,10 +646,10 @@
     del state.sums, state.balance, state.flows_local
     state.maps_cross, state.flows = closed.maps, closed.flows
     gathered, parts = exchange(sizes, closed.prices, closed.sums)
-    outputs, kept, negative = sweeps(sizes, owned, state, gathered, parts)
+    outputs, negative, kept = sweeps(sizes, owned, state, gathered, parts)
 
     def again():
-        return sweeps(sizes, owned, *restarted(sizes, kept, args.price_start))[0]
+        return sweeps(sizes, owned, *restarted(sizes, kept, args))[0]
 
     return lax.cond(negative > 0.0, again, lambda: outputs)
 
@@ -667,6 +682,7 @@
                 prices=shape(rows, nodes),
                 charge=shape(rows, units),
                 negative=shape(1, LANES),
+                kept=shape(rows + 2 * techs + 8 * (sizes.regions * sizes.slots // LANES), LANES),
             )
         results = call(functools.partial(sweep_kernel, sizes, iteration), given, outs)
         if iteration < ITERS - 1:
@@ -675,7 +691,7 @@
             vars(state).update(vars(results))
     dispatch = results.dispatch.reshape(rows, techs, nodes)
     outputs = (dispatch, results.capacity, results.prices, results.charge)
-    return outputs, state, results.negative[0, 0]
+    return outputs, results.negative[0, 0], results.kept
 
 
 def body(

time: 56.8 us -> 54.6 us (0.961)
  local copies, waits for them, and re-layouts: 2.6 us -> 1.39 us
  Pallas kernels: 7.52 us -> 6.41 us
    pallas_call x6, Pallas kernels: 7.52 us -> 6.41 us  [call(): pl.pallas_call(functools.partial(kernel, names_in, names_out), out_shape=...]
    unnamed x30, local copies, waits for them, and re-layouts: 2.36 us -> 1.34 us
  transfers between devices with their start and end apart: 22 -> 22, of which waited for: 15 -> 15; matrix products, arithmetic and copies ran while one was open for 0% -> 0% of each run, Pallas kernels for 2% -> 3%
where the time goes in v15:
time: 54.6 us; the launch traced here: 54.4 us
  starting transfers between devices  25.4 us (47%)
  waiting for transfers between devices  20 us (37%)
  Pallas kernels  6.41 us (12%)
  local copies, waits for them, and re-layouts  1.39 us (3%)
  between operations  1.05 us (2%)
    ppermute x22, starting transfers between devices, swap(): return lax.ppermute(value, ('hours', 'region'), pairs)  25.4 us
    ppermute x22, waiting for transfers between devices, swap(): return lax.ppermute(value, ('hours', 'region'), pairs)  20 us
    pallas_call x6, Pallas kernels, call(): pl.pallas_call(functools.partial(kernel, names_in, names_out), out_shape=...  6.41 us
    unnamed x30, local copies, waits for them, and re-layouts  1.34 us
  transfers between devices with their start and end apart: 22, of which 15 were waited for; matrix products, arithmetic and copies ran while one was open for 0% of the time, Pallas kernels for 3%

profile of v15, /device:TPU:0, one launch (start us, length us, event | category | flops | bytes accessed | tf_op | source)
XLA Modules:
  0.0 54.4 jit_solution(18050990187476133430)
XLA Ops:
  0.6 0.0 copy-start.4
  0.6 0.0 copy-start.7
  0.7 0.0 copy-start.8
  0.7 0.0 copy-start.10
  0.7 1.5 %shard_map.166 = f32[72,128]{1,0:T(8,128)} custom-call(f32[64,128]{1,0:T(8,128)} %refs_0_.1, s32[2,64]{1,0:T(2,128)} %bitcast.118, f32[1,64]{1,0:T(1,128)} %refs_2_.3, s32[1,2]{1,0:T(1,128)} %refs_3_.3), custom_call_target="tpu_custom_call" | custom-call | tf_op jit(solution)/shard_map/pallas_call | solution.py:419
  2.1 3.0 %collective-permute-start.22 = (f32[72,128]{1,0:T(8,128)}, f32[72,128]{1,0:T(8,128)S(1)}, u32[]{:S(2)}, u32[]{:S(2)}) collective-permute-start(f32[72,128]{1,0:T(8,128)} %shard_map.166), channel_id=1, source_target_pairs={{0,1},{1,0},{2,3},{3,2},{4,5},{5,4},{6,7},{7,6},{8,9},{9,8},{10,11... | collective-permute-start | bytes 110600 | tf_op jit(solution)/shard_map/ppermute | solution.py:441
  5.2 0.0 copy-start.2
  5.3 0.6 %copy-done.3 = f32[256]{0:T(256)S(1)} copy-done((f32[256]{0:T(256)S(1)}, f32[256]{0:T(256)}, u32[]{:S(2)}) %copy-start.3) | copy-done | bytes 1048
  5.9 0.0 copy-done.1
  5.9 0.0 copy-done
  5.9 1.7 %shard_map.165 = (f32[18,64,128]{2,1,0:T(8,128)S(1)}, bf16[128,512]{1,0:T(8,128)(2,1)S(1)}, f32[64,512]{1,0:T(8,128)S(1)}, f32[64,256]{1,0:T(8,128)S(1)}, f32[17...) custom-call(f32[1024,128]{1,0:T(8,128)} %bitcast.86, f32[64,128]{1,0:T(8,128)S(1)} %copy-done.7, ...), custom_call_target="tpu_custom_call" | custom-call | flops 1000000 | bytes 4000000 | tf_op jit(solution)/shard_map/pallas_call | solution.py:419
  7.7 0.0 collective-permute-done.22
  7.7 0.4 shard_map.167
  8.2 0.1 collective-permute-start.23
  8.3 1.2 %collective-permute-done.23.refs_10_ = f32[56,128]{1,0:T(8,128)S(1)} collective-permute-done((f32[56,128]{1,0:T(8,128)S(1)}, f32[56,128]{1,0:T(8,128)S(1)}, u32[]{:S(2)}, u32[]{:S(2)}) %collective-permute-start.23) | collective-permute-done | bytes 28704 | tf_op jit(solution)/shard_map/ppermute | solution.py:441
  9.5 2.4 %collective-permute-start.26 = (f32[3,128]{1,0:T(4,128)S(1)}, f32[3,128]{1,0:T(4,128)S(1)}, u32[]{:S(2)}, u32[]{:S(2)}) collective-permute-start(f32[3,128]{1,0:T(4,128)S(1)} %slice.411), channel_id=1, source_target_pairs={{0,7},{1,6},{2,5},{3,4},{4,3},{5,2},{6,1},{7,0},{8,15},{9,14},{10,... | collective-permute-start | bytes 4616 | tf_op jit(solution)/shard_map/ppermute | solution.py:441
  11.9 0.6 %collective-permute-start.24 = (f32[56,128]{1,0:T(8,128)S(1)}, f32[56,128]{1,0:T(8,128)S(1)}, u32[]{:S(2)}, u32[]{:S(2)}) collective-permute-start(f32[56,128]{1,0:T(8,128)S(1)} %pad_maximum_fusion.10), channel_id=1, source_target_pairs={{0,6},{1,7},{2,4},{3,5},{4,2},{5,3},{6,0},{7,1},{8,14},{9,15},{10,... | collective-permute-start | bytes 86024 | tf_op jit(solution)/shard_map/ppermute | solution.py:441
  12.4 0.4 collective-permute-start.25
  12.8 2.4 %collective-permute-done.24.refs_11_ = f32[56,128]{1,0:T(8,128)S(1)} collective-permute-done((f32[56,128]{1,0:T(8,128)S(1)}, f32[56,128]{1,0:T(8,128)S(1)}, u32[]{:S(2)}, u32[]{:S(2)}) %collective-permute-start.24) | collective-permute-done | bytes 28704 | tf_op jit(solution)/shard_map/ppermute | solution.py:441
  15.3 0.0 collective-permute-done.26
  15.3 1.1 %collective-permute-done.25 = f32[67,128]{1,0:T(8,128)S(1)} collective-permute-done((f32[67,128]{1,0:T(8,128)S(1)}, f32[67,128]{1,0:T(8,128)S(1)}, u32[]{:S(2)}, u32[]{:S(2)}) %collective-permute-start.25) | collective-permute-done | bytes 34336 | tf_op jit(solution)/shard_map/ppermute | solution.py:441
  16.4 2.5 %collective-permute-start.29 = (f32[56,128]{1,0:T(8,128)S(1)}, f32[56,128]{1,0:T(8,128)S(1)}, u32[]{:S(2)}, u32[]{:S(2)}) collective-permute-start(f32[56,128]{1,0:T(8,128)S(1)} %maximum_add_fusion.3.refs_6_), channel_id=1, source_target_pairs={{0,26},{1,27},{2,24},{3,25},{4,30},{5,31},{6,28},{7,29},{8,18},{9,... | collective-permute-start | bytes 86024 | tf_op jit(solution)/shard_map/ppermute | solution.py:441
  19.0 0.3 collective-permute-start.28
  19.2 1.2 %collective-permute-start.27 = (f32[56,128]{1,0:T(8,128)S(1)}, f32[56,128]{1,0:T(8,128)S(1)}, u32[]{:S(2)}, u32[]{:S(2)}) collective-permute-start(f32[56,128]{1,0:T(8,128)S(1)} %maximum_add_fusion.3.refs_6_), channel_id=1, source_target_pairs={{0,10},{1,11},{2,8},{3,9},{4,14},{5,15},{6,12},{7,13},{8,2},{9,3},... | collective-permute-start | bytes 86024 | tf_op jit(solution)/shard_map/ppermute | solution.py:441
  20.5 1.1 %collective-permute-done.29.refs_9_ = f32[56,128]{1,0:T(8,128)S(1)} collective-permute-done((f32[56,128]{1,0:T(8,128)S(1)}, f32[56,128]{1,0:T(8,128)S(1)}, u32[]{:S(2)}, u32[]{:S(2)}) %collective-permute-start.29) | collective-permute-done | bytes 28704 | tf_op jit(solution)/shard_map/ppermute | solution.py:441
  21.6 1.6 %collective-permute-done.28.refs_8_ = f32[56,128]{1,0:T(8,128)S(1)} collective-permute-done((f32[56,128]{1,0:T(8,128)S(1)}, f32[56,128]{1,0:T(8,128)S(1)}, u32[]{:S(2)}, u32[]{:S(2)}) %collective-permute-start.28) | collective-permute-done | bytes 28704 | tf_op jit(solution)/shard_map/ppermute | solution.py:441
  23.2 0.0 collective-permute-done.27.refs_7_
  23.2 0.8 %shard_map.168 = (f32[17,64,128]{2,1,0:T(8,128)S(1)}, f32[17,64,128]{2,1,0:T(8,128)S(1)}, f32[72,640]{1,0:T(8,128)S(1)}, f32[64,256]{1,0:T(8,128)S(1)}, f32[64,2...) custom-call(f32[18,64,128]{2,1,0:T(8,128)S(1)} %get-tuple-element.112.refs_0_, ...), custom_call_target="tpu_custom_call" | custom-call | tf_op jit(solution)/shard_map/pallas_call | solution.py:419
  24.0 1.3 %collective-permute-start.30 = (f32[24,128]{1,0:T(8,128)S(1)}, f32[24,128]{1,0:T(8,128)S(1)}, u32[]{:S(2)}, u32[]{:S(2)}) collective-permute-start(f32[24,128]{1,0:T(8,128)S(1)} %get-tuple-element.128), channel_id=1, source_target_pairs={{0,2},{1,3},{2,0},{3,1},{4,6},{5,7},{6,4},{7,5},{8,10},{9,11},{10,... | collective-permute-start | bytes 36872 | tf_op jit(solution)/shard_map/ppermute | solution.py:441
  25.3 0.8 %collective-permute-done.30.refs_12_ = f32[24,128]{1,0:T(8,128)S(1)} collective-permute-done((f32[24,128]{1,0:T(8,128)S(1)}, f32[24,128]{1,0:T(8,128)S(1)}, u32[]{:S(2)}, u32[]{:S(2)}) %collective-permute-start.30) | collective-permute-done | bytes 12320 | tf_op jit(solution)/shard_map/ppermute | solution.py:441
  26.1 1.4 %collective-permute-start.33 = (f32[3,128]{1,0:T(4,128)S(1)}, f32[3,128]{1,0:T(4,128)S(1)}, u32[]{:S(2)}, u32[]{:S(2)}) collective-permute-start(f32[3,128]{1,0:T(4,128)S(1)} %slice.422), channel_id=1, source_target_pairs={{0,7},{1,6},{2,5},{3,4},{4,3},{5,2},{6,1},{7,0},{8,15},{9,14},{10,... | collective-permute-start | bytes 4616 | tf_op jit(solution)/shard_map/ppermute | solution.py:441
  27.6 0.4 collective-permute-start.31
  28.0 1.5 %collective-permute-start.32 = (f32[67,128]{1,0:T(8,128)S(1)}, f32[67,128]{1,0:T(8,128)S(1)}, u32[]{:S(2)}, u32[]{:S(2)}) collective-permute-start(f32[67,128]{1,0:T(8,128)S(1)} %pad_maximum_fusion.8), channel_id=1, source_target_pairs={{0,1},{1,0},{2,3},{3,2},{4,5},{5,4},{6,7},{7,6},{8,9},{9,8},{10,11... | collective-permute-start | bytes 102920 | tf_op jit(solution)/shard_map/ppermute | solution.py:441
  29.5 1.3 %collective-permute-done.31.refs_13_ = f32[24,128]{1,0:T(8,128)S(1)} collective-permute-done((f32[24,128]{1,0:T(8,128)S(1)}, f32[24,128]{1,0:T(8,128)S(1)}, u32[]{:S(2)}, u32[]{:S(2)}) %collective-permute-start.31) | collective-permute-done | bytes 12320 | tf_op jit(solution)/shard_map/ppermute | solution.py:441
  30.8 0.0 collective-permute-done.33
  30.8 1.1 %collective-permute-done.32 = f32[67,128]{1,0:T(8,128)S(1)} collective-permute-done((f32[67,128]{1,0:T(8,128)S(1)}, f32[67,128]{1,0:T(8,128)S(1)}, u32[]{:S(2)}, u32[]{:S(2)}) %collective-permute-start.32) | collective-permute-done | bytes 34336 | tf_op jit(solution)/shard_map/ppermute | solution.py:441
  31.9 0.5 collective-permute-start.36
  32.4 0.9 %collective-permute-start.35 = (f32[24,128]{1,0:T(8,128)S(1)}, f32[24,128]{1,0:T(8,128)S(1)}, u32[]{:S(2)}, u32[]{:S(2)}) collective-permute-start(f32[24,128]{1,0:T(8,128)S(1)} %maximum_add_fusion.4.refs_8_), channel_id=1, source_target_pairs={{0,18},{1,19},{2,16},{3,17},{4,22},{5,23},{6,20},{7,21},{8,26},{9,... | collective-permute-start | bytes 36872 | tf_op jit(solution)/shard_map/ppermute | solution.py:441
  33.4 1.6 %collective-permute-start.34 = (f32[24,128]{1,0:T(8,128)S(1)}, f32[24,128]{1,0:T(8,128)S(1)}, u32[]{:S(2)}, u32[]{:S(2)}) collective-permute-start(f32[24,128]{1,0:T(8,128)S(1)} %maximum_add_fusion.4.refs_8_), channel_id=1, source_target_pairs={{0,10},{1,11},{2,8},{3,9},{4,14},{5,15},{6,12},{7,13},{8,2},{9,3},... | collective-permute-start | bytes 36872 | tf_op jit(solution)/shard_map/ppermute | solution.py:441
  34.9 2.0 %collective-permute-done.36.refs_11_ = f32[24,128]{1,0:T(8,128)S(1)} collective-permute-done((f32[24,128]{1,0:T(8,128)S(1)}, f32[24,128]{1,0:T(8,128)S(1)}, u32[]{:S(2)}, u32[]{:S(2)}) %collective-permute-start.36) | collective-permute-done | bytes 12320 | tf_op jit(solution)/shard_map/ppermute | solution.py:441
  36.9 0.0 collective-permute-done.35.refs_10_
  36.9 0.0 collective-permute-done.34.refs_9_
  36.9 0.7 %shard_map.169 = (f32[17,64,128]{2,1,0:T(8,128)S(1)}, f32[17,64,128]{2,1,0:T(8,128)S(1)}, f32[72,640]{1,0:T(8,128)S(1)}, f32[64,256]{1,0:T(8,128)S(1)}, f32[64,2...) custom-call(f32[18,64,128]{2,1,0:T(8,128)S(1)} %get-tuple-element.112.refs_0_, ...), custom_call_target="tpu_custom_call" | custom-call | tf_op jit(solution)/shard_map/pallas_call | solution.py:419
  37.7 0.9 %collective-permute-start.37 = (f32[24,128]{1,0:T(8,128)S(1)}, f32[24,128]{1,0:T(8,128)S(1)}, u32[]{:S(2)}, u32[]{:S(2)}) collective-permute-start(f32[24,128]{1,0:T(8,128)S(1)} %get-tuple-element.135), channel_id=1, source_target_pairs={{0,2},{1,3},{2,0},{3,1},{4,6},{5,7},{6,4},{7,5},{8,10},{9,11},{10,... | collective-permute-start | bytes 36872 | tf_op jit(solution)/shard_map/ppermute | solution.py:441
  38.5 0.8 %collective-permute-done.37.refs_12_ = f32[24,128]{1,0:T(8,128)S(1)} collective-permute-done((f32[24,128]{1,0:T(8,128)S(1)}, f32[24,128]{1,0:T(8,128)S(1)}, u32[]{:S(2)}, u32[]{:S(2)}) %collective-permute-start.37) | collective-permute-done | bytes 12320 | tf_op jit(solution)/shard_map/ppermute | solution.py:441
  39.4 2.6 %collective-permute-start.40 = (f32[3,128]{1,0:T(4,128)S(1)}, f32[3,128]{1,0:T(4,128)S(1)}, u32[]{:S(2)}, u32[]{:S(2)}) collective-permute-start(f32[3,128]{1,0:T(4,128)S(1)} %slice.433), channel_id=1, source_target_pairs={{0,7},{1,6},{2,5},{3,4},{4,3},{5,2},{6,1},{7,0},{8,15},{9,14},{10,... | collective-permute-start | bytes 4616 | tf_op jit(solution)/shard_map/ppermute | solution.py:441
  42.0 0.3 collective-permute-start.38
  42.3 0.5 collective-permute-start.39
  42.8 2.4 %collective-permute-done.38.refs_13_ = f32[24,128]{1,0:T(8,128)S(1)} collective-permute-done((f32[24,128]{1,0:T(8,128)S(1)}, f32[24,128]{1,0:T(8,128)S(1)}, u32[]{:S(2)}, u32[]{:S(2)}) %collective-permute-start.38) | collective-permute-done | bytes 12320 | tf_op jit(solution)/shard_map/ppermute | solution.py:441
  45.2 0.0 collective-permute-done.40
  45.2 1.0 %collective-permute-done.39 = f32[67,128]{1,0:T(8,128)S(1)} collective-permute-done((f32[67,128]{1,0:T(8,128)S(1)}, f32[67,128]{1,0:T(8,128)S(1)}, u32[]{:S(2)}, u32[]{:S(2)}) %collective-permute-start.39) | collective-permute-done | bytes 34336 | tf_op jit(solution)/shard_map/ppermute | solution.py:441
  46.2 1.1 %collective-permute-start.43 = (f32[24,128]{1,0:T(8,128)S(1)}, f32[24,128]{1,0:T(8,128)S(1)}, u32[]{:S(2)}, u32[]{:S(2)}) collective-permute-start(f32[24,128]{1,0:T(8,128)S(1)} %maximum_add_fusion.5.refs_8_), channel_id=1, source_target_pairs={{0,26},{1,27},{2,24},{3,25},{4,30},{5,31},{6,28},{7,29},{8,18},{9,... | collective-permute-start | bytes 36872 | tf_op jit(solution)/shard_map/ppermute | solution.py:441
  47.3 2.0 %collective-permute-start.42 = (f32[24,128]{1,0:T(8,128)S(1)}, f32[24,128]{1,0:T(8,128)S(1)}, u32[]{:S(2)}, u32[]{:S(2)}) collective-permute-start(f32[24,128]{1,0:T(8,128)S(1)} %maximum_add_fusion.5.refs_8_), channel_id=1, source_target_pairs={{0,18},{1,19},{2,16},{3,17},{4,22},{5,23},{6,20},{7,21},{8,26},{9,... | collective-permute-start | bytes 36872 | tf_op jit(solution)/shard_map/ppermute | solution.py:441
  49.3 0.0 collective-permute-start.41
  49.3 1.9 %collective-permute-done.43.refs_11_ = f32[24,128]{1,0:T(8,128)S(1)} collective-permute-done((f32[24,128]{1,0:T(8,128)S(1)}, f32[24,128]{1,0:T(8,128)S(1)}, u32[]{:S(2)}, u32[]{:S(2)}) %collective-permute-start.43) | collective-permute-done | bytes 12320 | tf_op jit(solution)/shard_map/ppermute | solution.py:441
  51.2 0.1 collective-permute-done.42.refs_10_
  51.3 1.1 %collective-permute-done.41.refs_9_ = f32[24,128]{1,0:T(8,128)S(1)} collective-permute-done((f32[24,128]{1,0:T(8,128)S(1)}, f32[24,128]{1,0:T(8,128)S(1)}, u32[]{:S(2)}, u32[]{:S(2)}) %collective-permute-start.41) | collective-permute-done | bytes 12320 | tf_op jit(solution)/shard_map/ppermute | solution.py:441
  52.4 1.3 %shard_map.170 = (f32[1024,128]{1,0:T(8,128)}, f32[1,128]{1,0:T(1,128)S(1)}, f32[64,128]{1,0:T(8,128)S(1)}, f32[64,256]{1,0:T(8,128)S(1)}, f32[1,128]{1,0:T(1,128)S(1)}, /*index=5*/f32[104,128]{1,0:T(8,128)S(1)}) custom-call(f32[18,64,128]{2,1,0:T(8,128)S(1)} %get-tuple-element.112.refs_0_, bf16[128,512]{1,0:T(8,128)(2,1)S(1)} %get-tuple-element.113.refs_1_, ...), custom_call_target="tpu_custom_call" | custom-call | tf_op jit(solution)/shard_map/pallas_call | solution.py:419
  53.7 0.0 copy-start.14
  53.8 0.0 copy-start.12
  53.8 0.0 copy-start.13
  53.8 0.5 copy-done.14
  54.3 0.1 copy-done.12
  54.4 0.0 copy-done.13
  (59 shorter events, 0.3 us)
Async XLA Ops:
  0.6 4.6 %copy-start.4 = (f32[256]{0:T(256)S(1)}, f32[256]{0:T(256)}, u32[]{:S(2)}) copy-start(f32[256]{0:T(256)} %param.31) | copy-start | bytes 3076
  0.6 4.6 %copy-start.7 = (f32[64,128]{1,0:T(8,128)S(1)}, f32[64,128]{1,0:T(8,128)}, u32[]{:S(2)}) copy-start(f32[64,128]{1,0:T(8,128)} %refs_0_.1) | copy-start | bytes 98308
  0.7 4.6 %copy-start.8 = (f32[64,128]{1,0:T(8,128)S(1)}, f32[64,128]{1,0:T(8,128)}, u32[]{:S(2)}) copy-start(f32[64,128]{1,0:T(8,128)} %refs_2_.2) | copy-start | bytes 98308
  0.7 4.6 %copy-start.10 = (s32[2,256]{1,0:T(2,128)S(1)}, s32[2,256]{1,0:T(2,128)}, u32[]{:S(2)}) copy-start(s32[2,256]{1,0:T(2,128)} %refs_6_.1) | copy-start | bytes 6148
  0.7 4.6 %copy-start.11 = (s32[256]{0:T(256)S(1)}, s32[256]{0:T(256)}, u32[]{:S(2)}) copy-start(s32[256]{0:T(256)} %param.30) | copy-start | bytes 3076
  2.1 5.5 %collective-permute-start.22 = (f32[72,128]{1,0:T(8,128)}, f32[72,128]{1,0:T(8,128)S(1)}, u32[]{:S(2)}, u32[]{:S(2)}) collective-permute-start(f32[72,128]{1,0:T(8,128)} %shard_map.166), channel_id=1, source_target_pairs={{0,1},{1,0},{2,3},{3,2},{4,5},{5,4},{6,7},{7,6},{8,9},{9,8},{10,11... | collective-permute-start | bytes 110600 | tf_op jit(solution)/shard_map/ppermute | solution.py:441
  5.2 0.7 %copy-start.3 = (f32[256]{0:T(256)S(1)}, f32[256]{0:T(256)}, u32[]{:S(2)}) copy-start(f32[256]{0:T(256)} %param.32) | copy-start | bytes 3076
  5.2 0.7 %copy-start.5 = (f32[1,128]{1,0:T(1,128)S(1)}, f32[1,128]{1,0:T(1,128)}, u32[]{:S(2)}) copy-start(f32[1,128]{1,0:T(1,128)} %refs_4_.1) | copy-start | bytes 1540
  5.2 0.7 %copy-start.1 = (s32[1,2048]{1,0:T(1,128)S(1)}, s32[1,2048]{1,0:T(1,128)}, u32[]{:S(2)}) copy-start(s32[1,2048]{1,0:T(1,128)} %param.24) | copy-start | bytes 24580
  5.2 0.7 %copy-start = (f32[16,128]{1,0:T(8,128)S(1)}, f32[16,128]{1,0:T(8,128)}, u32[]{:S(2)}) copy-start(f32[16,128]{1,0:T(8,128)} %refs_3_.2) | copy-start | bytes 24580
  5.2 0.7 %copy-start.2 = (f32[256]{0:T(256)S(1)}, f32[256]{0:T(256)}, u32[]{:S(2)}) copy-start(f32[256]{0:T(256)} %param.26) | copy-start | bytes 3076
  5.9 1.8 %copy-start.9 = (f32[72,128]{1,0:T(8,128)S(1)}, f32[72,128]{1,0:T(8,128)}, u32[]{:S(2)}) copy-start(f32[72,128]{1,0:T(8,128)} %shard_map.166) | copy-start | bytes 110596
  8.2 1.3 %collective-permute-start.23 = (f32[56,128]{1,0:T(8,128)S(1)}, f32[56,128]{1,0:T(8,128)S(1)}, u32[]{:S(2)}, u32[]{:S(2)}) collective-permute-start(f32[56,128]{1,0:T(8,128)S(1)} %get-tuple-element.121), channel_id=1, source_target_pairs={{0,2},{1,3},{2,0},{3,1},{4,6},{5,7},{6,4},{7,5},{8,10},{9,11},{10,... | collective-permute-start | bytes 86024 | tf_op jit(solution)/shard_map/ppermute | solution.py:441
  9.5 5.8 %collective-permute-start.26 = (f32[3,128]{1,0:T(4,128)S(1)}, f32[3,128]{1,0:T(4,128)S(1)}, u32[]{:S(2)}, u32[]{:S(2)}) collective-permute-start(f32[3,128]{1,0:T(4,128)S(1)} %slice.411), channel_id=1, source_target_pairs={{0,7},{1,6},{2,5},{3,4},{4,3},{5,2},{6,1},{7,0},{8,15},{9,14},{10,... | collective-permute-start | bytes 4616 | tf_op jit(solution)/shard_map/ppermute | solution.py:441
  11.9 3.4 %collective-permute-start.24 = (f32[56,128]{1,0:T(8,128)S(1)}, f32[56,128]{1,0:T(8,128)S(1)}, u32[]{:S(2)}, u32[]{:S(2)}) collective-permute-start(f32[56,128]{1,0:T(8,128)S(1)} %pad_maximum_fusion.10), channel_id=1, source_target_pairs={{0,6},{1,7},{2,4},{3,5},{4,2},{5,3},{6,0},{7,1},{8,14},{9,15},{10,... | collective-permute-start | bytes 86024 | tf_op jit(solution)/shard_map/ppermute | solution.py:441
  12.4 4.0 %collective-permute-start.25 = (f32[67,128]{1,0:T(8,128)S(1)}, f32[67,128]{1,0:T(8,128)S(1)}, u32[]{:S(2)}, u32[]{:S(2)}) collective-permute-start(f32[67,128]{1,0:T(8,128)S(1)} %pad_maximum_fusion.7), channel_id=1, source_target_pairs={{0,1},{1,0},{2,3},{3,2},{4,5},{5,4},{6,7},{7,6},{8,9},{9,8},{10,11... | collective-permute-start | bytes 102920 | tf_op jit(solution)/shard_map/ppermute | solution.py:441
  16.4 5.2 %collective-permute-start.29 = (f32[56,128]{1,0:T(8,128)S(1)}, f32[56,128]{1,0:T(8,128)S(1)}, u32[]{:S(2)}, u32[]{:S(2)}) collective-permute-start(f32[56,128]{1,0:T(8,128)S(1)} %maximum_add_fusion.3.refs_6_), channel_id=1, source_target_pairs={{0,26},{1,27},{2,24},{3,25},{4,30},{5,31},{6,28},{7,29},{8,18},{9,... | collective-permute-start | bytes 86024 | tf_op jit(solution)/shard_map/ppermute | solution.py:441
  19.0 4.2 %collective-permute-start.28 = (f32[56,128]{1,0:T(8,128)S(1)}, f32[56,128]{1,0:T(8,128)S(1)}, u32[]{:S(2)}, u32[]{:S(2)}) collective-permute-start(f32[56,128]{1,0:T(8,128)S(1)} %maximum_add_fusion.3.refs_6_), channel_id=1, source_target_pairs={{0,18},{1,19},{2,16},{3,17},{4,22},{5,23},{6,20},{7,21},{8,26},{9,... | collective-permute-start | bytes 86024 | tf_op jit(solution)/shard_map/ppermute | solution.py:441
  19.2 3.9 %collective-permute-start.27 = (f32[56,128]{1,0:T(8,128)S(1)}, f32[56,128]{1,0:T(8,128)S(1)}, u32[]{:S(2)}, u32[]{:S(2)}) collective-permute-start(f32[56,128]{1,0:T(8,128)S(1)} %maximum_add_fusion.3.refs_6_), channel_id=1, source_target_pairs={{0,10},{1,11},{2,8},{3,9},{4,14},{5,15},{6,12},{7,13},{8,2},{9,3},... | collective-permute-start | bytes 86024 | tf_op jit(solution)/shard_map/ppermute | solution.py:441
  24.0 2.1 %collective-permute-start.30 = (f32[24,128]{1,0:T(8,128)S(1)}, f32[24,128]{1,0:T(8,128)S(1)}, u32[]{:S(2)}, u32[]{:S(2)}) collective-permute-start(f32[24,128]{1,0:T(8,128)S(1)} %get-tuple-element.128), channel_id=1, source_target_pairs={{0,2},{1,3},{2,0},{3,1},{4,6},{5,7},{6,4},{7,5},{8,10},{9,11},{10,... | collective-permute-start | bytes 36872 | tf_op jit(solution)/shard_map/ppermute | solution.py:441
  26.1 4.7 %collective-permute-start.33 = (f32[3,128]{1,0:T(4,128)S(1)}, f32[3,128]{1,0:T(4,128)S(1)}, u32[]{:S(2)}, u32[]{:S(2)}) collective-permute-start(f32[3,128]{1,0:T(4,128)S(1)} %slice.422), channel_id=1, source_target_pairs={{0,7},{1,6},{2,5},{3,4},{4,3},{5,2},{6,1},{7,0},{8,15},{9,14},{10,... | collective-permute-start | bytes 4616 | tf_op jit(solution)/shard_map/ppermute | solution.py:441
  27.6 3.2 %collective-permute-start.31 = (f32[24,128]{1,0:T(8,128)S(1)}, f32[24,128]{1,0:T(8,128)S(1)}, u32[]{:S(2)}, u32[]{:S(2)}) collective-permute-start(f32[24,128]{1,0:T(8,128)S(1)} %pad_maximum_fusion.11), channel_id=1, source_target_pairs={{0,6},{1,7},{2,4},{3,5},{4,2},{5,3},{6,0},{7,1},{8,14},{9,15},{10,... | collective-permute-start | bytes 36872 | tf_op jit(solution)/shard_map/ppermute | solution.py:441
  28.0 4.0 %collective-permute-start.32 = (f32[67,128]{1,0:T(8,128)S(1)}, f32[67,128]{1,0:T(8,128)S(1)}, u32[]{:S(2)}, u32[]{:S(2)}) collective-permute-start(f32[67,128]{1,0:T(8,128)S(1)} %pad_maximum_fusion.8), channel_id=1, source_target_pairs={{0,1},{1,0},{2,3},{3,2},{4,5},{5,4},{6,7},{7,6},{8,9},{9,8},{10,11... | collective-permute-start | bytes 102920 | tf_op jit(solution)/shard_map/ppermute | solution.py:441
  31.9 5.0 %collective-permute-start.36 = (f32[24,128]{1,0:T(8,128)S(1)}, f32[24,128]{1,0:T(8,128)S(1)}, u32[]{:S(2)}, u32[]{:S(2)}) collective-permute-start(f32[24,128]{1,0:T(8,128)S(1)} %maximum_add_fusion.4.refs_8_), channel_id=1, source_target_pairs={{0,26},{1,27},{2,24},{3,25},{4,30},{5,31},{6,28},{7,29},{8,18},{9,... | collective-permute-start | bytes 36872 | tf_op jit(solution)/shard_map/ppermute | solution.py:441
  32.4 4.5 %collective-permute-start.35 = (f32[24,128]{1,0:T(8,128)S(1)}, f32[24,128]{1,0:T(8,128)S(1)}, u32[]{:S(2)}, u32[]{:S(2)}) collective-permute-start(f32[24,128]{1,0:T(8,128)S(1)} %maximum_add_fusion.4.refs_8_), channel_id=1, source_target_pairs={{0,18},{1,19},{2,16},{3,17},{4,22},{5,23},{6,20},{7,21},{8,26},{9,... | collective-permute-start | bytes 36872 | tf_op jit(solution)/shard_map/ppermute | solution.py:441
  33.4 3.6 %collective-permute-start.34 = (f32[24,128]{1,0:T(8,128)S(1)}, f32[24,128]{1,0:T(8,128)S(1)}, u32[]{:S(2)}, u32[]{:S(2)}) collective-permute-start(f32[24,128]{1,0:T(8,128)S(1)} %maximum_add_fusion.4.refs_8_), channel_id=1, source_target_pairs={{0,10},{1,11},{2,8},{3,9},{4,14},{5,15},{6,12},{7,13},{8,2},{9,3},... | collective-permute-start | bytes 36872 | tf_op jit(solution)/shard_map/ppermute | solution.py:441
  37.7 1.7 %collective-permute-start.37 = (f32[24,128]{1,0:T(8,128)S(1)}, f32[24,128]{1,0:T(8,128)S(1)}, u32[]{:S(2)}, u32[]{:S(2)}) collective-permute-start(f32[24,128]{1,0:T(8,128)S(1)} %get-tuple-element.135), channel_id=1, source_target_pairs={{0,2},{1,3},{2,0},{3,1},{4,6},{5,7},{6,4},{7,5},{8,10},{9,11},{10,... | collective-permute-start | bytes 36872 | tf_op jit(solution)/shard_map/ppermute | solution.py:441
  39.4 5.8 %collective-permute-start.40 = (f32[3,128]{1,0:T(4,128)S(1)}, f32[3,128]{1,0:T(4,128)S(1)}, u32[]{:S(2)}, u32[]{:S(2)}) collective-permute-start(f32[3,128]{1,0:T(4,128)S(1)} %slice.433), channel_id=1, source_target_pairs={{0,7},{1,6},{2,5},{3,4},{4,3},{5,2},{6,1},{7,0},{8,15},{9,14},{10,... | collective-permute-start | bytes 4616 | tf_op jit(solution)/shard_map/ppermute | solution.py:441
  42.0 3.2 %collective-permute-start.38 = (f32[24,128]{1,0:T(8,128)S(1)}, f32[24,128]{1,0:T(8,128)S(1)}, u32[]{:S(2)}, u32[]{:S(2)}) collective-permute-start(f32[24,128]{1,0:T(8,128)S(1)} %pad_maximum_fusion.12), channel_id=1, source_target_pairs={{0,6},{1,7},{2,4},{3,5},{4,2},{5,3},{6,0},{7,1},{8,14},{9,15},{10,... | collective-permute-start | bytes 36872 | tf_op jit(solution)/shard_map/ppermute | solution.py:441
  42.3 4.0 %collective-permute-start.39 = (f32[67,128]{1,0:T(8,128)S(1)}, f32[67,128]{1,0:T(8,128)S(1)}, u32[]{:S(2)}, u32[]{:S(2)}) collective-permute-start(f32[67,128]{1,0:T(8,128)S(1)} %pad_maximum_fusion.9), channel_id=1, source_target_pairs={{0,1},{1,0},{2,3},{3,2},{4,5},{5,4},{6,7},{7,6},{8,9},{9,8},{10,11... | collective-permute-start | bytes 102920 | tf_op jit(solution)/shard_map/ppermute | solution.py:441
  46.2 5.0 %collective-permute-start.43 = (f32[24,128]{1,0:T(8,128)S(1)}, f32[24,128]{1,0:T(8,128)S(1)}, u32[]{:S(2)}, u32[]{:S(2)}) collective-permute-start(f32[24,128]{1,0:T(8,128)S(1)} %maximum_add_fusion.5.refs_8_), channel_id=1, source_target_pairs={{0,26},{1,27},{2,24},{3,25},{4,30},{5,31},{6,28},{7,29},{8,18},{9,... | collective-permute-start | bytes 36872 | tf_op jit(solution)/shard_map/ppermute | solution.py:441
  47.3 4.0 %collective-permute-start.42 = (f32[24,128]{1,0:T(8,128)S(1)}, f32[24,128]{1,0:T(8,128)S(1)}, u32[]{:S(2)}, u32[]{:S(2)}) collective-permute-start(f32[24,128]{1,0:T(8,128)S(1)} %maximum_add_fusion.5.refs_8_), channel_id=1, source_target_pairs={{0,18},{1,19},{2,16},{3,17},{4,22},{5,23},{6,20},{7,21},{8,26},{9,... | collective-permute-start | bytes 36872 | tf_op jit(solution)/shard_map/ppermute | solution.py:441
  49.3 3.1 %collective-permute-start.41 = (f32[24,128]{1,0:T(8,128)S(1)}, f32[24,128]{1,0:T(8,128)S(1)}, u32[]{:S(2)}, u32[]{:S(2)}) collective-permute-start(f32[24,128]{1,0:T(8,128)S(1)} %maximum_add_fusion.5.refs_8_), channel_id=1, source_target_pairs={{0,10},{1,11},{2,8},{3,9},{4,14},{5,15},{6,12},{7,13},{8,2},{9,3},... | collective-permute-start | bytes 36872 | tf_op jit(solution)/shard_map/ppermute | solution.py:441
  52.4 1.3 %copy-start.6 = (f32[64,16,128]{2,1,0:T(8,128)S(1)}, f32[64,16,128]{2,1,0:T(8,128)}, u32[]{:S(2)}) copy-start(f32[64,16,128]{2,1,0:T(8,128)} %param.20) | copy-start | bytes 1572868
  53.7 0.5 copy-start.14
  53.8 0.6 %copy-start.12 = (f32[64,256]{1,0:T(8,128)}, f32[64,256]{1,0:T(8,128)S(1)}, u32[]{:S(2)}) copy-start(f32[64,256]{1,0:T(8,128)S(1)} %get-tuple-element.145) | copy-start | bytes 196612
  53.8 0.6 %copy-start.13 = (f32[64,128]{1,0:T(8,128)}, f32[64,128]{1,0:T(8,128)S(1)}, u32[]{:S(2)}) copy-start(f32[64,128]{1,0:T(8,128)S(1)} %get-tuple-element.144) | copy-start | bytes 98308

commit v16 on v15

--- a/solution.py
+++ b/solution.py
@@ -99,9 +99,11 @@
     )
 
 
-def first_kernel(sizes, sources, block_ref, ends_ref, limit_ref, pairs_ref, sems):
-    rows = sizes.rows
-    targets = (block_ref.at[pl.ds(0, rows)], ends_ref, limit_ref, pairs_ref)
+def first_kernel(sizes, names_in, names_out, *refs):
+    rows, count = sizes.rows, len(names_in)
+    sources, (block_ref, *outs) = refs[:count], refs[count : count + len(names_out)]
+    ends_ref, limit_ref, pairs_ref, sems = refs[count + len(names_out) :]
+    targets = (block_ref.at[pl.ds(0, rows)], ends_ref, limit_ref, pairs_ref, *outs)
     copies = [
         pltpu.make_async_copy(source, target, sems.at[i])
         for i, (source, target) in enumerate(zip(sources, targets))
@@ -113,7 +115,7 @@
     width = slots // regions
     slot = lax.broadcasted_iota(jnp.int32, (1, slots), 1)
     pair = slot // width
-    for copy in copies[1:]:
+    for copy in copies[1:4]:
         copy.wait()
     in_use = jnp.zeros((1, slots), jnp.int32)
     for target in range(regions):
@@ -128,6 +130,8 @@
         for i, row in enumerate((start, end, bound)):
             block_ref[at + i : at + i + 1, :width] = row[:, chunk * width : (chunk + 1) * width]
     copies[0].wait()
+    for copy in copies[4:]:
+        copy.wait()
 
 
 def start_kernel(sizes, names_in, names_out, *refs):
@@ -199,8 +203,7 @@
     sums_in_ref,
     maps_ref,
     flows_ref,
-    prices_ref,
-    sums_ref,
+    block_ref,
 ):
     rows, techs, nodes = sizes.rows, sizes.techs, sizes.nodes
     slots, regions = sizes.slots, sizes.regions
@@ -227,16 +230,17 @@
     maps_own = maps_ref[pl.ds(pl.multiple_of(own * nodes, nodes), nodes), :]
     balance = balance_ref[...] + dot3(2.0 * flows, maps_own, True)
     step_up = (1.0 / (techs + 8.0)) * balance
-    prices_ref[...] = gathered[own, :rows, :] + step_up
+    block_ref[:rows, :] = gathered[own, :rows, :] + step_up
     change = row_sum(flows * flows)
     slot = lax.broadcasted_iota(jnp.int32, change.shape, 1)
     primal = fold_lanes(jnp.where(slot // slots == own, change, 0.0))
     more = jnp.concatenate(
         [primal, row_sum(step_up * step_up), jnp.zeros((SQUARES - 2, LANES), jnp.float32)], axis=0
     )
-    sums_ref[...] = sums_in_ref[...]
-    squares = sums_in_ref[techs : techs + SQUARES, :] + more
-    sums_ref[techs : techs + SQUARES, :] = squares
+    block_ref[rows:, :] = sums_in_ref[...]
+    block_ref[rows + techs : rows + techs + SQUARES, :] = (
+        sums_in_ref[techs : techs + SQUARES, :] + more
+    )
 
 
 def neighbour_rows(sizes, given, hour_index):
@@ -279,6 +283,7 @@
     at = places(sizes)
     fixed = given.available.at[techs + 1]
     small = given.dispatch.at[techs]
+    out_sums = None if last else gives.block.at[pl.ds(rows, sums_rows(sizes))]
     sums = total_of(given)
     squares = jnp.sum(sums[techs : techs + 2], axis=1, keepdims=True)
     old_weight = jnp.ones((1, 1), jnp.float32) if second else small[at.weight : at.weight + 1, :1]
@@ -368,7 +373,7 @@
         duals_new = jnp.maximum(duals + half_weight * cap_rows, 0.0)
         dual_acc = dual_acc + (duals_new - duals) ** 2
         gives.cap_duals[tech] = duals_new
-        gives.sums[tech : tech + 1, :] = row_sum(avail * duals_new)
+        out_sums[tech : tech + 1, :] = row_sum(avail * duals_new)
 
     step_up = weight / (techs + 8.0) * balance
     if last:
@@ -386,7 +391,7 @@
             first = rows + 2 * techs + 8 * chunk
             gives.kept[first : first + 8, :] = given.flows[rows:, low : low + LANES]
         return
-    gives.prices[...] = prices + step_up
+    gives.block[:rows, :] = prices + step_up
     gives.flows[rows:, local:] = given.flows[rows:, local:]
     gives.cap_duals[techs, :techs, :] = col_weight
     gives.cap_duals[techs, techs : 2 * techs, :] = cost
@@ -410,8 +415,8 @@
     squares = jnp.concatenate(
         [primal_row, dual_row, jnp.zeros((SQUARES - 2, LANES), jnp.float32)], axis=0
     )
-    gives.sums[techs : techs + SQUARES, :] = squares
-    write_halo(sizes, gives.sums, store_new)
+    out_sums[techs : techs + SQUARES, :] = squares
+    write_halo(sizes, out_sums, store_new)
 
 
 def call(kernel, given, outs, flops=0, left=(), scratch=(), limit=VMEM_BYTES):
@@ -458,10 +463,11 @@
     )
 
 
-def exchange(sizes, prices, sums):
+def exchange(sizes, block):
     hours, regions = lax.axis_size("hours"), lax.axis_size("region")
     techs, span = sizes.techs, sizes.units // LANES
     halo = halo_at(sizes)
+    prices, sums = block[: sizes.rows], block[sizes.rows :]
     if regions != 2 or hours != 16:
         gathered = lax.all_gather(prices, "region")
         totals = lax.psum(sums, "hours")
@@ -480,11 +486,12 @@
         return jnp.concatenate([total[:halo], *edges, total[last + span :]], axis=0)
 
     hour = lax.axis_index("hours")
-    partner = swap(sums, 1, 0)
+    beside_core = swap(block, 1, 0)
+    partner_prices, partner = beside_core[: sizes.rows], beside_core[sizes.rows :]
     chip = merged(sums, partner, hour % 2 == 0)
     across = swap(chip, 2 + 1, 0)
     diagonal = swap(chip[techs:halo], 2 + 1, 1)
-    beside = swap(jnp.concatenate([prices, chip[techs:halo]], axis=0), 0, 1)
+    beside = swap(jnp.concatenate([partner_prices, chip[techs:halo]], axis=0), 1, 1)
     other, squares = beside[: sizes.rows], beside[sizes.rows :]
     slab = merged(chip, across, hour // 2 % 2 == 0)
     slab = slab + jnp.pad(squares + diagonal, ((techs, slab.shape[0] - halo), (0, 0)))
@@ -556,7 +563,8 @@
     used = halo_at(sizes) + 2 * sizes.units // LANES
     rows_of.append(jnp.zeros((sums_rows(sizes) - used, nodes)))
     rows_of += [jnp.where(first_hour, part, 0.0) for part in (col_weight, cost)]
-    gathered, parts = exchange(sizes, price_start + step_up, jnp.concatenate(rows_of, axis=0))
+    block = jnp.concatenate([price_start + step_up, *rows_of], axis=0)
+    gathered, parts = exchange(sizes, block)
     flows = jnp.concatenate([flows_local, flows_cross], axis=1)
     spare = jnp.concatenate([jnp.zeros((8, local)), info], axis=1)
     state = Bag(
@@ -580,40 +588,49 @@
     )
     cross = regions * slots
 
-    gathered = both_regions(
-        call(
-            lambda names_in, names_out, *refs: first_kernel(sizes, refs[:4], *refs[4:]),
-            Bag(
-                price=args.price_start,
-                ends=args.cross_ends[:, 0],
-                limit=args.cross_limit,
-                pairs=args.pair_counts,
-            ),
-            Bag(block=shape(rows + 8 * max(1, slots // LANES), nodes)),
-            left=(0, 1, 2, 3),
-            scratch=[
-                pltpu.VMEM((2, slots), jnp.int32),
-                pltpu.VMEM((1, slots), jnp.float32),
-                pltpu.VMEM((1, regions), jnp.int32),
-                pltpu.SemaphoreType.DMA((4,)),
-            ],
-            limit=None,
-        ).block
-    )
+    small = Bag(
+        demand=args.demand,
+        gen_cost=args.gen_cost,
+        cap_cost=args.cap_cost,
+        owner=args.owner_map.reshape(hours, owned),
+        line_ends=args.line_ends,
+        line_limit=args.line_limit[None],
+        store_node=args.store_node[None],
+        store_power=args.store_power[None],
+        store_energy=args.store_energy[None],
+    )
+    given = Bag(
+        price=args.price_start,
+        ends=args.cross_ends[:, 0],
+        limit=args.cross_limit,
+        pairs=args.pair_counts,
+        **vars(small),
+    )
+    first = call(
+        functools.partial(first_kernel, sizes),
+        given,
+        Bag(
+            block=shape(rows + 8 * max(1, slots // LANES), nodes),
+            **{name: shape(*value.shape, dtype=value.dtype) for name, value in vars(small).items()},
+        ),
+        left=range(len(vars(given))),
+        scratch=[
+            pltpu.VMEM((2, slots), jnp.int32),
+            pltpu.VMEM((1, slots), jnp.float32),
+            pltpu.VMEM((1, regions), jnp.int32),
+            pltpu.SemaphoreType.DMA((len(vars(given)),)),
+        ],
+        limit=None,
+    )
+    block = first.block
+    del first.block
+    gathered = both_regions(block)
     state = call(
         functools.partial(start_kernel, sizes),
         Bag(
             availability=args.availability.reshape(rows * techs, nodes),
-            price=args.price_start,
-            demand=args.demand,
-            gen_cost=args.gen_cost,
-            cap_cost=args.cap_cost,
-            owner=args.owner_map.reshape(hours, owned),
-            line_ends=args.line_ends,
-            line_limit=args.line_limit[None],
-            store_node=args.store_node[None],
-            store_power=args.store_power[None],
-            store_energy=args.store_energy[None],
+            price=block[:rows],
+            **vars(first),
         ),
         Bag(
             available=shape(techs + 2, rows, nodes),
@@ -639,13 +656,12 @@
         Bag(
             maps=shape(regions * nodes, cross, dtype=jnp.bfloat16),
             flows=shape(rows + 8, lines + units + cross),
-            prices=shape(rows, nodes),
-            sums=shape(*state.sums.shape),
+            block=shape(rows + state.sums.shape[0], nodes),
         ),
     )
     del state.sums, state.balance, state.flows_local
     state.maps_cross, state.flows = closed.maps, closed.flows
-    gathered, parts = exchange(sizes, closed.prices, closed.sums)
+    gathered, parts = exchange(sizes, closed.block)
     outputs, negative, kept = sweeps(sizes, owned, state, gathered, parts)
 
     def again():
@@ -672,8 +688,7 @@
                 flows=shape(rows + 8, lines + units + sizes.regions * sizes.slots),
                 store_duals=shape(rows, units),
                 charge=shape(rows, units),
-                prices=shape(rows, nodes),
-                sums=shape(sums_rows(sizes), nodes),
+                block=shape(rows + sums_rows(sizes), nodes),
             )
         else:
             outs = Bag(
@@ -686,8 +701,8 @@
             )
         results = call(functools.partial(sweep_kernel, sizes, iteration), given, outs)
         if iteration < ITERS - 1:
-            gathered, parts = exchange(sizes, results.prices, results.sums)
-            del results.prices, results.sums
+            gathered, parts = exchange(sizes, results.block)
+            del results.block
             vars(state).update(vars(results))
     dispatch = results.dispatch.reshape(rows, techs, nodes)
     outputs = (dispatch, results.capacity, results.prices, results.charge)

time: 54.6 us -> 54.6 us (level)
  waiting for transfers between devices: 20 us -> 18.1 us
  local copies, waits for them, and re-layouts: 1.39 us -> 2.13 us
  starting transfers between devices: 25.4 us -> 26.1 us
    ppermute x22, waiting for transfers between devices: 20 us -> 18.1 us  [swap(): return lax.ppermute(value, ('hours', 'region'), pairs)]
    ppermute x22, starting transfers between devices: 25.4 us -> 26.1 us  [swap(): return lax.ppermute(value, ('hours', 'region'), pairs)]
    unnamed x30 -> x36, local copies, waits for them, and re-layouts: 1.34 us -> 2.05 us
where the time goes in v16:
time: 54.6 us; the launch traced here: 54.2 us
  starting transfers between devices  26.1 us (48%)
  waiting for transfers between devices  18.1 us (33%)
  Pallas kernels  6.61 us (12%)
  local copies, waits for them, and re-layouts  2.13 us (4%)
  between operations  1.07 us (2%)
    ppermute x22, starting transfers between devices, swap(): return lax.ppermute(value, ('hours', 'region'), pairs)  26.1 us
    ppermute x22, waiting for transfers between devices, swap(): return lax.ppermute(value, ('hours', 'region'), pairs)  18.1 us
    pallas_call x6, Pallas kernels, call(): pl.pallas_call(functools.partial(kernel, names_in, names_out), out_shape=...  6.61 us
    unnamed x36, local copies, waits for them, and re-layouts  2.05 us
  transfers between devices with their start and end apart: 22, of which 15 were waited for; matrix products, arithmetic and copies ran while one was open for 0% of the time, Pallas kernels for 3%

profile of v16, /device:TPU:0, one launch (start us, length us, event | category | flops | bytes accessed | tf_op | source)
XLA Modules:
  0.0 54.2 jit_solution(18285486188898751708)
XLA Ops:
  0.7 0.7 %copy-done.13 = s32[2,256]{1,0:T(2,128)S(1)} copy-done((s32[2,256]{1,0:T(2,128)S(1)}, s32[2,256]{1,0:T(2,128)}, u32[]{:S(2)}) %copy-start.13) | copy-done | bytes 2072
  1.3 0.0 copy-done.14
  1.3 1.6 %shard_map.165 = (f32[72,128]{1,0:T(8,128)}, f32[64,128]{1,0:T(8,128)}, f32[16,128]{1,0:T(8,128)}, f32[1,128]{1,0:T(1,128)}, s32[16,128]{1,0:T(8,128)}, /*index=...) custom-call(f32[64,128]{1,0:T(8,128)} %refs_0_.1, ...), custom_call_target="tpu_custom_call" | custom-call | tf_op jit(solution)/shard_map/pallas_call | solution.py:424
  2.9 0.0 copy-start.12
  3.0 3.0 %collective-permute-start.22 = (f32[72,128]{1,0:T(8,128)}, f32[72,128]{1,0:T(8,128)S(1)}, u32[]{:S(2)}, u32[]{:S(2)}) collective-permute-start(f32[72,128]{1,0:T(8,128)} %get-tuple-element.117), channel_id=1, source_target_pairs={{0,1},{1,0},{2,3},{3,2},{4,5},{5,4},{6,7},{7,6},{8,9},{9,8},{10,11... | collective-permute-start | bytes 110600 | tf_op jit(solution)/shard_map/ppermute | solution.py:446
  6.0 0.0 copy-start.8
  6.0 0.0 copy-start
  6.1 0.6 %copy-done.1 = f32[16,128]{1,0:T(8,128)S(1)} copy-done((f32[16,128]{1,0:T(8,128)S(1)}, f32[16,128]{1,0:T(8,128)}, u32[]{:S(2)}) %copy-start.1) | copy-done | bytes 8216
  6.7 0.0 copy-done.2
  6.7 0.1 copy-done
  6.8 1.7 %shard_map.166 = (f32[18,64,128]{2,1,0:T(8,128)S(1)}, bf16[128,512]{1,0:T(8,128)(2,1)S(1)}, f32[64,512]{1,0:T(8,128)S(1)}, f32[64,256]{1,0:T(8,128)S(1)}, f32[17...) custom-call(f32[1024,128]{1,0:T(8,128)} %bitcast.82, f32[64,128]{1,0:T(8,128)S(1)} %slice.422.refs_1_, ...), custom_call_target="tpu_custom_call" | custom-call | flops 1000000 | bytes 4000000 | tf_op jit(solution)/shard_map/pallas_call | solution.py:424
  8.6 0.0 collective-permute-done.22
  8.6 0.4 shard_map.167
  9.0 0.1 collective-permute-start.23
  9.1 1.2 %collective-permute-done.23 = f32[120,128]{1,0:T(8,128)S(1)} collective-permute-done((f32[120,128]{1,0:T(8,128)S(1)}, f32[120,128]{1,0:T(8,128)S(1)}, u32[]{:S(2)}, u32[]{:S(2)}) %collective-permute-start.23) | collective-permute-done | bytes 61472 | tf_op jit(solution)/shard_map/ppermute | solution.py:446
  10.4 2.3 %collective-permute-start.26 = (f32[3,128]{1,0:T(4,128)S(1)}, f32[3,128]{1,0:T(4,128)S(1)}, u32[]{:S(2)}, u32[]{:S(2)}) collective-permute-start(f32[3,128]{1,0:T(4,128)S(1)} %slice.527), channel_id=1, source_target_pairs={{0,7},{1,6},{2,5},{3,4},{4,3},{5,2},{6,1},{7,0},{8,15},{9,14},{10,... | collective-permute-start | bytes 4616 | tf_op jit(solution)/shard_map/ppermute | solution.py:446
  12.7 0.6 %collective-permute-start.24 = (f32[56,128]{1,0:T(8,128)S(1)}, f32[56,128]{1,0:T(8,128)S(1)}, u32[]{:S(2)}, u32[]{:S(2)}) collective-permute-start(f32[56,128]{1,0:T(8,128)S(1)} %pad_maximum_fusion.10), channel_id=1, source_target_pairs={{0,6},{1,7},{2,4},{3,5},{4,2},{5,3},{6,0},{7,1},{8,14},{9,15},{10,... | collective-permute-start | bytes 86024 | tf_op jit(solution)/shard_map/ppermute | solution.py:446
  13.3 0.3 collective-permute-start.25
  13.6 2.5 %collective-permute-done.24.refs_11_ = f32[56,128]{1,0:T(8,128)S(1)} collective-permute-done((f32[56,128]{1,0:T(8,128)S(1)}, f32[56,128]{1,0:T(8,128)S(1)}, u32[]{:S(2)}, u32[]{:S(2)}) %collective-permute-start.24) | collective-permute-done | bytes 28704 | tf_op jit(solution)/shard_map/ppermute | solution.py:446
  16.1 0.0 collective-permute-done.26
  16.2 0.6 %collective-permute-done.25 = f32[67,128]{1,0:T(8,128)S(1)} collective-permute-done((f32[67,128]{1,0:T(8,128)S(1)}, f32[67,128]{1,0:T(8,128)S(1)}, u32[]{:S(2)}, u32[]{:S(2)}) %collective-permute-start.25) | collective-permute-done | bytes 34336 | tf_op jit(solution)/shard_map/ppermute | solution.py:446
  16.8 3.4 %collective-permute-start.29 = (f32[56,128]{1,0:T(8,128)S(1)}, f32[56,128]{1,0:T(8,128)S(1)}, u32[]{:S(2)}, u32[]{:S(2)}) collective-permute-start(f32[56,128]{1,0:T(8,128)S(1)} %maximum_add_fusion.3.refs_6_), channel_id=1, source_target_pairs={{0,26},{1,27},{2,24},{3,25},{4,30},{5,31},{6,28},{7,29},{8,18},{9,... | collective-permute-start | bytes 86024 | tf_op jit(solution)/shard_map/ppermute | solution.py:446
  20.3 0.0 collective-permute-start.28
  20.3 0.6 %collective-permute-start.27 = (f32[56,128]{1,0:T(8,128)S(1)}, f32[56,128]{1,0:T(8,128)S(1)}, u32[]{:S(2)}, u32[]{:S(2)}) collective-permute-start(f32[56,128]{1,0:T(8,128)S(1)} %maximum_add_fusion.3.refs_6_), channel_id=1, source_target_pairs={{0,10},{1,11},{2,8},{3,9},{4,14},{5,15},{6,12},{7,13},{8,2},{9,3},... | collective-permute-start | bytes 86024 | tf_op jit(solution)/shard_map/ppermute | solution.py:446
  20.9 1.1 %collective-permute-done.29.refs_9_ = f32[56,128]{1,0:T(8,128)S(1)} collective-permute-done((f32[56,128]{1,0:T(8,128)S(1)}, f32[56,128]{1,0:T(8,128)S(1)}, u32[]{:S(2)}, u32[]{:S(2)}) %collective-permute-start.29) | collective-permute-done | bytes 28704 | tf_op jit(solution)/shard_map/ppermute | solution.py:446
  22.0 2.5 %collective-permute-done.28.refs_8_ = f32[56,128]{1,0:T(8,128)S(1)} collective-permute-done((f32[56,128]{1,0:T(8,128)S(1)}, f32[56,128]{1,0:T(8,128)S(1)}, u32[]{:S(2)}, u32[]{:S(2)}) %collective-permute-start.28) | collective-permute-done | bytes 28704 | tf_op jit(solution)/shard_map/ppermute | solution.py:446
  24.4 0.0 collective-permute-done.27.refs_7_
  24.4 0.8 %shard_map.168 = (f32[17,64,128]{2,1,0:T(8,128)S(1)}, f32[17,64,128]{2,1,0:T(8,128)S(1)}, f32[72,640]{1,0:T(8,128)S(1)}, f32[64,256]{1,0:T(8,128)S(1)}, f32[64,256]{1,0:T(8,128)S(1)}, /*index=5*/f32[88,128]{1,0:T(8,128)S(1)}) custom-call(f32[18,64,128]{2,1,0:T(8,128)S(1)} %get-tuple-element.127.refs_0_, bf16[128,512]{1,0:T(8,128)(2,1)S(1)} %get-tuple-element.128.refs_1_, ...), custom_call_target="tpu_custom_call" | custom-call | tf_op jit(solution)/shard_map/pallas_call | solution.py:424
  25.3 0.4 collective-permute-start.30
  25.7 0.9 %collective-permute-done.30 = f32[88,128]{1,0:T(8,128)S(1)} collective-permute-done((f32[88,128]{1,0:T(8,128)S(1)}, f32[88,128]{1,0:T(8,128)S(1)}, u32[]{:S(2)}, u32[]{:S(2)}) %collective-permute-start.30) | collective-permute-done | bytes 45088 | tf_op jit(solution)/shard_map/ppermute | solution.py:446
  26.6 1.5 %collective-permute-start.33 = (f32[3,128]{1,0:T(4,128)S(1)}, f32[3,128]{1,0:T(4,128)S(1)}, u32[]{:S(2)}, u32[]{:S(2)}) collective-permute-start(f32[3,128]{1,0:T(4,128)S(1)} %slice.540), channel_id=1, source_target_pairs={{0,7},{1,6},{2,5},{3,4},{4,3},{5,2},{6,1},{7,0},{8,15},{9,14},{10,... | collective-permute-start | bytes 4616 | tf_op jit(solution)/shard_map/ppermute | solution.py:446
  28.1 0.4 collective-permute-start.31
  28.4 1.5 %collective-permute-start.32 = (f32[67,128]{1,0:T(8,128)S(1)}, f32[67,128]{1,0:T(8,128)S(1)}, u32[]{:S(2)}, u32[]{:S(2)}) collective-permute-start(f32[67,128]{1,0:T(8,128)S(1)} %pad_maximum_fusion.8), channel_id=1, source_target_pairs={{0,3},{1,2},{2,1},{3,0},{4,7},{5,6},{6,5},{7,4},{8,11},{9,10},{10,... | collective-permute-start | bytes 102920 | tf_op jit(solution)/shard_map/ppermute | solution.py:446
  30.0 1.3 %collective-permute-done.31.refs_13_ = f32[24,128]{1,0:T(8,128)S(1)} collective-permute-done((f32[24,128]{1,0:T(8,128)S(1)}, f32[24,128]{1,0:T(8,128)S(1)}, u32[]{:S(2)}, u32[]{:S(2)}) %collective-permute-start.31) | collective-permute-done | bytes 12320 | tf_op jit(solution)/shard_map/ppermute | solution.py:446
  31.3 0.0 collective-permute-done.33
  31.3 0.6 %collective-permute-done.32 = f32[67,128]{1,0:T(8,128)S(1)} collective-permute-done((f32[67,128]{1,0:T(8,128)S(1)}, f32[67,128]{1,0:T(8,128)S(1)}, u32[]{:S(2)}, u32[]{:S(2)}) %collective-permute-start.32) | collective-permute-done | bytes 34336 | tf_op jit(solution)/shard_map/ppermute | solution.py:446
  31.9 1.7 %collective-permute-start.36 = (f32[24,128]{1,0:T(8,128)S(1)}, f32[24,128]{1,0:T(8,128)S(1)}, u32[]{:S(2)}, u32[]{:S(2)}) collective-permute-start(f32[24,128]{1,0:T(8,128)S(1)} %maximum_add_fusion.4.refs_8_), channel_id=1, source_target_pairs={{0,26},{1,27},{2,24},{3,25},{4,30},{5,31},{6,28},{7,29},{8,18},{9,... | collective-permute-start | bytes 36872 | tf_op jit(solution)/shard_map/ppermute | solution.py:446
  33.6 0.2 collective-permute-start.35
  33.9 2.1 %collective-permute-start.34 = (f32[24,128]{1,0:T(8,128)S(1)}, f32[24,128]{1,0:T(8,128)S(1)}, u32[]{:S(2)}, u32[]{:S(2)}) collective-permute-start(f32[24,128]{1,0:T(8,128)S(1)} %maximum_add_fusion.4.refs_8_), channel_id=1, source_target_pairs={{0,10},{1,11},{2,8},{3,9},{4,14},{5,15},{6,12},{7,13},{8,2},{9,3},... | collective-permute-start | bytes 36872 | tf_op jit(solution)/shard_map/ppermute | solution.py:446
  36.0 0.8 %collective-permute-done.36.refs_11_ = f32[24,128]{1,0:T(8,128)S(1)} collective-permute-done((f32[24,128]{1,0:T(8,128)S(1)}, f32[24,128]{1,0:T(8,128)S(1)}, u32[]{:S(2)}, u32[]{:S(2)}) %collective-permute-start.36) | collective-permute-done | bytes 12320 | tf_op jit(solution)/shard_map/ppermute | solution.py:446
  36.9 0.8 %collective-permute-done.35.refs_10_ = f32[24,128]{1,0:T(8,128)S(1)} collective-permute-done((f32[24,128]{1,0:T(8,128)S(1)}, f32[24,128]{1,0:T(8,128)S(1)}, u32[]{:S(2)}, u32[]{:S(2)}) %collective-permute-start.35) | collective-permute-done | bytes 12320 | tf_op jit(solution)/shard_map/ppermute | solution.py:446
  37.7 0.0 collective-permute-done.34.refs_9_
  37.7 0.7 %shard_map.169 = (f32[17,64,128]{2,1,0:T(8,128)S(1)}, f32[17,64,128]{2,1,0:T(8,128)S(1)}, f32[72,640]{1,0:T(8,128)S(1)}, f32[64,256]{1,0:T(8,128)S(1)}, f32[64,256]{1,0:T(8,128)S(1)}, /*index=5*/f32[88,128]{1,0:T(8,128)S(1)}) custom-call(f32[18,64,128]{2,1,0:T(8,128)S(1)} %get-tuple-element.127.refs_0_, bf16[128,512]{1,0:T(8,128)(2,1)S(1)} %get-tuple-element.128.refs_1_, ...), custom_call_target="tpu_custom_call" | custom-call | tf_op jit(solution)/shard_map/pallas_call | solution.py:424
  38.4 0.5 collective-permute-start.37
  38.9 0.9 %collective-permute-done.37 = f32[88,128]{1,0:T(8,128)S(1)} collective-permute-done((f32[88,128]{1,0:T(8,128)S(1)}, f32[88,128]{1,0:T(8,128)S(1)}, u32[]{:S(2)}, u32[]{:S(2)}) %collective-permute-start.37) | collective-permute-done | bytes 45088 | tf_op jit(solution)/shard_map/ppermute | solution.py:446
  39.8 2.5 %collective-permute-start.40 = (f32[3,128]{1,0:T(4,128)S(1)}, f32[3,128]{1,0:T(4,128)S(1)}, u32[]{:S(2)}, u32[]{:S(2)}) collective-permute-start(f32[3,128]{1,0:T(4,128)S(1)} %slice.553), channel_id=1, source_target_pairs={{0,7},{1,6},{2,5},{3,4},{4,3},{5,2},{6,1},{7,0},{8,15},{9,14},{10,... | collective-permute-start | bytes 4616 | tf_op jit(solution)/shard_map/ppermute | solution.py:446
  42.3 0.4 collective-permute-start.38
  42.6 0.5 collective-permute-start.39
  43.2 2.3 %collective-permute-done.38.refs_13_ = f32[24,128]{1,0:T(8,128)S(1)} collective-permute-done((f32[24,128]{1,0:T(8,128)S(1)}, f32[24,128]{1,0:T(8,128)S(1)}, u32[]{:S(2)}, u32[]{:S(2)}) %collective-permute-start.38) | collective-permute-done | bytes 12320 | tf_op jit(solution)/shard_map/ppermute | solution.py:446
  45.5 0.0 collective-permute-done.40
  45.5 0.6 %collective-permute-done.39 = f32[67,128]{1,0:T(8,128)S(1)} collective-permute-done((f32[67,128]{1,0:T(8,128)S(1)}, f32[67,128]{1,0:T(8,128)S(1)}, u32[]{:S(2)}, u32[]{:S(2)}) %collective-permute-start.39) | collective-permute-done | bytes 34336 | tf_op jit(solution)/shard_map/ppermute | solution.py:446
  46.1 2.1 %collective-permute-start.43 = (f32[24,128]{1,0:T(8,128)S(1)}, f32[24,128]{1,0:T(8,128)S(1)}, u32[]{:S(2)}, u32[]{:S(2)}) collective-permute-start(f32[24,128]{1,0:T(8,128)S(1)} %maximum_add_fusion.5.refs_8_), channel_id=1, source_target_pairs={{0,26},{1,27},{2,24},{3,25},{4,30},{5,31},{6,28},{7,29},{8,18},{9,... | collective-permute-start | bytes 36872 | tf_op jit(solution)/shard_map/ppermute | solution.py:446
  48.2 0.6 %collective-permute-start.42 = (f32[24,128]{1,0:T(8,128)S(1)}, f32[24,128]{1,0:T(8,128)S(1)}, u32[]{:S(2)}, u32[]{:S(2)}) collective-permute-start(f32[24,128]{1,0:T(8,128)S(1)} %maximum_add_fusion.5.refs_8_), channel_id=1, source_target_pairs={{0,18},{1,19},{2,16},{3,17},{4,22},{5,23},{6,20},{7,21},{8,26},{9,... | collective-permute-start | bytes 36872 | tf_op jit(solution)/shard_map/ppermute | solution.py:446
  48.8 1.4 %collective-permute-start.41 = (f32[24,128]{1,0:T(8,128)S(1)}, f32[24,128]{1,0:T(8,128)S(1)}, u32[]{:S(2)}, u32[]{:S(2)}) collective-permute-start(f32[24,128]{1,0:T(8,128)S(1)} %maximum_add_fusion.5.refs_8_), channel_id=1, source_target_pairs={{0,10},{1,11},{2,8},{3,9},{4,14},{5,15},{6,12},{7,13},{8,2},{9,3},... | collective-permute-start | bytes 36872 | tf_op jit(solution)/shard_map/ppermute | solution.py:446
  50.2 0.8 %collective-permute-done.43.refs_11_ = f32[24,128]{1,0:T(8,128)S(1)} collective-permute-done((f32[24,128]{1,0:T(8,128)S(1)}, f32[24,128]{1,0:T(8,128)S(1)}, u32[]{:S(2)}, u32[]{:S(2)}) %collective-permute-start.43) | collective-permute-done | bytes 12320 | tf_op jit(solution)/shard_map/ppermute | solution.py:446
  51.1 1.1 %collective-permute-done.42.refs_10_ = f32[24,128]{1,0:T(8,128)S(1)} collective-permute-done((f32[24,128]{1,0:T(8,128)S(1)}, f32[24,128]{1,0:T(8,128)S(1)}, u32[]{:S(2)}, u32[]{:S(2)}) %collective-permute-start.42) | collective-permute-done | bytes 12320 | tf_op jit(solution)/shard_map/ppermute | solution.py:446
  52.2 0.0 collective-permute-done.41.refs_9_
  52.2 1.3 %shard_map.170 = (f32[1024,128]{1,0:T(8,128)}, f32[1,128]{1,0:T(1,128)S(1)}, f32[64,128]{1,0:T(8,128)S(1)}, f32[64,256]{1,0:T(8,128)S(1)}, f32[1,128]{1,0:T(1,128)S(1)}, /*index=5*/f32[104,128]{1,0:T(8,128)S(1)}) custom-call(f32[18,64,128]{2,1,0:T(8,128)S(1)} %get-tuple-element.127.refs_0_, bf16[128,512]{1,0:T(8,128)(2,1)S(1)} %get-tuple-element.128.refs_1_, ...), custom_call_target="tpu_custom_call" | custom-call | tf_op jit(solution)/shard_map/pallas_call | solution.py:424
  53.6 0.0 copy-start.17
  53.6 0.0 copy-start.15
  53.6 0.0 copy-start.16
  53.6 0.5 copy-done.17
  54.1 0.1 copy-done.15
  54.2 0.0 copy-done.16
  (72 shorter events, 0.4 us)
Async XLA Ops:
  0.6 0.7 %copy-start.13 = (s32[2,256]{1,0:T(2,128)S(1)}, s32[2,256]{1,0:T(2,128)}, u32[]{:S(2)}) copy-start(s32[2,256]{1,0:T(2,128)} %refs_8_.1) | copy-start | bytes 6148
  0.6 0.7 %copy-start.14 = (s32[256]{0:T(256)S(1)}, s32[256]{0:T(256)}, u32[]{:S(2)}) copy-start(s32[256]{0:T(256)} %param.30) | copy-start | bytes 3076
  2.9 3.0 %copy-start.12 = (f32[72,128]{1,0:T(8,128)S(1)}, f32[72,128]{1,0:T(8,128)}, u32[]{:S(2)}) copy-start(f32[72,128]{1,0:T(8,128)} %get-tuple-element.117) | copy-start | bytes 110596
  3.0 5.6 %collective-permute-start.22 = (f32[72,128]{1,0:T(8,128)}, f32[72,128]{1,0:T(8,128)S(1)}, u32[]{:S(2)}, u32[]{:S(2)}) collective-permute-start(f32[72,128]{1,0:T(8,128)} %get-tuple-element.117), channel_id=1, source_target_pairs={{0,1},{1,0},{2,3},{3,2},{4,5},{5,4},{6,7},{7,6},{8,9},{9,8},{10,11... | collective-permute-start | bytes 110600 | tf_op jit(solution)/shard_map/ppermute | solution.py:446
  6.0 0.7 %copy-start.1 = (f32[16,128]{1,0:T(8,128)S(1)}, f32[16,128]{1,0:T(8,128)}, u32[]{:S(2)}) copy-start(f32[16,128]{1,0:T(8,128)} %get-tuple-element.119.refs_3_) | copy-start | bytes 24580
  6.0 0.7 %copy-start.2 = (s32[16,128]{1,0:T(8,128)S(1)}, s32[16,128]{1,0:T(8,128)}, u32[]{:S(2)}) copy-start(s32[16,128]{1,0:T(8,128)} %get-tuple-element.121.refs_5_) | copy-start | bytes 24580
  6.0 0.7 %copy-start.4 = (f32[1,256]{1,0:T(1,128)S(1)}, f32[1,256]{1,0:T(1,128)}, u32[]{:S(2)}) copy-start(f32[1,256]{1,0:T(1,128)} %get-tuple-element.123.refs_7_) | copy-start | bytes 3076
  6.0 0.7 %copy-start.5 = (s32[1,256]{1,0:T(1,128)S(1)}, s32[1,256]{1,0:T(1,128)}, u32[]{:S(2)}) copy-start(s32[1,256]{1,0:T(1,128)} %get-tuple-element.124.refs_8_) | copy-start | bytes 3076
  6.0 0.7 %copy-start.6 = (f32[1,256]{1,0:T(1,128)S(1)}, f32[1,256]{1,0:T(1,128)}, u32[]{:S(2)}) copy-start(f32[1,256]{1,0:T(1,128)} %get-tuple-element.125.refs_9_) | copy-start | bytes 3076
  6.0 0.7 %copy-start.7 = (f32[1,256]{1,0:T(1,128)S(1)}, f32[1,256]{1,0:T(1,128)}, u32[]{:S(2)}) copy-start(f32[1,256]{1,0:T(1,128)} %get-tuple-element.126.refs_10_) | copy-start | bytes 3076
  6.0 0.7 %copy-start.8 = (f32[1,128]{1,0:T(1,128)S(1)}, f32[1,128]{1,0:T(1,128)}, u32[]{:S(2)}) copy-start(f32[1,128]{1,0:T(1,128)} %get-tuple-element.120.refs_4_) | copy-start | bytes 1540
  6.0 0.8 %copy-start = (f32[64,128]{1,0:T(8,128)S(1)}, f32[64,128]{1,0:T(8,128)}, u32[]{:S(2)}) copy-start(f32[64,128]{1,0:T(8,128)} %get-tuple-element.118.refs_2_) | copy-start | bytes 98308
  6.1 0.7 %copy-start.3 = (s32[2,256]{1,0:T(2,128)S(1)}, s32[2,256]{1,0:T(2,128)}, u32[]{:S(2)}) copy-start(s32[2,256]{1,0:T(2,128)} %get-tuple-element.122.refs_6_) | copy-start | bytes 6148
  9.0 1.3 %collective-permute-start.23 = (f32[120,128]{1,0:T(8,128)S(1)}, f32[120,128]{1,0:T(8,128)S(1)}, u32[]{:S(2)}, u32[]{:S(2)}) collective-permute-start(f32[120,128]{1,0:T(8,128)S(1)} %get-tuple-element.136), channel_id=1, source_target_pairs={{0,2},{1,3},{2,0},{3,1},{4,6},{5,7},{6,4},{7,5},{8,10},{9,11},{10,... | collective-permute-start | bytes 184328 | tf_op jit(solution)/shard_map/ppermute | solution.py:446
  10.4 5.8 %collective-permute-start.26 = (f32[3,128]{1,0:T(4,128)S(1)}, f32[3,128]{1,0:T(4,128)S(1)}, u32[]{:S(2)}, u32[]{:S(2)}) collective-permute-start(f32[3,128]{1,0:T(4,128)S(1)} %slice.527), channel_id=1, source_target_pairs={{0,7},{1,6},{2,5},{3,4},{4,3},{5,2},{6,1},{7,0},{8,15},{9,14},{10,... | collective-permute-start | bytes 4616 | tf_op jit(solution)/shard_map/ppermute | solution.py:446
  12.7 3.4 %collective-permute-start.24 = (f32[56,128]{1,0:T(8,128)S(1)}, f32[56,128]{1,0:T(8,128)S(1)}, u32[]{:S(2)}, u32[]{:S(2)}) collective-permute-start(f32[56,128]{1,0:T(8,128)S(1)} %pad_maximum_fusion.10), channel_id=1, source_target_pairs={{0,6},{1,7},{2,4},{3,5},{4,2},{5,3},{6,0},{7,1},{8,14},{9,15},{10,... | collective-permute-start | bytes 86024 | tf_op jit(solution)/shard_map/ppermute | solution.py:446
  13.3 3.5 %collective-permute-start.25 = (f32[67,128]{1,0:T(8,128)S(1)}, f32[67,128]{1,0:T(8,128)S(1)}, u32[]{:S(2)}, u32[]{:S(2)}) collective-permute-start(f32[67,128]{1,0:T(8,128)S(1)} %pad_maximum_fusion.7), channel_id=1, source_target_pairs={{0,3},{1,2},{2,1},{3,0},{4,7},{5,6},{6,5},{7,4},{8,11},{9,10},{10,... | collective-permute-start | bytes 102920 | tf_op jit(solution)/shard_map/ppermute | solution.py:446
  16.8 5.2 %collective-permute-start.29 = (f32[56,128]{1,0:T(8,128)S(1)}, f32[56,128]{1,0:T(8,128)S(1)}, u32[]{:S(2)}, u32[]{:S(2)}) collective-permute-start(f32[56,128]{1,0:T(8,128)S(1)} %maximum_add_fusion.3.refs_6_), channel_id=1, source_target_pairs={{0,26},{1,27},{2,24},{3,25},{4,30},{5,31},{6,28},{7,29},{8,18},{9,... | collective-permute-start | bytes 86024 | tf_op jit(solution)/shard_map/ppermute | solution.py:446
  20.3 4.2 %collective-permute-start.28 = (f32[56,128]{1,0:T(8,128)S(1)}, f32[56,128]{1,0:T(8,128)S(1)}, u32[]{:S(2)}, u32[]{:S(2)}) collective-permute-start(f32[56,128]{1,0:T(8,128)S(1)} %maximum_add_fusion.3.refs_6_), channel_id=1, source_target_pairs={{0,18},{1,19},{2,16},{3,17},{4,22},{5,23},{6,20},{7,21},{8,26},{9,... | collective-permute-start | bytes 86024 | tf_op jit(solution)/shard_map/ppermute | solution.py:446
  20.3 4.2 %collective-permute-start.27 = (f32[56,128]{1,0:T(8,128)S(1)}, f32[56,128]{1,0:T(8,128)S(1)}, u32[]{:S(2)}, u32[]{:S(2)}) collective-permute-start(f32[56,128]{1,0:T(8,128)S(1)} %maximum_add_fusion.3.refs_6_), channel_id=1, source_target_pairs={{0,10},{1,11},{2,8},{3,9},{4,14},{5,15},{6,12},{7,13},{8,2},{9,3},... | collective-permute-start | bytes 86024 | tf_op jit(solution)/shard_map/ppermute | solution.py:446
  25.3 1.3 %collective-permute-start.30 = (f32[88,128]{1,0:T(8,128)S(1)}, f32[88,128]{1,0:T(8,128)S(1)}, u32[]{:S(2)}, u32[]{:S(2)}) collective-permute-start(f32[88,128]{1,0:T(8,128)S(1)} %get-tuple-element.142), channel_id=1, source_target_pairs={{0,2},{1,3},{2,0},{3,1},{4,6},{5,7},{6,4},{7,5},{8,10},{9,11},{10,... | collective-permute-start | bytes 135176 | tf_op jit(solution)/shard_map/ppermute | solution.py:446
  26.6 4.7 %collective-permute-start.33 = (f32[3,128]{1,0:T(4,128)S(1)}, f32[3,128]{1,0:T(4,128)S(1)}, u32[]{:S(2)}, u32[]{:S(2)}) collective-permute-start(f32[3,128]{1,0:T(4,128)S(1)} %slice.540), channel_id=1, source_target_pairs={{0,7},{1,6},{2,5},{3,4},{4,3},{5,2},{6,1},{7,0},{8,15},{9,14},{10,... | collective-permute-start | bytes 4616 | tf_op jit(solution)/shard_map/ppermute | solution.py:446
  28.1 3.2 %collective-permute-start.31 = (f32[24,128]{1,0:T(8,128)S(1)}, f32[24,128]{1,0:T(8,128)S(1)}, u32[]{:S(2)}, u32[]{:S(2)}) collective-permute-start(f32[24,128]{1,0:T(8,128)S(1)} %pad_maximum_fusion.11), channel_id=1, source_target_pairs={{0,6},{1,7},{2,4},{3,5},{4,2},{5,3},{6,0},{7,1},{8,14},{9,15},{10,... | collective-permute-start | bytes 36872 | tf_op jit(solution)/shard_map/ppermute | solution.py:446
  28.4 3.4 %collective-permute-start.32 = (f32[67,128]{1,0:T(8,128)S(1)}, f32[67,128]{1,0:T(8,128)S(1)}, u32[]{:S(2)}, u32[]{:S(2)}) collective-permute-start(f32[67,128]{1,0:T(8,128)S(1)} %pad_maximum_fusion.8), channel_id=1, source_target_pairs={{0,3},{1,2},{2,1},{3,0},{4,7},{5,6},{6,5},{7,4},{8,11},{9,10},{10,... | collective-permute-start | bytes 102920 | tf_op jit(solution)/shard_map/ppermute | solution.py:446
  31.9 5.0 %collective-permute-start.36 = (f32[24,128]{1,0:T(8,128)S(1)}, f32[24,128]{1,0:T(8,128)S(1)}, u32[]{:S(2)}, u32[]{:S(2)}) collective-permute-start(f32[24,128]{1,0:T(8,128)S(1)} %maximum_add_fusion.4.refs_8_), channel_id=1, source_target_pairs={{0,26},{1,27},{2,24},{3,25},{4,30},{5,31},{6,28},{7,29},{8,18},{9,... | collective-permute-start | bytes 36872 | tf_op jit(solution)/shard_map/ppermute | solution.py:446
  33.6 4.0 %collective-permute-start.35 = (f32[24,128]{1,0:T(8,128)S(1)}, f32[24,128]{1,0:T(8,128)S(1)}, u32[]{:S(2)}, u32[]{:S(2)}) collective-permute-start(f32[24,128]{1,0:T(8,128)S(1)} %maximum_add_fusion.4.refs_8_), channel_id=1, source_target_pairs={{0,18},{1,19},{2,16},{3,17},{4,22},{5,23},{6,20},{7,21},{8,26},{9,... | collective-permute-start | bytes 36872 | tf_op jit(solution)/shard_map/ppermute | solution.py:446
  33.9 3.8 %collective-permute-start.34 = (f32[24,128]{1,0:T(8,128)S(1)}, f32[24,128]{1,0:T(8,128)S(1)}, u32[]{:S(2)}, u32[]{:S(2)}) collective-permute-start(f32[24,128]{1,0:T(8,128)S(1)} %maximum_add_fusion.4.refs_8_), channel_id=1, source_target_pairs={{0,10},{1,11},{2,8},{3,9},{4,14},{5,15},{6,12},{7,13},{8,2},{9,3},... | collective-permute-start | bytes 36872 | tf_op jit(solution)/shard_map/ppermute | solution.py:446
  38.4 1.4 %collective-permute-start.37 = (f32[88,128]{1,0:T(8,128)S(1)}, f32[88,128]{1,0:T(8,128)S(1)}, u32[]{:S(2)}, u32[]{:S(2)}) collective-permute-start(f32[88,128]{1,0:T(8,128)S(1)} %get-tuple-element.148), channel_id=1, source_target_pairs={{0,2},{1,3},{2,0},{3,1},{4,6},{5,7},{6,4},{7,5},{8,10},{9,11},{10,... | collective-permute-start | bytes 135176 | tf_op jit(solution)/shard_map/ppermute | solution.py:446
  39.8 5.7 %collective-permute-start.40 = (f32[3,128]{1,0:T(4,128)S(1)}, f32[3,128]{1,0:T(4,128)S(1)}, u32[]{:S(2)}, u32[]{:S(2)}) collective-permute-start(f32[3,128]{1,0:T(4,128)S(1)} %slice.553), channel_id=1, source_target_pairs={{0,7},{1,6},{2,5},{3,4},{4,3},{5,2},{6,1},{7,0},{8,15},{9,14},{10,... | collective-permute-start | bytes 4616 | tf_op jit(solution)/shard_map/ppermute | solution.py:446
  42.3 3.2 %collective-permute-start.38 = (f32[24,128]{1,0:T(8,128)S(1)}, f32[24,128]{1,0:T(8,128)S(1)}, u32[]{:S(2)}, u32[]{:S(2)}) collective-permute-start(f32[24,128]{1,0:T(8,128)S(1)} %pad_maximum_fusion.12), channel_id=1, source_target_pairs={{0,6},{1,7},{2,4},{3,5},{4,2},{5,3},{6,0},{7,1},{8,14},{9,15},{10,... | collective-permute-start | bytes 36872 | tf_op jit(solution)/shard_map/ppermute | solution.py:446
  42.6 3.4 %collective-permute-start.39 = (f32[67,128]{1,0:T(8,128)S(1)}, f32[67,128]{1,0:T(8,128)S(1)}, u32[]{:S(2)}, u32[]{:S(2)}) collective-permute-start(f32[67,128]{1,0:T(8,128)S(1)} %pad_maximum_fusion.9), channel_id=1, source_target_pairs={{0,3},{1,2},{2,1},{3,0},{4,7},{5,6},{6,5},{7,4},{8,11},{9,10},{10,... | collective-permute-start | bytes 102920 | tf_op jit(solution)/shard_map/ppermute | solution.py:446
  46.1 5.0 %collective-permute-start.43 = (f32[24,128]{1,0:T(8,128)S(1)}, f32[24,128]{1,0:T(8,128)S(1)}, u32[]{:S(2)}, u32[]{:S(2)}) collective-permute-start(f32[24,128]{1,0:T(8,128)S(1)} %maximum_add_fusion.5.refs_8_), channel_id=1, source_target_pairs={{0,26},{1,27},{2,24},{3,25},{4,30},{5,31},{6,28},{7,29},{8,18},{9,... | collective-permute-start | bytes 36872 | tf_op jit(solution)/shard_map/ppermute | solution.py:446
  48.2 4.0 %collective-permute-start.42 = (f32[24,128]{1,0:T(8,128)S(1)}, f32[24,128]{1,0:T(8,128)S(1)}, u32[]{:S(2)}, u32[]{:S(2)}) collective-permute-start(f32[24,128]{1,0:T(8,128)S(1)} %maximum_add_fusion.5.refs_8_), channel_id=1, source_target_pairs={{0,18},{1,19},{2,16},{3,17},{4,22},{5,23},{6,20},{7,21},{8,26},{9,... | collective-permute-start | bytes 36872 | tf_op jit(solution)/shard_map/ppermute | solution.py:446
  48.8 3.4 %collective-permute-start.41 = (f32[24,128]{1,0:T(8,128)S(1)}, f32[24,128]{1,0:T(8,128)S(1)}, u32[]{:S(2)}, u32[]{:S(2)}) collective-permute-start(f32[24,128]{1,0:T(8,128)S(1)} %maximum_add_fusion.5.refs_8_), channel_id=1, source_target_pairs={{0,10},{1,11},{2,8},{3,9},{4,14},{5,15},{6,12},{7,13},{8,2},{9,3},... | collective-permute-start | bytes 36872 | tf_op jit(solution)/shard_map/ppermute | solution.py:446
  52.2 1.3 %copy-start.9 = (f32[64,16,128]{2,1,0:T(8,128)S(1)}, f32[64,16,128]{2,1,0:T(8,128)}, u32[]{:S(2)}) copy-start(f32[64,16,128]{2,1,0:T(8,128)} %param.20) | copy-start | bytes 1572868
  52.2 1.4 %copy-start.10 = (f32[64,128]{1,0:T(8,128)S(1)}, f32[64,128]{1,0:T(8,128)}, u32[]{:S(2)}) copy-start(f32[64,128]{1,0:T(8,128)} %refs_0_.1) | copy-start | bytes 98308
  52.2 1.4 %copy-start.11 = (f32[64,128]{1,0:T(8,128)S(1)}, f32[64,128]{1,0:T(8,128)}, u32[]{:S(2)}) copy-start(f32[64,128]{1,0:T(8,128)} %refs_4_.1) | copy-start | bytes 98308
  53.6 0.5 copy-start.17
  53.6 0.6 %copy-start.15 = (f32[64,256]{1,0:T(8,128)}, f32[64,256]{1,0:T(8,128)S(1)}, u32[]{:S(2)}) copy-start(f32[64,256]{1,0:T(8,128)S(1)} %get-tuple-element.157) | copy-start | bytes 196612
  53.6 0.6 %copy-start.16 = (f32[64,128]{1,0:T(8,128)}, f32[64,128]{1,0:T(8,128)S(1)}, u32[]{:S(2)}) copy-start(f32[64,128]{1,0:T(8,128)S(1)} %get-tuple-element.156) | copy-start | bytes 98308

commit v17 on v15

--- a/solution.py
+++ b/solution.py
@@ -199,8 +199,7 @@
     sums_in_ref,
     maps_ref,
     flows_ref,
-    prices_ref,
-    sums_ref,
+    block_ref,
 ):
     rows, techs, nodes = sizes.rows, sizes.techs, sizes.nodes
     slots, regions = sizes.slots, sizes.regions
@@ -227,16 +226,17 @@
     maps_own = maps_ref[pl.ds(pl.multiple_of(own * nodes, nodes), nodes), :]
     balance = balance_ref[...] + dot3(2.0 * flows, maps_own, True)
     step_up = (1.0 / (techs + 8.0)) * balance
-    prices_ref[...] = gathered[own, :rows, :] + step_up
+    block_ref[:rows, :] = gathered[own, :rows, :] + step_up
     change = row_sum(flows * flows)
     slot = lax.broadcasted_iota(jnp.int32, change.shape, 1)
     primal = fold_lanes(jnp.where(slot // slots == own, change, 0.0))
     more = jnp.concatenate(
         [primal, row_sum(step_up * step_up), jnp.zeros((SQUARES - 2, LANES), jnp.float32)], axis=0
     )
-    sums_ref[...] = sums_in_ref[...]
-    squares = sums_in_ref[techs : techs + SQUARES, :] + more
-    sums_ref[techs : techs + SQUARES, :] = squares
+    block_ref[rows:, :] = sums_in_ref[...]
+    block_ref[rows + techs : rows + techs + SQUARES, :] = (
+        sums_in_ref[techs : techs + SQUARES, :] + more
+    )
 
 
 def neighbour_rows(sizes, given, hour_index):
@@ -272,6 +272,8 @@
     last = iteration == ITERS - 1
     given = Bag(**dict(zip(names_in, refs[: len(names_in)])))
     gives = Bag(**dict(zip(names_out, refs[len(names_in) :])))
+    if last:
+        staged, sem = refs[-2:]
     own = lax.axis_index("region")
     hour_index = lax.axis_index("hours")
     gathered = given.gathered
@@ -279,6 +281,7 @@
     at = places(sizes)
     fixed = given.available.at[techs + 1]
     small = given.dispatch.at[techs]
+    out_sums = None if last else gives.block.at[pl.ds(rows, sums_rows(sizes))]
     sums = total_of(given)
     squares = jnp.sum(sums[techs : techs + 2], axis=1, keepdims=True)
     old_weight = jnp.ones((1, 1), jnp.float32) if second else small[at.weight : at.weight + 1, :1]
@@ -302,6 +305,36 @@
 
     prices_all = jnp.concatenate([gathered[region, :rows, :] for region in range(regions)], axis=1)
     prices = gathered[own, :rows, :]
+    gen_cost = fixed[:techs, :]
+    half_weight = weight / 2.0
+    primal_acc = jnp.zeros((rows, nodes), jnp.float32)
+    dual_acc = jnp.zeros((rows, nodes), jnp.float32)
+    supply = jnp.zeros((rows, nodes), jnp.float32)
+    for tech in range(techs):
+        slope = gen_cost[tech : tech + 1] + prices
+        dispatch = given.dispatch[tech]
+        avail = given.available[tech]
+        if second:
+            duals = jnp.maximum(0.5 * (2.0 * dispatch - avail * first_bar[tech : tech + 1]), 0.0)
+        else:
+            duals = given.cap_duals[tech]
+        dispatch_new = jnp.maximum(dispatch - primal_step * (slope + duals), 0.0)
+        dispatch_bar = 2.0 * dispatch_new - dispatch
+        supply = supply + dispatch_bar
+        if last:
+            staged[pl.ds(tech, rows, stride=techs), :] = dispatch_new
+            continue
+        gives.dispatch[tech] = dispatch_new
+        cap_rows = dispatch_bar - avail * capacity_bar[tech : tech + 1]
+        primal_acc = primal_acc + (dispatch_new - dispatch) ** 2
+        duals_new = jnp.maximum(duals + half_weight * cap_rows, 0.0)
+        dual_acc = dual_acc + (duals_new - duals) ** 2
+        gives.cap_duals[tech] = duals_new
+        out_sums[tech : tech + 1, :] = row_sum(avail * duals_new)
+    if last:
+        copy = pltpu.make_async_copy(staged, gives.dispatch, sem)
+        copy.start()
+
     maps_local = given.maps_local[...]
     slope_local = dot3(prices, maps_local, False)
     slope_cross = dot3(prices_all, given.maps_cross[...], False)
@@ -342,33 +375,7 @@
             primal_row = primal_row + fold_lanes(change)
     maps_own = given.maps_cross[pl.ds(pl.multiple_of(own * nodes, nodes), nodes), :]
     balance = dot3(jnp.concatenate(bars[:2], axis=1), maps_local, True) - given.available[techs]
-    balance = balance + dot3(bars[2], maps_own, True)
-
-    gen_cost = fixed[:techs, :]
-    half_weight = weight / 2.0
-    primal_acc = jnp.zeros((rows, nodes), jnp.float32)
-    dual_acc = jnp.zeros((rows, nodes), jnp.float32)
-    for tech in range(techs):
-        slope = gen_cost[tech : tech + 1] + prices
-        dispatch = given.dispatch[tech]
-        avail = given.available[tech]
-        if second:
-            duals = jnp.maximum(0.5 * (2.0 * dispatch - avail * first_bar[tech : tech + 1]), 0.0)
-        else:
-            duals = given.cap_duals[tech]
-        dispatch_new = jnp.maximum(dispatch - primal_step * (slope + duals), 0.0)
-        dispatch_bar = 2.0 * dispatch_new - dispatch
-        balance = balance + dispatch_bar
-        if last:
-            gives.dispatch[pl.ds(tech, rows, stride=techs), :] = dispatch_new
-            continue
-        gives.dispatch[tech] = dispatch_new
-        cap_rows = dispatch_bar - avail * capacity_bar[tech : tech + 1]
-        primal_acc = primal_acc + (dispatch_new - dispatch) ** 2
-        duals_new = jnp.maximum(duals + half_weight * cap_rows, 0.0)
-        dual_acc = dual_acc + (duals_new - duals) ** 2
-        gives.cap_duals[tech] = duals_new
-        gives.sums[tech : tech + 1, :] = row_sum(avail * duals_new)
+    balance = balance + supply + dot3(bars[2], maps_own, True)
 
     step_up = weight / (techs + 8.0) * balance
     if last:
@@ -385,8 +392,9 @@
             low = local + chunk * LANES
             first = rows + 2 * techs + 8 * chunk
             gives.kept[first : first + 8, :] = given.flows[rows:, low : low + LANES]
+        copy.wait()
         return
-    gives.prices[...] = prices + step_up
+    gives.block[:rows, :] = prices + step_up
     gives.flows[rows:, local:] = given.flows[rows:, local:]
     gives.cap_duals[techs, :techs, :] = col_weight
     gives.cap_duals[techs, techs : 2 * techs, :] = cost
@@ -410,11 +418,11 @@
     squares = jnp.concatenate(
         [primal_row, dual_row, jnp.zeros((SQUARES - 2, LANES), jnp.float32)], axis=0
     )
-    gives.sums[techs : techs + SQUARES, :] = squares
-    write_halo(sizes, gives.sums, store_new)
-
-
-def call(kernel, given, outs, flops=0, left=(), scratch=(), limit=VMEM_BYTES):
+    out_sums[techs : techs + SQUARES, :] = squares
+    write_halo(sizes, out_sums, store_new)
+
+
+def call(kernel, given, outs, flops=0, left=(), scratch=(), limit=VMEM_BYTES, copied=0):
     names_in, names_out = tuple(vars(given)), tuple(vars(outs))
     values = pl.pallas_call(
         functools.partial(kernel, names_in, names_out),
@@ -423,7 +431,10 @@
             pl.BlockSpec(memory_space=pl.ANY if i in left else pltpu.VMEM)
             for i in range(len(names_in))
         ],
-        out_specs=[pl.BlockSpec(memory_space=pltpu.VMEM)] * len(names_out),
+        out_specs=[
+            pl.BlockSpec(memory_space=pl.ANY if i < copied else pltpu.VMEM)
+            for i in range(len(names_out))
+        ],
         scratch_shapes=scratch,
         cost_estimate=pl.CostEstimate(flops=flops, bytes_accessed=4 * flops, transcendentals=0),
         compiler_params=pltpu.CompilerParams(vmem_limit_bytes=limit),
@@ -458,10 +469,11 @@
     )
 
 
-def exchange(sizes, prices, sums):
+def exchange(sizes, block):
     hours, regions = lax.axis_size("hours"), lax.axis_size("region")
     techs, span = sizes.techs, sizes.units // LANES
     halo = halo_at(sizes)
+    prices, sums = block[: sizes.rows], block[sizes.rows :]
     if regions != 2 or hours != 16:
         gathered = lax.all_gather(prices, "region")
         totals = lax.psum(sums, "hours")
@@ -480,11 +492,12 @@
         return jnp.concatenate([total[:halo], *edges, total[last + span :]], axis=0)
 
     hour = lax.axis_index("hours")
-    partner = swap(sums, 1, 0)
+    beside_core = swap(block, 1, 0)
+    partner_prices, partner = beside_core[: sizes.rows], beside_core[sizes.rows :]
     chip = merged(sums, partner, hour % 2 == 0)
     across = swap(chip, 2 + 1, 0)
     diagonal = swap(chip[techs:halo], 2 + 1, 1)
-    beside = swap(jnp.concatenate([prices, chip[techs:halo]], axis=0), 0, 1)
+    beside = swap(jnp.concatenate([partner_prices, chip[techs:halo]], axis=0), 1, 1)
     other, squares = beside[: sizes.rows], beside[sizes.rows :]
     slab = merged(chip, across, hour // 2 % 2 == 0)
     slab = slab + jnp.pad(squares + diagonal, ((techs, slab.shape[0] - halo), (0, 0)))
@@ -556,7 +569,8 @@
     used = halo_at(sizes) + 2 * sizes.units // LANES
     rows_of.append(jnp.zeros((sums_rows(sizes) - used, nodes)))
     rows_of += [jnp.where(first_hour, part, 0.0) for part in (col_weight, cost)]
-    gathered, parts = exchange(sizes, price_start + step_up, jnp.concatenate(rows_of, axis=0))
+    block = jnp.concatenate([price_start + step_up, *rows_of], axis=0)
+    gathered, parts = exchange(sizes, block)
     flows = jnp.concatenate([flows_local, flows_cross], axis=1)
     spare = jnp.concatenate([jnp.zeros((8, local)), info], axis=1)
     state = Bag(
@@ -639,13 +653,12 @@
         Bag(
             maps=shape(regions * nodes, cross, dtype=jnp.bfloat16),
             flows=shape(rows + 8, lines + units + cross),
-            prices=shape(rows, nodes),
-            sums=shape(*state.sums.shape),
+            block=shape(rows + state.sums.shape[0], nodes),
         ),
     )
     del state.sums, state.balance, state.flows_local
     state.maps_cross, state.flows = closed.maps, closed.flows
-    gathered, parts = exchange(sizes, closed.prices, closed.sums)
+    gathered, parts = exchange(sizes, closed.block)
     outputs, negative, kept = sweeps(sizes, owned, state, gathered, parts)
 
     def again():
@@ -672,8 +685,7 @@
                 flows=shape(rows + 8, lines + units + sizes.regions * sizes.slots),
                 store_duals=shape(rows, units),
                 charge=shape(rows, units),
-                prices=shape(rows, nodes),
-                sums=shape(sums_rows(sizes), nodes),
+                block=shape(rows + sums_rows(sizes), nodes),
             )
         else:
             outs = Bag(
@@ -684,10 +696,19 @@
                 negative=shape(1, LANES),
                 kept=shape(rows + 2 * techs + 8 * (sizes.regions * sizes.slots // LANES), LANES),
             )
-        results = call(functools.partial(sweep_kernel, sizes, iteration), given, outs)
+        final = iteration == ITERS - 1
+        results = call(
+            functools.partial(sweep_kernel, sizes, iteration),
+            given,
+            outs,
+            copied=int(final),
+            scratch=[pltpu.VMEM(outs.dispatch.shape, jnp.float32), pltpu.SemaphoreType.DMA]
+            if final
+            else [],
+        )
         if iteration < ITERS - 1:
-            gathered, parts = exchange(sizes, results.prices, results.sums)
-            del results.prices, results.sums
+            gathered, parts = exchange(sizes, results.block)
+            del results.block
             vars(state).update(vars(results))
     dispatch = results.dispatch.reshape(rows, techs, nodes)
     outputs = (dispatch, results.capacity, results.prices, results.charge)

time: 54.6 us -> 53.6 us (0.982)
  waiting for transfers between devices: 20 us -> 18 us
  starting transfers between devices: 25.4 us -> 26.2 us
    ppermute x22, waiting for transfers between devices: 20 us -> 18 us  [swap(): return lax.ppermute(value, ('hours', 'region'), pairs)]
    ppermute x22, starting transfers between devices: 25.4 us -> 26.2 us  [swap(): return lax.ppermute(value, ('hours', 'region'), pairs)]
where the time goes in v17:
time: 53.6 us; the launch traced here: 53.3 us
  starting transfers between devices  26.2 us (49%)
  waiting for transfers between devices  18 us (34%)
  Pallas kernels  6.43 us (12%)
  local copies, waits for them, and re-layouts  1.46 us (3%)
  between operations  1.02 us (2%)
    ppermute x22, starting transfers between devices, swap(): return lax.ppermute(value, ('hours', 'region'), pairs)  26.2 us
    ppermute x22, waiting for transfers between devices, swap(): return lax.ppermute(value, ('hours', 'region'), pairs)  18 us
    pallas_call x6, Pallas kernels, call(): pl.pallas_call(functools.partial(kernel, names_in, names_out), out_shape=...  6.43 us
    unnamed x30, local copies, waits for them, and re-layouts  1.38 us
  transfers between devices with their start and end apart: 22, of which 15 were waited for; matrix products, arithmetic and copies ran while one was open for 0% of the time, Pallas kernels for 3%

profile of v17, /device:TPU:0, one launch (start us, length us, event | category | flops | bytes accessed | tf_op | source)
XLA Modules:
  0.0 53.3 jit_solution(1198528103105204958)
XLA Ops:
  0.6 1.4 %shard_map.166 = f32[72,128]{1,0:T(8,128)} custom-call(f32[64,128]{1,0:T(8,128)} %refs_0_.1, s32[2,64]{1,0:T(2,128)} %bitcast.120, f32[1,64]{1,0:T(1,128)} %refs_2_.3, s32[1,2]{1,0:T(1,128)} %refs_3_.3), custom_call_target="tpu_custom_call" | custom-call | tf_op jit(solution)/shard_map/pallas_call | solution.py:427
  2.1 3.0 %collective-permute-start.22 = (f32[72,128]{1,0:T(8,128)}, f32[72,128]{1,0:T(8,128)S(1)}, u32[]{:S(2)}, u32[]{:S(2)}) collective-permute-start(f32[72,128]{1,0:T(8,128)} %shard_map.166), channel_id=1, source_target_pairs={{0,1},{1,0},{2,3},{3,2},{4,5},{5,4},{6,7},{7,6},{8,9},{9,8},{10,11... | collective-permute-start | bytes 110600 | tf_op jit(solution)/shard_map/ppermute | solution.py:452
  5.1 0.0 copy-start.3
  5.1 0.0 copy-start.4
  5.2 0.0 copy-start.1
  5.2 0.0 copy-start
  5.2 0.0 copy-start.2
  5.2 0.6 %copy-done.10 = s32[2,256]{1,0:T(2,128)S(1)} copy-done((s32[2,256]{1,0:T(2,128)S(1)}, s32[2,256]{1,0:T(2,128)}, u32[]{:S(2)}) %copy-start.10) | copy-done | bytes 2072
  5.8 0.1 copy-done.8
  5.9 0.0 copy-done.7
  5.9 0.0 copy-done
  5.9 1.7 %shard_map.165 = (f32[18,64,128]{2,1,0:T(8,128)S(1)}, bf16[128,512]{1,0:T(8,128)(2,1)S(1)}, f32[64,512]{1,0:T(8,128)S(1)}, f32[64,256]{1,0:T(8,128)S(1)}, f32[17...) custom-call(f32[1024,128]{1,0:T(8,128)} %bitcast.86, f32[64,128]{1,0:T(8,128)S(1)} %copy-done.7, ...), custom_call_target="tpu_custom_call" | custom-call | flops 1000000 | bytes 4000000 | tf_op jit(solution)/shard_map/pallas_call | solution.py:427
  7.7 0.0 collective-permute-done.22
  7.7 0.4 shard_map.167
  8.2 0.1 collective-permute-start.23
  8.3 1.2 %collective-permute-done.23 = f32[120,128]{1,0:T(8,128)S(1)} collective-permute-done((f32[120,128]{1,0:T(8,128)S(1)}, f32[120,128]{1,0:T(8,128)S(1)}, u32[]{:S(2)}, u32[]{:S(2)}) %collective-permute-start.23) | collective-permute-done | bytes 61472 | tf_op jit(solution)/shard_map/ppermute | solution.py:452
  9.5 2.3 %collective-permute-start.26 = (f32[3,128]{1,0:T(4,128)S(1)}, f32[3,128]{1,0:T(4,128)S(1)}, u32[]{:S(2)}, u32[]{:S(2)}) collective-permute-start(f32[3,128]{1,0:T(4,128)S(1)} %slice.523), channel_id=1, source_target_pairs={{0,7},{1,6},{2,5},{3,4},{4,3},{5,2},{6,1},{7,0},{8,15},{9,14},{10,... | collective-permute-start | bytes 4616 | tf_op jit(solution)/shard_map/ppermute | solution.py:452
  11.9 0.6 %collective-permute-start.24 = (f32[56,128]{1,0:T(8,128)S(1)}, f32[56,128]{1,0:T(8,128)S(1)}, u32[]{:S(2)}, u32[]{:S(2)}) collective-permute-start(f32[56,128]{1,0:T(8,128)S(1)} %pad_maximum_fusion.10), channel_id=1, source_target_pairs={{0,6},{1,7},{2,4},{3,5},{4,2},{5,3},{6,0},{7,1},{8,14},{9,15},{10,... | collective-permute-start | bytes 86024 | tf_op jit(solution)/shard_map/ppermute | solution.py:452
  12.4 0.3 collective-permute-start.25
  12.7 2.5 %collective-permute-done.24.refs_11_ = f32[56,128]{1,0:T(8,128)S(1)} collective-permute-done((f32[56,128]{1,0:T(8,128)S(1)}, f32[56,128]{1,0:T(8,128)S(1)}, u32[]{:S(2)}, u32[]{:S(2)}) %collective-permute-start.24) | collective-permute-done | bytes 28704 | tf_op jit(solution)/shard_map/ppermute | solution.py:452
  15.3 0.0 collective-permute-done.26
  15.3 0.6 %collective-permute-done.25 = f32[67,128]{1,0:T(8,128)S(1)} collective-permute-done((f32[67,128]{1,0:T(8,128)S(1)}, f32[67,128]{1,0:T(8,128)S(1)}, u32[]{:S(2)}, u32[]{:S(2)}) %collective-permute-start.25) | collective-permute-done | bytes 34336 | tf_op jit(solution)/shard_map/ppermute | solution.py:452
  16.0 3.4 %collective-permute-start.29 = (f32[56,128]{1,0:T(8,128)S(1)}, f32[56,128]{1,0:T(8,128)S(1)}, u32[]{:S(2)}, u32[]{:S(2)}) collective-permute-start(f32[56,128]{1,0:T(8,128)S(1)} %maximum_add_fusion.3.refs_6_), channel_id=1, source_target_pairs={{0,26},{1,27},{2,24},{3,25},{4,30},{5,31},{6,28},{7,29},{8,18},{9,... | collective-permute-start | bytes 86024 | tf_op jit(solution)/shard_map/ppermute | solution.py:452
  19.4 0.0 collective-permute-start.28
  19.4 0.6 %collective-permute-start.27 = (f32[56,128]{1,0:T(8,128)S(1)}, f32[56,128]{1,0:T(8,128)S(1)}, u32[]{:S(2)}, u32[]{:S(2)}) collective-permute-start(f32[56,128]{1,0:T(8,128)S(1)} %maximum_add_fusion.3.refs_6_), channel_id=1, source_target_pairs={{0,10},{1,11},{2,8},{3,9},{4,14},{5,15},{6,12},{7,13},{8,2},{9,3},... | collective-permute-start | bytes 86024 | tf_op jit(solution)/shard_map/ppermute | solution.py:452
  20.0 1.1 %collective-permute-done.29.refs_9_ = f32[56,128]{1,0:T(8,128)S(1)} collective-permute-done((f32[56,128]{1,0:T(8,128)S(1)}, f32[56,128]{1,0:T(8,128)S(1)}, u32[]{:S(2)}, u32[]{:S(2)}) %collective-permute-start.29) | collective-permute-done | bytes 28704 | tf_op jit(solution)/shard_map/ppermute | solution.py:452
  21.1 2.5 %collective-permute-done.28.refs_8_ = f32[56,128]{1,0:T(8,128)S(1)} collective-permute-done((f32[56,128]{1,0:T(8,128)S(1)}, f32[56,128]{1,0:T(8,128)S(1)}, u32[]{:S(2)}, u32[]{:S(2)}) %collective-permute-start.28) | collective-permute-done | bytes 28704 | tf_op jit(solution)/shard_map/ppermute | solution.py:452
  23.6 0.0 collective-permute-done.27.refs_7_
  23.6 0.8 %shard_map.168 = (f32[17,64,128]{2,1,0:T(8,128)S(1)}, f32[17,64,128]{2,1,0:T(8,128)S(1)}, f32[72,640]{1,0:T(8,128)S(1)}, f32[64,256]{1,0:T(8,128)S(1)}, f32[64,256]{1,0:T(8,128)S(1)}, /*index=5*/f32[88,128]{1,0:T(8,128)S(1)}) custom-call(f32[18,64,128]{2,1,0:T(8,128)S(1)} %get-tuple-element.107.refs_0_, bf16[128,512]{1,0:T(8,128)(2,1)S(1)} %get-tuple-element.108.refs_1_, ...), custom_call_target="tpu_custom_call" | custom-call | tf_op jit(solution)/shard_map/pallas_call | solution.py:427
  24.4 0.4 collective-permute-start.30
  24.8 0.9 %collective-permute-done.30 = f32[88,128]{1,0:T(8,128)S(1)} collective-permute-done((f32[88,128]{1,0:T(8,128)S(1)}, f32[88,128]{1,0:T(8,128)S(1)}, u32[]{:S(2)}, u32[]{:S(2)}) %collective-permute-start.30) | collective-permute-done | bytes 45088 | tf_op jit(solution)/shard_map/ppermute | solution.py:452
  25.7 1.4 %collective-permute-start.33 = (f32[3,128]{1,0:T(4,128)S(1)}, f32[3,128]{1,0:T(4,128)S(1)}, u32[]{:S(2)}, u32[]{:S(2)}) collective-permute-start(f32[3,128]{1,0:T(4,128)S(1)} %slice.536), channel_id=1, source_target_pairs={{0,7},{1,6},{2,5},{3,4},{4,3},{5,2},{6,1},{7,0},{8,15},{9,14},{10,... | collective-permute-start | bytes 4616 | tf_op jit(solution)/shard_map/ppermute | solution.py:452
  27.2 0.4 collective-permute-start.31
  27.6 1.5 %collective-permute-start.32 = (f32[67,128]{1,0:T(8,128)S(1)}, f32[67,128]{1,0:T(8,128)S(1)}, u32[]{:S(2)}, u32[]{:S(2)}) collective-permute-start(f32[67,128]{1,0:T(8,128)S(1)} %pad_maximum_fusion.8), channel_id=1, source_target_pairs={{0,3},{1,2},{2,1},{3,0},{4,7},{5,6},{6,5},{7,4},{8,11},{9,10},{10,... | collective-permute-start | bytes 102920 | tf_op jit(solution)/shard_map/ppermute | solution.py:452
  29.1 1.3 %collective-permute-done.31.refs_13_ = f32[24,128]{1,0:T(8,128)S(1)} collective-permute-done((f32[24,128]{1,0:T(8,128)S(1)}, f32[24,128]{1,0:T(8,128)S(1)}, u32[]{:S(2)}, u32[]{:S(2)}) %collective-permute-start.31) | collective-permute-done | bytes 12320 | tf_op jit(solution)/shard_map/ppermute | solution.py:452
  30.4 0.0 collective-permute-done.33
  30.4 0.6 %collective-permute-done.32 = f32[67,128]{1,0:T(8,128)S(1)} collective-permute-done((f32[67,128]{1,0:T(8,128)S(1)}, f32[67,128]{1,0:T(8,128)S(1)}, u32[]{:S(2)}, u32[]{:S(2)}) %collective-permute-start.32) | collective-permute-done | bytes 34336 | tf_op jit(solution)/shard_map/ppermute | solution.py:452
  31.0 1.7 %collective-permute-start.36 = (f32[24,128]{1,0:T(8,128)S(1)}, f32[24,128]{1,0:T(8,128)S(1)}, u32[]{:S(2)}, u32[]{:S(2)}) collective-permute-start(f32[24,128]{1,0:T(8,128)S(1)} %maximum_add_fusion.4.refs_8_), channel_id=1, source_target_pairs={{0,26},{1,27},{2,24},{3,25},{4,30},{5,31},{6,28},{7,29},{8,18},{9,... | collective-permute-start | bytes 36872 | tf_op jit(solution)/shard_map/ppermute | solution.py:452
  32.7 0.2 collective-permute-start.35
  33.0 2.2 %collective-permute-start.34 = (f32[24,128]{1,0:T(8,128)S(1)}, f32[24,128]{1,0:T(8,128)S(1)}, u32[]{:S(2)}, u32[]{:S(2)}) collective-permute-start(f32[24,128]{1,0:T(8,128)S(1)} %maximum_add_fusion.4.refs_8_), channel_id=1, source_target_pairs={{0,10},{1,11},{2,8},{3,9},{4,14},{5,15},{6,12},{7,13},{8,2},{9,3},... | collective-permute-start | bytes 36872 | tf_op jit(solution)/shard_map/ppermute | solution.py:452
  35.2 0.8 %collective-permute-done.36.refs_11_ = f32[24,128]{1,0:T(8,128)S(1)} collective-permute-done((f32[24,128]{1,0:T(8,128)S(1)}, f32[24,128]{1,0:T(8,128)S(1)}, u32[]{:S(2)}, u32[]{:S(2)}) %collective-permute-start.36) | collective-permute-done | bytes 12320 | tf_op jit(solution)/shard_map/ppermute | solution.py:452
  36.0 0.8 %collective-permute-done.35.refs_10_ = f32[24,128]{1,0:T(8,128)S(1)} collective-permute-done((f32[24,128]{1,0:T(8,128)S(1)}, f32[24,128]{1,0:T(8,128)S(1)}, u32[]{:S(2)}, u32[]{:S(2)}) %collective-permute-start.35) | collective-permute-done | bytes 12320 | tf_op jit(solution)/shard_map/ppermute | solution.py:452
  36.8 0.0 collective-permute-done.34.refs_9_
  36.8 0.7 %shard_map.169 = (f32[17,64,128]{2,1,0:T(8,128)S(1)}, f32[17,64,128]{2,1,0:T(8,128)S(1)}, f32[72,640]{1,0:T(8,128)S(1)}, f32[64,256]{1,0:T(8,128)S(1)}, f32[64,256]{1,0:T(8,128)S(1)}, /*index=5*/f32[88,128]{1,0:T(8,128)S(1)}) custom-call(f32[18,64,128]{2,1,0:T(8,128)S(1)} %get-tuple-element.107.refs_0_, bf16[128,512]{1,0:T(8,128)(2,1)S(1)} %get-tuple-element.108.refs_1_, ...), custom_call_target="tpu_custom_call" | custom-call | tf_op jit(solution)/shard_map/pallas_call | solution.py:427
  37.5 0.5 collective-permute-start.37
  38.0 0.9 %collective-permute-done.37 = f32[88,128]{1,0:T(8,128)S(1)} collective-permute-done((f32[88,128]{1,0:T(8,128)S(1)}, f32[88,128]{1,0:T(8,128)S(1)}, u32[]{:S(2)}, u32[]{:S(2)}) %collective-permute-start.37) | collective-permute-done | bytes 45088 | tf_op jit(solution)/shard_map/ppermute | solution.py:452
  38.9 2.5 %collective-permute-start.40 = (f32[3,128]{1,0:T(4,128)S(1)}, f32[3,128]{1,0:T(4,128)S(1)}, u32[]{:S(2)}, u32[]{:S(2)}) collective-permute-start(f32[3,128]{1,0:T(4,128)S(1)} %slice.549), channel_id=1, source_target_pairs={{0,7},{1,6},{2,5},{3,4},{4,3},{5,2},{6,1},{7,0},{8,15},{9,14},{10,... | collective-permute-start | bytes 4616 | tf_op jit(solution)/shard_map/ppermute | solution.py:452
  41.4 0.4 collective-permute-start.38
  41.8 0.5 collective-permute-start.39
  42.3 2.3 %collective-permute-done.38.refs_13_ = f32[24,128]{1,0:T(8,128)S(1)} collective-permute-done((f32[24,128]{1,0:T(8,128)S(1)}, f32[24,128]{1,0:T(8,128)S(1)}, u32[]{:S(2)}, u32[]{:S(2)}) %collective-permute-start.38) | collective-permute-done | bytes 12320 | tf_op jit(solution)/shard_map/ppermute | solution.py:452
  44.6 0.0 collective-permute-done.40
  44.6 0.6 %collective-permute-done.39 = f32[67,128]{1,0:T(8,128)S(1)} collective-permute-done((f32[67,128]{1,0:T(8,128)S(1)}, f32[67,128]{1,0:T(8,128)S(1)}, u32[]{:S(2)}, u32[]{:S(2)}) %collective-permute-start.39) | collective-permute-done | bytes 34336 | tf_op jit(solution)/shard_map/ppermute | solution.py:452
  45.2 2.1 %collective-permute-start.43 = (f32[24,128]{1,0:T(8,128)S(1)}, f32[24,128]{1,0:T(8,128)S(1)}, u32[]{:S(2)}, u32[]{:S(2)}) collective-permute-start(f32[24,128]{1,0:T(8,128)S(1)} %maximum_add_fusion.5.refs_8_), channel_id=1, source_target_pairs={{0,26},{1,27},{2,24},{3,25},{4,30},{5,31},{6,28},{7,29},{8,18},{9,... | collective-permute-start | bytes 36872 | tf_op jit(solution)/shard_map/ppermute | solution.py:452
  47.3 0.6 %collective-permute-start.42 = (f32[24,128]{1,0:T(8,128)S(1)}, f32[24,128]{1,0:T(8,128)S(1)}, u32[]{:S(2)}, u32[]{:S(2)}) collective-permute-start(f32[24,128]{1,0:T(8,128)S(1)} %maximum_add_fusion.5.refs_8_), channel_id=1, source_target_pairs={{0,18},{1,19},{2,16},{3,17},{4,22},{5,23},{6,20},{7,21},{8,26},{9,... | collective-permute-start | bytes 36872 | tf_op jit(solution)/shard_map/ppermute | solution.py:452
  47.9 1.4 %collective-permute-start.41 = (f32[24,128]{1,0:T(8,128)S(1)}, f32[24,128]{1,0:T(8,128)S(1)}, u32[]{:S(2)}, u32[]{:S(2)}) collective-permute-start(f32[24,128]{1,0:T(8,128)S(1)} %maximum_add_fusion.5.refs_8_), channel_id=1, source_target_pairs={{0,10},{1,11},{2,8},{3,9},{4,14},{5,15},{6,12},{7,13},{8,2},{9,3},... | collective-permute-start | bytes 36872 | tf_op jit(solution)/shard_map/ppermute | solution.py:452
  49.4 0.8 %collective-permute-done.43.refs_11_ = f32[24,128]{1,0:T(8,128)S(1)} collective-permute-done((f32[24,128]{1,0:T(8,128)S(1)}, f32[24,128]{1,0:T(8,128)S(1)}, u32[]{:S(2)}, u32[]{:S(2)}) %collective-permute-start.43) | collective-permute-done | bytes 12320 | tf_op jit(solution)/shard_map/ppermute | solution.py:452
  50.2 1.1 %collective-permute-done.42.refs_10_ = f32[24,128]{1,0:T(8,128)S(1)} collective-permute-done((f32[24,128]{1,0:T(8,128)S(1)}, f32[24,128]{1,0:T(8,128)S(1)}, u32[]{:S(2)}, u32[]{:S(2)}) %collective-permute-start.42) | collective-permute-done | bytes 12320 | tf_op jit(solution)/shard_map/ppermute | solution.py:452
  51.3 1.3 %shard_map.170 = (f32[1024,128]{1,0:T(8,128)}, f32[1,128]{1,0:T(1,128)S(1)}, f32[64,128]{1,0:T(8,128)S(1)}, f32[64,256]{1,0:T(8,128)S(1)}, f32[1,128]{1,0:T(1,128)S(1)}, /*index=5*/f32[104,128]{1,0:T(8,128)S(1)}) custom-call(f32[18,64,128]{2,1,0:T(8,128)S(1)} %get-tuple-element.107.refs_0_, bf16[128,512]{1,0:T(8,128)(2,1)S(1)} %get-tuple-element.108.refs_1_, ...), custom_call_target="tpu_custom_call" | custom-call | tf_op jit(solution)/shard_map/pallas_call | solution.py:427
  52.7 0.0 copy-start.14
  52.7 0.0 copy-start.12
  52.7 0.0 copy-start.13
  52.7 0.5 copy-done.14
  53.2 0.1 copy-done.12
  53.3 0.0 copy-done.13
  (65 shorter events, 0.3 us)
Async XLA Ops:
  0.6 4.6 %copy-start.11 = (s32[256]{0:T(256)S(1)}, s32[256]{0:T(256)}, u32[]{:S(2)}) copy-start(s32[256]{0:T(256)} %param.30) | copy-start | bytes 3076
  2.1 5.6 %collective-permute-start.22 = (f32[72,128]{1,0:T(8,128)}, f32[72,128]{1,0:T(8,128)S(1)}, u32[]{:S(2)}, u32[]{:S(2)}) collective-permute-start(f32[72,128]{1,0:T(8,128)} %shard_map.166), channel_id=1, source_target_pairs={{0,1},{1,0},{2,3},{3,2},{4,5},{5,4},{6,7},{7,6},{8,9},{9,8},{10,11... | collective-permute-start | bytes 110600 | tf_op jit(solution)/shard_map/ppermute | solution.py:452
  5.1 0.7 %copy-start.10 = (s32[2,256]{1,0:T(2,128)S(1)}, s32[2,256]{1,0:T(2,128)}, u32[]{:S(2)}) copy-start(s32[2,256]{1,0:T(2,128)} %refs_6_.1) | copy-start | bytes 6148
  5.1 0.8 %copy-start.8 = (f32[64,128]{1,0:T(8,128)S(1)}, f32[64,128]{1,0:T(8,128)}, u32[]{:S(2)}) copy-start(f32[64,128]{1,0:T(8,128)} %refs_2_.2) | copy-start | bytes 98308
  5.1 0.8 %copy-start.7 = (f32[64,128]{1,0:T(8,128)S(1)}, f32[64,128]{1,0:T(8,128)}, u32[]{:S(2)}) copy-start(f32[64,128]{1,0:T(8,128)} %refs_0_.1) | copy-start | bytes 98308
  5.1 0.8 %copy-start.5 = (f32[1,128]{1,0:T(1,128)S(1)}, f32[1,128]{1,0:T(1,128)}, u32[]{:S(2)}) copy-start(f32[1,128]{1,0:T(1,128)} %refs_4_.1) | copy-start | bytes 1540
  5.1 0.8 %copy-start.3 = (f32[256]{0:T(256)S(1)}, f32[256]{0:T(256)}, u32[]{:S(2)}) copy-start(f32[256]{0:T(256)} %param.32) | copy-start | bytes 3076
  5.1 0.8 %copy-start.4 = (f32[256]{0:T(256)S(1)}, f32[256]{0:T(256)}, u32[]{:S(2)}) copy-start(f32[256]{0:T(256)} %param.31) | copy-start | bytes 3076
  5.2 0.8 %copy-start.1 = (s32[1,2048]{1,0:T(1,128)S(1)}, s32[1,2048]{1,0:T(1,128)}, u32[]{:S(2)}) copy-start(s32[1,2048]{1,0:T(1,128)} %param.24) | copy-start | bytes 24580
  5.2 0.8 %copy-start = (f32[16,128]{1,0:T(8,128)S(1)}, f32[16,128]{1,0:T(8,128)}, u32[]{:S(2)}) copy-start(f32[16,128]{1,0:T(8,128)} %refs_3_.2) | copy-start | bytes 24580
  5.2 0.7 %copy-start.2 = (f32[256]{0:T(256)S(1)}, f32[256]{0:T(256)}, u32[]{:S(2)}) copy-start(f32[256]{0:T(256)} %param.26) | copy-start | bytes 3076
  5.9 1.8 %copy-start.9 = (f32[72,128]{1,0:T(8,128)S(1)}, f32[72,128]{1,0:T(8,128)}, u32[]{:S(2)}) copy-start(f32[72,128]{1,0:T(8,128)} %shard_map.166) | copy-start | bytes 110596
  8.2 1.3 %collective-permute-start.23 = (f32[120,128]{1,0:T(8,128)S(1)}, f32[120,128]{1,0:T(8,128)S(1)}, u32[]{:S(2)}, u32[]{:S(2)}) collective-permute-start(f32[120,128]{1,0:T(8,128)S(1)} %get-tuple-element.116), channel_id=1, source_target_pairs={{0,2},{1,3},{2,0},{3,1},{4,6},{5,7},{6,4},{7,5},{8,10},{9,11},{10,... | collective-permute-start | bytes 184328 | tf_op jit(solution)/shard_map/ppermute | solution.py:452
  9.5 5.8 %collective-permute-start.26 = (f32[3,128]{1,0:T(4,128)S(1)}, f32[3,128]{1,0:T(4,128)S(1)}, u32[]{:S(2)}, u32[]{:S(2)}) collective-permute-start(f32[3,128]{1,0:T(4,128)S(1)} %slice.523), channel_id=1, source_target_pairs={{0,7},{1,6},{2,5},{3,4},{4,3},{5,2},{6,1},{7,0},{8,15},{9,14},{10,... | collective-permute-start | bytes 4616 | tf_op jit(solution)/shard_map/ppermute | solution.py:452
  11.9 3.4 %collective-permute-start.24 = (f32[56,128]{1,0:T(8,128)S(1)}, f32[56,128]{1,0:T(8,128)S(1)}, u32[]{:S(2)}, u32[]{:S(2)}) collective-permute-start(f32[56,128]{1,0:T(8,128)S(1)} %pad_maximum_fusion.10), channel_id=1, source_target_pairs={{0,6},{1,7},{2,4},{3,5},{4,2},{5,3},{6,0},{7,1},{8,14},{9,15},{10,... | collective-permute-start | bytes 86024 | tf_op jit(solution)/shard_map/ppermute | solution.py:452
  12.4 3.5 %collective-permute-start.25 = (f32[67,128]{1,0:T(8,128)S(1)}, f32[67,128]{1,0:T(8,128)S(1)}, u32[]{:S(2)}, u32[]{:S(2)}) collective-permute-start(f32[67,128]{1,0:T(8,128)S(1)} %pad_maximum_fusion.7), channel_id=1, source_target_pairs={{0,3},{1,2},{2,1},{3,0},{4,7},{5,6},{6,5},{7,4},{8,11},{9,10},{10,... | collective-permute-start | bytes 102920 | tf_op jit(solution)/shard_map/ppermute | solution.py:452
  16.0 5.2 %collective-permute-start.29 = (f32[56,128]{1,0:T(8,128)S(1)}, f32[56,128]{1,0:T(8,128)S(1)}, u32[]{:S(2)}, u32[]{:S(2)}) collective-permute-start(f32[56,128]{1,0:T(8,128)S(1)} %maximum_add_fusion.3.refs_6_), channel_id=1, source_target_pairs={{0,26},{1,27},{2,24},{3,25},{4,30},{5,31},{6,28},{7,29},{8,18},{9,... | collective-permute-start | bytes 86024 | tf_op jit(solution)/shard_map/ppermute | solution.py:452
  19.4 4.2 %collective-permute-start.28 = (f32[56,128]{1,0:T(8,128)S(1)}, f32[56,128]{1,0:T(8,128)S(1)}, u32[]{:S(2)}, u32[]{:S(2)}) collective-permute-start(f32[56,128]{1,0:T(8,128)S(1)} %maximum_add_fusion.3.refs_6_), channel_id=1, source_target_pairs={{0,18},{1,19},{2,16},{3,17},{4,22},{5,23},{6,20},{7,21},{8,26},{9,... | collective-permute-start | bytes 86024 | tf_op jit(solution)/shard_map/ppermute | solution.py:452
  19.4 4.2 %collective-permute-start.27 = (f32[56,128]{1,0:T(8,128)S(1)}, f32[56,128]{1,0:T(8,128)S(1)}, u32[]{:S(2)}, u32[]{:S(2)}) collective-permute-start(f32[56,128]{1,0:T(8,128)S(1)} %maximum_add_fusion.3.refs_6_), channel_id=1, source_target_pairs={{0,10},{1,11},{2,8},{3,9},{4,14},{5,15},{6,12},{7,13},{8,2},{9,3},... | collective-permute-start | bytes 86024 | tf_op jit(solution)/shard_map/ppermute | solution.py:452
  24.4 1.3 %collective-permute-start.30 = (f32[88,128]{1,0:T(8,128)S(1)}, f32[88,128]{1,0:T(8,128)S(1)}, u32[]{:S(2)}, u32[]{:S(2)}) collective-permute-start(f32[88,128]{1,0:T(8,128)S(1)} %get-tuple-element.122), channel_id=1, source_target_pairs={{0,2},{1,3},{2,0},{3,1},{4,6},{5,7},{6,4},{7,5},{8,10},{9,11},{10,... | collective-permute-start | bytes 135176 | tf_op jit(solution)/shard_map/ppermute | solution.py:452
  25.7 4.7 %collective-permute-start.33 = (f32[3,128]{1,0:T(4,128)S(1)}, f32[3,128]{1,0:T(4,128)S(1)}, u32[]{:S(2)}, u32[]{:S(2)}) collective-permute-start(f32[3,128]{1,0:T(4,128)S(1)} %slice.536), channel_id=1, source_target_pairs={{0,7},{1,6},{2,5},{3,4},{4,3},{5,2},{6,1},{7,0},{8,15},{9,14},{10,... | collective-permute-start | bytes 4616 | tf_op jit(solution)/shard_map/ppermute | solution.py:452
  27.2 3.2 %collective-permute-start.31 = (f32[24,128]{1,0:T(8,128)S(1)}, f32[24,128]{1,0:T(8,128)S(1)}, u32[]{:S(2)}, u32[]{:S(2)}) collective-permute-start(f32[24,128]{1,0:T(8,128)S(1)} %pad_maximum_fusion.11), channel_id=1, source_target_pairs={{0,6},{1,7},{2,4},{3,5},{4,2},{5,3},{6,0},{7,1},{8,14},{9,15},{10,... | collective-permute-start | bytes 36872 | tf_op jit(solution)/shard_map/ppermute | solution.py:452
  27.6 3.4 %collective-permute-start.32 = (f32[67,128]{1,0:T(8,128)S(1)}, f32[67,128]{1,0:T(8,128)S(1)}, u32[]{:S(2)}, u32[]{:S(2)}) collective-permute-start(f32[67,128]{1,0:T(8,128)S(1)} %pad_maximum_fusion.8), channel_id=1, source_target_pairs={{0,3},{1,2},{2,1},{3,0},{4,7},{5,6},{6,5},{7,4},{8,11},{9,10},{10,... | collective-permute-start | bytes 102920 | tf_op jit(solution)/shard_map/ppermute | solution.py:452
  31.0 5.0 %collective-permute-start.36 = (f32[24,128]{1,0:T(8,128)S(1)}, f32[24,128]{1,0:T(8,128)S(1)}, u32[]{:S(2)}, u32[]{:S(2)}) collective-permute-start(f32[24,128]{1,0:T(8,128)S(1)} %maximum_add_fusion.4.refs_8_), channel_id=1, source_target_pairs={{0,26},{1,27},{2,24},{3,25},{4,30},{5,31},{6,28},{7,29},{8,18},{9,... | collective-permute-start | bytes 36872 | tf_op jit(solution)/shard_map/ppermute | solution.py:452
  32.7 4.0 %collective-permute-start.35 = (f32[24,128]{1,0:T(8,128)S(1)}, f32[24,128]{1,0:T(8,128)S(1)}, u32[]{:S(2)}, u32[]{:S(2)}) collective-permute-start(f32[24,128]{1,0:T(8,128)S(1)} %maximum_add_fusion.4.refs_8_), channel_id=1, source_target_pairs={{0,18},{1,19},{2,16},{3,17},{4,22},{5,23},{6,20},{7,21},{8,26},{9,... | collective-permute-start | bytes 36872 | tf_op jit(solution)/shard_map/ppermute | solution.py:452
  33.0 3.8 %collective-permute-start.34 = (f32[24,128]{1,0:T(8,128)S(1)}, f32[24,128]{1,0:T(8,128)S(1)}, u32[]{:S(2)}, u32[]{:S(2)}) collective-permute-start(f32[24,128]{1,0:T(8,128)S(1)} %maximum_add_fusion.4.refs_8_), channel_id=1, source_target_pairs={{0,10},{1,11},{2,8},{3,9},{4,14},{5,15},{6,12},{7,13},{8,2},{9,3},... | collective-permute-start | bytes 36872 | tf_op jit(solution)/shard_map/ppermute | solution.py:452
  37.5 1.4 %collective-permute-start.37 = (f32[88,128]{1,0:T(8,128)S(1)}, f32[88,128]{1,0:T(8,128)S(1)}, u32[]{:S(2)}, u32[]{:S(2)}) collective-permute-start(f32[88,128]{1,0:T(8,128)S(1)} %get-tuple-element.128), channel_id=1, source_target_pairs={{0,2},{1,3},{2,0},{3,1},{4,6},{5,7},{6,4},{7,5},{8,10},{9,11},{10,... | collective-permute-start | bytes 135176 | tf_op jit(solution)/shard_map/ppermute | solution.py:452
  38.9 5.7 %collective-permute-start.40 = (f32[3,128]{1,0:T(4,128)S(1)}, f32[3,128]{1,0:T(4,128)S(1)}, u32[]{:S(2)}, u32[]{:S(2)}) collective-permute-start(f32[3,128]{1,0:T(4,128)S(1)} %slice.549), channel_id=1, source_target_pairs={{0,7},{1,6},{2,5},{3,4},{4,3},{5,2},{6,1},{7,0},{8,15},{9,14},{10,... | collective-permute-start | bytes 4616 | tf_op jit(solution)/shard_map/ppermute | solution.py:452
  41.4 3.2 %collective-permute-start.38 = (f32[24,128]{1,0:T(8,128)S(1)}, f32[24,128]{1,0:T(8,128)S(1)}, u32[]{:S(2)}, u32[]{:S(2)}) collective-permute-start(f32[24,128]{1,0:T(8,128)S(1)} %pad_maximum_fusion.12), channel_id=1, source_target_pairs={{0,6},{1,7},{2,4},{3,5},{4,2},{5,3},{6,0},{7,1},{8,14},{9,15},{10,... | collective-permute-start | bytes 36872 | tf_op jit(solution)/shard_map/ppermute | solution.py:452
  41.8 3.4 %collective-permute-start.39 = (f32[67,128]{1,0:T(8,128)S(1)}, f32[67,128]{1,0:T(8,128)S(1)}, u32[]{:S(2)}, u32[]{:S(2)}) collective-permute-start(f32[67,128]{1,0:T(8,128)S(1)} %pad_maximum_fusion.9), channel_id=1, source_target_pairs={{0,3},{1,2},{2,1},{3,0},{4,7},{5,6},{6,5},{7,4},{8,11},{9,10},{10,... | collective-permute-start | bytes 102920 | tf_op jit(solution)/shard_map/ppermute | solution.py:452
  45.2 5.0 %collective-permute-start.43 = (f32[24,128]{1,0:T(8,128)S(1)}, f32[24,128]{1,0:T(8,128)S(1)}, u32[]{:S(2)}, u32[]{:S(2)}) collective-permute-start(f32[24,128]{1,0:T(8,128)S(1)} %maximum_add_fusion.5.refs_8_), channel_id=1, source_target_pairs={{0,26},{1,27},{2,24},{3,25},{4,30},{5,31},{6,28},{7,29},{8,18},{9,... | collective-permute-start | bytes 36872 | tf_op jit(solution)/shard_map/ppermute | solution.py:452
  47.3 4.0 %collective-permute-start.42 = (f32[24,128]{1,0:T(8,128)S(1)}, f32[24,128]{1,0:T(8,128)S(1)}, u32[]{:S(2)}, u32[]{:S(2)}) collective-permute-start(f32[24,128]{1,0:T(8,128)S(1)} %maximum_add_fusion.5.refs_8_), channel_id=1, source_target_pairs={{0,18},{1,19},{2,16},{3,17},{4,22},{5,23},{6,20},{7,21},{8,26},{9,... | collective-permute-start | bytes 36872 | tf_op jit(solution)/shard_map/ppermute | solution.py:452
  47.9 3.4 %collective-permute-start.41 = (f32[24,128]{1,0:T(8,128)S(1)}, f32[24,128]{1,0:T(8,128)S(1)}, u32[]{:S(2)}, u32[]{:S(2)}) collective-permute-start(f32[24,128]{1,0:T(8,128)S(1)} %maximum_add_fusion.5.refs_8_), channel_id=1, source_target_pairs={{0,10},{1,11},{2,8},{3,9},{4,14},{5,15},{6,12},{7,13},{8,2},{9,3},... | collective-permute-start | bytes 36872 | tf_op jit(solution)/shard_map/ppermute | solution.py:452
  51.3 1.3 %copy-start.6 = (f32[64,16,128]{2,1,0:T(8,128)S(1)}, f32[64,16,128]{2,1,0:T(8,128)}, u32[]{:S(2)}) copy-start(f32[64,16,128]{2,1,0:T(8,128)} %param.20) | copy-start | bytes 1572868
  52.7 0.5 copy-start.14
  52.7 0.6 %copy-start.12 = (f32[64,256]{1,0:T(8,128)}, f32[64,256]{1,0:T(8,128)S(1)}, u32[]{:S(2)}) copy-start(f32[64,256]{1,0:T(8,128)S(1)} %get-tuple-element.137) | copy-start | bytes 196612
  52.7 0.6 %copy-start.13 = (f32[64,128]{1,0:T(8,128)}, f32[64,128]{1,0:T(8,128)S(1)}, u32[]{:S(2)}) copy-start(f32[64,128]{1,0:T(8,128)S(1)} %get-tuple-element.136) | copy-start | bytes 98308

commit v18 on v17

--- a/solution.py
+++ b/solution.py
@@ -273,7 +273,7 @@
     given = Bag(**dict(zip(names_in, refs[: len(names_in)])))
     gives = Bag(**dict(zip(names_out, refs[len(names_in) :])))
     if last:
-        staged, sem = refs[-2:]
+        staged, staged_charge, sems = refs[-3:]
     own = lax.axis_index("region")
     hour_index = lax.axis_index("hours")
     gathered = given.gathered
@@ -332,8 +332,11 @@
         gives.cap_duals[tech] = duals_new
         out_sums[tech : tech + 1, :] = row_sum(avail * duals_new)
     if last:
-        copy = pltpu.make_async_copy(staged, gives.dispatch, sem)
-        copy.start()
+        copies = [
+            pltpu.make_async_copy(staged, gives.dispatch, sems.at[0]),
+            pltpu.make_async_copy(staged_charge, gives.charge, sems.at[1]),
+        ]
+        copies[0].start()
 
     maps_local = given.maps_local[...]
     slope_local = dot3(prices, maps_local, False)
@@ -351,7 +354,11 @@
         charge = given.charge[...]
         charge_before = read_lanes(small, at.before, units)
     charge_new = jnp.clip(charge - primal_step * (store_duals - next_duals), 0.0, energy)
-    gives.charge[...] = charge_new
+    if last:
+        staged_charge[...] = charge_new
+        copies[1].start()
+    else:
+        gives.charge[...] = charge_new
 
     primal_row = jnp.zeros((1, LANES), jnp.float32)
     bars = []
@@ -392,7 +399,8 @@
             low = local + chunk * LANES
             first = rows + 2 * techs + 8 * chunk
             gives.kept[first : first + 8, :] = given.flows[rows:, low : low + LANES]
-        copy.wait()
+        for copy in copies:
+            copy.wait()
         return
     gives.block[:rows, :] = prices + step_up
     gives.flows[rows:, local:] = given.flows[rows:, local:]
@@ -612,6 +620,7 @@
                 pltpu.SemaphoreType.DMA((4,)),
             ],
             limit=None,
+            flops=25 * 10**5,
         ).block
     )
     state = call(
@@ -690,9 +699,9 @@
         else:
             outs = Bag(
                 dispatch=shape(rows * techs, nodes),
+                charge=shape(rows, units),
                 capacity=shape(1, owned),
                 prices=shape(rows, nodes),
-                charge=shape(rows, units),
                 negative=shape(1, LANES),
                 kept=shape(rows + 2 * techs + 8 * (sizes.regions * sizes.slots // LANES), LANES),
             )
@@ -701,8 +710,12 @@
             functools.partial(sweep_kernel, sizes, iteration),
             given,
             outs,
-            copied=int(final),
-            scratch=[pltpu.VMEM(outs.dispatch.shape, jnp.float32), pltpu.SemaphoreType.DMA]
+            copied=2 if final else 0,
+            scratch=[
+                pltpu.VMEM(outs.dispatch.shape, jnp.float32),
+                pltpu.VMEM(outs.charge.shape, jnp.float32),
+                pltpu.SemaphoreType.DMA((2,)),
+            ]
             if final
             else [],
         )

time: 53.6 us -> 53.7 us (level)
  no operation moved by 1% of the time
where the time goes in v18:
time: 53.7 us; the launch traced here: 53.4 us
  starting transfers between devices  26.2 us (49%)
  waiting for transfers between devices  18 us (34%)
  Pallas kernels  6.52 us (12%)
  local copies, waits for them, and re-layouts  1.46 us (3%)
  between operations  1.02 us (2%)
    ppermute x22, starting transfers between devices, swap(): return lax.ppermute(value, ('hours', 'region'), pairs)  26.2 us
    ppermute x22, waiting for transfers between devices, swap(): return lax.ppermute(value, ('hours', 'region'), pairs)  18 us
    pallas_call x6, Pallas kernels, call(): pl.pallas_call(functools.partial(kernel, names_in, names_out), out_shape=...  6.52 us
    unnamed x30, local copies, waits for them, and re-layouts  1.38 us
  transfers between devices with their start and end apart: 22, of which 15 were waited for; matrix products, arithmetic and copies ran while one was open for 0% of the time, Pallas kernels for 3%

profile of v18, /device:TPU:0, one launch (start us, length us, event | category | flops | bytes accessed | tf_op | source)
XLA Modules:
  0.0 53.4 jit_solution(9409678742743525139)
XLA Ops:
  0.6 1.4 %shard_map.166 = f32[72,128]{1,0:T(8,128)} custom-call(f32[64,128]{1,0:T(8,128)} %refs_0_.1, s32[2,64]{1,0:T(2,128)} %bitcast.120, f32[1,64]{1,0:T(1,128)} %refs_2_.3, s32[1,2]{1,0:T(1,128)} %refs_3_.3), custom_call_target="tpu_custom_call" | custom-call | flops 2500000 | bytes 10000000 | tf_op jit(solution)/shard_map/pallas_call | solution.py:435
  2.1 3.0 %collective-permute-start.22 = (f32[72,128]{1,0:T(8,128)}, f32[72,128]{1,0:T(8,128)S(1)}, u32[]{:S(2)}, u32[]{:S(2)}) collective-permute-start(f32[72,128]{1,0:T(8,128)} %shard_map.166), channel_id=1, source_target_pairs={{0,1},{1,0},{2,3},{3,2},{4,5},{5,4},{6,7},{7,6},{8,9},{9,8},{10,11... | collective-permute-start | bytes 110600 | tf_op jit(solution)/shard_map/ppermute | solution.py:460
  5.1 0.0 copy-start.3
  5.1 0.0 copy-start.4
  5.2 0.0 copy-start.1
  5.2 0.0 copy-start
  5.2 0.0 copy-start.2
  5.2 0.6 %copy-done.10 = s32[2,256]{1,0:T(2,128)S(1)} copy-done((s32[2,256]{1,0:T(2,128)S(1)}, s32[2,256]{1,0:T(2,128)}, u32[]{:S(2)}) %copy-start.10) | copy-done | bytes 2072
  5.8 0.1 copy-done.8
  5.9 0.0 copy-done.7
  5.9 0.0 copy-done
  5.9 1.7 %shard_map.165 = (f32[18,64,128]{2,1,0:T(8,128)S(1)}, bf16[128,512]{1,0:T(8,128)(2,1)S(1)}, f32[64,512]{1,0:T(8,128)S(1)}, f32[64,256]{1,0:T(8,128)S(1)}, f32[17...) custom-call(f32[1024,128]{1,0:T(8,128)} %bitcast.86, f32[64,128]{1,0:T(8,128)S(1)} %copy-done.7, ...), custom_call_target="tpu_custom_call" | custom-call | flops 1000000 | bytes 4000000 | tf_op jit(solution)/shard_map/pallas_call | solution.py:435
  7.7 0.0 collective-permute-done.22
  7.7 0.4 shard_map.167
  8.2 0.1 collective-permute-start.23
  8.3 1.2 %collective-permute-done.23 = f32[120,128]{1,0:T(8,128)S(1)} collective-permute-done((f32[120,128]{1,0:T(8,128)S(1)}, f32[120,128]{1,0:T(8,128)S(1)}, u32[]{:S(2)}, u32[]{:S(2)}) %collective-permute-start.23) | collective-permute-done | bytes 61472 | tf_op jit(solution)/shard_map/ppermute | solution.py:460
  9.5 2.3 %collective-permute-start.26 = (f32[3,128]{1,0:T(4,128)S(1)}, f32[3,128]{1,0:T(4,128)S(1)}, u32[]{:S(2)}, u32[]{:S(2)}) collective-permute-start(f32[3,128]{1,0:T(4,128)S(1)} %slice.523), channel_id=1, source_target_pairs={{0,7},{1,6},{2,5},{3,4},{4,3},{5,2},{6,1},{7,0},{8,15},{9,14},{10,... | collective-permute-start | bytes 4616 | tf_op jit(solution)/shard_map/ppermute | solution.py:460
  11.9 0.6 %collective-permute-start.24 = (f32[56,128]{1,0:T(8,128)S(1)}, f32[56,128]{1,0:T(8,128)S(1)}, u32[]{:S(2)}, u32[]{:S(2)}) collective-permute-start(f32[56,128]{1,0:T(8,128)S(1)} %pad_maximum_fusion.10), channel_id=1, source_target_pairs={{0,6},{1,7},{2,4},{3,5},{4,2},{5,3},{6,0},{7,1},{8,14},{9,15},{10,... | collective-permute-start | bytes 86024 | tf_op jit(solution)/shard_map/ppermute | solution.py:460
  12.4 0.3 collective-permute-start.25
  12.7 2.5 %collective-permute-done.24.refs_11_ = f32[56,128]{1,0:T(8,128)S(1)} collective-permute-done((f32[56,128]{1,0:T(8,128)S(1)}, f32[56,128]{1,0:T(8,128)S(1)}, u32[]{:S(2)}, u32[]{:S(2)}) %collective-permute-start.24) | collective-permute-done | bytes 28704 | tf_op jit(solution)/shard_map/ppermute | solution.py:460
  15.3 0.0 collective-permute-done.26
  15.3 0.6 %collective-permute-done.25 = f32[67,128]{1,0:T(8,128)S(1)} collective-permute-done((f32[67,128]{1,0:T(8,128)S(1)}, f32[67,128]{1,0:T(8,128)S(1)}, u32[]{:S(2)}, u32[]{:S(2)}) %collective-permute-start.25) | collective-permute-done | bytes 34336 | tf_op jit(solution)/shard_map/ppermute | solution.py:460
  16.0 3.4 %collective-permute-start.29 = (f32[56,128]{1,0:T(8,128)S(1)}, f32[56,128]{1,0:T(8,128)S(1)}, u32[]{:S(2)}, u32[]{:S(2)}) collective-permute-start(f32[56,128]{1,0:T(8,128)S(1)} %maximum_add_fusion.3.refs_6_), channel_id=1, source_target_pairs={{0,26},{1,27},{2,24},{3,25},{4,30},{5,31},{6,28},{7,29},{8,18},{9,... | collective-permute-start | bytes 86024 | tf_op jit(solution)/shard_map/ppermute | solution.py:460
  19.4 0.0 collective-permute-start.28
  19.4 0.6 %collective-permute-start.27 = (f32[56,128]{1,0:T(8,128)S(1)}, f32[56,128]{1,0:T(8,128)S(1)}, u32[]{:S(2)}, u32[]{:S(2)}) collective-permute-start(f32[56,128]{1,0:T(8,128)S(1)} %maximum_add_fusion.3.refs_6_), channel_id=1, source_target_pairs={{0,10},{1,11},{2,8},{3,9},{4,14},{5,15},{6,12},{7,13},{8,2},{9,3},... | collective-permute-start | bytes 86024 | tf_op jit(solution)/shard_map/ppermute | solution.py:460
  20.0 1.1 %collective-permute-done.29.refs_9_ = f32[56,128]{1,0:T(8,128)S(1)} collective-permute-done((f32[56,128]{1,0:T(8,128)S(1)}, f32[56,128]{1,0:T(8,128)S(1)}, u32[]{:S(2)}, u32[]{:S(2)}) %collective-permute-start.29) | collective-permute-done | bytes 28704 | tf_op jit(solution)/shard_map/ppermute | solution.py:460
  21.1 2.5 %collective-permute-done.28.refs_8_ = f32[56,128]{1,0:T(8,128)S(1)} collective-permute-done((f32[56,128]{1,0:T(8,128)S(1)}, f32[56,128]{1,0:T(8,128)S(1)}, u32[]{:S(2)}, u32[]{:S(2)}) %collective-permute-start.28) | collective-permute-done | bytes 28704 | tf_op jit(solution)/shard_map/ppermute | solution.py:460
  23.6 0.0 collective-permute-done.27.refs_7_
  23.6 0.8 %shard_map.168 = (f32[17,64,128]{2,1,0:T(8,128)S(1)}, f32[17,64,128]{2,1,0:T(8,128)S(1)}, f32[72,640]{1,0:T(8,128)S(1)}, f32[64,256]{1,0:T(8,128)S(1)}, f32[64,256]{1,0:T(8,128)S(1)}, /*index=5*/f32[88,128]{1,0:T(8,128)S(1)}) custom-call(f32[18,64,128]{2,1,0:T(8,128)S(1)} %get-tuple-element.107.refs_0_, bf16[128,512]{1,0:T(8,128)(2,1)S(1)} %get-tuple-element.108.refs_1_, ...), custom_call_target="tpu_custom_call" | custom-call | tf_op jit(solution)/shard_map/pallas_call | solution.py:435
  24.4 0.4 collective-permute-start.30
  24.8 0.9 %collective-permute-done.30 = f32[88,128]{1,0:T(8,128)S(1)} collective-permute-done((f32[88,128]{1,0:T(8,128)S(1)}, f32[88,128]{1,0:T(8,128)S(1)}, u32[]{:S(2)}, u32[]{:S(2)}) %collective-permute-start.30) | collective-permute-done | bytes 45088 | tf_op jit(solution)/shard_map/ppermute | solution.py:460
  25.7 1.4 %collective-permute-start.33 = (f32[3,128]{1,0:T(4,128)S(1)}, f32[3,128]{1,0:T(4,128)S(1)}, u32[]{:S(2)}, u32[]{:S(2)}) collective-permute-start(f32[3,128]{1,0:T(4,128)S(1)} %slice.536), channel_id=1, source_target_pairs={{0,7},{1,6},{2,5},{3,4},{4,3},{5,2},{6,1},{7,0},{8,15},{9,14},{10,... | collective-permute-start | bytes 4616 | tf_op jit(solution)/shard_map/ppermute | solution.py:460
  27.2 0.4 collective-permute-start.31
  27.6 1.5 %collective-permute-start.32 = (f32[67,128]{1,0:T(8,128)S(1)}, f32[67,128]{1,0:T(8,128)S(1)}, u32[]{:S(2)}, u32[]{:S(2)}) collective-permute-start(f32[67,128]{1,0:T(8,128)S(1)} %pad_maximum_fusion.8), channel_id=1, source_target_pairs={{0,3},{1,2},{2,1},{3,0},{4,7},{5,6},{6,5},{7,4},{8,11},{9,10},{10,... | collective-permute-start | bytes 102920 | tf_op jit(solution)/shard_map/ppermute | solution.py:460
  29.1 1.3 %collective-permute-done.31.refs_13_ = f32[24,128]{1,0:T(8,128)S(1)} collective-permute-done((f32[24,128]{1,0:T(8,128)S(1)}, f32[24,128]{1,0:T(8,128)S(1)}, u32[]{:S(2)}, u32[]{:S(2)}) %collective-permute-start.31) | collective-permute-done | bytes 12320 | tf_op jit(solution)/shard_map/ppermute | solution.py:460
  30.4 0.0 collective-permute-done.33
  30.4 0.6 %collective-permute-done.32 = f32[67,128]{1,0:T(8,128)S(1)} collective-permute-done((f32[67,128]{1,0:T(8,128)S(1)}, f32[67,128]{1,0:T(8,128)S(1)}, u32[]{:S(2)}, u32[]{:S(2)}) %collective-permute-start.32) | collective-permute-done | bytes 34336 | tf_op jit(solution)/shard_map/ppermute | solution.py:460
  31.0 1.7 %collective-permute-start.36 = (f32[24,128]{1,0:T(8,128)S(1)}, f32[24,128]{1,0:T(8,128)S(1)}, u32[]{:S(2)}, u32[]{:S(2)}) collective-permute-start(f32[24,128]{1,0:T(8,128)S(1)} %maximum_add_fusion.4.refs_8_), channel_id=1, source_target_pairs={{0,26},{1,27},{2,24},{3,25},{4,30},{5,31},{6,28},{7,29},{8,18},{9,... | collective-permute-start | bytes 36872 | tf_op jit(solution)/shard_map/ppermute | solution.py:460
  32.7 0.2 collective-permute-start.35
  33.0 2.2 %collective-permute-start.34 = (f32[24,128]{1,0:T(8,128)S(1)}, f32[24,128]{1,0:T(8,128)S(1)}, u32[]{:S(2)}, u32[]{:S(2)}) collective-permute-start(f32[24,128]{1,0:T(8,128)S(1)} %maximum_add_fusion.4.refs_8_), channel_id=1, source_target_pairs={{0,10},{1,11},{2,8},{3,9},{4,14},{5,15},{6,12},{7,13},{8,2},{9,3},... | collective-permute-start | bytes 36872 | tf_op jit(solution)/shard_map/ppermute | solution.py:460
  35.2 0.8 %collective-permute-done.36.refs_11_ = f32[24,128]{1,0:T(8,128)S(1)} collective-permute-done((f32[24,128]{1,0:T(8,128)S(1)}, f32[24,128]{1,0:T(8,128)S(1)}, u32[]{:S(2)}, u32[]{:S(2)}) %collective-permute-start.36) | collective-permute-done | bytes 12320 | tf_op jit(solution)/shard_map/ppermute | solution.py:460
  36.0 0.8 %collective-permute-done.35.refs_10_ = f32[24,128]{1,0:T(8,128)S(1)} collective-permute-done((f32[24,128]{1,0:T(8,128)S(1)}, f32[24,128]{1,0:T(8,128)S(1)}, u32[]{:S(2)}, u32[]{:S(2)}) %collective-permute-start.35) | collective-permute-done | bytes 12320 | tf_op jit(solution)/shard_map/ppermute | solution.py:460
  36.8 0.0 collective-permute-done.34.refs_9_
  36.8 0.7 %shard_map.169 = (f32[17,64,128]{2,1,0:T(8,128)S(1)}, f32[17,64,128]{2,1,0:T(8,128)S(1)}, f32[72,640]{1,0:T(8,128)S(1)}, f32[64,256]{1,0:T(8,128)S(1)}, f32[64,256]{1,0:T(8,128)S(1)}, /*index=5*/f32[88,128]{1,0:T(8,128)S(1)}) custom-call(f32[18,64,128]{2,1,0:T(8,128)S(1)} %get-tuple-element.107.refs_0_, bf16[128,512]{1,0:T(8,128)(2,1)S(1)} %get-tuple-element.108.refs_1_, ...), custom_call_target="tpu_custom_call" | custom-call | tf_op jit(solution)/shard_map/pallas_call | solution.py:435
  37.5 0.5 collective-permute-start.37
  38.0 0.9 %collective-permute-done.37 = f32[88,128]{1,0:T(8,128)S(1)} collective-permute-done((f32[88,128]{1,0:T(8,128)S(1)}, f32[88,128]{1,0:T(8,128)S(1)}, u32[]{:S(2)}, u32[]{:S(2)}) %collective-permute-start.37) | collective-permute-done | bytes 45088 | tf_op jit(solution)/shard_map/ppermute | solution.py:460
  38.9 2.5 %collective-permute-start.40 = (f32[3,128]{1,0:T(4,128)S(1)}, f32[3,128]{1,0:T(4,128)S(1)}, u32[]{:S(2)}, u32[]{:S(2)}) collective-permute-start(f32[3,128]{1,0:T(4,128)S(1)} %slice.549), channel_id=1, source_target_pairs={{0,7},{1,6},{2,5},{3,4},{4,3},{5,2},{6,1},{7,0},{8,15},{9,14},{10,... | collective-permute-start | bytes 4616 | tf_op jit(solution)/shard_map/ppermute | solution.py:460
  41.4 0.4 collective-permute-start.38
  41.8 0.5 collective-permute-start.39
  42.3 2.3 %collective-permute-done.38.refs_13_ = f32[24,128]{1,0:T(8,128)S(1)} collective-permute-done((f32[24,128]{1,0:T(8,128)S(1)}, f32[24,128]{1,0:T(8,128)S(1)}, u32[]{:S(2)}, u32[]{:S(2)}) %collective-permute-start.38) | collective-permute-done | bytes 12320 | tf_op jit(solution)/shard_map/ppermute | solution.py:460
  44.6 0.0 collective-permute-done.40
  44.6 0.6 %collective-permute-done.39 = f32[67,128]{1,0:T(8,128)S(1)} collective-permute-done((f32[67,128]{1,0:T(8,128)S(1)}, f32[67,128]{1,0:T(8,128)S(1)}, u32[]{:S(2)}, u32[]{:S(2)}) %collective-permute-start.39) | collective-permute-done | bytes 34336 | tf_op jit(solution)/shard_map/ppermute | solution.py:460
  45.2 2.1 %collective-permute-start.43 = (f32[24,128]{1,0:T(8,128)S(1)}, f32[24,128]{1,0:T(8,128)S(1)}, u32[]{:S(2)}, u32[]{:S(2)}) collective-permute-start(f32[24,128]{1,0:T(8,128)S(1)} %maximum_add_fusion.5.refs_8_), channel_id=1, source_target_pairs={{0,26},{1,27},{2,24},{3,25},{4,30},{5,31},{6,28},{7,29},{8,18},{9,... | collective-permute-start | bytes 36872 | tf_op jit(solution)/shard_map/ppermute | solution.py:460
  47.3 0.6 %collective-permute-start.42 = (f32[24,128]{1,0:T(8,128)S(1)}, f32[24,128]{1,0:T(8,128)S(1)}, u32[]{:S(2)}, u32[]{:S(2)}) collective-permute-start(f32[24,128]{1,0:T(8,128)S(1)} %maximum_add_fusion.5.refs_8_), channel_id=1, source_target_pairs={{0,18},{1,19},{2,16},{3,17},{4,22},{5,23},{6,20},{7,21},{8,26},{9,... | collective-permute-start | bytes 36872 | tf_op jit(solution)/shard_map/ppermute | solution.py:460
  47.9 1.4 %collective-permute-start.41 = (f32[24,128]{1,0:T(8,128)S(1)}, f32[24,128]{1,0:T(8,128)S(1)}, u32[]{:S(2)}, u32[]{:S(2)}) collective-permute-start(f32[24,128]{1,0:T(8,128)S(1)} %maximum_add_fusion.5.refs_8_), channel_id=1, source_target_pairs={{0,10},{1,11},{2,8},{3,9},{4,14},{5,15},{6,12},{7,13},{8,2},{9,3},... | collective-permute-start | bytes 36872 | tf_op jit(solution)/shard_map/ppermute | solution.py:460
  49.4 0.8 %collective-permute-done.43.refs_11_ = f32[24,128]{1,0:T(8,128)S(1)} collective-permute-done((f32[24,128]{1,0:T(8,128)S(1)}, f32[24,128]{1,0:T(8,128)S(1)}, u32[]{:S(2)}, u32[]{:S(2)}) %collective-permute-start.43) | collective-permute-done | bytes 12320 | tf_op jit(solution)/shard_map/ppermute | solution.py:460
  50.2 1.1 %collective-permute-done.42.refs_10_ = f32[24,128]{1,0:T(8,128)S(1)} collective-permute-done((f32[24,128]{1,0:T(8,128)S(1)}, f32[24,128]{1,0:T(8,128)S(1)}, u32[]{:S(2)}, u32[]{:S(2)}) %collective-permute-start.42) | collective-permute-done | bytes 12320 | tf_op jit(solution)/shard_map/ppermute | solution.py:460
  51.3 1.4 %shard_map.170 = (f32[1024,128]{1,0:T(8,128)}, f32[64,256]{1,0:T(8,128)S(1)}, f32[1,128]{1,0:T(1,128)S(1)}, f32[64,128]{1,0:T(8,128)S(1)}, f32[1,128]{1,0:T(1,128)S(1)}, /*index=5*/f32[104,128]{1,0:T(8,128)S(1)}) custom-call(f32[18,64,128]{2,1,0:T(8,128)S(1)} %get-tuple-element.107.refs_0_, bf16[128,512]{1,0:T(8,128)(2,1)S(1)} %get-tuple-element.108.refs_1_, ...), custom_call_target="tpu_custom_call" | custom-call | tf_op jit(solution)/shard_map/pallas_call | solution.py:435
  52.8 0.0 copy-start.14
  52.8 0.0 copy-start.12
  52.8 0.0 copy-start.13
  52.8 0.5 copy-done.14
  53.3 0.1 copy-done.12
  53.4 0.0 copy-done.13
  (65 shorter events, 0.3 us)
Async XLA Ops:
  0.6 4.6 %copy-start.11 = (s32[256]{0:T(256)S(1)}, s32[256]{0:T(256)}, u32[]{:S(2)}) copy-start(s32[256]{0:T(256)} %param.30) | copy-start | bytes 3076
  2.1 5.6 %collective-permute-start.22 = (f32[72,128]{1,0:T(8,128)}, f32[72,128]{1,0:T(8,128)S(1)}, u32[]{:S(2)}, u32[]{:S(2)}) collective-permute-start(f32[72,128]{1,0:T(8,128)} %shard_map.166), channel_id=1, source_target_pairs={{0,1},{1,0},{2,3},{3,2},{4,5},{5,4},{6,7},{7,6},{8,9},{9,8},{10,11... | collective-permute-start | bytes 110600 | tf_op jit(solution)/shard_map/ppermute | solution.py:460
  5.1 0.7 %copy-start.10 = (s32[2,256]{1,0:T(2,128)S(1)}, s32[2,256]{1,0:T(2,128)}, u32[]{:S(2)}) copy-start(s32[2,256]{1,0:T(2,128)} %refs_6_.1) | copy-start | bytes 6148
  5.1 0.8 %copy-start.8 = (f32[64,128]{1,0:T(8,128)S(1)}, f32[64,128]{1,0:T(8,128)}, u32[]{:S(2)}) copy-start(f32[64,128]{1,0:T(8,128)} %refs_2_.2) | copy-start | bytes 98308
  5.1 0.8 %copy-start.7 = (f32[64,128]{1,0:T(8,128)S(1)}, f32[64,128]{1,0:T(8,128)}, u32[]{:S(2)}) copy-start(f32[64,128]{1,0:T(8,128)} %refs_0_.1) | copy-start | bytes 98308
  5.1 0.8 %copy-start.5 = (f32[1,128]{1,0:T(1,128)S(1)}, f32[1,128]{1,0:T(1,128)}, u32[]{:S(2)}) copy-start(f32[1,128]{1,0:T(1,128)} %refs_4_.1) | copy-start | bytes 1540
  5.1 0.8 %copy-start.3 = (f32[256]{0:T(256)S(1)}, f32[256]{0:T(256)}, u32[]{:S(2)}) copy-start(f32[256]{0:T(256)} %param.32) | copy-start | bytes 3076
  5.1 0.8 %copy-start.4 = (f32[256]{0:T(256)S(1)}, f32[256]{0:T(256)}, u32[]{:S(2)}) copy-start(f32[256]{0:T(256)} %param.31) | copy-start | bytes 3076
  5.2 0.8 %copy-start.1 = (s32[1,2048]{1,0:T(1,128)S(1)}, s32[1,2048]{1,0:T(1,128)}, u32[]{:S(2)}) copy-start(s32[1,2048]{1,0:T(1,128)} %param.24) | copy-start | bytes 24580
  5.2 0.8 %copy-start = (f32[16,128]{1,0:T(8,128)S(1)}, f32[16,128]{1,0:T(8,128)}, u32[]{:S(2)}) copy-start(f32[16,128]{1,0:T(8,128)} %refs_3_.2) | copy-start | bytes 24580
  5.2 0.7 %copy-start.2 = (f32[256]{0:T(256)S(1)}, f32[256]{0:T(256)}, u32[]{:S(2)}) copy-start(f32[256]{0:T(256)} %param.26) | copy-start | bytes 3076
  5.9 1.8 %copy-start.9 = (f32[72,128]{1,0:T(8,128)S(1)}, f32[72,128]{1,0:T(8,128)}, u32[]{:S(2)}) copy-start(f32[72,128]{1,0:T(8,128)} %shard_map.166) | copy-start | bytes 110596
  8.2 1.3 %collective-permute-start.23 = (f32[120,128]{1,0:T(8,128)S(1)}, f32[120,128]{1,0:T(8,128)S(1)}, u32[]{:S(2)}, u32[]{:S(2)}) collective-permute-start(f32[120,128]{1,0:T(8,128)S(1)} %get-tuple-element.116), channel_id=1, source_target_pairs={{0,2},{1,3},{2,0},{3,1},{4,6},{5,7},{6,4},{7,5},{8,10},{9,11},{10,... | collective-permute-start | bytes 184328 | tf_op jit(solution)/shard_map/ppermute | solution.py:460
  9.5 5.8 %collective-permute-start.26 = (f32[3,128]{1,0:T(4,128)S(1)}, f32[3,128]{1,0:T(4,128)S(1)}, u32[]{:S(2)}, u32[]{:S(2)}) collective-permute-start(f32[3,128]{1,0:T(4,128)S(1)} %slice.523), channel_id=1, source_target_pairs={{0,7},{1,6},{2,5},{3,4},{4,3},{5,2},{6,1},{7,0},{8,15},{9,14},{10,... | collective-permute-start | bytes 4616 | tf_op jit(solution)/shard_map/ppermute | solution.py:460
  11.9 3.4 %collective-permute-start.24 = (f32[56,128]{1,0:T(8,128)S(1)}, f32[56,128]{1,0:T(8,128)S(1)}, u32[]{:S(2)}, u32[]{:S(2)}) collective-permute-start(f32[56,128]{1,0:T(8,128)S(1)} %pad_maximum_fusion.10), channel_id=1, source_target_pairs={{0,6},{1,7},{2,4},{3,5},{4,2},{5,3},{6,0},{7,1},{8,14},{9,15},{10,... | collective-permute-start | bytes 86024 | tf_op jit(solution)/shard_map/ppermute | solution.py:460
  12.4 3.5 %collective-permute-start.25 = (f32[67,128]{1,0:T(8,128)S(1)}, f32[67,128]{1,0:T(8,128)S(1)}, u32[]{:S(2)}, u32[]{:S(2)}) collective-permute-start(f32[67,128]{1,0:T(8,128)S(1)} %pad_maximum_fusion.7), channel_id=1, source_target_pairs={{0,3},{1,2},{2,1},{3,0},{4,7},{5,6},{6,5},{7,4},{8,11},{9,10},{10,... | collective-permute-start | bytes 102920 | tf_op jit(solution)/shard_map/ppermute | solution.py:460
  16.0 5.2 %collective-permute-start.29 = (f32[56,128]{1,0:T(8,128)S(1)}, f32[56,128]{1,0:T(8,128)S(1)}, u32[]{:S(2)}, u32[]{:S(2)}) collective-permute-start(f32[56,128]{1,0:T(8,128)S(1)} %maximum_add_fusion.3.refs_6_), channel_id=1, source_target_pairs={{0,26},{1,27},{2,24},{3,25},{4,30},{5,31},{6,28},{7,29},{8,18},{9,... | collective-permute-start | bytes 86024 | tf_op jit(solution)/shard_map/ppermute | solution.py:460
  19.4 4.2 %collective-permute-start.28 = (f32[56,128]{1,0:T(8,128)S(1)}, f32[56,128]{1,0:T(8,128)S(1)}, u32[]{:S(2)}, u32[]{:S(2)}) collective-permute-start(f32[56,128]{1,0:T(8,128)S(1)} %maximum_add_fusion.3.refs_6_), channel_id=1, source_target_pairs={{0,18},{1,19},{2,16},{3,17},{4,22},{5,23},{6,20},{7,21},{8,26},{9,... | collective-permute-start | bytes 86024 | tf_op jit(solution)/shard_map/ppermute | solution.py:460
  19.4 4.2 %collective-permute-start.27 = (f32[56,128]{1,0:T(8,128)S(1)}, f32[56,128]{1,0:T(8,128)S(1)}, u32[]{:S(2)}, u32[]{:S(2)}) collective-permute-start(f32[56,128]{1,0:T(8,128)S(1)} %maximum_add_fusion.3.refs_6_), channel_id=1, source_target_pairs={{0,10},{1,11},{2,8},{3,9},{4,14},{5,15},{6,12},{7,13},{8,2},{9,3},... | collective-permute-start | bytes 86024 | tf_op jit(solution)/shard_map/ppermute | solution.py:460
  24.4 1.3 %collective-permute-start.30 = (f32[88,128]{1,0:T(8,128)S(1)}, f32[88,128]{1,0:T(8,128)S(1)}, u32[]{:S(2)}, u32[]{:S(2)}) collective-permute-start(f32[88,128]{1,0:T(8,128)S(1)} %get-tuple-element.122), channel_id=1, source_target_pairs={{0,2},{1,3},{2,0},{3,1},{4,6},{5,7},{6,4},{7,5},{8,10},{9,11},{10,... | collective-permute-start | bytes 135176 | tf_op jit(solution)/shard_map/ppermute | solution.py:460
  25.7 4.7 %collective-permute-start.33 = (f32[3,128]{1,0:T(4,128)S(1)}, f32[3,128]{1,0:T(4,128)S(1)}, u32[]{:S(2)}, u32[]{:S(2)}) collective-permute-start(f32[3,128]{1,0:T(4,128)S(1)} %slice.536), channel_id=1, source_target_pairs={{0,7},{1,6},{2,5},{3,4},{4,3},{5,2},{6,1},{7,0},{8,15},{9,14},{10,... | collective-permute-start | bytes 4616 | tf_op jit(solution)/shard_map/ppermute | solution.py:460
  27.2 3.2 %collective-permute-start.31 = (f32[24,128]{1,0:T(8,128)S(1)}, f32[24,128]{1,0:T(8,128)S(1)}, u32[]{:S(2)}, u32[]{:S(2)}) collective-permute-start(f32[24,128]{1,0:T(8,128)S(1)} %pad_maximum_fusion.11), channel_id=1, source_target_pairs={{0,6},{1,7},{2,4},{3,5},{4,2},{5,3},{6,0},{7,1},{8,14},{9,15},{10,... | collective-permute-start | bytes 36872 | tf_op jit(solution)/shard_map/ppermute | solution.py:460
  27.6 3.4 %collective-permute-start.32 = (f32[67,128]{1,0:T(8,128)S(1)}, f32[67,128]{1,0:T(8,128)S(1)}, u32[]{:S(2)}, u32[]{:S(2)}) collective-permute-start(f32[67,128]{1,0:T(8,128)S(1)} %pad_maximum_fusion.8), channel_id=1, source_target_pairs={{0,3},{1,2},{2,1},{3,0},{4,7},{5,6},{6,5},{7,4},{8,11},{9,10},{10,... | collective-permute-start | bytes 102920 | tf_op jit(solution)/shard_map/ppermute | solution.py:460
  31.0 5.0 %collective-permute-start.36 = (f32[24,128]{1,0:T(8,128)S(1)}, f32[24,128]{1,0:T(8,128)S(1)}, u32[]{:S(2)}, u32[]{:S(2)}) collective-permute-start(f32[24,128]{1,0:T(8,128)S(1)} %maximum_add_fusion.4.refs_8_), channel_id=1, source_target_pairs={{0,26},{1,27},{2,24},{3,25},{4,30},{5,31},{6,28},{7,29},{8,18},{9,... | collective-permute-start | bytes 36872 | tf_op jit(solution)/shard_map/ppermute | solution.py:460
  32.7 4.0 %collective-permute-start.35 = (f32[24,128]{1,0:T(8,128)S(1)}, f32[24,128]{1,0:T(8,128)S(1)}, u32[]{:S(2)}, u32[]{:S(2)}) collective-permute-start(f32[24,128]{1,0:T(8,128)S(1)} %maximum_add_fusion.4.refs_8_), channel_id=1, source_target_pairs={{0,18},{1,19},{2,16},{3,17},{4,22},{5,23},{6,20},{7,21},{8,26},{9,... | collective-permute-start | bytes 36872 | tf_op jit(solution)/shard_map/ppermute | solution.py:460
  33.0 3.8 %collective-permute-start.34 = (f32[24,128]{1,0:T(8,128)S(1)}, f32[24,128]{1,0:T(8,128)S(1)}, u32[]{:S(2)}, u32[]{:S(2)}) collective-permute-start(f32[24,128]{1,0:T(8,128)S(1)} %maximum_add_fusion.4.refs_8_), channel_id=1, source_target_pairs={{0,10},{1,11},{2,8},{3,9},{4,14},{5,15},{6,12},{7,13},{8,2},{9,3},... | collective-permute-start | bytes 36872 | tf_op jit(solution)/shard_map/ppermute | solution.py:460
  37.5 1.4 %collective-permute-start.37 = (f32[88,128]{1,0:T(8,128)S(1)}, f32[88,128]{1,0:T(8,128)S(1)}, u32[]{:S(2)}, u32[]{:S(2)}) collective-permute-start(f32[88,128]{1,0:T(8,128)S(1)} %get-tuple-element.128), channel_id=1, source_target_pairs={{0,2},{1,3},{2,0},{3,1},{4,6},{5,7},{6,4},{7,5},{8,10},{9,11},{10,... | collective-permute-start | bytes 135176 | tf_op jit(solution)/shard_map/ppermute | solution.py:460
  38.9 5.7 %collective-permute-start.40 = (f32[3,128]{1,0:T(4,128)S(1)}, f32[3,128]{1,0:T(4,128)S(1)}, u32[]{:S(2)}, u32[]{:S(2)}) collective-permute-start(f32[3,128]{1,0:T(4,128)S(1)} %slice.549), channel_id=1, source_target_pairs={{0,7},{1,6},{2,5},{3,4},{4,3},{5,2},{6,1},{7,0},{8,15},{9,14},{10,... | collective-permute-start | bytes 4616 | tf_op jit(solution)/shard_map/ppermute | solution.py:460
  41.4 3.2 %collective-permute-start.38 = (f32[24,128]{1,0:T(8,128)S(1)}, f32[24,128]{1,0:T(8,128)S(1)}, u32[]{:S(2)}, u32[]{:S(2)}) collective-permute-start(f32[24,128]{1,0:T(8,128)S(1)} %pad_maximum_fusion.12), channel_id=1, source_target_pairs={{0,6},{1,7},{2,4},{3,5},{4,2},{5,3},{6,0},{7,1},{8,14},{9,15},{10,... | collective-permute-start | bytes 36872 | tf_op jit(solution)/shard_map/ppermute | solution.py:460
  41.8 3.4 %collective-permute-start.39 = (f32[67,128]{1,0:T(8,128)S(1)}, f32[67,128]{1,0:T(8,128)S(1)}, u32[]{:S(2)}, u32[]{:S(2)}) collective-permute-start(f32[67,128]{1,0:T(8,128)S(1)} %pad_maximum_fusion.9), channel_id=1, source_target_pairs={{0,3},{1,2},{2,1},{3,0},{4,7},{5,6},{6,5},{7,4},{8,11},{9,10},{10,... | collective-permute-start | bytes 102920 | tf_op jit(solution)/shard_map/ppermute | solution.py:460
  45.2 5.0 %collective-permute-start.43 = (f32[24,128]{1,0:T(8,128)S(1)}, f32[24,128]{1,0:T(8,128)S(1)}, u32[]{:S(2)}, u32[]{:S(2)}) collective-permute-start(f32[24,128]{1,0:T(8,128)S(1)} %maximum_add_fusion.5.refs_8_), channel_id=1, source_target_pairs={{0,26},{1,27},{2,24},{3,25},{4,30},{5,31},{6,28},{7,29},{8,18},{9,... | collective-permute-start | bytes 36872 | tf_op jit(solution)/shard_map/ppermute | solution.py:460
  47.3 4.0 %collective-permute-start.42 = (f32[24,128]{1,0:T(8,128)S(1)}, f32[24,128]{1,0:T(8,128)S(1)}, u32[]{:S(2)}, u32[]{:S(2)}) collective-permute-start(f32[24,128]{1,0:T(8,128)S(1)} %maximum_add_fusion.5.refs_8_), channel_id=1, source_target_pairs={{0,18},{1,19},{2,16},{3,17},{4,22},{5,23},{6,20},{7,21},{8,26},{9,... | collective-permute-start | bytes 36872 | tf_op jit(solution)/shard_map/ppermute | solution.py:460
  47.9 3.4 %collective-permute-start.41 = (f32[24,128]{1,0:T(8,128)S(1)}, f32[24,128]{1,0:T(8,128)S(1)}, u32[]{:S(2)}, u32[]{:S(2)}) collective-permute-start(f32[24,128]{1,0:T(8,128)S(1)} %maximum_add_fusion.5.refs_8_), channel_id=1, source_target_pairs={{0,10},{1,11},{2,8},{3,9},{4,14},{5,15},{6,12},{7,13},{8,2},{9,3},... | collective-permute-start | bytes 36872 | tf_op jit(solution)/shard_map/ppermute | solution.py:460
  51.3 1.4 %copy-start.6 = (f32[64,16,128]{2,1,0:T(8,128)S(1)}, f32[64,16,128]{2,1,0:T(8,128)}, u32[]{:S(2)}) copy-start(f32[64,16,128]{2,1,0:T(8,128)} %param.20) | copy-start | bytes 1572868
  52.8 0.5 copy-start.14
  52.8 0.6 %copy-start.12 = (f32[64,256]{1,0:T(8,128)}, f32[64,256]{1,0:T(8,128)S(1)}, u32[]{:S(2)}) copy-start(f32[64,256]{1,0:T(8,128)S(1)} %get-tuple-element.137) | copy-start | bytes 196612
  52.8 0.6 %copy-start.13 = (f32[64,128]{1,0:T(8,128)}, f32[64,128]{1,0:T(8,128)S(1)}, u32[]{:S(2)}) copy-start(f32[64,128]{1,0:T(8,128)S(1)} %get-tuple-element.136) | copy-start | bytes 98308

commit v19 on v17

--- a/solution.py
+++ b/solution.py
@@ -265,6 +265,15 @@
     return (parts.slab[...] + parts.near[...]) + (parts.middle[...] + parts.far[...])
 
 
+def slopes_kernel(sizes, names_in, names_out, gathered, maps_local, maps_cross, slopes_ref):
+    rows, regions = sizes.rows, sizes.regions
+    local = sizes.lines + sizes.units
+    prices_all = jnp.concatenate([gathered[region, :rows, :] for region in range(regions)], axis=1)
+    prices = gathered[lax.axis_index("region"), :rows, :]
+    slopes_ref[:, :local] = dot3(prices, maps_local[...], False)
+    slopes_ref[:, local:] = dot3(prices_all, maps_cross[...], False)
+
+
 def sweep_kernel(sizes, iteration, names_in, names_out, *refs):
     rows, techs, nodes = sizes.rows, sizes.techs, sizes.nodes
     slots, regions, lines, units = sizes.slots, sizes.regions, sizes.lines, sizes.units
@@ -303,7 +312,6 @@
     capacity_new = jnp.maximum(capacity - (cost - sums[:techs]) / (weight * col_weight), 0.0)
     capacity_bar = 2.0 * capacity_new - capacity
 
-    prices_all = jnp.concatenate([gathered[region, :rows, :] for region in range(regions)], axis=1)
     prices = gathered[own, :rows, :]
     gen_cost = fixed[:techs, :]
     half_weight = weight / 2.0
@@ -336,8 +344,6 @@
         copy.start()
 
     maps_local = given.maps_local[...]
-    slope_local = dot3(prices, maps_local, False)
-    slope_cross = dot3(prices_all, given.maps_cross[...], False)
 
     energy = read_lanes(fixed, at.energy, units)
     row_id = lax.broadcasted_iota(jnp.int32, (rows, units), 0)
@@ -358,11 +364,14 @@
     local, total_flows = lines + units, lines + units + regions * slots
     local_limits = read_lanes(fixed, at.limits, local)
     cross_limits = given.flows[rows + 2 : rows + 3, local:]
-    for bound, slope, low, high in (
-        (local_limits[:, :lines], slope_local[:, :lines], 0, lines),
-        (local_limits[:, lines:], slope_local[:, lines:] + store_duals, lines, local),
-        (cross_limits, slope_cross, local, total_flows),
+    for bound, low, high in (
+        (local_limits[:, :lines], 0, lines),
+        (local_limits[:, lines:], lines, local),
+        (cross_limits, local, total_flows),
     ):
+        slope = given.slopes[:, low:high]
+        if low == lines:
+            slope = slope + store_duals
         old = given.flows[:rows, low:high]
         new = jnp.clip(old - primal_step * slope, -bound, bound)
         bars.append(2.0 * new - old)
@@ -677,7 +686,12 @@
     )
     state = Bag(**vars(state))
     for iteration in range(1, ITERS):
-        given = Bag(**vars(state), **vars(parts), gathered=gathered)
+        slopes = call(
+            functools.partial(slopes_kernel, sizes),
+            Bag(gathered=gathered, maps_local=state.maps_local, maps_cross=state.maps_cross),
+            Bag(slopes=shape(rows, lines + units + sizes.regions * sizes.slots)),
+        ).slopes
+        given = Bag(**vars(state), **vars(parts), gathered=gathered, slopes=slopes)
         if iteration < ITERS - 1:
             outs = Bag(
                 dispatch=shape(techs + 1, rows, nodes),

time: 53.6 us -> 53.5 us (level)
  waiting for transfers between devices: 18 us -> 17.3 us
  Pallas kernels: 6.43 us -> 7.02 us
    ppermute x22, waiting for transfers between devices: 18 us -> 17.3 us  [swap(): return lax.ppermute(value, ('hours', 'region'), pairs)]
    pallas_call x6 -> x9, Pallas kernels: 6.43 us -> 7.02 us  [call(): pl.pallas_call(functools.partial(kernel, names_in, names_out), out_shape=...]
  transfers between devices with their start and end apart: 22 -> 22, of which waited for: 15 -> 15; matrix products, arithmetic and copies ran while one was open for 0% -> 0% of each run, Pallas kernels for 3% -> 5%
where the time goes in v19:
time: 53.5 us; the launch traced here: 53.2 us
  starting transfers between devices  26.2 us (49%)
  waiting for transfers between devices  17.3 us (32%)
  Pallas kernels  7.02 us (13%)
  local copies, waits for them, and re-layouts  1.46 us (3%)
  between operations  1.05 us (2%)
    ppermute x22, starting transfers between devices, swap(): return lax.ppermute(value, ('hours', 'region'), pairs)  26.2 us
    ppermute x22, waiting for transfers between devices, swap(): return lax.ppermute(value, ('hours', 'region'), pairs)  17.3 us
    pallas_call x9, Pallas kernels, call(): pl.pallas_call(functools.partial(kernel, names_in, names_out), out_shape=...  7.02 us
    unnamed x30, local copies, waits for them, and re-layouts  1.38 us
  transfers between devices with their start and end apart: 22, of which 15 were waited for; matrix products, arithmetic and copies ran while one was open for 0% of the time, Pallas kernels for 5%

profile of v19, /device:TPU:0, one launch (start us, length us, event | category | flops | bytes accessed | tf_op | source)
XLA Modules:
  0.0 53.2 jit_solution(6144375078277823009)
XLA Ops:
  0.6 1.4 %shard_map.166 = f32[72,128]{1,0:T(8,128)} custom-call(f32[64,128]{1,0:T(8,128)} %refs_0_.1, s32[2,64]{1,0:T(2,128)} %bitcast.120, f32[1,64]{1,0:T(1,128)} %refs_2_.3, s32[1,2]{1,0:T(1,128)} %refs_3_.3), custom_call_target="tpu_custom_call" | custom-call | tf_op jit(solution)/shard_map/pallas_call | solution.py:436
  2.1 3.0 %collective-permute-start.22 = (f32[72,128]{1,0:T(8,128)}, f32[72,128]{1,0:T(8,128)S(1)}, u32[]{:S(2)}, u32[]{:S(2)}) collective-permute-start(f32[72,128]{1,0:T(8,128)} %shard_map.166), channel_id=1, source_target_pairs={{0,1},{1,0},{2,3},{3,2},{4,5},{5,4},{6,7},{7,6},{8,9},{9,8},{10,11... | collective-permute-start | bytes 110600 | tf_op jit(solution)/shard_map/ppermute | solution.py:461
  5.1 0.0 copy-start.3
  5.1 0.0 copy-start.4
  5.2 0.0 copy-start.1
  5.2 0.0 copy-start
  5.2 0.0 copy-start.2
  5.2 0.6 %copy-done.10 = s32[2,256]{1,0:T(2,128)S(1)} copy-done((s32[2,256]{1,0:T(2,128)S(1)}, s32[2,256]{1,0:T(2,128)}, u32[]{:S(2)}) %copy-start.10) | copy-done | bytes 2072
  5.8 0.1 copy-done.8
  5.9 0.0 copy-done.7
  5.9 0.0 copy-done
  5.9 1.7 %shard_map.165 = (f32[18,64,128]{2,1,0:T(8,128)S(1)}, bf16[128,512]{1,0:T(8,128)(2,1)S(1)}, f32[64,512]{1,0:T(8,128)S(1)}, f32[64,256]{1,0:T(8,128)S(1)}, f32[17...) custom-call(f32[1024,128]{1,0:T(8,128)} %bitcast.86, f32[64,128]{1,0:T(8,128)S(1)} %copy-done.7, ...), custom_call_target="tpu_custom_call" | custom-call | flops 1000000 | bytes 4000000 | tf_op jit(solution)/shard_map/pallas_call | solution.py:436
  7.7 0.4 shard_map.167
  8.2 0.1 collective-permute-start.23
  8.3 1.2 %collective-permute-done.23 = f32[120,128]{1,0:T(8,128)S(1)} collective-permute-done((f32[120,128]{1,0:T(8,128)S(1)}, f32[120,128]{1,0:T(8,128)S(1)}, u32[]{:S(2)}, u32[]{:S(2)}) %collective-permute-start.23) | collective-permute-done | bytes 61472 | tf_op jit(solution)/shard_map/ppermute | solution.py:461
  9.5 2.3 %collective-permute-start.26 = (f32[3,128]{1,0:T(4,128)S(1)}, f32[3,128]{1,0:T(4,128)S(1)}, u32[]{:S(2)}, u32[]{:S(2)}) collective-permute-start(f32[3,128]{1,0:T(4,128)S(1)} %slice.523), channel_id=1, source_target_pairs={{0,7},{1,6},{2,5},{3,4},{4,3},{5,2},{6,1},{7,0},{8,15},{9,14},{10,... | collective-permute-start | bytes 4616 | tf_op jit(solution)/shard_map/ppermute | solution.py:461
  11.9 0.6 %collective-permute-start.24 = (f32[56,128]{1,0:T(8,128)S(1)}, f32[56,128]{1,0:T(8,128)S(1)}, u32[]{:S(2)}, u32[]{:S(2)}) collective-permute-start(f32[56,128]{1,0:T(8,128)S(1)} %pad_maximum_fusion.10), channel_id=1, source_target_pairs={{0,6},{1,7},{2,4},{3,5},{4,2},{5,3},{6,0},{7,1},{8,14},{9,15},{10,... | collective-permute-start | bytes 86024 | tf_op jit(solution)/shard_map/ppermute | solution.py:461
  12.4 0.3 collective-permute-start.25
  12.7 2.5 %collective-permute-done.24.refs_11_ = f32[56,128]{1,0:T(8,128)S(1)} collective-permute-done((f32[56,128]{1,0:T(8,128)S(1)}, f32[56,128]{1,0:T(8,128)S(1)}, u32[]{:S(2)}, u32[]{:S(2)}) %collective-permute-start.24) | collective-permute-done | bytes 28704 | tf_op jit(solution)/shard_map/ppermute | solution.py:461
  15.3 0.0 collective-permute-done.26
  15.3 0.6 %collective-permute-done.25 = f32[67,128]{1,0:T(8,128)S(1)} collective-permute-done((f32[67,128]{1,0:T(8,128)S(1)}, f32[67,128]{1,0:T(8,128)S(1)}, u32[]{:S(2)}, u32[]{:S(2)}) %collective-permute-start.25) | collective-permute-done | bytes 34336 | tf_op jit(solution)/shard_map/ppermute | solution.py:461
  16.0 3.4 %collective-permute-start.29 = (f32[56,128]{1,0:T(8,128)S(1)}, f32[56,128]{1,0:T(8,128)S(1)}, u32[]{:S(2)}, u32[]{:S(2)}) collective-permute-start(f32[56,128]{1,0:T(8,128)S(1)} %maximum_add_fusion.3.refs_6_), channel_id=1, source_target_pairs={{0,26},{1,27},{2,24},{3,25},{4,30},{5,31},{6,28},{7,29},{8,18},{9,... | collective-permute-start | bytes 86024 | tf_op jit(solution)/shard_map/ppermute | solution.py:461
  19.4 0.0 collective-permute-start.28
  19.4 0.6 %collective-permute-start.27 = (f32[56,128]{1,0:T(8,128)S(1)}, f32[56,128]{1,0:T(8,128)S(1)}, u32[]{:S(2)}, u32[]{:S(2)}) collective-permute-start(f32[56,128]{1,0:T(8,128)S(1)} %maximum_add_fusion.3.refs_6_), channel_id=1, source_target_pairs={{0,10},{1,11},{2,8},{3,9},{4,14},{5,15},{6,12},{7,13},{8,2},{9,3},... | collective-permute-start | bytes 86024 | tf_op jit(solution)/shard_map/ppermute | solution.py:461
  20.0 0.2 shard_map.168.refs_13_
  20.2 0.9 %collective-permute-done.29.refs_9_ = f32[56,128]{1,0:T(8,128)S(1)} collective-permute-done((f32[56,128]{1,0:T(8,128)S(1)}, f32[56,128]{1,0:T(8,128)S(1)}, u32[]{:S(2)}, u32[]{:S(2)}) %collective-permute-start.29) | collective-permute-done | bytes 28704 | tf_op jit(solution)/shard_map/ppermute | solution.py:461
  21.1 2.5 %collective-permute-done.28.refs_8_ = f32[56,128]{1,0:T(8,128)S(1)} collective-permute-done((f32[56,128]{1,0:T(8,128)S(1)}, f32[56,128]{1,0:T(8,128)S(1)}, u32[]{:S(2)}, u32[]{:S(2)}) %collective-permute-start.28) | collective-permute-done | bytes 28704 | tf_op jit(solution)/shard_map/ppermute | solution.py:461
  23.6 0.0 collective-permute-done.27.refs_7_
  23.6 0.8 %shard_map.169 = (f32[17,64,128]{2,1,0:T(8,128)S(1)}, f32[17,64,128]{2,1,0:T(8,128)S(1)}, f32[72,640]{1,0:T(8,128)S(1)}, f32[64,256]{1,0:T(8,128)S(1)}, f32[64,256]{1,0:T(8,128)S(1)}, /*index=5*/f32[88,128]{1,0:T(8,128)S(1)}) custom-call(f32[18,64,128]{2,1,0:T(8,128)S(1)} %get-tuple-element.107.refs_0_, ...), custom_call_target="tpu_custom_call" | custom-call | tf_op jit(solution)/shard_map/pallas_call | solution.py:436
  24.4 0.4 collective-permute-start.30
  24.8 0.9 %collective-permute-done.30 = f32[88,128]{1,0:T(8,128)S(1)} collective-permute-done((f32[88,128]{1,0:T(8,128)S(1)}, f32[88,128]{1,0:T(8,128)S(1)}, u32[]{:S(2)}, u32[]{:S(2)}) %collective-permute-start.30) | collective-permute-done | bytes 45088 | tf_op jit(solution)/shard_map/ppermute | solution.py:461
  25.7 1.4 %collective-permute-start.33 = (f32[3,128]{1,0:T(4,128)S(1)}, f32[3,128]{1,0:T(4,128)S(1)}, u32[]{:S(2)}, u32[]{:S(2)}) collective-permute-start(f32[3,128]{1,0:T(4,128)S(1)} %slice.536), channel_id=1, source_target_pairs={{0,7},{1,6},{2,5},{3,4},{4,3},{5,2},{6,1},{7,0},{8,15},{9,14},{10,... | collective-permute-start | bytes 4616 | tf_op jit(solution)/shard_map/ppermute | solution.py:461
  27.2 0.4 collective-permute-start.31
  27.5 1.5 %collective-permute-start.32 = (f32[67,128]{1,0:T(8,128)S(1)}, f32[67,128]{1,0:T(8,128)S(1)}, u32[]{:S(2)}, u32[]{:S(2)}) collective-permute-start(f32[67,128]{1,0:T(8,128)S(1)} %pad_maximum_fusion.8), channel_id=1, source_target_pairs={{0,3},{1,2},{2,1},{3,0},{4,7},{5,6},{6,5},{7,4},{8,11},{9,10},{10,... | collective-permute-start | bytes 102920 | tf_op jit(solution)/shard_map/ppermute | solution.py:461
  29.1 1.3 %collective-permute-done.31.refs_13_ = f32[24,128]{1,0:T(8,128)S(1)} collective-permute-done((f32[24,128]{1,0:T(8,128)S(1)}, f32[24,128]{1,0:T(8,128)S(1)}, u32[]{:S(2)}, u32[]{:S(2)}) %collective-permute-start.31) | collective-permute-done | bytes 12320 | tf_op jit(solution)/shard_map/ppermute | solution.py:461
  30.4 0.6 %collective-permute-done.32 = f32[67,128]{1,0:T(8,128)S(1)} collective-permute-done((f32[67,128]{1,0:T(8,128)S(1)}, f32[67,128]{1,0:T(8,128)S(1)}, u32[]{:S(2)}, u32[]{:S(2)}) %collective-permute-start.32) | collective-permute-done | bytes 34336 | tf_op jit(solution)/shard_map/ppermute | solution.py:461
  31.0 1.7 %collective-permute-start.36 = (f32[24,128]{1,0:T(8,128)S(1)}, f32[24,128]{1,0:T(8,128)S(1)}, u32[]{:S(2)}, u32[]{:S(2)}) collective-permute-start(f32[24,128]{1,0:T(8,128)S(1)} %maximum_add_fusion.4.refs_8_), channel_id=1, source_target_pairs={{0,26},{1,27},{2,24},{3,25},{4,30},{5,31},{6,28},{7,29},{8,18},{9,... | collective-permute-start | bytes 36872 | tf_op jit(solution)/shard_map/ppermute | solution.py:461
  32.7 0.2 collective-permute-start.35
  33.0 2.1 %collective-permute-start.34 = (f32[24,128]{1,0:T(8,128)S(1)}, f32[24,128]{1,0:T(8,128)S(1)}, u32[]{:S(2)}, u32[]{:S(2)}) collective-permute-start(f32[24,128]{1,0:T(8,128)S(1)} %maximum_add_fusion.4.refs_8_), channel_id=1, source_target_pairs={{0,10},{1,11},{2,8},{3,9},{4,14},{5,15},{6,12},{7,13},{8,2},{9,3},... | collective-permute-start | bytes 36872 | tf_op jit(solution)/shard_map/ppermute | solution.py:461
  35.1 0.2 shard_map.170.refs_15_
  35.4 0.6 %collective-permute-done.36.refs_11_ = f32[24,128]{1,0:T(8,128)S(1)} collective-permute-done((f32[24,128]{1,0:T(8,128)S(1)}, f32[24,128]{1,0:T(8,128)S(1)}, u32[]{:S(2)}, u32[]{:S(2)}) %collective-permute-start.36) | collective-permute-done | bytes 12320 | tf_op jit(solution)/shard_map/ppermute | solution.py:461
  36.0 0.8 %collective-permute-done.35.refs_10_ = f32[24,128]{1,0:T(8,128)S(1)} collective-permute-done((f32[24,128]{1,0:T(8,128)S(1)}, f32[24,128]{1,0:T(8,128)S(1)}, u32[]{:S(2)}, u32[]{:S(2)}) %collective-permute-start.35) | collective-permute-done | bytes 12320 | tf_op jit(solution)/shard_map/ppermute | solution.py:461
  36.8 0.0 collective-permute-done.34.refs_9_
  36.8 0.7 %shard_map.171 = (f32[17,64,128]{2,1,0:T(8,128)S(1)}, f32[17,64,128]{2,1,0:T(8,128)S(1)}, f32[72,640]{1,0:T(8,128)S(1)}, f32[64,256]{1,0:T(8,128)S(1)}, f32[64,256]{1,0:T(8,128)S(1)}, /*index=5*/f32[88,128]{1,0:T(8,128)S(1)}) custom-call(f32[18,64,128]{2,1,0:T(8,128)S(1)} %get-tuple-element.107.refs_0_, ...), custom_call_target="tpu_custom_call" | custom-call | tf_op jit(solution)/shard_map/pallas_call | solution.py:436
  37.5 0.5 collective-permute-start.37
  38.0 0.9 %collective-permute-done.37 = f32[88,128]{1,0:T(8,128)S(1)} collective-permute-done((f32[88,128]{1,0:T(8,128)S(1)}, f32[88,128]{1,0:T(8,128)S(1)}, u32[]{:S(2)}, u32[]{:S(2)}) %collective-permute-start.37) | collective-permute-done | bytes 45088 | tf_op jit(solution)/shard_map/ppermute | solution.py:461
  38.8 2.5 %collective-permute-start.40 = (f32[3,128]{1,0:T(4,128)S(1)}, f32[3,128]{1,0:T(4,128)S(1)}, u32[]{:S(2)}, u32[]{:S(2)}) collective-permute-start(f32[3,128]{1,0:T(4,128)S(1)} %slice.549), channel_id=1, source_target_pairs={{0,7},{1,6},{2,5},{3,4},{4,3},{5,2},{6,1},{7,0},{8,15},{9,14},{10,... | collective-permute-start | bytes 4616 | tf_op jit(solution)/shard_map/ppermute | solution.py:461
  41.3 0.4 collective-permute-start.38
  41.7 0.5 collective-permute-start.39
  42.2 2.3 %collective-permute-done.38.refs_13_ = f32[24,128]{1,0:T(8,128)S(1)} collective-permute-done((f32[24,128]{1,0:T(8,128)S(1)}, f32[24,128]{1,0:T(8,128)S(1)}, u32[]{:S(2)}, u32[]{:S(2)}) %collective-permute-start.38) | collective-permute-done | bytes 12320 | tf_op jit(solution)/shard_map/ppermute | solution.py:461
  44.6 0.6 %collective-permute-done.39 = f32[67,128]{1,0:T(8,128)S(1)} collective-permute-done((f32[67,128]{1,0:T(8,128)S(1)}, f32[67,128]{1,0:T(8,128)S(1)}, u32[]{:S(2)}, u32[]{:S(2)}) %collective-permute-start.39) | collective-permute-done | bytes 34336 | tf_op jit(solution)/shard_map/ppermute | solution.py:461
  45.2 2.0 %collective-permute-start.43 = (f32[24,128]{1,0:T(8,128)S(1)}, f32[24,128]{1,0:T(8,128)S(1)}, u32[]{:S(2)}, u32[]{:S(2)}) collective-permute-start(f32[24,128]{1,0:T(8,128)S(1)} %maximum_add_fusion.5.refs_8_), channel_id=1, source_target_pairs={{0,26},{1,27},{2,24},{3,25},{4,30},{5,31},{6,28},{7,29},{8,18},{9,... | collective-permute-start | bytes 36872 | tf_op jit(solution)/shard_map/ppermute | solution.py:461
  47.2 0.7 %collective-permute-start.42 = (f32[24,128]{1,0:T(8,128)S(1)}, f32[24,128]{1,0:T(8,128)S(1)}, u32[]{:S(2)}, u32[]{:S(2)}) collective-permute-start(f32[24,128]{1,0:T(8,128)S(1)} %maximum_add_fusion.5.refs_8_), channel_id=1, source_target_pairs={{0,18},{1,19},{2,16},{3,17},{4,22},{5,23},{6,20},{7,21},{8,26},{9,... | collective-permute-start | bytes 36872 | tf_op jit(solution)/shard_map/ppermute | solution.py:461
  47.9 1.4 %collective-permute-start.41 = (f32[24,128]{1,0:T(8,128)S(1)}, f32[24,128]{1,0:T(8,128)S(1)}, u32[]{:S(2)}, u32[]{:S(2)}) collective-permute-start(f32[24,128]{1,0:T(8,128)S(1)} %maximum_add_fusion.5.refs_8_), channel_id=1, source_target_pairs={{0,10},{1,11},{2,8},{3,9},{4,14},{5,15},{6,12},{7,13},{8,2},{9,3},... | collective-permute-start | bytes 36872 | tf_op jit(solution)/shard_map/ppermute | solution.py:461
  49.3 0.2 shard_map.172.refs_15_
  49.6 0.6 %collective-permute-done.43.refs_11_ = f32[24,128]{1,0:T(8,128)S(1)} collective-permute-done((f32[24,128]{1,0:T(8,128)S(1)}, f32[24,128]{1,0:T(8,128)S(1)}, u32[]{:S(2)}, u32[]{:S(2)}) %collective-permute-start.43) | collective-permute-done | bytes 12320 | tf_op jit(solution)/shard_map/ppermute | solution.py:461
  50.2 1.1 %collective-permute-done.42.refs_10_ = f32[24,128]{1,0:T(8,128)S(1)} collective-permute-done((f32[24,128]{1,0:T(8,128)S(1)}, f32[24,128]{1,0:T(8,128)S(1)}, u32[]{:S(2)}, u32[]{:S(2)}) %collective-permute-start.42) | collective-permute-done | bytes 12320 | tf_op jit(solution)/shard_map/ppermute | solution.py:461
  51.2 1.3 %shard_map.173 = (f32[1024,128]{1,0:T(8,128)}, f32[1,128]{1,0:T(1,128)S(1)}, f32[64,128]{1,0:T(8,128)S(1)}, f32[64,256]{1,0:T(8,128)S(1)}, f32[1,128]{1,0:T(1,128)S(1)}, /*index=5*/f32[104,128]{1,0:T(8,128)S(1)}) custom-call(f32[18,64,128]{2,1,0:T(8,128)S(1)} %get-tuple-element.107.refs_0_, bf16[128,512]{1,0:T(8,128)(2,1)S(1)} %get-tuple-element.108.maps_local.refs_1_, ...), custom_call_target="tpu_custom_call" | custom-call | tf_op jit(solution)/shard_map/pallas_call | solution.py:436
  52.6 0.0 copy-start.14
  52.6 0.0 copy-start.12
  52.6 0.0 copy-start.13
  52.6 0.5 copy-done.14
  53.1 0.1 copy-done.12
  53.2 0.0 copy-done.13
  (68 shorter events, 0.3 us)
Async XLA Ops:
  0.6 4.6 %copy-start.11 = (s32[256]{0:T(256)S(1)}, s32[256]{0:T(256)}, u32[]{:S(2)}) copy-start(s32[256]{0:T(256)} %param.30) | copy-start | bytes 3076
  2.1 5.6 %collective-permute-start.22 = (f32[72,128]{1,0:T(8,128)}, f32[72,128]{1,0:T(8,128)S(1)}, u32[]{:S(2)}, u32[]{:S(2)}) collective-permute-start(f32[72,128]{1,0:T(8,128)} %shard_map.166), channel_id=1, source_target_pairs={{0,1},{1,0},{2,3},{3,2},{4,5},{5,4},{6,7},{7,6},{8,9},{9,8},{10,11... | collective-permute-start | bytes 110600 | tf_op jit(solution)/shard_map/ppermute | solution.py:461
  5.1 0.7 %copy-start.10 = (s32[2,256]{1,0:T(2,128)S(1)}, s32[2,256]{1,0:T(2,128)}, u32[]{:S(2)}) copy-start(s32[2,256]{1,0:T(2,128)} %refs_6_.1) | copy-start | bytes 6148
  5.1 0.8 %copy-start.8 = (f32[64,128]{1,0:T(8,128)S(1)}, f32[64,128]{1,0:T(8,128)}, u32[]{:S(2)}) copy-start(f32[64,128]{1,0:T(8,128)} %refs_2_.2) | copy-start | bytes 98308
  5.1 0.8 %copy-start.7 = (f32[64,128]{1,0:T(8,128)S(1)}, f32[64,128]{1,0:T(8,128)}, u32[]{:S(2)}) copy-start(f32[64,128]{1,0:T(8,128)} %refs_0_.1) | copy-start | bytes 98308
  5.1 0.8 %copy-start.5 = (f32[1,128]{1,0:T(1,128)S(1)}, f32[1,128]{1,0:T(1,128)}, u32[]{:S(2)}) copy-start(f32[1,128]{1,0:T(1,128)} %refs_4_.1) | copy-start | bytes 1540
  5.1 0.8 %copy-start.3 = (f32[256]{0:T(256)S(1)}, f32[256]{0:T(256)}, u32[]{:S(2)}) copy-start(f32[256]{0:T(256)} %param.32) | copy-start | bytes 3076
  5.1 0.8 %copy-start.4 = (f32[256]{0:T(256)S(1)}, f32[256]{0:T(256)}, u32[]{:S(2)}) copy-start(f32[256]{0:T(256)} %param.31) | copy-start | bytes 3076
  5.2 0.8 %copy-start.1 = (s32[1,2048]{1,0:T(1,128)S(1)}, s32[1,2048]{1,0:T(1,128)}, u32[]{:S(2)}) copy-start(s32[1,2048]{1,0:T(1,128)} %param.24) | copy-start | bytes 24580
  5.2 0.8 %copy-start = (f32[16,128]{1,0:T(8,128)S(1)}, f32[16,128]{1,0:T(8,128)}, u32[]{:S(2)}) copy-start(f32[16,128]{1,0:T(8,128)} %refs_3_.2) | copy-start | bytes 24580
  5.2 0.7 %copy-start.2 = (f32[256]{0:T(256)S(1)}, f32[256]{0:T(256)}, u32[]{:S(2)}) copy-start(f32[256]{0:T(256)} %param.26) | copy-start | bytes 3076
  5.9 1.8 %copy-start.9 = (f32[72,128]{1,0:T(8,128)S(1)}, f32[72,128]{1,0:T(8,128)}, u32[]{:S(2)}) copy-start(f32[72,128]{1,0:T(8,128)} %shard_map.166) | copy-start | bytes 110596
  8.2 1.3 %collective-permute-start.23 = (f32[120,128]{1,0:T(8,128)S(1)}, f32[120,128]{1,0:T(8,128)S(1)}, u32[]{:S(2)}, u32[]{:S(2)}) collective-permute-start(f32[120,128]{1,0:T(8,128)S(1)} %get-tuple-element.116), channel_id=1, source_target_pairs={{0,2},{1,3},{2,0},{3,1},{4,6},{5,7},{6,4},{7,5},{8,10},{9,11},{10,... | collective-permute-start | bytes 184328 | tf_op jit(solution)/shard_map/ppermute | solution.py:461
  9.5 5.8 %collective-permute-start.26 = (f32[3,128]{1,0:T(4,128)S(1)}, f32[3,128]{1,0:T(4,128)S(1)}, u32[]{:S(2)}, u32[]{:S(2)}) collective-permute-start(f32[3,128]{1,0:T(4,128)S(1)} %slice.523), channel_id=1, source_target_pairs={{0,7},{1,6},{2,5},{3,4},{4,3},{5,2},{6,1},{7,0},{8,15},{9,14},{10,... | collective-permute-start | bytes 4616 | tf_op jit(solution)/shard_map/ppermute | solution.py:461
  11.9 3.4 %collective-permute-start.24 = (f32[56,128]{1,0:T(8,128)S(1)}, f32[56,128]{1,0:T(8,128)S(1)}, u32[]{:S(2)}, u32[]{:S(2)}) collective-permute-start(f32[56,128]{1,0:T(8,128)S(1)} %pad_maximum_fusion.10), channel_id=1, source_target_pairs={{0,6},{1,7},{2,4},{3,5},{4,2},{5,3},{6,0},{7,1},{8,14},{9,15},{10,... | collective-permute-start | bytes 86024 | tf_op jit(solution)/shard_map/ppermute | solution.py:461
  12.4 3.5 %collective-permute-start.25 = (f32[67,128]{1,0:T(8,128)S(1)}, f32[67,128]{1,0:T(8,128)S(1)}, u32[]{:S(2)}, u32[]{:S(2)}) collective-permute-start(f32[67,128]{1,0:T(8,128)S(1)} %pad_maximum_fusion.7), channel_id=1, source_target_pairs={{0,3},{1,2},{2,1},{3,0},{4,7},{5,6},{6,5},{7,4},{8,11},{9,10},{10,... | collective-permute-start | bytes 102920 | tf_op jit(solution)/shard_map/ppermute | solution.py:461
  16.0 5.2 %collective-permute-start.29 = (f32[56,128]{1,0:T(8,128)S(1)}, f32[56,128]{1,0:T(8,128)S(1)}, u32[]{:S(2)}, u32[]{:S(2)}) collective-permute-start(f32[56,128]{1,0:T(8,128)S(1)} %maximum_add_fusion.3.refs_6_), channel_id=1, source_target_pairs={{0,26},{1,27},{2,24},{3,25},{4,30},{5,31},{6,28},{7,29},{8,18},{9,... | collective-permute-start | bytes 86024 | tf_op jit(solution)/shard_map/ppermute | solution.py:461
  19.4 4.2 %collective-permute-start.28 = (f32[56,128]{1,0:T(8,128)S(1)}, f32[56,128]{1,0:T(8,128)S(1)}, u32[]{:S(2)}, u32[]{:S(2)}) collective-permute-start(f32[56,128]{1,0:T(8,128)S(1)} %maximum_add_fusion.3.refs_6_), channel_id=1, source_target_pairs={{0,18},{1,19},{2,16},{3,17},{4,22},{5,23},{6,20},{7,21},{8,26},{9,... | collective-permute-start | bytes 86024 | tf_op jit(solution)/shard_map/ppermute | solution.py:461
  19.4 4.2 %collective-permute-start.27 = (f32[56,128]{1,0:T(8,128)S(1)}, f32[56,128]{1,0:T(8,128)S(1)}, u32[]{:S(2)}, u32[]{:S(2)}) collective-permute-start(f32[56,128]{1,0:T(8,128)S(1)} %maximum_add_fusion.3.refs_6_), channel_id=1, source_target_pairs={{0,10},{1,11},{2,8},{3,9},{4,14},{5,15},{6,12},{7,13},{8,2},{9,3},... | collective-permute-start | bytes 86024 | tf_op jit(solution)/shard_map/ppermute | solution.py:461
  24.4 1.3 %collective-permute-start.30 = (f32[88,128]{1,0:T(8,128)S(1)}, f32[88,128]{1,0:T(8,128)S(1)}, u32[]{:S(2)}, u32[]{:S(2)}) collective-permute-start(f32[88,128]{1,0:T(8,128)S(1)} %get-tuple-element.122), channel_id=1, source_target_pairs={{0,2},{1,3},{2,0},{3,1},{4,6},{5,7},{6,4},{7,5},{8,10},{9,11},{10,... | collective-permute-start | bytes 135176 | tf_op jit(solution)/shard_map/ppermute | solution.py:461
  25.7 4.7 %collective-permute-start.33 = (f32[3,128]{1,0:T(4,128)S(1)}, f32[3,128]{1,0:T(4,128)S(1)}, u32[]{:S(2)}, u32[]{:S(2)}) collective-permute-start(f32[3,128]{1,0:T(4,128)S(1)} %slice.536), channel_id=1, source_target_pairs={{0,7},{1,6},{2,5},{3,4},{4,3},{5,2},{6,1},{7,0},{8,15},{9,14},{10,... | collective-permute-start | bytes 4616 | tf_op jit(solution)/shard_map/ppermute | solution.py:461
  27.2 3.2 %collective-permute-start.31 = (f32[24,128]{1,0:T(8,128)S(1)}, f32[24,128]{1,0:T(8,128)S(1)}, u32[]{:S(2)}, u32[]{:S(2)}) collective-permute-start(f32[24,128]{1,0:T(8,128)S(1)} %pad_maximum_fusion.11), channel_id=1, source_target_pairs={{0,6},{1,7},{2,4},{3,5},{4,2},{5,3},{6,0},{7,1},{8,14},{9,15},{10,... | collective-permute-start | bytes 36872 | tf_op jit(solution)/shard_map/ppermute | solution.py:461
  27.5 3.4 %collective-permute-start.32 = (f32[67,128]{1,0:T(8,128)S(1)}, f32[67,128]{1,0:T(8,128)S(1)}, u32[]{:S(2)}, u32[]{:S(2)}) collective-permute-start(f32[67,128]{1,0:T(8,128)S(1)} %pad_maximum_fusion.8), channel_id=1, source_target_pairs={{0,3},{1,2},{2,1},{3,0},{4,7},{5,6},{6,5},{7,4},{8,11},{9,10},{10,... | collective-permute-start | bytes 102920 | tf_op jit(solution)/shard_map/ppermute | solution.py:461
  31.0 5.0 %collective-permute-start.36 = (f32[24,128]{1,0:T(8,128)S(1)}, f32[24,128]{1,0:T(8,128)S(1)}, u32[]{:S(2)}, u32[]{:S(2)}) collective-permute-start(f32[24,128]{1,0:T(8,128)S(1)} %maximum_add_fusion.4.refs_8_), channel_id=1, source_target_pairs={{0,26},{1,27},{2,24},{3,25},{4,30},{5,31},{6,28},{7,29},{8,18},{9,... | collective-permute-start | bytes 36872 | tf_op jit(solution)/shard_map/ppermute | solution.py:461
  32.7 4.0 %collective-permute-start.35 = (f32[24,128]{1,0:T(8,128)S(1)}, f32[24,128]{1,0:T(8,128)S(1)}, u32[]{:S(2)}, u32[]{:S(2)}) collective-permute-start(f32[24,128]{1,0:T(8,128)S(1)} %maximum_add_fusion.4.refs_8_), channel_id=1, source_target_pairs={{0,18},{1,19},{2,16},{3,17},{4,22},{5,23},{6,20},{7,21},{8,26},{9,... | collective-permute-start | bytes 36872 | tf_op jit(solution)/shard_map/ppermute | solution.py:461
  33.0 3.8 %collective-permute-start.34 = (f32[24,128]{1,0:T(8,128)S(1)}, f32[24,128]{1,0:T(8,128)S(1)}, u32[]{:S(2)}, u32[]{:S(2)}) collective-permute-start(f32[24,128]{1,0:T(8,128)S(1)} %maximum_add_fusion.4.refs_8_), channel_id=1, source_target_pairs={{0,10},{1,11},{2,8},{3,9},{4,14},{5,15},{6,12},{7,13},{8,2},{9,3},... | collective-permute-start | bytes 36872 | tf_op jit(solution)/shard_map/ppermute | solution.py:461
  37.5 1.4 %collective-permute-start.37 = (f32[88,128]{1,0:T(8,128)S(1)}, f32[88,128]{1,0:T(8,128)S(1)}, u32[]{:S(2)}, u32[]{:S(2)}) collective-permute-start(f32[88,128]{1,0:T(8,128)S(1)} %get-tuple-element.128), channel_id=1, source_target_pairs={{0,2},{1,3},{2,0},{3,1},{4,6},{5,7},{6,4},{7,5},{8,10},{9,11},{10,... | collective-permute-start | bytes 135176 | tf_op jit(solution)/shard_map/ppermute | solution.py:461
  38.8 5.7 %collective-permute-start.40 = (f32[3,128]{1,0:T(4,128)S(1)}, f32[3,128]{1,0:T(4,128)S(1)}, u32[]{:S(2)}, u32[]{:S(2)}) collective-permute-start(f32[3,128]{1,0:T(4,128)S(1)} %slice.549), channel_id=1, source_target_pairs={{0,7},{1,6},{2,5},{3,4},{4,3},{5,2},{6,1},{7,0},{8,15},{9,14},{10,... | collective-permute-start | bytes 4616 | tf_op jit(solution)/shard_map/ppermute | solution.py:461
  41.3 3.2 %collective-permute-start.38 = (f32[24,128]{1,0:T(8,128)S(1)}, f32[24,128]{1,0:T(8,128)S(1)}, u32[]{:S(2)}, u32[]{:S(2)}) collective-permute-start(f32[24,128]{1,0:T(8,128)S(1)} %pad_maximum_fusion.12), channel_id=1, source_target_pairs={{0,6},{1,7},{2,4},{3,5},{4,2},{5,3},{6,0},{7,1},{8,14},{9,15},{10,... | collective-permute-start | bytes 36872 | tf_op jit(solution)/shard_map/ppermute | solution.py:461
  41.7 3.4 %collective-permute-start.39 = (f32[67,128]{1,0:T(8,128)S(1)}, f32[67,128]{1,0:T(8,128)S(1)}, u32[]{:S(2)}, u32[]{:S(2)}) collective-permute-start(f32[67,128]{1,0:T(8,128)S(1)} %pad_maximum_fusion.9), channel_id=1, source_target_pairs={{0,3},{1,2},{2,1},{3,0},{4,7},{5,6},{6,5},{7,4},{8,11},{9,10},{10,... | collective-permute-start | bytes 102920 | tf_op jit(solution)/shard_map/ppermute | solution.py:461
  45.2 5.0 %collective-permute-start.43 = (f32[24,128]{1,0:T(8,128)S(1)}, f32[24,128]{1,0:T(8,128)S(1)}, u32[]{:S(2)}, u32[]{:S(2)}) collective-permute-start(f32[24,128]{1,0:T(8,128)S(1)} %maximum_add_fusion.5.refs_8_), channel_id=1, source_target_pairs={{0,26},{1,27},{2,24},{3,25},{4,30},{5,31},{6,28},{7,29},{8,18},{9,... | collective-permute-start | bytes 36872 | tf_op jit(solution)/shard_map/ppermute | solution.py:461
  47.2 4.0 %collective-permute-start.42 = (f32[24,128]{1,0:T(8,128)S(1)}, f32[24,128]{1,0:T(8,128)S(1)}, u32[]{:S(2)}, u32[]{:S(2)}) collective-permute-start(f32[24,128]{1,0:T(8,128)S(1)} %maximum_add_fusion.5.refs_8_), channel_id=1, source_target_pairs={{0,18},{1,19},{2,16},{3,17},{4,22},{5,23},{6,20},{7,21},{8,26},{9,... | collective-permute-start | bytes 36872 | tf_op jit(solution)/shard_map/ppermute | solution.py:461
  47.9 3.4 %collective-permute-start.41 = (f32[24,128]{1,0:T(8,128)S(1)}, f32[24,128]{1,0:T(8,128)S(1)}, u32[]{:S(2)}, u32[]{:S(2)}) collective-permute-start(f32[24,128]{1,0:T(8,128)S(1)} %maximum_add_fusion.5.refs_8_), channel_id=1, source_target_pairs={{0,10},{1,11},{2,8},{3,9},{4,14},{5,15},{6,12},{7,13},{8,2},{9,3},... | collective-permute-start | bytes 36872 | tf_op jit(solution)/shard_map/ppermute | solution.py:461
  51.2 1.3 %copy-start.6 = (f32[64,16,128]{2,1,0:T(8,128)S(1)}, f32[64,16,128]{2,1,0:T(8,128)}, u32[]{:S(2)}) copy-start(f32[64,16,128]{2,1,0:T(8,128)} %param.20) | copy-start | bytes 1572868
  52.6 0.5 copy-start.14
  52.6 0.6 %copy-start.12 = (f32[64,256]{1,0:T(8,128)}, f32[64,256]{1,0:T(8,128)S(1)}, u32[]{:S(2)}) copy-start(f32[64,256]{1,0:T(8,128)S(1)} %get-tuple-element.137) | copy-start | bytes 196612
  52.6 0.6 %copy-start.13 = (f32[64,128]{1,0:T(8,128)}, f32[64,128]{1,0:T(8,128)S(1)}, u32[]{:S(2)}) copy-start(f32[64,128]{1,0:T(8,128)S(1)} %get-tuple-element.136) | copy-start | bytes 98308

commit v20 on v19

--- a/solution.py
+++ b/solution.py
@@ -12,6 +12,7 @@
 EPSILON = 1e-06
 LANES = 128
 VMEM_BYTES = 24 * 1024 * 1024
+PARTS = 4
 SQUARES = 3
 
 
@@ -77,6 +78,15 @@
 def write_lanes(ref, start, row):
     for i in range(row.shape[1] // LANES):
         ref[start + i : start + i + 1, :] = row[:, i * LANES : (i + 1) * LANES]
+
+
+def part_copies(source, target, sems):
+    rows = source.shape[0] // PARTS
+    spans = [pl.ds(part * rows, rows) for part in range(PARTS)]
+    return [
+        pltpu.make_async_copy(source.at[span], target.at[span], sems.at[part])
+        for part, span in enumerate(spans)
+    ]
 
 
 def read_lanes(ref, start, length):
@@ -99,7 +109,7 @@
     )
 
 
-def first_kernel(sizes, sources, block_ref, ends_ref, limit_ref, pairs_ref, sems):
+def first_kernel(sizes, sources, block_ref, ends_ref, limit_ref, pairs_ref, info_ref, sems):
     rows = sizes.rows
     targets = (block_ref.at[pl.ds(0, rows)], ends_ref, limit_ref, pairs_ref)
     copies = [
@@ -121,21 +131,26 @@
     bound = jnp.where(slot % width < in_use, limit_ref[...], 0.0)
     start = (ends_ref[0:1, :] + own * nodes).astype(jnp.float32)
     end = (ends_ref[1:2, :] + pair * nodes).astype(jnp.float32)
-    block_ref[rows:, :] = jnp.zeros((block_ref.shape[0] - rows, LANES), jnp.float32)
+    info_ref[...] = jnp.zeros(info_ref.shape, jnp.float32)
     width = min(slots, LANES)
     for chunk in range(slots // width):
-        at = rows + 8 * chunk
         for i, row in enumerate((start, end, bound)):
-            block_ref[at + i : at + i + 1, :width] = row[:, chunk * width : (chunk + 1) * width]
+            at = 8 * chunk + i
+            info_ref[at : at + 1, :width] = row[:, chunk * width : (chunk + 1) * width]
+    target = block_ref.at[pl.ds(rows, info_ref.shape[0])]
+    copy = pltpu.make_async_copy(info_ref, target, sems.at[len(copies)])
+    copy.start()
     copies[0].wait()
+    copy.wait()
 
 
 def start_kernel(sizes, names_in, names_out, *refs):
     given = Bag(**dict(zip(names_in, refs[: len(names_in)])))
     gives = Bag(**dict(zip(names_out, refs[len(names_in) : -2])))
-    availability, sem = refs[-2:]
-    copy = pltpu.make_async_copy(given.availability, availability, sem)
-    copy.start()
+    availability, sems = refs[-2:]
+    copies = part_copies(given.availability, availability, sems)
+    for copy in copies:
+        copy.start()
     rows, techs, nodes, lines = sizes.rows, sizes.techs, sizes.nodes, sizes.lines
     at = places(sizes)
     fixed = gives.available.at[techs + 1]
@@ -160,7 +175,8 @@
     dual_row = fold_lanes(row_sum(store_new * store_new))
     balance = dot3(2.0 * flows, maps, True) - given.demand[...]
     gen_cost = given.gen_cost[...]
-    copy.wait()
+    for copy in copies:
+        copy.wait()
     acc = jnp.zeros((rows, nodes), jnp.float32)
     weights = jnp.zeros((techs, nodes), jnp.float32)
     for hour in range(rows):
@@ -282,7 +298,7 @@
     given = Bag(**dict(zip(names_in, refs[: len(names_in)])))
     gives = Bag(**dict(zip(names_out, refs[len(names_in) :])))
     if last:
-        staged, sem = refs[-2:]
+        staged, sems = refs[-2:]
     own = lax.axis_index("region")
     hour_index = lax.axis_index("hours")
     gathered = given.gathered
@@ -318,7 +334,23 @@
     primal_acc = jnp.zeros((rows, nodes), jnp.float32)
     dual_acc = jnp.zeros((rows, nodes), jnp.float32)
     supply = jnp.zeros((rows, nodes), jnp.float32)
-    for tech in range(techs):
+    if last:
+        copies = part_copies(staged, gives.dispatch, sems)
+        count, pieces = rows // PARTS, []
+        for part in range(PARTS):
+            hours = slice(part * count, (part + 1) * count)
+            piece = jnp.zeros((count, nodes), jnp.float32)
+            for tech in range(techs):
+                slope = gen_cost[tech : tech + 1] + prices[hours]
+                dispatch = given.dispatch[tech, hours, :]
+                duals = given.cap_duals[tech, hours, :]
+                dispatch_new = jnp.maximum(dispatch - primal_step * (slope + duals), 0.0)
+                piece = piece + (2.0 * dispatch_new - dispatch)
+                staged[pl.ds(part * count * techs + tech, count, stride=techs), :] = dispatch_new
+            copies[part].start()
+            pieces.append(piece)
+        supply = jnp.concatenate(pieces, axis=0)
+    for tech in range(0 if last else techs):
         slope = gen_cost[tech : tech + 1] + prices
         dispatch = given.dispatch[tech]
         avail = given.available[tech]
@@ -329,9 +361,6 @@
         dispatch_new = jnp.maximum(dispatch - primal_step * (slope + duals), 0.0)
         dispatch_bar = 2.0 * dispatch_new - dispatch
         supply = supply + dispatch_bar
-        if last:
-            staged[pl.ds(tech, rows, stride=techs), :] = dispatch_new
-            continue
         gives.dispatch[tech] = dispatch_new
         cap_rows = dispatch_bar - avail * capacity_bar[tech : tech + 1]
         primal_acc = primal_acc + (dispatch_new - dispatch) ** 2
@@ -339,9 +368,6 @@
         dual_acc = dual_acc + (duals_new - duals) ** 2
         gives.cap_duals[tech] = duals_new
         out_sums[tech : tech + 1, :] = row_sum(avail * duals_new)
-    if last:
-        copy = pltpu.make_async_copy(staged, gives.dispatch, sem)
-        copy.start()
 
     maps_local = given.maps_local[...]
 
@@ -401,7 +427,8 @@
             low = local + chunk * LANES
             first = rows + 2 * techs + 8 * chunk
             gives.kept[first : first + 8, :] = given.flows[rows:, low : low + LANES]
-        copy.wait()
+        for copy in copies:
+            copy.wait()
         return
     gives.block[:rows, :] = prices + step_up
     gives.flows[rows:, local:] = given.flows[rows:, local:]
@@ -618,9 +645,11 @@
                 pltpu.VMEM((2, slots), jnp.int32),
                 pltpu.VMEM((1, slots), jnp.float32),
                 pltpu.VMEM((1, regions), jnp.int32),
-                pltpu.SemaphoreType.DMA((4,)),
+                pltpu.VMEM((8 * max(1, slots // LANES), nodes), jnp.float32),
+                pltpu.SemaphoreType.DMA((5,)),
             ],
             limit=None,
+            copied=1,
         ).block
     )
     state = call(
@@ -649,7 +678,10 @@
         ),
         flops=10**6,
         left=(0,),
-        scratch=[pltpu.VMEM((rows * techs, nodes), jnp.float32), pltpu.SemaphoreType.DMA],
+        scratch=[
+            pltpu.VMEM((rows * techs, nodes), jnp.float32),
+            pltpu.SemaphoreType.DMA((PARTS,)),
+        ],
     )
     closed = call(
         lambda names_in, names_out, *refs: close_kernel(sizes, *refs),
@@ -716,7 +748,10 @@
             given,
             outs,
             copied=int(final),
-            scratch=[pltpu.VMEM(outs.dispatch.shape, jnp.float32), pltpu.SemaphoreType.DMA]
+            scratch=[
+                pltpu.VMEM(outs.dispatch.shape, jnp.float32),
+                pltpu.SemaphoreType.DMA((PARTS,)),
+            ]
             if final
             else [],
         )

time: 53.5 us -> 54.1 us (1.011)
  Pallas kernels: 7.02 us -> 7.77 us
    pallas_call x9, Pallas kernels: 7.02 us -> 7.77 us  [call(): pl.pallas_call(functools.partial(kernel, names_in, names_out), out_shape=...]
where the time goes in v20:
time: 54.1 us; the launch traced here: 53.9 us
  starting transfers between devices  26.2 us (48%)
  waiting for transfers between devices  17.2 us (32%)
  Pallas kernels  7.77 us (14%)
  local copies, waits for them, and re-layouts  1.46 us (3%)
  between operations  1.05 us (2%)
    ppermute x22, starting transfers between devices, swap(): return lax.ppermute(value, ('hours', 'region'), pairs)  26.2 us
    ppermute x22, waiting for transfers between devices, swap(): return lax.ppermute(value, ('hours', 'region'), pairs)  17.2 us
    pallas_call x9, Pallas kernels, call(): pl.pallas_call(functools.partial(kernel, names_in, names_out), out_shape=...  7.77 us
    unnamed x30, local copies, waits for them, and re-layouts  1.38 us
  transfers between devices with their start and end apart: 22, of which 15 were waited for; matrix products, arithmetic and copies ran while one was open for 0% of the time, Pallas kernels for 5%

profile of v20, /device:TPU:0, one launch (start us, length us, event | category | flops | bytes accessed | tf_op | source)
XLA Modules:
  0.0 53.9 jit_solution(8427546171757028636)
XLA Ops:
  0.6 2.1 %shard_map.166 = f32[72,128]{1,0:T(8,128)} custom-call(f32[64,128]{1,0:T(8,128)} %refs_0_.1, s32[2,64]{1,0:T(2,128)} %bitcast.120, f32[1,64]{1,0:T(1,128)} %refs_2_.3, s32[1,2]{1,0:T(1,128)} %refs_3_.3), custom_call_target="tpu_custom_call" | custom-call | tf_op jit(solution)/shard_map/pallas_call | solution.py:463
  2.8 3.0 %collective-permute-start.22 = (f32[72,128]{1,0:T(8,128)}, f32[72,128]{1,0:T(8,128)S(1)}, u32[]{:S(2)}, u32[]{:S(2)}) collective-permute-start(f32[72,128]{1,0:T(8,128)} %shard_map.166), channel_id=1, source_target_pairs={{0,1},{1,0},{2,3},{3,2},{4,5},{5,4},{6,7},{7,6},{8,9},{9,8},{10,11... | collective-permute-start | bytes 110600 | tf_op jit(solution)/shard_map/ppermute | solution.py:488
  5.8 0.0 copy-start.3
  5.8 0.0 copy-start.4
  5.9 0.0 copy-start.1
  5.9 0.0 copy-start
  5.9 0.0 copy-start.2
  5.9 0.6 %copy-done.10 = s32[2,256]{1,0:T(2,128)S(1)} copy-done((s32[2,256]{1,0:T(2,128)S(1)}, s32[2,256]{1,0:T(2,128)}, u32[]{:S(2)}) %copy-start.10) | copy-done | bytes 2072
  6.5 0.1 copy-done.8
  6.6 0.0 copy-done.7
  6.6 0.0 copy-done
  6.7 1.8 %shard_map.165 = (f32[18,64,128]{2,1,0:T(8,128)S(1)}, bf16[128,512]{1,0:T(8,128)(2,1)S(1)}, f32[64,512]{1,0:T(8,128)S(1)}, f32[64,256]{1,0:T(8,128)S(1)}, f32[17...) custom-call(f32[1024,128]{1,0:T(8,128)} %bitcast.86, f32[64,128]{1,0:T(8,128)S(1)} %copy-done.7, ...), custom_call_target="tpu_custom_call" | custom-call | flops 1000000 | bytes 4000000 | tf_op jit(solution)/shard_map/pallas_call | solution.py:463
  8.5 0.0 collective-permute-done.22
  8.5 0.4 shard_map.167
  9.0 0.1 collective-permute-start.23
  9.1 1.2 %collective-permute-done.23 = f32[120,128]{1,0:T(8,128)S(1)} collective-permute-done((f32[120,128]{1,0:T(8,128)S(1)}, f32[120,128]{1,0:T(8,128)S(1)}, u32[]{:S(2)}, u32[]{:S(2)}) %collective-permute-start.23) | collective-permute-done | bytes 61472 | tf_op jit(solution)/shard_map/ppermute | solution.py:488
  10.3 2.2 %collective-permute-start.26 = (f32[3,128]{1,0:T(4,128)S(1)}, f32[3,128]{1,0:T(4,128)S(1)}, u32[]{:S(2)}, u32[]{:S(2)}) collective-permute-start(f32[3,128]{1,0:T(4,128)S(1)} %slice.523), channel_id=1, source_target_pairs={{0,7},{1,6},{2,5},{3,4},{4,3},{5,2},{6,1},{7,0},{8,15},{9,14},{10,... | collective-permute-start | bytes 4616 | tf_op jit(solution)/shard_map/ppermute | solution.py:488
  12.6 0.6 %collective-permute-start.24 = (f32[56,128]{1,0:T(8,128)S(1)}, f32[56,128]{1,0:T(8,128)S(1)}, u32[]{:S(2)}, u32[]{:S(2)}) collective-permute-start(f32[56,128]{1,0:T(8,128)S(1)} %pad_maximum_fusion.10), channel_id=1, source_target_pairs={{0,6},{1,7},{2,4},{3,5},{4,2},{5,3},{6,0},{7,1},{8,14},{9,15},{10,... | collective-permute-start | bytes 86024 | tf_op jit(solution)/shard_map/ppermute | solution.py:488
  13.1 0.4 collective-permute-start.25
  13.5 2.4 %collective-permute-done.24.refs_11_ = f32[56,128]{1,0:T(8,128)S(1)} collective-permute-done((f32[56,128]{1,0:T(8,128)S(1)}, f32[56,128]{1,0:T(8,128)S(1)}, u32[]{:S(2)}, u32[]{:S(2)}) %collective-permute-start.24) | collective-permute-done | bytes 28704 | tf_op jit(solution)/shard_map/ppermute | solution.py:488
  16.0 0.6 %collective-permute-done.25 = f32[67,128]{1,0:T(8,128)S(1)} collective-permute-done((f32[67,128]{1,0:T(8,128)S(1)}, f32[67,128]{1,0:T(8,128)S(1)}, u32[]{:S(2)}, u32[]{:S(2)}) %collective-permute-start.25) | collective-permute-done | bytes 34336 | tf_op jit(solution)/shard_map/ppermute | solution.py:488
  16.7 3.4 %collective-permute-start.29 = (f32[56,128]{1,0:T(8,128)S(1)}, f32[56,128]{1,0:T(8,128)S(1)}, u32[]{:S(2)}, u32[]{:S(2)}) collective-permute-start(f32[56,128]{1,0:T(8,128)S(1)} %maximum_add_fusion.3.refs_6_), channel_id=1, source_target_pairs={{0,26},{1,27},{2,24},{3,25},{4,30},{5,31},{6,28},{7,29},{8,18},{9,... | collective-permute-start | bytes 86024 | tf_op jit(solution)/shard_map/ppermute | solution.py:488
  20.1 0.6 %collective-permute-start.27 = (f32[56,128]{1,0:T(8,128)S(1)}, f32[56,128]{1,0:T(8,128)S(1)}, u32[]{:S(2)}, u32[]{:S(2)}) collective-permute-start(f32[56,128]{1,0:T(8,128)S(1)} %maximum_add_fusion.3.refs_6_), channel_id=1, source_target_pairs={{0,10},{1,11},{2,8},{3,9},{4,14},{5,15},{6,12},{7,13},{8,2},{9,3},... | collective-permute-start | bytes 86024 | tf_op jit(solution)/shard_map/ppermute | solution.py:488
  20.7 0.2 shard_map.168.refs_13_
  20.9 0.9 %collective-permute-done.29.refs_9_ = f32[56,128]{1,0:T(8,128)S(1)} collective-permute-done((f32[56,128]{1,0:T(8,128)S(1)}, f32[56,128]{1,0:T(8,128)S(1)}, u32[]{:S(2)}, u32[]{:S(2)}) %collective-permute-start.29) | collective-permute-done | bytes 28704 | tf_op jit(solution)/shard_map/ppermute | solution.py:488
  21.8 2.5 %collective-permute-done.28.refs_8_ = f32[56,128]{1,0:T(8,128)S(1)} collective-permute-done((f32[56,128]{1,0:T(8,128)S(1)}, f32[56,128]{1,0:T(8,128)S(1)}, u32[]{:S(2)}, u32[]{:S(2)}) %collective-permute-start.28) | collective-permute-done | bytes 28704 | tf_op jit(solution)/shard_map/ppermute | solution.py:488
  24.3 0.8 %shard_map.169 = (f32[17,64,128]{2,1,0:T(8,128)S(1)}, f32[17,64,128]{2,1,0:T(8,128)S(1)}, f32[72,640]{1,0:T(8,128)S(1)}, f32[64,256]{1,0:T(8,128)S(1)}, f32[64,256]{1,0:T(8,128)S(1)}, /*index=5*/f32[88,128]{1,0:T(8,128)S(1)}) custom-call(f32[18,64,128]{2,1,0:T(8,128)S(1)} %get-tuple-element.107.refs_0_, ...), custom_call_target="tpu_custom_call" | custom-call | tf_op jit(solution)/shard_map/pallas_call | solution.py:463
  25.1 0.4 collective-permute-start.30
  25.5 0.9 %collective-permute-done.30 = f32[88,128]{1,0:T(8,128)S(1)} collective-permute-done((f32[88,128]{1,0:T(8,128)S(1)}, f32[88,128]{1,0:T(8,128)S(1)}, u32[]{:S(2)}, u32[]{:S(2)}) %collective-permute-start.30) | collective-permute-done | bytes 45088 | tf_op jit(solution)/shard_map/ppermute | solution.py:488
  26.4 1.5 %collective-permute-start.33 = (f32[3,128]{1,0:T(4,128)S(1)}, f32[3,128]{1,0:T(4,128)S(1)}, u32[]{:S(2)}, u32[]{:S(2)}) collective-permute-start(f32[3,128]{1,0:T(4,128)S(1)} %slice.536), channel_id=1, source_target_pairs={{0,7},{1,6},{2,5},{3,4},{4,3},{5,2},{6,1},{7,0},{8,15},{9,14},{10,... | collective-permute-start | bytes 4616 | tf_op jit(solution)/shard_map/ppermute | solution.py:488
  27.9 0.4 collective-permute-start.31
  28.3 1.5 %collective-permute-start.32 = (f32[67,128]{1,0:T(8,128)S(1)}, f32[67,128]{1,0:T(8,128)S(1)}, u32[]{:S(2)}, u32[]{:S(2)}) collective-permute-start(f32[67,128]{1,0:T(8,128)S(1)} %pad_maximum_fusion.8), channel_id=1, source_target_pairs={{0,3},{1,2},{2,1},{3,0},{4,7},{5,6},{6,5},{7,4},{8,11},{9,10},{10,... | collective-permute-start | bytes 102920 | tf_op jit(solution)/shard_map/ppermute | solution.py:488
  29.8 1.3 %collective-permute-done.31.refs_13_ = f32[24,128]{1,0:T(8,128)S(1)} collective-permute-done((f32[24,128]{1,0:T(8,128)S(1)}, f32[24,128]{1,0:T(8,128)S(1)}, u32[]{:S(2)}, u32[]{:S(2)}) %collective-permute-start.31) | collective-permute-done | bytes 12320 | tf_op jit(solution)/shard_map/ppermute | solution.py:488
  31.1 0.0 collective-permute-done.33
  31.1 0.6 %collective-permute-done.32 = f32[67,128]{1,0:T(8,128)S(1)} collective-permute-done((f32[67,128]{1,0:T(8,128)S(1)}, f32[67,128]{1,0:T(8,128)S(1)}, u32[]{:S(2)}, u32[]{:S(2)}) %collective-permute-start.32) | collective-permute-done | bytes 34336 | tf_op jit(solution)/shard_map/ppermute | solution.py:488
  31.7 1.7 %collective-permute-start.36 = (f32[24,128]{1,0:T(8,128)S(1)}, f32[24,128]{1,0:T(8,128)S(1)}, u32[]{:S(2)}, u32[]{:S(2)}) collective-permute-start(f32[24,128]{1,0:T(8,128)S(1)} %maximum_add_fusion.4.refs_8_), channel_id=1, source_target_pairs={{0,26},{1,27},{2,24},{3,25},{4,30},{5,31},{6,28},{7,29},{8,18},{9,... | collective-permute-start | bytes 36872 | tf_op jit(solution)/shard_map/ppermute | solution.py:488
  33.5 0.2 collective-permute-start.35
  33.7 2.2 %collective-permute-start.34 = (f32[24,128]{1,0:T(8,128)S(1)}, f32[24,128]{1,0:T(8,128)S(1)}, u32[]{:S(2)}, u32[]{:S(2)}) collective-permute-start(f32[24,128]{1,0:T(8,128)S(1)} %maximum_add_fusion.4.refs_8_), channel_id=1, source_target_pairs={{0,10},{1,11},{2,8},{3,9},{4,14},{5,15},{6,12},{7,13},{8,2},{9,3},... | collective-permute-start | bytes 36872 | tf_op jit(solution)/shard_map/ppermute | solution.py:488
  35.9 0.2 shard_map.170.refs_15_
  36.1 0.6 %collective-permute-done.36.refs_11_ = f32[24,128]{1,0:T(8,128)S(1)} collective-permute-done((f32[24,128]{1,0:T(8,128)S(1)}, f32[24,128]{1,0:T(8,128)S(1)}, u32[]{:S(2)}, u32[]{:S(2)}) %collective-permute-start.36) | collective-permute-done | bytes 12320 | tf_op jit(solution)/shard_map/ppermute | solution.py:488
  36.7 0.8 %collective-permute-done.35.refs_10_ = f32[24,128]{1,0:T(8,128)S(1)} collective-permute-done((f32[24,128]{1,0:T(8,128)S(1)}, f32[24,128]{1,0:T(8,128)S(1)}, u32[]{:S(2)}, u32[]{:S(2)}) %collective-permute-start.35) | collective-permute-done | bytes 12320 | tf_op jit(solution)/shard_map/ppermute | solution.py:488
  37.5 0.0 collective-permute-done.34.refs_9_
  37.5 0.7 %shard_map.171 = (f32[17,64,128]{2,1,0:T(8,128)S(1)}, f32[17,64,128]{2,1,0:T(8,128)S(1)}, f32[72,640]{1,0:T(8,128)S(1)}, f32[64,256]{1,0:T(8,128)S(1)}, f32[64,256]{1,0:T(8,128)S(1)}, /*index=5*/f32[88,128]{1,0:T(8,128)S(1)}) custom-call(f32[18,64,128]{2,1,0:T(8,128)S(1)} %get-tuple-element.107.refs_0_, ...), custom_call_target="tpu_custom_call" | custom-call | tf_op jit(solution)/shard_map/pallas_call | solution.py:463
  38.2 0.5 collective-permute-start.37
  38.7 0.9 %collective-permute-done.37 = f32[88,128]{1,0:T(8,128)S(1)} collective-permute-done((f32[88,128]{1,0:T(8,128)S(1)}, f32[88,128]{1,0:T(8,128)S(1)}, u32[]{:S(2)}, u32[]{:S(2)}) %collective-permute-start.37) | collective-permute-done | bytes 45088 | tf_op jit(solution)/shard_map/ppermute | solution.py:488
  39.6 2.4 %collective-permute-start.40 = (f32[3,128]{1,0:T(4,128)S(1)}, f32[3,128]{1,0:T(4,128)S(1)}, u32[]{:S(2)}, u32[]{:S(2)}) collective-permute-start(f32[3,128]{1,0:T(4,128)S(1)} %slice.549), channel_id=1, source_target_pairs={{0,7},{1,6},{2,5},{3,4},{4,3},{5,2},{6,1},{7,0},{8,15},{9,14},{10,... | collective-permute-start | bytes 4616 | tf_op jit(solution)/shard_map/ppermute | solution.py:488
  42.1 0.4 collective-permute-start.38
  42.4 0.5 %collective-permute-start.39 = (f32[67,128]{1,0:T(8,128)S(1)}, f32[67,128]{1,0:T(8,128)S(1)}, u32[]{:S(2)}, u32[]{:S(2)}) collective-permute-start(f32[67,128]{1,0:T(8,128)S(1)} %pad_maximum_fusion.9), channel_id=1, source_target_pairs={{0,3},{1,2},{2,1},{3,0},{4,7},{5,6},{6,5},{7,4},{8,11},{9,10},{10,... | collective-permute-start | bytes 102920 | tf_op jit(solution)/shard_map/ppermute | solution.py:488
  43.0 2.3 %collective-permute-done.38.refs_13_ = f32[24,128]{1,0:T(8,128)S(1)} collective-permute-done((f32[24,128]{1,0:T(8,128)S(1)}, f32[24,128]{1,0:T(8,128)S(1)}, u32[]{:S(2)}, u32[]{:S(2)}) %collective-permute-start.38) | collective-permute-done | bytes 12320 | tf_op jit(solution)/shard_map/ppermute | solution.py:488
  45.3 0.0 collective-permute-done.40
  45.3 0.6 %collective-permute-done.39 = f32[67,128]{1,0:T(8,128)S(1)} collective-permute-done((f32[67,128]{1,0:T(8,128)S(1)}, f32[67,128]{1,0:T(8,128)S(1)}, u32[]{:S(2)}, u32[]{:S(2)}) %collective-permute-start.39) | collective-permute-done | bytes 34336 | tf_op jit(solution)/shard_map/ppermute | solution.py:488
  45.9 2.0 %collective-permute-start.43 = (f32[24,128]{1,0:T(8,128)S(1)}, f32[24,128]{1,0:T(8,128)S(1)}, u32[]{:S(2)}, u32[]{:S(2)}) collective-permute-start(f32[24,128]{1,0:T(8,128)S(1)} %maximum_add_fusion.5.refs_8_), channel_id=1, source_target_pairs={{0,26},{1,27},{2,24},{3,25},{4,30},{5,31},{6,28},{7,29},{8,18},{9,... | collective-permute-start | bytes 36872 | tf_op jit(solution)/shard_map/ppermute | solution.py:488
  47.9 0.7 %collective-permute-start.42 = (f32[24,128]{1,0:T(8,128)S(1)}, f32[24,128]{1,0:T(8,128)S(1)}, u32[]{:S(2)}, u32[]{:S(2)}) collective-permute-start(f32[24,128]{1,0:T(8,128)S(1)} %maximum_add_fusion.5.refs_8_), channel_id=1, source_target_pairs={{0,18},{1,19},{2,16},{3,17},{4,22},{5,23},{6,20},{7,21},{8,26},{9,... | collective-permute-start | bytes 36872 | tf_op jit(solution)/shard_map/ppermute | solution.py:488
  48.6 1.4 %collective-permute-start.41 = (f32[24,128]{1,0:T(8,128)S(1)}, f32[24,128]{1,0:T(8,128)S(1)}, u32[]{:S(2)}, u32[]{:S(2)}) collective-permute-start(f32[24,128]{1,0:T(8,128)S(1)} %maximum_add_fusion.5.refs_8_), channel_id=1, source_target_pairs={{0,10},{1,11},{2,8},{3,9},{4,14},{5,15},{6,12},{7,13},{8,2},{9,3},... | collective-permute-start | bytes 36872 | tf_op jit(solution)/shard_map/ppermute | solution.py:488
  50.0 0.2 shard_map.172.refs_15_
  50.3 0.6 %collective-permute-done.43.refs_11_ = f32[24,128]{1,0:T(8,128)S(1)} collective-permute-done((f32[24,128]{1,0:T(8,128)S(1)}, f32[24,128]{1,0:T(8,128)S(1)}, u32[]{:S(2)}, u32[]{:S(2)}) %collective-permute-start.43) | collective-permute-done | bytes 12320 | tf_op jit(solution)/shard_map/ppermute | solution.py:488
  50.9 1.1 %collective-permute-done.42.refs_10_ = f32[24,128]{1,0:T(8,128)S(1)} collective-permute-done((f32[24,128]{1,0:T(8,128)S(1)}, f32[24,128]{1,0:T(8,128)S(1)}, u32[]{:S(2)}, u32[]{:S(2)}) %collective-permute-start.42) | collective-permute-done | bytes 12320 | tf_op jit(solution)/shard_map/ppermute | solution.py:488
  52.0 1.2 %shard_map.173 = (f32[1024,128]{1,0:T(8,128)}, f32[1,128]{1,0:T(1,128)S(1)}, f32[64,128]{1,0:T(8,128)S(1)}, f32[64,256]{1,0:T(8,128)S(1)}, f32[1,128]{1,0:T(1,128)S(1)}, /*index=5*/f32[104,128]{1,0:T(8,128)S(1)}) custom-call(f32[18,64,128]{2,1,0:T(8,128)S(1)} %get-tuple-element.107.refs_0_, bf16[128,512]{1,0:T(8,128)(2,1)S(1)} %get-tuple-element.108.maps_local.refs_1_, ...), custom_call_target="tpu_custom_call" | custom-call | tf_op jit(solution)/shard_map/pallas_call | solution.py:463
  53.2 0.0 copy-start.14
  53.3 0.0 copy-start.12
  53.3 0.0 copy-start.13
  53.3 0.5 copy-done.14
  53.8 0.1 copy-done.12
  53.9 0.0 copy-done.13
  (68 shorter events, 0.3 us)
Async XLA Ops:
  0.6 5.3 %copy-start.11 = (s32[256]{0:T(256)S(1)}, s32[256]{0:T(256)}, u32[]{:S(2)}) copy-start(s32[256]{0:T(256)} %param.30) | copy-start | bytes 3076
  2.8 5.7 %collective-permute-start.22 = (f32[72,128]{1,0:T(8,128)}, f32[72,128]{1,0:T(8,128)S(1)}, u32[]{:S(2)}, u32[]{:S(2)}) collective-permute-start(f32[72,128]{1,0:T(8,128)} %shard_map.166), channel_id=1, source_target_pairs={{0,1},{1,0},{2,3},{3,2},{4,5},{5,4},{6,7},{7,6},{8,9},{9,8},{10,11... | collective-permute-start | bytes 110600 | tf_op jit(solution)/shard_map/ppermute | solution.py:488
  5.8 0.7 %copy-start.10 = (s32[2,256]{1,0:T(2,128)S(1)}, s32[2,256]{1,0:T(2,128)}, u32[]{:S(2)}) copy-start(s32[2,256]{1,0:T(2,128)} %refs_6_.1) | copy-start | bytes 6148
  5.8 0.8 %copy-start.8 = (f32[64,128]{1,0:T(8,128)S(1)}, f32[64,128]{1,0:T(8,128)}, u32[]{:S(2)}) copy-start(f32[64,128]{1,0:T(8,128)} %refs_2_.2) | copy-start | bytes 98308
  5.8 0.8 %copy-start.7 = (f32[64,128]{1,0:T(8,128)S(1)}, f32[64,128]{1,0:T(8,128)}, u32[]{:S(2)}) copy-start(f32[64,128]{1,0:T(8,128)} %refs_0_.1) | copy-start | bytes 98308
  5.8 0.8 %copy-start.5 = (f32[1,128]{1,0:T(1,128)S(1)}, f32[1,128]{1,0:T(1,128)}, u32[]{:S(2)}) copy-start(f32[1,128]{1,0:T(1,128)} %refs_4_.1) | copy-start | bytes 1540
  5.8 0.8 %copy-start.3 = (f32[256]{0:T(256)S(1)}, f32[256]{0:T(256)}, u32[]{:S(2)}) copy-start(f32[256]{0:T(256)} %param.32) | copy-start | bytes 3076
  5.8 0.8 %copy-start.4 = (f32[256]{0:T(256)S(1)}, f32[256]{0:T(256)}, u32[]{:S(2)}) copy-start(f32[256]{0:T(256)} %param.31) | copy-start | bytes 3076
  5.9 0.8 %copy-start.1 = (s32[1,2048]{1,0:T(1,128)S(1)}, s32[1,2048]{1,0:T(1,128)}, u32[]{:S(2)}) copy-start(s32[1,2048]{1,0:T(1,128)} %param.24) | copy-start | bytes 24580
  5.9 0.8 %copy-start = (f32[16,128]{1,0:T(8,128)S(1)}, f32[16,128]{1,0:T(8,128)}, u32[]{:S(2)}) copy-start(f32[16,128]{1,0:T(8,128)} %refs_3_.2) | copy-start | bytes 24580
  5.9 0.7 %copy-start.2 = (f32[256]{0:T(256)S(1)}, f32[256]{0:T(256)}, u32[]{:S(2)}) copy-start(f32[256]{0:T(256)} %param.26) | copy-start | bytes 3076
  6.6 1.8 %copy-start.9 = (f32[72,128]{1,0:T(8,128)S(1)}, f32[72,128]{1,0:T(8,128)}, u32[]{:S(2)}) copy-start(f32[72,128]{1,0:T(8,128)} %shard_map.166) | copy-start | bytes 110596
  9.0 1.3 %collective-permute-start.23 = (f32[120,128]{1,0:T(8,128)S(1)}, f32[120,128]{1,0:T(8,128)S(1)}, u32[]{:S(2)}, u32[]{:S(2)}) collective-permute-start(f32[120,128]{1,0:T(8,128)S(1)} %get-tuple-element.116), channel_id=1, source_target_pairs={{0,2},{1,3},{2,0},{3,1},{4,6},{5,7},{6,4},{7,5},{8,10},{9,11},{10,... | collective-permute-start | bytes 184328 | tf_op jit(solution)/shard_map/ppermute | solution.py:488
  10.3 5.7 %collective-permute-start.26 = (f32[3,128]{1,0:T(4,128)S(1)}, f32[3,128]{1,0:T(4,128)S(1)}, u32[]{:S(2)}, u32[]{:S(2)}) collective-permute-start(f32[3,128]{1,0:T(4,128)S(1)} %slice.523), channel_id=1, source_target_pairs={{0,7},{1,6},{2,5},{3,4},{4,3},{5,2},{6,1},{7,0},{8,15},{9,14},{10,... | collective-permute-start | bytes 4616 | tf_op jit(solution)/shard_map/ppermute | solution.py:488
  12.6 3.4 %collective-permute-start.24 = (f32[56,128]{1,0:T(8,128)S(1)}, f32[56,128]{1,0:T(8,128)S(1)}, u32[]{:S(2)}, u32[]{:S(2)}) collective-permute-start(f32[56,128]{1,0:T(8,128)S(1)} %pad_maximum_fusion.10), channel_id=1, source_target_pairs={{0,6},{1,7},{2,4},{3,5},{4,2},{5,3},{6,0},{7,1},{8,14},{9,15},{10,... | collective-permute-start | bytes 86024 | tf_op jit(solution)/shard_map/ppermute | solution.py:488
  13.1 3.5 %collective-permute-start.25 = (f32[67,128]{1,0:T(8,128)S(1)}, f32[67,128]{1,0:T(8,128)S(1)}, u32[]{:S(2)}, u32[]{:S(2)}) collective-permute-start(f32[67,128]{1,0:T(8,128)S(1)} %pad_maximum_fusion.7), channel_id=1, source_target_pairs={{0,3},{1,2},{2,1},{3,0},{4,7},{5,6},{6,5},{7,4},{8,11},{9,10},{10,... | collective-permute-start | bytes 102920 | tf_op jit(solution)/shard_map/ppermute | solution.py:488
  16.7 5.2 %collective-permute-start.29 = (f32[56,128]{1,0:T(8,128)S(1)}, f32[56,128]{1,0:T(8,128)S(1)}, u32[]{:S(2)}, u32[]{:S(2)}) collective-permute-start(f32[56,128]{1,0:T(8,128)S(1)} %maximum_add_fusion.3.refs_6_), channel_id=1, source_target_pairs={{0,26},{1,27},{2,24},{3,25},{4,30},{5,31},{6,28},{7,29},{8,18},{9,... | collective-permute-start | bytes 86024 | tf_op jit(solution)/shard_map/ppermute | solution.py:488
  20.1 4.2 %collective-permute-start.28 = (f32[56,128]{1,0:T(8,128)S(1)}, f32[56,128]{1,0:T(8,128)S(1)}, u32[]{:S(2)}, u32[]{:S(2)}) collective-permute-start(f32[56,128]{1,0:T(8,128)S(1)} %maximum_add_fusion.3.refs_6_), channel_id=1, source_target_pairs={{0,18},{1,19},{2,16},{3,17},{4,22},{5,23},{6,20},{7,21},{8,26},{9,... | collective-permute-start | bytes 86024 | tf_op jit(solution)/shard_map/ppermute | solution.py:488
  20.1 4.2 %collective-permute-start.27 = (f32[56,128]{1,0:T(8,128)S(1)}, f32[56,128]{1,0:T(8,128)S(1)}, u32[]{:S(2)}, u32[]{:S(2)}) collective-permute-start(f32[56,128]{1,0:T(8,128)S(1)} %maximum_add_fusion.3.refs_6_), channel_id=1, source_target_pairs={{0,10},{1,11},{2,8},{3,9},{4,14},{5,15},{6,12},{7,13},{8,2},{9,3},... | collective-permute-start | bytes 86024 | tf_op jit(solution)/shard_map/ppermute | solution.py:488
  25.1 1.3 %collective-permute-start.30 = (f32[88,128]{1,0:T(8,128)S(1)}, f32[88,128]{1,0:T(8,128)S(1)}, u32[]{:S(2)}, u32[]{:S(2)}) collective-permute-start(f32[88,128]{1,0:T(8,128)S(1)} %get-tuple-element.122), channel_id=1, source_target_pairs={{0,2},{1,3},{2,0},{3,1},{4,6},{5,7},{6,4},{7,5},{8,10},{9,11},{10,... | collective-permute-start | bytes 135176 | tf_op jit(solution)/shard_map/ppermute | solution.py:488
  26.4 4.7 %collective-permute-start.33 = (f32[3,128]{1,0:T(4,128)S(1)}, f32[3,128]{1,0:T(4,128)S(1)}, u32[]{:S(2)}, u32[]{:S(2)}) collective-permute-start(f32[3,128]{1,0:T(4,128)S(1)} %slice.536), channel_id=1, source_target_pairs={{0,7},{1,6},{2,5},{3,4},{4,3},{5,2},{6,1},{7,0},{8,15},{9,14},{10,... | collective-permute-start | bytes 4616 | tf_op jit(solution)/shard_map/ppermute | solution.py:488
  27.9 3.2 %collective-permute-start.31 = (f32[24,128]{1,0:T(8,128)S(1)}, f32[24,128]{1,0:T(8,128)S(1)}, u32[]{:S(2)}, u32[]{:S(2)}) collective-permute-start(f32[24,128]{1,0:T(8,128)S(1)} %pad_maximum_fusion.11), channel_id=1, source_target_pairs={{0,6},{1,7},{2,4},{3,5},{4,2},{5,3},{6,0},{7,1},{8,14},{9,15},{10,... | collective-permute-start | bytes 36872 | tf_op jit(solution)/shard_map/ppermute | solution.py:488
  28.3 3.4 %collective-permute-start.32 = (f32[67,128]{1,0:T(8,128)S(1)}, f32[67,128]{1,0:T(8,128)S(1)}, u32[]{:S(2)}, u32[]{:S(2)}) collective-permute-start(f32[67,128]{1,0:T(8,128)S(1)} %pad_maximum_fusion.8), channel_id=1, source_target_pairs={{0,3},{1,2},{2,1},{3,0},{4,7},{5,6},{6,5},{7,4},{8,11},{9,10},{10,... | collective-permute-start | bytes 102920 | tf_op jit(solution)/shard_map/ppermute | solution.py:488
  31.7 5.0 %collective-permute-start.36 = (f32[24,128]{1,0:T(8,128)S(1)}, f32[24,128]{1,0:T(8,128)S(1)}, u32[]{:S(2)}, u32[]{:S(2)}) collective-permute-start(f32[24,128]{1,0:T(8,128)S(1)} %maximum_add_fusion.4.refs_8_), channel_id=1, source_target_pairs={{0,26},{1,27},{2,24},{3,25},{4,30},{5,31},{6,28},{7,29},{8,18},{9,... | collective-permute-start | bytes 36872 | tf_op jit(solution)/shard_map/ppermute | solution.py:488
  33.5 4.0 %collective-permute-start.35 = (f32[24,128]{1,0:T(8,128)S(1)}, f32[24,128]{1,0:T(8,128)S(1)}, u32[]{:S(2)}, u32[]{:S(2)}) collective-permute-start(f32[24,128]{1,0:T(8,128)S(1)} %maximum_add_fusion.4.refs_8_), channel_id=1, source_target_pairs={{0,18},{1,19},{2,16},{3,17},{4,22},{5,23},{6,20},{7,21},{8,26},{9,... | collective-permute-start | bytes 36872 | tf_op jit(solution)/shard_map/ppermute | solution.py:488
  33.7 3.8 %collective-permute-start.34 = (f32[24,128]{1,0:T(8,128)S(1)}, f32[24,128]{1,0:T(8,128)S(1)}, u32[]{:S(2)}, u32[]{:S(2)}) collective-permute-start(f32[24,128]{1,0:T(8,128)S(1)} %maximum_add_fusion.4.refs_8_), channel_id=1, source_target_pairs={{0,10},{1,11},{2,8},{3,9},{4,14},{5,15},{6,12},{7,13},{8,2},{9,3},... | collective-permute-start | bytes 36872 | tf_op jit(solution)/shard_map/ppermute | solution.py:488
  38.2 1.4 %collective-permute-start.37 = (f32[88,128]{1,0:T(8,128)S(1)}, f32[88,128]{1,0:T(8,128)S(1)}, u32[]{:S(2)}, u32[]{:S(2)}) collective-permute-start(f32[88,128]{1,0:T(8,128)S(1)} %get-tuple-element.128), channel_id=1, source_target_pairs={{0,2},{1,3},{2,0},{3,1},{4,6},{5,7},{6,4},{7,5},{8,10},{9,11},{10,... | collective-permute-start | bytes 135176 | tf_op jit(solution)/shard_map/ppermute | solution.py:488
  39.6 5.7 %collective-permute-start.40 = (f32[3,128]{1,0:T(4,128)S(1)}, f32[3,128]{1,0:T(4,128)S(1)}, u32[]{:S(2)}, u32[]{:S(2)}) collective-permute-start(f32[3,128]{1,0:T(4,128)S(1)} %slice.549), channel_id=1, source_target_pairs={{0,7},{1,6},{2,5},{3,4},{4,3},{5,2},{6,1},{7,0},{8,15},{9,14},{10,... | collective-permute-start | bytes 4616 | tf_op jit(solution)/shard_map/ppermute | solution.py:488
  42.1 3.2 %collective-permute-start.38 = (f32[24,128]{1,0:T(8,128)S(1)}, f32[24,128]{1,0:T(8,128)S(1)}, u32[]{:S(2)}, u32[]{:S(2)}) collective-permute-start(f32[24,128]{1,0:T(8,128)S(1)} %pad_maximum_fusion.12), channel_id=1, source_target_pairs={{0,6},{1,7},{2,4},{3,5},{4,2},{5,3},{6,0},{7,1},{8,14},{9,15},{10,... | collective-permute-start | bytes 36872 | tf_op jit(solution)/shard_map/ppermute | solution.py:488
  42.4 3.4 %collective-permute-start.39 = (f32[67,128]{1,0:T(8,128)S(1)}, f32[67,128]{1,0:T(8,128)S(1)}, u32[]{:S(2)}, u32[]{:S(2)}) collective-permute-start(f32[67,128]{1,0:T(8,128)S(1)} %pad_maximum_fusion.9), channel_id=1, source_target_pairs={{0,3},{1,2},{2,1},{3,0},{4,7},{5,6},{6,5},{7,4},{8,11},{9,10},{10,... | collective-permute-start | bytes 102920 | tf_op jit(solution)/shard_map/ppermute | solution.py:488
  45.9 5.0 %collective-permute-start.43 = (f32[24,128]{1,0:T(8,128)S(1)}, f32[24,128]{1,0:T(8,128)S(1)}, u32[]{:S(2)}, u32[]{:S(2)}) collective-permute-start(f32[24,128]{1,0:T(8,128)S(1)} %maximum_add_fusion.5.refs_8_), channel_id=1, source_target_pairs={{0,26},{1,27},{2,24},{3,25},{4,30},{5,31},{6,28},{7,29},{8,18},{9,... | collective-permute-start | bytes 36872 | tf_op jit(solution)/shard_map/ppermute | solution.py:488
  47.9 4.0 %collective-permute-start.42 = (f32[24,128]{1,0:T(8,128)S(1)}, f32[24,128]{1,0:T(8,128)S(1)}, u32[]{:S(2)}, u32[]{:S(2)}) collective-permute-start(f32[24,128]{1,0:T(8,128)S(1)} %maximum_add_fusion.5.refs_8_), channel_id=1, source_target_pairs={{0,18},{1,19},{2,16},{3,17},{4,22},{5,23},{6,20},{7,21},{8,26},{9,... | collective-permute-start | bytes 36872 | tf_op jit(solution)/shard_map/ppermute | solution.py:488
  48.6 3.4 %collective-permute-start.41 = (f32[24,128]{1,0:T(8,128)S(1)}, f32[24,128]{1,0:T(8,128)S(1)}, u32[]{:S(2)}, u32[]{:S(2)}) collective-permute-start(f32[24,128]{1,0:T(8,128)S(1)} %maximum_add_fusion.5.refs_8_), channel_id=1, source_target_pairs={{0,10},{1,11},{2,8},{3,9},{4,14},{5,15},{6,12},{7,13},{8,2},{9,3},... | collective-permute-start | bytes 36872 | tf_op jit(solution)/shard_map/ppermute | solution.py:488
  51.9 1.3 %copy-start.6 = (f32[64,16,128]{2,1,0:T(8,128)S(1)}, f32[64,16,128]{2,1,0:T(8,128)}, u32[]{:S(2)}) copy-start(f32[64,16,128]{2,1,0:T(8,128)} %param.20) | copy-start | bytes 1572868
  53.2 0.5 copy-start.14
  53.3 0.6 %copy-start.12 = (f32[64,256]{1,0:T(8,128)}, f32[64,256]{1,0:T(8,128)S(1)}, u32[]{:S(2)}) copy-start(f32[64,256]{1,0:T(8,128)S(1)} %get-tuple-element.137) | copy-start | bytes 196612
  53.3 0.6 %copy-start.13 = (f32[64,128]{1,0:T(8,128)}, f32[64,128]{1,0:T(8,128)S(1)}, u32[]{:S(2)}) copy-start(f32[64,128]{1,0:T(8,128)S(1)} %get-tuple-element.136) | copy-start | bytes 98308

commit v21 on v20

--- a/solution.py
+++ b/solution.py
@@ -12,6 +12,7 @@
 EPSILON = 1e-06
 LANES = 128
 VMEM_BYTES = 24 * 1024 * 1024
+FIRST_BYTES = 56 * 1024 * 1024
 PARTS = 4
 SQUARES = 3
 
@@ -109,7 +110,7 @@
     )
 
 
-def first_kernel(sizes, sources, block_ref, ends_ref, limit_ref, pairs_ref, info_ref, sems):
+def first_kernel(sizes, sources, block_ref, ends_ref, limit_ref, pairs_ref, sems):
     rows = sizes.rows
     targets = (block_ref.at[pl.ds(0, rows)], ends_ref, limit_ref, pairs_ref)
     copies = [
@@ -131,26 +132,21 @@
     bound = jnp.where(slot % width < in_use, limit_ref[...], 0.0)
     start = (ends_ref[0:1, :] + own * nodes).astype(jnp.float32)
     end = (ends_ref[1:2, :] + pair * nodes).astype(jnp.float32)
-    info_ref[...] = jnp.zeros(info_ref.shape, jnp.float32)
+    block_ref[rows:, :] = jnp.zeros((block_ref.shape[0] - rows, LANES), jnp.float32)
     width = min(slots, LANES)
     for chunk in range(slots // width):
+        at = rows + 8 * chunk
         for i, row in enumerate((start, end, bound)):
-            at = 8 * chunk + i
-            info_ref[at : at + 1, :width] = row[:, chunk * width : (chunk + 1) * width]
-    target = block_ref.at[pl.ds(rows, info_ref.shape[0])]
-    copy = pltpu.make_async_copy(info_ref, target, sems.at[len(copies)])
-    copy.start()
+            block_ref[at + i : at + i + 1, :width] = row[:, chunk * width : (chunk + 1) * width]
     copies[0].wait()
-    copy.wait()
 
 
 def start_kernel(sizes, names_in, names_out, *refs):
     given = Bag(**dict(zip(names_in, refs[: len(names_in)])))
     gives = Bag(**dict(zip(names_out, refs[len(names_in) : -2])))
-    availability, sems = refs[-2:]
-    copies = part_copies(given.availability, availability, sems)
-    for copy in copies:
-        copy.start()
+    availability, sem = refs[-2:]
+    copy = pltpu.make_async_copy(given.availability, availability, sem)
+    copy.start()
     rows, techs, nodes, lines = sizes.rows, sizes.techs, sizes.nodes, sizes.lines
     at = places(sizes)
     fixed = gives.available.at[techs + 1]
@@ -175,8 +171,7 @@
     dual_row = fold_lanes(row_sum(store_new * store_new))
     balance = dot3(2.0 * flows, maps, True) - given.demand[...]
     gen_cost = given.gen_cost[...]
-    for copy in copies:
-        copy.wait()
+    copy.wait()
     acc = jnp.zeros((rows, nodes), jnp.float32)
     weights = jnp.zeros((techs, nodes), jnp.float32)
     for hour in range(rows):
@@ -645,11 +640,9 @@
                 pltpu.VMEM((2, slots), jnp.int32),
                 pltpu.VMEM((1, slots), jnp.float32),
                 pltpu.VMEM((1, regions), jnp.int32),
-                pltpu.VMEM((8 * max(1, slots // LANES), nodes), jnp.float32),
-                pltpu.SemaphoreType.DMA((5,)),
+                pltpu.SemaphoreType.DMA((4,)),
             ],
-            limit=None,
-            copied=1,
+            limit=FIRST_BYTES,
         ).block
     )
     state = call(
@@ -678,10 +671,7 @@
         ),
         flops=10**6,
         left=(0,),
-        scratch=[
-            pltpu.VMEM((rows * techs, nodes), jnp.float32),
-            pltpu.SemaphoreType.DMA((PARTS,)),
-        ],
+        scratch=[pltpu.VMEM((rows * techs, nodes), jnp.float32), pltpu.SemaphoreType.DMA],
     )
     closed = call(
         lambda names_in, names_out, *refs: close_kernel(sizes, *refs),

time: 54.1 us -> 53.5 us (0.989)
  Pallas kernels: 7.77 us -> 6.98 us
    pallas_call x9, Pallas kernels: 7.77 us -> 6.98 us  [call(): pl.pallas_call(functools.partial(kernel, names_in, names_out), out_shape=...]
where the time goes in v21:
time: 53.5 us; the launch traced here: 53.2 us
  starting transfers between devices  26.2 us (49%)
  waiting for transfers between devices  17.3 us (32%)
  Pallas kernels  6.98 us (13%)
  local copies, waits for them, and re-layouts  1.46 us (3%)
  between operations  1.05 us (2%)
    ppermute x22, starting transfers between devices, swap(): return lax.ppermute(value, ('hours', 'region'), pairs)  26.2 us
    ppermute x22, waiting for transfers between devices, swap(): return lax.ppermute(value, ('hours', 'region'), pairs)  17.3 us
    pallas_call x9, Pallas kernels, call(): pl.pallas_call(functools.partial(kernel, names_in, names_out), out_shape=...  6.98 us
    unnamed x30, local copies, waits for them, and re-layouts  1.38 us
  transfers between devices with their start and end apart: 22, of which 15 were waited for; matrix products, arithmetic and copies ran while one was open for 0% of the time, Pallas kernels for 5%

profile of v21, /device:TPU:0, one launch (start us, length us, event | category | flops | bytes accessed | tf_op | source)
XLA Modules:
  0.0 53.2 jit_solution(15880329974270390257)
XLA Ops:
  0.6 1.4 %shard_map.166 = f32[72,128]{1,0:T(8,128)} custom-call(f32[64,128]{1,0:T(8,128)} %refs_0_.1, s32[2,64]{1,0:T(2,128)} %bitcast.120, f32[1,64]{1,0:T(1,128)} %refs_2_.3, s32[1,2]{1,0:T(1,128)} %refs_3_.3), custom_call_target="tpu_custom_call" | custom-call | tf_op jit(solution)/shard_map/pallas_call | solution.py:458
  2.1 3.0 %collective-permute-start.22 = (f32[72,128]{1,0:T(8,128)}, f32[72,128]{1,0:T(8,128)S(1)}, u32[]{:S(2)}, u32[]{:S(2)}) collective-permute-start(f32[72,128]{1,0:T(8,128)} %shard_map.166), channel_id=1, source_target_pairs={{0,1},{1,0},{2,3},{3,2},{4,5},{5,4},{6,7},{7,6},{8,9},{9,8},{10,11... | collective-permute-start | bytes 110600 | tf_op jit(solution)/shard_map/ppermute | solution.py:483
  5.1 0.0 copy-start.3
  5.1 0.0 copy-start.4
  5.2 0.0 copy-start.1
  5.2 0.0 copy-start
  5.2 0.0 copy-start.2
  5.2 0.6 %copy-done.10 = s32[2,256]{1,0:T(2,128)S(1)} copy-done((s32[2,256]{1,0:T(2,128)S(1)}, s32[2,256]{1,0:T(2,128)}, u32[]{:S(2)}) %copy-start.10) | copy-done | bytes 2072
  5.8 0.1 copy-done.8
  5.9 0.0 copy-done.7
  5.9 0.0 copy-done
  5.9 1.7 %shard_map.165 = (f32[18,64,128]{2,1,0:T(8,128)S(1)}, bf16[128,512]{1,0:T(8,128)(2,1)S(1)}, f32[64,512]{1,0:T(8,128)S(1)}, f32[64,256]{1,0:T(8,128)S(1)}, f32[17...) custom-call(f32[1024,128]{1,0:T(8,128)} %bitcast.86, f32[64,128]{1,0:T(8,128)S(1)} %copy-done.7, ...), custom_call_target="tpu_custom_call" | custom-call | flops 1000000 | bytes 4000000 | tf_op jit(solution)/shard_map/pallas_call | solution.py:458
  7.7 0.4 shard_map.167
  8.2 0.1 collective-permute-start.23
  8.3 1.2 %collective-permute-done.23 = f32[120,128]{1,0:T(8,128)S(1)} collective-permute-done((f32[120,128]{1,0:T(8,128)S(1)}, f32[120,128]{1,0:T(8,128)S(1)}, u32[]{:S(2)}, u32[]{:S(2)}) %collective-permute-start.23) | collective-permute-done | bytes 61472 | tf_op jit(solution)/shard_map/ppermute | solution.py:483
  9.5 2.3 %collective-permute-start.26 = (f32[3,128]{1,0:T(4,128)S(1)}, f32[3,128]{1,0:T(4,128)S(1)}, u32[]{:S(2)}, u32[]{:S(2)}) collective-permute-start(f32[3,128]{1,0:T(4,128)S(1)} %slice.523), channel_id=1, source_target_pairs={{0,7},{1,6},{2,5},{3,4},{4,3},{5,2},{6,1},{7,0},{8,15},{9,14},{10,... | collective-permute-start | bytes 4616 | tf_op jit(solution)/shard_map/ppermute | solution.py:483
  11.9 0.6 %collective-permute-start.24 = (f32[56,128]{1,0:T(8,128)S(1)}, f32[56,128]{1,0:T(8,128)S(1)}, u32[]{:S(2)}, u32[]{:S(2)}) collective-permute-start(f32[56,128]{1,0:T(8,128)S(1)} %pad_maximum_fusion.10), channel_id=1, source_target_pairs={{0,6},{1,7},{2,4},{3,5},{4,2},{5,3},{6,0},{7,1},{8,14},{9,15},{10,... | collective-permute-start | bytes 86024 | tf_op jit(solution)/shard_map/ppermute | solution.py:483
  12.4 0.3 collective-permute-start.25
  12.7 2.5 %collective-permute-done.24.refs_11_ = f32[56,128]{1,0:T(8,128)S(1)} collective-permute-done((f32[56,128]{1,0:T(8,128)S(1)}, f32[56,128]{1,0:T(8,128)S(1)}, u32[]{:S(2)}, u32[]{:S(2)}) %collective-permute-start.24) | collective-permute-done | bytes 28704 | tf_op jit(solution)/shard_map/ppermute | solution.py:483
  15.3 0.0 collective-permute-done.26
  15.3 0.6 %collective-permute-done.25 = f32[67,128]{1,0:T(8,128)S(1)} collective-permute-done((f32[67,128]{1,0:T(8,128)S(1)}, f32[67,128]{1,0:T(8,128)S(1)}, u32[]{:S(2)}, u32[]{:S(2)}) %collective-permute-start.25) | collective-permute-done | bytes 34336 | tf_op jit(solution)/shard_map/ppermute | solution.py:483
  16.0 3.4 %collective-permute-start.29 = (f32[56,128]{1,0:T(8,128)S(1)}, f32[56,128]{1,0:T(8,128)S(1)}, u32[]{:S(2)}, u32[]{:S(2)}) collective-permute-start(f32[56,128]{1,0:T(8,128)S(1)} %maximum_add_fusion.3.refs_6_), channel_id=1, source_target_pairs={{0,26},{1,27},{2,24},{3,25},{4,30},{5,31},{6,28},{7,29},{8,18},{9,... | collective-permute-start | bytes 86024 | tf_op jit(solution)/shard_map/ppermute | solution.py:483
  19.4 0.0 collective-permute-start.28
  19.4 0.6 %collective-permute-start.27 = (f32[56,128]{1,0:T(8,128)S(1)}, f32[56,128]{1,0:T(8,128)S(1)}, u32[]{:S(2)}, u32[]{:S(2)}) collective-permute-start(f32[56,128]{1,0:T(8,128)S(1)} %maximum_add_fusion.3.refs_6_), channel_id=1, source_target_pairs={{0,10},{1,11},{2,8},{3,9},{4,14},{5,15},{6,12},{7,13},{8,2},{9,3},... | collective-permute-start | bytes 86024 | tf_op jit(solution)/shard_map/ppermute | solution.py:483
  20.0 0.2 shard_map.168.refs_13_
  20.2 0.9 %collective-permute-done.29.refs_9_ = f32[56,128]{1,0:T(8,128)S(1)} collective-permute-done((f32[56,128]{1,0:T(8,128)S(1)}, f32[56,128]{1,0:T(8,128)S(1)}, u32[]{:S(2)}, u32[]{:S(2)}) %collective-permute-start.29) | collective-permute-done | bytes 28704 | tf_op jit(solution)/shard_map/ppermute | solution.py:483
  21.1 2.5 %collective-permute-done.28.refs_8_ = f32[56,128]{1,0:T(8,128)S(1)} collective-permute-done((f32[56,128]{1,0:T(8,128)S(1)}, f32[56,128]{1,0:T(8,128)S(1)}, u32[]{:S(2)}, u32[]{:S(2)}) %collective-permute-start.28) | collective-permute-done | bytes 28704 | tf_op jit(solution)/shard_map/ppermute | solution.py:483
  23.6 0.0 collective-permute-done.27.refs_7_
  23.6 0.8 %shard_map.169 = (f32[17,64,128]{2,1,0:T(8,128)S(1)}, f32[17,64,128]{2,1,0:T(8,128)S(1)}, f32[72,640]{1,0:T(8,128)S(1)}, f32[64,256]{1,0:T(8,128)S(1)}, f32[64,256]{1,0:T(8,128)S(1)}, /*index=5*/f32[88,128]{1,0:T(8,128)S(1)}) custom-call(f32[18,64,128]{2,1,0:T(8,128)S(1)} %get-tuple-element.107.refs_0_, ...), custom_call_target="tpu_custom_call" | custom-call | tf_op jit(solution)/shard_map/pallas_call | solution.py:458
  24.4 0.4 collective-permute-start.30
  24.8 0.9 %collective-permute-done.30 = f32[88,128]{1,0:T(8,128)S(1)} collective-permute-done((f32[88,128]{1,0:T(8,128)S(1)}, f32[88,128]{1,0:T(8,128)S(1)}, u32[]{:S(2)}, u32[]{:S(2)}) %collective-permute-start.30) | collective-permute-done | bytes 45088 | tf_op jit(solution)/shard_map/ppermute | solution.py:483
  25.7 1.4 %collective-permute-start.33 = (f32[3,128]{1,0:T(4,128)S(1)}, f32[3,128]{1,0:T(4,128)S(1)}, u32[]{:S(2)}, u32[]{:S(2)}) collective-permute-start(f32[3,128]{1,0:T(4,128)S(1)} %slice.536), channel_id=1, source_target_pairs={{0,7},{1,6},{2,5},{3,4},{4,3},{5,2},{6,1},{7,0},{8,15},{9,14},{10,... | collective-permute-start | bytes 4616 | tf_op jit(solution)/shard_map/ppermute | solution.py:483
  27.2 0.4 collective-permute-start.31
  27.5 1.5 %collective-permute-start.32 = (f32[67,128]{1,0:T(8,128)S(1)}, f32[67,128]{1,0:T(8,128)S(1)}, u32[]{:S(2)}, u32[]{:S(2)}) collective-permute-start(f32[67,128]{1,0:T(8,128)S(1)} %pad_maximum_fusion.8), channel_id=1, source_target_pairs={{0,3},{1,2},{2,1},{3,0},{4,7},{5,6},{6,5},{7,4},{8,11},{9,10},{10,... | collective-permute-start | bytes 102920 | tf_op jit(solution)/shard_map/ppermute | solution.py:483
  29.1 1.3 %collective-permute-done.31.refs_13_ = f32[24,128]{1,0:T(8,128)S(1)} collective-permute-done((f32[24,128]{1,0:T(8,128)S(1)}, f32[24,128]{1,0:T(8,128)S(1)}, u32[]{:S(2)}, u32[]{:S(2)}) %collective-permute-start.31) | collective-permute-done | bytes 12320 | tf_op jit(solution)/shard_map/ppermute | solution.py:483
  30.4 0.6 %collective-permute-done.32 = f32[67,128]{1,0:T(8,128)S(1)} collective-permute-done((f32[67,128]{1,0:T(8,128)S(1)}, f32[67,128]{1,0:T(8,128)S(1)}, u32[]{:S(2)}, u32[]{:S(2)}) %collective-permute-start.32) | collective-permute-done | bytes 34336 | tf_op jit(solution)/shard_map/ppermute | solution.py:483
  31.0 1.7 %collective-permute-start.36 = (f32[24,128]{1,0:T(8,128)S(1)}, f32[24,128]{1,0:T(8,128)S(1)}, u32[]{:S(2)}, u32[]{:S(2)}) collective-permute-start(f32[24,128]{1,0:T(8,128)S(1)} %maximum_add_fusion.4.refs_8_), channel_id=1, source_target_pairs={{0,26},{1,27},{2,24},{3,25},{4,30},{5,31},{6,28},{7,29},{8,18},{9,... | collective-permute-start | bytes 36872 | tf_op jit(solution)/shard_map/ppermute | solution.py:483
  32.7 0.2 collective-permute-start.35
  33.0 2.1 %collective-permute-start.34 = (f32[24,128]{1,0:T(8,128)S(1)}, f32[24,128]{1,0:T(8,128)S(1)}, u32[]{:S(2)}, u32[]{:S(2)}) collective-permute-start(f32[24,128]{1,0:T(8,128)S(1)} %maximum_add_fusion.4.refs_8_), channel_id=1, source_target_pairs={{0,10},{1,11},{2,8},{3,9},{4,14},{5,15},{6,12},{7,13},{8,2},{9,3},... | collective-permute-start | bytes 36872 | tf_op jit(solution)/shard_map/ppermute | solution.py:483
  35.1 0.2 shard_map.170.refs_15_
  35.4 0.6 %collective-permute-done.36.refs_11_ = f32[24,128]{1,0:T(8,128)S(1)} collective-permute-done((f32[24,128]{1,0:T(8,128)S(1)}, f32[24,128]{1,0:T(8,128)S(1)}, u32[]{:S(2)}, u32[]{:S(2)}) %collective-permute-start.36) | collective-permute-done | bytes 12320 | tf_op jit(solution)/shard_map/ppermute | solution.py:483
  36.0 0.8 %collective-permute-done.35.refs_10_ = f32[24,128]{1,0:T(8,128)S(1)} collective-permute-done((f32[24,128]{1,0:T(8,128)S(1)}, f32[24,128]{1,0:T(8,128)S(1)}, u32[]{:S(2)}, u32[]{:S(2)}) %collective-permute-start.35) | collective-permute-done | bytes 12320 | tf_op jit(solution)/shard_map/ppermute | solution.py:483
  36.8 0.0 collective-permute-done.34.refs_9_
  36.8 0.7 %shard_map.171 = (f32[17,64,128]{2,1,0:T(8,128)S(1)}, f32[17,64,128]{2,1,0:T(8,128)S(1)}, f32[72,640]{1,0:T(8,128)S(1)}, f32[64,256]{1,0:T(8,128)S(1)}, f32[64,256]{1,0:T(8,128)S(1)}, /*index=5*/f32[88,128]{1,0:T(8,128)S(1)}) custom-call(f32[18,64,128]{2,1,0:T(8,128)S(1)} %get-tuple-element.107.refs_0_, ...), custom_call_target="tpu_custom_call" | custom-call | tf_op jit(solution)/shard_map/pallas_call | solution.py:458
  37.5 0.5 collective-permute-start.37
  38.0 0.9 %collective-permute-done.37 = f32[88,128]{1,0:T(8,128)S(1)} collective-permute-done((f32[88,128]{1,0:T(8,128)S(1)}, f32[88,128]{1,0:T(8,128)S(1)}, u32[]{:S(2)}, u32[]{:S(2)}) %collective-permute-start.37) | collective-permute-done | bytes 45088 | tf_op jit(solution)/shard_map/ppermute | solution.py:483
  38.8 2.5 %collective-permute-start.40 = (f32[3,128]{1,0:T(4,128)S(1)}, f32[3,128]{1,0:T(4,128)S(1)}, u32[]{:S(2)}, u32[]{:S(2)}) collective-permute-start(f32[3,128]{1,0:T(4,128)S(1)} %slice.549), channel_id=1, source_target_pairs={{0,7},{1,6},{2,5},{3,4},{4,3},{5,2},{6,1},{7,0},{8,15},{9,14},{10,... | collective-permute-start | bytes 4616 | tf_op jit(solution)/shard_map/ppermute | solution.py:483
  41.3 0.4 collective-permute-start.38
  41.7 0.5 collective-permute-start.39
  42.2 2.3 %collective-permute-done.38.refs_13_ = f32[24,128]{1,0:T(8,128)S(1)} collective-permute-done((f32[24,128]{1,0:T(8,128)S(1)}, f32[24,128]{1,0:T(8,128)S(1)}, u32[]{:S(2)}, u32[]{:S(2)}) %collective-permute-start.38) | collective-permute-done | bytes 12320 | tf_op jit(solution)/shard_map/ppermute | solution.py:483
  44.6 0.6 %collective-permute-done.39 = f32[67,128]{1,0:T(8,128)S(1)} collective-permute-done((f32[67,128]{1,0:T(8,128)S(1)}, f32[67,128]{1,0:T(8,128)S(1)}, u32[]{:S(2)}, u32[]{:S(2)}) %collective-permute-start.39) | collective-permute-done | bytes 34336 | tf_op jit(solution)/shard_map/ppermute | solution.py:483
  45.2 2.0 %collective-permute-start.43 = (f32[24,128]{1,0:T(8,128)S(1)}, f32[24,128]{1,0:T(8,128)S(1)}, u32[]{:S(2)}, u32[]{:S(2)}) collective-permute-start(f32[24,128]{1,0:T(8,128)S(1)} %maximum_add_fusion.5.refs_8_), channel_id=1, source_target_pairs={{0,26},{1,27},{2,24},{3,25},{4,30},{5,31},{6,28},{7,29},{8,18},{9,... | collective-permute-start | bytes 36872 | tf_op jit(solution)/shard_map/ppermute | solution.py:483
  47.2 0.7 %collective-permute-start.42 = (f32[24,128]{1,0:T(8,128)S(1)}, f32[24,128]{1,0:T(8,128)S(1)}, u32[]{:S(2)}, u32[]{:S(2)}) collective-permute-start(f32[24,128]{1,0:T(8,128)S(1)} %maximum_add_fusion.5.refs_8_), channel_id=1, source_target_pairs={{0,18},{1,19},{2,16},{3,17},{4,22},{5,23},{6,20},{7,21},{8,26},{9,... | collective-permute-start | bytes 36872 | tf_op jit(solution)/shard_map/ppermute | solution.py:483
  47.9 1.4 %collective-permute-start.41 = (f32[24,128]{1,0:T(8,128)S(1)}, f32[24,128]{1,0:T(8,128)S(1)}, u32[]{:S(2)}, u32[]{:S(2)}) collective-permute-start(f32[24,128]{1,0:T(8,128)S(1)} %maximum_add_fusion.5.refs_8_), channel_id=1, source_target_pairs={{0,10},{1,11},{2,8},{3,9},{4,14},{5,15},{6,12},{7,13},{8,2},{9,3},... | collective-permute-start | bytes 36872 | tf_op jit(solution)/shard_map/ppermute | solution.py:483
  49.3 0.2 shard_map.172.refs_15_
  49.6 0.6 %collective-permute-done.43.refs_11_ = f32[24,128]{1,0:T(8,128)S(1)} collective-permute-done((f32[24,128]{1,0:T(8,128)S(1)}, f32[24,128]{1,0:T(8,128)S(1)}, u32[]{:S(2)}, u32[]{:S(2)}) %collective-permute-start.43) | collective-permute-done | bytes 12320 | tf_op jit(solution)/shard_map/ppermute | solution.py:483
  50.2 1.1 %collective-permute-done.42.refs_10_ = f32[24,128]{1,0:T(8,128)S(1)} collective-permute-done((f32[24,128]{1,0:T(8,128)S(1)}, f32[24,128]{1,0:T(8,128)S(1)}, u32[]{:S(2)}, u32[]{:S(2)}) %collective-permute-start.42) | collective-permute-done | bytes 12320 | tf_op jit(solution)/shard_map/ppermute | solution.py:483
  51.2 1.2 %shard_map.173 = (f32[1024,128]{1,0:T(8,128)}, f32[1,128]{1,0:T(1,128)S(1)}, f32[64,128]{1,0:T(8,128)S(1)}, f32[64,256]{1,0:T(8,128)S(1)}, f32[1,128]{1,0:T(1,128)S(1)}, /*index=5*/f32[104,128]{1,0:T(8,128)S(1)}) custom-call(f32[18,64,128]{2,1,0:T(8,128)S(1)} %get-tuple-element.107.refs_0_, bf16[128,512]{1,0:T(8,128)(2,1)S(1)} %get-tuple-element.108.maps_local.refs_1_, ...), custom_call_target="tpu_custom_call" | custom-call | tf_op jit(solution)/shard_map/pallas_call | solution.py:458
  52.5 0.0 copy-start.14
  52.5 0.0 copy-start.12
  52.6 0.0 copy-start.13
  52.6 0.5 copy-done.14
  53.0 0.1 copy-done.12
  53.2 0.0 copy-done.13
  (68 shorter events, 0.3 us)
Async XLA Ops:
  0.6 4.6 %copy-start.11 = (s32[256]{0:T(256)S(1)}, s32[256]{0:T(256)}, u32[]{:S(2)}) copy-start(s32[256]{0:T(256)} %param.30) | copy-start | bytes 3076
  2.1 5.6 %collective-permute-start.22 = (f32[72,128]{1,0:T(8,128)}, f32[72,128]{1,0:T(8,128)S(1)}, u32[]{:S(2)}, u32[]{:S(2)}) collective-permute-start(f32[72,128]{1,0:T(8,128)} %shard_map.166), channel_id=1, source_target_pairs={{0,1},{1,0},{2,3},{3,2},{4,5},{5,4},{6,7},{7,6},{8,9},{9,8},{10,11... | collective-permute-start | bytes 110600 | tf_op jit(solution)/shard_map/ppermute | solution.py:483
  5.1 0.7 %copy-start.10 = (s32[2,256]{1,0:T(2,128)S(1)}, s32[2,256]{1,0:T(2,128)}, u32[]{:S(2)}) copy-start(s32[2,256]{1,0:T(2,128)} %refs_6_.1) | copy-start | bytes 6148
  5.1 0.8 %copy-start.8 = (f32[64,128]{1,0:T(8,128)S(1)}, f32[64,128]{1,0:T(8,128)}, u32[]{:S(2)}) copy-start(f32[64,128]{1,0:T(8,128)} %refs_2_.2) | copy-start | bytes 98308
  5.1 0.8 %copy-start.7 = (f32[64,128]{1,0:T(8,128)S(1)}, f32[64,128]{1,0:T(8,128)}, u32[]{:S(2)}) copy-start(f32[64,128]{1,0:T(8,128)} %refs_0_.1) | copy-start | bytes 98308
  5.1 0.8 %copy-start.5 = (f32[1,128]{1,0:T(1,128)S(1)}, f32[1,128]{1,0:T(1,128)}, u32[]{:S(2)}) copy-start(f32[1,128]{1,0:T(1,128)} %refs_4_.1) | copy-start | bytes 1540
  5.1 0.8 %copy-start.3 = (f32[256]{0:T(256)S(1)}, f32[256]{0:T(256)}, u32[]{:S(2)}) copy-start(f32[256]{0:T(256)} %param.32) | copy-start | bytes 3076
  5.1 0.8 %copy-start.4 = (f32[256]{0:T(256)S(1)}, f32[256]{0:T(256)}, u32[]{:S(2)}) copy-start(f32[256]{0:T(256)} %param.31) | copy-start | bytes 3076
  5.2 0.8 %copy-start.1 = (s32[1,2048]{1,0:T(1,128)S(1)}, s32[1,2048]{1,0:T(1,128)}, u32[]{:S(2)}) copy-start(s32[1,2048]{1,0:T(1,128)} %param.24) | copy-start | bytes 24580
  5.2 0.8 %copy-start = (f32[16,128]{1,0:T(8,128)S(1)}, f32[16,128]{1,0:T(8,128)}, u32[]{:S(2)}) copy-start(f32[16,128]{1,0:T(8,128)} %refs_3_.2) | copy-start | bytes 24580
  5.2 0.7 %copy-start.2 = (f32[256]{0:T(256)S(1)}, f32[256]{0:T(256)}, u32[]{:S(2)}) copy-start(f32[256]{0:T(256)} %param.26) | copy-start | bytes 3076
  5.9 1.8 %copy-start.9 = (f32[72,128]{1,0:T(8,128)S(1)}, f32[72,128]{1,0:T(8,128)}, u32[]{:S(2)}) copy-start(f32[72,128]{1,0:T(8,128)} %shard_map.166) | copy-start | bytes 110596
  8.2 1.3 %collective-permute-start.23 = (f32[120,128]{1,0:T(8,128)S(1)}, f32[120,128]{1,0:T(8,128)S(1)}, u32[]{:S(2)}, u32[]{:S(2)}) collective-permute-start(f32[120,128]{1,0:T(8,128)S(1)} %get-tuple-element.116), channel_id=1, source_target_pairs={{0,2},{1,3},{2,0},{3,1},{4,6},{5,7},{6,4},{7,5},{8,10},{9,11},{10,... | collective-permute-start | bytes 184328 | tf_op jit(solution)/shard_map/ppermute | solution.py:483
  9.5 5.8 %collective-permute-start.26 = (f32[3,128]{1,0:T(4,128)S(1)}, f32[3,128]{1,0:T(4,128)S(1)}, u32[]{:S(2)}, u32[]{:S(2)}) collective-permute-start(f32[3,128]{1,0:T(4,128)S(1)} %slice.523), channel_id=1, source_target_pairs={{0,7},{1,6},{2,5},{3,4},{4,3},{5,2},{6,1},{7,0},{8,15},{9,14},{10,... | collective-permute-start | bytes 4616 | tf_op jit(solution)/shard_map/ppermute | solution.py:483
  11.9 3.4 %collective-permute-start.24 = (f32[56,128]{1,0:T(8,128)S(1)}, f32[56,128]{1,0:T(8,128)S(1)}, u32[]{:S(2)}, u32[]{:S(2)}) collective-permute-start(f32[56,128]{1,0:T(8,128)S(1)} %pad_maximum_fusion.10), channel_id=1, source_target_pairs={{0,6},{1,7},{2,4},{3,5},{4,2},{5,3},{6,0},{7,1},{8,14},{9,15},{10,... | collective-permute-start | bytes 86024 | tf_op jit(solution)/shard_map/ppermute | solution.py:483
  12.4 3.5 %collective-permute-start.25 = (f32[67,128]{1,0:T(8,128)S(1)}, f32[67,128]{1,0:T(8,128)S(1)}, u32[]{:S(2)}, u32[]{:S(2)}) collective-permute-start(f32[67,128]{1,0:T(8,128)S(1)} %pad_maximum_fusion.7), channel_id=1, source_target_pairs={{0,3},{1,2},{2,1},{3,0},{4,7},{5,6},{6,5},{7,4},{8,11},{9,10},{10,... | collective-permute-start | bytes 102920 | tf_op jit(solution)/shard_map/ppermute | solution.py:483
  16.0 5.2 %collective-permute-start.29 = (f32[56,128]{1,0:T(8,128)S(1)}, f32[56,128]{1,0:T(8,128)S(1)}, u32[]{:S(2)}, u32[]{:S(2)}) collective-permute-start(f32[56,128]{1,0:T(8,128)S(1)} %maximum_add_fusion.3.refs_6_), channel_id=1, source_target_pairs={{0,26},{1,27},{2,24},{3,25},{4,30},{5,31},{6,28},{7,29},{8,18},{9,... | collective-permute-start | bytes 86024 | tf_op jit(solution)/shard_map/ppermute | solution.py:483
  19.4 4.2 %collective-permute-start.28 = (f32[56,128]{1,0:T(8,128)S(1)}, f32[56,128]{1,0:T(8,128)S(1)}, u32[]{:S(2)}, u32[]{:S(2)}) collective-permute-start(f32[56,128]{1,0:T(8,128)S(1)} %maximum_add_fusion.3.refs_6_), channel_id=1, source_target_pairs={{0,18},{1,19},{2,16},{3,17},{4,22},{5,23},{6,20},{7,21},{8,26},{9,... | collective-permute-start | bytes 86024 | tf_op jit(solution)/shard_map/ppermute | solution.py:483
  19.4 4.2 %collective-permute-start.27 = (f32[56,128]{1,0:T(8,128)S(1)}, f32[56,128]{1,0:T(8,128)S(1)}, u32[]{:S(2)}, u32[]{:S(2)}) collective-permute-start(f32[56,128]{1,0:T(8,128)S(1)} %maximum_add_fusion.3.refs_6_), channel_id=1, source_target_pairs={{0,10},{1,11},{2,8},{3,9},{4,14},{5,15},{6,12},{7,13},{8,2},{9,3},... | collective-permute-start | bytes 86024 | tf_op jit(solution)/shard_map/ppermute | solution.py:483
  24.4 1.3 %collective-permute-start.30 = (f32[88,128]{1,0:T(8,128)S(1)}, f32[88,128]{1,0:T(8,128)S(1)}, u32[]{:S(2)}, u32[]{:S(2)}) collective-permute-start(f32[88,128]{1,0:T(8,128)S(1)} %get-tuple-element.122), channel_id=1, source_target_pairs={{0,2},{1,3},{2,0},{3,1},{4,6},{5,7},{6,4},{7,5},{8,10},{9,11},{10,... | collective-permute-start | bytes 135176 | tf_op jit(solution)/shard_map/ppermute | solution.py:483
  25.7 4.7 %collective-permute-start.33 = (f32[3,128]{1,0:T(4,128)S(1)}, f32[3,128]{1,0:T(4,128)S(1)}, u32[]{:S(2)}, u32[]{:S(2)}) collective-permute-start(f32[3,128]{1,0:T(4,128)S(1)} %slice.536), channel_id=1, source_target_pairs={{0,7},{1,6},{2,5},{3,4},{4,3},{5,2},{6,1},{7,0},{8,15},{9,14},{10,... | collective-permute-start | bytes 4616 | tf_op jit(solution)/shard_map/ppermute | solution.py:483
  27.2 3.2 %collective-permute-start.31 = (f32[24,128]{1,0:T(8,128)S(1)}, f32[24,128]{1,0:T(8,128)S(1)}, u32[]{:S(2)}, u32[]{:S(2)}) collective-permute-start(f32[24,128]{1,0:T(8,128)S(1)} %pad_maximum_fusion.11), channel_id=1, source_target_pairs={{0,6},{1,7},{2,4},{3,5},{4,2},{5,3},{6,0},{7,1},{8,14},{9,15},{10,... | collective-permute-start | bytes 36872 | tf_op jit(solution)/shard_map/ppermute | solution.py:483
  27.5 3.4 %collective-permute-start.32 = (f32[67,128]{1,0:T(8,128)S(1)}, f32[67,128]{1,0:T(8,128)S(1)}, u32[]{:S(2)}, u32[]{:S(2)}) collective-permute-start(f32[67,128]{1,0:T(8,128)S(1)} %pad_maximum_fusion.8), channel_id=1, source_target_pairs={{0,3},{1,2},{2,1},{3,0},{4,7},{5,6},{6,5},{7,4},{8,11},{9,10},{10,... | collective-permute-start | bytes 102920 | tf_op jit(solution)/shard_map/ppermute | solution.py:483
  31.0 5.0 %collective-permute-start.36 = (f32[24,128]{1,0:T(8,128)S(1)}, f32[24,128]{1,0:T(8,128)S(1)}, u32[]{:S(2)}, u32[]{:S(2)}) collective-permute-start(f32[24,128]{1,0:T(8,128)S(1)} %maximum_add_fusion.4.refs_8_), channel_id=1, source_target_pairs={{0,26},{1,27},{2,24},{3,25},{4,30},{5,31},{6,28},{7,29},{8,18},{9,... | collective-permute-start | bytes 36872 | tf_op jit(solution)/shard_map/ppermute | solution.py:483
  32.7 4.0 %collective-permute-start.35 = (f32[24,128]{1,0:T(8,128)S(1)}, f32[24,128]{1,0:T(8,128)S(1)}, u32[]{:S(2)}, u32[]{:S(2)}) collective-permute-start(f32[24,128]{1,0:T(8,128)S(1)} %maximum_add_fusion.4.refs_8_), channel_id=1, source_target_pairs={{0,18},{1,19},{2,16},{3,17},{4,22},{5,23},{6,20},{7,21},{8,26},{9,... | collective-permute-start | bytes 36872 | tf_op jit(solution)/shard_map/ppermute | solution.py:483
  33.0 3.8 %collective-permute-start.34 = (f32[24,128]{1,0:T(8,128)S(1)}, f32[24,128]{1,0:T(8,128)S(1)}, u32[]{:S(2)}, u32[]{:S(2)}) collective-permute-start(f32[24,128]{1,0:T(8,128)S(1)} %maximum_add_fusion.4.refs_8_), channel_id=1, source_target_pairs={{0,10},{1,11},{2,8},{3,9},{4,14},{5,15},{6,12},{7,13},{8,2},{9,3},... | collective-permute-start | bytes 36872 | tf_op jit(solution)/shard_map/ppermute | solution.py:483
  37.5 1.4 %collective-permute-start.37 = (f32[88,128]{1,0:T(8,128)S(1)}, f32[88,128]{1,0:T(8,128)S(1)}, u32[]{:S(2)}, u32[]{:S(2)}) collective-permute-start(f32[88,128]{1,0:T(8,128)S(1)} %get-tuple-element.128), channel_id=1, source_target_pairs={{0,2},{1,3},{2,0},{3,1},{4,6},{5,7},{6,4},{7,5},{8,10},{9,11},{10,... | collective-permute-start | bytes 135176 | tf_op jit(solution)/shard_map/ppermute | solution.py:483
  38.8 5.7 %collective-permute-start.40 = (f32[3,128]{1,0:T(4,128)S(1)}, f32[3,128]{1,0:T(4,128)S(1)}, u32[]{:S(2)}, u32[]{:S(2)}) collective-permute-start(f32[3,128]{1,0:T(4,128)S(1)} %slice.549), channel_id=1, source_target_pairs={{0,7},{1,6},{2,5},{3,4},{4,3},{5,2},{6,1},{7,0},{8,15},{9,14},{10,... | collective-permute-start | bytes 4616 | tf_op jit(solution)/shard_map/ppermute | solution.py:483
  41.3 3.2 %collective-permute-start.38 = (f32[24,128]{1,0:T(8,128)S(1)}, f32[24,128]{1,0:T(8,128)S(1)}, u32[]{:S(2)}, u32[]{:S(2)}) collective-permute-start(f32[24,128]{1,0:T(8,128)S(1)} %pad_maximum_fusion.12), channel_id=1, source_target_pairs={{0,6},{1,7},{2,4},{3,5},{4,2},{5,3},{6,0},{7,1},{8,14},{9,15},{10,... | collective-permute-start | bytes 36872 | tf_op jit(solution)/shard_map/ppermute | solution.py:483
  41.7 3.4 %collective-permute-start.39 = (f32[67,128]{1,0:T(8,128)S(1)}, f32[67,128]{1,0:T(8,128)S(1)}, u32[]{:S(2)}, u32[]{:S(2)}) collective-permute-start(f32[67,128]{1,0:T(8,128)S(1)} %pad_maximum_fusion.9), channel_id=1, source_target_pairs={{0,3},{1,2},{2,1},{3,0},{4,7},{5,6},{6,5},{7,4},{8,11},{9,10},{10,... | collective-permute-start | bytes 102920 | tf_op jit(solution)/shard_map/ppermute | solution.py:483
  45.2 5.0 %collective-permute-start.43 = (f32[24,128]{1,0:T(8,128)S(1)}, f32[24,128]{1,0:T(8,128)S(1)}, u32[]{:S(2)}, u32[]{:S(2)}) collective-permute-start(f32[24,128]{1,0:T(8,128)S(1)} %maximum_add_fusion.5.refs_8_), channel_id=1, source_target_pairs={{0,26},{1,27},{2,24},{3,25},{4,30},{5,31},{6,28},{7,29},{8,18},{9,... | collective-permute-start | bytes 36872 | tf_op jit(solution)/shard_map/ppermute | solution.py:483
  47.2 4.0 %collective-permute-start.42 = (f32[24,128]{1,0:T(8,128)S(1)}, f32[24,128]{1,0:T(8,128)S(1)}, u32[]{:S(2)}, u32[]{:S(2)}) collective-permute-start(f32[24,128]{1,0:T(8,128)S(1)} %maximum_add_fusion.5.refs_8_), channel_id=1, source_target_pairs={{0,18},{1,19},{2,16},{3,17},{4,22},{5,23},{6,20},{7,21},{8,26},{9,... | collective-permute-start | bytes 36872 | tf_op jit(solution)/shard_map/ppermute | solution.py:483
  47.9 3.4 %collective-permute-start.41 = (f32[24,128]{1,0:T(8,128)S(1)}, f32[24,128]{1,0:T(8,128)S(1)}, u32[]{:S(2)}, u32[]{:S(2)}) collective-permute-start(f32[24,128]{1,0:T(8,128)S(1)} %maximum_add_fusion.5.refs_8_), channel_id=1, source_target_pairs={{0,10},{1,11},{2,8},{3,9},{4,14},{5,15},{6,12},{7,13},{8,2},{9,3},... | collective-permute-start | bytes 36872 | tf_op jit(solution)/shard_map/ppermute | solution.py:483
  51.2 1.3 %copy-start.6 = (f32[64,16,128]{2,1,0:T(8,128)S(1)}, f32[64,16,128]{2,1,0:T(8,128)}, u32[]{:S(2)}) copy-start(f32[64,16,128]{2,1,0:T(8,128)} %param.20) | copy-start | bytes 1572868
  52.5 0.5 copy-start.14
  52.5 0.6 %copy-start.12 = (f32[64,256]{1,0:T(8,128)}, f32[64,256]{1,0:T(8,128)S(1)}, u32[]{:S(2)}) copy-start(f32[64,256]{1,0:T(8,128)S(1)} %get-tuple-element.137) | copy-start | bytes 196612
  52.6 0.6 %copy-start.13 = (f32[64,128]{1,0:T(8,128)}, f32[64,128]{1,0:T(8,128)S(1)}, u32[]{:S(2)}) copy-start(f32[64,128]{1,0:T(8,128)S(1)} %get-tuple-element.136) | copy-start | bytes 98308

commit v22 on v21

--- a/solution.py
+++ b/solution.py
@@ -104,6 +104,7 @@
         limits=limits,
         energy=energy,
         owned=energy + span,
+        cost=energy + span + 1,
         weight=sizes.techs,
         before=sizes.techs + 1,
         negative=sizes.techs + 1 + span,
@@ -172,6 +173,11 @@
     balance = dot3(2.0 * flows, maps, True) - given.demand[...]
     gen_cost = given.gen_cost[...]
     copy.wait()
+    cost = given.cap_cost[...]
+    tech_hot, node_hot = owned_one_hots(owned, techs, nodes)
+    own_cost = dot3(jnp.where(tech_hot, cost, 0.0), node_hot, True)
+    fixed[at.cost : at.cost + techs, :] = own_cost
+    gives.dispatch[techs] = jnp.zeros((rows, nodes), jnp.float32)
     acc = jnp.zeros((rows, nodes), jnp.float32)
     weights = jnp.zeros((techs, nodes), jnp.float32)
     for hour in range(rows):
@@ -185,21 +191,16 @@
         balance = balance + dispatch_bar
         duals = jnp.maximum(0.5 * dispatch_bar, 0.0)
         acc = acc + dispatch * dispatch
-        gives.sums[tech : tech + 1, :] = row_sum(avail * duals)
+        gives.sums[tech : tech + 1, :] = own_cost[tech : tech + 1] - row_sum(avail * duals)
     gives.balance[...] = balance
     squares = row_sum(acc)
-    cost = given.cap_cost[...]
     negative = jnp.sum((cost < 0.0).astype(jnp.float32), axis=1, keepdims=True)
     write_halo(sizes, gives.sums, store_new)
     gives.sums[techs : techs + SQUARES, :] = jnp.concatenate(
         [primal_row + squares, dual_row + squares, jnp.broadcast_to(negative, (1, LANES))], axis=0
     )
-    tech_hot, node_hot = owned_one_hots(owned, techs, nodes)
     first = sums_rows(sizes)
     gives.sums[first : first + techs, :] = weights
-    gives.sums[first + techs : first + 2 * techs, :] = dot3(
-        jnp.where(tech_hot, cost, 0.0), node_hot, True
-    )
 
 
 def close_kernel(
@@ -311,16 +312,14 @@
     primal_step = 0.5 / weight
     if second:
         first = sums_rows(sizes)
-        col_weight, cost = sums[first : first + techs], sums[first + techs : first + 2 * techs]
+        col_weight = sums[first : first + techs]
         negative = sums[techs + 2 : techs + 3]
-        capacity = jnp.maximum(-cost / col_weight, 0.0)
-        first_bar = 2.0 * capacity
     else:
         col_weight = given.cap_duals[techs, :techs, :]
-        cost = given.cap_duals[techs, techs : 2 * techs, :]
-        capacity = small[:techs, :]
         negative = small[at.negative : at.negative + 1, :]
-    capacity_new = jnp.maximum(capacity - (cost - sums[:techs]) / (weight * col_weight), 0.0)
+    capacity = small[:techs, :]
+    first_bar = 2.0 * capacity
+    capacity_new = jnp.maximum(capacity - sums[:techs] / (weight * col_weight), 0.0)
     capacity_bar = 2.0 * capacity_new - capacity
 
     prices = gathered[own, :rows, :]
@@ -362,7 +361,8 @@
         duals_new = jnp.maximum(duals + half_weight * cap_rows, 0.0)
         dual_acc = dual_acc + (duals_new - duals) ** 2
         gives.cap_duals[tech] = duals_new
-        out_sums[tech : tech + 1, :] = row_sum(avail * duals_new)
+        cost = fixed[at.cost + tech : at.cost + tech + 1, :]
+        out_sums[tech : tech + 1, :] = cost - row_sum(avail * duals_new)
 
     maps_local = given.maps_local[...]
 
@@ -417,10 +417,9 @@
         gives.negative[...] = negative
         gives.kept[:rows, :] = fixed[...]
         gives.kept[rows : rows + techs, :] = col_weight
-        gives.kept[rows + techs : rows + 2 * techs, :] = cost
         for chunk in range(regions * slots // LANES):
             low = local + chunk * LANES
-            first = rows + 2 * techs + 8 * chunk
+            first = rows + techs + 8 * chunk
             gives.kept[first : first + 8, :] = given.flows[rows:, low : low + LANES]
         for copy in copies:
             copy.wait()
@@ -428,7 +427,6 @@
     gives.block[:rows, :] = prices + step_up
     gives.flows[rows:, local:] = given.flows[rows:, local:]
     gives.cap_duals[techs, :techs, :] = col_weight
-    gives.cap_duals[techs, techs : 2 * techs, :] = cost
     small_new = gives.dispatch.at[techs]
     small_new[:techs, :] = capacity_new
     small_new[at.weight : at.weight + 1, :] = jnp.broadcast_to(weight, (1, LANES))
@@ -548,8 +546,10 @@
     first_hour = lax.axis_index("hours") == 0
     price_start = args.price_start
     available = args.availability.transpose(1, 0, 2)
-    fixed, last = kept[:rows], rows + 2 * techs
-    col_weight, cost = kept[rows : rows + techs], kept[rows + techs : last]
+    fixed, last = kept[:rows], rows + techs
+    col_weight = kept[rows:last]
+    own_cost = fixed[at.cost : at.cost + techs]
+    cost = lax.psum(own_cost, "hours")
     info = kept[last:].reshape(-1, 8, LANES).transpose(1, 0, 2).reshape(8, cross)
     local_limits = fixed[at.limits : at.energy].reshape(1, local)
     cross_limits = info[2:3]
@@ -592,24 +592,25 @@
     )
     dual = jnp.sum(step_up**2) + jnp.sum(duals**2) + jnp.sum(store_duals**2)
     rows_of = [
-        jnp.sum(available * duals, axis=1),
+        own_cost - jnp.sum(available * duals, axis=1),
         jnp.zeros((SQUARES, nodes)).at[0, 0].set(primal).at[1, 0].set(dual),
         store_duals[:1].reshape(-1, LANES),
         store_duals[rows - 1 :].reshape(-1, LANES),
     ]
     used = halo_at(sizes) + 2 * sizes.units // LANES
     rows_of.append(jnp.zeros((sums_rows(sizes) - used, nodes)))
-    rows_of += [jnp.where(first_hour, part, 0.0) for part in (col_weight, cost)]
+    rows_of.append(jnp.where(first_hour, col_weight, 0.0))
     block = jnp.concatenate([price_start + step_up, *rows_of], axis=0)
     gathered, parts = exchange(sizes, block)
     flows = jnp.concatenate([flows_local, flows_cross], axis=1)
+    slab = jnp.pad(capacity, ((0, rows - techs), (0, 0)))
     spare = jnp.concatenate([jnp.zeros((8, local)), info], axis=1)
     state = Bag(
         available=jnp.concatenate([available, args.demand[None], fixed[None]], axis=0),
         maps_local=maps_local_low,
         maps_cross=maps_cross_low,
         store_duals=store_duals,
-        dispatch=jnp.concatenate([dispatch, jnp.zeros((1, rows, nodes))], axis=0),
+        dispatch=jnp.concatenate([dispatch, slab[None]], axis=0),
         flows=jnp.concatenate([flows, spare], axis=0),
     )
     return state, gathered, parts
@@ -667,7 +668,7 @@
             store_duals=shape(rows, units),
             dispatch=shape(techs + 1, rows, nodes),
             balance=shape(rows, nodes),
-            sums=shape(sums_rows(sizes) + 2 * techs, nodes),
+            sums=shape(sums_rows(sizes) + techs, nodes),
         ),
         flops=10**6,
         left=(0,),
@@ -730,7 +731,7 @@
                 prices=shape(rows, nodes),
                 charge=shape(rows, units),
                 negative=shape(1, LANES),
-                kept=shape(rows + 2 * techs + 8 * (sizes.regions * sizes.slots // LANES), LANES),
+                kept=shape(rows + techs + 8 * (sizes.regions * sizes.slots // LANES), LANES),
             )
         final = iteration == ITERS - 1
         results = call(

time: 53.5 us -> 53.4 us (level)
  no operation moved by 1% of the time
where the time goes in v22:
time: 53.4 us; the launch traced here: 53.1 us
  starting transfers between devices  25.8 us (48%)
  waiting for transfers between devices  17.6 us (33%)
  Pallas kernels  6.98 us (13%)
  local copies, waits for them, and re-layouts  1.45 us (3%)
  between operations  1.05 us (2%)
    ppermute x22, starting transfers between devices, swap(): return lax.ppermute(value, ('hours', 'region'), pairs)  25.8 us
    ppermute x22, waiting for transfers between devices, swap(): return lax.ppermute(value, ('hours', 'region'), pairs)  17.6 us
    pallas_call x9, Pallas kernels, call(): pl.pallas_call(functools.partial(kernel, names_in, names_out), out_shape=...  6.98 us
    unnamed x30, local copies, waits for them, and re-layouts  1.38 us
  transfers between devices with their start and end apart: 22, of which 15 were waited for; matrix products, arithmetic and copies ran while one was open for 0% of the time, Pallas kernels for 5%

profile of v22, /device:TPU:0, one launch (start us, length us, event | category | flops | bytes accessed | tf_op | source)
XLA Modules:
  0.0 53.1 jit_solution(15903748795078961419)
XLA Ops:
  0.6 1.4 %shard_map.166 = f32[72,128]{1,0:T(8,128)} custom-call(f32[64,128]{1,0:T(8,128)} %refs_0_.1, s32[2,64]{1,0:T(2,128)} %bitcast.122, f32[1,64]{1,0:T(1,128)} %refs_2_.3, s32[1,2]{1,0:T(1,128)} %refs_3_.3), custom_call_target="tpu_custom_call" | custom-call | tf_op jit(solution)/shard_map/pallas_call | solution.py:456
  2.1 3.0 %collective-permute-start.22 = (f32[72,128]{1,0:T(8,128)}, f32[72,128]{1,0:T(8,128)S(1)}, u32[]{:S(2)}, u32[]{:S(2)}) collective-permute-start(f32[72,128]{1,0:T(8,128)} %shard_map.166), channel_id=1, source_target_pairs={{0,1},{1,0},{2,3},{3,2},{4,5},{5,4},{6,7},{7,6},{8,9},{9,8},{10,11... | collective-permute-start | bytes 110600 | tf_op jit(solution)/shard_map/ppermute | solution.py:481
  5.1 0.0 copy-start.3
  5.1 0.0 copy-start.4
  5.2 0.0 copy-start.1
  5.2 0.0 copy-start
  5.2 0.0 copy-start.2
  5.2 0.6 %copy-done.10 = s32[2,256]{1,0:T(2,128)S(1)} copy-done((s32[2,256]{1,0:T(2,128)S(1)}, s32[2,256]{1,0:T(2,128)}, u32[]{:S(2)}) %copy-start.10) | copy-done | bytes 2072
  5.8 0.1 copy-done.8
  5.9 0.0 copy-done.7
  5.9 0.0 copy-done
  5.9 1.7 %shard_map.165 = (f32[18,64,128]{2,1,0:T(8,128)S(1)}, bf16[128,512]{1,0:T(8,128)(2,1)S(1)}, f32[64,512]{1,0:T(8,128)S(1)}, f32[64,256]{1,0:T(8,128)S(1)}, f32[17...) custom-call(f32[1024,128]{1,0:T(8,128)} %bitcast.88, f32[64,128]{1,0:T(8,128)S(1)} %copy-done.7, ...), custom_call_target="tpu_custom_call" | custom-call | flops 1000000 | bytes 4000000 | tf_op jit(solution)/shard_map/pallas_call | solution.py:456
  7.7 0.0 collective-permute-done.22
  7.7 0.4 shard_map.167
  8.2 0.1 collective-permute-start.23
  8.3 1.2 %collective-permute-done.23 = f32[104,128]{1,0:T(8,128)S(1)} collective-permute-done((f32[104,128]{1,0:T(8,128)S(1)}, f32[104,128]{1,0:T(8,128)S(1)}, u32[]{:S(2)}, u32[]{:S(2)}) %collective-permute-start.23) | collective-permute-done | bytes 53280 | tf_op jit(solution)/shard_map/ppermute | solution.py:481
  9.5 2.3 %collective-permute-start.26 = (f32[3,128]{1,0:T(4,128)S(1)}, f32[3,128]{1,0:T(4,128)S(1)}, u32[]{:S(2)}, u32[]{:S(2)}) collective-permute-start(f32[3,128]{1,0:T(4,128)S(1)} %slice.524), channel_id=1, source_target_pairs={{0,7},{1,6},{2,5},{3,4},{4,3},{5,2},{6,1},{7,0},{8,15},{9,14},{10,... | collective-permute-start | bytes 4616 | tf_op jit(solution)/shard_map/ppermute | solution.py:481
  11.8 0.6 %collective-permute-start.24 = (f32[40,128]{1,0:T(8,128)S(1)}, f32[40,128]{1,0:T(8,128)S(1)}, u32[]{:S(2)}, u32[]{:S(2)}) collective-permute-start(f32[40,128]{1,0:T(8,128)S(1)} %pad_maximum_fusion.11), channel_id=1, source_target_pairs={{0,6},{1,7},{2,4},{3,5},{4,2},{5,3},{6,0},{7,1},{8,14},{9,15},{10,... | collective-permute-start | bytes 61448 | tf_op jit(solution)/shard_map/ppermute | solution.py:481
  12.4 0.3 collective-permute-start.25
  12.7 2.4 %collective-permute-done.24.refs_11_ = f32[40,128]{1,0:T(8,128)S(1)} collective-permute-done((f32[40,128]{1,0:T(8,128)S(1)}, f32[40,128]{1,0:T(8,128)S(1)}, u32[]{:S(2)}, u32[]{:S(2)}) %collective-permute-start.24) | collective-permute-done | bytes 20512 | tf_op jit(solution)/shard_map/ppermute | solution.py:481
  15.2 0.7 %collective-permute-done.25 = f32[67,128]{1,0:T(8,128)S(1)} collective-permute-done((f32[67,128]{1,0:T(8,128)S(1)}, f32[67,128]{1,0:T(8,128)S(1)}, u32[]{:S(2)}, u32[]{:S(2)}) %collective-permute-start.25) | collective-permute-done | bytes 34336 | tf_op jit(solution)/shard_map/ppermute | solution.py:481
  15.9 3.4 %collective-permute-start.29 = (f32[40,128]{1,0:T(8,128)S(1)}, f32[40,128]{1,0:T(8,128)S(1)}, u32[]{:S(2)}, u32[]{:S(2)}) collective-permute-start(f32[40,128]{1,0:T(8,128)S(1)} %maximum_add_fusion.3.refs_6_), channel_id=1, source_target_pairs={{0,26},{1,27},{2,24},{3,25},{4,30},{5,31},{6,28},{7,29},{8,18},{9,... | collective-permute-start | bytes 61448 | tf_op jit(solution)/shard_map/ppermute | solution.py:481
  19.4 0.6 %collective-permute-start.27 = (f32[40,128]{1,0:T(8,128)S(1)}, f32[40,128]{1,0:T(8,128)S(1)}, u32[]{:S(2)}, u32[]{:S(2)}) collective-permute-start(f32[40,128]{1,0:T(8,128)S(1)} %maximum_add_fusion.3.refs_6_), channel_id=1, source_target_pairs={{0,10},{1,11},{2,8},{3,9},{4,14},{5,15},{6,12},{7,13},{8,2},{9,3},... | collective-permute-start | bytes 61448 | tf_op jit(solution)/shard_map/ppermute | solution.py:481
  20.0 0.2 shard_map.168.refs_13_
  20.2 0.8 %collective-permute-done.29.refs_9_ = f32[40,128]{1,0:T(8,128)S(1)} collective-permute-done((f32[40,128]{1,0:T(8,128)S(1)}, f32[40,128]{1,0:T(8,128)S(1)}, u32[]{:S(2)}, u32[]{:S(2)}) %collective-permute-start.29) | collective-permute-done | bytes 20512 | tf_op jit(solution)/shard_map/ppermute | solution.py:481
  21.0 2.5 %collective-permute-done.28.refs_8_ = f32[40,128]{1,0:T(8,128)S(1)} collective-permute-done((f32[40,128]{1,0:T(8,128)S(1)}, f32[40,128]{1,0:T(8,128)S(1)}, u32[]{:S(2)}, u32[]{:S(2)}) %collective-permute-start.28) | collective-permute-done | bytes 20512 | tf_op jit(solution)/shard_map/ppermute | solution.py:481
  23.5 0.0 collective-permute-done.27.refs_7_
  23.5 0.8 %shard_map.169 = (f32[17,64,128]{2,1,0:T(8,128)S(1)}, f32[17,64,128]{2,1,0:T(8,128)S(1)}, f32[72,640]{1,0:T(8,128)S(1)}, f32[64,256]{1,0:T(8,128)S(1)}, f32[64,256]{1,0:T(8,128)S(1)}, /*index=5*/f32[88,128]{1,0:T(8,128)S(1)}) custom-call(f32[18,64,128]{2,1,0:T(8,128)S(1)} %get-tuple-element.107.refs_0_, ...), custom_call_target="tpu_custom_call" | custom-call | tf_op jit(solution)/shard_map/pallas_call | solution.py:456
  24.3 0.4 collective-permute-start.30
  24.7 0.9 %collective-permute-done.30 = f32[88,128]{1,0:T(8,128)S(1)} collective-permute-done((f32[88,128]{1,0:T(8,128)S(1)}, f32[88,128]{1,0:T(8,128)S(1)}, u32[]{:S(2)}, u32[]{:S(2)}) %collective-permute-start.30) | collective-permute-done | bytes 45088 | tf_op jit(solution)/shard_map/ppermute | solution.py:481
  25.6 1.5 %collective-permute-start.33 = (f32[3,128]{1,0:T(4,128)S(1)}, f32[3,128]{1,0:T(4,128)S(1)}, u32[]{:S(2)}, u32[]{:S(2)}) collective-permute-start(f32[3,128]{1,0:T(4,128)S(1)} %slice.537), channel_id=1, source_target_pairs={{0,7},{1,6},{2,5},{3,4},{4,3},{5,2},{6,1},{7,0},{8,15},{9,14},{10,... | collective-permute-start | bytes 4616 | tf_op jit(solution)/shard_map/ppermute | solution.py:481
  27.1 0.4 collective-permute-start.31
  27.4 1.5 %collective-permute-start.32 = (f32[67,128]{1,0:T(8,128)S(1)}, f32[67,128]{1,0:T(8,128)S(1)}, u32[]{:S(2)}, u32[]{:S(2)}) collective-permute-start(f32[67,128]{1,0:T(8,128)S(1)} %pad_maximum_fusion.9), channel_id=1, source_target_pairs={{0,3},{1,2},{2,1},{3,0},{4,7},{5,6},{6,5},{7,4},{8,11},{9,10},{10,... | collective-permute-start | bytes 102920 | tf_op jit(solution)/shard_map/ppermute | solution.py:481
  29.0 1.3 %collective-permute-done.31.refs_13_ = f32[24,128]{1,0:T(8,128)S(1)} collective-permute-done((f32[24,128]{1,0:T(8,128)S(1)}, f32[24,128]{1,0:T(8,128)S(1)}, u32[]{:S(2)}, u32[]{:S(2)}) %collective-permute-start.31) | collective-permute-done | bytes 12320 | tf_op jit(solution)/shard_map/ppermute | solution.py:481
  30.3 0.0 collective-permute-done.33
  30.3 0.6 %collective-permute-done.32 = f32[67,128]{1,0:T(8,128)S(1)} collective-permute-done((f32[67,128]{1,0:T(8,128)S(1)}, f32[67,128]{1,0:T(8,128)S(1)}, u32[]{:S(2)}, u32[]{:S(2)}) %collective-permute-start.32) | collective-permute-done | bytes 34336 | tf_op jit(solution)/shard_map/ppermute | solution.py:481
  30.9 1.6 %collective-permute-start.36 = (f32[24,128]{1,0:T(8,128)S(1)}, f32[24,128]{1,0:T(8,128)S(1)}, u32[]{:S(2)}, u32[]{:S(2)}) collective-permute-start(f32[24,128]{1,0:T(8,128)S(1)} %maximum_add_fusion.4.refs_8_), channel_id=1, source_target_pairs={{0,26},{1,27},{2,24},{3,25},{4,30},{5,31},{6,28},{7,29},{8,18},{9,... | collective-permute-start | bytes 36872 | tf_op jit(solution)/shard_map/ppermute | solution.py:481
  32.5 0.3 collective-permute-start.35
  32.8 2.2 %collective-permute-start.34 = (f32[24,128]{1,0:T(8,128)S(1)}, f32[24,128]{1,0:T(8,128)S(1)}, u32[]{:S(2)}, u32[]{:S(2)}) collective-permute-start(f32[24,128]{1,0:T(8,128)S(1)} %maximum_add_fusion.4.refs_8_), channel_id=1, source_target_pairs={{0,10},{1,11},{2,8},{3,9},{4,14},{5,15},{6,12},{7,13},{8,2},{9,3},... | collective-permute-start | bytes 36872 | tf_op jit(solution)/shard_map/ppermute | solution.py:481
  35.0 0.2 shard_map.170.refs_15_
  35.3 0.6 %collective-permute-done.36.refs_11_ = f32[24,128]{1,0:T(8,128)S(1)} collective-permute-done((f32[24,128]{1,0:T(8,128)S(1)}, f32[24,128]{1,0:T(8,128)S(1)}, u32[]{:S(2)}, u32[]{:S(2)}) %collective-permute-start.36) | collective-permute-done | bytes 12320 | tf_op jit(solution)/shard_map/ppermute | solution.py:481
  35.9 0.8 %collective-permute-done.35.refs_10_ = f32[24,128]{1,0:T(8,128)S(1)} collective-permute-done((f32[24,128]{1,0:T(8,128)S(1)}, f32[24,128]{1,0:T(8,128)S(1)}, u32[]{:S(2)}, u32[]{:S(2)}) %collective-permute-start.35) | collective-permute-done | bytes 12320 | tf_op jit(solution)/shard_map/ppermute | solution.py:481
  36.6 0.0 collective-permute-done.34.refs_9_
  36.7 0.7 %shard_map.171 = (f32[17,64,128]{2,1,0:T(8,128)S(1)}, f32[17,64,128]{2,1,0:T(8,128)S(1)}, f32[72,640]{1,0:T(8,128)S(1)}, f32[64,256]{1,0:T(8,128)S(1)}, f32[64,256]{1,0:T(8,128)S(1)}, /*index=5*/f32[88,128]{1,0:T(8,128)S(1)}) custom-call(f32[18,64,128]{2,1,0:T(8,128)S(1)} %get-tuple-element.107.refs_0_, ...), custom_call_target="tpu_custom_call" | custom-call | tf_op jit(solution)/shard_map/pallas_call | solution.py:456
  37.4 0.3 collective-permute-start.37
  37.7 1.0 %collective-permute-done.37 = f32[88,128]{1,0:T(8,128)S(1)} collective-permute-done((f32[88,128]{1,0:T(8,128)S(1)}, f32[88,128]{1,0:T(8,128)S(1)}, u32[]{:S(2)}, u32[]{:S(2)}) %collective-permute-start.37) | collective-permute-done | bytes 45088 | tf_op jit(solution)/shard_map/ppermute | solution.py:481
  38.7 2.4 %collective-permute-start.40 = (f32[3,128]{1,0:T(4,128)S(1)}, f32[3,128]{1,0:T(4,128)S(1)}, u32[]{:S(2)}, u32[]{:S(2)}) collective-permute-start(f32[3,128]{1,0:T(4,128)S(1)} %slice.550), channel_id=1, source_target_pairs={{0,7},{1,6},{2,5},{3,4},{4,3},{5,2},{6,1},{7,0},{8,15},{9,14},{10,... | collective-permute-start | bytes 4616 | tf_op jit(solution)/shard_map/ppermute | solution.py:481
  41.1 0.5 collective-permute-start.38
  41.6 0.4 collective-permute-start.39
  42.0 2.3 %collective-permute-done.38.refs_13_ = f32[24,128]{1,0:T(8,128)S(1)} collective-permute-done((f32[24,128]{1,0:T(8,128)S(1)}, f32[24,128]{1,0:T(8,128)S(1)}, u32[]{:S(2)}, u32[]{:S(2)}) %collective-permute-start.38) | collective-permute-done | bytes 12320 | tf_op jit(solution)/shard_map/ppermute | solution.py:481
  44.3 0.7 %collective-permute-done.39 = f32[67,128]{1,0:T(8,128)S(1)} collective-permute-done((f32[67,128]{1,0:T(8,128)S(1)}, f32[67,128]{1,0:T(8,128)S(1)}, u32[]{:S(2)}, u32[]{:S(2)}) %collective-permute-start.39) | collective-permute-done | bytes 34336 | tf_op jit(solution)/shard_map/ppermute | solution.py:481
  45.0 2.1 %collective-permute-start.43 = (f32[24,128]{1,0:T(8,128)S(1)}, f32[24,128]{1,0:T(8,128)S(1)}, u32[]{:S(2)}, u32[]{:S(2)}) collective-permute-start(f32[24,128]{1,0:T(8,128)S(1)} %maximum_add_fusion.5.refs_8_), channel_id=1, source_target_pairs={{0,26},{1,27},{2,24},{3,25},{4,30},{5,31},{6,28},{7,29},{8,18},{9,... | collective-permute-start | bytes 36872 | tf_op jit(solution)/shard_map/ppermute | solution.py:481
  47.1 0.7 %collective-permute-start.42 = (f32[24,128]{1,0:T(8,128)S(1)}, f32[24,128]{1,0:T(8,128)S(1)}, u32[]{:S(2)}, u32[]{:S(2)}) collective-permute-start(f32[24,128]{1,0:T(8,128)S(1)} %maximum_add_fusion.5.refs_8_), channel_id=1, source_target_pairs={{0,18},{1,19},{2,16},{3,17},{4,22},{5,23},{6,20},{7,21},{8,26},{9,... | collective-permute-start | bytes 36872 | tf_op jit(solution)/shard_map/ppermute | solution.py:481
  47.8 1.3 %collective-permute-start.41 = (f32[24,128]{1,0:T(8,128)S(1)}, f32[24,128]{1,0:T(8,128)S(1)}, u32[]{:S(2)}, u32[]{:S(2)}) collective-permute-start(f32[24,128]{1,0:T(8,128)S(1)} %maximum_add_fusion.5.refs_8_), channel_id=1, source_target_pairs={{0,10},{1,11},{2,8},{3,9},{4,14},{5,15},{6,12},{7,13},{8,2},{9,3},... | collective-permute-start | bytes 36872 | tf_op jit(solution)/shard_map/ppermute | solution.py:481
  49.1 0.2 shard_map.172.refs_15_
  49.3 0.7 %collective-permute-done.43.refs_11_ = f32[24,128]{1,0:T(8,128)S(1)} collective-permute-done((f32[24,128]{1,0:T(8,128)S(1)}, f32[24,128]{1,0:T(8,128)S(1)}, u32[]{:S(2)}, u32[]{:S(2)}) %collective-permute-start.43) | collective-permute-done | bytes 12320 | tf_op jit(solution)/shard_map/ppermute | solution.py:481
  50.0 1.1 %collective-permute-done.42.refs_10_ = f32[24,128]{1,0:T(8,128)S(1)} collective-permute-done((f32[24,128]{1,0:T(8,128)S(1)}, f32[24,128]{1,0:T(8,128)S(1)}, u32[]{:S(2)}, u32[]{:S(2)}) %collective-permute-start.42) | collective-permute-done | bytes 12320 | tf_op jit(solution)/shard_map/ppermute | solution.py:481
  51.1 1.2 %shard_map.173 = (f32[1024,128]{1,0:T(8,128)}, f32[1,128]{1,0:T(1,128)S(1)}, f32[64,128]{1,0:T(8,128)S(1)}, f32[64,256]{1,0:T(8,128)S(1)}, f32[1,128]{1,0:T(1,128)S(1)}, /*index=5*/f32[88,128]{1,0:T(8,128)S(1)}) custom-call(f32[18,64,128]{2,1,0:T(8,128)S(1)} %get-tuple-element.107.refs_0_, bf16[128,512]{1,0:T(8,128)(2,1)S(1)} %get-tuple-element.108.maps_local.refs_1_, ...), custom_call_target="tpu_custom_call" | custom-call | tf_op jit(solution)/shard_map/pallas_call | solution.py:456
  52.4 0.0 copy-start.14
  52.4 0.0 copy-start.12
  52.5 0.0 copy-start.13
  52.5 0.5 copy-done.14
  52.9 0.1 copy-done.12
  53.1 0.0 copy-done.13
  (68 shorter events, 0.3 us)
Async XLA Ops:
  0.6 4.6 %copy-start.11 = (s32[256]{0:T(256)S(1)}, s32[256]{0:T(256)}, u32[]{:S(2)}) copy-start(s32[256]{0:T(256)} %param.30) | copy-start | bytes 3076
  2.1 5.6 %collective-permute-start.22 = (f32[72,128]{1,0:T(8,128)}, f32[72,128]{1,0:T(8,128)S(1)}, u32[]{:S(2)}, u32[]{:S(2)}) collective-permute-start(f32[72,128]{1,0:T(8,128)} %shard_map.166), channel_id=1, source_target_pairs={{0,1},{1,0},{2,3},{3,2},{4,5},{5,4},{6,7},{7,6},{8,9},{9,8},{10,11... | collective-permute-start | bytes 110600 | tf_op jit(solution)/shard_map/ppermute | solution.py:481
  5.1 0.7 %copy-start.10 = (s32[2,256]{1,0:T(2,128)S(1)}, s32[2,256]{1,0:T(2,128)}, u32[]{:S(2)}) copy-start(s32[2,256]{1,0:T(2,128)} %refs_6_.1) | copy-start | bytes 6148
  5.1 0.8 %copy-start.8 = (f32[64,128]{1,0:T(8,128)S(1)}, f32[64,128]{1,0:T(8,128)}, u32[]{:S(2)}) copy-start(f32[64,128]{1,0:T(8,128)} %refs_2_.2) | copy-start | bytes 98308
  5.1 0.8 %copy-start.7 = (f32[64,128]{1,0:T(8,128)S(1)}, f32[64,128]{1,0:T(8,128)}, u32[]{:S(2)}) copy-start(f32[64,128]{1,0:T(8,128)} %refs_0_.1) | copy-start | bytes 98308
  5.1 0.8 %copy-start.5 = (f32[1,128]{1,0:T(1,128)S(1)}, f32[1,128]{1,0:T(1,128)}, u32[]{:S(2)}) copy-start(f32[1,128]{1,0:T(1,128)} %refs_4_.1) | copy-start | bytes 1540
  5.1 0.8 %copy-start.3 = (f32[256]{0:T(256)S(1)}, f32[256]{0:T(256)}, u32[]{:S(2)}) copy-start(f32[256]{0:T(256)} %param.32) | copy-start | bytes 3076
  5.1 0.8 %copy-start.4 = (f32[256]{0:T(256)S(1)}, f32[256]{0:T(256)}, u32[]{:S(2)}) copy-start(f32[256]{0:T(256)} %param.31) | copy-start | bytes 3076
  5.2 0.8 %copy-start.1 = (s32[1,2048]{1,0:T(1,128)S(1)}, s32[1,2048]{1,0:T(1,128)}, u32[]{:S(2)}) copy-start(s32[1,2048]{1,0:T(1,128)} %param.24) | copy-start | bytes 24580
  5.2 0.8 %copy-start = (f32[16,128]{1,0:T(8,128)S(1)}, f32[16,128]{1,0:T(8,128)}, u32[]{:S(2)}) copy-start(f32[16,128]{1,0:T(8,128)} %refs_3_.2) | copy-start | bytes 24580
  5.2 0.7 %copy-start.2 = (f32[256]{0:T(256)S(1)}, f32[256]{0:T(256)}, u32[]{:S(2)}) copy-start(f32[256]{0:T(256)} %param.26) | copy-start | bytes 3076
  5.9 1.8 %copy-start.9 = (f32[72,128]{1,0:T(8,128)S(1)}, f32[72,128]{1,0:T(8,128)}, u32[]{:S(2)}) copy-start(f32[72,128]{1,0:T(8,128)} %shard_map.166) | copy-start | bytes 110596
  8.2 1.3 %collective-permute-start.23 = (f32[104,128]{1,0:T(8,128)S(1)}, f32[104,128]{1,0:T(8,128)S(1)}, u32[]{:S(2)}, u32[]{:S(2)}) collective-permute-start(f32[104,128]{1,0:T(8,128)S(1)} %get-tuple-element.116), channel_id=1, source_target_pairs={{0,2},{1,3},{2,0},{3,1},{4,6},{5,7},{6,4},{7,5},{8,10},{9,11},{10,... | collective-permute-start | bytes 159752 | tf_op jit(solution)/shard_map/ppermute | solution.py:481
  9.5 5.7 %collective-permute-start.26 = (f32[3,128]{1,0:T(4,128)S(1)}, f32[3,128]{1,0:T(4,128)S(1)}, u32[]{:S(2)}, u32[]{:S(2)}) collective-permute-start(f32[3,128]{1,0:T(4,128)S(1)} %slice.524), channel_id=1, source_target_pairs={{0,7},{1,6},{2,5},{3,4},{4,3},{5,2},{6,1},{7,0},{8,15},{9,14},{10,... | collective-permute-start | bytes 4616 | tf_op jit(solution)/shard_map/ppermute | solution.py:481
  11.8 3.3 %collective-permute-start.24 = (f32[40,128]{1,0:T(8,128)S(1)}, f32[40,128]{1,0:T(8,128)S(1)}, u32[]{:S(2)}, u32[]{:S(2)}) collective-permute-start(f32[40,128]{1,0:T(8,128)S(1)} %pad_maximum_fusion.11), channel_id=1, source_target_pairs={{0,6},{1,7},{2,4},{3,5},{4,2},{5,3},{6,0},{7,1},{8,14},{9,15},{10,... | collective-permute-start | bytes 61448 | tf_op jit(solution)/shard_map/ppermute | solution.py:481
  12.4 3.5 %collective-permute-start.25 = (f32[67,128]{1,0:T(8,128)S(1)}, f32[67,128]{1,0:T(8,128)S(1)}, u32[]{:S(2)}, u32[]{:S(2)}) collective-permute-start(f32[67,128]{1,0:T(8,128)S(1)} %pad_maximum_fusion.8), channel_id=1, source_target_pairs={{0,3},{1,2},{2,1},{3,0},{4,7},{5,6},{6,5},{7,4},{8,11},{9,10},{10,... | collective-permute-start | bytes 102920 | tf_op jit(solution)/shard_map/ppermute | solution.py:481
  15.9 5.1 %collective-permute-start.29 = (f32[40,128]{1,0:T(8,128)S(1)}, f32[40,128]{1,0:T(8,128)S(1)}, u32[]{:S(2)}, u32[]{:S(2)}) collective-permute-start(f32[40,128]{1,0:T(8,128)S(1)} %maximum_add_fusion.3.refs_6_), channel_id=1, source_target_pairs={{0,26},{1,27},{2,24},{3,25},{4,30},{5,31},{6,28},{7,29},{8,18},{9,... | collective-permute-start | bytes 61448 | tf_op jit(solution)/shard_map/ppermute | solution.py:481
  19.4 4.1 %collective-permute-start.28 = (f32[40,128]{1,0:T(8,128)S(1)}, f32[40,128]{1,0:T(8,128)S(1)}, u32[]{:S(2)}, u32[]{:S(2)}) collective-permute-start(f32[40,128]{1,0:T(8,128)S(1)} %maximum_add_fusion.3.refs_6_), channel_id=1, source_target_pairs={{0,18},{1,19},{2,16},{3,17},{4,22},{5,23},{6,20},{7,21},{8,26},{9,... | collective-permute-start | bytes 61448 | tf_op jit(solution)/shard_map/ppermute | solution.py:481
  19.4 4.1 %collective-permute-start.27 = (f32[40,128]{1,0:T(8,128)S(1)}, f32[40,128]{1,0:T(8,128)S(1)}, u32[]{:S(2)}, u32[]{:S(2)}) collective-permute-start(f32[40,128]{1,0:T(8,128)S(1)} %maximum_add_fusion.3.refs_6_), channel_id=1, source_target_pairs={{0,10},{1,11},{2,8},{3,9},{4,14},{5,15},{6,12},{7,13},{8,2},{9,3},... | collective-permute-start | bytes 61448 | tf_op jit(solution)/shard_map/ppermute | solution.py:481
  24.3 1.3 %collective-permute-start.30 = (f32[88,128]{1,0:T(8,128)S(1)}, f32[88,128]{1,0:T(8,128)S(1)}, u32[]{:S(2)}, u32[]{:S(2)}) collective-permute-start(f32[88,128]{1,0:T(8,128)S(1)} %get-tuple-element.122), channel_id=1, source_target_pairs={{0,2},{1,3},{2,0},{3,1},{4,6},{5,7},{6,4},{7,5},{8,10},{9,11},{10,... | collective-permute-start | bytes 135176 | tf_op jit(solution)/shard_map/ppermute | solution.py:481
  25.6 4.7 %collective-permute-start.33 = (f32[3,128]{1,0:T(4,128)S(1)}, f32[3,128]{1,0:T(4,128)S(1)}, u32[]{:S(2)}, u32[]{:S(2)}) collective-permute-start(f32[3,128]{1,0:T(4,128)S(1)} %slice.537), channel_id=1, source_target_pairs={{0,7},{1,6},{2,5},{3,4},{4,3},{5,2},{6,1},{7,0},{8,15},{9,14},{10,... | collective-permute-start | bytes 4616 | tf_op jit(solution)/shard_map/ppermute | solution.py:481
  27.1 3.2 %collective-permute-start.31 = (f32[24,128]{1,0:T(8,128)S(1)}, f32[24,128]{1,0:T(8,128)S(1)}, u32[]{:S(2)}, u32[]{:S(2)}) collective-permute-start(f32[24,128]{1,0:T(8,128)S(1)} %pad_maximum_fusion.12), channel_id=1, source_target_pairs={{0,6},{1,7},{2,4},{3,5},{4,2},{5,3},{6,0},{7,1},{8,14},{9,15},{10,... | collective-permute-start | bytes 36872 | tf_op jit(solution)/shard_map/ppermute | solution.py:481
  27.4 3.4 %collective-permute-start.32 = (f32[67,128]{1,0:T(8,128)S(1)}, f32[67,128]{1,0:T(8,128)S(1)}, u32[]{:S(2)}, u32[]{:S(2)}) collective-permute-start(f32[67,128]{1,0:T(8,128)S(1)} %pad_maximum_fusion.9), channel_id=1, source_target_pairs={{0,3},{1,2},{2,1},{3,0},{4,7},{5,6},{6,5},{7,4},{8,11},{9,10},{10,... | collective-permute-start | bytes 102920 | tf_op jit(solution)/shard_map/ppermute | solution.py:481
  30.9 5.0 %collective-permute-start.36 = (f32[24,128]{1,0:T(8,128)S(1)}, f32[24,128]{1,0:T(8,128)S(1)}, u32[]{:S(2)}, u32[]{:S(2)}) collective-permute-start(f32[24,128]{1,0:T(8,128)S(1)} %maximum_add_fusion.4.refs_8_), channel_id=1, source_target_pairs={{0,26},{1,27},{2,24},{3,25},{4,30},{5,31},{6,28},{7,29},{8,18},{9,... | collective-permute-start | bytes 36872 | tf_op jit(solution)/shard_map/ppermute | solution.py:481
  32.5 4.2 %collective-permute-start.35 = (f32[24,128]{1,0:T(8,128)S(1)}, f32[24,128]{1,0:T(8,128)S(1)}, u32[]{:S(2)}, u32[]{:S(2)}) collective-permute-start(f32[24,128]{1,0:T(8,128)S(1)} %maximum_add_fusion.4.refs_8_), channel_id=1, source_target_pairs={{0,18},{1,19},{2,16},{3,17},{4,22},{5,23},{6,20},{7,21},{8,26},{9,... | collective-permute-start | bytes 36872 | tf_op jit(solution)/shard_map/ppermute | solution.py:481
  32.8 3.8 %collective-permute-start.34 = (f32[24,128]{1,0:T(8,128)S(1)}, f32[24,128]{1,0:T(8,128)S(1)}, u32[]{:S(2)}, u32[]{:S(2)}) collective-permute-start(f32[24,128]{1,0:T(8,128)S(1)} %maximum_add_fusion.4.refs_8_), channel_id=1, source_target_pairs={{0,10},{1,11},{2,8},{3,9},{4,14},{5,15},{6,12},{7,13},{8,2},{9,3},... | collective-permute-start | bytes 36872 | tf_op jit(solution)/shard_map/ppermute | solution.py:481
  37.4 1.3 %collective-permute-start.37 = (f32[88,128]{1,0:T(8,128)S(1)}, f32[88,128]{1,0:T(8,128)S(1)}, u32[]{:S(2)}, u32[]{:S(2)}) collective-permute-start(f32[88,128]{1,0:T(8,128)S(1)} %get-tuple-element.128), channel_id=1, source_target_pairs={{0,2},{1,3},{2,0},{3,1},{4,6},{5,7},{6,4},{7,5},{8,10},{9,11},{10,... | collective-permute-start | bytes 135176 | tf_op jit(solution)/shard_map/ppermute | solution.py:481
  38.7 5.6 %collective-permute-start.40 = (f32[3,128]{1,0:T(4,128)S(1)}, f32[3,128]{1,0:T(4,128)S(1)}, u32[]{:S(2)}, u32[]{:S(2)}) collective-permute-start(f32[3,128]{1,0:T(4,128)S(1)} %slice.550), channel_id=1, source_target_pairs={{0,7},{1,6},{2,5},{3,4},{4,3},{5,2},{6,1},{7,0},{8,15},{9,14},{10,... | collective-permute-start | bytes 4616 | tf_op jit(solution)/shard_map/ppermute | solution.py:481
  41.1 3.2 %collective-permute-start.38 = (f32[24,128]{1,0:T(8,128)S(1)}, f32[24,128]{1,0:T(8,128)S(1)}, u32[]{:S(2)}, u32[]{:S(2)}) collective-permute-start(f32[24,128]{1,0:T(8,128)S(1)} %pad_maximum_fusion.13), channel_id=1, source_target_pairs={{0,6},{1,7},{2,4},{3,5},{4,2},{5,3},{6,0},{7,1},{8,14},{9,15},{10,... | collective-permute-start | bytes 36872 | tf_op jit(solution)/shard_map/ppermute | solution.py:481
  41.6 3.4 %collective-permute-start.39 = (f32[67,128]{1,0:T(8,128)S(1)}, f32[67,128]{1,0:T(8,128)S(1)}, u32[]{:S(2)}, u32[]{:S(2)}) collective-permute-start(f32[67,128]{1,0:T(8,128)S(1)} %pad_maximum_fusion.10), channel_id=1, source_target_pairs={{0,3},{1,2},{2,1},{3,0},{4,7},{5,6},{6,5},{7,4},{8,11},{9,10},{10,... | collective-permute-start | bytes 102920 | tf_op jit(solution)/shard_map/ppermute | solution.py:481
  45.0 5.0 %collective-permute-start.43 = (f32[24,128]{1,0:T(8,128)S(1)}, f32[24,128]{1,0:T(8,128)S(1)}, u32[]{:S(2)}, u32[]{:S(2)}) collective-permute-start(f32[24,128]{1,0:T(8,128)S(1)} %maximum_add_fusion.5.refs_8_), channel_id=1, source_target_pairs={{0,26},{1,27},{2,24},{3,25},{4,30},{5,31},{6,28},{7,29},{8,18},{9,... | collective-permute-start | bytes 36872 | tf_op jit(solution)/shard_map/ppermute | solution.py:481
  47.1 4.0 %collective-permute-start.42 = (f32[24,128]{1,0:T(8,128)S(1)}, f32[24,128]{1,0:T(8,128)S(1)}, u32[]{:S(2)}, u32[]{:S(2)}) collective-permute-start(f32[24,128]{1,0:T(8,128)S(1)} %maximum_add_fusion.5.refs_8_), channel_id=1, source_target_pairs={{0,18},{1,19},{2,16},{3,17},{4,22},{5,23},{6,20},{7,21},{8,26},{9,... | collective-permute-start | bytes 36872 | tf_op jit(solution)/shard_map/ppermute | solution.py:481
  47.8 3.4 %collective-permute-start.41 = (f32[24,128]{1,0:T(8,128)S(1)}, f32[24,128]{1,0:T(8,128)S(1)}, u32[]{:S(2)}, u32[]{:S(2)}) collective-permute-start(f32[24,128]{1,0:T(8,128)S(1)} %maximum_add_fusion.5.refs_8_), channel_id=1, source_target_pairs={{0,10},{1,11},{2,8},{3,9},{4,14},{5,15},{6,12},{7,13},{8,2},{9,3},... | collective-permute-start | bytes 36872 | tf_op jit(solution)/shard_map/ppermute | solution.py:481
  51.1 1.3 %copy-start.6 = (f32[64,16,128]{2,1,0:T(8,128)S(1)}, f32[64,16,128]{2,1,0:T(8,128)}, u32[]{:S(2)}) copy-start(f32[64,16,128]{2,1,0:T(8,128)} %param.20) | copy-start | bytes 1572868
  52.4 0.5 copy-start.14
  52.4 0.6 %copy-start.12 = (f32[64,256]{1,0:T(8,128)}, f32[64,256]{1,0:T(8,128)S(1)}, u32[]{:S(2)}) copy-start(f32[64,256]{1,0:T(8,128)S(1)} %get-tuple-element.137) | copy-start | bytes 196612
  52.5 0.6 %copy-start.13 = (f32[64,128]{1,0:T(8,128)}, f32[64,128]{1,0:T(8,128)S(1)}, u32[]{:S(2)}) copy-start(f32[64,128]{1,0:T(8,128)S(1)} %get-tuple-element.136) | copy-start | bytes 98308

commit v23 on v22

--- a/solution.py
+++ b/solution.py
@@ -528,8 +528,8 @@
     diagonal = swap(chip[techs:halo], 2 + 1, 1)
     beside = swap(jnp.concatenate([partner_prices, chip[techs:halo]], axis=0), 1, 1)
     other, squares = beside[: sizes.rows], beside[sizes.rows :]
+    chip = chip + jnp.pad(squares + diagonal, ((techs, chip.shape[0] - halo), (0, 0)))
     slab = merged(chip, across, hour // 2 % 2 == 0)
-    slab = slab + jnp.pad(squares + diagonal, ((techs, slab.shape[0] - halo), (0, 0)))
     near, middle, far = [swap(slab, 4 * step + 1, 0) for step in (1, 2, 3)]
     parts = Bag(slab=slab, near=near, middle=middle, far=far, partner=partner, across=across)
     return in_order(prices, other), parts

time: 53.4 us -> 52.6 us (0.985)
  transfers between devices with their start and end apart: 22 -> 22, of which waited for: 15 -> 17; matrix products, arithmetic and copies ran while one was open for 0% -> 0% of each run, Pallas kernels for 5% -> 5%
where the time goes in v23:
time: 52.6 us; the launch traced here: 52.3 us
  starting transfers between devices  25.5 us (48%)
  waiting for transfers between devices  17.1 us (33%)
  Pallas kernels  6.98 us (13%)
  local copies, waits for them, and re-layouts  1.46 us (3%)
  between operations  1.04 us (2%)
    ppermute x22, starting transfers between devices, swap(): return lax.ppermute(value, ('hours', 'region'), pairs)  25.5 us
    ppermute x22, waiting for transfers between devices, swap(): return lax.ppermute(value, ('hours', 'region'), pairs)  17.1 us
    pallas_call x9, Pallas kernels, call(): pl.pallas_call(functools.partial(kernel, names_in, names_out), out_shape=...  6.98 us
    unnamed x30, local copies, waits for them, and re-layouts  1.38 us
  transfers between devices with their start and end apart: 22, of which 17 were waited for; matrix products, arithmetic and copies ran while one was open for 0% of the time, Pallas kernels for 5%

profile of v23, /device:TPU:0, one launch (start us, length us, event | category | flops | bytes accessed | tf_op | source)
XLA Modules:
  0.0 52.3 jit_solution(14178522104635517019)
XLA Ops:
  0.6 1.4 %shard_map.166 = f32[72,128]{1,0:T(8,128)} custom-call(f32[64,128]{1,0:T(8,128)} %refs_0_.1, s32[2,64]{1,0:T(2,128)} %bitcast.122, f32[1,64]{1,0:T(1,128)} %refs_2_.3, s32[1,2]{1,0:T(1,128)} %refs_3_.3), custom_call_target="tpu_custom_call" | custom-call | tf_op jit(solution)/shard_map/pallas_call | solution.py:456
  2.1 3.0 %collective-permute-start.22 = (f32[72,128]{1,0:T(8,128)}, f32[72,128]{1,0:T(8,128)S(1)}, u32[]{:S(2)}, u32[]{:S(2)}) collective-permute-start(f32[72,128]{1,0:T(8,128)} %shard_map.166), channel_id=1, source_target_pairs={{0,1},{1,0},{2,3},{3,2},{4,5},{5,4},{6,7},{7,6},{8,9},{9,8},{10,11... | collective-permute-start | bytes 110600 | tf_op jit(solution)/shard_map/ppermute | solution.py:481
  5.1 0.0 copy-start.3
  5.1 0.0 copy-start.4
  5.2 0.0 copy-start.1
  5.2 0.0 copy-start
  5.2 0.0 copy-start.2
  5.2 0.6 %copy-done.10 = s32[2,256]{1,0:T(2,128)S(1)} copy-done((s32[2,256]{1,0:T(2,128)S(1)}, s32[2,256]{1,0:T(2,128)}, u32[]{:S(2)}) %copy-start.10) | copy-done | bytes 2072
  5.8 0.1 copy-done.8
  5.9 0.0 copy-done.7
  5.9 0.0 copy-done
  5.9 1.7 %shard_map.165 = (f32[18,64,128]{2,1,0:T(8,128)S(1)}, bf16[128,512]{1,0:T(8,128)(2,1)S(1)}, f32[64,512]{1,0:T(8,128)S(1)}, f32[64,256]{1,0:T(8,128)S(1)}, f32[17...) custom-call(f32[1024,128]{1,0:T(8,128)} %bitcast.88, f32[64,128]{1,0:T(8,128)S(1)} %copy-done.7, ...), custom_call_target="tpu_custom_call" | custom-call | flops 1000000 | bytes 4000000 | tf_op jit(solution)/shard_map/pallas_call | solution.py:456
  7.7 0.4 shard_map.167
  8.2 0.1 collective-permute-start.23
  8.3 1.2 %collective-permute-done.23 = f32[104,128]{1,0:T(8,128)S(1)} collective-permute-done((f32[104,128]{1,0:T(8,128)S(1)}, f32[104,128]{1,0:T(8,128)S(1)}, u32[]{:S(2)}, u32[]{:S(2)}) %collective-permute-start.23) | collective-permute-done | bytes 53280 | tf_op jit(solution)/shard_map/ppermute | solution.py:481
  9.5 2.3 %collective-permute-start.25 = (f32[3,128]{1,0:T(4,128)S(1)}, f32[3,128]{1,0:T(4,128)S(1)}, u32[]{:S(2)}, u32[]{:S(2)}) collective-permute-start(f32[3,128]{1,0:T(4,128)S(1)} %slice.568), channel_id=1, source_target_pairs={{0,7},{1,6},{2,5},{3,4},{4,3},{5,2},{6,1},{7,0},{8,15},{9,14},{10,... | collective-permute-start | bytes 4616 | tf_op jit(solution)/shard_map/ppermute | solution.py:481
  11.8 0.5 %collective-permute-start.24 = (f32[67,128]{1,0:T(8,128)S(1)}, f32[67,128]{1,0:T(8,128)S(1)}, u32[]{:S(2)}, u32[]{:S(2)}) collective-permute-start(f32[67,128]{1,0:T(8,128)S(1)} %pad_maximum_fusion.11), channel_id=1, source_target_pairs={{0,3},{1,2},{2,1},{3,0},{4,7},{5,6},{6,5},{7,4},{8,11},{9,10},{10,... | collective-permute-start | bytes 102920 | tf_op jit(solution)/shard_map/ppermute | solution.py:481
  12.4 0.3 collective-permute-start.26
  12.7 0.8 %collective-permute-done.25 = f32[3,128]{1,0:T(4,128)S(1)} collective-permute-done((f32[3,128]{1,0:T(4,128)S(1)}, f32[3,128]{1,0:T(4,128)S(1)}, u32[]{:S(2)}, u32[]{:S(2)}) %collective-permute-start.25) | collective-permute-done | bytes 1568 | tf_op jit(solution)/shard_map/ppermute | solution.py:481
  13.5 1.8 %collective-permute-done.24 = f32[67,128]{1,0:T(8,128)S(1)} collective-permute-done((f32[67,128]{1,0:T(8,128)S(1)}, f32[67,128]{1,0:T(8,128)S(1)}, u32[]{:S(2)}, u32[]{:S(2)}) %collective-permute-start.24) | collective-permute-done | bytes 34336 | tf_op jit(solution)/shard_map/ppermute | solution.py:481
  15.3 0.4 collective-permute-done.26.refs_11_
  15.7 3.4 %collective-permute-start.29 = (f32[40,128]{1,0:T(8,128)S(1)}, f32[40,128]{1,0:T(8,128)S(1)}, u32[]{:S(2)}, u32[]{:S(2)}) collective-permute-start(f32[40,128]{1,0:T(8,128)S(1)} %pad_maximum_fusion.15.refs_6_), channel_id=1, source_target_pairs={{0,26},{1,27},{2,24},{3,25},{4,30},{5,31},{6,28},{7,29},{8,18},{9,... | collective-permute-start | bytes 61448 | tf_op jit(solution)/shard_map/ppermute | solution.py:481
  19.2 0.6 %collective-permute-start.27 = (f32[40,128]{1,0:T(8,128)S(1)}, f32[40,128]{1,0:T(8,128)S(1)}, u32[]{:S(2)}, u32[]{:S(2)}) collective-permute-start(f32[40,128]{1,0:T(8,128)S(1)} %pad_maximum_fusion.15.refs_6_), channel_id=1, source_target_pairs={{0,10},{1,11},{2,8},{3,9},{4,14},{5,15},{6,12},{7,13},{8,2},{9,3},... | collective-permute-start | bytes 61448 | tf_op jit(solution)/shard_map/ppermute | solution.py:481
  19.8 0.2 shard_map.168.refs_13_
  20.0 0.8 %collective-permute-done.29.refs_9_ = f32[40,128]{1,0:T(8,128)S(1)} collective-permute-done((f32[40,128]{1,0:T(8,128)S(1)}, f32[40,128]{1,0:T(8,128)S(1)}, u32[]{:S(2)}, u32[]{:S(2)}) %collective-permute-start.29) | collective-permute-done | bytes 20512 | tf_op jit(solution)/shard_map/ppermute | solution.py:481
  20.8 2.5 %collective-permute-done.28.refs_8_ = f32[40,128]{1,0:T(8,128)S(1)} collective-permute-done((f32[40,128]{1,0:T(8,128)S(1)}, f32[40,128]{1,0:T(8,128)S(1)}, u32[]{:S(2)}, u32[]{:S(2)}) %collective-permute-start.28) | collective-permute-done | bytes 20512 | tf_op jit(solution)/shard_map/ppermute | solution.py:481
  23.3 0.8 %shard_map.169 = (f32[17,64,128]{2,1,0:T(8,128)S(1)}, f32[17,64,128]{2,1,0:T(8,128)S(1)}, f32[72,640]{1,0:T(8,128)S(1)}, f32[64,256]{1,0:T(8,128)S(1)}, f32[64,256]{1,0:T(8,128)S(1)}, /*index=5*/f32[88,128]{1,0:T(8,128)S(1)}) custom-call(f32[18,64,128]{2,1,0:T(8,128)S(1)} %get-tuple-element.107.refs_0_, ...), custom_call_target="tpu_custom_call" | custom-call | tf_op jit(solution)/shard_map/pallas_call | solution.py:456
  24.1 0.4 collective-permute-start.30
  24.5 0.9 %collective-permute-done.30 = f32[88,128]{1,0:T(8,128)S(1)} collective-permute-done((f32[88,128]{1,0:T(8,128)S(1)}, f32[88,128]{1,0:T(8,128)S(1)}, u32[]{:S(2)}, u32[]{:S(2)}) %collective-permute-start.30) | collective-permute-done | bytes 45088 | tf_op jit(solution)/shard_map/ppermute | solution.py:481
  25.4 1.5 %collective-permute-start.32 = (f32[3,128]{1,0:T(4,128)S(1)}, f32[3,128]{1,0:T(4,128)S(1)}, u32[]{:S(2)}, u32[]{:S(2)}) collective-permute-start(f32[3,128]{1,0:T(4,128)S(1)} %slice.583), channel_id=1, source_target_pairs={{0,7},{1,6},{2,5},{3,4},{4,3},{5,2},{6,1},{7,0},{8,15},{9,14},{10,... | collective-permute-start | bytes 4616 | tf_op jit(solution)/shard_map/ppermute | solution.py:481
  26.9 0.3 collective-permute-start.31
  27.3 1.5 %collective-permute-start.33 = (f32[24,128]{1,0:T(8,128)S(1)}, f32[24,128]{1,0:T(8,128)S(1)}, u32[]{:S(2)}, u32[]{:S(2)}) collective-permute-start(f32[24,128]{1,0:T(8,128)S(1)} %pad_maximum_fusion.16), channel_id=1, source_target_pairs={{0,6},{1,7},{2,4},{3,5},{4,2},{5,3},{6,0},{7,1},{8,14},{9,15},{10,... | collective-permute-start | bytes 36872 | tf_op jit(solution)/shard_map/ppermute | solution.py:481
  28.8 0.6 %collective-permute-done.32 = f32[3,128]{1,0:T(4,128)S(1)} collective-permute-done((f32[3,128]{1,0:T(4,128)S(1)}, f32[3,128]{1,0:T(4,128)S(1)}, u32[]{:S(2)}, u32[]{:S(2)}) %collective-permute-start.32) | collective-permute-done | bytes 1568 | tf_op jit(solution)/shard_map/ppermute | solution.py:481
  29.3 1.1 %collective-permute-done.31 = f32[67,128]{1,0:T(8,128)S(1)} collective-permute-done((f32[67,128]{1,0:T(8,128)S(1)}, f32[67,128]{1,0:T(8,128)S(1)}, u32[]{:S(2)}, u32[]{:S(2)}) %collective-permute-start.31) | collective-permute-done | bytes 34336 | tf_op jit(solution)/shard_map/ppermute | solution.py:481
  30.4 0.0 collective-permute-done.33.refs_13_
  30.5 1.5 %collective-permute-start.36 = (f32[24,128]{1,0:T(8,128)S(1)}, f32[24,128]{1,0:T(8,128)S(1)}, u32[]{:S(2)}, u32[]{:S(2)}) collective-permute-start(f32[24,128]{1,0:T(8,128)S(1)} %pad_maximum_fusion.17.refs_8_), channel_id=1, source_target_pairs={{0,26},{1,27},{2,24},{3,25},{4,30},{5,31},{6,28},{7,29},{8,18},{9,... | collective-permute-start | bytes 36872 | tf_op jit(solution)/shard_map/ppermute | solution.py:481
  32.0 0.4 collective-permute-start.35
  32.4 2.2 %collective-permute-start.34 = (f32[24,128]{1,0:T(8,128)S(1)}, f32[24,128]{1,0:T(8,128)S(1)}, u32[]{:S(2)}, u32[]{:S(2)}) collective-permute-start(f32[24,128]{1,0:T(8,128)S(1)} %pad_maximum_fusion.17.refs_8_), channel_id=1, source_target_pairs={{0,10},{1,11},{2,8},{3,9},{4,14},{5,15},{6,12},{7,13},{8,2},{9,3},... | collective-permute-start | bytes 36872 | tf_op jit(solution)/shard_map/ppermute | solution.py:481
  34.6 0.2 shard_map.170.refs_15_
  34.9 0.6 %collective-permute-done.36.refs_11_ = f32[24,128]{1,0:T(8,128)S(1)} collective-permute-done((f32[24,128]{1,0:T(8,128)S(1)}, f32[24,128]{1,0:T(8,128)S(1)}, u32[]{:S(2)}, u32[]{:S(2)}) %collective-permute-start.36) | collective-permute-done | bytes 12320 | tf_op jit(solution)/shard_map/ppermute | solution.py:481
  35.5 0.8 %collective-permute-done.35.refs_10_ = f32[24,128]{1,0:T(8,128)S(1)} collective-permute-done((f32[24,128]{1,0:T(8,128)S(1)}, f32[24,128]{1,0:T(8,128)S(1)}, u32[]{:S(2)}, u32[]{:S(2)}) %collective-permute-start.35) | collective-permute-done | bytes 12320 | tf_op jit(solution)/shard_map/ppermute | solution.py:481
  36.2 0.0 collective-permute-done.34.refs_9_
  36.3 0.7 %shard_map.171 = (f32[17,64,128]{2,1,0:T(8,128)S(1)}, f32[17,64,128]{2,1,0:T(8,128)S(1)}, f32[72,640]{1,0:T(8,128)S(1)}, f32[64,256]{1,0:T(8,128)S(1)}, f32[64,256]{1,0:T(8,128)S(1)}, /*index=5*/f32[88,128]{1,0:T(8,128)S(1)}) custom-call(f32[18,64,128]{2,1,0:T(8,128)S(1)} %get-tuple-element.107.refs_0_, ...), custom_call_target="tpu_custom_call" | custom-call | tf_op jit(solution)/shard_map/pallas_call | solution.py:456
  37.0 0.2 collective-permute-start.37
  37.2 1.1 %collective-permute-done.37 = f32[88,128]{1,0:T(8,128)S(1)} collective-permute-done((f32[88,128]{1,0:T(8,128)S(1)}, f32[88,128]{1,0:T(8,128)S(1)}, u32[]{:S(2)}, u32[]{:S(2)}) %collective-permute-start.37) | collective-permute-done | bytes 45088 | tf_op jit(solution)/shard_map/ppermute | solution.py:481
  38.3 2.3 %collective-permute-start.39 = (f32[3,128]{1,0:T(4,128)S(1)}, f32[3,128]{1,0:T(4,128)S(1)}, u32[]{:S(2)}, u32[]{:S(2)}) collective-permute-start(f32[3,128]{1,0:T(4,128)S(1)} %slice.598), channel_id=1, source_target_pairs={{0,7},{1,6},{2,5},{3,4},{4,3},{5,2},{6,1},{7,0},{8,15},{9,14},{10,... | collective-permute-start | bytes 4616 | tf_op jit(solution)/shard_map/ppermute | solution.py:481
  40.6 0.5 %collective-permute-start.38 = (f32[67,128]{1,0:T(8,128)S(1)}, f32[67,128]{1,0:T(8,128)S(1)}, u32[]{:S(2)}, u32[]{:S(2)}) collective-permute-start(f32[67,128]{1,0:T(8,128)S(1)} %pad_maximum_fusion.13), channel_id=1, source_target_pairs={{0,3},{1,2},{2,1},{3,0},{4,7},{5,6},{6,5},{7,4},{8,11},{9,10},{10,... | collective-permute-start | bytes 102920 | tf_op jit(solution)/shard_map/ppermute | solution.py:481
  41.1 0.4 collective-permute-start.40
  41.5 0.8 %collective-permute-done.39 = f32[3,128]{1,0:T(4,128)S(1)} collective-permute-done((f32[3,128]{1,0:T(4,128)S(1)}, f32[3,128]{1,0:T(4,128)S(1)}, u32[]{:S(2)}, u32[]{:S(2)}) %collective-permute-start.39) | collective-permute-done | bytes 1568 | tf_op jit(solution)/shard_map/ppermute | solution.py:481
  42.3 1.8 %collective-permute-done.38 = f32[67,128]{1,0:T(8,128)S(1)} collective-permute-done((f32[67,128]{1,0:T(8,128)S(1)}, f32[67,128]{1,0:T(8,128)S(1)}, u32[]{:S(2)}, u32[]{:S(2)}) %collective-permute-start.38) | collective-permute-done | bytes 34336 | tf_op jit(solution)/shard_map/ppermute | solution.py:481
  44.0 0.3 collective-permute-done.40.refs_13_
  44.4 2.0 %collective-permute-start.43 = (f32[24,128]{1,0:T(8,128)S(1)}, f32[24,128]{1,0:T(8,128)S(1)}, u32[]{:S(2)}, u32[]{:S(2)}) collective-permute-start(f32[24,128]{1,0:T(8,128)S(1)} %pad_maximum_fusion.19.refs_8_), channel_id=1, source_target_pairs={{0,26},{1,27},{2,24},{3,25},{4,30},{5,31},{6,28},{7,29},{8,18},{9,... | collective-permute-start | bytes 36872 | tf_op jit(solution)/shard_map/ppermute | solution.py:481
  46.4 0.8 %collective-permute-start.42 = (f32[24,128]{1,0:T(8,128)S(1)}, f32[24,128]{1,0:T(8,128)S(1)}, u32[]{:S(2)}, u32[]{:S(2)}) collective-permute-start(f32[24,128]{1,0:T(8,128)S(1)} %pad_maximum_fusion.19.refs_8_), channel_id=1, source_target_pairs={{0,18},{1,19},{2,16},{3,17},{4,22},{5,23},{6,20},{7,21},{8,26},{9,... | collective-permute-start | bytes 36872 | tf_op jit(solution)/shard_map/ppermute | solution.py:481
  47.1 1.2 %collective-permute-start.41 = (f32[24,128]{1,0:T(8,128)S(1)}, f32[24,128]{1,0:T(8,128)S(1)}, u32[]{:S(2)}, u32[]{:S(2)}) collective-permute-start(f32[24,128]{1,0:T(8,128)S(1)} %pad_maximum_fusion.19.refs_8_), channel_id=1, source_target_pairs={{0,10},{1,11},{2,8},{3,9},{4,14},{5,15},{6,12},{7,13},{8,2},{9,3},... | collective-permute-start | bytes 36872 | tf_op jit(solution)/shard_map/ppermute | solution.py:481
  48.3 0.2 shard_map.172.refs_15_
  48.6 0.8 %collective-permute-done.43.refs_11_ = f32[24,128]{1,0:T(8,128)S(1)} collective-permute-done((f32[24,128]{1,0:T(8,128)S(1)}, f32[24,128]{1,0:T(8,128)S(1)}, u32[]{:S(2)}, u32[]{:S(2)}) %collective-permute-start.43) | collective-permute-done | bytes 12320 | tf_op jit(solution)/shard_map/ppermute | solution.py:481
  49.4 1.0 %collective-permute-done.42.refs_10_ = f32[24,128]{1,0:T(8,128)S(1)} collective-permute-done((f32[24,128]{1,0:T(8,128)S(1)}, f32[24,128]{1,0:T(8,128)S(1)}, u32[]{:S(2)}, u32[]{:S(2)}) %collective-permute-start.42) | collective-permute-done | bytes 12320 | tf_op jit(solution)/shard_map/ppermute | solution.py:481
  50.4 1.2 %shard_map.173 = (f32[1024,128]{1,0:T(8,128)}, f32[1,128]{1,0:T(1,128)S(1)}, f32[64,128]{1,0:T(8,128)S(1)}, f32[64,256]{1,0:T(8,128)S(1)}, f32[1,128]{1,0:T(1,128)S(1)}, /*index=5*/f32[88,128]{1,0:T(8,128)S(1)}) custom-call(f32[18,64,128]{2,1,0:T(8,128)S(1)} %get-tuple-element.107.refs_0_, bf16[128,512]{1,0:T(8,128)(2,1)S(1)} %get-tuple-element.108.maps_local.refs_1_, ...), custom_call_target="tpu_custom_call" | custom-call | tf_op jit(solution)/shard_map/pallas_call | solution.py:456
  51.7 0.0 copy-start.14
  51.7 0.0 copy-start.12
  51.7 0.0 copy-start.13
  51.7 0.5 copy-done.14
  52.2 0.1 copy-done.12
  52.3 0.0 copy-done.13
  (68 shorter events, 0.3 us)
Async XLA Ops:
  0.6 4.6 %copy-start.11 = (s32[256]{0:T(256)S(1)}, s32[256]{0:T(256)}, u32[]{:S(2)}) copy-start(s32[256]{0:T(256)} %param.30) | copy-start | bytes 3076
  2.1 5.6 %collective-permute-start.22 = (f32[72,128]{1,0:T(8,128)}, f32[72,128]{1,0:T(8,128)S(1)}, u32[]{:S(2)}, u32[]{:S(2)}) collective-permute-start(f32[72,128]{1,0:T(8,128)} %shard_map.166), channel_id=1, source_target_pairs={{0,1},{1,0},{2,3},{3,2},{4,5},{5,4},{6,7},{7,6},{8,9},{9,8},{10,11... | collective-permute-start | bytes 110600 | tf_op jit(solution)/shard_map/ppermute | solution.py:481
  5.1 0.7 %copy-start.10 = (s32[2,256]{1,0:T(2,128)S(1)}, s32[2,256]{1,0:T(2,128)}, u32[]{:S(2)}) copy-start(s32[2,256]{1,0:T(2,128)} %refs_6_.1) | copy-start | bytes 6148
  5.1 0.8 %copy-start.8 = (f32[64,128]{1,0:T(8,128)S(1)}, f32[64,128]{1,0:T(8,128)}, u32[]{:S(2)}) copy-start(f32[64,128]{1,0:T(8,128)} %refs_2_.2) | copy-start | bytes 98308
  5.1 0.8 %copy-start.7 = (f32[64,128]{1,0:T(8,128)S(1)}, f32[64,128]{1,0:T(8,128)}, u32[]{:S(2)}) copy-start(f32[64,128]{1,0:T(8,128)} %refs_0_.1) | copy-start | bytes 98308
  5.1 0.8 %copy-start.5 = (f32[1,128]{1,0:T(1,128)S(1)}, f32[1,128]{1,0:T(1,128)}, u32[]{:S(2)}) copy-start(f32[1,128]{1,0:T(1,128)} %refs_4_.1) | copy-start | bytes 1540
  5.1 0.8 %copy-start.3 = (f32[256]{0:T(256)S(1)}, f32[256]{0:T(256)}, u32[]{:S(2)}) copy-start(f32[256]{0:T(256)} %param.32) | copy-start | bytes 3076
  5.1 0.8 %copy-start.4 = (f32[256]{0:T(256)S(1)}, f32[256]{0:T(256)}, u32[]{:S(2)}) copy-start(f32[256]{0:T(256)} %param.31) | copy-start | bytes 3076
  5.2 0.8 %copy-start.1 = (s32[1,2048]{1,0:T(1,128)S(1)}, s32[1,2048]{1,0:T(1,128)}, u32[]{:S(2)}) copy-start(s32[1,2048]{1,0:T(1,128)} %param.24) | copy-start | bytes 24580
  5.2 0.8 %copy-start = (f32[16,128]{1,0:T(8,128)S(1)}, f32[16,128]{1,0:T(8,128)}, u32[]{:S(2)}) copy-start(f32[16,128]{1,0:T(8,128)} %refs_3_.2) | copy-start | bytes 24580
  5.2 0.7 %copy-start.2 = (f32[256]{0:T(256)S(1)}, f32[256]{0:T(256)}, u32[]{:S(2)}) copy-start(f32[256]{0:T(256)} %param.26) | copy-start | bytes 3076
  5.9 1.8 %copy-start.9 = (f32[72,128]{1,0:T(8,128)S(1)}, f32[72,128]{1,0:T(8,128)}, u32[]{:S(2)}) copy-start(f32[72,128]{1,0:T(8,128)} %shard_map.166) | copy-start | bytes 110596
  8.2 1.3 %collective-permute-start.23 = (f32[104,128]{1,0:T(8,128)S(1)}, f32[104,128]{1,0:T(8,128)S(1)}, u32[]{:S(2)}, u32[]{:S(2)}) collective-permute-start(f32[104,128]{1,0:T(8,128)S(1)} %get-tuple-element.116), channel_id=1, source_target_pairs={{0,2},{1,3},{2,0},{3,1},{4,6},{5,7},{6,4},{7,5},{8,10},{9,11},{10,... | collective-permute-start | bytes 159752 | tf_op jit(solution)/shard_map/ppermute | solution.py:481
  9.5 4.0 %collective-permute-start.25 = (f32[3,128]{1,0:T(4,128)S(1)}, f32[3,128]{1,0:T(4,128)S(1)}, u32[]{:S(2)}, u32[]{:S(2)}) collective-permute-start(f32[3,128]{1,0:T(4,128)S(1)} %slice.568), channel_id=1, source_target_pairs={{0,7},{1,6},{2,5},{3,4},{4,3},{5,2},{6,1},{7,0},{8,15},{9,14},{10,... | collective-permute-start | bytes 4616 | tf_op jit(solution)/shard_map/ppermute | solution.py:481
  11.8 3.4 %collective-permute-start.24 = (f32[67,128]{1,0:T(8,128)S(1)}, f32[67,128]{1,0:T(8,128)S(1)}, u32[]{:S(2)}, u32[]{:S(2)}) collective-permute-start(f32[67,128]{1,0:T(8,128)S(1)} %pad_maximum_fusion.11), channel_id=1, source_target_pairs={{0,3},{1,2},{2,1},{3,0},{4,7},{5,6},{6,5},{7,4},{8,11},{9,10},{10,... | collective-permute-start | bytes 102920 | tf_op jit(solution)/shard_map/ppermute | solution.py:481
  12.4 3.3 %collective-permute-start.26 = (f32[40,128]{1,0:T(8,128)S(1)}, f32[40,128]{1,0:T(8,128)S(1)}, u32[]{:S(2)}, u32[]{:S(2)}) collective-permute-start(f32[40,128]{1,0:T(8,128)S(1)} %pad_maximum_fusion.14), channel_id=1, source_target_pairs={{0,6},{1,7},{2,4},{3,5},{4,2},{5,3},{6,0},{7,1},{8,14},{9,15},{10,... | collective-permute-start | bytes 61448 | tf_op jit(solution)/shard_map/ppermute | solution.py:481
  15.7 5.1 %collective-permute-start.29 = (f32[40,128]{1,0:T(8,128)S(1)}, f32[40,128]{1,0:T(8,128)S(1)}, u32[]{:S(2)}, u32[]{:S(2)}) collective-permute-start(f32[40,128]{1,0:T(8,128)S(1)} %pad_maximum_fusion.15.refs_6_), channel_id=1, source_target_pairs={{0,26},{1,27},{2,24},{3,25},{4,30},{5,31},{6,28},{7,29},{8,18},{9,... | collective-permute-start | bytes 61448 | tf_op jit(solution)/shard_map/ppermute | solution.py:481
  19.2 4.1 %collective-permute-start.28 = (f32[40,128]{1,0:T(8,128)S(1)}, f32[40,128]{1,0:T(8,128)S(1)}, u32[]{:S(2)}, u32[]{:S(2)}) collective-permute-start(f32[40,128]{1,0:T(8,128)S(1)} %pad_maximum_fusion.15.refs_6_), channel_id=1, source_target_pairs={{0,18},{1,19},{2,16},{3,17},{4,22},{5,23},{6,20},{7,21},{8,26},{9,... | collective-permute-start | bytes 61448 | tf_op jit(solution)/shard_map/ppermute | solution.py:481
  19.2 4.1 %collective-permute-start.27 = (f32[40,128]{1,0:T(8,128)S(1)}, f32[40,128]{1,0:T(8,128)S(1)}, u32[]{:S(2)}, u32[]{:S(2)}) collective-permute-start(f32[40,128]{1,0:T(8,128)S(1)} %pad_maximum_fusion.15.refs_6_), channel_id=1, source_target_pairs={{0,10},{1,11},{2,8},{3,9},{4,14},{5,15},{6,12},{7,13},{8,2},{9,3},... | collective-permute-start | bytes 61448 | tf_op jit(solution)/shard_map/ppermute | solution.py:481
  24.1 1.3 %collective-permute-start.30 = (f32[88,128]{1,0:T(8,128)S(1)}, f32[88,128]{1,0:T(8,128)S(1)}, u32[]{:S(2)}, u32[]{:S(2)}) collective-permute-start(f32[88,128]{1,0:T(8,128)S(1)} %get-tuple-element.122), channel_id=1, source_target_pairs={{0,2},{1,3},{2,0},{3,1},{4,6},{5,7},{6,4},{7,5},{8,10},{9,11},{10,... | collective-permute-start | bytes 135176 | tf_op jit(solution)/shard_map/ppermute | solution.py:481
  25.4 4.0 %collective-permute-start.32 = (f32[3,128]{1,0:T(4,128)S(1)}, f32[3,128]{1,0:T(4,128)S(1)}, u32[]{:S(2)}, u32[]{:S(2)}) collective-permute-start(f32[3,128]{1,0:T(4,128)S(1)} %slice.583), channel_id=1, source_target_pairs={{0,7},{1,6},{2,5},{3,4},{4,3},{5,2},{6,1},{7,0},{8,15},{9,14},{10,... | collective-permute-start | bytes 4616 | tf_op jit(solution)/shard_map/ppermute | solution.py:481
  26.9 3.5 %collective-permute-start.31 = (f32[67,128]{1,0:T(8,128)S(1)}, f32[67,128]{1,0:T(8,128)S(1)}, u32[]{:S(2)}, u32[]{:S(2)}) collective-permute-start(f32[67,128]{1,0:T(8,128)S(1)} %pad_maximum_fusion.12), channel_id=1, source_target_pairs={{0,3},{1,2},{2,1},{3,0},{4,7},{5,6},{6,5},{7,4},{8,11},{9,10},{10,... | collective-permute-start | bytes 102920 | tf_op jit(solution)/shard_map/ppermute | solution.py:481
  27.3 3.2 %collective-permute-start.33 = (f32[24,128]{1,0:T(8,128)S(1)}, f32[24,128]{1,0:T(8,128)S(1)}, u32[]{:S(2)}, u32[]{:S(2)}) collective-permute-start(f32[24,128]{1,0:T(8,128)S(1)} %pad_maximum_fusion.16), channel_id=1, source_target_pairs={{0,6},{1,7},{2,4},{3,5},{4,2},{5,3},{6,0},{7,1},{8,14},{9,15},{10,... | collective-permute-start | bytes 36872 | tf_op jit(solution)/shard_map/ppermute | solution.py:481
  30.5 5.0 %collective-permute-start.36 = (f32[24,128]{1,0:T(8,128)S(1)}, f32[24,128]{1,0:T(8,128)S(1)}, u32[]{:S(2)}, u32[]{:S(2)}) collective-permute-start(f32[24,128]{1,0:T(8,128)S(1)} %pad_maximum_fusion.17.refs_8_), channel_id=1, source_target_pairs={{0,26},{1,27},{2,24},{3,25},{4,30},{5,31},{6,28},{7,29},{8,18},{9,... | collective-permute-start | bytes 36872 | tf_op jit(solution)/shard_map/ppermute | solution.py:481
  32.0 4.2 %collective-permute-start.35 = (f32[24,128]{1,0:T(8,128)S(1)}, f32[24,128]{1,0:T(8,128)S(1)}, u32[]{:S(2)}, u32[]{:S(2)}) collective-permute-start(f32[24,128]{1,0:T(8,128)S(1)} %pad_maximum_fusion.17.refs_8_), channel_id=1, source_target_pairs={{0,18},{1,19},{2,16},{3,17},{4,22},{5,23},{6,20},{7,21},{8,26},{9,... | collective-permute-start | bytes 36872 | tf_op jit(solution)/shard_map/ppermute | solution.py:481
  32.4 3.9 %collective-permute-start.34 = (f32[24,128]{1,0:T(8,128)S(1)}, f32[24,128]{1,0:T(8,128)S(1)}, u32[]{:S(2)}, u32[]{:S(2)}) collective-permute-start(f32[24,128]{1,0:T(8,128)S(1)} %pad_maximum_fusion.17.refs_8_), channel_id=1, source_target_pairs={{0,10},{1,11},{2,8},{3,9},{4,14},{5,15},{6,12},{7,13},{8,2},{9,3},... | collective-permute-start | bytes 36872 | tf_op jit(solution)/shard_map/ppermute | solution.py:481
  37.0 1.3 %collective-permute-start.37 = (f32[88,128]{1,0:T(8,128)S(1)}, f32[88,128]{1,0:T(8,128)S(1)}, u32[]{:S(2)}, u32[]{:S(2)}) collective-permute-start(f32[88,128]{1,0:T(8,128)S(1)} %get-tuple-element.128), channel_id=1, source_target_pairs={{0,2},{1,3},{2,0},{3,1},{4,6},{5,7},{6,4},{7,5},{8,10},{9,11},{10,... | collective-permute-start | bytes 135176 | tf_op jit(solution)/shard_map/ppermute | solution.py:481
  38.3 4.0 %collective-permute-start.39 = (f32[3,128]{1,0:T(4,128)S(1)}, f32[3,128]{1,0:T(4,128)S(1)}, u32[]{:S(2)}, u32[]{:S(2)}) collective-permute-start(f32[3,128]{1,0:T(4,128)S(1)} %slice.598), channel_id=1, source_target_pairs={{0,7},{1,6},{2,5},{3,4},{4,3},{5,2},{6,1},{7,0},{8,15},{9,14},{10,... | collective-permute-start | bytes 4616 | tf_op jit(solution)/shard_map/ppermute | solution.py:481
  40.6 3.5 %collective-permute-start.38 = (f32[67,128]{1,0:T(8,128)S(1)}, f32[67,128]{1,0:T(8,128)S(1)}, u32[]{:S(2)}, u32[]{:S(2)}) collective-permute-start(f32[67,128]{1,0:T(8,128)S(1)} %pad_maximum_fusion.13), channel_id=1, source_target_pairs={{0,3},{1,2},{2,1},{3,0},{4,7},{5,6},{6,5},{7,4},{8,11},{9,10},{10,... | collective-permute-start | bytes 102920 | tf_op jit(solution)/shard_map/ppermute | solution.py:481
  41.1 3.2 %collective-permute-start.40 = (f32[24,128]{1,0:T(8,128)S(1)}, f32[24,128]{1,0:T(8,128)S(1)}, u32[]{:S(2)}, u32[]{:S(2)}) collective-permute-start(f32[24,128]{1,0:T(8,128)S(1)} %pad_maximum_fusion.18), channel_id=1, source_target_pairs={{0,6},{1,7},{2,4},{3,5},{4,2},{5,3},{6,0},{7,1},{8,14},{9,15},{10,... | collective-permute-start | bytes 36872 | tf_op jit(solution)/shard_map/ppermute | solution.py:481
  44.4 5.0 %collective-permute-start.43 = (f32[24,128]{1,0:T(8,128)S(1)}, f32[24,128]{1,0:T(8,128)S(1)}, u32[]{:S(2)}, u32[]{:S(2)}) collective-permute-start(f32[24,128]{1,0:T(8,128)S(1)} %pad_maximum_fusion.19.refs_8_), channel_id=1, source_target_pairs={{0,26},{1,27},{2,24},{3,25},{4,30},{5,31},{6,28},{7,29},{8,18},{9,... | collective-permute-start | bytes 36872 | tf_op jit(solution)/shard_map/ppermute | solution.py:481
  46.4 4.0 %collective-permute-start.42 = (f32[24,128]{1,0:T(8,128)S(1)}, f32[24,128]{1,0:T(8,128)S(1)}, u32[]{:S(2)}, u32[]{:S(2)}) collective-permute-start(f32[24,128]{1,0:T(8,128)S(1)} %pad_maximum_fusion.19.refs_8_), channel_id=1, source_target_pairs={{0,18},{1,19},{2,16},{3,17},{4,22},{5,23},{6,20},{7,21},{8,26},{9,... | collective-permute-start | bytes 36872 | tf_op jit(solution)/shard_map/ppermute | solution.py:481
  47.1 3.3 %collective-permute-start.41 = (f32[24,128]{1,0:T(8,128)S(1)}, f32[24,128]{1,0:T(8,128)S(1)}, u32[]{:S(2)}, u32[]{:S(2)}) collective-permute-start(f32[24,128]{1,0:T(8,128)S(1)} %pad_maximum_fusion.19.refs_8_), channel_id=1, source_target_pairs={{0,10},{1,11},{2,8},{3,9},{4,14},{5,15},{6,12},{7,13},{8,2},{9,3},... | collective-permute-start | bytes 36872 | tf_op jit(solution)/shard_map/ppermute | solution.py:481
  50.4 1.3 %copy-start.6 = (f32[64,16,128]{2,1,0:T(8,128)S(1)}, f32[64,16,128]{2,1,0:T(8,128)}, u32[]{:S(2)}) copy-start(f32[64,16,128]{2,1,0:T(8,128)} %param.20) | copy-start | bytes 1572868
  51.7 0.5 copy-start.14
  51.7 0.6 %copy-start.12 = (f32[64,256]{1,0:T(8,128)}, f32[64,256]{1,0:T(8,128)S(1)}, u32[]{:S(2)}) copy-start(f32[64,256]{1,0:T(8,128)S(1)} %get-tuple-element.137) | copy-start | bytes 196612
  51.7 0.6 %copy-start.13 = (f32[64,128]{1,0:T(8,128)}, f32[64,128]{1,0:T(8,128)S(1)}, u32[]{:S(2)}) copy-start(f32[64,128]{1,0:T(8,128)S(1)} %get-tuple-element.136) | copy-start | bytes 98308

commit v24 on v23

--- a/solution.py
+++ b/solution.py
@@ -13,7 +13,7 @@
 LANES = 128
 VMEM_BYTES = 24 * 1024 * 1024
 FIRST_BYTES = 56 * 1024 * 1024
-PARTS = 4
+PARTS = 8
 SQUARES = 3
 
 

time: 52.6 us -> 52.6 us (level)
  no operation moved by 1% of the time
where the time goes in v24:
time: 52.6 us; the launch traced here: 52.3 us
  starting transfers between devices  25.5 us (48%)
  waiting for transfers between devices  17.1 us (33%)
  Pallas kernels  6.99 us (13%)
  local copies, waits for them, and re-layouts  1.46 us (3%)
  between operations  1.04 us (2%)
    ppermute x22, starting transfers between devices, swap(): return lax.ppermute(value, ('hours', 'region'), pairs)  25.5 us
    ppermute x22, waiting for transfers between devices, swap(): return lax.ppermute(value, ('hours', 'region'), pairs)  17.1 us
    pallas_call x9, Pallas kernels, call(): pl.pallas_call(functools.partial(kernel, names_in, names_out), out_shape=...  6.99 us
    unnamed x30, local copies, waits for them, and re-layouts  1.38 us
  transfers between devices with their start and end apart: 22, of which 17 were waited for; matrix products, arithmetic and copies ran while one was open for 0% of the time, Pallas kernels for 5%

profile of v24, /device:TPU:0, one launch (start us, length us, event | category | flops | bytes accessed | tf_op | source)
XLA Modules:
  0.0 52.3 jit_solution(2015250842392604693)
XLA Ops:
  0.6 1.4 %shard_map.166 = f32[72,128]{1,0:T(8,128)} custom-call(f32[64,128]{1,0:T(8,128)} %refs_0_.1, s32[2,64]{1,0:T(2,128)} %bitcast.122, f32[1,64]{1,0:T(1,128)} %refs_2_.3, s32[1,2]{1,0:T(1,128)} %refs_3_.3), custom_call_target="tpu_custom_call" | custom-call | tf_op jit(solution)/shard_map/pallas_call | solution.py:456
  2.1 3.0 %collective-permute-start.22 = (f32[72,128]{1,0:T(8,128)}, f32[72,128]{1,0:T(8,128)S(1)}, u32[]{:S(2)}, u32[]{:S(2)}) collective-permute-start(f32[72,128]{1,0:T(8,128)} %shard_map.166), channel_id=1, source_target_pairs={{0,1},{1,0},{2,3},{3,2},{4,5},{5,4},{6,7},{7,6},{8,9},{9,8},{10,11... | collective-permute-start | bytes 110600 | tf_op jit(solution)/shard_map/ppermute | solution.py:481
  5.1 0.0 copy-start.3
  5.1 0.0 copy-start.4
  5.2 0.0 copy-start.1
  5.2 0.0 copy-start
  5.2 0.0 copy-start.2
  5.2 0.6 %copy-done.10 = s32[2,256]{1,0:T(2,128)S(1)} copy-done((s32[2,256]{1,0:T(2,128)S(1)}, s32[2,256]{1,0:T(2,128)}, u32[]{:S(2)}) %copy-start.10) | copy-done | bytes 2072
  5.8 0.1 copy-done.8
  5.9 0.0 copy-done.7
  5.9 0.0 copy-done
  5.9 1.7 %shard_map.165 = (f32[18,64,128]{2,1,0:T(8,128)S(1)}, bf16[128,512]{1,0:T(8,128)(2,1)S(1)}, f32[64,512]{1,0:T(8,128)S(1)}, f32[64,256]{1,0:T(8,128)S(1)}, f32[17...) custom-call(f32[1024,128]{1,0:T(8,128)} %bitcast.88, f32[64,128]{1,0:T(8,128)S(1)} %copy-done.7, ...), custom_call_target="tpu_custom_call" | custom-call | flops 1000000 | bytes 4000000 | tf_op jit(solution)/shard_map/pallas_call | solution.py:456
  7.7 0.4 shard_map.167
  8.2 0.1 collective-permute-start.23
  8.3 1.2 %collective-permute-done.23 = f32[104,128]{1,0:T(8,128)S(1)} collective-permute-done((f32[104,128]{1,0:T(8,128)S(1)}, f32[104,128]{1,0:T(8,128)S(1)}, u32[]{:S(2)}, u32[]{:S(2)}) %collective-permute-start.23) | collective-permute-done | bytes 53280 | tf_op jit(solution)/shard_map/ppermute | solution.py:481
  9.5 2.3 %collective-permute-start.25 = (f32[3,128]{1,0:T(4,128)S(1)}, f32[3,128]{1,0:T(4,128)S(1)}, u32[]{:S(2)}, u32[]{:S(2)}) collective-permute-start(f32[3,128]{1,0:T(4,128)S(1)} %slice.568), channel_id=1, source_target_pairs={{0,7},{1,6},{2,5},{3,4},{4,3},{5,2},{6,1},{7,0},{8,15},{9,14},{10,... | collective-permute-start | bytes 4616 | tf_op jit(solution)/shard_map/ppermute | solution.py:481
  11.8 0.5 %collective-permute-start.24 = (f32[67,128]{1,0:T(8,128)S(1)}, f32[67,128]{1,0:T(8,128)S(1)}, u32[]{:S(2)}, u32[]{:S(2)}) collective-permute-start(f32[67,128]{1,0:T(8,128)S(1)} %pad_maximum_fusion.11), channel_id=1, source_target_pairs={{0,3},{1,2},{2,1},{3,0},{4,7},{5,6},{6,5},{7,4},{8,11},{9,10},{10,... | collective-permute-start | bytes 102920 | tf_op jit(solution)/shard_map/ppermute | solution.py:481
  12.4 0.3 collective-permute-start.26
  12.7 0.8 %collective-permute-done.25 = f32[3,128]{1,0:T(4,128)S(1)} collective-permute-done((f32[3,128]{1,0:T(4,128)S(1)}, f32[3,128]{1,0:T(4,128)S(1)}, u32[]{:S(2)}, u32[]{:S(2)}) %collective-permute-start.25) | collective-permute-done | bytes 1568 | tf_op jit(solution)/shard_map/ppermute | solution.py:481
  13.5 1.8 %collective-permute-done.24 = f32[67,128]{1,0:T(8,128)S(1)} collective-permute-done((f32[67,128]{1,0:T(8,128)S(1)}, f32[67,128]{1,0:T(8,128)S(1)}, u32[]{:S(2)}, u32[]{:S(2)}) %collective-permute-start.24) | collective-permute-done | bytes 34336 | tf_op jit(solution)/shard_map/ppermute | solution.py:481
  15.3 0.4 collective-permute-done.26.refs_11_
  15.7 3.4 %collective-permute-start.29 = (f32[40,128]{1,0:T(8,128)S(1)}, f32[40,128]{1,0:T(8,128)S(1)}, u32[]{:S(2)}, u32[]{:S(2)}) collective-permute-start(f32[40,128]{1,0:T(8,128)S(1)} %pad_maximum_fusion.15.refs_6_), channel_id=1, source_target_pairs={{0,26},{1,27},{2,24},{3,25},{4,30},{5,31},{6,28},{7,29},{8,18},{9,... | collective-permute-start | bytes 61448 | tf_op jit(solution)/shard_map/ppermute | solution.py:481
  19.2 0.6 %collective-permute-start.27 = (f32[40,128]{1,0:T(8,128)S(1)}, f32[40,128]{1,0:T(8,128)S(1)}, u32[]{:S(2)}, u32[]{:S(2)}) collective-permute-start(f32[40,128]{1,0:T(8,128)S(1)} %pad_maximum_fusion.15.refs_6_), channel_id=1, source_target_pairs={{0,10},{1,11},{2,8},{3,9},{4,14},{5,15},{6,12},{7,13},{8,2},{9,3},... | collective-permute-start | bytes 61448 | tf_op jit(solution)/shard_map/ppermute | solution.py:481
  19.8 0.2 shard_map.168.refs_13_
  20.0 0.8 %collective-permute-done.29.refs_9_ = f32[40,128]{1,0:T(8,128)S(1)} collective-permute-done((f32[40,128]{1,0:T(8,128)S(1)}, f32[40,128]{1,0:T(8,128)S(1)}, u32[]{:S(2)}, u32[]{:S(2)}) %collective-permute-start.29) | collective-permute-done | bytes 20512 | tf_op jit(solution)/shard_map/ppermute | solution.py:481
  20.8 2.5 %collective-permute-done.28.refs_8_ = f32[40,128]{1,0:T(8,128)S(1)} collective-permute-done((f32[40,128]{1,0:T(8,128)S(1)}, f32[40,128]{1,0:T(8,128)S(1)}, u32[]{:S(2)}, u32[]{:S(2)}) %collective-permute-start.28) | collective-permute-done | bytes 20512 | tf_op jit(solution)/shard_map/ppermute | solution.py:481
  23.3 0.8 %shard_map.169 = (f32[17,64,128]{2,1,0:T(8,128)S(1)}, f32[17,64,128]{2,1,0:T(8,128)S(1)}, f32[72,640]{1,0:T(8,128)S(1)}, f32[64,256]{1,0:T(8,128)S(1)}, f32[64,256]{1,0:T(8,128)S(1)}, /*index=5*/f32[88,128]{1,0:T(8,128)S(1)}) custom-call(f32[18,64,128]{2,1,0:T(8,128)S(1)} %get-tuple-element.107.refs_0_, ...), custom_call_target="tpu_custom_call" | custom-call | tf_op jit(solution)/shard_map/pallas_call | solution.py:456
  24.1 0.4 collective-permute-start.30
  24.5 0.9 %collective-permute-done.30 = f32[88,128]{1,0:T(8,128)S(1)} collective-permute-done((f32[88,128]{1,0:T(8,128)S(1)}, f32[88,128]{1,0:T(8,128)S(1)}, u32[]{:S(2)}, u32[]{:S(2)}) %collective-permute-start.30) | collective-permute-done | bytes 45088 | tf_op jit(solution)/shard_map/ppermute | solution.py:481
  25.4 1.5 %collective-permute-start.32 = (f32[3,128]{1,0:T(4,128)S(1)}, f32[3,128]{1,0:T(4,128)S(1)}, u32[]{:S(2)}, u32[]{:S(2)}) collective-permute-start(f32[3,128]{1,0:T(4,128)S(1)} %slice.583), channel_id=1, source_target_pairs={{0,7},{1,6},{2,5},{3,4},{4,3},{5,2},{6,1},{7,0},{8,15},{9,14},{10,... | collective-permute-start | bytes 4616 | tf_op jit(solution)/shard_map/ppermute | solution.py:481
  26.9 0.3 collective-permute-start.31
  27.3 1.5 %collective-permute-start.33 = (f32[24,128]{1,0:T(8,128)S(1)}, f32[24,128]{1,0:T(8,128)S(1)}, u32[]{:S(2)}, u32[]{:S(2)}) collective-permute-start(f32[24,128]{1,0:T(8,128)S(1)} %pad_maximum_fusion.16), channel_id=1, source_target_pairs={{0,6},{1,7},{2,4},{3,5},{4,2},{5,3},{6,0},{7,1},{8,14},{9,15},{10,... | collective-permute-start | bytes 36872 | tf_op jit(solution)/shard_map/ppermute | solution.py:481
  28.8 0.6 %collective-permute-done.32 = f32[3,128]{1,0:T(4,128)S(1)} collective-permute-done((f32[3,128]{1,0:T(4,128)S(1)}, f32[3,128]{1,0:T(4,128)S(1)}, u32[]{:S(2)}, u32[]{:S(2)}) %collective-permute-start.32) | collective-permute-done | bytes 1568 | tf_op jit(solution)/shard_map/ppermute | solution.py:481
  29.3 1.1 %collective-permute-done.31 = f32[67,128]{1,0:T(8,128)S(1)} collective-permute-done((f32[67,128]{1,0:T(8,128)S(1)}, f32[67,128]{1,0:T(8,128)S(1)}, u32[]{:S(2)}, u32[]{:S(2)}) %collective-permute-start.31) | collective-permute-done | bytes 34336 | tf_op jit(solution)/shard_map/ppermute | solution.py:481
  30.4 0.0 collective-permute-done.33.refs_13_
  30.5 1.5 %collective-permute-start.36 = (f32[24,128]{1,0:T(8,128)S(1)}, f32[24,128]{1,0:T(8,128)S(1)}, u32[]{:S(2)}, u32[]{:S(2)}) collective-permute-start(f32[24,128]{1,0:T(8,128)S(1)} %pad_maximum_fusion.17.refs_8_), channel_id=1, source_target_pairs={{0,26},{1,27},{2,24},{3,25},{4,30},{5,31},{6,28},{7,29},{8,18},{9,... | collective-permute-start | bytes 36872 | tf_op jit(solution)/shard_map/ppermute | solution.py:481
  32.0 0.4 collective-permute-start.35
  32.4 2.2 %collective-permute-start.34 = (f32[24,128]{1,0:T(8,128)S(1)}, f32[24,128]{1,0:T(8,128)S(1)}, u32[]{:S(2)}, u32[]{:S(2)}) collective-permute-start(f32[24,128]{1,0:T(8,128)S(1)} %pad_maximum_fusion.17.refs_8_), channel_id=1, source_target_pairs={{0,10},{1,11},{2,8},{3,9},{4,14},{5,15},{6,12},{7,13},{8,2},{9,3},... | collective-permute-start | bytes 36872 | tf_op jit(solution)/shard_map/ppermute | solution.py:481
  34.6 0.2 shard_map.170.refs_15_
  34.9 0.6 %collective-permute-done.36.refs_11_ = f32[24,128]{1,0:T(8,128)S(1)} collective-permute-done((f32[24,128]{1,0:T(8,128)S(1)}, f32[24,128]{1,0:T(8,128)S(1)}, u32[]{:S(2)}, u32[]{:S(2)}) %collective-permute-start.36) | collective-permute-done | bytes 12320 | tf_op jit(solution)/shard_map/ppermute | solution.py:481
  35.5 0.8 %collective-permute-done.35.refs_10_ = f32[24,128]{1,0:T(8,128)S(1)} collective-permute-done((f32[24,128]{1,0:T(8,128)S(1)}, f32[24,128]{1,0:T(8,128)S(1)}, u32[]{:S(2)}, u32[]{:S(2)}) %collective-permute-start.35) | collective-permute-done | bytes 12320 | tf_op jit(solution)/shard_map/ppermute | solution.py:481
  36.2 0.0 collective-permute-done.34.refs_9_
  36.3 0.7 %shard_map.171 = (f32[17,64,128]{2,1,0:T(8,128)S(1)}, f32[17,64,128]{2,1,0:T(8,128)S(1)}, f32[72,640]{1,0:T(8,128)S(1)}, f32[64,256]{1,0:T(8,128)S(1)}, f32[64,256]{1,0:T(8,128)S(1)}, /*index=5*/f32[88,128]{1,0:T(8,128)S(1)}) custom-call(f32[18,64,128]{2,1,0:T(8,128)S(1)} %get-tuple-element.107.refs_0_, ...), custom_call_target="tpu_custom_call" | custom-call | tf_op jit(solution)/shard_map/pallas_call | solution.py:456
  37.0 0.2 collective-permute-start.37
  37.2 1.1 %collective-permute-done.37 = f32[88,128]{1,0:T(8,128)S(1)} collective-permute-done((f32[88,128]{1,0:T(8,128)S(1)}, f32[88,128]{1,0:T(8,128)S(1)}, u32[]{:S(2)}, u32[]{:S(2)}) %collective-permute-start.37) | collective-permute-done | bytes 45088 | tf_op jit(solution)/shard_map/ppermute | solution.py:481
  38.3 2.3 %collective-permute-start.39 = (f32[3,128]{1,0:T(4,128)S(1)}, f32[3,128]{1,0:T(4,128)S(1)}, u32[]{:S(2)}, u32[]{:S(2)}) collective-permute-start(f32[3,128]{1,0:T(4,128)S(1)} %slice.598), channel_id=1, source_target_pairs={{0,7},{1,6},{2,5},{3,4},{4,3},{5,2},{6,1},{7,0},{8,15},{9,14},{10,... | collective-permute-start | bytes 4616 | tf_op jit(solution)/shard_map/ppermute | solution.py:481
  40.6 0.5 %collective-permute-start.38 = (f32[67,128]{1,0:T(8,128)S(1)}, f32[67,128]{1,0:T(8,128)S(1)}, u32[]{:S(2)}, u32[]{:S(2)}) collective-permute-start(f32[67,128]{1,0:T(8,128)S(1)} %pad_maximum_fusion.13), channel_id=1, source_target_pairs={{0,3},{1,2},{2,1},{3,0},{4,7},{5,6},{6,5},{7,4},{8,11},{9,10},{10,... | collective-permute-start | bytes 102920 | tf_op jit(solution)/shard_map/ppermute | solution.py:481
  41.1 0.4 collective-permute-start.40
  41.5 0.8 %collective-permute-done.39 = f32[3,128]{1,0:T(4,128)S(1)} collective-permute-done((f32[3,128]{1,0:T(4,128)S(1)}, f32[3,128]{1,0:T(4,128)S(1)}, u32[]{:S(2)}, u32[]{:S(2)}) %collective-permute-start.39) | collective-permute-done | bytes 1568 | tf_op jit(solution)/shard_map/ppermute | solution.py:481
  42.3 1.8 %collective-permute-done.38 = f32[67,128]{1,0:T(8,128)S(1)} collective-permute-done((f32[67,128]{1,0:T(8,128)S(1)}, f32[67,128]{1,0:T(8,128)S(1)}, u32[]{:S(2)}, u32[]{:S(2)}) %collective-permute-start.38) | collective-permute-done | bytes 34336 | tf_op jit(solution)/shard_map/ppermute | solution.py:481
  44.0 0.3 collective-permute-done.40.refs_13_
  44.4 2.0 %collective-permute-start.43 = (f32[24,128]{1,0:T(8,128)S(1)}, f32[24,128]{1,0:T(8,128)S(1)}, u32[]{:S(2)}, u32[]{:S(2)}) collective-permute-start(f32[24,128]{1,0:T(8,128)S(1)} %pad_maximum_fusion.19.refs_8_), channel_id=1, source_target_pairs={{0,26},{1,27},{2,24},{3,25},{4,30},{5,31},{6,28},{7,29},{8,18},{9,... | collective-permute-start | bytes 36872 | tf_op jit(solution)/shard_map/ppermute | solution.py:481
  46.4 0.8 %collective-permute-start.42 = (f32[24,128]{1,0:T(8,128)S(1)}, f32[24,128]{1,0:T(8,128)S(1)}, u32[]{:S(2)}, u32[]{:S(2)}) collective-permute-start(f32[24,128]{1,0:T(8,128)S(1)} %pad_maximum_fusion.19.refs_8_), channel_id=1, source_target_pairs={{0,18},{1,19},{2,16},{3,17},{4,22},{5,23},{6,20},{7,21},{8,26},{9,... | collective-permute-start | bytes 36872 | tf_op jit(solution)/shard_map/ppermute | solution.py:481
  47.1 1.2 %collective-permute-start.41 = (f32[24,128]{1,0:T(8,128)S(1)}, f32[24,128]{1,0:T(8,128)S(1)}, u32[]{:S(2)}, u32[]{:S(2)}) collective-permute-start(f32[24,128]{1,0:T(8,128)S(1)} %pad_maximum_fusion.19.refs_8_), channel_id=1, source_target_pairs={{0,10},{1,11},{2,8},{3,9},{4,14},{5,15},{6,12},{7,13},{8,2},{9,3},... | collective-permute-start | bytes 36872 | tf_op jit(solution)/shard_map/ppermute | solution.py:481
  48.3 0.2 shard_map.172.refs_15_
  48.6 0.8 %collective-permute-done.43.refs_11_ = f32[24,128]{1,0:T(8,128)S(1)} collective-permute-done((f32[24,128]{1,0:T(8,128)S(1)}, f32[24,128]{1,0:T(8,128)S(1)}, u32[]{:S(2)}, u32[]{:S(2)}) %collective-permute-start.43) | collective-permute-done | bytes 12320 | tf_op jit(solution)/shard_map/ppermute | solution.py:481
  49.4 1.0 %collective-permute-done.42.refs_10_ = f32[24,128]{1,0:T(8,128)S(1)} collective-permute-done((f32[24,128]{1,0:T(8,128)S(1)}, f32[24,128]{1,0:T(8,128)S(1)}, u32[]{:S(2)}, u32[]{:S(2)}) %collective-permute-start.42) | collective-permute-done | bytes 12320 | tf_op jit(solution)/shard_map/ppermute | solution.py:481
  50.4 1.2 %shard_map.173 = (f32[1024,128]{1,0:T(8,128)}, f32[1,128]{1,0:T(1,128)S(1)}, f32[64,128]{1,0:T(8,128)S(1)}, f32[64,256]{1,0:T(8,128)S(1)}, f32[1,128]{1,0:T(1,128)S(1)}, /*index=5*/f32[88,128]{1,0:T(8,128)S(1)}) custom-call(f32[18,64,128]{2,1,0:T(8,128)S(1)} %get-tuple-element.107.refs_0_, bf16[128,512]{1,0:T(8,128)(2,1)S(1)} %get-tuple-element.108.maps_local.refs_1_, ...), custom_call_target="tpu_custom_call" | custom-call | tf_op jit(solution)/shard_map/pallas_call | solution.py:456
  51.7 0.0 copy-start.14
  51.7 0.0 copy-start.12
  51.7 0.0 copy-start.13
  51.7 0.5 copy-done.14
  52.2 0.1 copy-done.12
  52.3 0.0 copy-done.13
  (68 shorter events, 0.3 us)
Async XLA Ops:
  0.6 4.6 %copy-start.11 = (s32[256]{0:T(256)S(1)}, s32[256]{0:T(256)}, u32[]{:S(2)}) copy-start(s32[256]{0:T(256)} %param.30) | copy-start | bytes 3076
  2.1 5.6 %collective-permute-start.22 = (f32[72,128]{1,0:T(8,128)}, f32[72,128]{1,0:T(8,128)S(1)}, u32[]{:S(2)}, u32[]{:S(2)}) collective-permute-start(f32[72,128]{1,0:T(8,128)} %shard_map.166), channel_id=1, source_target_pairs={{0,1},{1,0},{2,3},{3,2},{4,5},{5,4},{6,7},{7,6},{8,9},{9,8},{10,11... | collective-permute-start | bytes 110600 | tf_op jit(solution)/shard_map/ppermute | solution.py:481
  5.1 0.7 %copy-start.10 = (s32[2,256]{1,0:T(2,128)S(1)}, s32[2,256]{1,0:T(2,128)}, u32[]{:S(2)}) copy-start(s32[2,256]{1,0:T(2,128)} %refs_6_.1) | copy-start | bytes 6148
  5.1 0.8 %copy-start.8 = (f32[64,128]{1,0:T(8,128)S(1)}, f32[64,128]{1,0:T(8,128)}, u32[]{:S(2)}) copy-start(f32[64,128]{1,0:T(8,128)} %refs_2_.2) | copy-start | bytes 98308
  5.1 0.8 %copy-start.7 = (f32[64,128]{1,0:T(8,128)S(1)}, f32[64,128]{1,0:T(8,128)}, u32[]{:S(2)}) copy-start(f32[64,128]{1,0:T(8,128)} %refs_0_.1) | copy-start | bytes 98308
  5.1 0.8 %copy-start.5 = (f32[1,128]{1,0:T(1,128)S(1)}, f32[1,128]{1,0:T(1,128)}, u32[]{:S(2)}) copy-start(f32[1,128]{1,0:T(1,128)} %refs_4_.1) | copy-start | bytes 1540
  5.1 0.8 %copy-start.3 = (f32[256]{0:T(256)S(1)}, f32[256]{0:T(256)}, u32[]{:S(2)}) copy-start(f32[256]{0:T(256)} %param.32) | copy-start | bytes 3076
  5.1 0.8 %copy-start.4 = (f32[256]{0:T(256)S(1)}, f32[256]{0:T(256)}, u32[]{:S(2)}) copy-start(f32[256]{0:T(256)} %param.31) | copy-start | bytes 3076
  5.2 0.8 %copy-start.1 = (s32[1,2048]{1,0:T(1,128)S(1)}, s32[1,2048]{1,0:T(1,128)}, u32[]{:S(2)}) copy-start(s32[1,2048]{1,0:T(1,128)} %param.24) | copy-start | bytes 24580
  5.2 0.8 %copy-start = (f32[16,128]{1,0:T(8,128)S(1)}, f32[16,128]{1,0:T(8,128)}, u32[]{:S(2)}) copy-start(f32[16,128]{1,0:T(8,128)} %refs_3_.2) | copy-start | bytes 24580
  5.2 0.7 %copy-start.2 = (f32[256]{0:T(256)S(1)}, f32[256]{0:T(256)}, u32[]{:S(2)}) copy-start(f32[256]{0:T(256)} %param.26) | copy-start | bytes 3076
  5.9 1.8 %copy-start.9 = (f32[72,128]{1,0:T(8,128)S(1)}, f32[72,128]{1,0:T(8,128)}, u32[]{:S(2)}) copy-start(f32[72,128]{1,0:T(8,128)} %shard_map.166) | copy-start | bytes 110596
  8.2 1.3 %collective-permute-start.23 = (f32[104,128]{1,0:T(8,128)S(1)}, f32[104,128]{1,0:T(8,128)S(1)}, u32[]{:S(2)}, u32[]{:S(2)}) collective-permute-start(f32[104,128]{1,0:T(8,128)S(1)} %get-tuple-element.116), channel_id=1, source_target_pairs={{0,2},{1,3},{2,0},{3,1},{4,6},{5,7},{6,4},{7,5},{8,10},{9,11},{10,... | collective-permute-start | bytes 159752 | tf_op jit(solution)/shard_map/ppermute | solution.py:481
  9.5 4.0 %collective-permute-start.25 = (f32[3,128]{1,0:T(4,128)S(1)}, f32[3,128]{1,0:T(4,128)S(1)}, u32[]{:S(2)}, u32[]{:S(2)}) collective-permute-start(f32[3,128]{1,0:T(4,128)S(1)} %slice.568), channel_id=1, source_target_pairs={{0,7},{1,6},{2,5},{3,4},{4,3},{5,2},{6,1},{7,0},{8,15},{9,14},{10,... | collective-permute-start | bytes 4616 | tf_op jit(solution)/shard_map/ppermute | solution.py:481
  11.8 3.4 %collective-permute-start.24 = (f32[67,128]{1,0:T(8,128)S(1)}, f32[67,128]{1,0:T(8,128)S(1)}, u32[]{:S(2)}, u32[]{:S(2)}) collective-permute-start(f32[67,128]{1,0:T(8,128)S(1)} %pad_maximum_fusion.11), channel_id=1, source_target_pairs={{0,3},{1,2},{2,1},{3,0},{4,7},{5,6},{6,5},{7,4},{8,11},{9,10},{10,... | collective-permute-start | bytes 102920 | tf_op jit(solution)/shard_map/ppermute | solution.py:481
  12.4 3.3 %collective-permute-start.26 = (f32[40,128]{1,0:T(8,128)S(1)}, f32[40,128]{1,0:T(8,128)S(1)}, u32[]{:S(2)}, u32[]{:S(2)}) collective-permute-start(f32[40,128]{1,0:T(8,128)S(1)} %pad_maximum_fusion.14), channel_id=1, source_target_pairs={{0,6},{1,7},{2,4},{3,5},{4,2},{5,3},{6,0},{7,1},{8,14},{9,15},{10,... | collective-permute-start | bytes 61448 | tf_op jit(solution)/shard_map/ppermute | solution.py:481
  15.7 5.1 %collective-permute-start.29 = (f32[40,128]{1,0:T(8,128)S(1)}, f32[40,128]{1,0:T(8,128)S(1)}, u32[]{:S(2)}, u32[]{:S(2)}) collective-permute-start(f32[40,128]{1,0:T(8,128)S(1)} %pad_maximum_fusion.15.refs_6_), channel_id=1, source_target_pairs={{0,26},{1,27},{2,24},{3,25},{4,30},{5,31},{6,28},{7,29},{8,18},{9,... | collective-permute-start | bytes 61448 | tf_op jit(solution)/shard_map/ppermute | solution.py:481
  19.2 4.1 %collective-permute-start.28 = (f32[40,128]{1,0:T(8,128)S(1)}, f32[40,128]{1,0:T(8,128)S(1)}, u32[]{:S(2)}, u32[]{:S(2)}) collective-permute-start(f32[40,128]{1,0:T(8,128)S(1)} %pad_maximum_fusion.15.refs_6_), channel_id=1, source_target_pairs={{0,18},{1,19},{2,16},{3,17},{4,22},{5,23},{6,20},{7,21},{8,26},{9,... | collective-permute-start | bytes 61448 | tf_op jit(solution)/shard_map/ppermute | solution.py:481
  19.2 4.1 %collective-permute-start.27 = (f32[40,128]{1,0:T(8,128)S(1)}, f32[40,128]{1,0:T(8,128)S(1)}, u32[]{:S(2)}, u32[]{:S(2)}) collective-permute-start(f32[40,128]{1,0:T(8,128)S(1)} %pad_maximum_fusion.15.refs_6_), channel_id=1, source_target_pairs={{0,10},{1,11},{2,8},{3,9},{4,14},{5,15},{6,12},{7,13},{8,2},{9,3},... | collective-permute-start | bytes 61448 | tf_op jit(solution)/shard_map/ppermute | solution.py:481
  24.1 1.3 %collective-permute-start.30 = (f32[88,128]{1,0:T(8,128)S(1)}, f32[88,128]{1,0:T(8,128)S(1)}, u32[]{:S(2)}, u32[]{:S(2)}) collective-permute-start(f32[88,128]{1,0:T(8,128)S(1)} %get-tuple-element.122), channel_id=1, source_target_pairs={{0,2},{1,3},{2,0},{3,1},{4,6},{5,7},{6,4},{7,5},{8,10},{9,11},{10,... | collective-permute-start | bytes 135176 | tf_op jit(solution)/shard_map/ppermute | solution.py:481
  25.4 4.0 %collective-permute-start.32 = (f32[3,128]{1,0:T(4,128)S(1)}, f32[3,128]{1,0:T(4,128)S(1)}, u32[]{:S(2)}, u32[]{:S(2)}) collective-permute-start(f32[3,128]{1,0:T(4,128)S(1)} %slice.583), channel_id=1, source_target_pairs={{0,7},{1,6},{2,5},{3,4},{4,3},{5,2},{6,1},{7,0},{8,15},{9,14},{10,... | collective-permute-start | bytes 4616 | tf_op jit(solution)/shard_map/ppermute | solution.py:481
  26.9 3.5 %collective-permute-start.31 = (f32[67,128]{1,0:T(8,128)S(1)}, f32[67,128]{1,0:T(8,128)S(1)}, u32[]{:S(2)}, u32[]{:S(2)}) collective-permute-start(f32[67,128]{1,0:T(8,128)S(1)} %pad_maximum_fusion.12), channel_id=1, source_target_pairs={{0,3},{1,2},{2,1},{3,0},{4,7},{5,6},{6,5},{7,4},{8,11},{9,10},{10,... | collective-permute-start | bytes 102920 | tf_op jit(solution)/shard_map/ppermute | solution.py:481
  27.3 3.2 %collective-permute-start.33 = (f32[24,128]{1,0:T(8,128)S(1)}, f32[24,128]{1,0:T(8,128)S(1)}, u32[]{:S(2)}, u32[]{:S(2)}) collective-permute-start(f32[24,128]{1,0:T(8,128)S(1)} %pad_maximum_fusion.16), channel_id=1, source_target_pairs={{0,6},{1,7},{2,4},{3,5},{4,2},{5,3},{6,0},{7,1},{8,14},{9,15},{10,... | collective-permute-start | bytes 36872 | tf_op jit(solution)/shard_map/ppermute | solution.py:481
  30.5 5.0 %collective-permute-start.36 = (f32[24,128]{1,0:T(8,128)S(1)}, f32[24,128]{1,0:T(8,128)S(1)}, u32[]{:S(2)}, u32[]{:S(2)}) collective-permute-start(f32[24,128]{1,0:T(8,128)S(1)} %pad_maximum_fusion.17.refs_8_), channel_id=1, source_target_pairs={{0,26},{1,27},{2,24},{3,25},{4,30},{5,31},{6,28},{7,29},{8,18},{9,... | collective-permute-start | bytes 36872 | tf_op jit(solution)/shard_map/ppermute | solution.py:481
  32.0 4.2 %collective-permute-start.35 = (f32[24,128]{1,0:T(8,128)S(1)}, f32[24,128]{1,0:T(8,128)S(1)}, u32[]{:S(2)}, u32[]{:S(2)}) collective-permute-start(f32[24,128]{1,0:T(8,128)S(1)} %pad_maximum_fusion.17.refs_8_), channel_id=1, source_target_pairs={{0,18},{1,19},{2,16},{3,17},{4,22},{5,23},{6,20},{7,21},{8,26},{9,... | collective-permute-start | bytes 36872 | tf_op jit(solution)/shard_map/ppermute | solution.py:481
  32.4 3.9 %collective-permute-start.34 = (f32[24,128]{1,0:T(8,128)S(1)}, f32[24,128]{1,0:T(8,128)S(1)}, u32[]{:S(2)}, u32[]{:S(2)}) collective-permute-start(f32[24,128]{1,0:T(8,128)S(1)} %pad_maximum_fusion.17.refs_8_), channel_id=1, source_target_pairs={{0,10},{1,11},{2,8},{3,9},{4,14},{5,15},{6,12},{7,13},{8,2},{9,3},... | collective-permute-start | bytes 36872 | tf_op jit(solution)/shard_map/ppermute | solution.py:481
  37.0 1.3 %collective-permute-start.37 = (f32[88,128]{1,0:T(8,128)S(1)}, f32[88,128]{1,0:T(8,128)S(1)}, u32[]{:S(2)}, u32[]{:S(2)}) collective-permute-start(f32[88,128]{1,0:T(8,128)S(1)} %get-tuple-element.128), channel_id=1, source_target_pairs={{0,2},{1,3},{2,0},{3,1},{4,6},{5,7},{6,4},{7,5},{8,10},{9,11},{10,... | collective-permute-start | bytes 135176 | tf_op jit(solution)/shard_map/ppermute | solution.py:481
  38.3 4.0 %collective-permute-start.39 = (f32[3,128]{1,0:T(4,128)S(1)}, f32[3,128]{1,0:T(4,128)S(1)}, u32[]{:S(2)}, u32[]{:S(2)}) collective-permute-start(f32[3,128]{1,0:T(4,128)S(1)} %slice.598), channel_id=1, source_target_pairs={{0,7},{1,6},{2,5},{3,4},{4,3},{5,2},{6,1},{7,0},{8,15},{9,14},{10,... | collective-permute-start | bytes 4616 | tf_op jit(solution)/shard_map/ppermute | solution.py:481
  40.6 3.5 %collective-permute-start.38 = (f32[67,128]{1,0:T(8,128)S(1)}, f32[67,128]{1,0:T(8,128)S(1)}, u32[]{:S(2)}, u32[]{:S(2)}) collective-permute-start(f32[67,128]{1,0:T(8,128)S(1)} %pad_maximum_fusion.13), channel_id=1, source_target_pairs={{0,3},{1,2},{2,1},{3,0},{4,7},{5,6},{6,5},{7,4},{8,11},{9,10},{10,... | collective-permute-start | bytes 102920 | tf_op jit(solution)/shard_map/ppermute | solution.py:481
  41.1 3.2 %collective-permute-start.40 = (f32[24,128]{1,0:T(8,128)S(1)}, f32[24,128]{1,0:T(8,128)S(1)}, u32[]{:S(2)}, u32[]{:S(2)}) collective-permute-start(f32[24,128]{1,0:T(8,128)S(1)} %pad_maximum_fusion.18), channel_id=1, source_target_pairs={{0,6},{1,7},{2,4},{3,5},{4,2},{5,3},{6,0},{7,1},{8,14},{9,15},{10,... | collective-permute-start | bytes 36872 | tf_op jit(solution)/shard_map/ppermute | solution.py:481
  44.4 5.0 %collective-permute-start.43 = (f32[24,128]{1,0:T(8,128)S(1)}, f32[24,128]{1,0:T(8,128)S(1)}, u32[]{:S(2)}, u32[]{:S(2)}) collective-permute-start(f32[24,128]{1,0:T(8,128)S(1)} %pad_maximum_fusion.19.refs_8_), channel_id=1, source_target_pairs={{0,26},{1,27},{2,24},{3,25},{4,30},{5,31},{6,28},{7,29},{8,18},{9,... | collective-permute-start | bytes 36872 | tf_op jit(solution)/shard_map/ppermute | solution.py:481
  46.4 4.0 %collective-permute-start.42 = (f32[24,128]{1,0:T(8,128)S(1)}, f32[24,128]{1,0:T(8,128)S(1)}, u32[]{:S(2)}, u32[]{:S(2)}) collective-permute-start(f32[24,128]{1,0:T(8,128)S(1)} %pad_maximum_fusion.19.refs_8_), channel_id=1, source_target_pairs={{0,18},{1,19},{2,16},{3,17},{4,22},{5,23},{6,20},{7,21},{8,26},{9,... | collective-permute-start | bytes 36872 | tf_op jit(solution)/shard_map/ppermute | solution.py:481
  47.1 3.3 %collective-permute-start.41 = (f32[24,128]{1,0:T(8,128)S(1)}, f32[24,128]{1,0:T(8,128)S(1)}, u32[]{:S(2)}, u32[]{:S(2)}) collective-permute-start(f32[24,128]{1,0:T(8,128)S(1)} %pad_maximum_fusion.19.refs_8_), channel_id=1, source_target_pairs={{0,10},{1,11},{2,8},{3,9},{4,14},{5,15},{6,12},{7,13},{8,2},{9,3},... | collective-permute-start | bytes 36872 | tf_op jit(solution)/shard_map/ppermute | solution.py:481
  50.4 1.3 %copy-start.6 = (f32[64,16,128]{2,1,0:T(8,128)S(1)}, f32[64,16,128]{2,1,0:T(8,128)}, u32[]{:S(2)}) copy-start(f32[64,16,128]{2,1,0:T(8,128)} %param.20) | copy-start | bytes 1572868
  51.7 0.5 copy-start.14
  51.7 0.6 %copy-start.12 = (f32[64,256]{1,0:T(8,128)}, f32[64,256]{1,0:T(8,128)S(1)}, u32[]{:S(2)}) copy-start(f32[64,256]{1,0:T(8,128)S(1)} %get-tuple-element.137) | copy-start | bytes 196612
  51.7 0.6 %copy-start.13 = (f32[64,128]{1,0:T(8,128)}, f32[64,128]{1,0:T(8,128)S(1)}, u32[]{:S(2)}) copy-start(f32[64,128]{1,0:T(8,128)S(1)} %get-tuple-element.136) | copy-start | bytes 98308
